TPU v7x, 32 devices: a whole 2x2x4 slice. The times are simulated.
32 devices in a mesh: ctx: 8 (over y, x, core), tp: 4 (over z).
Axes of the slice: x: 2, y: 2, z: 4, core: 2. Of those that a mesh axis runs over, the one named last changes fastest.
Arguments:
- tokens: bfloat16 [8192, 2048], P(('ctx', 'tp')), may hold values from -6 to 6
- cotangent: bfloat16 [8192, 2048], P(('ctx', 'tp')), may hold values from -6 to 6
- block_order: int32 [4, 16], replicated, may hold values from 0 to 15, each once within a row
- gain_one: float32 [2048], replicated, may hold values from 0.5 to 1.5
- shift_one: float32 [2048], replicated, may hold values from -1 to 1
- query_w: bfloat16 [2048, 2048], P(None, 'tp'), may hold values from -0.125 to 0.125
- key_w: bfloat16 [2048, 2048], P(None, 'tp'), may hold values from -0.125 to 0.125
- value_w: bfloat16 [2048, 2048], P(None, 'tp'), may hold values from -0.125 to 0.125
- query_b: float32 [2048], P('tp'), may hold values from -1.5 to 1.5
- key_b: float32 [32, 16], P('tp'), may hold values from -1.5 to 1.5
- value_b: float32 [2048], P('tp'), may hold values from -0.1 to 0.1
- output_w: bfloat16 [2048, 2048], P('tp'), may hold values from -3 to 3
- gain_two: float32 [2048], replicated, may hold values from 0.5 to 1.5
- shift_two: float32 [2048], replicated, may hold values from -1 to 1
- gate_w: bfloat16 [2048, 5632], P(None, 'tp'), may hold values from -0.125 to 0.125
- up_w: bfloat16 [2048, 5632], P(None, 'tp'), may hold values from -0.125 to 0.125
- down_w: bfloat16 [5632, 2048], P('tp'), may hold values from -0.078125 to 0.078125
Outputs:
- out_tokens: bfloat16 [8192, 2048], P(('ctx', 'tp'))
- grad_tokens: bfloat16 [8192, 2048], P(('ctx', 'tp'))
- grad_gain_one: float32 [2048], replicated
- grad_shift_one: float32 [2048], replicated
- grad_query_w: float32 [2048, 2048], P(None, 'tp')
- grad_key_w: float32 [2048, 2048], P(None, 'tp')
- grad_value_w: float32 [2048, 2048], P(None, 'tp')
- grad_query_b: float32 [2048], P('tp')
- grad_key_b: float32 [32, 16], P('tp')
- grad_value_b: float32 [2048], P('tp')
- grad_output_w: float32 [2048, 2048], P('tp')
- grad_gain_two: float32 [2048], replicated
- grad_shift_two: float32 [2048], replicated
- grad_gate_w: float32 [2048, 5632], P(None, 'tp')
- grad_up_w: float32 [2048, 5632], P(None, 'tp')
- grad_down_w: float32 [5632, 2048], P('tp')
Inputs may be any that keep to these rules, and one draw needn't show every extreme that they name: `block_order`: each row is a permutation of the (16) block numbers of one sequence.
All inputs are finite; a program needn't handle non-finite values.
Results may differ from a plain program's by a relative error of at most 0.03.
Values may be sent and summed in bfloat16 or wider, within the bound.
No kernel may reach another device: no remote copies, remote signals or barrier semaphores. Data moves between devices by JAX's collectives and lax.ppermute only.
A program may use at most 256 MiB of HBM per device.

v0:
```python
import math

import jax
import jax.numpy as jnp
from jax import lax
from jax.sharding import PartitionSpec as P

HEAD_DIM = 64
ROT = 16
SEQS = 4
HALF_BLOCK = 128


norm_eps = 1e-05
masked_score = -1e30


def matmul(left, right):
    return jnp.dot(left, right, preferred_element_type=jnp.float32)


def row_contract(left, right):
    return lax.dot_general(
        left, right, (((0,), (0,)), ((), ())), preferred_element_type=jnp.float32
    )


def right_contract(left, right):
    return lax.dot_general(
        left, right, (((1,), (1,)), ((), ())), preferred_element_type=jnp.float32
    )


def layer_stats(values, gain_vec, shift_vec):
    row_mean = jnp.mean(values, axis=-1, keepdims=True)
    centred = values - row_mean
    inverse = lax.rsqrt(jnp.mean(centred * centred, axis=-1, keepdims=True) + norm_eps)
    unit_rows = centred * inverse
    return (unit_rows * gain_vec + shift_vec, unit_rows, inverse)


def layer_back(grad_out, unit_rows, inverse, gain_vec):
    scaled = grad_out * gain_vec
    grad_in = inverse * (
        scaled
        - jnp.mean(scaled, axis=-1, keepdims=True)
        - unit_rows * jnp.mean(scaled * unit_rows, axis=-1, keepdims=True)
    )
    return (grad_in, jnp.sum(grad_out * unit_rows, axis=0), jnp.sum(grad_out, axis=0))


def rotary_parts(positions):
    half_rot = ROT // 2
    frequencies = 10000.0 ** (-2.0 * jnp.arange(half_rot, dtype=jnp.float32) / ROT)
    angles = positions.astype(jnp.float32)[:, None] * frequencies[None, :]
    return (jnp.cos(angles)[:, None, :], jnp.sin(angles)[:, None, :], half_rot)


def rotary(values, positions):
    cosine, sine_vals, half_rot = rotary_parts(positions)
    first_part = values[..., :half_rot]
    second_part = values[..., half_rot:ROT]
    return jnp.concatenate(
        [
            first_part * cosine - second_part * sine_vals,
            second_part * cosine + first_part * sine_vals,
            values[..., ROT:],
        ],
        axis=-1,
    )


def rotary_back(gradient, positions):
    cosine, sine_vals, half_rot = rotary_parts(positions)
    first_part = gradient[..., :half_rot]
    second_part = gradient[..., half_rot:ROT]
    return jnp.concatenate(
        [
            first_part * cosine + second_part * sine_vals,
            second_part * cosine - first_part * sine_vals,
            gradient[..., ROT:],
        ],
        axis=-1,
    )


def block_positions(block_order, row_count, half_rows):
    row_index = jnp.arange(row_count, dtype=jnp.int32)
    matches = (row_index // half_rows)[:, None] == jnp.arange(
        block_order.shape[1], dtype=jnp.int32
    )[None, :]
    chosen = jnp.sum(jnp.where(matches[None, :, :], block_order[:, None, :], 0), axis=-1)
    return chosen * half_rows + row_index % half_rows


def stack_blocks(array, block_rows):
    row_count = array.shape[1]
    shaped = array.reshape((array.shape[0], row_count // block_rows, block_rows) + array.shape[2:])
    return jnp.moveaxis(shaped, 1, 0)


def unstack_blocks(stacked):
    joined = jnp.moveaxis(stacked, 0, 1)
    return joined.reshape((joined.shape[0], joined.shape[1] * joined.shape[2]) + joined.shape[3:])


def score_block(queries, query_pos, key_part, key_pos, score_scale):
    scores = (
        jnp.einsum("sqhd,skhd->shqk", queries, key_part, preferred_element_type=jnp.float32)
        * score_scale
    )
    allowed = key_pos[:, None, None, :] <= query_pos[:, None, :, None]
    return (scores, allowed)


def grad_block(
    queries, query_pos, grad_out, log_total, delta_rows, key_part, value_part, key_pos, score_scale
):
    scores, allowed = score_block(queries, query_pos, key_part, key_pos, score_scale)
    probabilities = jnp.where(
        allowed, jnp.exp(scores - jnp.swapaxes(log_total, 1, 2)[..., None]), 0.0
    )
    grad_probs = jnp.einsum(
        "sqhd,skhd->shqk", grad_out, value_part, preferred_element_type=jnp.float32
    )
    grad_scores = (probabilities * (grad_probs - jnp.swapaxes(delta_rows, 1, 2)[..., None])).astype(
        jnp.bfloat16
    )
    query_grad = (
        jnp.einsum("shqk,skhd->sqhd", grad_scores, key_part, preferred_element_type=jnp.float32)
        * score_scale
    )
    key_grad = (
        jnp.einsum("shqk,sqhd->skhd", grad_scores, queries, preferred_element_type=jnp.float32)
        * score_scale
    )
    value_grad = jnp.einsum(
        "shqk,sqhd->skhd",
        probabilities.astype(jnp.bfloat16),
        grad_out,
        preferred_element_type=jnp.float32,
    )
    return (query_grad, key_grad, value_grad)


def local(
    tokens,
    cotangent,
    block_order,
    gain_one,
    shift_one,
    query_w,
    key_w,
    value_w,
    query_b,
    key_b,
    value_b,
    output_w,
    gain_two,
    shift_two,
    gate_w,
    up_w,
    down_w,
):
    head_count = key_b.shape[0]
    half_rows = HALF_BLOCK
    block_rows = 2 * half_rows
    seq_count = SEQS
    group_rows = seq_count * block_rows
    score_scale = 1.0 / math.sqrt(HEAD_DIM)
    ctx_count = lax.axis_size("ctx")
    ctx_index = lax.axis_index("ctx")
    local_order = lax.dynamic_slice_in_dim(block_order, 2 * ctx_index, 2, 1)
    own_pos = (
        local_order[:, :, None] * half_rows + jnp.arange(half_rows, dtype=jnp.int32)[None, None, :]
    ).reshape(seq_count, block_rows)
    flat_pos = own_pos.reshape(-1)
    attn_shape = (seq_count, block_rows, head_count, HEAD_DIM)
    head_shape = (group_rows, head_count, HEAD_DIM)
    x_float = tokens.astype(jnp.float32)
    normed_one, unit_one, inverse_one = layer_stats(x_float, gain_one, shift_one)
    rows_one = lax.all_gather(normed_one.astype(jnp.bfloat16), "tp", axis=0, tiled=True)
    key_bias = jnp.concatenate(
        [key_b, jnp.zeros((head_count, HEAD_DIM - ROT), jnp.float32)], axis=1
    ).reshape(-1)
    query_lin = matmul(rows_one, query_w) + query_b
    key_lin = matmul(rows_one, key_w) + key_bias
    value_rows = (matmul(rows_one, value_w) + value_b).astype(jnp.bfloat16)
    queries = (
        rotary(query_lin.reshape(head_shape), flat_pos).astype(jnp.bfloat16).reshape(attn_shape)
    )
    key_blocks = (
        rotary(key_lin.reshape(head_shape), flat_pos).astype(jnp.bfloat16).reshape(attn_shape)
    )
    value_blocks = value_rows.reshape(attn_shape)
    start_state = (
        jnp.zeros((seq_count, head_count, block_rows, HEAD_DIM), jnp.float32),
        jnp.full((seq_count, head_count, block_rows), masked_score, jnp.float32),
        jnp.zeros((seq_count, head_count, block_rows), jnp.float32),
    )
    key_part = lax.all_gather(key_blocks, "ctx", axis=1, tiled=True)
    value_part = lax.all_gather(value_blocks, "ctx", axis=1, tiled=True)
    row_count = key_part.shape[1]
    key_pos = block_positions(block_order, row_count, half_rows)

    def forward_one_block(inner, parts):
        accumulated, running_max, row_total = inner
        key_blk, value_blk, pos_blk = parts
        scores, allowed = score_block(queries, own_pos, key_blk, pos_blk, score_scale)
        scores = jnp.where(allowed, scores, masked_score)
        new_max = jnp.maximum(running_max, jnp.max(scores, axis=-1))
        weights = jnp.where(allowed, jnp.exp(scores - new_max[..., None]), 0.0)
        factor = jnp.exp(running_max - new_max)
        row_total = row_total * factor + jnp.sum(weights, axis=-1)
        accumulated = accumulated * factor[..., None] + jnp.einsum(
            "shqk,skhd->shqd",
            weights.astype(jnp.bfloat16),
            value_blk,
            preferred_element_type=jnp.float32,
        )
        return ((accumulated, new_max, row_total), None)

    result, unused = lax.scan(
        forward_one_block,
        start_state,
        (
            stack_blocks(key_part, block_rows),
            stack_blocks(value_part, block_rows),
            stack_blocks(key_pos, block_rows),
        ),
    )
    accumulated, running_max, row_total = result
    log_total = jnp.swapaxes(running_max + jnp.log(row_total), 1, 2)
    attention = jnp.swapaxes(accumulated / row_total[..., None], 1, 2).astype(jnp.bfloat16)
    attn_rows = attention.reshape(group_rows, head_count * HEAD_DIM)
    mixed = x_float + lax.psum_scatter(
        matmul(attn_rows, output_w).astype(jnp.bfloat16), "tp", scatter_dimension=0, tiled=True
    ).astype(jnp.float32)
    normed_two, unit_two, inverse_two = layer_stats(mixed, gain_two, shift_two)
    rows_two = lax.all_gather(normed_two.astype(jnp.bfloat16), "tp", axis=0, tiled=True)
    gate_lin = matmul(rows_two, gate_w)
    up_lin = matmul(rows_two, up_w)
    sigmoid_gate = jax.nn.sigmoid(gate_lin)
    silu_gate = gate_lin * sigmoid_gate
    activation = (silu_gate * up_lin).astype(jnp.bfloat16)
    out_float = mixed + lax.psum_scatter(
        matmul(activation, down_w).astype(jnp.bfloat16), "tp", scatter_dimension=0, tiled=True
    ).astype(jnp.float32)
    out_tokens = out_float.astype(jnp.bfloat16)
    grad_rows = lax.all_gather(cotangent, "tp", axis=0, tiled=True)
    grad_down_w = row_contract(activation, grad_rows)
    grad_act = right_contract(grad_rows, down_w)
    grad_gate = (grad_act * up_lin * sigmoid_gate * (1.0 + gate_lin * (1.0 - sigmoid_gate))).astype(
        jnp.bfloat16
    )
    grad_up = (grad_act * silu_gate).astype(jnp.bfloat16)
    grad_gate_w = row_contract(rows_two, grad_gate)
    grad_up_w = row_contract(rows_two, grad_up)
    grad_two = lax.psum_scatter(
        (right_contract(grad_gate, gate_w) + right_contract(grad_up, up_w)).astype(jnp.bfloat16),
        "tp",
        scatter_dimension=0,
        tiled=True,
    ).astype(jnp.float32)
    norm_grad_two, grad_gain_two, grad_shift_two = layer_back(
        grad_two, unit_two, inverse_two, gain_two
    )
    grad_mixed = cotangent.astype(jnp.float32) + norm_grad_two
    branch_rows = lax.all_gather(grad_mixed.astype(jnp.bfloat16), "tp", axis=0, tiled=True)
    grad_output_w = row_contract(attn_rows, branch_rows)
    grad_attn = right_contract(branch_rows, output_w).astype(jnp.bfloat16).reshape(attn_shape)
    delta_rows = jnp.sum(grad_attn.astype(jnp.float32) * attention.astype(jnp.float32), axis=-1)
    query_zero = jnp.zeros(attn_shape, jnp.float32)
    whole_zero = jnp.zeros((seq_count, ctx_count * block_rows, head_count, HEAD_DIM), jnp.float32)
    back_start = (query_zero, whole_zero, whole_zero)
    key_part = lax.all_gather(key_blocks, "ctx", axis=1, tiled=True)
    value_part = lax.all_gather(value_blocks, "ctx", axis=1, tiled=True)
    row_count = key_part.shape[1]
    key_pos = block_positions(block_order, row_count, half_rows)

    def key_one_block(inner, parts):
        key_blk, value_blk, pos_blk = parts
        query_grad, key_grad, value_grad = grad_block(
            queries,
            own_pos,
            grad_attn,
            log_total,
            delta_rows,
            key_blk,
            value_blk,
            pos_blk,
            score_scale,
        )
        return (inner + query_grad, (key_grad, value_grad))

    grad_queries, stacked = lax.scan(
        key_one_block,
        back_start[0],
        (
            stack_blocks(key_part, block_rows),
            stack_blocks(value_part, block_rows),
            stack_blocks(key_pos, block_rows),
        ),
    )
    key_new = unstack_blocks(stacked[0])
    value_new = unstack_blocks(stacked[1])
    folded = (grad_queries, key_new, value_new)
    grad_queries = folded[0]
    grad_keys, grad_values = (
        lax.psum_scatter(
            folded[1].astype(jnp.bfloat16), "ctx", scatter_dimension=1, tiled=True
        ).astype(jnp.float32),
        lax.psum_scatter(
            folded[2].astype(jnp.bfloat16), "ctx", scatter_dimension=1, tiled=True
        ).astype(jnp.float32),
    )
    grad_query_lin = rotary_back(grad_queries.reshape(head_shape), flat_pos).astype(jnp.bfloat16)
    grad_key_lin = rotary_back(grad_keys.reshape(head_shape), flat_pos).astype(jnp.bfloat16)
    grad_value_lin = grad_values.reshape(group_rows, head_count * HEAD_DIM).astype(jnp.bfloat16)
    grad_query_flat = grad_query_lin.reshape(group_rows, head_count * HEAD_DIM)
    grad_key_flat = grad_key_lin.reshape(group_rows, head_count * HEAD_DIM)
    grad_query_w = row_contract(rows_one, grad_query_flat)
    grad_key_w = row_contract(rows_one, grad_key_flat)
    grad_value_w = row_contract(rows_one, grad_value_lin)
    grad_query_b = jnp.sum(grad_query_flat.astype(jnp.float32), axis=0)
    grad_key_b = jnp.sum(grad_key_lin[:, :, :ROT].astype(jnp.float32), axis=0)
    grad_value_b = jnp.sum(grad_value_lin.astype(jnp.float32), axis=0)
    grad_one = lax.psum_scatter(
        (
            right_contract(grad_query_flat, query_w)
            + right_contract(grad_key_flat, key_w)
            + right_contract(grad_value_lin, value_w)
        ).astype(jnp.bfloat16),
        "tp",
        scatter_dimension=0,
        tiled=True,
    ).astype(jnp.float32)
    norm_grad_one, grad_gain_one, grad_shift_one = layer_back(
        grad_one, unit_one, inverse_one, gain_one
    )
    grad_tokens = (grad_mixed + norm_grad_one).astype(jnp.bfloat16)
    summed = (
        lax.psum(grad_query_w.astype(jnp.bfloat16), "ctx").astype(jnp.float32),
        lax.psum(grad_key_w.astype(jnp.bfloat16), "ctx").astype(jnp.float32),
        lax.psum(grad_value_w.astype(jnp.bfloat16), "ctx").astype(jnp.float32),
        lax.psum(grad_query_b.astype(jnp.bfloat16), "ctx").astype(jnp.float32),
        lax.psum(grad_key_b.astype(jnp.bfloat16), "ctx").astype(jnp.float32),
        lax.psum(grad_value_b.astype(jnp.bfloat16), "ctx").astype(jnp.float32),
        lax.psum(grad_output_w.astype(jnp.bfloat16), "ctx").astype(jnp.float32),
        lax.psum(grad_gate_w.astype(jnp.bfloat16), "ctx").astype(jnp.float32),
        lax.psum(grad_up_w.astype(jnp.bfloat16), "ctx").astype(jnp.float32),
        lax.psum(grad_down_w.astype(jnp.bfloat16), "ctx").astype(jnp.float32),
    )
    norm_summed = lax.psum(
        (grad_gain_one, grad_shift_one, grad_gain_two, grad_shift_two), ("ctx", "tp")
    )
    return (
        out_tokens,
        grad_tokens,
        norm_summed[0],
        norm_summed[1],
        summed[0],
        summed[1],
        summed[2],
        summed[3],
        summed[4],
        summed[5],
        summed[6],
        norm_summed[2],
        norm_summed[3],
        summed[7],
        summed[8],
        summed[9],
    )


def solution(mesh):
    in_specs = (
        P(("ctx", "tp"), None),
        P(("ctx", "tp"), None),
        P(),
        P(),
        P(),
        P(None, "tp"),
        P(None, "tp"),
        P(None, "tp"),
        P("tp"),
        P("tp", None),
        P("tp"),
        P("tp", None),
        P(),
        P(),
        P(None, "tp"),
        P(None, "tp"),
        P("tp", None),
    )
    out_specs = (
        P(("ctx", "tp"), None),
        P(("ctx", "tp"), None),
        P(),
        P(),
        P(None, "tp"),
        P(None, "tp"),
        P(None, "tp"),
        P("tp"),
        P("tp", None),
        P("tp"),
        P("tp", None),
        P(),
        P(),
        P(None, "tp"),
        P(None, "tp"),
        P("tp", None),
    )
    return jax.shard_map(local, mesh=mesh, in_specs=in_specs, out_specs=out_specs, check_vma=False)
```

profile of v0, /device:TPU:0, one launch (start us, length us, event | category | flops | bytes accessed | tf_op | source)
XLA Modules:
  0.0 1593.5 jit_solution(7165357676266340323)
XLA Ops:
  13.8 83.6 %all-gather.7.cloned.1.call-done = bf16[1024,2048]{1,0:T(8,128)(2,1)} async-done(((bf16[256,2048]{1,0:T(8,128)(2,1)}), bf16[1024,2048]{1,0:T(8,128)(2,1)}) %all-gather.7.cloned.1.call-update) | async-done | bytes 4194320 | tf_op jit(solution)/shard_map/all_gather | solution.py:182
  97.4 6.2 add_convert_fusion.4
  107.3 5.4 convolution_add_fusion.1
  125.0 36.4 %all-gather.11.cloned.1.call-done = bf16[4,2048,8,64]{1,0,3,2:T(4,128)(2,1)} async-done(((bf16[4,256,8,64]{1,0,3,2:T(4,128)(2,1)}), bf16[4,2048,8,64]{1,0,3,2:T(4,128)(2,1)}) %all-gather.11.cloned.1.call-update) | async-done | bytes 8388624 | tf_op jit(solution)/shard_map/all_gather | solution.py:202
  161.3 14.6 reshape.294
  175.9 11.4 copy.102
  187.3 32.5 %all-gather.9.cloned.1.call-done = bf16[4,2048,8,64]{1,3,2,0:T(8,128)(2,1)} async-done(((bf16[4,256,8,64]{1,3,2,0:T(8,128)(2,1)}), bf16[4,2048,8,64]{1,3,2,0:T(8,128)(2,1)}) %all-gather.9.cloned.1.call-update) | async-done | bytes 8388624 | tf_op jit(solution)/shard_map/all_gather | solution.py:201
  219.8 10.5 copy.130
  230.2 8.8 copy.100
  239.0 81.4 %while.30 = (s32[]{:T(128)}, f32[4,8,256,64]{2,3,1,0:T(8,128)}, f32[4,8,256]{2,1,0:T(8,128)S(1)}, f32[4,8,256]{2,1,0:T(8,128)S(1)}, s32[8,4,256]{2,1,0:T(4,128)S...) while((s32[]{:T(128)}, f32[4,8,256,64]{2,3,1,0:T(8,128)}, ...), condition=%wide.region_6.7_spmd.clone, body=%wide.region_3.6_spmd.clone.sunk | while | flops 566010880 | bytes 50884832 | solution.py:223
  244.5 3.6 fusion.162
  254.6 3.6 fusion.162
  264.8 3.6 fusion.162
  274.9 3.6 fusion.162
  285.1 3.6 fusion.162
  295.2 3.6 fusion.162
  305.3 3.6 fusion.162
  315.5 3.6 fusion.162
  324.6 4.4 convolution_convert_fusion.4
  329.1 76.8 %reduce-scatter.7.cloned.1.call-done = bf16[256,2048]{1,0:T(8,128)(2,1)} async-done(((bf16[1024,2048]{1,0:T(8,128)(2,1)}), bf16[256,2048]{1,0:T(8,128)(2,1)}) %reduce-scatter.7.cloned.1.call-update) | async-done | bytes 1048592 | tf_op jit(solution)/shard_map/reduce_scatter | solution.py:236
  412.3 80.8 %all-gather.13.cloned.1.call-done = bf16[1024,2048]{1,0:T(8,128)(2,1)} async-done(((bf16[256,2048]{1,0:T(8,128)(2,1)}), bf16[1024,2048]{1,0:T(8,128)(2,1)}) %all-gather.13.cloned.1.call-update) | async-done | bytes 4194320 | tf_op jit(solution)/shard_map/all_gather | solution.py:240
  493.1 12.3 fusion.82
  505.4 10.2 fusion.81
  515.6 58.4 %all-gather.15.cloned.1.call-done = bf16[1024,2048]{1,0:T(8,128)(2,1)} async-done(((bf16[256,2048]{1,0:T(8,128)(2,1)}), bf16[1024,2048]{1,0:T(8,128)(2,1)}) %all-gather.15.cloned.1.call-update) | async-done | bytes 4194320 | tf_op jit(solution)/shard_map/all_gather | solution.py:250
  573.9 15.6 multiply_convert_fusion
  589.5 10.8 fusion.83
  600.4 11.2 add_convert_fusion.1
  611.6 75.4 %reduce-scatter.11.cloned.1.call-done = bf16[256,2048]{1,0:T(8,128)(2,1)} async-done(((bf16[1024,2048]{1,0:T(8,128)(2,1)}), bf16[256,2048]{1,0:T(8,128)(2,1)}) %reduce-scatter.11.cloned.1.call-update) | async-done | bytes 1048592 | tf_op jit(solution)/shard_map/reduce_scatter | solution.py:259
  687.0 3.7 fusion.69
  694.8 81.3 %all-gather.17.cloned.1.call-done = bf16[1024,2048]{1,0:T(8,128)(2,1)} async-done(((bf16[256,2048]{1,0:T(8,128)(2,1)}), bf16[1024,2048]{1,0:T(8,128)(2,1)}) %all-gather.17.cloned.1.call-update) | async-done | bytes 4194320 | tf_op jit(solution)/shard_map/all_gather | solution.py:269
  776.1 5.5 convolution_convert_fusion.9
  784.9 4.0 multiply_reduce_fusion
  790.1 116.7 %while.31 = (s32[]{:T(128)}, f32[4,256,8,64]{1,3,2,0:T(8,128)S(1)}, bf16[8,4,256,8,64]{2,4,3,1,0:T(8,128)(2,1)}, bf16[8,4,256,8,64]{2,4,3,1,0:T(8,128)(2,1)}, bf...) while((s32[]{:T(128)}, f32[4,256,8,64]{1,3,2,0:T(8,128)S(1)}, ...), condition=%wide.region_16.17_spmd.clone, body=%wide.region_15.16_spmd.clone.sunk | while | flops 1365509120 | bytes 58585320 | solution.py:296
  793.1 4.5 fusion.174
  807.7 4.5 fusion.174
  822.3 4.5 fusion.174
  836.9 4.5 fusion.174
  851.4 4.5 fusion.174
  866.0 4.5 fusion.174
  880.6 4.5 fusion.174
  895.2 4.5 fusion.174
  906.9 8.0 copy.127
  914.9 8.8 copy.129
  925.8 58.9 %reduce-scatter.13.cloned.1.call-done = bf16[4,256,8,64]{1,3,2,0:T(8,128)(2,1)} async-done(((bf16[4,2048,8,64]{1,3,2,0:T(8,128)(2,1)}), bf16[4,256,8,64]{1,3,2,0:T(8,128)(2,1)}) %reduce-scatter.13.cloned.1.call-update) | async-done | bytes 1048592 | tf_op jit(solution)/shard_map/reduce_scatter | solution.py:310
  988.7 71.6 %reduce-scatter.15.cloned.1.call-done = bf16[4,256,8,64]{1,3,2,0:T(8,128)(2,1)} async-done(((bf16[4,2048,8,64]{1,3,2,0:T(8,128)(2,1)}), bf16[4,256,8,64]{1,3,2,0:T(8,128)(2,1)}) %reduce-scatter.15.cloned.1.call-update) | async-done | bytes 1048592 | tf_op jit(solution)/shard_map/reduce_scatter | solution.py:313
  1067.9 6.1 add_convert_fusion
  1074.1 10.9 convolution_convert_fusion.3
  1085.2 10.6 convolution_convert_fusion
  1095.8 8.7 convolution_convert_fusion.1
  1104.5 8.9 convolution_convert_fusion.2
  1113.4 3.7 convolution_convert_fusion.5
  1117.1 3.8 convolution_convert_fusion.6
  1120.9 3.8 convolution_convert_fusion.8
  1124.7 3.8 convolution_convert_fusion.7
  1131.5 13.5 all-reduce.2
  1146.7 4.2 reduce-scatter.17.cloned.1.call-done
  1153.2 47.4 %all-reduce.1 = (f32[2048]{0:T(1024)}, f32[2048]{0:T(1024)}, f32[2048]{0:T(1024)}, f32[2048]{0:T(1024)}) all-reduce(f32[2048]{0:T(1024)S(1)} %get-tuple-element.287, f32[2048]{0:T(1024)S(1)} %get-tuple-element.292, f32[2048]{0:T(1024)S(1)} %copy-done.35, f32[2048]{0:T(1024)S(1)} %copy-done.36), channel_id=1, replica_groups=mesh['ctx'=8,'tp'=4] {'ctx','tp'}, use_global_device_ids=true, to_apply=%region_23.24 | all-reduce | flops 8192 | bytes 65536 | tf_op jit(solution)/shard_map/psum | solution.py:354
  1200.7 31.5 %reduce-scatter.9.cloned.1.call-done = bf16[256,2048]{1,0:T(8,128)(2,1)} async-done(((bf16[1024,2048]{1,0:T(8,128)(2,1)}), bf16[256,2048]{1,0:T(8,128)(2,1)}) %reduce-scatter.9.cloned.1.call-update) | async-done | bytes 1048592 | tf_op jit(solution)/shard_map/reduce_scatter | solution.py:246
  1232.2 4.7 fusion.62
  1236.9 319.2 %all-reduce.6.cloned.1.call-done = (bf16[2048,512]{1,0:T(8,128)(2,1)}, bf16[2048,512]{1,0:T(8,128)(2,1)}, bf16[2048,512]{1,0:T(8,128)(2,1)}, bf16[512,2048]{1,0:...) async-done(((bf16[2048,512]{1,0:T(8,128)(2,1)}, bf16[2048,512]{1,0:T(8,128)(2,1)}, bf16[2048,512]{1,0:T(8,128)(2,1)}, ...) | async-done | bytes 25690128 | tf_op jit(solution)/shard_map/psum | solution.py:343
  1556.1 4.3 convert_element_type.233
  1569.6 5.7 convert_element_type.244
  1575.4 5.2 convert_element_type.246
  1580.6 6.0 convert_element_type.248
  (423 shorter events, 203.7 us)
Async XLA Ops:
  7.2 317.4 %copy-start = (bf16[512,2048]{1,0:T(8,128)(2,1)S(1)}, bf16[512,2048]{1,0:T(8,128)(2,1)}, u32[]{:S(2)}) copy-start(bf16[512,2048]{1,0:T(8,128)(2,1)} %param.32) | copy-start | bytes 6291460
  7.2 90.2 %copy-start.58 = (f32[512]{0:T(512)S(1)}, f32[512]{0:T(512)}, u32[]{:S(2)}) copy-start(f32[512]{0:T(512)} %param.31) | copy-start | bytes 6148
  7.2 90.2 %all-gather.7.cloned.1.call-start = ((), (), s32[]{:S(2)}) async-start(), calls=%async_computation.6 | async-start | bytes 5242880 | tf_op jit(solution)/shard_map/all_gather | solution.py:182
  13.8 147.6 %all-gather.11.cloned.1.call-start = ((), (), s32[]{:S(2)}) async-start(), calls=%async_computation.8 | async-start | bytes 9437184 | tf_op jit(solution)/shard_map/all_gather | solution.py:202
  103.6 3.2 copy-start.49
  103.6 3.3 copy-start.48
  106.7 113.1 %all-gather.9.cloned.1.call-start = ((), (), s32[]{:S(2)}) async-start(), calls=%async_computation.7 | async-start | bytes 9437184 | tf_op jit(solution)/shard_map/all_gather | solution.py:201
  107.2 9.7 copy-start.26
  107.2 9.7 copy-start.28
  107.2 5.6 copy-start.50
  119.4 286.5 %reduce-scatter.7.cloned.1.call-start = ((), (), s32[]{:S(2)}) async-start(), calls=%async_computation.9 | async-start | bytes 5242880 | tf_op jit(solution)/shard_map/reduce_scatter | solution.py:236
  329.0 81.0 %copy-start.30 = (f32[2048]{0:T(1024)S(1)}, f32[2048]{0:T(1024)}, u32[]{:S(2)}) copy-start(f32[2048]{0:T(1024)} %param.33) | copy-start | bytes 24580
  329.0 81.0 %copy-start.47 = (f32[2048]{0:T(1024)S(1)}, f32[2048]{0:T(1024)}, u32[]{:S(2)}) copy-start(f32[2048]{0:T(1024)} %param.34) | copy-start | bytes 24580
  329.1 164.1 %all-gather.13.cloned.1.call-start = ((), (), s32[]{:S(2)}) async-start(), calls=%async_computation.10 | async-start | bytes 5242880 | tf_op jit(solution)/shard_map/all_gather | solution.py:240
  405.9 4.1 copy-start.2
  406.0 4.1 copy-start.6
  408.0 282.8 %copy-start.33 = (f32[256]{0:T(256)}, f32[256]{0:T(256)S(1)}, u32[]{:S(2)}) copy-start(f32[256]{0:T(256)S(1)} %broadcast_multiply_fusion.5) | copy-start | bytes 3076
  410.1 280.7 %copy-start.39 = (f32[256]{0:T(256)}, f32[256]{0:T(256)S(1)}, u32[]{:S(2)}) copy-start(f32[256]{0:T(256)S(1)} %add_rsqrt_fusion) | copy-start | bytes 3076
  411.7 162.3 %all-gather.15.cloned.1.call-start = ((), (), s32[]{:S(2)}) async-start(), calls=%async_computation.12 | async-start | bytes 5242880 | tf_op jit(solution)/shard_map/all_gather | solution.py:250
  412.2 274.8 %reduce-scatter.11.cloned.1.call-start = ((), (), s32[]{:S(2)}) async-start(), calls=%async_computation.13 | async-start | bytes 5242880 | tf_op jit(solution)/shard_map/reduce_scatter | solution.py:259
  493.1 12.3 copy-start.52
  589.5 10.8 copy-start.60
  589.5 10.8 copy-start.62
  611.5 164.6 %all-gather.17.cloned.1.call-start = ((), (), s32[]{:S(2)}) async-start(), calls=%async_computation.14 | async-start | bytes 5242880 | tf_op jit(solution)/shard_map/all_gather | solution.py:269
  687.0 4.3 copy-start.3
  687.0 4.3 copy-start.7
  687.0 4.3 copy-start.10
  694.7 290.0 %reduce-scatter.13.cloned.1.call-start = ((), (), s32[]{:S(2)}) async-start(), calls=%async_computation.15 | async-start | bytes 9437184 | tf_op jit(solution)/shard_map/reduce_scatter | solution.py:310
  784.9 4.0 copy-start.9
  784.9 5.2 copy-start.5
  914.8 145.5 %reduce-scatter.15.cloned.1.call-start = ((), (), s32[]{:S(2)}) async-start(), calls=%async_computation.16 | async-start | bytes 9437184 | tf_op jit(solution)/shard_map/reduce_scatter | solution.py:313
  923.7 227.3 %reduce-scatter.17.cloned.1.call-start = ((), (), s32[]{:S(2)}) async-start(), calls=%async_computation.17 | async-start | bytes 5242880 | tf_op jit(solution)/shard_map/reduce_scatter | solution.py:328
  1062.9 61.9 %copy-start.19 = (bf16[1024,8,64]{0,2,1:T(8,128)(2,1)}, bf16[1024,8,64]{0,2,1:T(8,128)(2,1)S(1)}, u32[]{:S(2)}) copy-start(bf16[1024,8,64]{0,2,1:T(8,128)(2,1)S(1)} %maximum_convert_fusion.1) | copy-start | bytes 3145732
  1074.0 158.1 %reduce-scatter.9.cloned.1.call-start = ((), (), s32[]{:S(2)}) async-start(), calls=%async_computation.11 | async-start | bytes 5242880 | tf_op jit(solution)/shard_map/reduce_scatter | solution.py:246
  1085.0 471.2 %all-reduce.6.cloned.1.call-start = ((), (), s32[]{:S(2)}) async-start(), calls=%async_computation.18 | async-start | bytes 51380224 | tf_op jit(solution)/shard_map/psum | solution.py:343
  1085.2 10.6 copy-start.53
  1085.2 10.6 copy-start.63
  1095.8 8.7 copy-start.61
  1104.5 8.9 copy-start.23
  1104.5 8.9 copy-start.54
  1113.4 3.7 copy-start.51
  1117.1 3.8 copy-start.21
  1128.5 22.4 %copy-start.4 = (bf16[256,2048]{1,0:T(8,128)(2,1)S(1)}, bf16[256,2048]{1,0:T(8,128)(2,1)}, u32[]{:S(2)}) copy-start(bf16[256,2048]{1,0:T(8,128)(2,1)} %param.21) | copy-start | bytes 3145732
  1128.5 22.4 %copy-start.32 = (f32[2048]{0:T(1024)S(1)}, f32[2048]{0:T(1024)}, u32[]{:S(2)}) copy-start(f32[2048]{0:T(1024)} %param.24) | copy-start | bytes 24580
  1128.5 22.4 %copy-start.38 = (f32[256]{0:T(256)S(1)}, f32[256]{0:T(256)}, u32[]{:S(2)}) copy-start(f32[256]{0:T(256)} %copy-done.37) | copy-start | bytes 3076
  1128.5 22.4 %copy-start.42 = (f32[256]{0:T(256)S(1)}, f32[256]{0:T(256)}, u32[]{:S(2)}) copy-start(f32[256]{0:T(256)} %copy-done.41) | copy-start | bytes 3076
  1128.6 24.7 %copy-start.35 = (f32[2048]{0:T(1024)S(1)}, f32[2048]{0:T(1024)}, u32[]{:S(2)}) copy-start(f32[2048]{0:T(1024)} %get-tuple-element.285) | copy-start | bytes 24580
  1128.6 24.7 %copy-start.36 = (f32[2048]{0:T(1024)S(1)}, f32[2048]{0:T(1024)}, u32[]{:S(2)}) copy-start(f32[2048]{0:T(1024)} %get-tuple-element.291) | copy-start | bytes 24580
  1128.6 103.5 %copy-start.8 = (bf16[256,2048]{1,0:T(8,128)(2,1)S(1)}, bf16[256,2048]{1,0:T(8,128)(2,1)}, u32[]{:S(2)}) copy-start(bf16[256,2048]{1,0:T(8,128)(2,1)} %reduce-scatter.7.cloned.1.call-done) | copy-start | bytes 3145732
  1128.6 103.5 %copy-start.11 = (bf16[256,2048]{1,0:T(8,128)(2,1)S(1)}, bf16[256,2048]{1,0:T(8,128)(2,1)}, u32[]{:S(2)}) copy-start(bf16[256,2048]{1,0:T(8,128)(2,1)} %param.22) | copy-start | bytes 3145732
  1128.6 103.5 %copy-start.31 = (f32[2048]{0:T(1024)S(1)}, f32[2048]{0:T(1024)}, u32[]{:S(2)}) copy-start(f32[2048]{0:T(1024)} %param.33) | copy-start | bytes 24580
  1128.6 103.5 %copy-start.34 = (f32[256]{0:T(256)S(1)}, f32[256]{0:T(256)}, u32[]{:S(2)}) copy-start(f32[256]{0:T(256)} %copy-done.33) | copy-start | bytes 3076
  1128.6 103.5 %copy-start.40 = (f32[256]{0:T(256)S(1)}, f32[256]{0:T(256)}, u32[]{:S(2)}) copy-start(f32[256]{0:T(256)} %copy-done.39) | copy-start | bytes 3076
  1128.6 103.5 %copy-start.44 = (f32[256]{0:T(256)S(1)}, f32[256]{0:T(256)}, u32[]{:S(2)}) copy-start(f32[256]{0:T(256)} %copy-done.43) | copy-start | bytes 3076
  1128.6 103.5 %copy-start.46 = (f32[256]{0:T(256)S(1)}, f32[256]{0:T(256)}, u32[]{:S(2)}) copy-start(f32[256]{0:T(256)} %copy-done.45) | copy-start | bytes 3076
  1556.1 4.4 copy-start.18
  1560.5 9.1 slice-start.4
  1563.2 3.7 copy-start.16
  1563.2 6.4 slice-start.5
  1567.0 8.4 slice-start.2
  1569.6 5.7 slice-start.3
  1569.6 10.9 slice-start
  1575.4 5.2 slice-start.1
  1580.5 6.0 copy-start.1
  (40 other events, 74.4 us)
Sparse Core Ops, SparseCore 0:
  13.9 83.4 all-gather.6
  106.8 54.4 all-gather.10
  163.8 55.9 all-gather.8
  329.1 76.7 reduce-scatter.6
  411.8 81.2 all-gather.12
  494.6 79.2 all-gather.14
  611.7 75.2 reduce-scatter.10
  694.9 81.2 all-gather.16
  915.0 69.7 reduce-scatter.12
  989.0 71.2 reduce-scatter.14
  1074.2 76.7 reduce-scatter.16
  1153.8 78.3 reduce-scatter.8
  1238.4 317.7 all-reduce.5
where the time goes:
time: 1600 us; the launch traced here: 1590 us
  waiting for transfers between devices  1010 us (63%)
  matrix products  314 us (20%)
  local copies, waits for them, and re-layouts  95.6 us (6%)
  other arithmetic  94.3 us (6%)
  blocking collectives  60.9 us (4%)
    psum x1, waiting for transfers between devices, local(): lax.psum(grad_query_w.astype(jnp.bfloat16), 'ctx').astype(jnp.float32)  319 us
    all_gather x1, waiting for transfers between devices, local(): lax.all_gather(normed_one.astype(jnp.bfloat16), 'tp', axis=0, tiled=True)  83.6 us
    all_gather x1, waiting for transfers between devices, local(): lax.all_gather(grad_mixed.astype(jnp.bfloat16), 'tp', axis=0, tiled=True)  81.3 us
    all_gather x1, waiting for transfers between devices, local(): lax.all_gather(normed_two.astype(jnp.bfloat16), 'tp', axis=0, tiled=True)  80.8 us
    reduce_scatter x1, waiting for transfers between devices, local(): lax.psum_scatter(matmul(attn_rows, output_w).astype(jnp.bfloat16), 'tp',...  76.8 us
    reduce_scatter x1, waiting for transfers between devices, local(): lax.psum_scatter((right_contract(grad_gate, gate_w) + right_contract(grad...  75.4 us
    reduce_scatter x1, waiting for transfers between devices, local(): lax.psum_scatter(folded[2].astype(jnp.bfloat16), 'ctx', scatter_dimension...  71.6 us
    reduce_scatter x1, waiting for transfers between devices, local(): lax.psum_scatter(folded[1].astype(jnp.bfloat16), 'ctx', scatter_dimension...  58.9 us
  transfers between devices with their start and end apart: 13, of which 13 were waited for; matrix products, arithmetic and copies ran while one was open for 9% of the time, Pallas kernels for 0%

commit v1 on v0

v1 whole, which is shorter than its diff:
```python
import functools
import jax, jax.numpy as jnp
from jax import lax
from jax.experimental import pallas as pl
from jax.experimental.pallas import tpu as pltpu

BLK = 128
CB = 4
CH = BLK * CB
NEG = -1e30
SCALE = 0.125

def nt(a, b):
    return lax.dot_general(a, b, (((1,), (1,)), ((), ())), preferred_element_type=jnp.float32)

def nn(a, b):
    return lax.dot_general(a, b, (((1,), (0,)), ((), ())), preferred_element_type=jnp.float32)

def lane_of(shape):
    return lax.broadcasted_iota(jnp.int32, shape, 1)

def row_of(shape):
    return lax.broadcasted_iota(jnp.int32, shape, 0)

def split_heads(x):
    low = lane_of(x.shape) < 64
    zero = jnp.zeros_like(x)
    return jnp.concatenate([jnp.where(low, x, zero), jnp.where(low, zero, x)], axis=0)

def join_heads(x):
    low = lane_of((BLK, 128)) < 64
    return jnp.where(low, x[:BLK], x[BLK:])

def sort_rows(order_ref, s, src_ref, dst_ref, count):
    for p in range(count):
        slot = order_ref[s, p]
        dst_ref[p * BLK:(p + 1) * BLK, 0:128] = src_ref[slot // 2, 0, slot % 2]

def fwd_kernel(order_ref, own_ref, q_ref, k_ref, v_ref, o_ref, lse_ref, ks, vs, scr, acc, *, blocks):
    s = pl.program_id(0)
    @pl.when((s == 0) & (pl.program_id(1) == 0))
    def _():
        vs[:, 128:256] = jnp.ones((blocks * BLK, 128), jnp.bfloat16)
    sort_rows(order_ref, s, k_ref, ks, blocks)
    sort_rows(order_ref, s, v_ref, vs, blocks)
    for w in range(2):
        pos = own_ref[s, w]
        last = pos // CB
        qs = split_heads(q_ref[0, w * BLK:(w + 1) * BLK, :] * jnp.bfloat16(SCALE))

        def tiles_max(run, sc):
            for t in range(CB):
                run = jnp.maximum(run, sc[:, t * 128:(t + 1) * 128])
            return run

        def score(c, run):
            at = pl.multiple_of(c * CH, CH)
            sc = nt(qs, ks[pl.ds(at, CH), :])
            scr[c] = sc
            return tiles_max(run, sc)

        run = lax.fori_loop(0, last, score, jnp.full((2 * BLK, 128), NEG, jnp.float32))
        at = pl.multiple_of(last * CH, CH)
        sc = nt(qs, ks[pl.ds(at, CH), :])
        qpos = pos * BLK + row_of((2 * BLK, CH)) % BLK
        kpos = last * CH + lane_of((2 * BLK, CH))
        sc = jnp.where(kpos <= qpos, sc, NEG)
        scr[last] = sc
        run = tiles_max(run, sc)
        top = jnp.max(run, axis=1, keepdims=True)
        topb = jnp.broadcast_to(top, (2 * BLK, 128))
        topc = jnp.concatenate([topb] * CB, axis=1)
        acc[...] = jnp.zeros_like(acc)

        def weigh(c, carry):
            at = pl.multiple_of(c * CH, CH)
            p = jnp.exp(scr[c] - topc).astype(jnp.bfloat16)
            acc[...] += nn(p, vs[pl.ds(at, CH), :])
            return carry

        lax.fori_loop(0, last + 1, weigh, 0)
        total = acc[:, 128:256]
        out = acc[:, 0:128] / total
        o_ref[0, w * BLK:(w + 1) * BLK, :] = join_heads(out).astype(jnp.bfloat16)
        lse = topb + jnp.log(total)
        for h in range(2):
            lse_ref[0, 0, w, h:h + 1, :] = lse[h * BLK:(h + 1) * BLK].T[0:1, :]

def dq_kernel(order_ref, own_ref, q_ref, do_ref, lse_ref, delta_ref, k_ref, v_ref, c_ref, a_ref, b_ref, dq_ref, ks, vs, acc, *, blocks):
    s = pl.program_id(0)
    sort_rows(order_ref, s, k_ref, ks, blocks)
    sort_rows(order_ref, s, v_ref, vs, blocks)
    for w in range(2):
        pos = own_ref[s, w]
        last = pos // CB
        qs = split_heads(q_ref[0, w * BLK:(w + 1) * BLK, :] * jnp.bfloat16(SCALE))
        dos = split_heads(do_ref[0, w * BLK:(w + 1) * BLK, :])
        cols = []
        for ref in (lse_ref, delta_ref):
            both = [jnp.broadcast_to(ref[0, 0, w, h:h + 1, :], (BLK, 128)).T for h in range(2)]
            cols.append(jnp.concatenate([jnp.concatenate(both, axis=0)] * CB, axis=1))
        lse, delta = cols
        acc[...] = jnp.zeros_like(acc)

        def step(c, mask):
            at = pl.multiple_of(c * CH, CH)
            kc = ks[pl.ds(at, CH), :]
            p = jnp.exp(nt(qs, kc) - lse)
            if mask is not None:
                p = jnp.where(mask, p, 0.0)
            dp = nt(dos, vs[pl.ds(at, CH), :])
            ds = (p * (dp - delta)).astype(jnp.bfloat16)
            acc[...] += nn(ds, kc)

        def body(c, carry):
            step(c, None)
            return carry

        lax.fori_loop(0, last, body, 0)
        qpos = pos * BLK + row_of((2 * BLK, CH)) % BLK
        kpos = last * CH + lane_of((2 * BLK, CH))
        step(last, kpos <= qpos)
        rows = slice(w * BLK, (w + 1) * BLK)
        grad = join_heads(acc[...]) * SCALE
        dq_ref[0, rows, :] = turn(grad, c_ref[rows], a_ref[rows], b_ref[rows], -1.0).astype(jnp.bfloat16)

def dkv_kernel(order_ref, own_ref, k_ref, v_ref, q_ref, do_ref, lse_ref, delta_ref, c_ref, a_ref, b_ref, dk_ref, dv_ref,
               qs, dos, lses, deltas, acck, accv, *, blocks):
    s = pl.program_id(0)
    sort_rows(order_ref, s, q_ref, qs, blocks)
    sort_rows(order_ref, s, do_ref, dos, blocks)
    for p in range(blocks):
        slot = order_ref[s, p]
        at = (p % CB) * BLK
        lses[p // CB, :, at:at + BLK] = lse_ref[slot // 2, 0, 0, slot % 2]
        deltas[p // CB, :, at:at + BLK] = delta_ref[slot // 2, 0, 0, slot % 2]
    for w in range(2):
        pos = own_ref[s, w]
        first = pos // CB
        kw = split_heads(k_ref[0, w * BLK:(w + 1) * BLK, :] * jnp.bfloat16(SCALE))
        vw = split_heads(v_ref[0, w * BLK:(w + 1) * BLK, :])
        acck[...] = jnp.zeros_like(acck)
        accv[...] = jnp.zeros_like(accv)

        def step(c, mask):
            at = pl.multiple_of(c * CH, CH)
            qc = qs[pl.ds(at, CH), :]
            doc = dos[pl.ds(at, CH), :]
            lse2, delta2 = lses[c], deltas[c]
            lse = jnp.concatenate([jnp.broadcast_to(lse2[h:h + 1], (BLK, CH)) for h in range(2)], axis=0)
            delta = jnp.concatenate([jnp.broadcast_to(delta2[h:h + 1], (BLK, CH)) for h in range(2)], axis=0)
            p = jnp.exp(nt(kw, qc) - lse)
            if mask is not None:
                p = jnp.where(mask, p, 0.0)
            accv[...] += nn(p.astype(jnp.bfloat16), doc)
            ds = (p * (nt(vw, doc) - delta)).astype(jnp.bfloat16)
            acck[...] += nn(ds, qc)

        def body(c, carry):
            step(c, None)
            return carry

        kpos = pos * BLK + row_of((2 * BLK, CH)) % BLK
        qpos = first * CH + lane_of((2 * BLK, CH))
        step(first, kpos <= qpos)
        lax.fori_loop(first + 1, blocks // CB, body, 0)
        rows = slice(w * BLK, (w + 1) * BLK)
        grad = join_heads(acck[...]) * SCALE
        dk_ref[0, rows, :] = turn(grad, c_ref[rows], a_ref[rows], b_ref[rows], -1.0).astype(jnp.bfloat16)
        dv_ref[0, rows, :] = join_heads(accv[...]).astype(jnp.bfloat16)

def specs(n_ctx):
    own = pl.BlockSpec((1, 2 * BLK, 128), lambda s, h, *_: (s, 0, h))
    whole = pl.BlockSpec((n_ctx, 1, 2, BLK, 128), lambda s, h, *_: (0, s, 0, 0, h))
    row = pl.BlockSpec((1, 1, 2, 2, BLK), lambda s, h, *_: (s, h, 0, 0, 0))
    rows = pl.BlockSpec((n_ctx, 1, 1, 2, 2, BLK), lambda s, h, *_: (0, s, h, 0, 0, 0))
    table = pl.BlockSpec((2 * BLK, 128), lambda s, h, *_: (s, 0))
    return own, whole, row, rows, table

def cost(seqs, pairs, blocks, mats, n_bytes):
    work = seqs * pairs * 2 * 2 * BLK * blocks * BLK // 2
    return pl.CostEstimate(flops=work * 128 * 2 * mats, bytes_accessed=n_bytes, transcendentals=work)

def attend(order, own_order, q, k_all, v_all):
    n_ctx, seqs = k_all.shape[:2]
    pairs = q.shape[2] // 128
    blocks = 2 * n_ctx
    own, whole, row, rows, table = specs(n_ctx)
    return pl.pallas_call(
        functools.partial(fwd_kernel, blocks=blocks),
        grid_spec=pltpu.PrefetchScalarGridSpec(
            num_scalar_prefetch=2, grid=(seqs, pairs),
            in_specs=[own, whole, whole], out_specs=[own, row],
            scratch_shapes=[pltpu.VMEM((blocks * BLK, 128), jnp.bfloat16), pltpu.VMEM((blocks * BLK, 256), jnp.bfloat16),
                            pltpu.VMEM((blocks // CB, 2 * BLK, CH), jnp.float32), pltpu.VMEM((2 * BLK, 256), jnp.float32)]),
        out_shape=[jax.ShapeDtypeStruct(q.shape, jnp.bfloat16), jax.ShapeDtypeStruct((seqs, pairs, 2, 2, BLK), jnp.float32)],
        compiler_params=pltpu.CompilerParams(vmem_limit_bytes=40 * 2**20),
        cost_estimate=cost(seqs, pairs, blocks, 2, 4 * k_all.size),
        name="attend",
    )(order, own_order, q, k_all, v_all)

def query_grad(order, own_order, q, do, lse, delta, k_all, v_all, tabs):
    n_ctx, seqs = k_all.shape[:2]
    pairs = q.shape[2] // 128
    blocks = 2 * n_ctx
    own, whole, row, rows, table = specs(n_ctx)
    return pl.pallas_call(
        functools.partial(dq_kernel, blocks=blocks),
        grid_spec=pltpu.PrefetchScalarGridSpec(
            num_scalar_prefetch=2, grid=(seqs, pairs),
            in_specs=[own, own, row, row, whole, whole, table, table, table], out_specs=own,
            scratch_shapes=[pltpu.VMEM((blocks * BLK, 128), jnp.bfloat16), pltpu.VMEM((blocks * BLK, 128), jnp.bfloat16),
                            pltpu.VMEM((2 * BLK, 128), jnp.float32)]),
        out_shape=jax.ShapeDtypeStruct(q.shape, jnp.bfloat16),
        compiler_params=pltpu.CompilerParams(vmem_limit_bytes=40 * 2**20),
        cost_estimate=cost(seqs, pairs, blocks, 3, 4 * k_all.size),
        name="query_grad",
    )(order, own_order, q, do, lse, delta, k_all, v_all, *tabs)

def key_value_grad(order, own_order, k, v, q_all, do_all, lse_all, delta_all, tabs):
    n_ctx, seqs = q_all.shape[:2]
    pairs = k.shape[2] // 128
    blocks = 2 * n_ctx
    own, whole, row, rows, table = specs(n_ctx)
    return pl.pallas_call(
        functools.partial(dkv_kernel, blocks=blocks),
        grid_spec=pltpu.PrefetchScalarGridSpec(
            num_scalar_prefetch=2, grid=(seqs, pairs),
            in_specs=[own, own, whole, whole, rows, rows, table, table, table], out_specs=[own, own],
            scratch_shapes=[pltpu.VMEM((blocks * BLK, 128), jnp.bfloat16), pltpu.VMEM((blocks * BLK, 128), jnp.bfloat16),
                            pltpu.VMEM((blocks // CB, 2, CH), jnp.float32), pltpu.VMEM((blocks // CB, 2, CH), jnp.float32),
                            pltpu.VMEM((2 * BLK, 128), jnp.float32), pltpu.VMEM((2 * BLK, 128), jnp.float32)]),
        out_shape=[jax.ShapeDtypeStruct(k.shape, jnp.bfloat16)] * 2,
        compiler_params=pltpu.CompilerParams(vmem_limit_bytes=40 * 2**20),
        cost_estimate=cost(seqs, pairs, blocks, 4, 4 * q_all.size),
        name="key_value_grad",
    )(order, own_order, k, v, q_all, do_all, lse_all, delta_all, *tabs)


import math
from jax.sharding import PartitionSpec as P

HEAD_DIM = 64
ROT = 16
SEQS = 4
EPS = 1e-05
F32 = jnp.float32
BF16 = jnp.bfloat16


def rc(left, right):
    return lax.dot_general(left, right, (((0,), (0,)), ((), ())), preferred_element_type=F32)


def layer_stats(values, gain, shift):
    mean = jnp.mean(values, axis=-1, keepdims=True)
    centred = values - mean
    inverse = lax.rsqrt(jnp.mean(centred * centred, axis=-1, keepdims=True) + EPS)
    unit = centred * inverse
    return unit * gain + shift, unit, inverse


def layer_back(grad, unit, inverse, gain):
    scaled = grad * gain
    grad_in = inverse * (
        scaled
        - jnp.mean(scaled, axis=-1, keepdims=True)
        - unit * jnp.mean(scaled * unit, axis=-1, keepdims=True)
    )
    return grad_in, jnp.sum(grad * unit, axis=0), jnp.sum(grad, axis=0)


def rotary_tables(positions):
    half = ROT // 2
    freq = 10000.0 ** (-2.0 * jnp.arange(half, dtype=F32) / ROT)
    angles = positions.astype(F32)[:, None] * freq[None, :]
    cos, sin = jnp.cos(angles), jnp.sin(angles)
    rows = positions.shape[0]
    one, none = jnp.ones((rows, HEAD_DIM - ROT), F32), jnp.zeros((rows, HEAD_DIM - ROT), F32)
    zero = jnp.zeros_like(sin)
    ctab = jnp.concatenate([cos, cos, one] * 2, axis=1)
    above = jnp.concatenate([sin, zero, none] * 2, axis=1)
    below = jnp.concatenate([zero, sin, none] * 2, axis=1)
    return ctab, above, below


def turn(x, ctab, above, below, sign):
    up = pltpu.roll(x, 128 - ROT // 2, axis=1)
    down = pltpu.roll(x, ROT // 2, axis=1)
    return x * ctab + sign * (down * below - up * above)


def project_kernel(h_ref, wq_ref, wk_ref, wv_ref, bias_ref, c_ref, a_ref, b_ref, q_ref, kv_ref):
    h = h_ref[...]
    width = wq_ref.shape[1]
    tabs = c_ref[...], a_ref[...], b_ref[...]
    for at, (w_ref, out) in enumerate(((wq_ref, q_ref.at[0]), (wk_ref, kv_ref.at[0, 0]), (wv_ref, kv_ref.at[1, 0]))):
        lin = nn(h, w_ref[...]) + bias_ref[at:at + 1, :]
        for p in range(width // 128):
            part = lin[:, p * 128:(p + 1) * 128]
            if at < 2:
                part = turn(part, *tabs, 1.0)
            out[:, p * 128:(p + 1) * 128] = part.astype(BF16)


def project(rows, wq, wk, wv, bias, tabs):
    total, depth = rows.shape
    width = wq.shape[1]
    step = total // SEQS
    weight = pl.BlockSpec((depth, width), lambda i: (0, 0))
    table = pl.BlockSpec((step, 128), lambda i: (i, 0))
    return pl.pallas_call(
        project_kernel,
        grid=(SEQS,),
        in_specs=[pl.BlockSpec((step, depth), lambda i: (i, 0)), weight, weight, weight,
                  pl.BlockSpec((3, width), lambda i: (0, 0)), table, table, table],
        out_specs=[pl.BlockSpec((1, step, width), lambda i: (i, 0, 0)),
                   pl.BlockSpec((2, 1, step, width), lambda i: (0, i, 0, 0))],
        out_shape=[jax.ShapeDtypeStruct((SEQS, step, width), BF16), jax.ShapeDtypeStruct((2, SEQS, step, width), BF16)],
        compiler_params=pltpu.CompilerParams(vmem_limit_bytes=48 * 2**20),
        cost_estimate=pl.CostEstimate(flops=6 * total * depth * width, bytes_accessed=6 * depth * width, transcendentals=0),
        name="project",
    )(rows, wq, wk, wv, bias, *tabs)


def ctx_swap(x, mask):
    n = lax.axis_size("ctx")
    return lax.ppermute(x, "ctx", [(i, i ^ mask) for i in range(n)])


def add16(a, b):
    return (a.astype(F32) + b.astype(F32)).astype(BF16)


def reduce_step(x, bit):
    mine = (lax.axis_index("ctx") >> bit) & 1
    r = x.shape[0] // 2
    keep = lax.dynamic_slice_in_dim(x, mine * r, r, 0)
    send = lax.dynamic_slice_in_dim(x, (1 - mine) * r, r, 0)
    return add16(keep, ctx_swap(send, 1 << bit))


def gather_step(x, bit):
    mine = (lax.axis_index("ctx") >> bit) & 1
    other = ctx_swap(x, 1 << bit)
    return jnp.where(mine == 0, jnp.concatenate([x, other]), jnp.concatenate([other, x]))


def sum_over_ctx(half):
    bits = list(range(1, int(math.log2(lax.axis_size("ctx")))))
    orders = [bits, bits[::-1]]
    r = half.shape[0] // 2
    streams = [half[:r], half[r:]]
    for i in range(len(bits)):
        streams = [reduce_step(x, order[i]) for x, order in zip(streams, orders)]
    for i in reversed(range(len(bits))):
        streams = [gather_step(x, order[i]) for x, order in zip(streams, orders)]
    return jnp.concatenate(streams)


def weight_grad(left, right, split_left):
    core = lax.axis_index("ctx") & 1
    split = left if split_left else right
    w = split.shape[1] // 2

    def part(which):
        cut = lax.dynamic_slice_in_dim(split, which * w, w, 1)
        return rc(cut, right) if split_left else rc(left, cut)

    got = ctx_swap(part(1 - core).astype(BF16), 1)
    half = sum_over_ctx((part(core) + got.astype(F32)).astype(BF16))
    other = ctx_swap(half, 1)
    axis = 0 if split_left else 1
    return jnp.where(core == 0, jnp.concatenate([half, other], axis=axis), jnp.concatenate([other, half], axis=axis)).astype(F32)


def all_rows(x):
    return lax.all_gather(x, "tp", axis=0, tiled=True)


def sum_rows(x):
    return lax.psum_scatter(x, "tp", scatter_dimension=0, tiled=True).astype(F32)


def local(tokens, cotangent, block_order, gain_one, shift_one, query_w, key_w, value_w, query_b, key_b, value_b,
          output_w, gain_two, shift_two, gate_w, up_w, down_w):
    heads = key_b.shape[0]
    width = heads * HEAD_DIM
    n_ctx = lax.axis_size("ctx")
    ctx = lax.axis_index("ctx")
    blocks = 2 * n_ctx
    own_order = lax.dynamic_slice_in_dim(block_order, 2 * ctx, 2, 1)
    slots = jnp.arange(blocks, dtype=jnp.int32)
    order = jnp.sum(jnp.where(block_order[:, :, None] == slots[None, None, :], slots[None, :, None], 0), axis=1).astype(jnp.int32)
    positions = (own_order[:, :, None] * BLK + jnp.arange(BLK, dtype=jnp.int32)).reshape(-1)
    tabs = rotary_tables(positions)

    x = tokens.astype(F32)
    normed_one, unit_one, inverse_one = layer_stats(x, gain_one, shift_one)
    rows_one = all_rows(normed_one.astype(BF16))
    dy_rows = all_rows(cotangent)
    key_bias = jnp.concatenate([key_b, jnp.zeros((heads, HEAD_DIM - ROT), F32)], axis=1).reshape(-1)
    bias = jnp.stack([query_b, key_bias, value_b])
    q, kv = project(rows_one, query_w, key_w, value_w, bias, tabs)
    shape = (SEQS, 2, BLK, width)
    kv_all = lax.all_gather(kv.reshape((2,) + shape), "ctx", axis=0)
    k_all, v_all = kv_all[:, 0], kv_all[:, 1]
    attn, lse = attend(order, own_order, q, k_all, v_all)
    q_all = lax.all_gather(q.reshape(shape), "ctx", axis=0)
    lse_all = lax.all_gather(lse, "ctx", axis=0)
    attn_rows = attn.reshape(-1, width)
    mixed = x + sum_rows(nn(attn_rows, output_w).astype(BF16))
    normed_two, unit_two, inverse_two = layer_stats(mixed, gain_two, shift_two)
    rows_two = all_rows(normed_two.astype(BF16))
    gate = nn(rows_two, gate_w)
    up = nn(rows_two, up_w)
    sig = jax.nn.sigmoid(gate)
    silu = gate * sig
    act = (silu * up).astype(BF16)
    grad_act = nt(dy_rows, down_w)
    grad_gate = (grad_act * up * sig * (1.0 + gate * (1.0 - sig))).astype(BF16)
    grad_up = (grad_act * silu).astype(BF16)
    grad_two = sum_rows((nt(grad_gate, gate_w) + nt(grad_up, up_w)).astype(BF16))
    out_tokens = (mixed + sum_rows(nn(act, down_w).astype(BF16))).astype(BF16)
    grad_down_w = weight_grad(act, dy_rows, False)
    grad_gate_w = weight_grad(rows_two, grad_gate, True)
    grad_up_w = weight_grad(rows_two, grad_up, True)

    norm_two, grad_gain_two, grad_shift_two = layer_back(grad_two, unit_two, inverse_two, gain_two)
    grad_mixed = cotangent.astype(F32) + norm_two
    branch = all_rows(grad_mixed.astype(BF16))
    grad_attn = nt(branch, output_w).astype(BF16)
    ind = (jnp.arange(heads)[:, None] == (jnp.arange(width) // HEAD_DIM)[None, :]).astype(F32)
    delta = lax.dot_general(ind, grad_attn.astype(F32) * attn_rows.astype(F32), (((1,), (1,)), ((), ())),
                            precision=lax.Precision.HIGHEST, preferred_element_type=F32)
    delta = jnp.transpose(delta.reshape(heads // 2, 2, SEQS, 2, BLK), (2, 0, 3, 1, 4))
    do_all = lax.all_gather(grad_attn.reshape(shape), "ctx", axis=0)
    delta_all = lax.all_gather(delta, "ctx", axis=0)
    grad_output_w = weight_grad(attn_rows, branch, False)
    grad_q = query_grad(order, own_order, q, grad_attn.reshape(q.shape), lse, delta, k_all, v_all, tabs)
    grad_k, grad_v = key_value_grad(order, own_order, kv[0], kv[1], q_all, do_all, lse_all, delta_all, tabs)
    grad_q, grad_k, grad_v = (g.reshape(-1, width) for g in (grad_q, grad_k, grad_v))
    grad_one = sum_rows((nt(grad_q, query_w) + nt(grad_k, key_w) + nt(grad_v, value_w)).astype(BF16))
    grad_qkv = jnp.concatenate([grad_q, grad_k, grad_v], axis=1)
    grad_qkv_w = weight_grad(rows_one, grad_qkv, True)
    bias_sum = lax.psum(jnp.sum(grad_qkv.astype(F32), axis=0), "ctx")
    norm_one, grad_gain_one, grad_shift_one = layer_back(grad_one, unit_one, inverse_one, gain_one)
    grad_tokens = (grad_mixed + norm_one).astype(BF16)
    norms = lax.psum((grad_gain_one, grad_shift_one, grad_gain_two, grad_shift_two), ("ctx", "tp"))
    return (
        out_tokens, grad_tokens, norms[0], norms[1],
        grad_qkv_w[:, :width], grad_qkv_w[:, width:2 * width], grad_qkv_w[:, 2 * width:],
        bias_sum[:width], bias_sum[width:2 * width].reshape(heads, HEAD_DIM)[:, :ROT], bias_sum[2 * width:],
        grad_output_w, norms[2], norms[3], grad_gate_w, grad_up_w, grad_down_w,
    )


def solution(mesh):
    rows, cols, depth, flat = P(("ctx", "tp"), None), P(None, "tp"), P("tp", None), P("tp")
    in_specs = (rows, rows, P(), P(), P(), cols, cols, cols, flat, depth, flat, depth, P(), P(), cols, cols, depth)
    out_specs = (rows, rows, P(), P(), cols, cols, cols, flat, depth, flat, depth, P(), P(), cols, cols, depth)
    return jax.shard_map(local, mesh=mesh, in_specs=in_specs, out_specs=out_specs, check_vma=False)
```

time: 1600 us -> 1350 us (0.84)
  waiting for transfers between devices: 1010 us -> 737 us
  Pallas kernels: 0 us -> 168 us
  matrix products: 314 us -> 153 us
  local copies, waits for them, and re-layouts: 95.6 us -> 58 us
  starting transfers between devices: 1.11 us -> 33.8 us
    psum x1 -> x0, waiting for transfers between devices: 319 us -> none  [local(): lax.psum(grad_query_w.astype(jnp.bfloat16), 'ctx').astype(jnp.float32)]
    ppermute x0 -> x50, waiting for transfers between devices: none -> 171 us  [ctx_swap(): return lax.ppermute(x, 'ctx', [(i, i ^ mask) for i in range(n)])]
    pallas_call x0 -> x4, Pallas kernels: none -> 168 us  [the longest x1 59.4 us: key_value_grad(): pl.pallas_call(functools.partial(dkv_kernel, blocks=blocks), grid_spec=pl...]
    dot_general x77 -> x22, matrix products: 314 us -> 153 us  [the longest x7 63.4 us: nt(): lax.dot_general(a, b, (((1,), (1,)), ((), ())), preferred_element_type=jn...]
    reduce_scatter x6 -> x4, waiting for transfers between devices: 318 us -> 165 us  [sum_rows(): lax.psum_scatter(x, 'tp', scatter_dimension=0, tiled=True).astype(F32)]
    ppermute x0 -> x50, starting transfers between devices: none -> 32.9 us  [ctx_swap(): return lax.ppermute(x, 'ctx', [(i, i ^ mask) for i in range(n)])]
    all_gather x6 -> x7, waiting for transfers between devices: 373 us -> 400 us  [the longest x4 289 us: all_rows(): return lax.all_gather(x, 'tp', axis=0, tiled=True)]
    convert_element_type x17 -> x30, other arithmetic: 46.5 us -> 71.7 us  [the longest x5 57.7 us: weight_grad(): jnp.where(core == 0, jnp.concatenate([half, other], axis=axis), jnp.conca...]
  transfers between devices with their start and end apart: 13 -> 61, of which waited for: 13 -> 32; matrix products, arithmetic and copies ran while one was open for 9% -> 14% of each run, Pallas kernels for 0% -> 4%
where the time goes in v1:
time: 1350 us; the launch traced here: 1340 us
  waiting for transfers between devices  737 us (55%)
  Pallas kernels  168 us (12%)
  matrix products  153 us (11%)
  other arithmetic  98.7 us (7%)
  blocking collectives  73.1 us (5%)
  local copies, waits for them, and re-layouts  58 us (4%)
  starting transfers between devices  33.8 us (3%)
  between operations  15.7 us (1%)
    all_gather x4, waiting for transfers between devices, all_rows(): return lax.all_gather(x, 'tp', axis=0, tiled=True)  289 us
    ppermute x50, waiting for transfers between devices, ctx_swap(): return lax.ppermute(x, 'ctx', [(i, i ^ mask) for i in range(n)])  171 us
    reduce_scatter x4, waiting for transfers between devices, sum_rows(): lax.psum_scatter(x, 'tp', scatter_dimension=0, tiled=True).astype(F32)  165 us
    all_gather x1, waiting for transfers between devices, local(): kv_all = lax.all_gather(kv.reshape((2,) + shape), 'ctx', axis=0)  88.4 us
    dot_general x7, matrix products, nt(): lax.dot_general(a, b, (((1,), (1,)), ((), ())), preferred_element_type=jn...  63.4 us
    pallas_call x1, Pallas kernels, key_value_grad(): pl.pallas_call(functools.partial(dkv_kernel, blocks=blocks), grid_spec=pl...  59.4 us
    convert_element_type x5, other arithmetic, weight_grad(): jnp.where(core == 0, jnp.concatenate([half, other], axis=axis), jnp.conca...  57.7 us
    dot_general x10, matrix products, rc(): lax.dot_general(left, right, (((0,), (0,)), ((), ())), preferred_element_...  53.3 us
  transfers between devices with their start and end apart: 61, of which 32 were waited for; matrix products, arithmetic and copies ran while one was open for 14% of the time, Pallas kernels for 4%

profile of v1, /device:TPU:0, one launch (start us, length us, event | category | flops | bytes accessed | tf_op | source)
XLA Modules:
  0.0 1336.7 jit_solution(17079162075872455093)
XLA Ops:
  24.3 3.6 concatenate.187.c_ref
  28.0 69.4 %all-gather.10.cloned.1.call-done.h_ref = bf16[1024,2048]{1,0:T(8,128)(2,1)} async-done(((bf16[256,2048]{1,0:T(8,128)(2,1)}), bf16[1024,2048]{1,0:T(8,128)(2,1)}) %all-gather.10.cloned.1.call-update) | async-done | bytes 4194320 | tf_op jit(solution)/shard_map/all_gather | solution.py:378
  98.4 10.6 project.1
  110.5 88.4 %all-gather.12.cloned.1.call-done = bf16[8,2,4,2,128,512]{5,4,3,2,0,1:T(8,128)(2,1)} async-done(((bf16[1,2,4,2,128,512]{5,4,3,2,0,1:T(8,128)(2,1)}), bf16[8,2,4,2,128,512]{5,4,3,2,0,1:T(8,128)(2,1)}) %all-gather.12.cloned.1.call-update) | async-done | bytes 16777232 | tf_op jit(solution)/shard_map/all_gather | solution.py:406
  198.9 9.4 slice_bitcast_fusion
  208.4 49.9 %attend.1 = (bf16[4,256,512]{2,1,0:T(8,128)(2,1)S(1)}, f32[4,4,2,2,128]{4,3,2,1,0:T(2,128)S(1)}) custom-call(s32[4,16]{1,0:T(4,128)S(1)} %select_reduce_fusion.order_ref, s32[4,2]{1,0:T(4,128)S(1)} %get-tuple-element.41.own_ref, bf16[4,256,512]{2,1,0:T(8,128)(2,1)} %get-tuple-element.22.q_ref, bf16[8,4,2,128,512]{4,3,2,1,0:T(8,128)(2,1)S(1)} %get-tuple-element.43.k_ref, ...), custom_call_target="tpu_custom_call" | custom-call | flops 4294967296 | bytes 16777216 | tf_op jit(solution)/shard_map/attend/pallas_call | solution.py:189
  259.3 4.4 convolution_convert_fusion.1
  263.7 89.2 %reduce-scatter.5.cloned.1.call-done = bf16[256,2048]{1,0:T(8,128)(2,1)} async-done(((bf16[1024,2048]{1,0:T(8,128)(2,1)}), bf16[256,2048]{1,0:T(8,128)(2,1)}) %reduce-scatter.5.cloned.1.call-update) | async-done | bytes 1048592 | tf_op jit(solution)/shard_map/reduce_scatter | solution.py:382
  359.0 80.3 %all-gather.14.cloned.1.call-done = bf16[1024,2048]{1,0:T(8,128)(2,1)} async-done(((bf16[256,2048]{1,0:T(8,128)(2,1)}), bf16[1024,2048]{1,0:T(8,128)(2,1)}) %all-gather.14.cloned.1.call-update) | async-done | bytes 4194320 | tf_op jit(solution)/shard_map/all_gather | solution.py:378
  439.4 11.8 fusion.86
  451.2 10.3 fusion.87
  461.5 58.7 %all-gather.16.cloned.1.call-done = bf16[1024,2048]{1,0:T(8,128)(2,1)} async-done(((bf16[256,2048]{1,0:T(8,128)(2,1)}), bf16[1024,2048]{1,0:T(8,128)(2,1)}) %all-gather.16.cloned.1.call-update) | async-done | bytes 4194320 | tf_op jit(solution)/shard_map/all_gather | solution.py:378
  520.2 15.6 %multiply_convert_fusion = (bf16[1024,1408]{1,0:T(8,128)(2,1)S(1)}, bf16[1024,1408]{1,0:T(8,128)(2,1)S(1)}, bf16[1024,1408]{1,0:T(8,128)(2,1)}) fusion(f32[1024,1408]{1,0:T(8,128)} %fusion.86, f32[1024,1408]{1,0:T(8,128)} %fusion.87, bf16[1024,2048]{1,0:T(8,128)(2,1)} %all-gather.16.cloned.1.call-done, bf16[1408,2048]{1,0:T(8,128)(2,1)} %param.33), kind=kOutput, calls=%fused_computation.17 | convolution fusion | flops 5927206912 | bytes 30146560 | tf_op jit(solution)/shard_map/dot_general | solution.py:14
  535.7 10.8 fusion.88
  546.6 11.2 add_convert_fusion.1
  557.8 75.4 %reduce-scatter.9.cloned.1.call-done = bf16[256,2048]{1,0:T(8,128)(2,1)} async-done(((bf16[1024,2048]{1,0:T(8,128)(2,1)}), bf16[256,2048]{1,0:T(8,128)(2,1)}) %reduce-scatter.9.cloned.1.call-update) | async-done | bytes 1048592 | tf_op jit(solution)/shard_map/reduce_scatter | solution.py:382
  633.2 3.4 fusion.27
  639.7 80.6 %all-gather.18.cloned.1.call-done = bf16[1024,2048]{1,0:T(8,128)(2,1)} async-done(((bf16[256,2048]{1,0:T(8,128)(2,1)}), bf16[1024,2048]{1,0:T(8,128)(2,1)}) %all-gather.18.cloned.1.call-update) | async-done | bytes 4194320 | tf_op jit(solution)/shard_map/all_gather | solution.py:378
  720.3 5.5 convolution_convert_fusion.6
  729.0 10.3 all-gather
  740.8 9.3 all-gather.1
  750.9 3.5 copy-done.3
  757.6 47.7 %query_grad.1 = bf16[4,256,512]{2,1,0:T(8,128)(2,1)S(1)} custom-call(s32[4,16]{1,0:T(4,128)S(1)} %select_reduce_fusion.order_ref, s32[4,2]{1,0:T(4,128)S(1)} %get-tuple-element.41.own_ref, bf16[4,256,512]{2,1,0:T(8,128)(2,1)} %get-tuple-element.22.q_ref, bf16[4,256,512]{2,1,0:T(8,128)(2,1)S(1)} %bitcast.62, ...), custom_call_target="tpu_custom_call" | custom-call | flops 6442450944 | bytes 16777216 | tf_op jit(solution)/shard_map/query_grad/pallas_call | solution.py:207
  805.3 5.8 fusion.89
  811.0 22.8 %all-gather.22.cloned.1.call-done.do_ref = bf16[8,4,2,128,512]{4,3,2,1,0:T(8,128)(2,1)} async-done(((bf16[1,4,2,128,512]{4,3,2,1,0:T(8,128)(2,1)}), bf16[8,4,2,128,512]{4,3,2,1,0:T(8,128)(2,1)}) %all-gather.22.cloned.1.call-update) | async-done | bytes 8388624 | tf_op jit(solution)/shard_map/all_gather | solution.py:437
  839.2 59.4 %key_value_grad.1 = (bf16[4,256,512]{2,1,0:T(8,128)(2,1)S(1)}, bf16[4,256,512]{2,1,0:T(8,128)(2,1)S(1)}) custom-call(s32[4,16]{1,0:T(4,128)S(1)} %select_reduce_fusion.order_ref, s32[4,2]{1,0:T(4,128)S(1)} %get-tuple-element.41.own_ref, bf16[4,256,512]{2,1,0:T(8,128)(2,1)S(1)} %copy-done.14, bf16[4,256,512]{2,1,0:T(8,128)(2,1)S(1)} %copy-done.13, ...), custom_call_target="tpu_custom_call" | custom-call | flops 8589934592 | bytes 16777216 | tf_op jit(solution)/shard_map/key_value_grad/pallas_call | solution.py:225
  898.7 6.3 fusion.90
  905.4 8.2 add_convert_fusion
  913.7 7.7 convolution_convert_fusion.4
  921.4 5.3 convolution_convert_fusion.3
  927.2 8.2 convolution_convert_fusion
  935.4 7.2 convolution_convert_fusion.2
  942.7 6.9 add_convert_fusion.5
  949.9 5.9 collective-permute-start.25
  955.9 5.4 add_convert_fusion.4
  964.5 4.9 add_convert_fusion.3
  975.3 12.9 collective-permute-done.35
  990.7 12.9 collective-permute-done.45
  1006.3 7.2 collective-permute-done.26
  1013.8 7.4 collective-permute-done.36
  1021.5 7.4 collective-permute-done.46
  1029.3 7.3 collective-permute-done.27
  1039.1 5.3 collective-permute-done.37
  1044.8 7.3 collective-permute-done.47
  1052.8 12.7 collective-permute-done.28
  1069.9 11.0 collective-permute-done.38
  1087.5 7.1 convolution_convert_fusion.5
  1102.8 7.5 fusion.1
  1112.6 6.9 collective-permute-done.11
  1119.6 6.3 add_convert_fusion.2
  1128.6 18.7 %collective-permute-done.12 = bf16[64,1024]{1,0:T(8,128)(2,1)S(1)} collective-permute-done((bf16[64,1024]{1,0:T(8,128)(2,1)S(1)}, bf16[64,1024]{1,0:T(8,128)(2,1)S(1)}, u32[]{:S(2)}, u32[]{:S(2)}) %collective-permute-start.12) | collective-permute-done | bytes 131104 | tf_op jit(solution)/shard_map/ppermute | solution.py:328
  1148.5 16.3 %collective-permute-done.1 = bf16[256,1536]{1,0:T(8,128)(2,1)S(1)} collective-permute-done((bf16[256,1536]{1,0:T(8,128)(2,1)S(1)}, bf16[256,1536]{1,0:T(8,128)(2,1)S(1)}, u32[]{:S(2)}, u32[]{:S(2)}) %collective-permute-start.1) | collective-permute-done | bytes 786464 | tf_op jit(solution)/shard_map/ppermute | solution.py:328
  1166.0 6.9 collective-permute-done.6
  1173.0 8.3 collective-permute-done.2
  1186.2 7.5 collective-permute-done.7
  1196.3 7.9 fusion.2
  1204.6 7.0 collective-permute-done.8
  1215.0 24.4 %fusion.3 = f32[1408,2048]{1,0:T(8,128)} fusion(bf16[1408,1024]{1,0:T(8,128)(2,1)S(1)} %collective-permute-done.49, bf16[704,1024]{1,0:T(8,128)(2,1)S(1)} %maximum_select_fusion.12, bf16[704,1024]{1,0:T(8,128)(2,1)S(1)} %maximum_select_fusion.11, pred[]{:T(512)S(6)} %eq.24), kind=kLoop, calls=%fused_computation.13 | loop fusion | flops 40370176 | bytes 17301504 | tf_op jit(solution)/shard_map/convert_element_type | solution.py:374
  1239.4 9.7 fusion.29
  1249.8 13.1 psum.37
  1266.5 40.4 %all-reduce.1 = (f32[2048]{0:T(1024)}, f32[2048]{0:T(1024)}, f32[2048]{0:T(1024)}, f32[2048]{0:T(1024)}) all-reduce(f32[2048]{0:T(1024)S(1)} %get-tuple-element.30, f32[2048]{0:T(1024)S(1)} %get-tuple-element.35, f32[2048]{0:T(1024)S(1)} %copy-done.47, f32[2048]{0:T(1024)S(1)} %copy-done.48), channel_id=1, replica_groups=mesh['ctx'=8,'tp'=4] {'ctx','tp'}, use_global_device_ids=true, to_apply=%region_14.15 | all-reduce | flops 8192 | bytes 65536 | tf_op jit(solution)/shard_map/psum | solution.py:449
  1307.0 4.9 fusion.20
  1311.9 8.1 fusion
  1320.0 9.9 fusion.79
  (375 shorter events, 105.3 us)
Async XLA Ops:
  7.2 252.1 %copy-start = (bf16[512,2048]{1,0:T(8,128)(2,1)S(1)}, bf16[512,2048]{1,0:T(8,128)(2,1)}, u32[]{:S(2)}) copy-start(bf16[512,2048]{1,0:T(8,128)(2,1)} %param.28) | copy-start | bytes 6291460
  7.2 90.2 %all-gather.10.cloned.1.call-start = ((), (), s32[]{:S(2)}) async-start(), calls=%async_computation.4 | async-start | bytes 5242880 | tf_op jit(solution)/shard_map/all_gather | solution.py:378
  13.8 185.2 %all-gather.12.cloned.1.call-start = ((), (), s32[]{:S(2)}) async-start(), calls=%async_computation.5 | async-start | bytes 18874368 | tf_op jit(solution)/shard_map/all_gather | solution.py:406
  110.4 242.5 %reduce-scatter.5.cloned.1.call-start = ((), (), s32[]{:S(2)}) async-start(), calls=%async_computation.6 | async-start | bytes 5242880 | tf_op jit(solution)/shard_map/reduce_scatter | solution.py:382
  263.7 175.7 %all-gather.14.cloned.1.call-start = ((), (), s32[]{:S(2)}) async-start(), calls=%async_computation.7 | async-start | bytes 5242880 | tf_op jit(solution)/shard_map/all_gather | solution.py:378
  354.6 282.1 %copy-start.45 = (f32[256]{0:T(256)}, f32[256]{0:T(256)S(1)}, u32[]{:S(2)}) copy-start(f32[256]{0:T(256)S(1)} %broadcast_multiply_fusion.5) | copy-start | bytes 3076
  356.3 280.3 %copy-start.51 = (f32[256]{0:T(256)}, f32[256]{0:T(256)S(1)}, u32[]{:S(2)}) copy-start(f32[256]{0:T(256)S(1)} %add_rsqrt_fusion) | copy-start | bytes 3076
  357.9 162.3 %all-gather.16.cloned.1.call-start = ((), (), s32[]{:S(2)}) async-start(), calls=%async_computation.9 | async-start | bytes 5242880 | tf_op jit(solution)/shard_map/all_gather | solution.py:378
  358.5 274.7 %reduce-scatter.9.cloned.1.call-start = ((), (), s32[]{:S(2)}) async-start(), calls=%async_computation.10 | async-start | bytes 5242880 | tf_op jit(solution)/shard_map/reduce_scatter | solution.py:382
  557.8 162.5 %all-gather.18.cloned.1.call-start = ((), (), s32[]{:S(2)}) async-start(), calls=%async_computation.11 | async-start | bytes 5242880 | tf_op jit(solution)/shard_map/all_gather | solution.py:378
  638.9 172.1 %all-gather.20.cloned.1.call-start = ((), (), s32[]{:S(2)}) async-start(), calls=%async_computation.12 | async-start | bytes 9437184 | tf_op jit(solution)/shard_map/all_gather | solution.py:409
  639.7 194.2 %all-gather.22.cloned.1.call-start = ((), (), s32[]{:S(2)}) async-start(), calls=%async_computation.13 | async-start | bytes 9437184 | tf_op jit(solution)/shard_map/all_gather | solution.py:437
  725.8 538.3 %reduce-scatter.11.cloned.1.call-start = ((), (), s32[]{:S(2)}) async-start(), calls=%async_computation.14 | async-start | bytes 5242880 | tf_op jit(solution)/shard_map/reduce_scatter | solution.py:382
  913.6 393.3 %reduce-scatter.7.cloned.1.call-start = ((), (), s32[]{:S(2)}) async-start(), calls=%async_computation.8 | async-start | bytes 5242880 | tf_op jit(solution)/shard_map/reduce_scatter | solution.py:382
  921.4 21.3 %collective-permute-start.20 = (bf16[1024,1408]{1,0:T(8,128)(2,1)}, bf16[1024,1408]{1,0:T(8,128)(2,1)}, u32[]{:S(2)}, u32[]{:S(2)}) collective-permute-start(bf16[1024,1408]{1,0:T(8,128)(2,1)} %convolution_convert_fusion.4), channel_id=1, source_target_pairs={{0,4},{4,0},{8,12},{12,8},{16,20},{20,16},{24,28},{28,24},{1,5},{5... | collective-permute-start | bytes 8650760 | tf_op jit(solution)/shard_map/ppermute | solution.py:328
  926.7 29.2 %collective-permute-start.30 = (bf16[1024,1408]{1,0:T(8,128)(2,1)}, bf16[1024,1408]{1,0:T(8,128)(2,1)}, u32[]{:S(2)}, u32[]{:S(2)}) collective-permute-start(bf16[1024,1408]{1,0:T(8,128)(2,1)} %convolution_convert_fusion.3), channel_id=1, source_target_pairs={{0,4},{4,0},{8,12},{12,8},{16,20},{20,16},{24,28},{28,24},{1,5},{5... | collective-permute-start | bytes 8650760 | tf_op jit(solution)/shard_map/ppermute | solution.py:328
  942.6 21.8 %collective-permute-start.40 = (bf16[1408,1024]{1,0:T(8,128)(2,1)}, bf16[1408,1024]{1,0:T(8,128)(2,1)}, u32[]{:S(2)}, u32[]{:S(2)}) collective-permute-start(bf16[1408,1024]{1,0:T(8,128)(2,1)} %convolution_convert_fusion.2), channel_id=1, source_target_pairs={{0,4},{4,0},{8,12},{12,8},{16,20},{20,16},{24,28},{28,24},{1,5},{5... | collective-permute-start | bytes 8650760 | tf_op jit(solution)/shard_map/ppermute | solution.py:328
  949.9 22.9 %collective-permute-start.25 = (bf16[256,1408]{1,0:T(8,128)(2,1)S(1)}, bf16[256,1408]{1,0:T(8,128)(2,1)S(1)}, u32[]{:S(2)}, u32[]{:S(2)}) collective-permute-start(bf16[256,1408]{1,0:T(8,128)(2,1)S(1)} %constant_dynamic-slice_fusion.9), channel_id=1, source_target_pairs={{0,16},{4,20},{8,24},{12,28},{16,0},{20,4},{24,8},{28,12},{1,17},{... | collective-permute-start | bytes 2162696 | tf_op jit(solution)/shard_map/ppermute | solution.py:328
  955.8 19.0 %collective-permute-start.21 = (bf16[256,1408]{1,0:T(8,128)(2,1)S(1)}, bf16[256,1408]{1,0:T(8,128)(2,1)S(1)}, u32[]{:S(2)}, u32[]{:S(2)}) collective-permute-start(bf16[256,1408]{1,0:T(8,128)(2,1)S(1)} %constant_dynamic-slice_fusion.11), channel_id=1, source_target_pairs={{0,8},{4,12},{8,0},{12,4},{16,24},{20,28},{24,16},{28,20},{1,9},{5... | collective-permute-start | bytes 2162696 | tf_op jit(solution)/shard_map/ppermute | solution.py:328
  961.6 26.6 %collective-permute-start.35 = (bf16[256,1408]{1,0:T(8,128)(2,1)S(1)}, bf16[256,1408]{1,0:T(8,128)(2,1)S(1)}, u32[]{:S(2)}, u32[]{:S(2)}) collective-permute-start(bf16[256,1408]{1,0:T(8,128)(2,1)S(1)} %constant_dynamic-slice_fusion.5), channel_id=1, source_target_pairs={{0,16},{4,20},{8,24},{12,28},{16,0},{20,4},{24,8},{28,12},{1,17},{... | collective-permute-start | bytes 2162696 | tf_op jit(solution)/shard_map/ppermute | solution.py:328
  964.3 26.1 %collective-permute-start.31 = (bf16[256,1408]{1,0:T(8,128)(2,1)S(1)}, bf16[256,1408]{1,0:T(8,128)(2,1)S(1)}, u32[]{:S(2)}, u32[]{:S(2)}) collective-permute-start(bf16[256,1408]{1,0:T(8,128)(2,1)S(1)} %constant_dynamic-slice_fusion.7), channel_id=1, source_target_pairs={{0,8},{4,12},{8,0},{12,4},{16,24},{20,28},{24,16},{28,20},{1,9},{5... | collective-permute-start | bytes 2162696 | tf_op jit(solution)/shard_map/ppermute | solution.py:328
  969.7 34.0 %collective-permute-start.45 = (bf16[352,1024]{1,0:T(8,128)(2,1)S(1)}, bf16[352,1024]{1,0:T(8,128)(2,1)S(1)}, u32[]{:S(2)}, u32[]{:S(2)}) collective-permute-start(bf16[352,1024]{1,0:T(8,128)(2,1)S(1)} %constant_dynamic-slice_fusion.1), channel_id=1, source_target_pairs={{0,16},{4,20},{8,24},{12,28},{16,0},{20,4},{24,8},{28,12},{1,17},{... | collective-permute-start | bytes 2162696 | tf_op jit(solution)/shard_map/ppermute | solution.py:328
  972.8 33.2 %collective-permute-start.41 = (bf16[352,1024]{1,0:T(8,128)(2,1)S(1)}, bf16[352,1024]{1,0:T(8,128)(2,1)S(1)}, u32[]{:S(2)}, u32[]{:S(2)}) collective-permute-start(bf16[352,1024]{1,0:T(8,128)(2,1)S(1)} %constant_dynamic-slice_fusion.3), channel_id=1, source_target_pairs={{0,8},{4,12},{8,0},{12,4},{16,24},{20,28},{24,16},{28,20},{1,9},{5... | collective-permute-start | bytes 2162696 | tf_op jit(solution)/shard_map/ppermute | solution.py:328
  974.9 38.6 %collective-permute-start.26 = (bf16[128,1408]{1,0:T(8,128)(2,1)S(1)}, bf16[128,1408]{1,0:T(8,128)(2,1)S(1)}, u32[]{:S(2)}, u32[]{:S(2)}) collective-permute-start(bf16[128,1408]{1,0:T(8,128)(2,1)S(1)} %constant_dynamic-slice_fusion.8), channel_id=1, source_target_pairs={{0,8},{4,12},{8,0},{12,4},{16,24},{20,28},{24,16},{28,20},{1,9},{5... | collective-permute-start | bytes 1081352 | tf_op jit(solution)/shard_map/ppermute | solution.py:328
  988.2 25.4 %collective-permute-start.22 = (bf16[128,1408]{1,0:T(8,128)(2,1)S(1)}, bf16[128,1408]{1,0:T(8,128)(2,1)S(1)}, u32[]{:S(2)}, u32[]{:S(2)}) collective-permute-start(bf16[128,1408]{1,0:T(8,128)(2,1)S(1)} %constant_dynamic-slice_fusion.10), channel_id=1, source_target_pairs={{0,16},{4,20},{8,24},{12,28},{16,0},{20,4},{24,8},{28,12},{1,17},{... | collective-permute-start | bytes 1081352 | tf_op jit(solution)/shard_map/ppermute | solution.py:328
  990.4 30.8 %collective-permute-start.36 = (bf16[128,1408]{1,0:T(8,128)(2,1)S(1)}, bf16[128,1408]{1,0:T(8,128)(2,1)S(1)}, u32[]{:S(2)}, u32[]{:S(2)}) collective-permute-start(bf16[128,1408]{1,0:T(8,128)(2,1)S(1)} %constant_dynamic-slice_fusion.4), channel_id=1, source_target_pairs={{0,8},{4,12},{8,0},{12,4},{16,24},{20,28},{24,16},{28,20},{1,9},{5... | collective-permute-start | bytes 1081352 | tf_op jit(solution)/shard_map/ppermute | solution.py:328
  1003.7 17.7 %collective-permute-start.32 = (bf16[128,1408]{1,0:T(8,128)(2,1)S(1)}, bf16[128,1408]{1,0:T(8,128)(2,1)S(1)}, u32[]{:S(2)}, u32[]{:S(2)}) collective-permute-start(bf16[128,1408]{1,0:T(8,128)(2,1)S(1)} %constant_dynamic-slice_fusion.6), channel_id=1, source_target_pairs={{0,16},{4,20},{8,24},{12,28},{16,0},{20,4},{24,8},{28,12},{1,17},{... | collective-permute-start | bytes 1081352 | tf_op jit(solution)/shard_map/ppermute | solution.py:328
  1005.9 23.0 %collective-permute-start.46 = (bf16[176,1024]{1,0:T(8,128)(2,1)S(1)}, bf16[176,1024]{1,0:T(8,128)(2,1)S(1)}, u32[]{:S(2)}, u32[]{:S(2)}) collective-permute-start(bf16[176,1024]{1,0:T(8,128)(2,1)S(1)} %constant_dynamic-slice_fusion), channel_id=1, source_target_pairs={{0,8},{4,12},{8,0},{12,4},{16,24},{20,28},{24,16},{28,20},{1,9},{5... | collective-permute-start | bytes 1081352 | tf_op jit(solution)/shard_map/ppermute | solution.py:328
  1013.5 15.6 %collective-permute-start.42 = (bf16[176,1024]{1,0:T(8,128)(2,1)S(1)}, bf16[176,1024]{1,0:T(8,128)(2,1)S(1)}, u32[]{:S(2)}, u32[]{:S(2)}) collective-permute-start(bf16[176,1024]{1,0:T(8,128)(2,1)S(1)} %constant_dynamic-slice_fusion.2), channel_id=1, source_target_pairs={{0,16},{4,20},{8,24},{12,28},{16,0},{20,4},{24,8},{28,12},{1,17},{... | collective-permute-start | bytes 1081352 | tf_op jit(solution)/shard_map/ppermute | solution.py:328
  1013.6 23.1 %collective-permute-start.27 = (bf16[128,1408]{1,0:T(8,128)(2,1)S(1)}, bf16[128,1408]{1,0:T(8,128)(2,1)S(1)}, u32[]{:S(2)}, u32[]{:S(2)}) collective-permute-start(bf16[128,1408]{1,0:T(8,128)(2,1)S(1)} %add_convert_fusion.23), channel_id=1, source_target_pairs={{0,8},{4,12},{8,0},{12,4},{16,24},{20,28},{24,16},{28,20},{1,9},{5... | collective-permute-start | bytes 1081352 | tf_op jit(solution)/shard_map/ppermute | solution.py:328
  1021.2 15.6 %collective-permute-start.23 = (bf16[128,1408]{1,0:T(8,128)(2,1)S(1)}, bf16[128,1408]{1,0:T(8,128)(2,1)S(1)}, u32[]{:S(2)}, u32[]{:S(2)}) collective-permute-start(bf16[128,1408]{1,0:T(8,128)(2,1)S(1)} %add_convert_fusion.24), channel_id=1, source_target_pairs={{0,16},{4,20},{8,24},{12,28},{16,0},{20,4},{24,8},{28,12},{1,17},{... | collective-permute-start | bytes 1081352 | tf_op jit(solution)/shard_map/ppermute | solution.py:328
  1021.3 23.1 %collective-permute-start.37 = (bf16[128,1408]{1,0:T(8,128)(2,1)S(1)}, bf16[128,1408]{1,0:T(8,128)(2,1)S(1)}, u32[]{:S(2)}, u32[]{:S(2)}) collective-permute-start(bf16[128,1408]{1,0:T(8,128)(2,1)S(1)} %add_convert_fusion.21), channel_id=1, source_target_pairs={{0,8},{4,12},{8,0},{12,4},{16,24},{20,28},{24,16},{28,20},{1,9},{5... | collective-permute-start | bytes 1081352 | tf_op jit(solution)/shard_map/ppermute | solution.py:328
  1028.9 15.6 %collective-permute-start.33 = (bf16[128,1408]{1,0:T(8,128)(2,1)S(1)}, bf16[128,1408]{1,0:T(8,128)(2,1)S(1)}, u32[]{:S(2)}, u32[]{:S(2)}) collective-permute-start(bf16[128,1408]{1,0:T(8,128)(2,1)S(1)} %add_convert_fusion.22), channel_id=1, source_target_pairs={{0,16},{4,20},{8,24},{12,28},{16,0},{20,4},{24,8},{28,12},{1,17},{... | collective-permute-start | bytes 1081352 | tf_op jit(solution)/shard_map/ppermute | solution.py:328
  1029.1 23.0 %collective-permute-start.47 = (bf16[176,1024]{1,0:T(8,128)(2,1)S(1)}, bf16[176,1024]{1,0:T(8,128)(2,1)S(1)}, u32[]{:S(2)}, u32[]{:S(2)}) collective-permute-start(bf16[176,1024]{1,0:T(8,128)(2,1)S(1)} %add_convert_fusion.19), channel_id=1, source_target_pairs={{0,8},{4,12},{8,0},{12,4},{16,24},{20,28},{24,16},{28,20},{1,9},{5... | collective-permute-start | bytes 1081352 | tf_op jit(solution)/shard_map/ppermute | solution.py:328
  1036.7 15.7 %collective-permute-start.43 = (bf16[176,1024]{1,0:T(8,128)(2,1)S(1)}, bf16[176,1024]{1,0:T(8,128)(2,1)S(1)}, u32[]{:S(2)}, u32[]{:S(2)}) collective-permute-start(bf16[176,1024]{1,0:T(8,128)(2,1)S(1)} %add_convert_fusion.20), channel_id=1, source_target_pairs={{0,16},{4,20},{8,24},{12,28},{16,0},{20,4},{24,8},{28,12},{1,17},{... | collective-permute-start | bytes 1081352 | tf_op jit(solution)/shard_map/ppermute | solution.py:328
  1036.8 28.6 %collective-permute-start.28 = (bf16[256,1408]{1,0:T(8,128)(2,1)S(1)}, bf16[256,1408]{1,0:T(8,128)(2,1)S(1)}, u32[]{:S(2)}, u32[]{:S(2)}) collective-permute-start(bf16[256,1408]{1,0:T(8,128)(2,1)S(1)} %maximum_select_fusion.16), channel_id=1, source_target_pairs={{0,16},{4,20},{8,24},{12,28},{16,0},{20,4},{24,8},{28,12},{1,17},{... | collective-permute-start | bytes 2162696 | tf_op jit(solution)/shard_map/ppermute | solution.py:328
  1044.4 23.2 %collective-permute-start.24 = (bf16[256,1408]{1,0:T(8,128)(2,1)S(1)}, bf16[256,1408]{1,0:T(8,128)(2,1)S(1)}, u32[]{:S(2)}, u32[]{:S(2)}) collective-permute-start(bf16[256,1408]{1,0:T(8,128)(2,1)S(1)} %maximum_select_fusion.15), channel_id=1, source_target_pairs={{0,8},{4,12},{8,0},{12,4},{16,24},{20,28},{24,16},{28,20},{1,9},{5... | collective-permute-start | bytes 2162696 | tf_op jit(solution)/shard_map/ppermute | solution.py:328
  1044.6 36.3 %collective-permute-start.38 = (bf16[256,1408]{1,0:T(8,128)(2,1)S(1)}, bf16[256,1408]{1,0:T(8,128)(2,1)S(1)}, u32[]{:S(2)}, u32[]{:S(2)}) collective-permute-start(bf16[256,1408]{1,0:T(8,128)(2,1)S(1)} %maximum_select_fusion.18), channel_id=1, source_target_pairs={{0,16},{4,20},{8,24},{12,28},{16,0},{20,4},{24,8},{28,12},{1,17},{... | collective-permute-start | bytes 2162696 | tf_op jit(solution)/shard_map/ppermute | solution.py:328
  1052.1 30.9 %collective-permute-start.34 = (bf16[256,1408]{1,0:T(8,128)(2,1)S(1)}, bf16[256,1408]{1,0:T(8,128)(2,1)S(1)}, u32[]{:S(2)}, u32[]{:S(2)}) collective-permute-start(bf16[256,1408]{1,0:T(8,128)(2,1)S(1)} %maximum_select_fusion.17), channel_id=1, source_target_pairs={{0,8},{4,12},{8,0},{12,4},{16,24},{20,28},{24,16},{28,20},{1,9},{5... | collective-permute-start | bytes 2162696 | tf_op jit(solution)/shard_map/ppermute | solution.py:328
  1052.4 43.8 %collective-permute-start.48 = (bf16[352,1024]{1,0:T(8,128)(2,1)S(1)}, bf16[352,1024]{1,0:T(8,128)(2,1)S(1)}, u32[]{:S(2)}, u32[]{:S(2)}) collective-permute-start(bf16[352,1024]{1,0:T(8,128)(2,1)S(1)} %maximum_select_fusion.20), channel_id=1, source_target_pairs={{0,16},{4,20},{8,24},{12,28},{16,0},{20,4},{24,8},{28,12},{1,17},{... | collective-permute-start | bytes 2162696 | tf_op jit(solution)/shard_map/ppermute | solution.py:328
  1065.4 32.3 %collective-permute-start.44 = (bf16[352,1024]{1,0:T(8,128)(2,1)S(1)}, bf16[352,1024]{1,0:T(8,128)(2,1)S(1)}, u32[]{:S(2)}, u32[]{:S(2)}) collective-permute-start(bf16[352,1024]{1,0:T(8,128)(2,1)S(1)} %maximum_select_fusion.19), channel_id=1, source_target_pairs={{0,8},{4,12},{8,0},{12,4},{16,24},{20,28},{24,16},{28,20},{1,9},{5... | collective-permute-start | bytes 2162696 | tf_op jit(solution)/shard_map/ppermute | solution.py:328
  1069.9 32.9 %collective-permute-start.29 = (bf16[1024,1408]{1,0:T(8,128)(2,1)}, bf16[1024,1408]{1,0:T(8,128)(2,1)S(1)}, u32[]{:S(2)}, u32[]{:S(2)}) collective-permute-start(bf16[1024,1408]{1,0:T(8,128)(2,1)} %pad_maximum_fusion.2), channel_id=1, source_target_pairs={{0,4},{4,0},{8,12},{12,8},{16,20},{20,16},{24,28},{28,24},{1,5},{5... | collective-permute-start | bytes 8650760 | tf_op jit(solution)/shard_map/ppermute | solution.py:328
  1083.8 112.3 %collective-permute-start.39 = (bf16[1024,1408]{1,0:T(8,128)(2,1)S(1)}, bf16[1024,1408]{1,0:T(8,128)(2,1)S(1)}, u32[]{:S(2)}, u32[]{:S(2)}) collective-permute-start(bf16[1024,1408]{1,0:T(8,128)(2,1)S(1)} %pad_maximum_fusion.3), channel_id=1, source_target_pairs={{0,4},{4,0},{8,12},{12,8},{16,20},{20,16},{24,28},{28,24},{1,5},{5... | collective-permute-start | bytes 8650760 | tf_op jit(solution)/shard_map/ppermute | solution.py:328
  1087.4 11.3 collective-permute-start.10
  1096.1 23.5 %collective-permute-start = (bf16[1024,1536]{1,0:T(8,128)(2,1)}, bf16[1024,1536]{1,0:T(8,128)(2,1)}, u32[]{:S(2)}, u32[]{:S(2)}) collective-permute-start(bf16[1024,1536]{1,0:T(8,128)(2,1)} %convolution_convert_fusion.5), channel_id=1, source_target_pairs={{0,4},{4,0},{8,12},{12,8},{16,20},{20,16},{24,28},{28,24},{1,5},{5... | collective-permute-start | bytes 9437192 | tf_op jit(solution)/shard_map/ppermute | solution.py:328
  1098.6 116.4 %collective-permute-start.49 = (bf16[1408,1024]{1,0:T(8,128)(2,1)S(1)}, bf16[1408,1024]{1,0:T(8,128)(2,1)S(1)}, u32[]{:S(2)}, u32[]{:S(2)}) collective-permute-start(bf16[1408,1024]{1,0:T(8,128)(2,1)S(1)} %pad_maximum_fusion.4), channel_id=1, source_target_pairs={{0,4},{4,0},{8,12},{12,8},{16,20},{20,16},{24,28},{28,24},{1,5},{5... | collective-permute-start | bytes 8650760 | tf_op jit(solution)/shard_map/ppermute | solution.py:328
  1101.9 8.5 collective-permute-start.15
  1110.4 9.2 collective-permute-start.11
  1110.5 17.9 %collective-permute-start.16 = (bf16[64,1024]{1,0:T(8,128)(2,1)S(1)}, bf16[64,1024]{1,0:T(8,128)(2,1)S(1)}, u32[]{:S(2)}, u32[]{:S(2)}) collective-permute-start(bf16[64,1024]{1,0:T(8,128)(2,1)S(1)} %constant_dynamic-slice_fusion.12), channel_id=1, source_target_pairs={{0,8},{4,12},{8,0},{12,4},{16,24},{20,28},{24,16},{28,20},{1,9},{5... | collective-permute-start | bytes 393224 | tf_op jit(solution)/shard_map/ppermute | solution.py:328
  1126.2 21.7 %collective-permute-start.5 = (bf16[256,1536]{1,0:T(8,128)(2,1)S(1)}, bf16[256,1536]{1,0:T(8,128)(2,1)S(1)}, u32[]{:S(2)}, u32[]{:S(2)}) collective-permute-start(bf16[256,1536]{1,0:T(8,128)(2,1)S(1)} %constant_dynamic-slice_fusion.17), channel_id=1, source_target_pairs={{0,16},{4,20},{8,24},{12,28},{16,0},{20,4},{24,8},{28,12},{1,17},{... | collective-permute-start | bytes 2359304 | tf_op jit(solution)/shard_map/ppermute | solution.py:328
  1127.3 19.9 %collective-permute-start.12 = (bf16[64,1024]{1,0:T(8,128)(2,1)S(1)}, bf16[64,1024]{1,0:T(8,128)(2,1)S(1)}, u32[]{:S(2)}, u32[]{:S(2)}) collective-permute-start(bf16[64,1024]{1,0:T(8,128)(2,1)S(1)} %constant_dynamic-slice_fusion.14), channel_id=1, source_target_pairs={{0,16},{4,20},{8,24},{12,28},{16,0},{20,4},{24,8},{28,12},{1,17},{... | collective-permute-start | bytes 393224 | tf_op jit(solution)/shard_map/ppermute | solution.py:328
  1128.4 55.4 %collective-permute-start.17 = (bf16[64,1024]{1,0:T(8,128)(2,1)S(1)}, bf16[64,1024]{1,0:T(8,128)(2,1)S(1)}, u32[]{:S(2)}, u32[]{:S(2)}) collective-permute-start(bf16[64,1024]{1,0:T(8,128)(2,1)S(1)} %add_convert_fusion.27), channel_id=1, source_target_pairs={{0,8},{4,12},{8,0},{12,4},{16,24},{20,28},{24,16},{28,20},{1,9},{5... | collective-permute-start | bytes 393224 | tf_op jit(solution)/shard_map/ppermute | solution.py:328
  1147.3 17.6 %collective-permute-start.1 = (bf16[256,1536]{1,0:T(8,128)(2,1)S(1)}, bf16[256,1536]{1,0:T(8,128)(2,1)S(1)}, u32[]{:S(2)}, u32[]{:S(2)}) collective-permute-start(bf16[256,1536]{1,0:T(8,128)(2,1)S(1)} %constant_dynamic-slice_fusion.19), channel_id=1, source_target_pairs={{0,8},{4,12},{8,0},{12,4},{16,24},{20,28},{24,16},{28,20},{1,9},{5... | collective-permute-start | bytes 2359304 | tf_op jit(solution)/shard_map/ppermute | solution.py:328
  1147.9 36.1 %collective-permute-start.13 = (bf16[64,1024]{1,0:T(8,128)(2,1)S(1)}, bf16[64,1024]{1,0:T(8,128)(2,1)S(1)}, u32[]{:S(2)}, u32[]{:S(2)}) collective-permute-start(bf16[64,1024]{1,0:T(8,128)(2,1)S(1)} %add_convert_fusion.28), channel_id=1, source_target_pairs={{0,16},{4,20},{8,24},{12,28},{16,0},{20,4},{24,8},{28,12},{1,17},{... | collective-permute-start | bytes 393224 | tf_op jit(solution)/shard_map/ppermute | solution.py:328
  1164.8 8.1 collective-permute-start.6
  1172.9 8.5 collective-permute-start.2
  1181.4 12.2 collective-permute-start.7
  1183.9 12.1 collective-permute-start.3
  1184.0 20.1 %collective-permute-start.18 = (bf16[128,1024]{1,0:T(8,128)(2,1)S(1)}, bf16[128,1024]{1,0:T(8,128)(2,1)S(1)}, u32[]{:S(2)}, u32[]{:S(2)}) collective-permute-start(bf16[128,1024]{1,0:T(8,128)(2,1)S(1)} %maximum_select_fusion.24), channel_id=1, source_target_pairs={{0,16},{4,20},{8,24},{12,28},{16,0},{20,4},{24,8},{28,12},{1,17},{... | collective-permute-start | bytes 786440 | tf_op jit(solution)/shard_map/ppermute | solution.py:328
  1193.6 10.7 collective-permute-start.14
  1196.0 15.6 %collective-permute-start.8 = (bf16[256,1536]{1,0:T(8,128)(2,1)S(1)}, bf16[256,1536]{1,0:T(8,128)(2,1)S(1)}, u32[]{:S(2)}, u32[]{:S(2)}) collective-permute-start(bf16[256,1536]{1,0:T(8,128)(2,1)S(1)} %maximum_select_fusion.14), channel_id=1, source_target_pairs={{0,16},{4,20},{8,24},{12,28},{16,0},{20,4},{24,8},{28,12},{1,17},{... | collective-permute-start | bytes 2359304 | tf_op jit(solution)/shard_map/ppermute | solution.py:328
  1196.2 16.1 %collective-permute-start.4 = (bf16[256,1536]{1,0:T(8,128)(2,1)S(1)}, bf16[256,1536]{1,0:T(8,128)(2,1)S(1)}, u32[]{:S(2)}, u32[]{:S(2)}) collective-permute-start(bf16[256,1536]{1,0:T(8,128)(2,1)S(1)} %maximum_select_fusion.13), channel_id=1, source_target_pairs={{0,8},{4,12},{8,0},{12,4},{16,24},{20,28},{24,16},{28,20},{1,9},{5... | collective-permute-start | bytes 2359304 | tf_op jit(solution)/shard_map/ppermute | solution.py:328
  1204.5 34.9 %collective-permute-start.19 = (bf16[512,1024]{1,0:T(8,128)(2,1)S(1)}, bf16[512,1024]{1,0:T(8,128)(2,1)S(1)}, u32[]{:S(2)}, u32[]{:S(2)}) collective-permute-start(bf16[512,1024]{1,0:T(8,128)(2,1)S(1)} %pad_maximum_fusion.5), channel_id=1, source_target_pairs={{0,4},{4,0},{8,12},{12,8},{16,20},{20,16},{24,28},{28,24},{1,5},{5... | collective-permute-start | bytes 3145736 | tf_op jit(solution)/shard_map/ppermute | solution.py:328
  1215.0 96.9 %collective-permute-start.9 = (bf16[1024,1536]{1,0:T(8,128)(2,1)}, bf16[1024,1536]{1,0:T(8,128)(2,1)}, u32[]{:S(2)}, u32[]{:S(2)}) collective-permute-start(bf16[1024,1536]{1,0:T(8,128)(2,1)} %pad_maximum_fusion.1), channel_id=1, source_target_pairs={{0,4},{4,0},{8,12},{12,8},{16,20},{20,16},{24,28},{28,24},{1,5},{5... | collective-permute-start | bytes 9437192 | tf_op jit(solution)/shard_map/ppermute | solution.py:328
  (75 other events, 1361.5 us)
Sparse Core Ops, SparseCore 0:
  13.9 83.4 all-gather.9
  110.5 88.3 all-gather.11
  263.8 89.0 reduce-scatter.4
  358.0 81.2 all-gather.13
  440.8 79.2 all-gather.15
  557.9 75.2 reduce-scatter.8
  639.0 81.2 all-gather.17
  722.8 54.1 all-gather.19
  779.4 54.4 all-gather.21
  913.7 81.1 reduce-scatter.10
  997.9 77.2 reduce-scatter.6

commit v2 on v1

v2 whole, which is shorter than its diff:
```python
import functools
import jax, jax.numpy as jnp
from jax import lax
from jax.experimental import pallas as pl
from jax.experimental.pallas import tpu as pltpu

BLK = 128
CB = 4
CH = BLK * CB
NEG = -1e30
SCALE = 0.125


def nt(a, b):
    return lax.dot_general(a, b, (((1,), (1,)), ((), ())), preferred_element_type=jnp.float32)


def nn(a, b):
    return lax.dot_general(a, b, (((1,), (0,)), ((), ())), preferred_element_type=jnp.float32)


def lane_of(shape):
    return lax.broadcasted_iota(jnp.int32, shape, 1)


def row_of(shape):
    return lax.broadcasted_iota(jnp.int32, shape, 0)


def split_heads(x):
    low = lane_of(x.shape) < 64
    zero = jnp.zeros_like(x)
    return jnp.concatenate([jnp.where(low, x, zero), jnp.where(low, zero, x)], axis=0)


def join_heads(x):
    low = lane_of((BLK, 128)) < 64
    return jnp.where(low, x[:BLK], x[BLK:])


def own_lanes(pair):
    shape = (2 * BLK, 128)
    return lane_of(shape) // 3 == 2 * pair + row_of(shape) // BLK


def terms(x, lane):
    first = x.astype(jnp.bfloat16).astype(jnp.float32)
    second = (x - first).astype(jnp.bfloat16).astype(jnp.float32)
    return jnp.where(lane % 3 == 0, first, jnp.where(lane % 3 == 1, second, x - first - second))


def place_rows(place_ref, s, refs, dst_ref, lane=0):
    at = 0
    for ref in refs:
        for j in range(ref.shape[0]):
            for w in range(2):
                row = pl.multiple_of(place_ref[s, at] * BLK, BLK)
                dst_ref[pl.ds(row, BLK), lane:lane + 128] = ref[j, 0, w]
                at += 1


def fwd_kernel(place_ref, own_ref, q_ref, *refs, blocks, n):
    k_refs, v_refs, (o_ref, ext_ref, ks, vs, scr, acc) = refs[:n], refs[n:2 * n], refs[2 * n:]
    s, pair = pl.program_id(0), pl.program_id(1)

    @pl.when((s == 0) & (pair == 0))
    def _():
        vs[:, 128:256] = jnp.ones((blocks * BLK, 128), jnp.bfloat16)

    @pl.when(pair == 0)
    def _():
        ext_ref[...] = jnp.zeros_like(ext_ref)

    place_rows(place_ref, s, k_refs, ks)
    place_rows(place_ref, s, v_refs, vs)
    for w in range(2):
        rows = slice(w * BLK, (w + 1) * BLK)
        pos = own_ref[s, w]
        last = pos // CB
        qs = split_heads(q_ref[0, rows, :] * jnp.bfloat16(SCALE))

        def tiles_max(run, sc):
            for t in range(CB):
                run = jnp.maximum(run, sc[:, t * 128:(t + 1) * 128])
            return run

        def score(c, run):
            at = pl.multiple_of(c * CH, CH)
            sc = nt(qs, ks[pl.ds(at, CH), :])
            scr[c] = sc
            return tiles_max(run, sc)

        run = lax.fori_loop(0, last, score, jnp.full((2 * BLK, 128), NEG, jnp.float32))
        at = pl.multiple_of(last * CH, CH)
        sc = nt(qs, ks[pl.ds(at, CH), :])
        qpos = pos * BLK + row_of((2 * BLK, CH)) % BLK
        kpos = last * CH + lane_of((2 * BLK, CH))
        sc = jnp.where(kpos <= qpos, sc, NEG)
        scr[last] = sc
        run = tiles_max(run, sc)
        top = jnp.broadcast_to(jnp.max(run, axis=1, keepdims=True), (2 * BLK, 128))
        topc = jnp.concatenate([top] * CB, axis=1)
        acc[...] = jnp.zeros_like(acc)

        def weigh(c, carry):
            at = pl.multiple_of(c * CH, CH)
            p = jnp.exp(scr[c] - topc).astype(jnp.bfloat16)
            acc[...] += nn(p, vs[pl.ds(at, CH), :])
            return carry

        lax.fori_loop(0, last + 1, weigh, 0)
        total = acc[:, 128:256]
        o_ref[0, rows, :] = join_heads(acc[:, 0:128] / total).astype(jnp.bfloat16)
        lane = lane_of((2 * BLK, 128))
        mine = jnp.where(own_lanes(pair), terms(-(top + jnp.log(total)), lane), 0.0)
        ext_ref[0, rows, :] = (ext_ref[0, rows, :].astype(jnp.float32) + mine[:BLK] + mine[BLK:]).astype(jnp.bfloat16)


def dq_kernel(place_ref, own_ref, q_ref, do_ref, qx_ref, dox_ref, c_ref, a_ref, b_ref, *refs, blocks, n):
    k_refs, v_refs, (dq_ref, ks, vs, acc) = refs[:n], refs[n:2 * n], refs[2 * n:]
    s, pair = pl.program_id(0), pl.program_id(1)

    @pl.when((s == 0) & (pair == 0))
    def _():
        ks[:, 128:256] = jnp.ones((blocks * BLK, 128), jnp.bfloat16)
        vs[:, 128:256] = jnp.ones((blocks * BLK, 128), jnp.bfloat16)

    place_rows(place_ref, s, k_refs, ks)
    place_rows(place_ref, s, v_refs, vs)
    mine = own_lanes(pair)
    for w in range(2):
        rows = slice(w * BLK, (w + 1) * BLK)
        pos = own_ref[s, w]
        last = pos // CB

        def extend(tile, ext):
            both = jnp.concatenate([ext, ext], axis=0)
            return jnp.concatenate([split_heads(tile), jnp.where(mine, both, jnp.zeros_like(both))], axis=1)

        qs = extend(q_ref[0, rows, :] * jnp.bfloat16(SCALE), qx_ref[0, rows, :])
        dos = extend(do_ref[0, rows, :], dox_ref[0, rows, :])
        acc[...] = jnp.zeros_like(acc)

        def step(c, mask):
            at = pl.multiple_of(c * CH, CH)
            p = jnp.exp(nt(qs, ks[pl.ds(at, CH), :]))
            if mask is not None:
                p = jnp.where(mask, p, 0.0)
            ds = (p * nt(dos, vs[pl.ds(at, CH), :])).astype(jnp.bfloat16)
            acc[...] += nn(ds, ks[pl.ds(at, CH), 0:128])

        def body(c, carry):
            step(c, None)
            return carry

        lax.fori_loop(0, last, body, 0)
        qpos = pos * BLK + row_of((2 * BLK, CH)) % BLK
        kpos = last * CH + lane_of((2 * BLK, CH))
        step(last, kpos <= qpos)
        grad = join_heads(acc[...]) * SCALE
        dq_ref[0, rows, :] = turn(grad, c_ref[rows], a_ref[rows], b_ref[rows], -1.0).astype(jnp.bfloat16)


def dkv_kernel(place_ref, own_ref, k_ref, v_ref, c_ref, a_ref, b_ref, *refs, blocks, n):
    q_refs, do_refs, qx_refs, dox_refs = (refs[i * n:(i + 1) * n] for i in range(4))
    dk_ref, dv_ref, qs, dos, acck, accv = refs[4 * n:]
    s, pair = pl.program_id(0), pl.program_id(1)
    place_rows(place_ref, s, q_refs, qs)
    place_rows(place_ref, s, do_refs, dos)

    @pl.when(pair == 0)
    def _():
        place_rows(place_ref, s, qx_refs, qs, 128)
        place_rows(place_ref, s, dox_refs, dos, 128)

    ones = own_lanes(pair).astype(jnp.bfloat16)
    for w in range(2):
        rows = slice(w * BLK, (w + 1) * BLK)
        pos = own_ref[s, w]
        first = pos // CB
        kw = jnp.concatenate([split_heads(k_ref[0, 0, rows, :] * jnp.bfloat16(SCALE)), ones], axis=1)
        vw = jnp.concatenate([split_heads(v_ref[0, 0, rows, :]), ones], axis=1)
        acck[...] = jnp.zeros_like(acck)
        accv[...] = jnp.zeros_like(accv)

        def step(c, mask):
            at = pl.multiple_of(c * CH, CH)
            p = jnp.exp(nt(kw, qs[pl.ds(at, CH), :]))
            if mask is not None:
                p = jnp.where(mask, p, 0.0)
            accv[...] += nn(p.astype(jnp.bfloat16), dos[pl.ds(at, CH), 0:128])
            ds = (p * nt(vw, dos[pl.ds(at, CH), :])).astype(jnp.bfloat16)
            acck[...] += nn(ds, qs[pl.ds(at, CH), 0:128])

        def body(c, carry):
            step(c, None)
            return carry

        kpos = pos * BLK + row_of((2 * BLK, CH)) % BLK
        qpos = first * CH + lane_of((2 * BLK, CH))
        step(first, kpos <= qpos)
        lax.fori_loop(first + 1, blocks // CB, body, 0)
        grad = join_heads(acck[...]) * SCALE
        dk_ref[0, rows, :] = turn(grad, c_ref[rows], a_ref[rows], b_ref[rows], -1.0).astype(jnp.bfloat16)
        dv_ref[0, rows, :] = join_heads(accv[...]).astype(jnp.bfloat16)


OWN = pl.BlockSpec((1, 2 * BLK, 128), lambda s, h, *_: (s, 0, h))
EXT = pl.BlockSpec((1, 2 * BLK, 128), lambda s, h, *_: (s, 0, 0))
TABLE = pl.BlockSpec((2 * BLK, 128), lambda s, h, *_: (s, 0))


def piece(x, first=0, lane=None):
    count = x.shape[0] if first is None else 1
    lead = 0 if first is None else first
    if lane is None:
        return pl.BlockSpec((count, 1, 2, BLK, 128), lambda s, h, *_: (lead, s, 0, 0, h))
    return pl.BlockSpec((count, 1, 2, BLK, 128), lambda s, h, *_: (lead, s, 0, 0, lane))


def attention_call(kernel, name, mats, seqs, pairs, blocks, in_specs, out_specs, out_shape, scratch, args):
    work = seqs * pairs * 2 * 2 * BLK * blocks * BLK // 2
    return pl.pallas_call(
        kernel,
        grid_spec=pltpu.PrefetchScalarGridSpec(
            num_scalar_prefetch=2, grid=(seqs, pairs), in_specs=in_specs, out_specs=out_specs, scratch_shapes=scratch),
        out_shape=out_shape,
        compiler_params=pltpu.CompilerParams(vmem_limit_bytes=40 * 2**20),
        cost_estimate=pl.CostEstimate(flops=work * 512 * mats, bytes_accessed=4 * seqs * pairs * blocks * BLK * 128, transcendentals=work),
        name=name,
    )(*args)


def rows_of(blocks, lanes):
    return pltpu.VMEM((blocks * BLK, lanes), jnp.bfloat16)


def acc_of(lanes):
    return pltpu.VMEM((2 * BLK, lanes), jnp.float32)


def attend(place, own, q, keys, values):
    seqs, pairs, blocks = q.shape[0], q.shape[2] // 128, place.shape[1]
    return attention_call(
        functools.partial(fwd_kernel, blocks=blocks, n=len(keys)), "attend", 2, seqs, pairs, blocks,
        [OWN] + [piece(*e) for e in keys + values], [OWN, EXT],
        [jax.ShapeDtypeStruct(q.shape, jnp.bfloat16), jax.ShapeDtypeStruct(q.shape[:2] + (128,), jnp.bfloat16)],
        [rows_of(blocks, 128), rows_of(blocks, 256), pltpu.VMEM((blocks // CB, 2 * BLK, CH), jnp.float32), acc_of(256)],
        [place, own, q] + [e[0] for e in keys + values])


def query_grad(place, own, q, do, q_ext, do_ext, tabs, keys, values):
    seqs, pairs, blocks = q.shape[0], q.shape[2] // 128, place.shape[1]
    return attention_call(
        functools.partial(dq_kernel, blocks=blocks, n=len(keys)), "query_grad", 3, seqs, pairs, blocks,
        [OWN, OWN, EXT, EXT, TABLE, TABLE, TABLE] + [piece(*e) for e in keys + values], OWN,
        jax.ShapeDtypeStruct(q.shape, jnp.bfloat16),
        [rows_of(blocks, 256), rows_of(blocks, 256), acc_of(128)],
        [place, own, q, do, q_ext, do_ext, *tabs] + [e[0] for e in keys + values])


def key_value_grad(place, own, kv, tabs, queries, grads):
    seqs, pairs, blocks = kv.shape[1], kv.shape[3] // 128, place.shape[1]
    shape = kv.shape[1:]

    def own_part(i):
        return pl.BlockSpec((1, 1, 2 * BLK, 128), lambda s, h, *_: (i, s, 0, h))

    return attention_call(
        functools.partial(dkv_kernel, blocks=blocks, n=len(queries)), "key_value_grad", 4, seqs, pairs, blocks,
        [own_part(0), own_part(1), TABLE, TABLE, TABLE] + [piece(*e) for e in queries + grads]
        + [piece(*e, lane=pairs) for e in queries + grads], [OWN, OWN],
        [jax.ShapeDtypeStruct(shape, jnp.bfloat16)] * 2,
        [rows_of(blocks, 256), rows_of(blocks, 256), acc_of(128), acc_of(128)],
        [place, own, kv, kv, *tabs] + [e[0] for e in queries + grads] * 2)


import math
from jax.sharding import PartitionSpec as P

HEAD_DIM = 64
ROT = 16
SEQS = 4
EPS = 1e-05
F32 = jnp.float32
BF16 = jnp.bfloat16


def rc(left, right):
    return lax.dot_general(left, right, (((0,), (0,)), ((), ())), preferred_element_type=F32)


def layer_stats(values, gain, shift):
    mean = jnp.mean(values, axis=-1, keepdims=True)
    centred = values - mean
    inverse = lax.rsqrt(jnp.mean(centred * centred, axis=-1, keepdims=True) + EPS)
    unit = centred * inverse
    return unit * gain + shift, unit, inverse


def layer_back(grad, unit, inverse, gain):
    scaled = grad * gain
    grad_in = inverse * (
        scaled
        - jnp.mean(scaled, axis=-1, keepdims=True)
        - unit * jnp.mean(scaled * unit, axis=-1, keepdims=True)
    )
    return grad_in, jnp.sum(grad * unit, axis=0), jnp.sum(grad, axis=0)


def rotary_tables(positions):
    half = ROT // 2
    freq = 10000.0 ** (-2.0 * jnp.arange(half, dtype=F32) / ROT)
    angles = positions.astype(F32)[:, None] * freq[None, :]
    cos, sin = jnp.cos(angles), jnp.sin(angles)
    rows = positions.shape[0]
    one, none = jnp.ones((rows, HEAD_DIM - ROT), F32), jnp.zeros((rows, HEAD_DIM - ROT), F32)
    zero = jnp.zeros_like(sin)
    ctab = jnp.concatenate([cos, cos, one] * 2, axis=1)
    above = jnp.concatenate([sin, zero, none] * 2, axis=1)
    below = jnp.concatenate([zero, sin, none] * 2, axis=1)
    return ctab, above, below


def turn(x, ctab, above, below, sign):
    up = pltpu.roll(x, 128 - ROT // 2, axis=1)
    down = pltpu.roll(x, ROT // 2, axis=1)
    return x * ctab + sign * (down * below - up * above)


def project_kernel(h_ref, wq_ref, wk_ref, wv_ref, bias_ref, c_ref, a_ref, b_ref, q_ref, kv_ref):
    h = h_ref[...]
    width = wq_ref.shape[1]
    tabs = c_ref[...], a_ref[...], b_ref[...]
    for at, (w_ref, out) in enumerate(((wq_ref, q_ref.at[0]), (wk_ref, kv_ref.at[0, 0]), (wv_ref, kv_ref.at[1, 0]))):
        lin = nn(h, w_ref[...]) + bias_ref[at:at + 1, :]
        for p in range(width // 128):
            part = lin[:, p * 128:(p + 1) * 128]
            if at < 2:
                part = turn(part, *tabs, 1.0)
            out[:, p * 128:(p + 1) * 128] = part.astype(BF16)


def project(rows, wq, wk, wv, bias, tabs):
    total, depth = rows.shape
    width = wq.shape[1]
    step = total // SEQS
    weight = pl.BlockSpec((depth, width), lambda i: (0, 0))
    table = pl.BlockSpec((step, 128), lambda i: (i, 0))
    return pl.pallas_call(
        project_kernel,
        grid=(SEQS,),
        in_specs=[pl.BlockSpec((step, depth), lambda i: (i, 0)), weight, weight, weight,
                  pl.BlockSpec((3, width), lambda i: (0, 0)), table, table, table],
        out_specs=[pl.BlockSpec((1, step, width), lambda i: (i, 0, 0)),
                   pl.BlockSpec((2, 1, step, width), lambda i: (0, i, 0, 0))],
        out_shape=[jax.ShapeDtypeStruct((SEQS, step, width), BF16), jax.ShapeDtypeStruct((2, SEQS, step, width), BF16)],
        compiler_params=pltpu.CompilerParams(vmem_limit_bytes=48 * 2**20),
        cost_estimate=pl.CostEstimate(flops=6 * total * depth * width, bytes_accessed=6 * depth * width, transcendentals=0),
        name="project",
    )(rows, wq, wk, wv, bias, *tabs)


def mlp_kernel(h_ref, dy_ref, gate_ref, up_ref, down_ref, act_ref, *grad_refs):
    width = gate_ref.shape[1]
    gate = nn(h_ref[...], gate_ref[...])
    up = nn(h_ref[...], up_ref[...])
    grad = nt(dy_ref[...], down_ref[...])
    sig = 1.0 / (1.0 + jnp.exp(-gate))
    silu = gate * sig
    act_ref[...] = (silu * up).astype(BF16)
    outs = grad_refs if len(grad_refs) == 2 else (grad_refs[0].at[:, :width], grad_refs[0].at[:, width:])
    outs[0][...] = (grad * up * (sig + silu * (1.0 - sig))).astype(BF16)
    outs[1][...] = (grad * silu).astype(BF16)


def mlp(rows, dy, gate_w, up_w, down_w, step=256):
    total, depth = rows.shape
    width = gate_w.shape[1]
    joined = width % 128 == 0
    block = pl.BlockSpec((step, depth), lambda i: (i, 0))

    def whole(x):
        return pl.BlockSpec(x.shape, lambda i: (0, 0), pipeline_mode=pl.Buffered(1))

    def out(n):
        return pl.BlockSpec((step, n), lambda i: (i, 0)), jax.ShapeDtypeStruct((total, n), BF16)

    outs = [out(width), out(2 * width)] if joined else [out(width)] * 3
    act, *grads = pl.pallas_call(
        mlp_kernel,
        grid=(total // step,),
        in_specs=[block, block, whole(gate_w), whole(up_w), whole(down_w)],
        out_specs=[o[0] for o in outs],
        out_shape=[o[1] for o in outs],
        compiler_params=pltpu.CompilerParams(vmem_limit_bytes=56 * 2**20),
        cost_estimate=pl.CostEstimate(flops=6 * total * depth * width, bytes_accessed=6 * depth * width + 10 * total * depth,
                                      transcendentals=total * width),
        name="mlp",
    )(rows, dy, gate_w, up_w, down_w)
    return act, grads[0] if joined else jnp.concatenate(grads, axis=1)


def ctx_swap(x, mask):
    n = lax.axis_size("ctx")
    return lax.ppermute(x, "ctx", [(i, i ^ mask) for i in range(n)])


def add16(a, b):
    return (a.astype(F32) + b.astype(F32)).astype(BF16)


def after(x, *deps):
    return lax.optimization_barrier((x, deps))[0]


def half_of(x, bit, mine):
    side = (lax.axis_index("ctx") >> bit) & 1
    r = x.shape[0] // 2
    return lax.dynamic_slice_in_dim(x, (side if mine else 1 - side) * r, r, 0)


def weight_grad(left, right, split_left):
    core = lax.axis_index("ctx") & 1
    split = left if split_left else right
    w = split.shape[1] // 2

    def part(which):
        cut = lax.dynamic_slice_in_dim(split, which * w, w, 1)
        return rc(cut, right) if split_left else rc(left, cut)

    got = ctx_swap(part(1 - core).astype(BF16), 1)
    gate = yield [got]
    half = (part(core) + got.astype(F32)).astype(BF16)
    bits = list(range(1, int(math.log2(lax.axis_size("ctx")))))
    orders = [bits, bits[::-1]]
    r = half.shape[0] // 2
    streams = [half[:r], half[r:]]
    for i in range(len(bits)):
        streams = after(streams, gate)
        got = [ctx_swap(half_of(x, o[i], False), 1 << o[i]) for x, o in zip(streams, orders)]
        gate = yield got
        streams = [add16(half_of(x, o[i], True), g) for x, o, g in zip(streams, orders, got)]
    for i in reversed(range(len(bits))):
        streams = after(streams, gate)
        got = [ctx_swap(x, 1 << o[i]) for x, o in zip(streams, orders)]
        gate = yield got
        streams = [
            jnp.where(((lax.axis_index("ctx") >> o[i]) & 1) == 0, jnp.concatenate([x, g]), jnp.concatenate([g, x]))
            for x, o, g in zip(streams, orders, got)
        ]
    half = after(jnp.concatenate(streams), gate)
    other = ctx_swap(half, 1)
    yield [other]
    yield half, other


def advance(chains, gate=None):
    fly = []
    for chain in chains:
        fly += chain.send(gate)
    return fly


def begin(*args):
    chain = weight_grad(*args)
    return chain, next(chain)


def finish(chain):
    for got in chain:
        pass
    return got


def unpack_rows_kernel(core_ref, half_ref, other_ref, *out_refs):
    def put(src):
        at = 0
        for out in out_refs:
            out[...] = src[:, at:at + out.shape[1]].astype(F32)
            at += out.shape[1]

    @pl.when(pl.program_id(0) == core_ref[0])
    def _():
        put(half_ref)

    @pl.when(pl.program_id(0) != core_ref[0])
    def _():
        put(other_ref)


def unpack_rows(half, other, parts):
    r, c = half.shape
    step = math.gcd(r, 256)
    blocks = r // step
    core = lax.axis_index("ctx") & 1

    def mine(i, j, core_ref):
        return jnp.where(i == core_ref[0], j, jnp.where(core_ref[0] == 0, blocks - 1, 0)), 0

    def theirs(i, j, core_ref):
        return jnp.where(i != core_ref[0], j, jnp.where(core_ref[0] == 1, blocks - 1, 0)), 0

    return pl.pallas_call(
        unpack_rows_kernel,
        grid_spec=pltpu.PrefetchScalarGridSpec(
            num_scalar_prefetch=1, grid=(2, blocks),
            in_specs=[pl.BlockSpec((step, c), mine), pl.BlockSpec((step, c), theirs)],
            out_specs=[pl.BlockSpec((step, c // parts), lambda i, j, _: (i * blocks + j, 0))] * parts),
        out_shape=[jax.ShapeDtypeStruct((2 * r, c // parts), F32)] * parts,
        compiler_params=pltpu.CompilerParams(vmem_limit_bytes=40 * 2**20),
        cost_estimate=pl.CostEstimate(flops=0, bytes_accessed=12 * r * c, transcendentals=0),
        name="unpack_rows",
    )(core[None], half, other)


def unpack_cols_kernel(core_ref, half_ref, other_ref, out_ref):
    c = half_ref.shape[1]
    core = core_ref[0]
    out_ref[:, pl.ds(pl.multiple_of(core * c, 128), c)] = half_ref[...].astype(F32)
    out_ref[:, pl.ds(pl.multiple_of((1 - core) * c, 128), c)] = other_ref[...].astype(F32)


def unpack_cols(half, other):
    r, c = half.shape
    step = math.gcd(r, 256)
    block = pl.BlockSpec((step, c), lambda i, _: (i, 0))
    return pl.pallas_call(
        unpack_cols_kernel,
        grid_spec=pltpu.PrefetchScalarGridSpec(
            num_scalar_prefetch=1, grid=(r // step,), in_specs=[block, block],
            out_specs=pl.BlockSpec((step, 2 * c), lambda i, _: (i, 0))),
        out_shape=jax.ShapeDtypeStruct((r, 2 * c), F32),
        compiler_params=pltpu.CompilerParams(vmem_limit_bytes=40 * 2**20),
        cost_estimate=pl.CostEstimate(flops=0, bytes_accessed=12 * r * c, transcendentals=0),
        name="unpack_cols",
    )((lax.axis_index("ctx") & 1)[None], half, other)


def all_rows(x):
    return lax.all_gather(x, "tp", axis=0, tiled=True)


def sum_rows(x):
    return lax.psum_scatter(x, "tp", scatter_dimension=0, tiled=True).astype(F32)


def gather_pair(kv):
    n = lax.axis_size("ctx")
    held = {0: ((kv, 0), (kv, 1))}
    for bit in range(1, int(math.log2(n))):
        mask = 1 << bit
        for j in list(held):
            if j == 0:
                got = ctx_swap(kv, mask)
                held[mask] = (got, 0), (got, 1)
            elif mask == 4 and j == 2:
                held[6] = (ctx_swap(held[2][0][0][0:1], 4), 0), (ctx_swap(held[4][1][0][1:2], 2), 0)
            else:
                (k, i), (v, t) = held[j]
                if k is v:
                    got = ctx_swap(k, mask)
                    held[j | mask] = (got, i), (got, t)
                else:
                    held[j | mask] = (ctx_swap(k, mask), i), (ctx_swap(v, mask), t)
    for j in list(held):
        (k, i), (v, t) = held[j]
        got = ctx_swap(k, 1)
        held[j | 1] = (got, i), (got if k is v else ctx_swap(v, 1), t)
    return [held[j][0] for j in range(n)], [held[j][1] for j in range(n)]


def gather_ctx(x):
    n = lax.axis_size("ctx")
    held = [x] + [None] * (n - 1)
    for j in range(2, n, 2):
        held[j] = ctx_swap(x, j)
    for j in range(0, n, 2):
        held[j + 1] = ctx_swap(held[j], 1)
    return held


def local(tokens, cotangent, block_order, gain_one, shift_one, query_w, key_w, value_w, query_b, key_b, value_b,
          output_w, gain_two, shift_two, gate_w, up_w, down_w):
    heads = key_b.shape[0]
    width = heads * HEAD_DIM
    n_ctx, n_tp = lax.axis_size("ctx"), lax.axis_size("tp")
    ctx = lax.axis_index("ctx")
    own = lax.dynamic_slice_in_dim(block_order, 2 * ctx, 2, 1)
    picked = (jnp.arange(n_ctx, dtype=jnp.int32) ^ ctx)[:, None] == jnp.arange(n_ctx, dtype=jnp.int32)[None, :]
    by_ctx = block_order.reshape(SEQS, 1, n_ctx, 2)
    place = jnp.sum(jnp.where(picked[None, :, :, None], by_ctx, 0), axis=2).astype(jnp.int32).reshape(SEQS, 2 * n_ctx)
    positions = (own[:, :, None] * BLK + jnp.arange(BLK, dtype=jnp.int32)).reshape(-1)
    tabs = rotary_tables(positions)

    x = tokens.astype(F32)
    normed_one, unit_one, inverse_one = layer_stats(x, gain_one, shift_one)
    rows_one = all_rows(normed_one.astype(BF16))
    key_bias = jnp.concatenate([key_b, jnp.zeros((heads, HEAD_DIM - ROT), F32)], axis=1).reshape(-1)
    bias = jnp.stack([query_b, key_bias, value_b])
    q, kv = project(rows_one, query_w, key_w, value_w, bias, tabs)
    keys, values = gather_pair(kv.reshape(2, SEQS, 2, BLK, width))

    rows_w = output_w.shape[0] // n_ctx
    part = lax.dynamic_slice_in_dim(output_w, ctx * rows_w, rows_w, 0)
    part = lax.all_gather(after(part, rows_one), "tp", axis=0)
    dy_rows = all_rows(after(cotangent, kv))
    whole_w = lax.all_gather(after(part, dy_rows), "ctx", axis=1).reshape(n_tp * output_w.shape[0], -1)

    attn, q_ext = attend(place, own, q, keys, values)
    attn_rows = attn.reshape(-1, width)
    attn_own = lax.all_to_all(attn_rows, "tp", split_axis=0, concat_axis=1, tiled=True)
    mixed = x + nn(attn_own, whole_w)
    normed_two, unit_two, inverse_two = layer_stats(mixed, gain_two, shift_two)
    rows_two = all_rows(after(normed_two.astype(BF16), dy_rows, whole_w))
    shape = (1, SEQS, 2, BLK, width + 128)
    queries = gather_ctx(after(jnp.concatenate([q, q_ext], axis=2).reshape(shape), attn_own))
    rows_two = after(rows_two, queries)

    act, grad_gu = mlp(rows_two, dy_rows, gate_w, up_w, down_w)
    ff = gate_w.shape[1]
    part_two = (nt(grad_gu[:, :ff], gate_w) + nt(grad_gu[:, ff:], up_w)).astype(BF16)
    grad_two = sum_rows(part_two)
    act, rows_two, dy_rows, grad_gu = after((act, rows_two, dy_rows, grad_gu), part_two)
    down_chain, fly = begin(act, dy_rows, False)
    gu_chain, more = begin(rows_two, grad_gu, True)
    down = nn(act, down_w).astype(BF16)
    fly = advance([down_chain, gu_chain], fly + more)
    grad_two = after(grad_two, fly, down)

    norm_two, grad_gain_two, grad_shift_two = layer_back(grad_two, unit_two, inverse_two, gain_two)
    grad_mixed = cotangent.astype(F32) + norm_two
    branch_own = grad_mixed.astype(BF16)
    grad_attn = nt(branch_own, whole_w).astype(BF16)
    for _ in range(int(math.log2(n_ctx)) - 2):
        fly = advance([down_chain, gu_chain])
    grad_attn = lax.all_to_all(grad_attn, "tp", split_axis=1, concat_axis=0, tiled=True)
    branch = all_rows(after(branch_own, grad_attn))
    out_tokens = (mixed + sum_rows(after(down, branch))).astype(BF16)
    lane = jnp.arange(128)[None, :]
    ind = ((jnp.arange(width) // HEAD_DIM)[:, None] == lane // 3).astype(F32)
    delta = lax.dot_general(grad_attn.astype(F32) * attn_rows.astype(F32), ind, (((1,), (0,)), ((), ())),
                            precision=lax.Precision.HIGHEST, preferred_element_type=F32)
    do_ext = terms(-delta, lane).astype(BF16)
    grads = gather_ctx(jnp.concatenate([grad_attn, do_ext], axis=1).reshape(shape))
    grad_attn = after(grad_attn, fly)
    fly = advance([down_chain, gu_chain])
    grad_q = query_grad(place, own, q, grad_attn.reshape(q.shape), q_ext, do_ext.reshape(q_ext.shape), tabs, keys, values)
    grad_q = grad_q.reshape(-1, width)
    q_part = nt(grad_q, query_w)
    branch, grads = after((branch, grads), fly, q_part)
    for _ in range(int(math.log2(n_ctx)) - 2):
        fly = advance([down_chain, gu_chain], grads)
    out_chain, more = begin(attn_rows, branch, False)
    grad_k, grad_v = key_value_grad(place, own, kv, tabs, [(x, 0) for x in queries], [(x, 0) for x in grads])
    grad_k, grad_v = after((grad_k, grad_v), fly, more)
    grad_k, grad_v = (g.reshape(-1, width) for g in (grad_k, grad_v))
    part_one = q_part + nt(grad_k, key_w) + nt(grad_v, value_w)
    part_sent = part_one.astype(BF16)
    grad_one = sum_rows(part_sent)

    rows_one, grad_q, grad_k, grad_v = after((rows_one, grad_q, grad_k, grad_v), part_sent)
    unit_rows = (rows_one.astype(F32) - shift_one) / gain_one
    grad_qkv = jnp.concatenate([grad_q, grad_k, grad_v], axis=1)
    bias_grad = jnp.sum(grad_qkv.astype(F32), axis=0)
    tp_row = (jnp.arange(n_tp) == lax.axis_index("tp"))[:, None]
    small = jnp.concatenate([
        jnp.sum(part_one * unit_rows, axis=0), jnp.sum(part_one, axis=0), grad_gain_two, grad_shift_two,
        jnp.where(tp_row, bias_grad[None, :], 0.0).reshape(-1)])
    qkv_chain, more = begin(rows_one, grad_qkv, True)
    fly = advance([down_chain, gu_chain, out_chain])
    small = lax.psum(small, ("ctx", "tp"))
    depth = x.shape[1]
    norms = small[:4 * depth].reshape(4, depth)
    bias_sum = jnp.sum(jnp.where(tp_row, small[4 * depth:].reshape(n_tp, -1), 0.0), axis=0)
    grad_gate_w, grad_up_w = unpack_rows(*finish(gu_chain), 2)
    grad_query_w, grad_key_w, grad_value_w = unpack_rows(*finish(qkv_chain), 3)
    grad_down_w, grad_output_w = unpack_cols(*finish(down_chain)), unpack_cols(*finish(out_chain))
    norm_one, _, _ = layer_back(grad_one, unit_one, inverse_one, gain_one)
    grad_tokens = (grad_mixed + norm_one).astype(BF16)
    return (
        out_tokens, grad_tokens, norms[0], norms[1], grad_query_w, grad_key_w, grad_value_w,
        bias_sum[:width], bias_sum[width:2 * width].reshape(heads, HEAD_DIM)[:, :ROT], bias_sum[2 * width:],
        grad_output_w, norms[2], norms[3], grad_gate_w, grad_up_w, grad_down_w,
    )


def solution(mesh):
    rows, cols, depth, flat = P(("ctx", "tp"), None), P(None, "tp"), P("tp", None), P("tp")
    in_specs = (rows, rows, P(), P(), P(), cols, cols, cols, flat, depth, flat, depth, P(), P(), cols, cols, depth)
    out_specs = (rows, rows, P(), P(), cols, cols, cols, flat, depth, flat, depth, P(), P(), cols, cols, depth)
    return jax.shard_map(local, mesh=mesh, in_specs=in_specs, out_specs=out_specs, check_vma=False)
```

time: 1350 us -> 1190 us (0.88)
  waiting for transfers between devices: 737 us -> 555 us
  Pallas kernels: 168 us -> 231 us
  starting transfers between devices: 33.8 us -> 90.6 us
  matrix products: 153 us -> 117 us
  other arithmetic: 98.7 us -> 76.1 us
  local copies, waits for them, and re-layouts: 58 us -> 36.2 us
    ppermute x50 -> x63, waiting for transfers between devices: 171 us -> 307 us  [ctx_swap(): return lax.ppermute(x, 'ctx', [(i, i ^ mask) for i in range(n)])]
    reduce_scatter x4 -> x3, waiting for transfers between devices: 165 us -> 28.9 us  [sum_rows(): lax.psum_scatter(x, 'tp', scatter_dimension=0, tiled=True).astype(F32)]
    all_gather x4, waiting for transfers between devices: 289 us -> 185 us  [all_rows(): return lax.all_gather(x, 'tp', axis=0, tiled=True)]
    all_gather x3 -> x2, waiting for transfers between devices: 111 us -> 11.1 us  [the longest x1 11.1 us: local(): part = lax.all_gather(after(part, rows_one), 'tp', axis=0)]
    pallas_call x3 -> x8, Pallas kernels: 157 us -> 219 us  [the longest x3 156 us: attention_call(): pl.pallas_call(kernel, grid_spec=pltpu.PrefetchScalarGridSpec(num_scalar_...]
    ppermute x50 -> x63, starting transfers between devices: 32.9 us -> 86.8 us  [ctx_swap(): return lax.ppermute(x, 'ctx', [(i, i ^ mask) for i in range(n)])]
    convert_element_type x7 -> x4, other arithmetic: 61.4 us -> 7.84 us  [the longest x1 2.56 us: local(): out_tokens = (mixed + sum_rows(after(down, branch))).astype(BF16)]
    all_to_all x0 -> x1, blocking collectives: none -> 27.5 us  [local(): lax.all_to_all(attn_rows, 'tp', split_axis=0, concat_axis=1, tiled=True)]
  transfers between devices with their start and end apart: 61 -> 73, of which waited for: 32 -> 37; matrix products, arithmetic and copies ran while one was open for 14% -> 13% of each run, Pallas kernels for 4% -> 16%
where the time goes in v2:
time: 1190 us
  waiting for transfers between devices  555 us (47%)
  Pallas kernels  231 us (19%)
  matrix products  117 us (10%)
  starting transfers between devices  90.6 us (8%)
  other arithmetic  76.1 us (6%)
  blocking collectives  65.4 us (5%)
  local copies, waits for them, and re-layouts  36.2 us (3%)
  between operations  15.4 us (1%)
    ppermute x63, waiting for transfers between devices, ctx_swap(): return lax.ppermute(x, 'ctx', [(i, i ^ mask) for i in range(n)])  307 us
    all_gather x4, waiting for transfers between devices, all_rows(): return lax.all_gather(x, 'tp', axis=0, tiled=True)  185 us
    pallas_call x3, Pallas kernels, attention_call(): pl.pallas_call(kernel, grid_spec=pltpu.PrefetchScalarGridSpec(num_scalar_...  156 us
    ppermute x63, starting transfers between devices, ctx_swap(): return lax.ppermute(x, 'ctx', [(i, i ^ mask) for i in range(n)])  86.8 us
    dot_general x8, matrix products, rc(): lax.dot_general(left, right, (((0,), (0,)), ((), ())), preferred_element_...  50.9 us
    dot_general x6, matrix products, nt(): lax.dot_general(a, b, (((1,), (1,)), ((), ())), preferred_element_type=jn...  50.1 us
    psum x1, blocking collectives, local(): small = lax.psum(small, ('ctx', 'tp'))  37.9 us
    reduce_scatter x3, waiting for transfers between devices, sum_rows(): lax.psum_scatter(x, 'tp', scatter_dimension=0, tiled=True).astype(F32)  28.9 us
  transfers between devices with their start and end apart: 73, of which 37 were waited for; matrix products, arithmetic and copies ran while one was open for 13% of the time, Pallas kernels for 16%

profile of v2, /device:TPU:0, one launch (start us, length us, event | category | flops | bytes accessed | tf_op | source)
XLA Modules:
  0.0 1186.7 jit_solution(1731922872121688949)
XLA Ops:
  13.4 82.8 %all-gather.9.cloned.1.call-done.h_ref = bf16[1024,2048]{1,0:T(8,128)(2,1)} async-done(((bf16[256,2048]{1,0:T(8,128)(2,1)}), bf16[1024,2048]{1,0:T(8,128)(2,1)}) %all-gather.9.cloned.1.call-update) | async-done | bytes 4194320 | tf_op jit(solution)/shard_map/all_gather | solution.py:541
  102.0 11.6 project.1
  113.7 11.1 all-gather.17.cloned.1.call-done
  124.8 81.9 %all-gather.11.cloned.1.call-done.dy_ref = bf16[1024,2048]{1,0:T(8,128)(2,1)} async-done(((bf16[256,2048]{1,0:T(8,128)(2,1)}), bf16[1024,2048]{1,0:T(8,128)(2,1)}) %all-gather.11.cloned.1.call-update) | async-done | bytes 4194320 | tf_op jit(solution)/shard_map/all_gather | solution.py:541
  209.8 74.5 %collective-permute-done.3.refs_4_.refs_12_ = bf16[2,4,2,128,512]{4,3,2,1,0:T(8,128)(2,1)} collective-permute-done((bf16[2,4,2,128,512]{4,3,2,1,0:T(8,128)(2,1)}, bf16[2,4,2,128,512]{4,3,2,1,0:T(8,128)(2,1)}, u32[]{:S(2)}, u32[]{:S(2)}) %collective-permute-start.3) | collective-permute-done | bytes 2097184 | tf_op jit(solution)/shard_map/ppermute | solution.py:406
  290.1 21.8 %collective-permute-done.7.refs_14_ = bf16[1,4,2,128,512]{4,3,2,1,0:T(8,128)(2,1)} collective-permute-done((bf16[1,4,2,128,512]{4,3,2,1,0:T(8,128)(2,1)S(1)}, bf16[1,4,2,128,512]{4,3,2,1,0:T(8,128)(2,1)}, u32[]{:S(2)}, u32[]{:S(2)}) %collective-permute-start.7) | collective-permute-done | bytes 1048608 | tf_op jit(solution)/shard_map/ppermute | solution.py:406
  318.0 42.7 %attend.1 = (bf16[4,256,512]{2,1,0:T(8,128)(2,1)S(1)}, bf16[4,256,128]{2,1,0:T(8,128)(2,1)S(1)}) custom-call(s32[4,16]{1,0:T(4,128)S(1)} %copy.49.place_ref, s32[4,2]{1,0:T(4,128)S(1)} %get-tuple-element.177.own_ref, bf16[4,256,512]{2,1,0:T(8,128)(2,1)S(1)} %get-tuple-element.90.q_ref, bf16[2,4,2,128,512]{4,3,2,1,0:T(8,128)(2,1)} %bitcast.5.refs_0_.refs_8_, ...), custom_call_target="tpu_custom_call" | custom-call | flops 8589934592 | bytes 16777216 | tf_op jit(solution)/shard_map/attend/pallas_call | solution.py:223
  361.4 27.5 %all_to_all.35 = bf16[4,256,512]{2,1,0:T(8,128)(2,1)} all-to-all(bf16[4,256,512]{2,1,0:T(8,128)(2,1)S(1)} %get-tuple-element.92), channel_id=1, replica_groups=mesh['ctx'=8,'tp'=4] {'tp'}, dimensions={0} | all-to-all | bytes 2097152 | tf_op jit(solution)/shard_map/all_to_all | solution.py:612
  391.2 6.1 fusion.75
  401.2 11.4 collective-permute-start.14
  413.3 5.1 collective-permute-start.9
  418.4 24.1 %collective-permute-done.14.refs_6_.refs_22_ = bf16[1,4,2,128,640]{4,3,2,1,0:T(8,128)(2,1)} collective-permute-done((bf16[1,4,2,128,640]{4,3,2,1,0:T(8,128)(2,1)S(1)}, bf16[1,4,2,128,640]{4,3,2,1,0:T(8,128)(2,1)}, u32[]{:S(2)}, u32[]{:S(2)}) %collective-permute-start.14) | collective-permute-done | bytes 1310752 | tf_op jit(solution)/shard_map/ppermute | solution.py:406
  442.5 25.1 %collective-permute-done.12.refs_4_.refs_20_ = bf16[1,4,2,128,640]{4,3,2,1,0:T(8,128)(2,1)} collective-permute-done((bf16[1,4,2,128,640]{4,3,2,1,0:T(8,128)(2,1)S(1)}, bf16[1,4,2,128,640]{4,3,2,1,0:T(8,128)(2,1)}, u32[]{:S(2)}, u32[]{:S(2)}) %collective-permute-start.12) | collective-permute-done | bytes 1310752 | tf_op jit(solution)/shard_map/ppermute | solution.py:406
  472.8 20.7 %all-gather.13.cloned.1.call-done.h_ref = bf16[1024,2048]{1,0:T(8,128)(2,1)} async-done(((bf16[256,2048]{1,0:T(8,128)(2,1)}), bf16[1024,2048]{1,0:T(8,128)(2,1)}) %all-gather.13.cloned.1.call-update) | async-done | bytes 4194320 | tf_op jit(solution)/shard_map/all_gather | solution.py:541
  493.5 28.4 %mlp.1 = (bf16[1024,1408]{1,0:T(8,128)(2,1)}, bf16[1024,2816]{1,0:T(8,128)(2,1)}) custom-call(bf16[1024,2048]{1,0:T(8,128)(2,1)} %all-gather.13.cloned.1.call-done.h_ref, bf16[1024,2048]{1,0:T(8,128)(2,1)} %all-gather.11.cloned.1.call-done.dy_ref, bf16[2048,1408]{1,0:T(8,128)(2,1)} %gate_ref.1, bf16[2048,1408]{1,0:T(8,128)(2,1)} %up_ref.1, ...), custom_call_target="tpu_custom_call" | custom-call | flops 17716740096 | bytes 38273024 | tf_op jit(solution)/shard_map/mlp/pallas_call | solution.py:390
  521.9 9.7 fusion.1
  531.7 11.1 add_convert_fusion.1
  542.8 11.1 convolution_convert_fusion
  553.9 4.9 convolution_convert_fusion.3
  559.3 8.4 collective-permute-done.16
  567.7 6.5 add_convert_fusion.3
  574.6 2.9 copy-done.66
  577.5 10.8 add_convert_fusion
  597.6 8.3 convolution_convert_fusion.1
  605.9 28.8 %reduce-scatter.4.cloned.1.call-done = bf16[256,2048]{1,0:T(8,128)(2,1)} async-done(((bf16[1024,2048]{1,0:T(8,128)(2,1)}), bf16[256,2048]{1,0:T(8,128)(2,1)}) %reduce-scatter.4.cloned.1.call-update) | async-done | bytes 1048592 | tf_op jit(solution)/shard_map/reduce_scatter | solution.py:545
  645.0 6.1 convolution_convert_fusion.4
  652.2 3.5 all-to-all-start.1
  658.3 22.6 %all-to-all-done.1 = bf16[256,4,512]{2,0,1:T(8,128)(2,1)S(1)} async-done(((bf16[256,4,512]{2,0,1:T(8,128)(2,1)}), bf16[256,4,512]{2,0,1:T(8,128)(2,1)S(1)}, u32[]{:S(2)}, u32[]{:S(2)}) %all-to-all-start.1) | async-done | bytes 1048608 | tf_op jit(solution)/shard_map/all_to_all | solution.py:637
  691.0 3.7 collective-permute-done.23
  699.0 11.1 collective-permute-done.25
  722.8 24.7 %collective-permute-done.33 = bf16[176,1024]{1,0:T(8,128)(2,1)S(1)} collective-permute-done((bf16[176,1024]{1,0:T(8,128)(2,1)S(1)}, bf16[176,1024]{1,0:T(8,128)(2,1)S(1)}, u32[]{:S(2)}, u32[]{:S(2)}) %collective-permute-start.33) | collective-permute-done | bytes 360480 | tf_op jit(solution)/shard_map/ppermute | solution.py:406
  755.7 9.7 collective-permute-done.35
  765.4 3.4 maximum_select_fusion.4
  768.8 19.4 %collective-permute-done.36 = bf16[128,2816]{1,0:T(8,128)(2,1)} collective-permute-done((bf16[128,2816]{1,0:T(8,128)(2,1)}, bf16[128,2816]{1,0:T(8,128)(2,1)}, u32[]{:S(2)}, u32[]{:S(2)}) %collective-permute-start.36) | collective-permute-done | bytes 720928 | tf_op jit(solution)/shard_map/ppermute | solution.py:406
  788.2 3.3 maximum_select_fusion.5
  799.0 42.1 %query_grad.1 = bf16[4,256,512]{2,1,0:T(8,128)(2,1)S(1)} custom-call(s32[4,16]{1,0:T(4,128)S(1)} %copy.49.place_ref, s32[4,2]{1,0:T(4,128)S(1)} %get-tuple-element.177.own_ref, bf16[4,256,512]{2,1,0:T(8,128)(2,1)S(1)} %copy-done.3, bf16[4,256,512]{2,1,0:T(8,128)(2,1)S(1)} %bitcast.55, bf16[4,256,128]{2,1,0:T(8,128)(2,1)S(1)} %copy-done.17, ...), custom_call_target="tpu_custom_call" | custom-call | flops 12884901888 | bytes 16777216 | tf_op jit(solution)/shard_map/query_grad/pallas_call | solution.py:223
  841.2 4.4 fusion.76
  845.7 7.2 collective-permute-start.37
  852.8 6.9 collective-permute-start.38
  862.0 12.1 %collective-permute-start.41 = (bf16[512,1024]{1,0:T(8,128)(2,1)}, bf16[512,1024]{1,0:T(8,128)(2,1)}, u32[]{:S(2)}, u32[]{:S(2)}) collective-permute-start(bf16[512,1024]{1,0:T(8,128)(2,1)} %fusion.40), channel_id=1, source_target_pairs={{0,4},{4,0},{8,12},{12,8},{16,20},{20,16},{24,28},{28,24},{1,5},{5... | collective-permute-start | bytes 3145736 | tf_op jit(solution)/shard_map/ppermute | solution.py:406
  876.0 71.0 %key_value_grad.1 = (bf16[4,256,512]{2,1,0:T(8,128)(2,1)S(1)}, bf16[4,256,512]{2,1,0:T(8,128)(2,1)S(1)}) custom-call(s32[4,16]{1,0:T(4,128)S(1)} %copy.49.place_ref, s32[4,2]{1,0:T(4,128)S(1)} %get-tuple-element.177.own_ref, bf16[2,4,256,512]{3,2,1,0:T(8,128)(2,1)} %get-tuple-element.91.k_ref.v_ref, bf16[2,4,256,512]{3,2,1,0:T(8,128)(2,1)} %get-tuple-element.91.k_ref.v_ref, ...), custom_call_target="tpu_custom_call" | custom-call | flops 17179869184 | bytes 16777216 | tf_op jit(solution)/shard_map/key_value_grad/pallas_call | solution.py:223
  947.1 7.7 fusion.77
  954.9 11.0 fusion.67
  968.3 5.2 convolution_convert_fusion.2
  976.6 3.1 add_convert_fusion.6
  983.7 5.0 collective-permute-done.53
  991.4 3.9 collective-permute-done.55
  997.4 7.0 add_convert_fusion.2
  1006.5 3.1 maximum_select_fusion
  1011.4 4.3 maximum_select_fusion.1
  1015.7 7.9 collective-permute-done.44
  1023.8 4.5 collective-permute-done.43
  1031.2 5.3 pad_maximum_fusion.half_ref
  1038.9 10.3 collective-permute-done.45
  1049.6 3.9 fusion.66
  1054.2 5.9 collective-permute-done.47
  1060.3 5.3 collective-permute-done.48
  1070.8 18.6 %collective-permute-done.58 = bf16[128,1024]{1,0:T(8,128)(2,1)S(1)} collective-permute-done((bf16[128,1024]{1,0:T(8,128)(2,1)S(1)}, bf16[128,1024]{1,0:T(8,128)(2,1)S(1)}, u32[]{:S(2)}, u32[]{:S(2)}) %collective-permute-start.58) | collective-permute-done | bytes 262176 | tf_op jit(solution)/shard_map/ppermute | solution.py:406
  1097.0 37.9 %psum.7 = f32[14336]{0:T(1024)S(1)} all-reduce(f32[14336]{0:T(1024)S(1)} %constant_dynamic-update-slice_fusion.4), channel_id=1, replica_groups=mesh['ctx'=8,'tp'=4] {'ctx','tp'}, use_global_device_ids=true, to_apply=%region_17.18 | all-reduce | flops 14336 | bytes 114688 | tf_op jit(solution)/shard_map/psum | solution.py:672
  1136.9 3.4 unpack_cols.2
  1140.3 8.8 unpack_cols.3
  1149.1 13.6 %unpack_rows.3 = (f32[2048,1408]{1,0:T(8,128)}, f32[2048,1408]{1,0:T(8,128)}) custom-call(s32[1]{0:T(128)} %bitcast.22.core_ref, bf16[1024,2816]{1,0:T(8,128)(2,1)} %pad_maximum_fusion.half_ref, bf16[1024,2816]{1,0:T(8,128)(2,1)} %collective-permute-done.61.other_ref), custom_call_target="tpu_custom_call" | custom-call | bytes 34603008 | tf_op jit(solution)/shard_map/unpack_rows/pallas_call | solution.py:504
  1167.4 3.2 fusion.14
  1170.6 9.4 unpack_rows.2
  (392 shorter events, 154.4 us)
Async XLA Ops:
  7.2 88.9 %all-gather.9.cloned.1.call-start = ((), (), s32[]{:S(2)}) async-start(), calls=%async_computation.5 | async-start | bytes 5242880 | tf_op jit(solution)/shard_map/all_gather | solution.py:541
  12.6 112.3 %all-gather.17.cloned.1.call-start = ((), (), s32[]{:S(2)}) async-start(), calls=%async_computation.12 | async-start | bytes 1310720 | tf_op jit(solution)/shard_map/all_gather | solution.py:606
  96.2 110.5 %all-gather.11.cloned.1.call-start = ((), (), s32[]{:S(2)}) async-start(), calls=%async_computation.6 | async-start | bytes 5242880 | tf_op jit(solution)/shard_map/all_gather | solution.py:541
  113.7 277.5 %all-gather.19.cloned.1.call-start = ((), (), s32[]{:S(2)}) async-start(), calls=%async_computation.13 | async-start | bytes 9437184 | tf_op jit(solution)/shard_map/all_gather | solution.py:608
  206.7 286.8 %all-gather.13.cloned.1.call-start = ((), (), s32[]{:S(2)}) async-start(), calls=%async_computation.7 | async-start | bytes 5242880 | tf_op jit(solution)/shard_map/all_gather | solution.py:541
  206.8 77.6 %collective-permute-start.3 = (bf16[2,4,2,128,512]{4,3,2,1,0:T(8,128)(2,1)}, bf16[2,4,2,128,512]{4,3,2,1,0:T(8,128)(2,1)}, u32[]{:S(2)}, u32[]{:S(2)}) collective-permute-start(bf16[2,4,2,128,512]{4,3,2,1,0:T(8,128)(2,1)} %bitcast.5.refs_0_.refs_8_), channel_id=1, source_target_pairs={{0,16},{4,20},{8,24},{12,28},{16,0},{20,4},{24,8},{28,12},{1,17},{... | collective-permute-start | bytes 6291464 | tf_op jit(solution)/shard_map/ppermute | solution.py:406
  208.3 79.8 %collective-permute-start.1 = (bf16[2,4,2,128,512]{4,3,2,1,0:T(8,128)(2,1)}, bf16[2,4,2,128,512]{4,3,2,1,0:T(8,128)(2,1)S(1)}, u32[]{:S(2)}, u32[]{:S(2)}) collective-permute-start(bf16[2,4,2,128,512]{4,3,2,1,0:T(8,128)(2,1)} %bitcast.5.refs_0_.refs_8_), channel_id=1, source_target_pairs={{0,8},{4,12},{8,0},{12,4},{16,24},{20,28},{24,16},{28,20},{1,9},{5... | collective-permute-start | bytes 6291464 | tf_op jit(solution)/shard_map/ppermute | solution.py:406
  209.8 103.3 %collective-permute-start = (bf16[2,4,2,128,512]{4,3,2,1,0:T(8,128)(2,1)}, bf16[2,4,2,128,512]{4,3,2,1,0:T(8,128)(2,1)}, u32[]{:S(2)}, u32[]{:S(2)}) collective-permute-start(bf16[2,4,2,128,512]{4,3,2,1,0:T(8,128)(2,1)} %bitcast.5.refs_0_.refs_8_), channel_id=1, source_target_pairs={{0,4},{4,0},{8,12},{12,8},{16,20},{20,16},{24,28},{28,24},{1,5},{5... | collective-permute-start | bytes 6291464 | tf_op jit(solution)/shard_map/ppermute | solution.py:406
  285.7 26.2 %collective-permute-start.7 = (bf16[1,4,2,128,512]{4,3,2,1,0:T(8,128)(2,1)S(1)}, bf16[1,4,2,128,512]{4,3,2,1,0:T(8,128)(2,1)}, u32[]{:S(2)}, u32[]{:S(2)}) collective-permute-start(bf16[1,4,2,128,512]{4,3,2,1,0:T(8,128)(2,1)S(1)} %slice.102), channel_id=1, source_target_pairs={{0,8},{4,12},{8,0},{12,4},{16,24},{20,28},{24,16},{28,20},{1,9},{5... | collective-permute-start | bytes 3145736 | tf_op jit(solution)/shard_map/ppermute | solution.py:406
  288.2 23.7 %collective-permute-start.5 = (bf16[1,4,2,128,512]{4,3,2,1,0:T(8,128)(2,1)S(1)}, bf16[1,4,2,128,512]{4,3,2,1,0:T(8,128)(2,1)}, u32[]{:S(2)}, u32[]{:S(2)}) collective-permute-start(bf16[1,4,2,128,512]{4,3,2,1,0:T(8,128)(2,1)S(1)} %slice.101), channel_id=1, source_target_pairs={{0,16},{4,20},{8,24},{12,28},{16,0},{20,4},{24,8},{28,12},{1,17},{... | collective-permute-start | bytes 3145736 | tf_op jit(solution)/shard_map/ppermute | solution.py:406
  289.6 26.8 %collective-permute-start.4 = (bf16[2,4,2,128,512]{4,3,2,1,0:T(8,128)(2,1)}, bf16[2,4,2,128,512]{4,3,2,1,0:T(8,128)(2,1)}, u32[]{:S(2)}, u32[]{:S(2)}) collective-permute-start(bf16[2,4,2,128,512]{4,3,2,1,0:T(8,128)(2,1)} %collective-permute-done.3.refs_4_.refs_12_), channel_id=1, source_target_pairs={{0,4},{4,0},{8,12},{12,8},{16,20},{20,16},{24,28},{28,24},{1,5},{5... | collective-permute-start | bytes 6291464 | tf_op jit(solution)/shard_map/ppermute | solution.py:406
  289.6 26.8 %collective-permute-start.2 = (bf16[2,4,2,128,512]{4,3,2,1,0:T(8,128)(2,1)S(1)}, bf16[2,4,2,128,512]{4,3,2,1,0:T(8,128)(2,1)}, u32[]{:S(2)}, u32[]{:S(2)}) collective-permute-start(bf16[2,4,2,128,512]{4,3,2,1,0:T(8,128)(2,1)S(1)} %collective-permute-done.1.refs_2_.refs_10_), channel_id=1, source_target_pairs={{0,4},{4,0},{8,12},{12,8},{16,20},{20,16},{24,28},{28,24},{1,5},{5... | collective-permute-start | bytes 6291464 | tf_op jit(solution)/shard_map/ppermute | solution.py:406
  400.1 234.7 %reduce-scatter.4.cloned.1.call-start = ((), (), s32[]{:S(2)}) async-start(), calls=%async_computation.8 | async-start | bytes 5242880 | tf_op jit(solution)/shard_map/reduce_scatter | solution.py:545
  401.2 41.3 %collective-permute-start.14 = (bf16[1,4,2,128,640]{4,3,2,1,0:T(8,128)(2,1)S(1)}, bf16[1,4,2,128,640]{4,3,2,1,0:T(8,128)(2,1)}, u32[]{:S(2)}, u32[]{:S(2)}) collective-permute-start(bf16[1,4,2,128,640]{4,3,2,1,0:T(8,128)(2,1)S(1)} %bitcast.59), channel_id=1, source_target_pairs={{0,24},{4,28},{8,16},{12,20},{16,8},{20,12},{24,0},{28,4},{1,25},{... | collective-permute-start | bytes 3932168 | tf_op jit(solution)/shard_map/ppermute | solution.py:406
  412.6 54.9 %collective-permute-start.12 = (bf16[1,4,2,128,640]{4,3,2,1,0:T(8,128)(2,1)S(1)}, bf16[1,4,2,128,640]{4,3,2,1,0:T(8,128)(2,1)}, u32[]{:S(2)}, u32[]{:S(2)}) collective-permute-start(bf16[1,4,2,128,640]{4,3,2,1,0:T(8,128)(2,1)S(1)} %bitcast.60), channel_id=1, source_target_pairs={{0,16},{4,20},{8,24},{12,28},{16,0},{20,4},{24,8},{28,12},{1,17},{... | collective-permute-start | bytes 3932168 | tf_op jit(solution)/shard_map/ppermute | solution.py:406
  412.6 55.1 %collective-permute-start.10 = (bf16[1,4,2,128,640]{4,3,2,1,0:T(8,128)(2,1)S(1)}, bf16[1,4,2,128,640]{4,3,2,1,0:T(8,128)(2,1)}, u32[]{:S(2)}, u32[]{:S(2)}) collective-permute-start(bf16[1,4,2,128,640]{4,3,2,1,0:T(8,128)(2,1)S(1)} %bitcast.61), channel_id=1, source_target_pairs={{0,8},{4,12},{8,0},{12,4},{16,24},{20,28},{24,16},{28,20},{1,9},{5... | collective-permute-start | bytes 3932168 | tf_op jit(solution)/shard_map/ppermute | solution.py:406
  413.3 54.8 %collective-permute-start.9 = (bf16[1,4,2,128,640]{4,3,2,1,0:T(8,128)(2,1)S(1)}, bf16[1,4,2,128,640]{4,3,2,1,0:T(8,128)(2,1)}, u32[]{:S(2)}, u32[]{:S(2)}) collective-permute-start(bf16[1,4,2,128,640]{4,3,2,1,0:T(8,128)(2,1)S(1)} %bitcast.62), channel_id=1, source_target_pairs={{0,4},{4,0},{8,12},{12,8},{16,20},{20,16},{24,28},{28,24},{1,5},{5... | collective-permute-start | bytes 3932168 | tf_op jit(solution)/shard_map/ppermute | solution.py:406
  442.5 25.6 %collective-permute-start.15 = (bf16[1,4,2,128,640]{4,3,2,1,0:T(8,128)(2,1)}, bf16[1,4,2,128,640]{4,3,2,1,0:T(8,128)(2,1)}, u32[]{:S(2)}, u32[]{:S(2)}) collective-permute-start(bf16[1,4,2,128,640]{4,3,2,1,0:T(8,128)(2,1)} %collective-permute-done.14.refs_6_.refs_22_), channel_id=1, source_target_pairs={{0,4},{4,0},{8,12},{12,8},{16,20},{20,16},{24,28},{28,24},{1,5},{5... | collective-permute-start | bytes 3932168 | tf_op jit(solution)/shard_map/ppermute | solution.py:406
  553.9 20.7 %collective-permute-start.17 = (bf16[1024,2816]{1,0:T(8,128)(2,1)}, bf16[1024,2816]{1,0:T(8,128)(2,1)}, u32[]{:S(2)}, u32[]{:S(2)}) collective-permute-start(bf16[1024,2816]{1,0:T(8,128)(2,1)} %convolution_convert_fusion), channel_id=1, source_target_pairs={{0,4},{4,0},{8,12},{12,8},{16,20},{20,16},{24,28},{28,24},{1,5},{5... | collective-permute-start | bytes 17301512 | tf_op jit(solution)/shard_map/ppermute | solution.py:406
  558.8 8.9 collective-permute-start.16
  589.7 46.7 %collective-permute-start.19 = (bf16[352,1024]{1,0:T(8,128)(2,1)}, bf16[352,1024]{1,0:T(8,128)(2,1)}, u32[]{:S(2)}, u32[]{:S(2)}) collective-permute-start(bf16[352,1024]{1,0:T(8,128)(2,1)} %constant_dynamic-slice_fusion.13), channel_id=1, source_target_pairs={{0,16},{4,20},{8,24},{12,28},{16,0},{20,4},{24,8},{28,12},{1,17},{... | collective-permute-start | bytes 2162696 | tf_op jit(solution)/shard_map/ppermute | solution.py:406
  592.1 44.3 %collective-permute-start.18 = (bf16[352,1024]{1,0:T(8,128)(2,1)}, bf16[352,1024]{1,0:T(8,128)(2,1)S(1)}, u32[]{:S(2)}, u32[]{:S(2)}) collective-permute-start(bf16[352,1024]{1,0:T(8,128)(2,1)} %constant_dynamic-slice_fusion.14), channel_id=1, source_target_pairs={{0,8},{4,12},{8,0},{12,4},{16,24},{20,28},{24,16},{28,20},{1,9},{5... | collective-permute-start | bytes 2162696 | tf_op jit(solution)/shard_map/ppermute | solution.py:406
  594.8 44.3 %collective-permute-start.21 = (bf16[256,2816]{1,0:T(8,128)(2,1)}, bf16[256,2816]{1,0:T(8,128)(2,1)}, u32[]{:S(2)}, u32[]{:S(2)}) collective-permute-start(bf16[256,2816]{1,0:T(8,128)(2,1)} %constant_dynamic-slice_fusion.11), channel_id=1, source_target_pairs={{0,16},{4,20},{8,24},{12,28},{16,0},{20,4},{24,8},{28,12},{1,17},{... | collective-permute-start | bytes 4325384 | tf_op jit(solution)/shard_map/ppermute | solution.py:406
  597.0 44.2 %collective-permute-start.20 = (bf16[256,2816]{1,0:T(8,128)(2,1)}, bf16[256,2816]{1,0:T(8,128)(2,1)}, u32[]{:S(2)}, u32[]{:S(2)}) collective-permute-start(bf16[256,2816]{1,0:T(8,128)(2,1)} %constant_dynamic-slice_fusion.12), channel_id=1, source_target_pairs={{0,8},{4,12},{8,0},{12,4},{16,24},{20,28},{24,16},{28,20},{1,9},{5... | collective-permute-start | bytes 4325384 | tf_op jit(solution)/shard_map/ppermute | solution.py:406
  652.2 28.6 %all-to-all-start.1 = ((bf16[256,4,512]{2,0,1:T(8,128)(2,1)}), bf16[256,4,512]{2,0,1:T(8,128)(2,1)S(1)}, u32[]{:S(2)}, u32[]{:S(2)}) async-start(bf16[256,4,512]{2,0,1:T(8,128)(2,1)} %bitcast.76), calls=%async_computation.2 | async-start | bytes 2097152 | tf_op jit(solution)/shard_map/all_to_all | solution.py:637
  655.7 136.8 %all-gather.15.cloned.1.call-start = ((), (), s32[]{:S(2)}) async-start(), calls=%async_computation.9 | async-start | bytes 5242880 | tf_op jit(solution)/shard_map/all_gather | solution.py:541
  680.8 481.9 %reduce-scatter.6.cloned.1.call-start = ((), (), s32[]{:S(2)}) async-start(), calls=%async_computation.10 | async-start | bytes 5242880 | tf_op jit(solution)/shard_map/reduce_scatter | solution.py:545
  683.7 11.0 collective-permute-start.23
  685.2 10.8 collective-permute-start.22
  690.4 19.7 %collective-permute-start.25 = (bf16[128,2816]{1,0:T(8,128)(2,1)S(1)}, bf16[128,2816]{1,0:T(8,128)(2,1)S(1)}, u32[]{:S(2)}, u32[]{:S(2)}) collective-permute-start(bf16[128,2816]{1,0:T(8,128)(2,1)S(1)} %constant_dynamic-slice_fusion.7), channel_id=1, source_target_pairs={{0,8},{4,12},{8,0},{12,4},{16,24},{20,28},{24,16},{28,20},{1,9},{5... | collective-permute-start | bytes 2162696 | tf_op jit(solution)/shard_map/ppermute | solution.py:406
  694.9 19.1 %collective-permute-start.24 = (bf16[128,2816]{1,0:T(8,128)(2,1)S(1)}, bf16[128,2816]{1,0:T(8,128)(2,1)S(1)}, u32[]{:S(2)}, u32[]{:S(2)}) collective-permute-start(bf16[128,2816]{1,0:T(8,128)(2,1)S(1)} %constant_dynamic-slice_fusion.8), channel_id=1, source_target_pairs={{0,16},{4,20},{8,24},{12,28},{16,0},{20,4},{24,8},{28,12},{1,17},{... | collective-permute-start | bytes 2162696 | tf_op jit(solution)/shard_map/ppermute | solution.py:406
  696.2 51.3 %collective-permute-start.33 = (bf16[176,1024]{1,0:T(8,128)(2,1)S(1)}, bf16[176,1024]{1,0:T(8,128)(2,1)S(1)}, u32[]{:S(2)}, u32[]{:S(2)}) collective-permute-start(bf16[176,1024]{1,0:T(8,128)(2,1)S(1)} %add_convert_fusion.18), channel_id=1, source_target_pairs={{0,16},{4,20},{8,24},{12,28},{16,0},{20,4},{24,8},{28,12},{1,17},{... | collective-permute-start | bytes 1081352 | tf_op jit(solution)/shard_map/ppermute | solution.py:406
  697.2 52.1 %collective-permute-start.34 = (bf16[176,1024]{1,0:T(8,128)(2,1)S(1)}, bf16[176,1024]{1,0:T(8,128)(2,1)S(1)}, u32[]{:S(2)}, u32[]{:S(2)}) collective-permute-start(bf16[176,1024]{1,0:T(8,128)(2,1)S(1)} %add_convert_fusion.17), channel_id=1, source_target_pairs={{0,8},{4,12},{8,0},{12,4},{16,24},{20,28},{24,16},{28,20},{1,9},{5... | collective-permute-start | bytes 1081352 | tf_op jit(solution)/shard_map/ppermute | solution.py:406
  715.1 50.3 %collective-permute-start.35 = (bf16[128,2816]{1,0:T(8,128)(2,1)}, bf16[128,2816]{1,0:T(8,128)(2,1)}, u32[]{:S(2)}, u32[]{:S(2)}) collective-permute-start(bf16[128,2816]{1,0:T(8,128)(2,1)} %add_convert_fusion.12), channel_id=1, source_target_pairs={{0,16},{4,20},{8,24},{12,28},{16,0},{20,4},{24,8},{28,12},{1,17},{... | collective-permute-start | bytes 2162696 | tf_op jit(solution)/shard_map/ppermute | solution.py:406
  719.4 72.1 %collective-permute-start.31 = (bf16[1,4,2,128,640]{4,3,2,1,0:T(8,128)(2,1)}, bf16[1,4,2,128,640]{4,3,2,1,0:T(8,128)(2,1)}, u32[]{:S(2)}, u32[]{:S(2)}) collective-permute-start(bf16[1,4,2,128,640]{4,3,2,1,0:T(8,128)(2,1)} %pad_maximum_fusion.4.refs_8_.refs_24_), channel_id=1, source_target_pairs={{0,24},{4,28},{8,16},{12,20},{16,8},{20,12},{24,0},{28,4},{1,25},{... | collective-permute-start | bytes 3932168 | tf_op jit(solution)/shard_map/ppermute | solution.py:406
  721.6 70.4 %collective-permute-start.29 = (bf16[1,4,2,128,640]{4,3,2,1,0:T(8,128)(2,1)}, bf16[1,4,2,128,640]{4,3,2,1,0:T(8,128)(2,1)}, u32[]{:S(2)}, u32[]{:S(2)}) collective-permute-start(bf16[1,4,2,128,640]{4,3,2,1,0:T(8,128)(2,1)} %pad_maximum_fusion.4.refs_8_.refs_24_), channel_id=1, source_target_pairs={{0,16},{4,20},{8,24},{12,28},{16,0},{20,4},{24,8},{28,12},{1,17},{... | collective-permute-start | bytes 3932168 | tf_op jit(solution)/shard_map/ppermute | solution.py:406
  747.5 44.6 %collective-permute-start.27 = (bf16[1,4,2,128,640]{4,3,2,1,0:T(8,128)(2,1)}, bf16[1,4,2,128,640]{4,3,2,1,0:T(8,128)(2,1)}, u32[]{:S(2)}, u32[]{:S(2)}) collective-permute-start(bf16[1,4,2,128,640]{4,3,2,1,0:T(8,128)(2,1)} %pad_maximum_fusion.4.refs_8_.refs_24_), channel_id=1, source_target_pairs={{0,8},{4,12},{8,0},{12,4},{16,24},{20,28},{24,16},{28,20},{1,9},{5... | collective-permute-start | bytes 3932168 | tf_op jit(solution)/shard_map/ppermute | solution.py:406
  750.0 38.2 %collective-permute-start.36 = (bf16[128,2816]{1,0:T(8,128)(2,1)}, bf16[128,2816]{1,0:T(8,128)(2,1)}, u32[]{:S(2)}, u32[]{:S(2)}) collective-permute-start(bf16[128,2816]{1,0:T(8,128)(2,1)} %add_convert_fusion.11), channel_id=1, source_target_pairs={{0,8},{4,12},{8,0},{12,4},{16,24},{20,28},{24,16},{28,20},{1,9},{5... | collective-permute-start | bytes 2162696 | tf_op jit(solution)/shard_map/ppermute | solution.py:406
  791.5 54.1 %collective-permute-start.26 = (bf16[1,4,2,128,640]{4,3,2,1,0:T(8,128)(2,1)}, bf16[1,4,2,128,640]{4,3,2,1,0:T(8,128)(2,1)}, u32[]{:S(2)}, u32[]{:S(2)}) collective-permute-start(bf16[1,4,2,128,640]{4,3,2,1,0:T(8,128)(2,1)} %pad_maximum_fusion.4.refs_8_.refs_24_), channel_id=1, source_target_pairs={{0,4},{4,0},{8,12},{12,8},{16,20},{20,16},{24,28},{28,24},{1,5},{5... | collective-permute-start | bytes 3932168 | tf_op jit(solution)/shard_map/ppermute | solution.py:406
  791.5 54.1 %collective-permute-start.32 = (bf16[1,4,2,128,640]{4,3,2,1,0:T(8,128)(2,1)}, bf16[1,4,2,128,640]{4,3,2,1,0:T(8,128)(2,1)}, u32[]{:S(2)}, u32[]{:S(2)}) collective-permute-start(bf16[1,4,2,128,640]{4,3,2,1,0:T(8,128)(2,1)} %collective-permute-done.31.refs_14_.refs_30_), channel_id=1, source_target_pairs={{0,4},{4,0},{8,12},{12,8},{16,20},{20,16},{24,28},{28,24},{1,5},{5... | collective-permute-start | bytes 3932168 | tf_op jit(solution)/shard_map/ppermute | solution.py:406
  792.0 53.6 %collective-permute-start.30 = (bf16[1,4,2,128,640]{4,3,2,1,0:T(8,128)(2,1)}, bf16[1,4,2,128,640]{4,3,2,1,0:T(8,128)(2,1)}, u32[]{:S(2)}, u32[]{:S(2)}) collective-permute-start(bf16[1,4,2,128,640]{4,3,2,1,0:T(8,128)(2,1)} %collective-permute-done.29.refs_12_.refs_28_), channel_id=1, source_target_pairs={{0,4},{4,0},{8,12},{12,8},{16,20},{20,16},{24,28},{28,24},{1,5},{5... | collective-permute-start | bytes 3932168 | tf_op jit(solution)/shard_map/ppermute | solution.py:406
  792.1 53.6 %collective-permute-start.28 = (bf16[1,4,2,128,640]{4,3,2,1,0:T(8,128)(2,1)}, bf16[1,4,2,128,640]{4,3,2,1,0:T(8,128)(2,1)}, u32[]{:S(2)}, u32[]{:S(2)}) collective-permute-start(bf16[1,4,2,128,640]{4,3,2,1,0:T(8,128)(2,1)} %collective-permute-done.27.refs_10_.refs_26_), channel_id=1, source_target_pairs={{0,4},{4,0},{8,12},{12,8},{16,20},{20,16},{24,28},{28,24},{1,5},{5... | collective-permute-start | bytes 3932168 | tf_op jit(solution)/shard_map/ppermute | solution.py:406
  792.5 372.7 %reduce-scatter.8.cloned.1.call-start = ((), (), s32[]{:S(2)}) async-start(), calls=%async_computation.11 | async-start | bytes 5242880 | tf_op jit(solution)/shard_map/reduce_scatter | solution.py:545
  845.7 101.4 %collective-permute-start.37 = (bf16[352,1024]{1,0:T(8,128)(2,1)}, bf16[352,1024]{1,0:T(8,128)(2,1)}, u32[]{:S(2)}, u32[]{:S(2)}) collective-permute-start(bf16[352,1024]{1,0:T(8,128)(2,1)} %maximum_select_fusion.10), channel_id=1, source_target_pairs={{0,8},{4,12},{8,0},{12,4},{16,24},{20,28},{24,16},{28,20},{1,9},{5... | collective-permute-start | bytes 2162696 | tf_op jit(solution)/shard_map/ppermute | solution.py:406
  852.8 94.2 %collective-permute-start.38 = (bf16[352,1024]{1,0:T(8,128)(2,1)S(1)}, bf16[352,1024]{1,0:T(8,128)(2,1)}, u32[]{:S(2)}, u32[]{:S(2)}) collective-permute-start(bf16[352,1024]{1,0:T(8,128)(2,1)S(1)} %copy-done.40), channel_id=1, source_target_pairs={{0,16},{4,20},{8,24},{12,28},{16,0},{20,4},{24,8},{28,12},{1,17},{... | collective-permute-start | bytes 2162696 | tf_op jit(solution)/shard_map/ppermute | solution.py:406
  862.0 85.1 %collective-permute-start.41 = (bf16[512,1024]{1,0:T(8,128)(2,1)}, bf16[512,1024]{1,0:T(8,128)(2,1)}, u32[]{:S(2)}, u32[]{:S(2)}) collective-permute-start(bf16[512,1024]{1,0:T(8,128)(2,1)} %fusion.40), channel_id=1, source_target_pairs={{0,4},{4,0},{8,12},{12,8},{16,20},{20,16},{24,28},{28,24},{1,5},{5... | collective-permute-start | bytes 3145736 | tf_op jit(solution)/shard_map/ppermute | solution.py:406
  874.1 73.0 %collective-permute-start.39 = (bf16[256,2816]{1,0:T(8,128)(2,1)}, bf16[256,2816]{1,0:T(8,128)(2,1)}, u32[]{:S(2)}, u32[]{:S(2)}) collective-permute-start(bf16[256,2816]{1,0:T(8,128)(2,1)} %maximum_select_fusion.4), channel_id=1, source_target_pairs={{0,8},{4,12},{8,0},{12,4},{16,24},{20,28},{24,16},{28,20},{1,9},{5... | collective-permute-start | bytes 4325384 | tf_op jit(solution)/shard_map/ppermute | solution.py:406
  875.7 71.4 %collective-permute-start.40 = (bf16[256,2816]{1,0:T(8,128)(2,1)}, bf16[256,2816]{1,0:T(8,128)(2,1)}, u32[]{:S(2)}, u32[]{:S(2)}) collective-permute-start(bf16[256,2816]{1,0:T(8,128)(2,1)} %maximum_select_fusion.5), channel_id=1, source_target_pairs={{0,16},{4,20},{8,24},{12,28},{16,0},{20,4},{24,8},{28,12},{1,17},{... | collective-permute-start | bytes 4325384 | tf_op jit(solution)/shard_map/ppermute | solution.py:406
  973.6 23.9 %collective-permute-start.42 = (bf16[1024,1536]{1,0:T(8,128)(2,1)}, bf16[1024,1536]{1,0:T(8,128)(2,1)}, u32[]{:S(2)}, u32[]{:S(2)}) collective-permute-start(bf16[1024,1536]{1,0:T(8,128)(2,1)} %convolution_convert_fusion.2), channel_id=1, source_target_pairs={{0,4},{4,0},{8,12},{12,8},{16,20},{20,16},{24,28},{28,24},{1,5},{5... | collective-permute-start | bytes 9437192 | tf_op jit(solution)/shard_map/ppermute | solution.py:406
  979.9 8.8 collective-permute-start.53
  990.9 149.3 %collective-permute-start.62 = (bf16[1408,1024]{1,0:T(8,128)(2,1)S(1)}, bf16[1408,1024]{1,0:T(8,128)(2,1)}, u32[]{:S(2)}, u32[]{:S(2)}) collective-permute-start(bf16[1408,1024]{1,0:T(8,128)(2,1)S(1)} %pad_maximum_fusion.2.half_ref), channel_id=1, source_target_pairs={{0,4},{4,0},{8,12},{12,8},{16,20},{20,16},{24,28},{28,24},{1,5},{5... | collective-permute-start | bytes 8650760 | tf_op jit(solution)/shard_map/ppermute | solution.py:406
  997.0 68.9 %collective-permute-start.56 = (bf16[64,1024]{1,0:T(8,128)(2,1)S(1)}, bf16[64,1024]{1,0:T(8,128)(2,1)}, u32[]{:S(2)}, u32[]{:S(2)}) collective-permute-start(bf16[64,1024]{1,0:T(8,128)(2,1)S(1)} %add_convert_fusion.22), channel_id=1, source_target_pairs={{0,16},{4,20},{8,24},{12,28},{16,0},{20,4},{24,8},{28,12},{1,17},{... | collective-permute-start | bytes 393224 | tf_op jit(solution)/shard_map/ppermute | solution.py:406
  1004.7 18.9 %collective-permute-start.44 = (bf16[256,1536]{1,0:T(8,128)(2,1)S(1)}, bf16[256,1536]{1,0:T(8,128)(2,1)S(1)}, u32[]{:S(2)}, u32[]{:S(2)}) collective-permute-start(bf16[256,1536]{1,0:T(8,128)(2,1)S(1)} %constant_dynamic-slice_fusion.5), channel_id=1, source_target_pairs={{0,16},{4,20},{8,24},{12,28},{16,0},{20,4},{24,8},{28,12},{1,17},{... | collective-permute-start | bytes 2359304 | tf_op jit(solution)/shard_map/ppermute | solution.py:406
  1009.6 18.6 %collective-permute-start.43 = (bf16[256,1536]{1,0:T(8,128)(2,1)S(1)}, bf16[256,1536]{1,0:T(8,128)(2,1)S(1)}, u32[]{:S(2)}, u32[]{:S(2)}) collective-permute-start(bf16[256,1536]{1,0:T(8,128)(2,1)S(1)} %constant_dynamic-slice_fusion.6), channel_id=1, source_target_pairs={{0,8},{4,12},{8,0},{12,4},{16,24},{20,28},{24,16},{28,20},{1,9},{5... | collective-permute-start | bytes 2359304 | tf_op jit(solution)/shard_map/ppermute | solution.py:406
  1029.4 9.4 collective-permute-start.46
  1036.5 112.6 %collective-permute-start.61 = (bf16[1024,2816]{1,0:T(8,128)(2,1)}, bf16[1024,2816]{1,0:T(8,128)(2,1)}, u32[]{:S(2)}, u32[]{:S(2)}) collective-permute-start(bf16[1024,2816]{1,0:T(8,128)(2,1)} %pad_maximum_fusion.half_ref), channel_id=1, source_target_pairs={{0,4},{4,0},{8,12},{12,8},{16,20},{20,16},{24,28},{28,24},{1,5},{5... | collective-permute-start | bytes 17301512 | tf_op jit(solution)/shard_map/ppermute | solution.py:406
  1037.6 11.5 collective-permute-start.45
  1049.3 10.8 collective-permute-start.47
  1053.5 12.0 %collective-permute-start.48 = (bf16[128,1536]{1,0:T(8,128)(2,1)S(1)}, bf16[128,1536]{1,0:T(8,128)(2,1)S(1)}, u32[]{:S(2)}, u32[]{:S(2)}) collective-permute-start(bf16[128,1536]{1,0:T(8,128)(2,1)S(1)} %add_convert_fusion.15), channel_id=1, source_target_pairs={{0,8},{4,12},{8,0},{12,4},{16,24},{20,28},{24,16},{28,20},{1,9},{5... | collective-permute-start | bytes 1179656 | tf_op jit(solution)/shard_map/ppermute | solution.py:406
  1065.7 25.6 %collective-permute-start.49 = (bf16[256,1536]{1,0:T(8,128)(2,1)S(1)}, bf16[256,1536]{1,0:T(8,128)(2,1)S(1)}, u32[]{:S(2)}, u32[]{:S(2)}) collective-permute-start(bf16[256,1536]{1,0:T(8,128)(2,1)S(1)} %maximum_select_fusion.8), channel_id=1, source_target_pairs={{0,8},{4,12},{8,0},{12,4},{16,24},{20,28},{24,16},{28,20},{1,9},{5... | collective-permute-start | bytes 2359304 | tf_op jit(solution)/shard_map/ppermute | solution.py:406
  1068.2 21.2 %collective-permute-start.58 = (bf16[128,1024]{1,0:T(8,128)(2,1)S(1)}, bf16[128,1024]{1,0:T(8,128)(2,1)S(1)}, u32[]{:S(2)}, u32[]{:S(2)}) collective-permute-start(bf16[128,1024]{1,0:T(8,128)(2,1)S(1)} %maximum_select_fusion.14), channel_id=1, source_target_pairs={{0,8},{4,12},{8,0},{12,4},{16,24},{20,28},{24,16},{28,20},{1,9},{5... | collective-permute-start | bytes 786440 | tf_op jit(solution)/shard_map/ppermute | solution.py:406
  1069.0 22.9 %collective-permute-start.50 = (bf16[256,1536]{1,0:T(8,128)(2,1)S(1)}, bf16[256,1536]{1,0:T(8,128)(2,1)S(1)}, u32[]{:S(2)}, u32[]{:S(2)}) collective-permute-start(bf16[256,1536]{1,0:T(8,128)(2,1)S(1)} %maximum_select_fusion.9), channel_id=1, source_target_pairs={{0,16},{4,20},{8,24},{12,28},{16,0},{20,4},{24,8},{28,12},{1,17},{... | collective-permute-start | bytes 2359304 | tf_op jit(solution)/shard_map/ppermute | solution.py:406
  1094.4 76.2 %collective-permute-start.51 = (bf16[1024,1536]{1,0:T(8,128)(2,1)}, bf16[1024,1536]{1,0:T(8,128)(2,1)}, u32[]{:S(2)}, u32[]{:S(2)}) collective-permute-start(bf16[1024,1536]{1,0:T(8,128)(2,1)} %pad_maximum_fusion.1.half_ref), channel_id=1, source_target_pairs={{0,4},{4,0},{8,12},{12,8},{16,20},{20,16},{24,28},{28,24},{1,5},{5... | collective-permute-start | bytes 9437192 | tf_op jit(solution)/shard_map/ppermute | solution.py:406
  1097.0 40.0 %collective-permute-start.60 = (bf16[512,1024]{1,0:T(8,128)(2,1)}, bf16[512,1024]{1,0:T(8,128)(2,1)}, u32[]{:S(2)}, u32[]{:S(2)}) collective-permute-start(bf16[512,1024]{1,0:T(8,128)(2,1)} %pad_maximum_fusion.5.half_ref), channel_id=1, source_target_pairs={{0,4},{4,0},{8,12},{12,8},{16,20},{20,16},{24,28},{28,24},{1,5},{5... | collective-permute-start | bytes 3145736 | tf_op jit(solution)/shard_map/ppermute | solution.py:406
  (83 other events, 949.1 us)
Sparse Core Ops, SparseCore 0:
  12.7 83.4 all-gather.8
  98.3 26.4 all-gather.16
  126.4 80.2 all-gather.10
  208.4 88.5 all-gather.18
  400.2 93.2 all-gather.12
  559.4 75.2 reduce-scatter.3
  681.0 79.4 all-gather.14
  792.7 74.4 reduce-scatter.5
  997.6 75.5 reduce-scatter.7

commit v3 on v2

--- a/solution.py
+++ b/solution.py
@@ -431,46 +431,48 @@
 
     got = ctx_swap(part(1 - core).astype(BF16), 1)
     gate = yield [got]
-    half = (part(core) + got.astype(F32)).astype(BF16)
+    half = (part(core) + after(got, gate).astype(F32)).astype(BF16)
     bits = list(range(1, int(math.log2(lax.axis_size("ctx")))))
     orders = [bits, bits[::-1]]
     r = half.shape[0] // 2
     streams = [half[:r], half[r:]]
+    yield streams
     for i in range(len(bits)):
-        streams = after(streams, gate)
         got = [ctx_swap(half_of(x, o[i], False), 1 << o[i]) for x, o in zip(streams, orders)]
         gate = yield got
+        streams, got = after((streams, got), gate)
         streams = [add16(half_of(x, o[i], True), g) for x, o, g in zip(streams, orders, got)]
+        yield streams
     for i in reversed(range(len(bits))):
-        streams = after(streams, gate)
         got = [ctx_swap(x, 1 << o[i]) for x, o in zip(streams, orders)]
         gate = yield got
+        streams, got = after((streams, got), gate)
         streams = [
             jnp.where(((lax.axis_index("ctx") >> o[i]) & 1) == 0, jnp.concatenate([x, g]), jnp.concatenate([g, x]))
             for x, o, g in zip(streams, orders, got)
         ]
-    half = after(jnp.concatenate(streams), gate)
-    other = ctx_swap(half, 1)
-    yield [other]
-    yield half, other
-
-
-def advance(chains, gate=None):
-    fly = []
-    for chain in chains:
-        fly += chain.send(gate)
-    return fly
+        if i == 0:
+            streams = jnp.concatenate(streams)
+        yield streams
+    other = ctx_swap(streams, 1)
+    gate = yield [other]
+    yield after((streams, other), gate)
+
+
+def advance(chain, gate=None):
+    held = chain.send(gate)
+    next(chain)
+    return held
 
 
 def begin(*args):
     chain = weight_grad(*args)
-    return chain, next(chain)
-
-
-def finish(chain):
-    for got in chain:
-        pass
-    return got
+    next(chain)
+    return chain
+
+
+def finish(chain, gate=None):
+    return chain.send(gate)
 
 
 def unpack_rows_kernel(core_ref, half_ref, other_ref, *out_refs):
@@ -600,12 +602,13 @@
     bias = jnp.stack([query_b, key_bias, value_b])
     q, kv = project(rows_one, query_w, key_w, value_w, bias, tabs)
     keys, values = gather_pair(kv.reshape(2, SEQS, 2, BLK, width))
+    arrived = [e[0] for e in keys + values]
 
     rows_w = output_w.shape[0] // n_ctx
     part = lax.dynamic_slice_in_dim(output_w, ctx * rows_w, rows_w, 0)
     part = lax.all_gather(after(part, rows_one), "tp", axis=0)
     dy_rows = all_rows(after(cotangent, kv))
-    whole_w = lax.all_gather(after(part, dy_rows), "ctx", axis=1).reshape(n_tp * output_w.shape[0], -1)
+    whole_w = lax.all_gather(after(part, dy_rows, arrived), "ctx", axis=1).reshape(n_tp * output_w.shape[0], -1)
 
     attn, q_ext = attend(place, own, q, keys, values)
     attn_rows = attn.reshape(-1, width)
@@ -622,18 +625,18 @@
     part_two = (nt(grad_gu[:, :ff], gate_w) + nt(grad_gu[:, ff:], up_w)).astype(BF16)
     grad_two = sum_rows(part_two)
     act, rows_two, dy_rows, grad_gu = after((act, rows_two, dy_rows, grad_gu), part_two)
-    down_chain, fly = begin(act, dy_rows, False)
-    gu_chain, more = begin(rows_two, grad_gu, True)
+    extra = 2 * int(math.log2(n_ctx)) - 6
+    gu = begin(rows_two, grad_gu, True)
     down = nn(act, down_w).astype(BF16)
-    fly = advance([down_chain, gu_chain], fly + more)
-    grad_two = after(grad_two, fly, down)
+    held = advance(gu)
+    dw = begin(act, after(dy_rows, held), False)
+    held = advance(dw), advance(gu)
+    grad_two = after(grad_two, held, down)
 
     norm_two, grad_gain_two, grad_shift_two = layer_back(grad_two, unit_two, inverse_two, gain_two)
     grad_mixed = cotangent.astype(F32) + norm_two
     branch_own = grad_mixed.astype(BF16)
     grad_attn = nt(branch_own, whole_w).astype(BF16)
-    for _ in range(int(math.log2(n_ctx)) - 2):
-        fly = advance([down_chain, gu_chain])
     grad_attn = lax.all_to_all(grad_attn, "tp", split_axis=1, concat_axis=0, tiled=True)
     branch = all_rows(after(branch_own, grad_attn))
     out_tokens = (mixed + sum_rows(after(down, branch))).astype(BF16)
@@ -642,24 +645,21 @@
     delta = lax.dot_general(grad_attn.astype(F32) * attn_rows.astype(F32), ind, (((1,), (0,)), ((), ())),
                             precision=lax.Precision.HIGHEST, preferred_element_type=F32)
     do_ext = terms(-delta, lane).astype(BF16)
+    held = advance(gu), advance(dw)
     grads = gather_ctx(jnp.concatenate([grad_attn, do_ext], axis=1).reshape(shape))
-    grad_attn = after(grad_attn, fly)
-    fly = advance([down_chain, gu_chain])
+    grad_attn = after(grad_attn, held)
     grad_q = query_grad(place, own, q, grad_attn.reshape(q.shape), q_ext, do_ext.reshape(q_ext.shape), tabs, keys, values)
     grad_q = grad_q.reshape(-1, width)
     q_part = nt(grad_q, query_w)
-    branch, grads = after((branch, grads), fly, q_part)
-    for _ in range(int(math.log2(n_ctx)) - 2):
-        fly = advance([down_chain, gu_chain], grads)
-    out_chain, more = begin(attn_rows, branch, False)
-    grad_k, grad_v = key_value_grad(place, own, kv, tabs, [(x, 0) for x in queries], [(x, 0) for x in grads])
-    grad_k, grad_v = after((grad_k, grad_v), fly, more)
+    grads = after(grads, q_part)
+    held = [advance(gu, grads) for _ in range(1 + extra)] + [advance(dw, grads)]
+    grad_k, grad_v = key_value_grad(place, own, kv, tabs, [(x, 0) for x in queries], [(x, 0) for x in after(grads, held)])
     grad_k, grad_v = (g.reshape(-1, width) for g in (grad_k, grad_v))
     part_one = q_part + nt(grad_k, key_w) + nt(grad_v, value_w)
     part_sent = part_one.astype(BF16)
     grad_one = sum_rows(part_sent)
 
-    rows_one, grad_q, grad_k, grad_v = after((rows_one, grad_q, grad_k, grad_v), part_sent)
+    rows_one, branch, grad_q, grad_k, grad_v = after((rows_one, branch, grad_q, grad_k, grad_v), part_sent)
     unit_rows = (rows_one.astype(F32) - shift_one) / gain_one
     grad_qkv = jnp.concatenate([grad_q, grad_k, grad_v], axis=1)
     bias_grad = jnp.sum(grad_qkv.astype(F32), axis=0)
@@ -667,15 +667,30 @@
     small = jnp.concatenate([
         jnp.sum(part_one * unit_rows, axis=0), jnp.sum(part_one, axis=0), grad_gain_two, grad_shift_two,
         jnp.where(tp_row, bias_grad[None, :], 0.0).reshape(-1)])
-    qkv_chain, more = begin(rows_one, grad_qkv, True)
-    fly = advance([down_chain, gu_chain, out_chain])
-    small = lax.psum(small, ("ctx", "tp"))
+    qkv = begin(rows_one, grad_qkv, True)
+    for _ in range(1 + extra):
+        advance(dw, part_sent)
+    out = begin(attn_rows, branch, False)
+    held = advance(qkv)
+    advance(gu, held)
+    held = advance(out, held)
+    small = lax.psum(after(small, held), ("ctx", "tp"))
     depth = x.shape[1]
     norms = small[:4 * depth].reshape(4, depth)
     bias_sum = jnp.sum(jnp.where(tp_row, small[4 * depth:].reshape(n_tp, -1), 0.0), axis=0)
-    grad_gate_w, grad_up_w = unpack_rows(*finish(gu_chain), 2)
-    grad_query_w, grad_key_w, grad_value_w = unpack_rows(*finish(qkv_chain), 3)
-    grad_down_w, grad_output_w = unpack_cols(*finish(down_chain)), unpack_cols(*finish(out_chain))
+    advance(qkv, small)
+    advance(dw, small)
+    grad_gate_w, grad_up_w = unpack_rows(*finish(gu), 2)
+    held = advance(out), advance(qkv, (grad_gate_w, grad_up_w))
+    grad_down_w = unpack_cols(*finish(dw, held))
+    for _ in range(1 + extra):
+        advance(out)
+        advance(qkv, grad_down_w)
+    advance(qkv)
+    for _ in range(2):
+        advance(out)
+    grad_output_w = unpack_cols(*finish(out))
+    grad_query_w, grad_key_w, grad_value_w = unpack_rows(*finish(qkv), 3)
     norm_one, _, _ = layer_back(grad_one, unit_one, inverse_one, gain_one)
     grad_tokens = (grad_mixed + norm_one).astype(BF16)
     return (

time: 1190 us -> 1070 us (0.90)
  waiting for transfers between devices: 555 us -> 382 us
  local copies, waits for them, and re-layouts: 36.2 us -> 56.8 us
  other arithmetic: 76.1 us -> 90.9 us
  blocking collectives: 65.4 us -> 80 us
  starting transfers between devices: 90.6 us -> 77.3 us
    all_gather x4, waiting for transfers between devices: 185 us -> 113 us  [all_rows(): return lax.all_gather(x, 'tp', axis=0, tiled=True)]
    ppermute x63, waiting for transfers between devices: 307 us -> 248 us  [ctx_swap(): return lax.ppermute(x, 'ctx', [(i, i ^ mask) for i in range(n)])]
    reduce_scatter x3, waiting for transfers between devices: 28.9 us -> 2.98 us  [sum_rows(): lax.psum_scatter(x, 'tp', scatter_dimension=0, tiled=True).astype(F32)]
    convert_element_type x0 -> x3, other arithmetic: none -> 17.2 us  [weight_grad(): half = (part(core) + after(got, gate).astype(F32)).astype(BF16)]
    pallas_call x3, Pallas kernels: 156 us -> 172 us  [attention_call(): pl.pallas_call(kernel, grid_spec=pltpu.PrefetchScalarGridSpec(num_scalar_...]
    ppermute x63, starting transfers between devices: 86.8 us -> 72.8 us  [ctx_swap(): return lax.ppermute(x, 'ctx', [(i, i ^ mask) for i in range(n)])]
    psum x1, blocking collectives: 37.9 us -> 50.5 us  [local(): small = lax.psum(after(small, held), ('ctx', 'tp'))]
    unnamed x155 -> x177, local copies, waits for them, and re-layouts: 17.2 us -> 25.2 us
  transfers between devices with their start and end apart: 73 -> 73, of which waited for: 37 -> 31; matrix products, arithmetic and copies ran while one was open for 13% -> 19% of each run, Pallas kernels for 16% -> 19%
where the time goes in v3:
time: 1070 us; the launch traced here: 1060 us
  waiting for transfers between devices  382 us (36%)
  Pallas kernels  242 us (23%)
  matrix products  120 us (11%)
  other arithmetic  90.9 us (8%)
  blocking collectives  80 us (7%)
  starting transfers between devices  77.3 us (7%)
  local copies, waits for them, and re-layouts  56.8 us (5%)
  between operations  15.4 us (1%)
    ppermute x63, waiting for transfers between devices, ctx_swap(): return lax.ppermute(x, 'ctx', [(i, i ^ mask) for i in range(n)])  248 us
    pallas_call x3, Pallas kernels, attention_call(): pl.pallas_call(kernel, grid_spec=pltpu.PrefetchScalarGridSpec(num_scalar_...  172 us
    all_gather x4, waiting for transfers between devices, all_rows(): return lax.all_gather(x, 'tp', axis=0, tiled=True)  113 us
    ppermute x63, starting transfers between devices, ctx_swap(): return lax.ppermute(x, 'ctx', [(i, i ^ mask) for i in range(n)])  72.8 us
    dot_general x8, matrix products, rc(): lax.dot_general(left, right, (((0,), (0,)), ((), ())), preferred_element_...  51.7 us
    psum x1, blocking collectives, local(): small = lax.psum(after(small, held), ('ctx', 'tp'))  50.5 us
    dot_general x6, matrix products, nt(): lax.dot_general(a, b, (((1,), (1,)), ((), ())), preferred_element_type=jn...  49.7 us
    all_to_all x1, blocking collectives, local(): lax.all_to_all(attn_rows, 'tp', split_axis=0, concat_axis=1, tiled=True)  29.5 us
  transfers between devices with their start and end apart: 73, of which 31 were waited for; matrix products, arithmetic and copies ran while one was open for 19% of the time, Pallas kernels for 19%

profile of v3, /device:TPU:0, one launch (start us, length us, event | category | flops | bytes accessed | tf_op | source)
XLA Modules:
  0.0 1064.1 jit_solution(5705772405462918808)
XLA Ops:
  13.4 82.8 %all-gather.9.cloned.1.call-done.h_ref = bf16[1024,2048]{1,0:T(8,128)(2,1)} async-done(((bf16[256,2048]{1,0:T(8,128)(2,1)}), bf16[1024,2048]{1,0:T(8,128)(2,1)}) %all-gather.9.cloned.1.call-update) | async-done | bytes 4194320 | tf_op jit(solution)/shard_map/all_gather | solution.py:543
  102.1 10.9 %project.1 = (bf16[4,256,512]{2,1,0:T(8,128)(2,1)S(1)}, bf16[2,4,256,512]{3,2,1,0:T(8,128)(2,1)S(1)}) custom-call(bf16[1024,2048]{1,0:T(8,128)(2,1)} %all-gather.9.cloned.1.call-done.h_ref, bf16[2048,512]{1,0:T(8,128)(2,1)} %wq_ref.1, bf16[2048,512]{1,0:T(8,128)(2,1)} %wk_ref.1, bf16[2048,512]{1,0:T(8,128)(2,1)} %wv_ref.1, ...), custom_call_target="tpu_custom_call" | custom-call | flops 6442450944 | bytes 6291456 | tf_op jit(solution)/shard_map/project/pallas_call | solution.py:350
  117.4 44.6 %collective-permute-done.1.refs_2_.refs_10_ = bf16[2,4,2,128,512]{4,3,2,1,0:T(8,128)(2,1)S(1)} collective-permute-done((bf16[2,4,2,128,512]{4,3,2,1,0:T(8,128)(2,1)}, bf16[2,4,2,128,512]{4,3,2,1,0:T(8,128)(2,1)S(1)}, u32[]{:S(2)}, u32[]{:S(2)}) %collective-permute-start.1) | collective-permute-done | bytes 2097184 | tf_op jit(solution)/shard_map/ppermute | solution.py:406
  167.0 19.3 %collective-permute-done.5.refs_6_ = bf16[1,4,2,128,512]{4,3,2,1,0:T(8,128)(2,1)} collective-permute-done((bf16[1,4,2,128,512]{4,3,2,1,0:T(8,128)(2,1)S(1)}, bf16[1,4,2,128,512]{4,3,2,1,0:T(8,128)(2,1)}, u32[]{:S(2)}, u32[]{:S(2)}) %collective-permute-start.5) | collective-permute-done | bytes 1048608 | tf_op jit(solution)/shard_map/ppermute | solution.py:406
  186.3 2.6 collective-permute-done.7.refs_14_
  189.3 2.6 collective-permute-done.8.refs_15_
  191.9 14.8 %all-gather.11.cloned.1.call-done.dy_ref = bf16[1024,2048]{1,0:T(8,128)(2,1)} async-done(((bf16[256,2048]{1,0:T(8,128)(2,1)}), bf16[1024,2048]{1,0:T(8,128)(2,1)}) %all-gather.11.cloned.1.call-update) | async-done | bytes 4194320 | tf_op jit(solution)/shard_map/all_gather | solution.py:543
  210.6 64.0 %attend.1 = (bf16[4,256,512]{2,1,0:T(8,128)(2,1)S(1)}, bf16[4,256,128]{2,1,0:T(8,128)(2,1)S(1)}) custom-call(s32[4,16]{1,0:T(4,128)S(1)} %copy.49.place_ref, s32[4,2]{1,0:T(4,128)S(1)} %get-tuple-element.275.own_ref, bf16[4,256,512]{2,1,0:T(8,128)(2,1)S(1)} %get-tuple-element.139.q_ref, bf16[2,4,2,128,512]{4,3,2,1,0:T(8,128)(2,1)S(1)} %bitcast.74, ...), custom_call_target="tpu_custom_call" | custom-call | flops 8589934592 | bytes 16777216 | tf_op jit(solution)/shard_map/attend/pallas_call | solution.py:223
  275.4 29.5 %all_to_all.35 = bf16[4,256,512]{2,1,0:T(8,128)(2,1)} all-to-all(bf16[4,256,512]{2,1,0:T(8,128)(2,1)S(1)} %get-tuple-element.141), channel_id=1, replica_groups=mesh['ctx'=8,'tp'=4] {'tp'}, dimensions={0} | all-to-all | bytes 2097152 | tf_op jit(solution)/shard_map/all_to_all | solution.py:615
  307.2 6.2 fusion.69
  317.4 3.4 collective-permute-start.14
  320.8 28.3 %collective-permute-done.10.refs_2_.refs_18_ = bf16[1,4,2,128,640]{4,3,2,1,0:T(8,128)(2,1)} collective-permute-done((bf16[1,4,2,128,640]{4,3,2,1,0:T(8,128)(2,1)S(1)}, bf16[1,4,2,128,640]{4,3,2,1,0:T(8,128)(2,1)}, u32[]{:S(2)}, u32[]{:S(2)}) %collective-permute-start.10) | collective-permute-done | bytes 1310752 | tf_op jit(solution)/shard_map/ppermute | solution.py:406
  349.2 24.1 %collective-permute-done.12.refs_4_.refs_20_ = bf16[1,4,2,128,640]{4,3,2,1,0:T(8,128)(2,1)} collective-permute-done((bf16[1,4,2,128,640]{4,3,2,1,0:T(8,128)(2,1)S(1)}, bf16[1,4,2,128,640]{4,3,2,1,0:T(8,128)(2,1)}, u32[]{:S(2)}, u32[]{:S(2)}) %collective-permute-start.12) | collective-permute-done | bytes 1310752 | tf_op jit(solution)/shard_map/ppermute | solution.py:406
  373.8 2.9 collective-permute-done.13.refs_5_.refs_21_
  378.5 15.8 %all-gather.13.cloned.1.call-done.h_ref = bf16[1024,2048]{1,0:T(8,128)(2,1)} async-done(((bf16[256,2048]{1,0:T(8,128)(2,1)}), bf16[1024,2048]{1,0:T(8,128)(2,1)}) %all-gather.13.cloned.1.call-update) | async-done | bytes 4194320 | tf_op jit(solution)/shard_map/all_gather | solution.py:543
  394.3 28.4 %mlp.1 = (bf16[1024,1408]{1,0:T(8,128)(2,1)}, bf16[1024,2816]{1,0:T(8,128)(2,1)}) custom-call(bf16[1024,2048]{1,0:T(8,128)(2,1)} %all-gather.13.cloned.1.call-done.h_ref, bf16[1024,2048]{1,0:T(8,128)(2,1)} %all-gather.11.cloned.1.call-done.dy_ref, bf16[2048,1408]{1,0:T(8,128)(2,1)} %gate_ref.1, bf16[2048,1408]{1,0:T(8,128)(2,1)} %up_ref.1, ...), custom_call_target="tpu_custom_call" | custom-call | flops 17716740096 | bytes 38273024 | tf_op jit(solution)/shard_map/mlp/pallas_call | solution.py:390
  422.7 9.7 fusion.1
  432.5 11.1 %add_convert_fusion.1 = bf16[1024,2048]{1,0:T(8,128)(2,1)} fusion(f32[1024,2048]{1,0:T(8,128)S(1)} %fusion.1, bf16[2048,1408]{1,0:T(8,128)(2,1)} %up_ref.1, bf16[1024,2816]{1,0:T(8,128)(2,1)S(1)} %copy-done.80), kind=kOutput, calls=%fused_computation.3 | convolution fusion | flops 5909774336 | bytes 21233664 | tf_op jit(solution)/shard_map/dot_general | solution.py:15
  443.5 11.0 %convolution_convert_fusion = bf16[1024,2816]{1,0:T(8,128)(2,1)} fusion(bf16[1024,2816]{1,0:T(8,128)(2,1)} %get-tuple-element.154, bf16[1024,2048]{1,0:T(8,128)(2,1)} %all-gather.13.cloned.1.call-done.h_ref, s32[]{:T(128)S(6)} %select_n.267), kind=kOutput, calls=%fused_computation.8 | convolution fusion | flops 5908463616 | bytes 13631492 | tf_op jit(solution)/shard_map/dot_general | solution.py:290
  454.5 12.3 %fusion.32 = f32[1024,2816]{1,0:T(8,128)} fusion(bf16[1024,2816]{1,0:T(8,128)(2,1)} %get-tuple-element.154, bf16[1024,2048]{1,0:T(8,128)(2,1)} %all-gather.13.cloned.1.call-done.h_ref, s32[]{:T(128)S(6)} %select_n.266), kind=kOutput, calls=%fused_computation.60 | convolution fusion | flops 5905580032 | bytes 19398660 | tf_op jit(solution)/shard_map/dot_general | solution.py:290
  466.9 9.7 add_convert_fusion
  476.6 3.1 fusion.63
  485.3 10.8 %convolution_convert_fusion.1 = bf16[1024,2048]{1,0:T(8,128)(2,1)} fusion(bf16[1024,1408]{1,0:T(8,128)(2,1)S(1)} %copy-done.81, bf16[1408,2048]{1,0:T(8,128)(2,1)} %down_ref.1), kind=kOutput, calls=%fused_computation.9 | convolution fusion | flops 5907677184 | bytes 12845056 | tf_op jit(solution)/shard_map/dot_general | solution.py:19
  496.1 7.4 convolution_convert_fusion.3
  503.5 5.2 fusion.29
  508.7 6.7 collective-permute-done.18
  527.2 3.0 reduce-scatter.4.cloned.1.call-done
  531.6 4.6 add_convert_fusion.3
  542.1 6.1 convolution_convert_fusion.4
  549.3 4.2 all-to-all-start.1
  562.0 17.2 %all-to-all-done.1 = bf16[256,4,512]{2,0,1:T(8,128)(2,1)S(1)} async-done(((bf16[256,4,512]{2,0,1:T(8,128)(2,1)}), bf16[256,4,512]{2,0,1:T(8,128)(2,1)S(1)}, u32[]{:S(2)}, u32[]{:S(2)}) %all-to-all-start.1) | async-done | bytes 1048608 | tf_op jit(solution)/shard_map/all_to_all | solution.py:640
  594.3 19.5 %collective-permute-done.25.refs_10_.refs_26_ = bf16[1,4,2,128,640]{4,3,2,1,0:T(8,128)(2,1)} collective-permute-done((bf16[1,4,2,128,640]{4,3,2,1,0:T(8,128)(2,1)}, bf16[1,4,2,128,640]{4,3,2,1,0:T(8,128)(2,1)}, u32[]{:S(2)}, u32[]{:S(2)}) %collective-permute-start.25) | collective-permute-done | bytes 1310752 | tf_op jit(solution)/shard_map/ppermute | solution.py:406
  613.8 25.6 %collective-permute-done.27.refs_12_.refs_28_ = bf16[1,4,2,128,640]{4,3,2,1,0:T(8,128)(2,1)} collective-permute-done((bf16[1,4,2,128,640]{4,3,2,1,0:T(8,128)(2,1)}, bf16[1,4,2,128,640]{4,3,2,1,0:T(8,128)(2,1)}, u32[]{:S(2)}, u32[]{:S(2)}) %collective-permute-start.27) | collective-permute-done | bytes 1310752 | tf_op jit(solution)/shard_map/ppermute | solution.py:406
  651.6 64.0 %query_grad.1 = bf16[4,256,512]{2,1,0:T(8,128)(2,1)S(1)} custom-call(s32[4,16]{1,0:T(4,128)S(1)} %copy.49.place_ref, s32[4,2]{1,0:T(4,128)S(1)} %get-tuple-element.275.own_ref, bf16[4,256,512]{2,1,0:T(8,128)(2,1)S(1)} %copy-done.3, bf16[4,256,512]{2,1,0:T(8,128)(2,1)S(1)} %bitcast.55, bf16[4,256,128]{2,1,0:T(8,128)(2,1)S(1)} %copy-done.17, ...), custom_call_target="tpu_custom_call" | custom-call | flops 12884901888 | bytes 16777216 | tf_op jit(solution)/shard_map/query_grad/pallas_call | solution.py:223
  717.2 4.1 fusion.70
  725.2 3.3 maximum_select_fusion.5
  728.6 3.0 maximum_select_fusion.4
  731.5 43.5 %key_value_grad.1 = (bf16[4,256,512]{2,1,0:T(8,128)(2,1)S(1)}, bf16[4,256,512]{2,1,0:T(8,128)(2,1)S(1)}) custom-call(s32[4,16]{1,0:T(4,128)S(1)} %copy.49.place_ref, s32[4,2]{1,0:T(4,128)S(1)} %get-tuple-element.275.own_ref, bf16[2,4,256,512]{3,2,1,0:T(8,128)(2,1)} %copy-done.20, bf16[2,4,256,512]{3,2,1,0:T(8,128)(2,1)} %copy-done.20, ...), custom_call_target="tpu_custom_call" | custom-call | flops 17179869184 | bytes 16777216 | tf_op jit(solution)/shard_map/key_value_grad/pallas_call | solution.py:223
  775.1 7.8 fusion.71
  782.9 10.9 %fusion.61 = (bf16[1024,2048]{1,0:T(8,128)(2,1)}, f32[1024,2048]{1,0:T(8,128)}) fusion(f32[1024,2048]{1,0:T(8,128)S(1)} %fusion.70, f32[1024,2048]{1,0:T(8,128)} %fusion.71, bf16[1024,512]{1,0:T(8,128)(2,1)S(1)} %bitcast.51, bf16[2048,512]{1,0:T(8,128)(2,1)S(1)} %copy-done.55), kind=kOutput, calls=%fused_computation.177 | convolution fusion | flops 2153775104 | bytes 32505856 | tf_op jit(solution)/shard_map/dot_general | solution.py:15
  797.5 5.3 convolution_convert_fusion.2
  802.8 7.8 collective-permute-start.36
  810.6 14.2 %collective-permute-start.47 = (bf16[176,1024]{1,0:T(8,128)(2,1)S(1)}, bf16[176,1024]{1,0:T(8,128)(2,1)}, u32[]{:S(2)}, u32[]{:S(2)}) collective-permute-start(bf16[176,1024]{1,0:T(8,128)(2,1)S(1)} %copy-done.60), channel_id=1, source_target_pairs={{0,8},{4,12},{8,0},{12,4},{16,24},{20,28},{24,16},{28,20},{1,9},{5... | collective-permute-start | bytes 1081352 | tf_op jit(solution)/shard_map/ppermute | solution.py:406
  824.7 5.0 collective-permute-start.46
  830.0 4.1 collective-permute-done.47
  834.1 4.9 collective-permute-done.46
  842.8 2.6 maximum_select_fusion.10
  845.4 4.0 fusion.34
  849.4 3.5 fusion.17
  853.0 2.9 add_convert_fusion.2
  857.8 12.1 %collective-permute-done.42 = bf16[256,2816]{1,0:T(8,128)(2,1)S(1)} collective-permute-done((bf16[256,2816]{1,0:T(8,128)(2,1)S(1)}, bf16[256,2816]{1,0:T(8,128)(2,1)S(1)}, u32[]{:S(2)}, u32[]{:S(2)}) %collective-permute-start.42) | collective-permute-done | bytes 1441824 | tf_op jit(solution)/shard_map/ppermute | solution.py:406
  875.7 5.0 pad_maximum_fusion.half_ref
  880.8 3.9 fusion.60
  890.6 3.1 add_convert_fusion.6
  893.8 50.5 %psum.7 = f32[14336]{0:T(1024)S(1)} all-reduce(f32[14336]{0:T(1024)S(1)} %constant_dynamic-update-slice_fusion.4), channel_id=1, replica_groups=mesh['ctx'=8,'tp'=4] {'ctx','tp'}, use_global_device_ids=true, to_apply=%region_17.18 | all-reduce | flops 14336 | bytes 114688 | tf_op jit(solution)/shard_map/psum | solution.py:677
  956.6 14.0 %collective-permute-done.52 = bf16[128,1024]{1,0:T(8,128)(2,1)S(1)} collective-permute-done((bf16[128,1024]{1,0:T(8,128)(2,1)S(1)}, bf16[128,1024]{1,0:T(8,128)(2,1)S(1)}, u32[]{:S(2)}, u32[]{:S(2)}) %collective-permute-start.52) | collective-permute-done | bytes 262176 | tf_op jit(solution)/shard_map/ppermute | solution.py:406
  970.6 13.4 %unpack_rows.2 = (f32[2048,1408]{1,0:T(8,128)}, f32[2048,1408]{1,0:T(8,128)}) custom-call(s32[1]{0:T(128)} %bitcast.22.core_ref, bf16[1024,2816]{1,0:T(8,128)(2,1)} %pad_maximum_fusion.half_ref, bf16[1024,2816]{1,0:T(8,128)(2,1)} %collective-permute-done.43.other_ref), custom_call_target="tpu_custom_call" | custom-call | bytes 34603008 | tf_op jit(solution)/shard_map/unpack_rows/pallas_call | solution.py:506
  987.0 6.3 unpack_cols.2
  999.8 16.6 %collective-permute-done.57 = bf16[64,1024]{1,0:T(8,128)(2,1)S(1)} collective-permute-done((bf16[64,1024]{1,0:T(8,128)(2,1)S(1)}, bf16[64,1024]{1,0:T(8,128)(2,1)S(1)}, u32[]{:S(2)}, u32[]{:S(2)}) %collective-permute-start.57) | collective-permute-done | bytes 131104 | tf_op jit(solution)/shard_map/ppermute | solution.py:406
  1023.2 5.2 collective-permute-done.58
  1032.6 3.9 collective-permute-done.61
  1039.5 3.1 fusion.14
  1044.7 3.3 add_convert_fusion.7
  1048.0 9.4 unpack_rows.3
  (416 shorter events, 160.8 us)
Async XLA Ops:
  7.2 89.0 %all-gather.9.cloned.1.call-start = ((), (), s32[]{:S(2)}) async-start(), calls=%async_computation.5 | async-start | bytes 5242880 | tf_op jit(solution)/shard_map/all_gather | solution.py:543
  12.6 176.3 %all-gather.17.cloned.1.call-start = ((), (), s32[]{:S(2)}) async-start(), calls=%async_computation.12 | async-start | bytes 1310720 | tf_op jit(solution)/shard_map/all_gather | solution.py:609
  96.2 110.5 %all-gather.11.cloned.1.call-start = ((), (), s32[]{:S(2)}) async-start(), calls=%async_computation.6 | async-start | bytes 5242880 | tf_op jit(solution)/shard_map/all_gather | solution.py:543
  114.3 192.8 %all-gather.19.cloned.1.call-start = ((), (), s32[]{:S(2)}) async-start(), calls=%async_computation.13 | async-start | bytes 9437184 | tf_op jit(solution)/shard_map/all_gather | solution.py:611
  114.4 47.6 %collective-permute-start.1 = (bf16[2,4,2,128,512]{4,3,2,1,0:T(8,128)(2,1)}, bf16[2,4,2,128,512]{4,3,2,1,0:T(8,128)(2,1)S(1)}, u32[]{:S(2)}, u32[]{:S(2)}) collective-permute-start(bf16[2,4,2,128,512]{4,3,2,1,0:T(8,128)(2,1)} %bitcast.71), channel_id=1, source_target_pairs={{0,8},{4,12},{8,0},{12,4},{16,24},{20,28},{24,16},{28,20},{1,9},{5... | collective-permute-start | bytes 6291464 | tf_op jit(solution)/shard_map/ppermute | solution.py:406
  115.9 47.7 %collective-permute-start.3 = (bf16[2,4,2,128,512]{4,3,2,1,0:T(8,128)(2,1)}, bf16[2,4,2,128,512]{4,3,2,1,0:T(8,128)(2,1)}, u32[]{:S(2)}, u32[]{:S(2)}) collective-permute-start(bf16[2,4,2,128,512]{4,3,2,1,0:T(8,128)(2,1)} %bitcast.72), channel_id=1, source_target_pairs={{0,16},{4,20},{8,24},{12,28},{16,0},{20,4},{24,8},{28,12},{1,17},{... | collective-permute-start | bytes 6291464 | tf_op jit(solution)/shard_map/ppermute | solution.py:406
  117.4 71.5 %collective-permute-start = (bf16[2,4,2,128,512]{4,3,2,1,0:T(8,128)(2,1)}, bf16[2,4,2,128,512]{4,3,2,1,0:T(8,128)(2,1)}, u32[]{:S(2)}, u32[]{:S(2)}) collective-permute-start(bf16[2,4,2,128,512]{4,3,2,1,0:T(8,128)(2,1)} %bitcast.73), channel_id=1, source_target_pairs={{0,4},{4,0},{8,12},{12,8},{16,20},{20,16},{24,28},{28,24},{1,5},{5... | collective-permute-start | bytes 6291464 | tf_op jit(solution)/shard_map/ppermute | solution.py:406
  162.1 24.2 %collective-permute-start.5 = (bf16[1,4,2,128,512]{4,3,2,1,0:T(8,128)(2,1)S(1)}, bf16[1,4,2,128,512]{4,3,2,1,0:T(8,128)(2,1)}, u32[]{:S(2)}, u32[]{:S(2)}) collective-permute-start(bf16[1,4,2,128,512]{4,3,2,1,0:T(8,128)(2,1)S(1)} %slice.101), channel_id=1, source_target_pairs={{0,16},{4,20},{8,24},{12,28},{16,0},{20,4},{24,8},{28,12},{1,17},{... | collective-permute-start | bytes 3145736 | tf_op jit(solution)/shard_map/ppermute | solution.py:406
  164.9 24.0 %collective-permute-start.7 = (bf16[1,4,2,128,512]{4,3,2,1,0:T(8,128)(2,1)S(1)}, bf16[1,4,2,128,512]{4,3,2,1,0:T(8,128)(2,1)}, u32[]{:S(2)}, u32[]{:S(2)}) collective-permute-start(bf16[1,4,2,128,512]{4,3,2,1,0:T(8,128)(2,1)S(1)} %slice.102), channel_id=1, source_target_pairs={{0,8},{4,12},{8,0},{12,4},{16,24},{20,28},{24,16},{28,20},{1,9},{5... | collective-permute-start | bytes 3145736 | tf_op jit(solution)/shard_map/ppermute | solution.py:406
  166.5 25.4 %collective-permute-start.2 = (bf16[2,4,2,128,512]{4,3,2,1,0:T(8,128)(2,1)S(1)}, bf16[2,4,2,128,512]{4,3,2,1,0:T(8,128)(2,1)}, u32[]{:S(2)}, u32[]{:S(2)}) collective-permute-start(bf16[2,4,2,128,512]{4,3,2,1,0:T(8,128)(2,1)S(1)} %collective-permute-done.1.refs_2_.refs_10_), channel_id=1, source_target_pairs={{0,4},{4,0},{8,12},{12,8},{16,20},{20,16},{24,28},{28,24},{1,5},{5... | collective-permute-start | bytes 6291464 | tf_op jit(solution)/shard_map/ppermute | solution.py:406
  166.5 25.4 %collective-permute-start.4 = (bf16[2,4,2,128,512]{4,3,2,1,0:T(8,128)(2,1)}, bf16[2,4,2,128,512]{4,3,2,1,0:T(8,128)(2,1)}, u32[]{:S(2)}, u32[]{:S(2)}) collective-permute-start(bf16[2,4,2,128,512]{4,3,2,1,0:T(8,128)(2,1)} %collective-permute-done.3.refs_4_.refs_12_), channel_id=1, source_target_pairs={{0,4},{4,0},{8,12},{12,8},{16,20},{20,16},{24,28},{28,24},{1,5},{5... | collective-permute-start | bytes 6291464 | tf_op jit(solution)/shard_map/ppermute | solution.py:406
  206.7 187.5 %all-gather.13.cloned.1.call-start = ((), (), s32[]{:S(2)}) async-start(), calls=%async_computation.7 | async-start | bytes 5242880 | tf_op jit(solution)/shard_map/all_gather | solution.py:543
  316.1 214.0 %reduce-scatter.4.cloned.1.call-start = ((), (), s32[]{:S(2)}) async-start(), calls=%async_computation.8 | async-start | bytes 5242880 | tf_op jit(solution)/shard_map/reduce_scatter | solution.py:547
  317.3 31.9 %collective-permute-start.10 = (bf16[1,4,2,128,640]{4,3,2,1,0:T(8,128)(2,1)S(1)}, bf16[1,4,2,128,640]{4,3,2,1,0:T(8,128)(2,1)}, u32[]{:S(2)}, u32[]{:S(2)}) collective-permute-start(bf16[1,4,2,128,640]{4,3,2,1,0:T(8,128)(2,1)S(1)} %bitcast.59), channel_id=1, source_target_pairs={{0,8},{4,12},{8,0},{12,4},{16,24},{20,28},{24,16},{28,20},{1,9},{5... | collective-permute-start | bytes 3932168 | tf_op jit(solution)/shard_map/ppermute | solution.py:406
  317.4 55.9 %collective-permute-start.12 = (bf16[1,4,2,128,640]{4,3,2,1,0:T(8,128)(2,1)S(1)}, bf16[1,4,2,128,640]{4,3,2,1,0:T(8,128)(2,1)}, u32[]{:S(2)}, u32[]{:S(2)}) collective-permute-start(bf16[1,4,2,128,640]{4,3,2,1,0:T(8,128)(2,1)S(1)} %bitcast.60), channel_id=1, source_target_pairs={{0,16},{4,20},{8,24},{12,28},{16,0},{20,4},{24,8},{28,12},{1,17},{... | collective-permute-start | bytes 3932168 | tf_op jit(solution)/shard_map/ppermute | solution.py:406
  317.4 55.8 %collective-permute-start.14 = (bf16[1,4,2,128,640]{4,3,2,1,0:T(8,128)(2,1)S(1)}, bf16[1,4,2,128,640]{4,3,2,1,0:T(8,128)(2,1)}, u32[]{:S(2)}, u32[]{:S(2)}) collective-permute-start(bf16[1,4,2,128,640]{4,3,2,1,0:T(8,128)(2,1)S(1)} %bitcast.61), channel_id=1, source_target_pairs={{0,24},{4,28},{8,16},{12,20},{16,8},{20,12},{24,0},{28,4},{1,25},{... | collective-permute-start | bytes 3932168 | tf_op jit(solution)/shard_map/ppermute | solution.py:406
  320.8 52.9 %collective-permute-start.9 = (bf16[1,4,2,128,640]{4,3,2,1,0:T(8,128)(2,1)S(1)}, bf16[1,4,2,128,640]{4,3,2,1,0:T(8,128)(2,1)}, u32[]{:S(2)}, u32[]{:S(2)}) collective-permute-start(bf16[1,4,2,128,640]{4,3,2,1,0:T(8,128)(2,1)S(1)} %bitcast.62), channel_id=1, source_target_pairs={{0,4},{4,0},{8,12},{12,8},{16,20},{20,16},{24,28},{28,24},{1,5},{5... | collective-permute-start | bytes 3932168 | tf_op jit(solution)/shard_map/ppermute | solution.py:406
  349.2 24.6 %collective-permute-start.11 = (bf16[1,4,2,128,640]{4,3,2,1,0:T(8,128)(2,1)}, bf16[1,4,2,128,640]{4,3,2,1,0:T(8,128)(2,1)}, u32[]{:S(2)}, u32[]{:S(2)}) collective-permute-start(bf16[1,4,2,128,640]{4,3,2,1,0:T(8,128)(2,1)} %collective-permute-done.10.refs_2_.refs_18_), channel_id=1, source_target_pairs={{0,4},{4,0},{8,12},{12,8},{16,20},{20,16},{24,28},{28,24},{1,5},{5... | collective-permute-start | bytes 3932168 | tf_op jit(solution)/shard_map/ppermute | solution.py:406
  454.5 12.4 %collective-permute-start.16 = (bf16[1024,2816]{1,0:T(8,128)(2,1)}, bf16[1024,2816]{1,0:T(8,128)(2,1)}, u32[]{:S(2)}, u32[]{:S(2)}) collective-permute-start(bf16[1024,2816]{1,0:T(8,128)(2,1)} %convolution_convert_fusion), channel_id=1, source_target_pairs={{0,4},{4,0},{8,12},{12,8},{16,20},{20,16},{24,28},{28,24},{1,5},{5... | collective-permute-start | bytes 17301512 | tf_op jit(solution)/shard_map/ppermute | solution.py:406
  481.0 34.3 %collective-permute-start.18 = (bf16[256,2816]{1,0:T(8,128)(2,1)}, bf16[256,2816]{1,0:T(8,128)(2,1)}, u32[]{:S(2)}, u32[]{:S(2)}) collective-permute-start(bf16[256,2816]{1,0:T(8,128)(2,1)} %constant_dynamic-slice_fusion.15), channel_id=1, source_target_pairs={{0,8},{4,12},{8,0},{12,4},{16,24},{20,28},{24,16},{28,20},{1,9},{5... | collective-permute-start | bytes 4325384 | tf_op jit(solution)/shard_map/ppermute | solution.py:406
  483.8 34.1 %collective-permute-start.19 = (bf16[256,2816]{1,0:T(8,128)(2,1)}, bf16[256,2816]{1,0:T(8,128)(2,1)}, u32[]{:S(2)}, u32[]{:S(2)}) collective-permute-start(bf16[256,2816]{1,0:T(8,128)(2,1)} %constant_dynamic-slice_fusion.14), channel_id=1, source_target_pairs={{0,16},{4,20},{8,24},{12,28},{16,0},{20,4},{24,8},{28,12},{1,17},{... | collective-permute-start | bytes 4325384 | tf_op jit(solution)/shard_map/ppermute | solution.py:406
  503.5 28.1 %collective-permute-start.17 = (bf16[1408,1024]{1,0:T(8,128)(2,1)}, bf16[1408,1024]{1,0:T(8,128)(2,1)}, u32[]{:S(2)}, u32[]{:S(2)}) collective-permute-start(bf16[1408,1024]{1,0:T(8,128)(2,1)} %convolution_convert_fusion.3), channel_id=1, source_target_pairs={{0,4},{4,0},{8,12},{12,8},{16,20},{20,16},{24,28},{28,24},{1,5},{5... | collective-permute-start | bytes 8650760 | tf_op jit(solution)/shard_map/ppermute | solution.py:406
  520.7 32.8 %collective-permute-start.21 = (bf16[128,2816]{1,0:T(8,128)(2,1)}, bf16[128,2816]{1,0:T(8,128)(2,1)}, u32[]{:S(2)}, u32[]{:S(2)}) collective-permute-start(bf16[128,2816]{1,0:T(8,128)(2,1)} %constant_dynamic-slice_fusion.12), channel_id=1, source_target_pairs={{0,8},{4,12},{8,0},{12,4},{16,24},{20,28},{24,16},{28,20},{1,9},{5... | collective-permute-start | bytes 2162696 | tf_op jit(solution)/shard_map/ppermute | solution.py:406
  525.7 27.8 %collective-permute-start.20 = (bf16[128,2816]{1,0:T(8,128)(2,1)}, bf16[128,2816]{1,0:T(8,128)(2,1)}, u32[]{:S(2)}, u32[]{:S(2)}) collective-permute-start(bf16[128,2816]{1,0:T(8,128)(2,1)} %constant_dynamic-slice_fusion.13), channel_id=1, source_target_pairs={{0,16},{4,20},{8,24},{12,28},{16,0},{20,4},{24,8},{28,12},{1,17},{... | collective-permute-start | bytes 2162696 | tf_op jit(solution)/shard_map/ppermute | solution.py:406
  549.3 30.0 %all-to-all-start.1 = ((bf16[256,4,512]{2,0,1:T(8,128)(2,1)}), bf16[256,4,512]{2,0,1:T(8,128)(2,1)S(1)}, u32[]{:S(2)}, u32[]{:S(2)}) async-start(bf16[256,4,512]{2,0,1:T(8,128)(2,1)} %bitcast.83), calls=%async_computation.2 | async-start | bytes 2097152 | tf_op jit(solution)/shard_map/all_to_all | solution.py:640
  553.5 240.4 %all-gather.15.cloned.1.call-start = ((), (), s32[]{:S(2)}) async-start(), calls=%async_computation.9 | async-start | bytes 5242880 | tf_op jit(solution)/shard_map/all_gather | solution.py:543
  555.8 29.5 %collective-permute-start.22 = (bf16[352,1024]{1,0:T(8,128)(2,1)}, bf16[352,1024]{1,0:T(8,128)(2,1)}, u32[]{:S(2)}, u32[]{:S(2)}) collective-permute-start(bf16[352,1024]{1,0:T(8,128)(2,1)} %constant_dynamic-slice_fusion.11), channel_id=1, source_target_pairs={{0,8},{4,12},{8,0},{12,4},{16,24},{20,28},{24,16},{28,20},{1,9},{5... | collective-permute-start | bytes 2162696 | tf_op jit(solution)/shard_map/ppermute | solution.py:406
  560.6 27.0 %collective-permute-start.23 = (bf16[352,1024]{1,0:T(8,128)(2,1)}, bf16[352,1024]{1,0:T(8,128)(2,1)}, u32[]{:S(2)}, u32[]{:S(2)}) collective-permute-start(bf16[352,1024]{1,0:T(8,128)(2,1)} %constant_dynamic-slice_fusion.10), channel_id=1, source_target_pairs={{0,16},{4,20},{8,24},{12,28},{16,0},{20,4},{24,8},{28,12},{1,17},{... | collective-permute-start | bytes 2162696 | tf_op jit(solution)/shard_map/ppermute | solution.py:406
  581.8 32.0 %collective-permute-start.25 = (bf16[1,4,2,128,640]{4,3,2,1,0:T(8,128)(2,1)}, bf16[1,4,2,128,640]{4,3,2,1,0:T(8,128)(2,1)}, u32[]{:S(2)}, u32[]{:S(2)}) collective-permute-start(bf16[1,4,2,128,640]{4,3,2,1,0:T(8,128)(2,1)} %pad_maximum_fusion.4.refs_8_.refs_24_), channel_id=1, source_target_pairs={{0,8},{4,12},{8,0},{12,4},{16,24},{20,28},{24,16},{28,20},{1,9},{5... | collective-permute-start | bytes 3932168 | tf_op jit(solution)/shard_map/ppermute | solution.py:406
  583.3 56.1 %collective-permute-start.27 = (bf16[1,4,2,128,640]{4,3,2,1,0:T(8,128)(2,1)}, bf16[1,4,2,128,640]{4,3,2,1,0:T(8,128)(2,1)}, u32[]{:S(2)}, u32[]{:S(2)}) collective-permute-start(bf16[1,4,2,128,640]{4,3,2,1,0:T(8,128)(2,1)} %pad_maximum_fusion.4.refs_8_.refs_24_), channel_id=1, source_target_pairs={{0,16},{4,20},{8,24},{12,28},{16,0},{20,4},{24,8},{28,12},{1,17},{... | collective-permute-start | bytes 3932168 | tf_op jit(solution)/shard_map/ppermute | solution.py:406
  584.7 58.1 %collective-permute-start.29 = (bf16[1,4,2,128,640]{4,3,2,1,0:T(8,128)(2,1)}, bf16[1,4,2,128,640]{4,3,2,1,0:T(8,128)(2,1)}, u32[]{:S(2)}, u32[]{:S(2)}) collective-permute-start(bf16[1,4,2,128,640]{4,3,2,1,0:T(8,128)(2,1)} %pad_maximum_fusion.4.refs_8_.refs_24_), channel_id=1, source_target_pairs={{0,24},{4,28},{8,16},{12,20},{16,8},{20,12},{24,0},{28,4},{1,25},{... | collective-permute-start | bytes 3932168 | tf_op jit(solution)/shard_map/ppermute | solution.py:406
  585.3 58.3 %collective-permute-start.24 = (bf16[1,4,2,128,640]{4,3,2,1,0:T(8,128)(2,1)}, bf16[1,4,2,128,640]{4,3,2,1,0:T(8,128)(2,1)}, u32[]{:S(2)}, u32[]{:S(2)}) collective-permute-start(bf16[1,4,2,128,640]{4,3,2,1,0:T(8,128)(2,1)} %pad_maximum_fusion.4.refs_8_.refs_24_), channel_id=1, source_target_pairs={{0,4},{4,0},{8,12},{12,8},{16,20},{20,16},{24,28},{28,24},{1,5},{5... | collective-permute-start | bytes 3932168 | tf_op jit(solution)/shard_map/ppermute | solution.py:406
  587.5 135.9 %collective-permute-start.32 = (bf16[128,2816]{1,0:T(8,128)(2,1)}, bf16[128,2816]{1,0:T(8,128)(2,1)}, u32[]{:S(2)}, u32[]{:S(2)}) collective-permute-start(bf16[128,2816]{1,0:T(8,128)(2,1)} %add_convert_fusion.13), channel_id=1, source_target_pairs={{0,8},{4,12},{8,0},{12,4},{16,24},{20,28},{24,16},{28,20},{1,9},{5... | collective-permute-start | bytes 2162696 | tf_op jit(solution)/shard_map/ppermute | solution.py:406
  594.3 443.1 %reduce-scatter.8.cloned.1.call-start = ((), (), s32[]{:S(2)}) async-start(), calls=%async_computation.11 | async-start | bytes 5242880 | tf_op jit(solution)/shard_map/reduce_scatter | solution.py:547
  613.8 101.8 %collective-permute-start.26 = (bf16[1,4,2,128,640]{4,3,2,1,0:T(8,128)(2,1)}, bf16[1,4,2,128,640]{4,3,2,1,0:T(8,128)(2,1)S(1)}, u32[]{:S(2)}, u32[]{:S(2)}) collective-permute-start(bf16[1,4,2,128,640]{4,3,2,1,0:T(8,128)(2,1)} %collective-permute-done.25.refs_10_.refs_26_), channel_id=1, source_target_pairs={{0,4},{4,0},{8,12},{12,8},{16,20},{20,16},{24,28},{28,24},{1,5},{5... | collective-permute-start | bytes 3932168 | tf_op jit(solution)/shard_map/ppermute | solution.py:406
  639.4 76.3 %collective-permute-start.28 = (bf16[1,4,2,128,640]{4,3,2,1,0:T(8,128)(2,1)}, bf16[1,4,2,128,640]{4,3,2,1,0:T(8,128)(2,1)S(1)}, u32[]{:S(2)}, u32[]{:S(2)}) collective-permute-start(bf16[1,4,2,128,640]{4,3,2,1,0:T(8,128)(2,1)} %collective-permute-done.27.refs_12_.refs_28_), channel_id=1, source_target_pairs={{0,4},{4,0},{8,12},{12,8},{16,20},{20,16},{24,28},{28,24},{1,5},{5... | collective-permute-start | bytes 3932168 | tf_op jit(solution)/shard_map/ppermute | solution.py:406
  642.9 80.6 %collective-permute-start.31 = (bf16[128,2816]{1,0:T(8,128)(2,1)}, bf16[128,2816]{1,0:T(8,128)(2,1)}, u32[]{:S(2)}, u32[]{:S(2)}) collective-permute-start(bf16[128,2816]{1,0:T(8,128)(2,1)} %add_convert_fusion.14), channel_id=1, source_target_pairs={{0,16},{4,20},{8,24},{12,28},{16,0},{20,4},{24,8},{28,12},{1,17},{... | collective-permute-start | bytes 2162696 | tf_op jit(solution)/shard_map/ppermute | solution.py:406
  643.6 77.7 %collective-permute-start.30 = (bf16[1,4,2,128,640]{4,3,2,1,0:T(8,128)(2,1)}, bf16[1,4,2,128,640]{4,3,2,1,0:T(8,128)(2,1)}, u32[]{:S(2)}, u32[]{:S(2)}) collective-permute-start(bf16[1,4,2,128,640]{4,3,2,1,0:T(8,128)(2,1)} %collective-permute-done.29.refs_14_.refs_30_), channel_id=1, source_target_pairs={{0,4},{4,0},{8,12},{12,8},{16,20},{20,16},{24,28},{28,24},{1,5},{5... | collective-permute-start | bytes 3932168 | tf_op jit(solution)/shard_map/ppermute | solution.py:406
  793.8 250.9 %reduce-scatter.6.cloned.1.call-start = ((), (), s32[]{:S(2)}) async-start(), calls=%async_computation.10 | async-start | bytes 5242880 | tf_op jit(solution)/shard_map/reduce_scatter | solution.py:547
  802.8 50.1 %collective-permute-start.36 = (bf16[1024,1536]{1,0:T(8,128)(2,1)}, bf16[1024,1536]{1,0:T(8,128)(2,1)}, u32[]{:S(2)}, u32[]{:S(2)}) collective-permute-start(bf16[1024,1536]{1,0:T(8,128)(2,1)} %convolution_convert_fusion.2), channel_id=1, source_target_pairs={{0,4},{4,0},{8,12},{12,8},{16,20},{20,16},{24,28},{28,24},{1,5},{5... | collective-permute-start | bytes 9437192 | tf_op jit(solution)/shard_map/ppermute | solution.py:406
  810.6 23.5 %collective-permute-start.47 = (bf16[176,1024]{1,0:T(8,128)(2,1)S(1)}, bf16[176,1024]{1,0:T(8,128)(2,1)}, u32[]{:S(2)}, u32[]{:S(2)}) collective-permute-start(bf16[176,1024]{1,0:T(8,128)(2,1)S(1)} %copy-done.60), channel_id=1, source_target_pairs={{0,8},{4,12},{8,0},{12,4},{16,24},{20,28},{24,16},{28,20},{1,9},{5... | collective-permute-start | bytes 1081352 | tf_op jit(solution)/shard_map/ppermute | solution.py:406
  824.7 14.3 %collective-permute-start.46 = (bf16[176,1024]{1,0:T(8,128)(2,1)S(1)}, bf16[176,1024]{1,0:T(8,128)(2,1)}, u32[]{:S(2)}, u32[]{:S(2)}) collective-permute-start(bf16[176,1024]{1,0:T(8,128)(2,1)S(1)} %copy-done.59), channel_id=1, source_target_pairs={{0,16},{4,20},{8,24},{12,28},{16,0},{20,4},{24,8},{28,12},{1,17},{... | collective-permute-start | bytes 1081352 | tf_op jit(solution)/shard_map/ppermute | solution.py:406
  829.8 40.1 %collective-permute-start.42 = (bf16[256,2816]{1,0:T(8,128)(2,1)S(1)}, bf16[256,2816]{1,0:T(8,128)(2,1)S(1)}, u32[]{:S(2)}, u32[]{:S(2)}) collective-permute-start(bf16[256,2816]{1,0:T(8,128)(2,1)S(1)} %copy-done.42), channel_id=1, source_target_pairs={{0,16},{4,20},{8,24},{12,28},{16,0},{20,4},{24,8},{28,12},{1,17},{... | collective-permute-start | bytes 4325384 | tf_op jit(solution)/shard_map/ppermute | solution.py:406
  829.8 40.0 %collective-permute-start.41 = (bf16[256,2816]{1,0:T(8,128)(2,1)}, bf16[256,2816]{1,0:T(8,128)(2,1)S(1)}, u32[]{:S(2)}, u32[]{:S(2)}) collective-permute-start(bf16[256,2816]{1,0:T(8,128)(2,1)} %maximum_select_fusion.4), channel_id=1, source_target_pairs={{0,8},{4,12},{8,0},{12,4},{16,24},{20,28},{24,16},{28,20},{1,9},{5... | collective-permute-start | bytes 4325384 | tf_op jit(solution)/shard_map/ppermute | solution.py:406
  840.6 103.7 %collective-permute-start.49 = (bf16[352,1024]{1,0:T(8,128)(2,1)S(1)}, bf16[352,1024]{1,0:T(8,128)(2,1)}, u32[]{:S(2)}, u32[]{:S(2)}) collective-permute-start(bf16[352,1024]{1,0:T(8,128)(2,1)S(1)} %maximum_select_fusion.11), channel_id=1, source_target_pairs={{0,16},{4,20},{8,24},{12,28},{16,0},{20,4},{24,8},{28,12},{1,17},{... | collective-permute-start | bytes 2162696 | tf_op jit(solution)/shard_map/ppermute | solution.py:406
  845.4 101.3 %collective-permute-start.48 = (bf16[352,1024]{1,0:T(8,128)(2,1)}, bf16[352,1024]{1,0:T(8,128)(2,1)}, u32[]{:S(2)}, u32[]{:S(2)}) collective-permute-start(bf16[352,1024]{1,0:T(8,128)(2,1)} %maximum_select_fusion.10), channel_id=1, source_target_pairs={{0,8},{4,12},{8,0},{12,4},{16,24},{20,28},{24,16},{28,20},{1,9},{5... | collective-permute-start | bytes 2162696 | tf_op jit(solution)/shard_map/ppermute | solution.py:406
  852.9 32.5 %collective-permute-start.35 = (bf16[512,1024]{1,0:T(8,128)(2,1)}, bf16[512,1024]{1,0:T(8,128)(2,1)}, u32[]{:S(2)}, u32[]{:S(2)}) collective-permute-start(bf16[512,1024]{1,0:T(8,128)(2,1)} %fusion.34), channel_id=1, source_target_pairs={{0,4},{4,0},{8,12},{12,8},{16,20},{20,16},{24,28},{28,24},{1,5},{5... | collective-permute-start | bytes 3145736 | tf_op jit(solution)/shard_map/ppermute | solution.py:406
  880.7 89.8 %collective-permute-start.43 = (bf16[1024,2816]{1,0:T(8,128)(2,1)}, bf16[1024,2816]{1,0:T(8,128)(2,1)}, u32[]{:S(2)}, u32[]{:S(2)}) collective-permute-start(bf16[1024,2816]{1,0:T(8,128)(2,1)} %pad_maximum_fusion.half_ref), channel_id=1, source_target_pairs={{0,4},{4,0},{8,12},{12,8},{16,20},{20,16},{24,28},{28,24},{1,5},{5... | collective-permute-start | bytes 17301512 | tf_op jit(solution)/shard_map/ppermute | solution.py:406
  887.6 64.0 %collective-permute-start.37 = (bf16[256,1536]{1,0:T(8,128)(2,1)}, bf16[256,1536]{1,0:T(8,128)(2,1)S(1)}, u32[]{:S(2)}, u32[]{:S(2)}) collective-permute-start(bf16[256,1536]{1,0:T(8,128)(2,1)} %constant_dynamic-slice_fusion.7), channel_id=1, source_target_pairs={{0,8},{4,12},{8,0},{12,4},{16,24},{20,28},{24,16},{28,20},{1,9},{5... | collective-permute-start | bytes 2359304 | tf_op jit(solution)/shard_map/ppermute | solution.py:406
  888.6 63.1 %collective-permute-start.38 = (bf16[256,1536]{1,0:T(8,128)(2,1)}, bf16[256,1536]{1,0:T(8,128)(2,1)}, u32[]{:S(2)}, u32[]{:S(2)}) collective-permute-start(bf16[256,1536]{1,0:T(8,128)(2,1)} %constant_dynamic-slice_fusion.6), channel_id=1, source_target_pairs={{0,16},{4,20},{8,24},{12,28},{16,0},{20,4},{24,8},{28,12},{1,17},{... | collective-permute-start | bytes 2359304 | tf_op jit(solution)/shard_map/ppermute | solution.py:406
  944.4 12.1 %collective-permute-start.51 = (bf16[128,1024]{1,0:T(8,128)(2,1)S(1)}, bf16[128,1024]{1,0:T(8,128)(2,1)S(1)}, u32[]{:S(2)}, u32[]{:S(2)}) collective-permute-start(bf16[128,1024]{1,0:T(8,128)(2,1)S(1)} %constant_dynamic-slice_fusion.3), channel_id=1, source_target_pairs={{0,8},{4,12},{8,0},{12,4},{16,24},{20,28},{24,16},{28,20},{1,9},{5... | collective-permute-start | bytes 786440 | tf_op jit(solution)/shard_map/ppermute | solution.py:406
  951.6 35.4 %collective-permute-start.50 = (bf16[1408,1024]{1,0:T(8,128)(2,1)S(1)}, bf16[1408,1024]{1,0:T(8,128)(2,1)S(1)}, u32[]{:S(2)}, u32[]{:S(2)}) collective-permute-start(bf16[1408,1024]{1,0:T(8,128)(2,1)S(1)} %pad_maximum_fusion.2.half_ref), channel_id=1, source_target_pairs={{0,4},{4,0},{8,12},{12,8},{16,20},{20,16},{24,28},{28,24},{1,5},{5... | collective-permute-start | bytes 8650760 | tf_op jit(solution)/shard_map/ppermute | solution.py:406
  954.0 30.0 %collective-permute-start.40 = (bf16[128,1536]{1,0:T(8,128)(2,1)S(1)}, bf16[128,1536]{1,0:T(8,128)(2,1)S(1)}, u32[]{:S(2)}, u32[]{:S(2)}) collective-permute-start(bf16[128,1536]{1,0:T(8,128)(2,1)S(1)} %constant_dynamic-slice_fusion.4), channel_id=1, source_target_pairs={{0,8},{4,12},{8,0},{12,4},{16,24},{20,28},{24,16},{28,20},{1,9},{5... | collective-permute-start | bytes 1179656 | tf_op jit(solution)/shard_map/ppermute | solution.py:406
  954.4 29.6 %collective-permute-start.39 = (bf16[128,1536]{1,0:T(8,128)(2,1)S(1)}, bf16[128,1536]{1,0:T(8,128)(2,1)S(1)}, u32[]{:S(2)}, u32[]{:S(2)}) collective-permute-start(bf16[128,1536]{1,0:T(8,128)(2,1)S(1)} %constant_dynamic-slice_fusion.5), channel_id=1, source_target_pairs={{0,16},{4,20},{8,24},{12,28},{16,0},{20,4},{24,8},{28,12},{1,17},{... | collective-permute-start | bytes 1179656 | tf_op jit(solution)/shard_map/ppermute | solution.py:406
  956.4 14.1 %collective-permute-start.52 = (bf16[128,1024]{1,0:T(8,128)(2,1)S(1)}, bf16[128,1024]{1,0:T(8,128)(2,1)S(1)}, u32[]{:S(2)}, u32[]{:S(2)}) collective-permute-start(bf16[128,1024]{1,0:T(8,128)(2,1)S(1)} %constant_dynamic-slice_fusion.2), channel_id=1, source_target_pairs={{0,16},{4,20},{8,24},{12,28},{16,0},{20,4},{24,8},{28,12},{1,17},{... | collective-permute-start | bytes 786440 | tf_op jit(solution)/shard_map/ppermute | solution.py:406
  984.1 9.7 collective-permute-start.45
  986.0 9.2 collective-permute-start.44
  995.3 22.7 %collective-permute-start.54 = (bf16[256,1536]{1,0:T(8,128)(2,1)S(1)}, bf16[256,1536]{1,0:T(8,128)(2,1)S(1)}, u32[]{:S(2)}, u32[]{:S(2)}) collective-permute-start(bf16[256,1536]{1,0:T(8,128)(2,1)S(1)} %maximum_select_fusion.9), channel_id=1, source_target_pairs={{0,16},{4,20},{8,24},{12,28},{16,0},{20,4},{24,8},{28,12},{1,17},{... | collective-permute-start | bytes 2359304 | tf_op jit(solution)/shard_map/ppermute | solution.py:406
  996.2 21.8 %collective-permute-start.53 = (bf16[256,1536]{1,0:T(8,128)(2,1)S(1)}, bf16[256,1536]{1,0:T(8,128)(2,1)}, u32[]{:S(2)}, u32[]{:S(2)}) collective-permute-start(bf16[256,1536]{1,0:T(8,128)(2,1)S(1)} %maximum_select_fusion.8), channel_id=1, source_target_pairs={{0,8},{4,12},{8,0},{12,4},{16,24},{20,28},{24,16},{28,20},{1,9},{5... | collective-permute-start | bytes 2359304 | tf_op jit(solution)/shard_map/ppermute | solution.py:406
  997.7 18.8 %collective-permute-start.57 = (bf16[64,1024]{1,0:T(8,128)(2,1)S(1)}, bf16[64,1024]{1,0:T(8,128)(2,1)S(1)}, u32[]{:S(2)}, u32[]{:S(2)}) collective-permute-start(bf16[64,1024]{1,0:T(8,128)(2,1)S(1)} %constant_dynamic-slice_fusion), channel_id=1, source_target_pairs={{0,8},{4,12},{8,0},{12,4},{16,24},{20,28},{24,16},{28,20},{1,9},{5... | collective-permute-start | bytes 393224 | tf_op jit(solution)/shard_map/ppermute | solution.py:406
  998.4 18.0 %collective-permute-start.56 = (bf16[64,1024]{1,0:T(8,128)(2,1)S(1)}, bf16[64,1024]{1,0:T(8,128)(2,1)S(1)}, u32[]{:S(2)}, u32[]{:S(2)}) collective-permute-start(bf16[64,1024]{1,0:T(8,128)(2,1)S(1)} %constant_dynamic-slice_fusion.1), channel_id=1, source_target_pairs={{0,16},{4,20},{8,24},{12,28},{16,0},{20,4},{24,8},{28,12},{1,17},{... | collective-permute-start | bytes 393224 | tf_op jit(solution)/shard_map/ppermute | solution.py:406
  1022.4 25.6 %collective-permute-start.55 = (bf16[1024,1536]{1,0:T(8,128)(2,1)}, bf16[1024,1536]{1,0:T(8,128)(2,1)}, u32[]{:S(2)}, u32[]{:S(2)}) collective-permute-start(bf16[1024,1536]{1,0:T(8,128)(2,1)} %pad_maximum_fusion.1.half_ref), channel_id=1, source_target_pairs={{0,4},{4,0},{8,12},{12,8},{16,20},{20,16},{24,28},{28,24},{1,5},{5... | collective-permute-start | bytes 9437192 | tf_op jit(solution)/shard_map/ppermute | solution.py:406
  1028.5 8.0 collective-permute-start.61
  1029.2 7.7 collective-permute-start.60
  (94 other events, 820.4 us)
Sparse Core Ops, SparseCore 0:
  12.7 83.4 all-gather.8
  98.4 26.4 all-gather.16
  126.4 80.2 all-gather.10
  208.5 52.9 all-gather.18
  316.3 77.9 all-gather.12
  454.7 75.4 reduce-scatter.3
  594.4 78.8 all-gather.14
  793.9 99.4 reduce-scatter.7
  896.2 78.3 reduce-scatter.5

commit v4 on v3

--- a/solution.py
+++ b/solution.py
@@ -161,10 +161,10 @@
         dq_ref[0, rows, :] = turn(grad, c_ref[rows], a_ref[rows], b_ref[rows], -1.0).astype(jnp.bfloat16)
 
 
-def dkv_kernel(place_ref, own_ref, k_ref, v_ref, c_ref, a_ref, b_ref, *refs, blocks, n):
+def dkv_kernel(place_ref, own_ref, k_ref, v_ref, c_ref, a_ref, b_ref, *refs, blocks, n, lead):
     q_refs, do_refs, qx_refs, dox_refs = (refs[i * n:(i + 1) * n] for i in range(4))
     dk_ref, dv_ref, qs, dos, acck, accv = refs[4 * n:]
-    s, pair = pl.program_id(0), pl.program_id(1)
+    s, pair = pl.program_id(0) + lead, pl.program_id(1)
     place_rows(place_ref, s, q_refs, qs)
     place_rows(place_ref, s, do_refs, dos)
 
@@ -207,15 +207,14 @@
 
 OWN = pl.BlockSpec((1, 2 * BLK, 128), lambda s, h, *_: (s, 0, h))
 EXT = pl.BlockSpec((1, 2 * BLK, 128), lambda s, h, *_: (s, 0, 0))
-TABLE = pl.BlockSpec((2 * BLK, 128), lambda s, h, *_: (s, 0))
-
-
-def piece(x, first=0, lane=None):
-    count = x.shape[0] if first is None else 1
-    lead = 0 if first is None else first
-    if lane is None:
-        return pl.BlockSpec((count, 1, 2, BLK, 128), lambda s, h, *_: (lead, s, 0, 0, h))
-    return pl.BlockSpec((count, 1, 2, BLK, 128), lambda s, h, *_: (lead, s, 0, 0, lane))
+
+
+def table(lead=0):
+    return pl.BlockSpec((2 * BLK, 128), lambda s, h, *_: (s + lead, 0))
+
+
+def piece(x, first=0, lane=None, lead=0):
+    return pl.BlockSpec((1, 1, 2, BLK, 128), lambda s, h, *_: (first, s + lead, 0, 0, h if lane is None else lane))
 
 
 def attention_call(kernel, name, mats, seqs, pairs, blocks, in_specs, out_specs, out_shape, scratch, args):
@@ -253,26 +252,27 @@
     seqs, pairs, blocks = q.shape[0], q.shape[2] // 128, place.shape[1]
     return attention_call(
         functools.partial(dq_kernel, blocks=blocks, n=len(keys)), "query_grad", 3, seqs, pairs, blocks,
-        [OWN, OWN, EXT, EXT, TABLE, TABLE, TABLE] + [piece(*e) for e in keys + values], OWN,
+        [OWN, OWN, EXT, EXT] + [table()] * 3 + [piece(*e) for e in keys + values], OWN,
         jax.ShapeDtypeStruct(q.shape, jnp.bfloat16),
         [rows_of(blocks, 256), rows_of(blocks, 256), acc_of(128)],
         [place, own, q, do, q_ext, do_ext, *tabs] + [e[0] for e in keys + values])
 
 
-def key_value_grad(place, own, kv, tabs, queries, grads):
-    seqs, pairs, blocks = kv.shape[1], kv.shape[3] // 128, place.shape[1]
-    shape = kv.shape[1:]
+def key_value_grad(place, own, kv, tabs, queries, grads, lead, count):
+    pairs, blocks = kv.shape[3] // 128, place.shape[1]
+    shape = (count,) + kv.shape[2:]
+    both = queries + grads
 
     def own_part(i):
-        return pl.BlockSpec((1, 1, 2 * BLK, 128), lambda s, h, *_: (i, s, 0, h))
+        return pl.BlockSpec((1, 1, 2 * BLK, 128), lambda s, h, *_: (i, s + lead, 0, h))
 
     return attention_call(
-        functools.partial(dkv_kernel, blocks=blocks, n=len(queries)), "key_value_grad", 4, seqs, pairs, blocks,
-        [own_part(0), own_part(1), TABLE, TABLE, TABLE] + [piece(*e) for e in queries + grads]
-        + [piece(*e, lane=pairs) for e in queries + grads], [OWN, OWN],
+        functools.partial(dkv_kernel, blocks=blocks, n=len(queries), lead=lead), "key_value_grad", 4, count, pairs, blocks,
+        [own_part(0), own_part(1)] + [table(lead)] * 3 + [piece(x, lead=lead) for x in both]
+        + [piece(x, lane=pairs, lead=lead) for x in both], [OWN, OWN],
         [jax.ShapeDtypeStruct(shape, jnp.bfloat16)] * 2,
         [rows_of(blocks, 256), rows_of(blocks, 256), acc_of(128), acc_of(128)],
-        [place, own, kv, kv, *tabs] + [e[0] for e in queries + grads] * 2)
+        [place, own, kv, kv, *tabs] + both * 2)
 
 
 import math
@@ -420,32 +420,27 @@
     return lax.dynamic_slice_in_dim(x, (side if mine else 1 - side) * r, r, 0)
 
 
-def weight_grad(left, right, split_left):
+def weight_grad(part):
     core = lax.axis_index("ctx") & 1
-    split = left if split_left else right
-    w = split.shape[1] // 2
-
-    def part(which):
-        cut = lax.dynamic_slice_in_dim(split, which * w, w, 1)
-        return rc(cut, right) if split_left else rc(left, cut)
-
     got = ctx_swap(part(1 - core).astype(BF16), 1)
-    gate = yield [got]
+    gate = yield
     half = (part(core) + after(got, gate).astype(F32)).astype(BF16)
     bits = list(range(1, int(math.log2(lax.axis_size("ctx")))))
     orders = [bits, bits[::-1]]
     r = half.shape[0] // 2
     streams = [half[:r], half[r:]]
-    yield streams
+    gate = yield streams
     for i in range(len(bits)):
+        streams = after(streams, gate)
         got = [ctx_swap(half_of(x, o[i], False), 1 << o[i]) for x, o in zip(streams, orders)]
-        gate = yield got
+        gate = yield
         streams, got = after((streams, got), gate)
         streams = [add16(half_of(x, o[i], True), g) for x, o, g in zip(streams, orders, got)]
-        yield streams
+        gate = yield streams
     for i in reversed(range(len(bits))):
+        streams = after(streams, gate)
         got = [ctx_swap(x, 1 << o[i]) for x, o in zip(streams, orders)]
-        gate = yield got
+        gate = yield
         streams, got = after((streams, got), gate)
         streams = [
             jnp.where(((lax.axis_index("ctx") >> o[i]) & 1) == 0, jnp.concatenate([x, g]), jnp.concatenate([g, x]))
@@ -453,16 +448,11 @@
         ]
         if i == 0:
             streams = jnp.concatenate(streams)
-        yield streams
+        gate = yield streams
+    streams = after(streams, gate)
     other = ctx_swap(streams, 1)
-    gate = yield [other]
+    gate = yield
     yield after((streams, other), gate)
-
-
-def advance(chain, gate=None):
-    held = chain.send(gate)
-    next(chain)
-    return held
 
 
 def begin(*args):
@@ -471,8 +461,18 @@
     return chain
 
 
-def finish(chain, gate=None):
+def take(chain, gate=None):
     return chain.send(gate)
+
+
+def go(chain, gate=None):
+    chain.send(gate)
+
+
+def take_extra(chain):
+    for _ in range(2 * int(math.log2(lax.axis_size("ctx"))) - 6):
+        go(chain)
+        take(chain)
 
 
 def unpack_rows_kernel(core_ref, half_ref, other_ref, *out_refs):
@@ -516,6 +516,11 @@
     )(core[None], half, other)
 
 
+def columns(x, which):
+    w = x.shape[1] // 2
+    return lax.dynamic_slice_in_dim(x, which * w, w, 1)
+
+
 def unpack_cols_kernel(core_ref, half_ref, other_ref, out_ref):
     c = half_ref.shape[1]
     core = core_ref[0]
@@ -523,8 +528,8 @@
     out_ref[:, pl.ds(pl.multiple_of((1 - core) * c, 128), c)] = other_ref[...].astype(F32)
 
 
-def unpack_cols(half, other):
-    r, c = half.shape
+def unpack_cols(half, other, r):
+    c = half.shape[1]
     step = math.gcd(r, 256)
     block = pl.BlockSpec((step, c), lambda i, _: (i, 0))
     return pl.pallas_call(
@@ -536,6 +541,33 @@
         compiler_params=pltpu.CompilerParams(vmem_limit_bytes=40 * 2**20),
         cost_estimate=pl.CostEstimate(flops=0, bytes_accessed=12 * r * c, transcendentals=0),
         name="unpack_cols",
+    )((lax.axis_index("ctx") & 1)[None], half, other)
+
+
+def unpack_turned_kernel(core_ref, half_ref, other_ref, out_ref):
+    @pl.when(pl.program_id(0) == core_ref[0])
+    def _():
+        out_ref[...] = half_ref[...].astype(F32).T
+
+    @pl.when(pl.program_id(0) != core_ref[0])
+    def _():
+        out_ref[...] = other_ref[...].astype(F32).T
+
+
+def unpack_turned(half, other, r):
+    c = half.shape[1]
+    step = 256
+    blocks = c // step
+    block = pl.BlockSpec((r, step), lambda i, j, _: (1, j))
+    return pl.pallas_call(
+        unpack_turned_kernel,
+        grid_spec=pltpu.PrefetchScalarGridSpec(
+            num_scalar_prefetch=1, grid=(2, blocks), in_specs=[block, block],
+            out_specs=pl.BlockSpec((step, r), lambda i, j, _: (i * blocks + j, 0))),
+        out_shape=jax.ShapeDtypeStruct((2 * c, r), F32),
+        compiler_params=pltpu.CompilerParams(vmem_limit_bytes=40 * 2**20),
+        cost_estimate=pl.CostEstimate(flops=0, bytes_accessed=12 * r * c, transcendentals=0),
+        name="unpack_turned",
     )((lax.axis_index("ctx") & 1)[None], half, other)
 
 
@@ -572,14 +604,26 @@
     return [held[j][0] for j in range(n)], [held[j][1] for j in range(n)]
 
 
-def gather_ctx(x):
+def gather_other(x):
+    held = {0: x, 1: ctx_swap(x, 1)}
+    for j in range(2, lax.axis_size("ctx"), 2):
+        held[j] = ctx_swap(x, j)
+    return held
+
+
+def gather_cores(held, gate=None):
     n = lax.axis_size("ctx")
-    held = [x] + [None] * (n - 1)
     for j in range(2, n, 2):
-        held[j] = ctx_swap(x, j)
-    for j in range(0, n, 2):
-        held[j + 1] = ctx_swap(held[j], 1)
-    return held
+        held[j + 1] = ctx_swap(after(held[j], gate), 1)
+    return [held[j] for j in range(n)]
+
+
+def sum_over_all(x):
+    for axis in ("ctx", "tp"):
+        n = lax.axis_size(axis)
+        for bit in range(int(math.log2(n))):
+            x = x + lax.ppermute(x, axis, [(i, i ^ (1 << bit)) for i in range(n)])
+    return x
 
 
 def local(tokens, cotangent, block_order, gain_one, shift_one, query_w, key_w, value_w, query_b, key_b, value_b,
@@ -607,8 +651,8 @@
     rows_w = output_w.shape[0] // n_ctx
     part = lax.dynamic_slice_in_dim(output_w, ctx * rows_w, rows_w, 0)
     part = lax.all_gather(after(part, rows_one), "tp", axis=0)
-    dy_rows = all_rows(after(cotangent, kv))
-    whole_w = lax.all_gather(after(part, dy_rows, arrived), "ctx", axis=1).reshape(n_tp * output_w.shape[0], -1)
+    dy_rows = all_rows(after(cotangent, rows_one))
+    whole_w = lax.all_gather(after(part, arrived), "ctx", axis=1).reshape(n_tp * output_w.shape[0], -1)
 
     attn, q_ext = attend(place, own, q, keys, values)
     attn_rows = attn.reshape(-1, width)
@@ -617,7 +661,7 @@
     normed_two, unit_two, inverse_two = layer_stats(mixed, gain_two, shift_two)
     rows_two = all_rows(after(normed_two.astype(BF16), dy_rows, whole_w))
     shape = (1, SEQS, 2, BLK, width + 128)
-    queries = gather_ctx(after(jnp.concatenate([q, q_ext], axis=2).reshape(shape), attn_own))
+    queries = gather_cores(gather_other(after(jnp.concatenate([q, q_ext], axis=2).reshape(shape), attn_own)))
     rows_two = after(rows_two, queries)
 
     act, grad_gu = mlp(rows_two, dy_rows, gate_w, up_w, down_w)
@@ -625,13 +669,17 @@
     part_two = (nt(grad_gu[:, :ff], gate_w) + nt(grad_gu[:, ff:], up_w)).astype(BF16)
     grad_two = sum_rows(part_two)
     act, rows_two, dy_rows, grad_gu = after((act, rows_two, dy_rows, grad_gu), part_two)
-    extra = 2 * int(math.log2(n_ctx)) - 6
-    gu = begin(rows_two, grad_gu, True)
+    gu = begin(lambda core: rc(columns(rows_two, core), grad_gu))
     down = nn(act, down_w).astype(BF16)
-    held = advance(gu)
-    dw = begin(act, after(dy_rows, held), False)
-    held = advance(dw), advance(gu)
-    grad_two = after(grad_two, held, down)
+    held = take(gu)
+    go(gu)
+    dy_late = after(dy_rows, held)
+    dw = begin(lambda core: rc(act, columns(dy_late, core)))
+    take(gu)
+    go(gu)
+    grad_two = after(grad_two, take(gu), take(dw), down)
+    go(gu)
+    go(dw)
 
     norm_two, grad_gain_two, grad_shift_two = layer_back(grad_two, unit_two, inverse_two, gain_two)
     grad_mixed = cotangent.astype(F32) + norm_two
@@ -639,58 +687,73 @@
     grad_attn = nt(branch_own, whole_w).astype(BF16)
     grad_attn = lax.all_to_all(grad_attn, "tp", split_axis=1, concat_axis=0, tiled=True)
     branch = all_rows(after(branch_own, grad_attn))
-    out_tokens = (mixed + sum_rows(after(down, branch))).astype(BF16)
+    out_tokens = (mixed + sum_rows(after(down, grad_attn))).astype(BF16)
     lane = jnp.arange(128)[None, :]
     ind = ((jnp.arange(width) // HEAD_DIM)[:, None] == lane // 3).astype(F32)
     delta = lax.dot_general(grad_attn.astype(F32) * attn_rows.astype(F32), ind, (((1,), (0,)), ((), ())),
                             precision=lax.Precision.HIGHEST, preferred_element_type=F32)
     do_ext = terms(-delta, lane).astype(BF16)
-    held = advance(gu), advance(dw)
-    grads = gather_ctx(jnp.concatenate([grad_attn, do_ext], axis=1).reshape(shape))
-    grad_attn = after(grad_attn, held)
+    do_sent = jnp.concatenate([grad_attn, do_ext], axis=1).reshape(shape)
+    grads = gather_other(after(do_sent, take(gu), take(dw)))
     grad_q = query_grad(place, own, q, grad_attn.reshape(q.shape), q_ext, do_ext.reshape(q_ext.shape), tabs, keys, values)
     grad_q = grad_q.reshape(-1, width)
     q_part = nt(grad_q, query_w)
-    grads = after(grads, q_part)
-    held = [advance(gu, grads) for _ in range(1 + extra)] + [advance(dw, grads)]
-    grad_k, grad_v = key_value_grad(place, own, kv, tabs, [(x, 0) for x in queries], [(x, 0) for x in after(grads, held)])
-    grad_k, grad_v = (g.reshape(-1, width) for g in (grad_k, grad_v))
+    grads = gather_cores(grads, q_part)
+    go(gu, grads)
+    go(dw, grads)
+    rows_q, branch = after((rows_one, branch), grads)
+    oq = begin(lambda core: jnp.concatenate([rc(attn_rows, columns(branch, core)), rc(grad_q, columns(rows_q, core))]))
+    first = key_value_grad(place, own, kv, tabs, queries, grads, 0, SEQS // 2)
+    grads = after(grads, take(gu, first), take(dw, first), take(oq, first))
+    take_extra(gu)
+    go(gu)
+    go(dw)
+    go(oq)
+    second = key_value_grad(place, own, kv, tabs, queries, grads, SEQS // 2, SEQS // 2)
+    grad_k, grad_v = (jnp.concatenate(pair).reshape(-1, width) for pair in zip(first, second))
     part_one = q_part + nt(grad_k, key_w) + nt(grad_v, value_w)
     part_sent = part_one.astype(BF16)
     grad_one = sum_rows(part_sent)
 
-    rows_one, branch, grad_q, grad_k, grad_v = after((rows_one, branch, grad_q, grad_k, grad_v), part_sent)
+    rows_one, grad_q, grad_k, grad_v = after((rows_one, grad_q, grad_k, grad_v), part_sent)
+    grad_kv = jnp.concatenate([grad_k, grad_v], axis=1)
+    dkv = begin(lambda core: rc(columns(rows_one, core), grad_kv))
+    take(dw, part_sent)
+    go(dw)
+    take(oq, part_sent)
+    go(oq)
     unit_rows = (rows_one.astype(F32) - shift_one) / gain_one
-    grad_qkv = jnp.concatenate([grad_q, grad_k, grad_v], axis=1)
-    bias_grad = jnp.sum(grad_qkv.astype(F32), axis=0)
+    bias_grad = jnp.concatenate([jnp.sum(g.astype(F32), axis=0) for g in (grad_q, grad_kv)])
     tp_row = (jnp.arange(n_tp) == lax.axis_index("tp"))[:, None]
     small = jnp.concatenate([
         jnp.sum(part_one * unit_rows, axis=0), jnp.sum(part_one, axis=0), grad_gain_two, grad_shift_two,
         jnp.where(tp_row, bias_grad[None, :], 0.0).reshape(-1)])
-    qkv = begin(rows_one, grad_qkv, True)
-    for _ in range(1 + extra):
-        advance(dw, part_sent)
-    out = begin(attn_rows, branch, False)
-    held = advance(qkv)
-    advance(gu, held)
-    held = advance(out, held)
-    small = lax.psum(after(small, held), ("ctx", "tp"))
+    held = take(dkv)
+    go(dkv)
+    small = sum_over_all(after(small, held).reshape(-1, 1024)).reshape(-1)
     depth = x.shape[1]
     norms = small[:4 * depth].reshape(4, depth)
     bias_sum = jnp.sum(jnp.where(tp_row, small[4 * depth:].reshape(n_tp, -1), 0.0), axis=0)
-    advance(qkv, small)
-    advance(dw, small)
-    grad_gate_w, grad_up_w = unpack_rows(*finish(gu), 2)
-    held = advance(out), advance(qkv, (grad_gate_w, grad_up_w))
-    grad_down_w = unpack_cols(*finish(dw, held))
-    for _ in range(1 + extra):
-        advance(out)
-        advance(qkv, grad_down_w)
-    advance(qkv)
-    for _ in range(2):
-        advance(out)
-    grad_output_w = unpack_cols(*finish(out))
-    grad_query_w, grad_key_w, grad_value_w = unpack_rows(*finish(qkv), 3)
+    grad_gate_w, grad_up_w = unpack_rows(*take(gu, held), 2)
+    held = take(dkv), take(oq), take(dw)
+    go(dkv)
+    go(oq)
+    take_extra(dw)
+    go(dw)
+    held = take(dkv, (held, grad_gate_w)), take(oq, held)
+    go(dkv)
+    go(oq)
+    grad_down_w = unpack_cols(*take(dw, held), act.shape[1])
+    held = take(dkv, grad_down_w), take(oq, grad_down_w)
+    take_extra(oq)
+    take_extra(dkv)
+    go(dkv)
+    go(oq)
+    halves = take(oq, held)
+    grad_output_w, grad_query_w = unpack_cols(*halves, width), unpack_turned(*halves, width)
+    take(dkv, held)
+    go(dkv)
+    grad_key_w, grad_value_w = unpack_rows(*take(dkv), 2)
     norm_one, _, _ = layer_back(grad_one, unit_one, inverse_one, gain_one)
     grad_tokens = (grad_mixed + norm_one).astype(BF16)
     return (

time: 1070 us -> 1050 us (0.981)
  blocking collectives: 80 us -> 64 us
  other arithmetic: 90.9 us -> 79.8 us
    psum x1 -> x0, blocking collectives: 50.5 us -> none  [local(): small = lax.psum(after(small, held), ('ctx', 'tp'))]
    all_to_all x0 -> x1, blocking collectives: none -> 28.9 us  [local(): lax.all_to_all(grad_attn, 'tp', split_axis=1, concat_axis=0, tiled=True)]
    all_gather x4, waiting for transfers between devices: 113 us -> 139 us  [all_rows(): return lax.all_gather(x, 'tp', axis=0, tiled=True)]
    ppermute x63, waiting for transfers between devices: 248 us -> 229 us  [ctx_swap(): return lax.ppermute(x, 'ctx', [(i, i ^ mask) for i in range(n)])]
    all_to_all x1 -> x0, waiting for transfers between devices: 17.2 us -> none  [local(): lax.all_to_all(grad_attn, 'tp', split_axis=1, concat_axis=0, tiled=True)]
    ppermute x0 -> x5, waiting for transfers between devices: none -> 15.9 us  [sum_over_all(): x = x + lax.ppermute(x, axis, [(i, i ^ 1 << bit) for i in range(n)])]
    pallas_call x3 -> x4, Pallas kernels: 172 us -> 161 us  [attention_call(): pl.pallas_call(kernel, grid_spec=pltpu.PrefetchScalarGridSpec(num_scalar_...]
    unnamed x177 -> x181, local copies, waits for them, and re-layouts: 25.2 us -> 16.4 us
  transfers between devices with their start and end apart: 73 -> 77, of which waited for: 31 -> 35; matrix products, arithmetic and copies ran while one was open for 19% -> 17% of each run, Pallas kernels for 19% -> 19%
where the time goes in v4:
time: 1050 us; the launch traced here: 1040 us
  waiting for transfers between devices  388 us (37%)
  Pallas kernels  238 us (23%)
  matrix products  121 us (12%)
  other arithmetic  79.8 us (8%)
  starting transfers between devices  78.3 us (7%)
  blocking collectives  64 us (6%)
  local copies, waits for them, and re-layouts  54.5 us (5%)
  between operations  15.9 us (2%)
    ppermute x63, waiting for transfers between devices, ctx_swap(): return lax.ppermute(x, 'ctx', [(i, i ^ mask) for i in range(n)])  229 us
    pallas_call x4, Pallas kernels, attention_call(): pl.pallas_call(kernel, grid_spec=pltpu.PrefetchScalarGridSpec(num_scalar_...  161 us
    all_gather x4, waiting for transfers between devices, all_rows(): return lax.all_gather(x, 'tp', axis=0, tiled=True)  139 us
    ppermute x63, starting transfers between devices, ctx_swap(): return lax.ppermute(x, 'ctx', [(i, i ^ mask) for i in range(n)])  74.2 us
    dot_general x10, matrix products, rc(): lax.dot_general(left, right, (((0,), (0,)), ((), ())), preferred_element_...  52.5 us
    dot_general x6, matrix products, nt(): lax.dot_general(a, b, (((1,), (1,)), ((), ())), preferred_element_type=jn...  50.1 us
    all_to_all x1, blocking collectives, local(): lax.all_to_all(attn_rows, 'tp', split_axis=0, concat_axis=1, tiled=True)  35.2 us
    pallas_call x1, Pallas kernels, mlp(): pl.pallas_call(mlp_kernel, grid=(total // step,), in_specs=[block, block,...  28.9 us
  transfers between devices with their start and end apart: 77, of which 35 were waited for; matrix products, arithmetic and copies ran while one was open for 17% of the time, Pallas kernels for 19%

profile of v4, /device:TPU:0, one launch (start us, length us, event | category | flops | bytes accessed | tf_op | source)
XLA Modules:
  0.0 1039.6 jit_solution(11780916208845031925)
XLA Ops:
  12.8 3.0 multiply_sine_fusion
  19.2 2.8 concatenate.156.b_ref
  23.0 3.7 concatenate.154.c_ref
  26.7 69.6 %all-gather.9.cloned.1.call-done.h_ref = bf16[1024,2048]{1,0:T(8,128)(2,1)} async-done(((bf16[256,2048]{1,0:T(8,128)(2,1)}), bf16[1024,2048]{1,0:T(8,128)(2,1)}) %all-gather.9.cloned.1.call-update) | async-done | bytes 4194320 | tf_op jit(solution)/shard_map/all_gather | solution.py:575
  97.3 11.3 %project.1 = (bf16[4,256,512]{2,1,0:T(8,128)(2,1)S(1)}, bf16[2,4,256,512]{3,2,1,0:T(8,128)(2,1)}) custom-call(bf16[1024,2048]{1,0:T(8,128)(2,1)} %all-gather.9.cloned.1.call-done.h_ref, bf16[2048,512]{1,0:T(8,128)(2,1)} %wq_ref.1, bf16[2048,512]{1,0:T(8,128)(2,1)} %wk_ref.1, bf16[2048,512]{1,0:T(8,128)(2,1)} %wv_ref.1, ...), custom_call_target="tpu_custom_call" | custom-call | flops 6442450944 | bytes 6291456 | tf_op jit(solution)/shard_map/project/pallas_call | solution.py:350
  111.5 44.7 %collective-permute-done.1.refs_2_.refs_10_ = bf16[2,4,2,128,512]{4,3,2,1,0:T(8,128)(2,1)} collective-permute-done((bf16[2,4,2,128,512]{4,3,2,1,0:T(8,128)(2,1)}, bf16[2,4,2,128,512]{4,3,2,1,0:T(8,128)(2,1)}, u32[]{:S(2)}, u32[]{:S(2)}) %collective-permute-start.1) | collective-permute-done | bytes 2097184 | tf_op jit(solution)/shard_map/ppermute | solution.py:406
  165.0 17.8 %collective-permute-done.5.refs_6_ = bf16[1,4,2,128,512]{4,3,2,1,0:T(8,128)(2,1)} collective-permute-done((bf16[1,4,2,128,512]{4,3,2,1,0:T(8,128)(2,1)}, bf16[1,4,2,128,512]{4,3,2,1,0:T(8,128)(2,1)}, u32[]{:S(2)}, u32[]{:S(2)}) %collective-permute-start.5) | collective-permute-done | bytes 1048608 | tf_op jit(solution)/shard_map/ppermute | solution.py:406
  182.8 3.4 collective-permute-done.7.refs_14_
  186.3 3.6 all-gather.17.cloned.1.call-done
  191.2 46.4 %attend.1 = (bf16[4,256,512]{2,1,0:T(8,128)(2,1)S(1)}, bf16[4,256,128]{2,1,0:T(8,128)(2,1)S(1)}) custom-call(s32[4,16]{1,0:T(4,128)S(1)} %copy.51.place_ref, s32[4,2]{1,0:T(4,128)S(1)} %get-tuple-element.331.own_ref, bf16[4,256,512]{2,1,0:T(8,128)(2,1)S(1)} %copy-done.19, bf16[2,4,2,128,512]{4,3,2,1,0:T(8,128)(2,1)} %bitcast.5.refs_0_.refs_8_, ...), custom_call_target="tpu_custom_call" | custom-call | flops 8589934592 | bytes 16777216 | tf_op jit(solution)/shard_map/attend/pallas_call | solution.py:222
  238.6 35.2 %all_to_all.35 = bf16[4,256,512]{2,1,0:T(8,128)(2,1)} all-to-all(bf16[4,256,512]{2,1,0:T(8,128)(2,1)S(1)} %get-tuple-element.170), channel_id=1, replica_groups=mesh['ctx'=8,'tp'=4] {'tp'}, dimensions={0} | all-to-all | bytes 2097152 | tf_op jit(solution)/shard_map/all_to_all | solution.py:659
  276.0 6.1 fusion.79
  285.0 51.9 %all-gather.11.cloned.1.call-done.dy_ref = bf16[1024,2048]{1,0:T(8,128)(2,1)} async-done(((bf16[256,2048]{1,0:T(8,128)(2,1)}), bf16[1024,2048]{1,0:T(8,128)(2,1)}) %all-gather.11.cloned.1.call-update) | async-done | bytes 4194320 | tf_op jit(solution)/shard_map/all_gather | solution.py:575
  337.3 5.8 collective-permute-start.12
  344.5 24.2 %collective-permute-done.10.refs_2_.refs_18_ = bf16[1,4,2,128,640]{4,3,2,1,0:T(8,128)(2,1)S(1)} collective-permute-done((bf16[1,4,2,128,640]{4,3,2,1,0:T(8,128)(2,1)S(1)}, bf16[1,4,2,128,640]{4,3,2,1,0:T(8,128)(2,1)S(1)}, u32[]{:S(2)}, u32[]{:S(2)}) %collective-permute-start.10) | collective-permute-done | bytes 1310752 | tf_op jit(solution)/shard_map/ppermute | solution.py:406
  368.7 30.7 %collective-permute-done.12.refs_4_.refs_20_ = bf16[1,4,2,128,640]{4,3,2,1,0:T(8,128)(2,1)} collective-permute-done((bf16[1,4,2,128,640]{4,3,2,1,0:T(8,128)(2,1)S(1)}, bf16[1,4,2,128,640]{4,3,2,1,0:T(8,128)(2,1)}, u32[]{:S(2)}, u32[]{:S(2)}) %collective-permute-start.12) | collective-permute-done | bytes 1310752 | tf_op jit(solution)/shard_map/ppermute | solution.py:406
  404.8 17.5 %all-gather.13.cloned.1.call-done.h_ref = bf16[1024,2048]{1,0:T(8,128)(2,1)} async-done(((bf16[256,2048]{1,0:T(8,128)(2,1)}), bf16[1024,2048]{1,0:T(8,128)(2,1)}) %all-gather.13.cloned.1.call-update) | async-done | bytes 4194320 | tf_op jit(solution)/shard_map/all_gather | solution.py:575
  422.3 28.9 %mlp.1 = (bf16[1024,1408]{1,0:T(8,128)(2,1)}, bf16[1024,2816]{1,0:T(8,128)(2,1)}) custom-call(bf16[1024,2048]{1,0:T(8,128)(2,1)} %all-gather.13.cloned.1.call-done.h_ref, bf16[1024,2048]{1,0:T(8,128)(2,1)} %all-gather.11.cloned.1.call-done.dy_ref, bf16[2048,1408]{1,0:T(8,128)(2,1)} %gate_ref.1, bf16[2048,1408]{1,0:T(8,128)(2,1)} %up_ref.1, ...), custom_call_target="tpu_custom_call" | custom-call | flops 17716740096 | bytes 38273024 | tf_op jit(solution)/shard_map/mlp/pallas_call | solution.py:390
  451.2 9.8 fusion.2
  461.0 11.1 %add_convert_fusion.1 = bf16[1024,2048]{1,0:T(8,128)(2,1)} fusion(f32[1024,2048]{1,0:T(8,128)S(1)} %fusion.2, bf16[2048,1408]{1,0:T(8,128)(2,1)} %up_ref.1, bf16[1024,2816]{1,0:T(8,128)(2,1)S(1)} %copy-done.79), kind=kOutput, calls=%fused_computation.3 | convolution fusion | flops 5909774336 | bytes 21233664 | tf_op jit(solution)/shard_map/dot_general | solution.py:15
  472.0 11.0 %convolution_convert_fusion = bf16[1024,2816]{1,0:T(8,128)(2,1)} fusion(bf16[1024,2816]{1,0:T(8,128)(2,1)} %get-tuple-element.182, bf16[1024,2048]{1,0:T(8,128)(2,1)} %all-gather.13.cloned.1.call-done.h_ref, s32[]{:T(128)S(6)} %select_n.249), kind=kOutput, calls=%fused_computation.6 | convolution fusion | flops 5908463616 | bytes 13631492 | tf_op jit(solution)/shard_map/dot_general | solution.py:290
  483.1 12.1 %fusion.38 = f32[1024,2816]{1,0:T(8,128)} fusion(bf16[1024,2816]{1,0:T(8,128)(2,1)} %get-tuple-element.182, bf16[1024,2048]{1,0:T(8,128)(2,1)} %all-gather.13.cloned.1.call-done.h_ref, s32[]{:T(128)S(6)} %select_n.248), kind=kOutput, calls=%fused_computation.68 | convolution fusion | flops 5905580032 | bytes 19398660 | tf_op jit(solution)/shard_map/dot_general | solution.py:290
  495.2 9.7 add_convert_fusion
  504.9 3.1 fusion.74
  513.5 7.4 convolution_convert_fusion.2
  520.9 22.8 %collective-permute-done.17 = bf16[256,2816]{1,0:T(8,128)(2,1)} collective-permute-done((bf16[256,2816]{1,0:T(8,128)(2,1)}, bf16[256,2816]{1,0:T(8,128)(2,1)}, u32[]{:S(2)}, u32[]{:S(2)}) %collective-permute-start.17) | collective-permute-done | bytes 1441824 | tf_op jit(solution)/shard_map/ppermute | solution.py:406
  553.2 11.0 %convolution_convert_fusion.1 = bf16[1024,2048]{1,0:T(8,128)(2,1)} fusion(bf16[1024,1408]{1,0:T(8,128)(2,1)S(1)} %copy-done.80, bf16[1408,2048]{1,0:T(8,128)(2,1)} %down_ref.1), kind=kOutput, calls=%fused_computation.11 | convolution fusion | flops 5907677184 | bytes 12845056 | tf_op jit(solution)/shard_map/dot_general | solution.py:19
  564.2 8.3 fusion.35
  577.7 4.6 add_convert_fusion.2
  588.6 7.1 convolution_convert_fusion.3
  598.4 28.9 %all_to_all.36 = bf16[256,4,512]{2,0,1:T(8,128)(2,1)S(1)} all-to-all(bf16[256,4,512]{2,0,1:T(8,128)(2,1)} %copy.54), channel_id=1, replica_groups=mesh['ctx'=8,'tp'=4] {'tp'}, dimensions={1} | all-to-all | bytes 2097152 | tf_op jit(solution)/shard_map/all_to_all | solution.py:688
  630.0 14.8 %collective-permute-done.22 = bf16[128,2816]{1,0:T(8,128)(2,1)} collective-permute-done((bf16[128,2816]{1,0:T(8,128)(2,1)}, bf16[128,2816]{1,0:T(8,128)(2,1)}, u32[]{:S(2)}, u32[]{:S(2)}) %collective-permute-start.22) | collective-permute-done | bytes 720928 | tf_op jit(solution)/shard_map/ppermute | solution.py:406
  650.0 2.9 maximum_select_fusion.2
  652.8 3.0 maximum_select_fusion.3
  655.8 6.8 collective-permute-done.24
  673.5 46.1 %query_grad.1 = bf16[4,256,512]{2,1,0:T(8,128)(2,1)S(1)} custom-call(s32[4,16]{1,0:T(4,128)S(1)} %copy.51.place_ref, s32[4,2]{1,0:T(4,128)S(1)} %get-tuple-element.331.own_ref, bf16[4,256,512]{2,1,0:T(8,128)(2,1)S(1)} %copy-done.20, bf16[4,256,512]{2,1,0:T(8,128)(2,1)S(1)} %bitcast.79, bf16[4,256,128]{2,1,0:T(8,128)(2,1)S(1)} %get-tuple-element.175.qx_ref, ...), custom_call_target="tpu_custom_call" | custom-call | flops 12884901888 | bytes 16777216 | tf_op jit(solution)/shard_map/query_grad/pallas_call | solution.py:222
  719.6 5.8 fusion.81
  725.3 9.4 collective-permute-start.28
  741.4 3.3 collective-permute-start.34
  751.0 34.1 %key_value_grad.2 = (bf16[2,256,512]{2,1,0:T(8,128)(2,1)S(1)}, bf16[2,256,512]{2,1,0:T(8,128)(2,1)S(1)}) custom-call(s32[4,16]{1,0:T(4,128)S(1)} %copy.51.place_ref, s32[4,2]{1,0:T(4,128)S(1)} %get-tuple-element.331.own_ref, bf16[2,4,256,512]{3,2,1,0:T(8,128)(2,1)} %get-tuple-element.169.k_ref.v_ref, ...), custom_call_target="tpu_custom_call" | custom-call | flops 8589934592 | bytes 8388608 | tf_op jit(solution)/shard_map/key_value_grad/pallas_call | solution.py:222
  788.4 3.3 fusion.46
  795.5 8.9 collective-permute-start.53
  808.9 3.3 pad_maximum_fusion.half_ref
  821.0 34.4 %key_value_grad.3 = (bf16[2,256,512]{2,1,0:T(8,128)(2,1)S(1)}, bf16[2,256,512]{2,1,0:T(8,128)(2,1)S(1)}) custom-call(s32[4,16]{1,0:T(4,128)S(1)} %copy.51.place_ref, s32[4,2]{1,0:T(4,128)S(1)} %get-tuple-element.331.own_ref, bf16[2,4,256,512]{3,2,1,0:T(8,128)(2,1)} %get-tuple-element.169.k_ref.v_ref, ...), custom_call_target="tpu_custom_call" | custom-call | flops 8589934592 | bytes 8388608 | tf_op jit(solution)/shard_map/key_value_grad/pallas_call | solution.py:222
  857.2 5.8 fusion.82
  863.0 10.7 %fusion.80 = (bf16[1024,2048]{1,0:T(8,128)(2,1)}, f32[1024,2048]{1,0:T(8,128)}) fusion(f32[1024,2048]{1,0:T(8,128)} %fusion.82, f32[1024,2048]{1,0:T(8,128)S(1)} %bitcast.96, bf16[1024,512]{1,0:T(8,128)(2,1)S(1)} %bitcast.93, bf16[2048,512]{1,0:T(8,128)(2,1)S(1)} %copy-done.58), kind=kOutput, calls=%fused_computation.204 | convolution fusion | flops 2153775104 | bytes 32505856 | tf_op jit(solution)/shard_map/dot_general | solution.py:15
  874.0 4.2 fusion.40
  878.3 4.8 collective-permute-start.44
  889.5 6.4 collective-permute-done.44
  898.4 12.3 %collective-permute-done.54 = bf16[352,1024]{1,0:T(8,128)(2,1)S(1)} collective-permute-done((bf16[352,1024]{1,0:T(8,128)(2,1)S(1)}, bf16[352,1024]{1,0:T(8,128)(2,1)S(1)}, u32[]{:S(2)}, u32[]{:S(2)}) %collective-permute-start.54) | collective-permute-done | bytes 720928 | tf_op jit(solution)/shard_map/ppermute | solution.py:406
  924.4 8.3 collective-permute-done.50
  936.1 13.5 %unpack_rows.2 = (f32[2048,1408]{1,0:T(8,128)}, f32[2048,1408]{1,0:T(8,128)}) custom-call(s32[1]{0:T(128)} %bitcast.22.core_ref, bf16[1024,2816]{1,0:T(8,128)(2,1)} %pad_maximum_fusion.half_ref, bf16[1024,2816]{1,0:T(8,128)(2,1)} %collective-permute-done.61.other_ref), custom_call_target="tpu_custom_call" | custom-call | bytes 34603008 | tf_op jit(solution)/shard_map/unpack_rows/pallas_call | solution.py:506
  954.6 6.3 unpack_cols.2
  965.0 7.6 collective-permute-done.56
  973.8 7.3 collective-permute-done.65
  984.4 3.1 collective-permute-done.39
  989.2 2.8 collective-permute-done.40
  992.5 3.9 collective-permute-done.41
  996.4 4.3 collective-permute-done.42
  1001.0 3.1 add_convert_fusion.6
  1009.9 6.5 unpack_turned.1
  1016.4 3.2 unpack_cols.3
  1019.6 7.7 unpack_rows.3
  1029.4 3.2 fusion.15
  (444 shorter events, 169.8 us)
Async XLA Ops:
  7.2 89.0 %all-gather.9.cloned.1.call-start = ((), (), s32[]{:S(2)}) async-start(), calls=%async_computation.5 | async-start | bytes 5242880 | tf_op jit(solution)/shard_map/all_gather | solution.py:575
  12.6 177.3 %all-gather.17.cloned.1.call-start = ((), (), s32[]{:S(2)}) async-start(), calls=%async_computation.12 | async-start | bytes 1310720 | tf_op jit(solution)/shard_map/all_gather | solution.py:653
  108.5 47.7 %collective-permute-start.1 = (bf16[2,4,2,128,512]{4,3,2,1,0:T(8,128)(2,1)}, bf16[2,4,2,128,512]{4,3,2,1,0:T(8,128)(2,1)}, u32[]{:S(2)}, u32[]{:S(2)}) collective-permute-start(bf16[2,4,2,128,512]{4,3,2,1,0:T(8,128)(2,1)} %bitcast.5.refs_0_.refs_8_), channel_id=1, source_target_pairs={{0,8},{4,12},{8,0},{12,4},{16,24},{20,28},{24,16},{28,20},{1,9},{5... | collective-permute-start | bytes 6291464 | tf_op jit(solution)/shard_map/ppermute | solution.py:406
  110.0 49.9 %collective-permute-start.3 = (bf16[2,4,2,128,512]{4,3,2,1,0:T(8,128)(2,1)}, bf16[2,4,2,128,512]{4,3,2,1,0:T(8,128)(2,1)}, u32[]{:S(2)}, u32[]{:S(2)}) collective-permute-start(bf16[2,4,2,128,512]{4,3,2,1,0:T(8,128)(2,1)} %bitcast.5.refs_0_.refs_8_), channel_id=1, source_target_pairs={{0,16},{4,20},{8,24},{12,28},{16,0},{20,4},{24,8},{28,12},{1,17},{... | collective-permute-start | bytes 6291464 | tf_op jit(solution)/shard_map/ppermute | solution.py:406
  111.5 78.3 %collective-permute-start = (bf16[2,4,2,128,512]{4,3,2,1,0:T(8,128)(2,1)}, bf16[2,4,2,128,512]{4,3,2,1,0:T(8,128)(2,1)}, u32[]{:S(2)}, u32[]{:S(2)}) collective-permute-start(bf16[2,4,2,128,512]{4,3,2,1,0:T(8,128)(2,1)} %bitcast.5.refs_0_.refs_8_), channel_id=1, source_target_pairs={{0,4},{4,0},{8,12},{12,8},{16,20},{20,16},{24,28},{28,24},{1,5},{5... | collective-permute-start | bytes 6291464 | tf_op jit(solution)/shard_map/ppermute | solution.py:406
  158.5 24.4 %collective-permute-start.5 = (bf16[1,4,2,128,512]{4,3,2,1,0:T(8,128)(2,1)}, bf16[1,4,2,128,512]{4,3,2,1,0:T(8,128)(2,1)}, u32[]{:S(2)}, u32[]{:S(2)}) collective-permute-start(bf16[1,4,2,128,512]{4,3,2,1,0:T(8,128)(2,1)} %slice.103), channel_id=1, source_target_pairs={{0,16},{4,20},{8,24},{12,28},{16,0},{20,4},{24,8},{28,12},{1,17},{... | collective-permute-start | bytes 3145736 | tf_op jit(solution)/shard_map/ppermute | solution.py:406
  162.2 24.0 %collective-permute-start.7 = (bf16[1,4,2,128,512]{4,3,2,1,0:T(8,128)(2,1)}, bf16[1,4,2,128,512]{4,3,2,1,0:T(8,128)(2,1)}, u32[]{:S(2)}, u32[]{:S(2)}) collective-permute-start(bf16[1,4,2,128,512]{4,3,2,1,0:T(8,128)(2,1)} %slice.104), channel_id=1, source_target_pairs={{0,8},{4,12},{8,0},{12,4},{16,24},{20,28},{24,16},{28,20},{1,9},{5... | collective-permute-start | bytes 3145736 | tf_op jit(solution)/shard_map/ppermute | solution.py:406
  163.7 26.2 %collective-permute-start.2 = (bf16[2,4,2,128,512]{4,3,2,1,0:T(8,128)(2,1)}, bf16[2,4,2,128,512]{4,3,2,1,0:T(8,128)(2,1)}, u32[]{:S(2)}, u32[]{:S(2)}) collective-permute-start(bf16[2,4,2,128,512]{4,3,2,1,0:T(8,128)(2,1)} %collective-permute-done.1.refs_2_.refs_10_), channel_id=1, source_target_pairs={{0,4},{4,0},{8,12},{12,8},{16,20},{20,16},{24,28},{28,24},{1,5},{5... | collective-permute-start | bytes 6291464 | tf_op jit(solution)/shard_map/ppermute | solution.py:406
  163.7 26.2 %collective-permute-start.4 = (bf16[2,4,2,128,512]{4,3,2,1,0:T(8,128)(2,1)}, bf16[2,4,2,128,512]{4,3,2,1,0:T(8,128)(2,1)}, u32[]{:S(2)}, u32[]{:S(2)}) collective-permute-start(bf16[2,4,2,128,512]{4,3,2,1,0:T(8,128)(2,1)} %collective-permute-done.3.refs_4_.refs_12_), channel_id=1, source_target_pairs={{0,4},{4,0},{8,12},{12,8},{16,20},{20,16},{24,28},{28,24},{1,5},{5... | collective-permute-start | bytes 6291464 | tf_op jit(solution)/shard_map/ppermute | solution.py:406
  165.0 111.1 %all-gather.19.cloned.1.call-start = ((), (), s32[]{:S(2)}) async-start(), calls=%async_computation.13 | async-start | bytes 9437184 | tf_op jit(solution)/shard_map/all_gather | solution.py:655
  189.9 146.9 %all-gather.11.cloned.1.call-start = ((), (), s32[]{:S(2)}) async-start(), calls=%async_computation.6 | async-start | bytes 5242880 | tf_op jit(solution)/shard_map/all_gather | solution.py:575
  190.5 231.8 %all-gather.13.cloned.1.call-start = ((), (), s32[]{:S(2)}) async-start(), calls=%async_computation.7 | async-start | bytes 5242880 | tf_op jit(solution)/shard_map/all_gather | solution.py:575
  336.9 239.4 %reduce-scatter.4.cloned.1.call-start = ((), (), s32[]{:S(2)}) async-start(), calls=%async_computation.8 | async-start | bytes 5242880 | tf_op jit(solution)/shard_map/reduce_scatter | solution.py:579
  337.0 31.7 %collective-permute-start.10 = (bf16[1,4,2,128,640]{4,3,2,1,0:T(8,128)(2,1)S(1)}, bf16[1,4,2,128,640]{4,3,2,1,0:T(8,128)(2,1)S(1)}, u32[]{:S(2)}, u32[]{:S(2)}) collective-permute-start(bf16[1,4,2,128,640]{4,3,2,1,0:T(8,128)(2,1)S(1)} %bitcast.69), channel_id=1, source_target_pairs={{0,8},{4,12},{8,0},{12,4},{16,24},{20,28},{24,16},{28,20},{1,9},{5... | collective-permute-start | bytes 3932168 | tf_op jit(solution)/shard_map/ppermute | solution.py:406
  337.3 62.1 %collective-permute-start.12 = (bf16[1,4,2,128,640]{4,3,2,1,0:T(8,128)(2,1)S(1)}, bf16[1,4,2,128,640]{4,3,2,1,0:T(8,128)(2,1)}, u32[]{:S(2)}, u32[]{:S(2)}) collective-permute-start(bf16[1,4,2,128,640]{4,3,2,1,0:T(8,128)(2,1)S(1)} %bitcast.70), channel_id=1, source_target_pairs={{0,16},{4,20},{8,24},{12,28},{16,0},{20,4},{24,8},{28,12},{1,17},{... | collective-permute-start | bytes 3932168 | tf_op jit(solution)/shard_map/ppermute | solution.py:406
  343.1 58.2 %collective-permute-start.14 = (bf16[1,4,2,128,640]{4,3,2,1,0:T(8,128)(2,1)S(1)}, bf16[1,4,2,128,640]{4,3,2,1,0:T(8,128)(2,1)}, u32[]{:S(2)}, u32[]{:S(2)}) collective-permute-start(bf16[1,4,2,128,640]{4,3,2,1,0:T(8,128)(2,1)S(1)} %bitcast.71), channel_id=1, source_target_pairs={{0,24},{4,28},{8,16},{12,20},{16,8},{20,12},{24,0},{28,4},{1,25},{... | collective-permute-start | bytes 3932168 | tf_op jit(solution)/shard_map/ppermute | solution.py:406
  344.5 56.9 %collective-permute-start.9 = (bf16[1,4,2,128,640]{4,3,2,1,0:T(8,128)(2,1)S(1)}, bf16[1,4,2,128,640]{4,3,2,1,0:T(8,128)(2,1)}, u32[]{:S(2)}, u32[]{:S(2)}) collective-permute-start(bf16[1,4,2,128,640]{4,3,2,1,0:T(8,128)(2,1)S(1)} %bitcast.72), channel_id=1, source_target_pairs={{0,4},{4,0},{8,12},{12,8},{16,20},{20,16},{24,28},{28,24},{1,5},{5... | collective-permute-start | bytes 3932168 | tf_op jit(solution)/shard_map/ppermute | solution.py:406
  368.7 32.7 %collective-permute-start.11 = (bf16[1,4,2,128,640]{4,3,2,1,0:T(8,128)(2,1)S(1)}, bf16[1,4,2,128,640]{4,3,2,1,0:T(8,128)(2,1)}, u32[]{:S(2)}, u32[]{:S(2)}) collective-permute-start(bf16[1,4,2,128,640]{4,3,2,1,0:T(8,128)(2,1)S(1)} %collective-permute-done.10.refs_2_.refs_18_), channel_id=1, source_target_pairs={{0,4},{4,0},{8,12},{12,8},{16,20},{20,16},{24,28},{28,24},{1,5},{5... | collective-permute-start | bytes 3932168 | tf_op jit(solution)/shard_map/ppermute | solution.py:406
  483.0 12.2 %collective-permute-start.16 = (bf16[1024,2816]{1,0:T(8,128)(2,1)}, bf16[1024,2816]{1,0:T(8,128)(2,1)}, u32[]{:S(2)}, u32[]{:S(2)}) collective-permute-start(bf16[1024,2816]{1,0:T(8,128)(2,1)} %convolution_convert_fusion), channel_id=1, source_target_pairs={{0,4},{4,0},{8,12},{12,8},{16,20},{20,16},{24,28},{28,24},{1,5},{5... | collective-permute-start | bytes 17301512 | tf_op jit(solution)/shard_map/ppermute | solution.py:406
  483.0 305.3 %all-gather.15.cloned.1.call-start = ((), (), s32[]{:S(2)}) async-start(), calls=%async_computation.10 | async-start | bytes 5242880 | tf_op jit(solution)/shard_map/all_gather | solution.py:575
  509.3 34.3 %collective-permute-start.17 = (bf16[256,2816]{1,0:T(8,128)(2,1)}, bf16[256,2816]{1,0:T(8,128)(2,1)}, u32[]{:S(2)}, u32[]{:S(2)}) collective-permute-start(bf16[256,2816]{1,0:T(8,128)(2,1)} %constant_dynamic-slice_fusion.15), channel_id=1, source_target_pairs={{0,8},{4,12},{8,0},{12,4},{16,24},{20,28},{24,16},{28,20},{1,9},{5... | collective-permute-start | bytes 4325384 | tf_op jit(solution)/shard_map/ppermute | solution.py:406
  512.0 34.0 %collective-permute-start.18 = (bf16[256,2816]{1,0:T(8,128)(2,1)}, bf16[256,2816]{1,0:T(8,128)(2,1)}, u32[]{:S(2)}, u32[]{:S(2)}) collective-permute-start(bf16[256,2816]{1,0:T(8,128)(2,1)} %constant_dynamic-slice_fusion.14), channel_id=1, source_target_pairs={{0,16},{4,20},{8,24},{12,28},{16,0},{20,4},{24,8},{28,12},{1,17},{... | collective-permute-start | bytes 4325384 | tf_op jit(solution)/shard_map/ppermute | solution.py:406
  520.9 56.8 %collective-permute-start.21 = (bf16[1408,1024]{1,0:T(8,128)(2,1)}, bf16[1408,1024]{1,0:T(8,128)(2,1)}, u32[]{:S(2)}, u32[]{:S(2)}) collective-permute-start(bf16[1408,1024]{1,0:T(8,128)(2,1)} %convolution_convert_fusion.2), channel_id=1, source_target_pairs={{0,4},{4,0},{8,12},{12,8},{16,20},{20,16},{24,28},{28,24},{1,5},{5... | collective-permute-start | bytes 8650760 | tf_op jit(solution)/shard_map/ppermute | solution.py:406
  549.7 22.9 %collective-permute-start.19 = (bf16[128,2816]{1,0:T(8,128)(2,1)}, bf16[128,2816]{1,0:T(8,128)(2,1)S(1)}, u32[]{:S(2)}, u32[]{:S(2)}) collective-permute-start(bf16[128,2816]{1,0:T(8,128)(2,1)} %constant_dynamic-slice_fusion.13), channel_id=1, source_target_pairs={{0,16},{4,20},{8,24},{12,28},{16,0},{20,4},{24,8},{28,12},{1,17},{... | collective-permute-start | bytes 2162696 | tf_op jit(solution)/shard_map/ppermute | solution.py:406
  552.0 20.5 %collective-permute-start.20 = (bf16[128,2816]{1,0:T(8,128)(2,1)}, bf16[128,2816]{1,0:T(8,128)(2,1)}, u32[]{:S(2)}, u32[]{:S(2)}) collective-permute-start(bf16[128,2816]{1,0:T(8,128)(2,1)} %constant_dynamic-slice_fusion.12), channel_id=1, source_target_pairs={{0,8},{4,12},{8,0},{12,4},{16,24},{20,28},{24,16},{28,20},{1,9},{5... | collective-permute-start | bytes 2162696 | tf_op jit(solution)/shard_map/ppermute | solution.py:406
  627.3 373.7 %reduce-scatter.6.cloned.1.call-start = ((), (), s32[]{:S(2)}) async-start(), calls=%async_computation.9 | async-start | bytes 5242880 | tf_op jit(solution)/shard_map/reduce_scatter | solution.py:579
  627.8 17.0 %collective-permute-start.22 = (bf16[128,2816]{1,0:T(8,128)(2,1)}, bf16[128,2816]{1,0:T(8,128)(2,1)}, u32[]{:S(2)}, u32[]{:S(2)}) collective-permute-start(bf16[128,2816]{1,0:T(8,128)(2,1)} %add_convert_fusion.11), channel_id=1, source_target_pairs={{0,16},{4,20},{8,24},{12,28},{16,0},{20,4},{24,8},{28,12},{1,17},{... | collective-permute-start | bytes 2162696 | tf_op jit(solution)/shard_map/ppermute | solution.py:406
  628.5 16.8 %collective-permute-start.23 = (bf16[128,2816]{1,0:T(8,128)(2,1)}, bf16[128,2816]{1,0:T(8,128)(2,1)}, u32[]{:S(2)}, u32[]{:S(2)}) collective-permute-start(bf16[128,2816]{1,0:T(8,128)(2,1)} %add_convert_fusion.10), channel_id=1, source_target_pairs={{0,8},{4,12},{8,0},{12,4},{16,24},{20,28},{24,16},{28,20},{1,9},{5... | collective-permute-start | bytes 2162696 | tf_op jit(solution)/shard_map/ppermute | solution.py:406
  646.6 16.0 %collective-permute-start.24 = (bf16[352,1024]{1,0:T(8,128)(2,1)S(1)}, bf16[352,1024]{1,0:T(8,128)(2,1)S(1)}, u32[]{:S(2)}, u32[]{:S(2)}) collective-permute-start(bf16[352,1024]{1,0:T(8,128)(2,1)S(1)} %constant_dynamic-slice_fusion.11), channel_id=1, source_target_pairs={{0,8},{4,12},{8,0},{12,4},{16,24},{20,28},{24,16},{28,20},{1,9},{5... | collective-permute-start | bytes 2162696 | tf_op jit(solution)/shard_map/ppermute | solution.py:406
  649.5 15.7 %collective-permute-start.25 = (bf16[352,1024]{1,0:T(8,128)(2,1)S(1)}, bf16[352,1024]{1,0:T(8,128)(2,1)S(1)}, u32[]{:S(2)}, u32[]{:S(2)}) collective-permute-start(bf16[352,1024]{1,0:T(8,128)(2,1)S(1)} %constant_dynamic-slice_fusion.10), channel_id=1, source_target_pairs={{0,16},{4,20},{8,24},{12,28},{16,0},{20,4},{24,8},{28,12},{1,17},{... | collective-permute-start | bytes 2162696 | tf_op jit(solution)/shard_map/ppermute | solution.py:406
  669.8 65.7 %collective-permute-start.26 = (bf16[1,4,2,128,640]{4,3,2,1,0:T(8,128)(2,1)S(1)}, bf16[1,4,2,128,640]{4,3,2,1,0:T(8,128)(2,1)}, u32[]{:S(2)}, u32[]{:S(2)}) collective-permute-start(bf16[1,4,2,128,640]{4,3,2,1,0:T(8,128)(2,1)S(1)} %pad_maximum_fusion.6.refs_8_.refs_24_), channel_id=1, source_target_pairs={{0,4},{4,0},{8,12},{12,8},{16,20},{20,16},{24,28},{28,24},{1,5},{5... | collective-permute-start | bytes 3932168 | tf_op jit(solution)/shard_map/ppermute | solution.py:406
  669.9 55.5 %collective-permute-start.27 = (bf16[1,4,2,128,640]{4,3,2,1,0:T(8,128)(2,1)S(1)}, bf16[1,4,2,128,640]{4,3,2,1,0:T(8,128)(2,1)}, u32[]{:S(2)}, u32[]{:S(2)}) collective-permute-start(bf16[1,4,2,128,640]{4,3,2,1,0:T(8,128)(2,1)S(1)} %pad_maximum_fusion.6.refs_8_.refs_24_), channel_id=1, source_target_pairs={{0,8},{4,12},{8,0},{12,4},{16,24},{20,28},{24,16},{28,20},{1,9},{5... | collective-permute-start | bytes 3932168 | tf_op jit(solution)/shard_map/ppermute | solution.py:406
  670.3 64.4 %collective-permute-start.29 = (bf16[1,4,2,128,640]{4,3,2,1,0:T(8,128)(2,1)S(1)}, bf16[1,4,2,128,640]{4,3,2,1,0:T(8,128)(2,1)}, u32[]{:S(2)}, u32[]{:S(2)}) collective-permute-start(bf16[1,4,2,128,640]{4,3,2,1,0:T(8,128)(2,1)S(1)} %pad_maximum_fusion.6.refs_8_.refs_24_), channel_id=1, source_target_pairs={{0,16},{4,20},{8,24},{12,28},{16,0},{20,4},{24,8},{28,12},{1,17},{... | collective-permute-start | bytes 3932168 | tf_op jit(solution)/shard_map/ppermute | solution.py:406
  670.9 63.8 %collective-permute-start.31 = (bf16[1,4,2,128,640]{4,3,2,1,0:T(8,128)(2,1)S(1)}, bf16[1,4,2,128,640]{4,3,2,1,0:T(8,128)(2,1)}, u32[]{:S(2)}, u32[]{:S(2)}) collective-permute-start(bf16[1,4,2,128,640]{4,3,2,1,0:T(8,128)(2,1)S(1)} %pad_maximum_fusion.6.refs_8_.refs_24_), channel_id=1, source_target_pairs={{0,24},{4,28},{8,16},{12,20},{16,8},{20,12},{24,0},{28,4},{1,25},{... | collective-permute-start | bytes 3932168 | tf_op jit(solution)/shard_map/ppermute | solution.py:406
  725.3 12.4 %collective-permute-start.28 = (bf16[1,4,2,128,640]{4,3,2,1,0:T(8,128)(2,1)}, bf16[1,4,2,128,640]{4,3,2,1,0:T(8,128)(2,1)}, u32[]{:S(2)}, u32[]{:S(2)}) collective-permute-start(bf16[1,4,2,128,640]{4,3,2,1,0:T(8,128)(2,1)} %collective-permute-done.27.refs_10_.refs_26_), channel_id=1, source_target_pairs={{0,4},{4,0},{8,12},{12,8},{16,20},{20,16},{24,28},{28,24},{1,5},{5... | collective-permute-start | bytes 3932168 | tf_op jit(solution)/shard_map/ppermute | solution.py:406
  735.2 292.1 %reduce-scatter.8.cloned.1.call-start = ((), (), s32[]{:S(2)}) async-start(), calls=%async_computation.11 | async-start | bytes 5242880 | tf_op jit(solution)/shard_map/reduce_scatter | solution.py:579
  741.4 63.0 %collective-permute-start.33 = (bf16[256,2816]{1,0:T(8,128)(2,1)}, bf16[256,2816]{1,0:T(8,128)(2,1)}, u32[]{:S(2)}, u32[]{:S(2)}) collective-permute-start(bf16[256,2816]{1,0:T(8,128)(2,1)} %maximum_select_fusion.2), channel_id=1, source_target_pairs={{0,8},{4,12},{8,0},{12,4},{16,24},{20,28},{24,16},{28,20},{1,9},{5... | collective-permute-start | bytes 4325384 | tf_op jit(solution)/shard_map/ppermute | solution.py:406
  741.4 63.0 %collective-permute-start.34 = (bf16[256,2816]{1,0:T(8,128)(2,1)}, bf16[256,2816]{1,0:T(8,128)(2,1)}, u32[]{:S(2)}, u32[]{:S(2)}) collective-permute-start(bf16[256,2816]{1,0:T(8,128)(2,1)} %maximum_select_fusion.3), channel_id=1, source_target_pairs={{0,16},{4,20},{8,24},{12,28},{16,0},{20,4},{24,8},{28,12},{1,17},{... | collective-permute-start | bytes 4325384 | tf_op jit(solution)/shard_map/ppermute | solution.py:406
  745.7 41.0 %collective-permute-start.35 = (bf16[176,1024]{1,0:T(8,128)(2,1)S(1)}, bf16[176,1024]{1,0:T(8,128)(2,1)S(1)}, u32[]{:S(2)}, u32[]{:S(2)}) collective-permute-start(bf16[176,1024]{1,0:T(8,128)(2,1)S(1)} %constant_dynamic-slice_fusion.9), channel_id=1, source_target_pairs={{0,16},{4,20},{8,24},{12,28},{16,0},{20,4},{24,8},{28,12},{1,17},{... | collective-permute-start | bytes 1081352 | tf_op jit(solution)/shard_map/ppermute | solution.py:406
  746.8 39.9 %collective-permute-start.36 = (bf16[176,1024]{1,0:T(8,128)(2,1)S(1)}, bf16[176,1024]{1,0:T(8,128)(2,1)S(1)}, u32[]{:S(2)}, u32[]{:S(2)}) collective-permute-start(bf16[176,1024]{1,0:T(8,128)(2,1)S(1)} %constant_dynamic-slice_fusion.8), channel_id=1, source_target_pairs={{0,8},{4,12},{8,0},{12,4},{16,24},{20,28},{24,16},{28,20},{1,9},{5... | collective-permute-start | bytes 1081352 | tf_op jit(solution)/shard_map/ppermute | solution.py:406
  794.6 21.6 %collective-permute-start.37 = (bf16[1024,1024]{1,0:T(8,128)(2,1)}, bf16[1024,1024]{1,0:T(8,128)(2,1)}, u32[]{:S(2)}, u32[]{:S(2)}) collective-permute-start(bf16[1024,1024]{1,0:T(8,128)(2,1)} %pad_maximum_fusion.2), channel_id=1, source_target_pairs={{0,4},{4,0},{8,12},{12,8},{16,20},{20,16},{24,28},{28,24},{1,5},{5... | collective-permute-start | bytes 6291464 | tf_op jit(solution)/shard_map/ppermute | solution.py:406
  795.5 87.7 %collective-permute-start.52 = (bf16[176,1024]{1,0:T(8,128)(2,1)}, bf16[176,1024]{1,0:T(8,128)(2,1)}, u32[]{:S(2)}, u32[]{:S(2)}) collective-permute-start(bf16[176,1024]{1,0:T(8,128)(2,1)} %add_convert_fusion.17), channel_id=1, source_target_pairs={{0,16},{4,20},{8,24},{12,28},{16,0},{20,4},{24,8},{28,12},{1,17},{... | collective-permute-start | bytes 1081352 | tf_op jit(solution)/shard_map/ppermute | solution.py:406
  795.5 87.8 %collective-permute-start.53 = (bf16[176,1024]{1,0:T(8,128)(2,1)}, bf16[176,1024]{1,0:T(8,128)(2,1)}, u32[]{:S(2)}, u32[]{:S(2)}) collective-permute-start(bf16[176,1024]{1,0:T(8,128)(2,1)} %add_convert_fusion.16), channel_id=1, source_target_pairs={{0,8},{4,12},{8,0},{12,4},{16,24},{20,28},{24,16},{28,20},{1,9},{5... | collective-permute-start | bytes 1081352 | tf_op jit(solution)/shard_map/ppermute | solution.py:406
  812.2 123.4 %collective-permute-start.61 = (bf16[1024,2816]{1,0:T(8,128)(2,1)}, bf16[1024,2816]{1,0:T(8,128)(2,1)}, u32[]{:S(2)}, u32[]{:S(2)}) collective-permute-start(bf16[1024,2816]{1,0:T(8,128)(2,1)} %pad_maximum_fusion.half_ref), channel_id=1, source_target_pairs={{0,4},{4,0},{8,12},{12,8},{16,20},{20,16},{24,28},{28,24},{1,5},{5... | collective-permute-start | bytes 17301512 | tf_op jit(solution)/shard_map/ppermute | solution.py:406
  878.2 38.4 %collective-permute-start.38 = (bf16[1024,1024]{1,0:T(8,128)(2,1)S(1)}, bf16[1024,1024]{1,0:T(8,128)(2,1)S(1)}, u32[]{:S(2)}, u32[]{:S(2)}) collective-permute-start(bf16[1024,1024]{1,0:T(8,128)(2,1)S(1)} %fusion.40), channel_id=1, source_target_pairs={{0,4},{4,0},{8,12},{12,8},{16,20},{20,16},{24,28},{28,24},{1,5},{5... | collective-permute-start | bytes 6291464 | tf_op jit(solution)/shard_map/ppermute | solution.py:406
  878.3 17.6 %collective-permute-start.44 = (bf16[256,1024]{1,0:T(8,128)(2,1)S(1)}, bf16[256,1024]{1,0:T(8,128)(2,1)S(1)}, u32[]{:S(2)}, u32[]{:S(2)}) collective-permute-start(bf16[256,1024]{1,0:T(8,128)(2,1)S(1)} %constant_dynamic-slice_fusion.7), channel_id=1, source_target_pairs={{0,8},{4,12},{8,0},{12,4},{16,24},{20,28},{24,16},{28,20},{1,9},{5... | collective-permute-start | bytes 1572872 | tf_op jit(solution)/shard_map/ppermute | solution.py:406
  883.2 13.7 %collective-permute-start.45 = (bf16[256,1024]{1,0:T(8,128)(2,1)S(1)}, bf16[256,1024]{1,0:T(8,128)(2,1)S(1)}, u32[]{:S(2)}, u32[]{:S(2)}) collective-permute-start(bf16[256,1024]{1,0:T(8,128)(2,1)S(1)} %constant_dynamic-slice_fusion.6), channel_id=1, source_target_pairs={{0,16},{4,20},{8,24},{12,28},{16,0},{20,4},{24,8},{28,12},{1,17},{... | collective-permute-start | bytes 1572872 | tf_op jit(solution)/shard_map/ppermute | solution.py:406
  886.5 24.2 %collective-permute-start.54 = (bf16[352,1024]{1,0:T(8,128)(2,1)S(1)}, bf16[352,1024]{1,0:T(8,128)(2,1)S(1)}, u32[]{:S(2)}, u32[]{:S(2)}) collective-permute-start(bf16[352,1024]{1,0:T(8,128)(2,1)S(1)} %maximum_select_fusion.10), channel_id=1, source_target_pairs={{0,8},{4,12},{8,0},{12,4},{16,24},{20,28},{24,16},{28,20},{1,9},{5... | collective-permute-start | bytes 2162696 | tf_op jit(solution)/shard_map/ppermute | solution.py:406
  895.9 19.1 %collective-permute-start.55 = (bf16[352,1024]{1,0:T(8,128)(2,1)S(1)}, bf16[352,1024]{1,0:T(8,128)(2,1)S(1)}, u32[]{:S(2)}, u32[]{:S(2)}) collective-permute-start(bf16[352,1024]{1,0:T(8,128)(2,1)S(1)} %maximum_select_fusion.11), channel_id=1, source_target_pairs={{0,16},{4,20},{8,24},{12,28},{16,0},{20,4},{24,8},{28,12},{1,17},{... | collective-permute-start | bytes 2162696 | tf_op jit(solution)/shard_map/ppermute | solution.py:406
  897.3 22.9 %collective-permute-start.46 = (bf16[128,1024]{1,0:T(8,128)(2,1)S(1)}, bf16[128,1024]{1,0:T(8,128)(2,1)S(1)}, u32[]{:S(2)}, u32[]{:S(2)}) collective-permute-start(bf16[128,1024]{1,0:T(8,128)(2,1)S(1)} %constant_dynamic-slice_fusion.5), channel_id=1, source_target_pairs={{0,16},{4,20},{8,24},{12,28},{16,0},{20,4},{24,8},{28,12},{1,17},{... | collective-permute-start | bytes 786440 | tf_op jit(solution)/shard_map/ppermute | solution.py:406
  910.7 11.4 %collective-permute-start.47 = (bf16[128,1024]{1,0:T(8,128)(2,1)S(1)}, bf16[128,1024]{1,0:T(8,128)(2,1)S(1)}, u32[]{:S(2)}, u32[]{:S(2)}) collective-permute-start(bf16[128,1024]{1,0:T(8,128)(2,1)S(1)} %constant_dynamic-slice_fusion.4), channel_id=1, source_target_pairs={{0,8},{4,12},{8,0},{12,4},{16,24},{20,28},{24,16},{28,20},{1,9},{5... | collective-permute-start | bytes 786440 | tf_op jit(solution)/shard_map/ppermute | solution.py:406
  916.5 38.1 %collective-permute-start.58 = (bf16[1408,1024]{1,0:T(8,128)(2,1)S(1)}, bf16[1408,1024]{1,0:T(8,128)(2,1)S(1)}, u32[]{:S(2)}, u32[]{:S(2)}) collective-permute-start(bf16[1408,1024]{1,0:T(8,128)(2,1)S(1)} %pad_maximum_fusion.1.half_ref), channel_id=1, source_target_pairs={{0,4},{4,0},{8,12},{12,8},{16,20},{20,16},{24,28},{28,24},{1,5},{5... | collective-permute-start | bytes 8650760 | tf_op jit(solution)/shard_map/ppermute | solution.py:406
  918.0 14.7 %collective-permute-start.50 = (bf16[256,1024]{1,0:T(8,128)(2,1)S(1)}, bf16[256,1024]{1,0:T(8,128)(2,1)S(1)}, u32[]{:S(2)}, u32[]{:S(2)}) collective-permute-start(bf16[256,1024]{1,0:T(8,128)(2,1)S(1)} %constant_dynamic-slice_fusion.3), channel_id=1, source_target_pairs={{0,8},{4,12},{8,0},{12,4},{16,24},{20,28},{24,16},{28,20},{1,9},{5... | collective-permute-start | bytes 1572872 | tf_op jit(solution)/shard_map/ppermute | solution.py:406
  920.2 14.8 %collective-permute-start.51 = (bf16[256,1024]{1,0:T(8,128)(2,1)S(1)}, bf16[256,1024]{1,0:T(8,128)(2,1)S(1)}, u32[]{:S(2)}, u32[]{:S(2)}) collective-permute-start(bf16[256,1024]{1,0:T(8,128)(2,1)S(1)} %constant_dynamic-slice_fusion.2), channel_id=1, source_target_pairs={{0,16},{4,20},{8,24},{12,28},{16,0},{20,4},{24,8},{28,12},{1,17},{... | collective-permute-start | bytes 1572872 | tf_op jit(solution)/shard_map/ppermute | solution.py:406
  922.3 27.2 %collective-permute-start.48 = (bf16[128,1024]{1,0:T(8,128)(2,1)S(1)}, bf16[128,1024]{1,0:T(8,128)(2,1)S(1)}, u32[]{:S(2)}, u32[]{:S(2)}) collective-permute-start(bf16[128,1024]{1,0:T(8,128)(2,1)S(1)} %add_convert_fusion.21), channel_id=1, source_target_pairs={{0,16},{4,20},{8,24},{12,28},{16,0},{20,4},{24,8},{28,12},{1,17},{... | collective-permute-start | bytes 786440 | tf_op jit(solution)/shard_map/ppermute | solution.py:406
  932.7 16.9 %collective-permute-start.49 = (bf16[128,1024]{1,0:T(8,128)(2,1)S(1)}, bf16[128,1024]{1,0:T(8,128)(2,1)S(1)}, u32[]{:S(2)}, u32[]{:S(2)}) collective-permute-start(bf16[128,1024]{1,0:T(8,128)(2,1)S(1)} %add_convert_fusion.20), channel_id=1, source_target_pairs={{0,8},{4,12},{8,0},{12,4},{16,24},{20,28},{24,16},{28,20},{1,9},{5... | collective-permute-start | bytes 786440 | tf_op jit(solution)/shard_map/ppermute | solution.py:406
  935.5 14.2 %collective-permute-start.59 = (bf16[128,1024]{1,0:T(8,128)(2,1)S(1)}, bf16[128,1024]{1,0:T(8,128)(2,1)S(1)}, u32[]{:S(2)}, u32[]{:S(2)}) collective-permute-start(bf16[128,1024]{1,0:T(8,128)(2,1)S(1)} %constant_dynamic-slice_fusion.1), channel_id=1, source_target_pairs={{0,16},{4,20},{8,24},{12,28},{16,0},{20,4},{24,8},{28,12},{1,17},{... | collective-permute-start | bytes 786440 | tf_op jit(solution)/shard_map/ppermute | solution.py:406
  935.6 14.1 %collective-permute-start.60 = (bf16[128,1024]{1,0:T(8,128)(2,1)S(1)}, bf16[128,1024]{1,0:T(8,128)(2,1)S(1)}, u32[]{:S(2)}, u32[]{:S(2)}) collective-permute-start(bf16[128,1024]{1,0:T(8,128)(2,1)S(1)} %constant_dynamic-slice_fusion), channel_id=1, source_target_pairs={{0,8},{4,12},{8,0},{12,4},{16,24},{20,28},{24,16},{28,20},{1,9},{5... | collective-permute-start | bytes 786440 | tf_op jit(solution)/shard_map/ppermute | solution.py:406
  954.0 18.6 %collective-permute-start.56 = (bf16[256,1024]{1,0:T(8,128)(2,1)S(1)}, bf16[256,1024]{1,0:T(8,128)(2,1)S(1)}, u32[]{:S(2)}, u32[]{:S(2)}) collective-permute-start(bf16[256,1024]{1,0:T(8,128)(2,1)S(1)} %maximum_select_fusion.12), channel_id=1, source_target_pairs={{0,8},{4,12},{8,0},{12,4},{16,24},{20,28},{24,16},{28,20},{1,9},{5... | collective-permute-start | bytes 1572872 | tf_op jit(solution)/shard_map/ppermute | solution.py:406
  954.3 18.3 %collective-permute-start.57 = (bf16[256,1024]{1,0:T(8,128)(2,1)S(1)}, bf16[256,1024]{1,0:T(8,128)(2,1)S(1)}, u32[]{:S(2)}, u32[]{:S(2)}) collective-permute-start(bf16[256,1024]{1,0:T(8,128)(2,1)S(1)} %maximum_select_fusion.13), channel_id=1, source_target_pairs={{0,16},{4,20},{8,24},{12,28},{16,0},{20,4},{24,8},{28,12},{1,17},{... | collective-permute-start | bytes 1572872 | tf_op jit(solution)/shard_map/ppermute | solution.py:406
  961.6 19.5 %collective-permute-start.65 = (bf16[256,1024]{1,0:T(8,128)(2,1)S(1)}, bf16[256,1024]{1,0:T(8,128)(2,1)S(1)}, u32[]{:S(2)}, u32[]{:S(2)}) collective-permute-start(bf16[256,1024]{1,0:T(8,128)(2,1)S(1)} %maximum_select_fusion.14), channel_id=1, source_target_pairs={{0,8},{4,12},{8,0},{12,4},{16,24},{20,28},{24,16},{28,20},{1,9},{5... | collective-permute-start | bytes 1572872 | tf_op jit(solution)/shard_map/ppermute | solution.py:406
  963.5 17.7 %collective-permute-start.66 = (bf16[256,1024]{1,0:T(8,128)(2,1)S(1)}, bf16[256,1024]{1,0:T(8,128)(2,1)S(1)}, u32[]{:S(2)}, u32[]{:S(2)}) collective-permute-start(bf16[256,1024]{1,0:T(8,128)(2,1)S(1)} %maximum_select_fusion.15), channel_id=1, source_target_pairs={{0,16},{4,20},{8,24},{12,28},{16,0},{20,4},{24,8},{28,12},{1,17},{... | collective-permute-start | bytes 1572872 | tf_op jit(solution)/shard_map/ppermute | solution.py:406
  973.7 36.1 %collective-permute-start.62 = (bf16[1024,1024]{1,0:T(8,128)(2,1)S(1)}, bf16[1024,1024]{1,0:T(8,128)(2,1)}, u32[]{:S(2)}, u32[]{:S(2)}) collective-permute-start(bf16[1024,1024]{1,0:T(8,128)(2,1)S(1)} %pad_maximum_fusion.3.half_ref), channel_id=1, source_target_pairs={{0,4},{4,0},{8,12},{12,8},{16,20},{20,16},{24,28},{28,24},{1,5},{5... | collective-permute-start | bytes 6291464 | tf_op jit(solution)/shard_map/ppermute | solution.py:406
  983.6 35.9 %collective-permute-start.67 = (bf16[1024,1024]{1,0:T(8,128)(2,1)}, bf16[1024,1024]{1,0:T(8,128)(2,1)}, u32[]{:S(2)}, u32[]{:S(2)}) collective-permute-start(bf16[1024,1024]{1,0:T(8,128)(2,1)} %pad_maximum_fusion.4.half_ref), channel_id=1, source_target_pairs={{0,4},{4,0},{8,12},{12,8},{16,20},{20,16},{24,28},{28,24},{1,5},{5... | collective-permute-start | bytes 6291464 | tf_op jit(solution)/shard_map/ppermute | solution.py:406
  (98 other events, 1116.2 us)
Sparse Core Ops, SparseCore 0:
  12.7 83.4 all-gather.8
  165.1 24.7 all-gather.16
  191.8 53.8 all-gather.18
  247.1 89.6 all-gather.10
  338.8 83.4 all-gather.12
  483.2 75.4 reduce-scatter.3
  627.4 78.9 all-gather.14
  735.3 76.8 reduce-scatter.5
  873.8 78.1 reduce-scatter.7

commit v5 on v4

--- a/solution.py
+++ b/solution.py
@@ -411,6 +411,8 @@
 
 
 def after(x, *deps):
+    if not jax.tree.leaves(deps):
+        return x
     return lax.optimization_barrier((x, deps))[0]
 
 
@@ -623,7 +625,18 @@
         n = lax.axis_size(axis)
         for bit in range(int(math.log2(n))):
             x = x + lax.ppermute(x, axis, [(i, i ^ (1 << bit)) for i in range(n)])
-    return x
+            yield x
+    while True:
+        yield x
+
+
+def gather_tp(x):
+    n, me = lax.axis_size("tp"), lax.axis_index("tp")
+    out = jnp.zeros((n,) + x.shape, x.dtype)
+    for d in range(n):
+        got = lax.ppermute(x, "tp", [(i, (i + d) % n) for i in range(n)]) if d else x
+        out = lax.dynamic_update_index_in_dim(out, got, (me + n - d) % n, 0)
+    return out
 
 
 def local(tokens, cotangent, block_order, gain_one, shift_one, query_w, key_w, value_w, query_b, key_b, value_b,
@@ -650,9 +663,9 @@
 
     rows_w = output_w.shape[0] // n_ctx
     part = lax.dynamic_slice_in_dim(output_w, ctx * rows_w, rows_w, 0)
-    part = lax.all_gather(after(part, rows_one), "tp", axis=0)
+    part = gather_tp(after(part, kv))
     dy_rows = all_rows(after(cotangent, rows_one))
-    whole_w = lax.all_gather(after(part, arrived), "ctx", axis=1).reshape(n_tp * output_w.shape[0], -1)
+    whole_w = lax.all_gather(after(part, arrived, dy_rows), "ctx", axis=1).reshape(n_tp * output_w.shape[0], -1)
 
     attn, q_ext = attend(place, own, q, keys, values)
     attn_rows = attn.reshape(-1, width)
@@ -670,21 +683,24 @@
     grad_two = sum_rows(part_two)
     act, rows_two, dy_rows, grad_gu = after((act, rows_two, dy_rows, grad_gu), part_two)
     gu = begin(lambda core: rc(columns(rows_two, core), grad_gu))
-    down = nn(act, down_w).astype(BF16)
     held = take(gu)
     go(gu)
-    dy_late = after(dy_rows, held)
-    dw = begin(lambda core: rc(act, columns(dy_late, core)))
-    take(gu)
+    dw = begin(lambda core: rc(act, columns(dy_rows, core)))
+    act_late = after(act, held)
+    down = nn(act_late, down_w).astype(BF16)
+    held = take(dw), take(gu, down)
     go(gu)
-    grad_two = after(grad_two, take(gu), take(dw), down)
+    go(dw, held)
+    grad_two = after(grad_two, take(gu, held))
     go(gu)
-    go(dw)
 
     norm_two, grad_gain_two, grad_shift_two = layer_back(grad_two, unit_two, inverse_two, gain_two)
     grad_mixed = cotangent.astype(F32) + norm_two
     branch_own = grad_mixed.astype(BF16)
     grad_attn = nt(branch_own, whole_w).astype(BF16)
+    grad_attn = after(grad_attn, take(gu), take(dw))
+    go(gu)
+    go(dw)
     grad_attn = lax.all_to_all(grad_attn, "tp", split_axis=1, concat_axis=0, tiled=True)
     branch = all_rows(after(branch_own, grad_attn))
     out_tokens = (mixed + sum_rows(after(down, grad_attn))).astype(BF16)
@@ -694,19 +710,22 @@
                             precision=lax.Precision.HIGHEST, preferred_element_type=F32)
     do_ext = terms(-delta, lane).astype(BF16)
     do_sent = jnp.concatenate([grad_attn, do_ext], axis=1).reshape(shape)
-    grads = gather_other(after(do_sent, take(gu), take(dw)))
+    grads = gather_other(after(do_sent, take(gu, grad_attn), take(dw, grad_attn)))
+    take_extra(gu)
+    go(gu)
     grad_q = query_grad(place, own, q, grad_attn.reshape(q.shape), q_ext, do_ext.reshape(q_ext.shape), tabs, keys, values)
     grad_q = grad_q.reshape(-1, width)
     q_part = nt(grad_q, query_w)
+    go(dw, q_part)
     grads = gather_cores(grads, q_part)
-    go(gu, grads)
-    go(dw, grads)
+    grad_gate_w, grad_up_w = unpack_rows(*take(gu, q_part), 2)
     rows_q, branch = after((rows_one, branch), grads)
     oq = begin(lambda core: jnp.concatenate([rc(attn_rows, columns(branch, core)), rc(grad_q, columns(rows_q, core))]))
-    first = key_value_grad(place, own, kv, tabs, queries, grads, 0, SEQS // 2)
-    grads = after(grads, take(gu, first), take(dw, first), take(oq, first))
-    take_extra(gu)
-    go(gu)
+    held = take(dw, grads)
+    go(dw)
+    first = key_value_grad(place, own, kv, tabs, queries, after(grads, held, grad_gate_w), 0, SEQS // 2)
+    grads = after(grads, take(dw, first), take(oq, first))
+    take_extra(dw)
     go(dw)
     go(oq)
     second = key_value_grad(place, own, kv, tabs, queries, grads, SEQS // 2, SEQS // 2)
@@ -718,10 +737,6 @@
     rows_one, grad_q, grad_k, grad_v = after((rows_one, grad_q, grad_k, grad_v), part_sent)
     grad_kv = jnp.concatenate([grad_k, grad_v], axis=1)
     dkv = begin(lambda core: rc(columns(rows_one, core), grad_kv))
-    take(dw, part_sent)
-    go(dw)
-    take(oq, part_sent)
-    go(oq)
     unit_rows = (rows_one.astype(F32) - shift_one) / gain_one
     bias_grad = jnp.concatenate([jnp.sum(g.astype(F32), axis=0) for g in (grad_q, grad_kv)])
     tp_row = (jnp.arange(n_tp) == lax.axis_index("tp"))[:, None]
@@ -730,29 +745,37 @@
         jnp.where(tp_row, bias_grad[None, :], 0.0).reshape(-1)])
     held = take(dkv)
     go(dkv)
-    small = sum_over_all(after(small, held).reshape(-1, 1024)).reshape(-1)
+    sums = sum_over_all(after(small, held).reshape(-1, 1024))
+    small = next(sums), next(sums)
+    take(oq, held)
+    held = take(dkv, small)
+    go(oq)
+    go(dkv)
+    grad_down_w = unpack_cols(*take(dw, held), act.shape[1])
+    small = next(sums), grad_down_w
+    take(oq, held)
+    held = take(dkv, small)
+    go(oq)
+    go(dkv)
+    small = next(sums)
+    take(oq, held)
+    held = take(dkv, small)
+    go(oq)
+    go(dkv)
+    for _ in range(4):
+        small = next(sums)
+    take(oq, held)
+    take(dkv)
+    take_extra(oq)
+    take_extra(dkv)
+    go(oq)
+    go(dkv)
     depth = x.shape[1]
+    small = small.reshape(-1)
     norms = small[:4 * depth].reshape(4, depth)
     bias_sum = jnp.sum(jnp.where(tp_row, small[4 * depth:].reshape(n_tp, -1), 0.0), axis=0)
-    grad_gate_w, grad_up_w = unpack_rows(*take(gu, held), 2)
-    held = take(dkv), take(oq), take(dw)
-    go(dkv)
-    go(oq)
-    take_extra(dw)
-    go(dw)
-    held = take(dkv, (held, grad_gate_w)), take(oq, held)
-    go(dkv)
-    go(oq)
-    grad_down_w = unpack_cols(*take(dw, held), act.shape[1])
-    held = take(dkv, grad_down_w), take(oq, grad_down_w)
-    take_extra(oq)
-    take_extra(dkv)
-    go(dkv)
-    go(oq)
-    halves = take(oq, held)
+    halves = take(oq)
     grad_output_w, grad_query_w = unpack_cols(*halves, width), unpack_turned(*halves, width)
-    take(dkv, held)
-    go(dkv)
     grad_key_w, grad_value_w = unpack_rows(*take(dkv), 2)
     norm_one, _, _ = layer_back(grad_one, unit_one, inverse_one, gain_one)
     grad_tokens = (grad_mixed + norm_one).astype(BF16)

time: 1050 us -> 1040 us (level)
  waiting for transfers between devices: 388 us -> 372 us
  Pallas kernels: 238 us -> 250 us
    all_gather x4, waiting for transfers between devices: 139 us -> 99.6 us  [all_rows(): return lax.all_gather(x, 'tp', axis=0, tiled=True)]
    ppermute x0 -> x3, waiting for transfers between devices: none -> 15.9 us  [gather_tp(): lax.ppermute(x, 'tp', [(i, (i + d) % n) for i in range(n)])]
    convert_element_type x4 -> x1, other arithmetic: 18 us -> 2.47 us  [weight_grad(): half = (part(core) + after(got, gate).astype(F32)).astype(BF16)]
    unnamed x181 -> x177, local copies, waits for them, and re-layouts: 16.4 us -> 23.3 us
  transfers between devices with their start and end apart: 77 -> 79, of which waited for: 35 -> 34; matrix products, arithmetic and copies ran while one was open for 17% -> 17% of each run, Pallas kernels for 19% -> 22%
where the time goes in v5:
time: 1040 us; the launch traced here: 1030 us
  waiting for transfers between devices  372 us (36%)
  Pallas kernels  250 us (24%)
  matrix products  118 us (11%)
  starting transfers between devices  82.1 us (8%)
  other arithmetic  73 us (7%)
  local copies, waits for them, and re-layouts  61.6 us (6%)
  blocking collectives  54.4 us (5%)
  between operations  15.7 us (2%)
    ppermute x63, waiting for transfers between devices, ctx_swap(): return lax.ppermute(x, 'ctx', [(i, i ^ mask) for i in range(n)])  236 us
    pallas_call x4, Pallas kernels, attention_call(): pl.pallas_call(kernel, grid_spec=pltpu.PrefetchScalarGridSpec(num_scalar_...  169 us
    all_gather x4, waiting for transfers between devices, all_rows(): return lax.all_gather(x, 'tp', axis=0, tiled=True)  99.6 us
    ppermute x63, starting transfers between devices, ctx_swap(): return lax.ppermute(x, 'ctx', [(i, i ^ mask) for i in range(n)])  74.5 us
    dot_general x10, matrix products, rc(): lax.dot_general(left, right, (((0,), (0,)), ((), ())), preferred_element_...  51.4 us
    dot_general x6, matrix products, nt(): lax.dot_general(a, b, (((1,), (1,)), ((), ())), preferred_element_type=jn...  50.2 us
    all_to_all x1, blocking collectives, local(): lax.all_to_all(attn_rows, 'tp', split_axis=0, concat_axis=1, tiled=True)  29.2 us
    pallas_call x1, Pallas kernels, mlp(): pl.pallas_call(mlp_kernel, grid=(total // step,), in_specs=[block, block,...  28.6 us
  transfers between devices with their start and end apart: 79, of which 34 were waited for; matrix products, arithmetic and copies ran while one was open for 17% of the time, Pallas kernels for 22%

profile of v5, /device:TPU:0, one launch (start us, length us, event | category | flops | bytes accessed | tf_op | source)
XLA Modules:
  0.0 1026.8 jit_solution(12556427195833380700)
XLA Ops:
  12.6 83.6 %all-gather.7.cloned.1.call-done.h_ref = bf16[1024,2048]{1,0:T(8,128)(2,1)} async-done(((bf16[256,2048]{1,0:T(8,128)(2,1)}), bf16[1024,2048]{1,0:T(8,128)(2,1)}) %all-gather.7.cloned.1.call-update) | async-done | bytes 4194320 | tf_op jit(solution)/shard_map/all_gather | solution.py:577
  96.5 3.0 multiply_sine_fusion
  106.7 3.5 concatenate.154.c_ref
  111.3 11.3 %project.1 = (bf16[4,256,512]{2,1,0:T(8,128)(2,1)S(1)}, bf16[2,4,256,512]{3,2,1,0:T(8,128)(2,1)}) custom-call(bf16[1024,2048]{1,0:T(8,128)(2,1)} %all-gather.7.cloned.1.call-done.h_ref, bf16[2048,512]{1,0:T(8,128)(2,1)} %wq_ref.1, bf16[2048,512]{1,0:T(8,128)(2,1)} %wk_ref.1, bf16[2048,512]{1,0:T(8,128)(2,1)} %wv_ref.1, ...), custom_call_target="tpu_custom_call" | custom-call | flops 6442450944 | bytes 6291456 | tf_op jit(solution)/shard_map/project/pallas_call | solution.py:350
  126.6 44.7 %collective-permute-done.1.refs_2_.refs_10_ = bf16[2,4,2,128,512]{4,3,2,1,0:T(8,128)(2,1)} collective-permute-done((bf16[2,4,2,128,512]{4,3,2,1,0:T(8,128)(2,1)}, bf16[2,4,2,128,512]{4,3,2,1,0:T(8,128)(2,1)}, u32[]{:S(2)}, u32[]{:S(2)}) %collective-permute-start.1) | collective-permute-done | bytes 2097184 | tf_op jit(solution)/shard_map/ppermute | solution.py:406
  182.7 7.3 collective-permute-done.9
  190.0 8.7 collective-permute-done.10
  203.9 4.7 collective-permute-done.6.refs_7_
  209.9 56.5 %attend.1 = (bf16[4,256,512]{2,1,0:T(8,128)(2,1)}, bf16[4,256,128]{2,1,0:T(8,128)(2,1)S(1)}) custom-call(s32[4,16]{1,0:T(4,128)S(1)} %copy.51.place_ref, s32[4,2]{1,0:T(4,128)S(1)} %get-tuple-element.261.own_ref, bf16[4,256,512]{2,1,0:T(8,128)(2,1)S(1)} %copy-done.13, bf16[2,4,2,128,512]{4,3,2,1,0:T(8,128)(2,1)} %bitcast.5.refs_0_.refs_8_, ...), custom_call_target="tpu_custom_call" | custom-call | flops 8589934592 | bytes 16777216 | tf_op jit(solution)/shard_map/attend/pallas_call | solution.py:222
  266.4 29.2 %all_to_all.35 = bf16[4,256,512]{2,1,0:T(8,128)(2,1)} all-to-all(bf16[4,256,512]{2,1,0:T(8,128)(2,1)} %get-tuple-element.135), channel_id=1, replica_groups=mesh['ctx'=8,'tp'=4] {'tp'}, dimensions={0} | all-to-all | bytes 2097152 | tf_op jit(solution)/shard_map/all_to_all | solution.py:672
  297.8 6.1 fusion.85
  307.1 3.4 collective-permute-start.17
  310.5 28.2 %collective-permute-done.13.refs_2_.refs_18_ = bf16[1,4,2,128,640]{4,3,2,1,0:T(8,128)(2,1)S(1)} collective-permute-done((bf16[1,4,2,128,640]{4,3,2,1,0:T(8,128)(2,1)S(1)}, bf16[1,4,2,128,640]{4,3,2,1,0:T(8,128)(2,1)S(1)}, u32[]{:S(2)}, u32[]{:S(2)}) %collective-permute-start.13) | collective-permute-done | bytes 1310752 | tf_op jit(solution)/shard_map/ppermute | solution.py:406
  338.7 25.0 %collective-permute-done.15.refs_4_.refs_20_ = bf16[1,4,2,128,640]{4,3,2,1,0:T(8,128)(2,1)} collective-permute-done((bf16[1,4,2,128,640]{4,3,2,1,0:T(8,128)(2,1)S(1)}, bf16[1,4,2,128,640]{4,3,2,1,0:T(8,128)(2,1)}, u32[]{:S(2)}, u32[]{:S(2)}) %collective-permute-start.15) | collective-permute-done | bytes 1310752 | tf_op jit(solution)/shard_map/ppermute | solution.py:406
  368.9 16.0 %all-gather.11.cloned.1.call-done.h_ref = bf16[1024,2048]{1,0:T(8,128)(2,1)} async-done(((bf16[256,2048]{1,0:T(8,128)(2,1)}), bf16[1024,2048]{1,0:T(8,128)(2,1)}) %all-gather.11.cloned.1.call-update) | async-done | bytes 4194320 | tf_op jit(solution)/shard_map/all_gather | solution.py:577
  384.9 28.6 %mlp.1 = (bf16[1024,1408]{1,0:T(8,128)(2,1)}, bf16[1024,2816]{1,0:T(8,128)(2,1)}) custom-call(bf16[1024,2048]{1,0:T(8,128)(2,1)} %all-gather.11.cloned.1.call-done.h_ref, bf16[1024,2048]{1,0:T(8,128)(2,1)} %all-gather.9.cloned.1.call-done.dy_ref, bf16[2048,1408]{1,0:T(8,128)(2,1)} %gate_ref.1, bf16[2048,1408]{1,0:T(8,128)(2,1)} %up_ref.1, ...), custom_call_target="tpu_custom_call" | custom-call | flops 17716740096 | bytes 38273024 | tf_op jit(solution)/shard_map/mlp/pallas_call | solution.py:390
  413.6 9.8 fusion.2
  423.3 11.1 %add_convert_fusion.1 = bf16[1024,2048]{1,0:T(8,128)(2,1)} fusion(f32[1024,2048]{1,0:T(8,128)S(1)} %fusion.2, bf16[2048,1408]{1,0:T(8,128)(2,1)} %up_ref.1, bf16[1024,2816]{1,0:T(8,128)(2,1)S(1)} %copy-done.74), kind=kOutput, calls=%fused_computation.3 | convolution fusion | flops 5909774336 | bytes 21233664 | tf_op jit(solution)/shard_map/dot_general | solution.py:15
  434.4 11.0 %convolution_convert_fusion = bf16[1024,2816]{1,0:T(8,128)(2,1)} fusion(bf16[1024,2816]{1,0:T(8,128)(2,1)} %get-tuple-element.147, bf16[1024,2048]{1,0:T(8,128)(2,1)} %all-gather.11.cloned.1.call-done.h_ref, s32[]{:T(128)S(6)} %select_n.288), kind=kOutput, calls=%fused_computation.6 | convolution fusion | flops 5908463616 | bytes 13631492 | tf_op jit(solution)/shard_map/dot_general | solution.py:290
  445.9 7.4 convolution_convert_fusion.2
  455.1 10.0 add_convert_fusion
  471.1 8.2 convolution_convert_fusion.1
  479.3 21.6 %collective-permute-done.20 = bf16[256,2816]{1,0:T(8,128)(2,1)} collective-permute-done((bf16[256,2816]{1,0:T(8,128)(2,1)}, bf16[256,2816]{1,0:T(8,128)(2,1)}, u32[]{:S(2)}, u32[]{:S(2)}) %collective-permute-start.20) | collective-permute-done | bytes 1441824 | tf_op jit(solution)/shard_map/ppermute | solution.py:406
  510.7 5.0 add_convert_fusion.2
  517.5 7.2 collective-permute-done.22
  524.7 3.8 collective-permute-done.23
  532.3 11.7 %collective-permute-done.27 = bf16[352,1024]{1,0:T(8,128)(2,1)S(1)} collective-permute-done((bf16[352,1024]{1,0:T(8,128)(2,1)S(1)}, bf16[352,1024]{1,0:T(8,128)(2,1)S(1)}, u32[]{:S(2)}, u32[]{:S(2)}) %collective-permute-start.27) | collective-permute-done | bytes 720928 | tf_op jit(solution)/shard_map/ppermute | solution.py:406
  552.0 7.1 convolution_convert_fusion.3
  559.0 3.3 maximum_select_fusion.2
  562.3 3.2 maximum_select_fusion.3
  568.4 25.3 %all_to_all.36 = bf16[256,4,512]{2,0,1:T(8,128)(2,1)S(1)} all-to-all(bf16[256,4,512]{2,0,1:T(8,128)(2,1)} %copy.54), channel_id=1, replica_groups=mesh['ctx'=8,'tp'=4] {'tp'}, dimensions={1} | all-to-all | bytes 2097152 | tf_op jit(solution)/shard_map/all_to_all | solution.py:704
  599.5 26.1 %collective-permute-done.29 = bf16[256,2816]{1,0:T(8,128)(2,1)} collective-permute-done((bf16[256,2816]{1,0:T(8,128)(2,1)}, bf16[256,2816]{1,0:T(8,128)(2,1)}, u32[]{:S(2)}, u32[]{:S(2)}) %collective-permute-start.29) | collective-permute-done | bytes 1441824 | tf_op jit(solution)/shard_map/ppermute | solution.py:406
  625.6 4.9 collective-permute-done.30
  630.6 3.4 maximum_select_fusion.1
  636.2 2.9 pad_maximum_fusion.half_ref
  640.0 11.0 %collective-permute-done.32 = bf16[176,1024]{1,0:T(8,128)(2,1)} collective-permute-done((bf16[176,1024]{1,0:T(8,128)(2,1)}, bf16[176,1024]{1,0:T(8,128)(2,1)}, u32[]{:S(2)}, u32[]{:S(2)}) %collective-permute-start.32) | collective-permute-done | bytes 360480 | tf_op jit(solution)/shard_map/ppermute | solution.py:406
  659.1 3.2 collective-permute-start.38
  669.1 56.0 %query_grad.1 = bf16[4,256,512]{2,1,0:T(8,128)(2,1)S(1)} custom-call(s32[4,16]{1,0:T(4,128)S(1)} %copy.51.place_ref, s32[4,2]{1,0:T(4,128)S(1)} %get-tuple-element.261.own_ref, bf16[4,256,512]{2,1,0:T(8,128)(2,1)S(1)} %copy-done.14, bf16[4,256,512]{2,1,0:T(8,128)(2,1)S(1)} %bitcast.86, bf16[4,256,128]{2,1,0:T(8,128)(2,1)S(1)} %get-tuple-element.140.qx_ref, ...), custom_call_target="tpu_custom_call" | custom-call | flops 12884901888 | bytes 16777216 | tf_op jit(solution)/shard_map/query_grad/pallas_call | solution.py:222
  725.1 5.7 fusion.87
  731.6 6.7 collective-permute-done.40
  746.2 3.3 fusion.52
  755.0 13.6 %unpack_rows.2 = (f32[2048,1408]{1,0:T(8,128)}, f32[2048,1408]{1,0:T(8,128)}) custom-call(s32[1]{0:T(128)} %bitcast.23.core_ref, bf16[1024,2816]{1,0:T(8,128)(2,1)} %pad_maximum_fusion.half_ref, bf16[1024,2816]{1,0:T(8,128)(2,1)} %collective-permute-done.42.other_ref), custom_call_target="tpu_custom_call" | custom-call | bytes 34603008 | tf_op jit(solution)/shard_map/unpack_rows/pallas_call | solution.py:508
  768.6 26.9 %key_value_grad.2 = (bf16[2,256,512]{2,1,0:T(8,128)(2,1)S(1)}, bf16[2,256,512]{2,1,0:T(8,128)(2,1)S(1)}) custom-call(s32[4,16]{1,0:T(4,128)S(1)} %copy.51.place_ref, s32[4,2]{1,0:T(4,128)S(1)} %get-tuple-element.261.own_ref, bf16[2,4,256,512]{3,2,1,0:T(8,128)(2,1)} %get-tuple-element.134.k_ref.v_ref, ...), custom_call_target="tpu_custom_call" | custom-call | flops 8589934592 | bytes 8388608 | tf_op jit(solution)/shard_map/key_value_grad/pallas_call | solution.py:222
  800.7 4.8 collective-permute-start.62
  813.3 29.6 %key_value_grad.3 = (bf16[2,256,512]{2,1,0:T(8,128)(2,1)S(1)}, bf16[2,256,512]{2,1,0:T(8,128)(2,1)S(1)}) custom-call(s32[4,16]{1,0:T(4,128)S(1)} %copy.51.place_ref, s32[4,2]{1,0:T(4,128)S(1)} %get-tuple-element.261.own_ref, bf16[2,4,256,512]{3,2,1,0:T(8,128)(2,1)} %get-tuple-element.134.k_ref.v_ref, ...), custom_call_target="tpu_custom_call" | custom-call | flops 8589934592 | bytes 8388608 | tf_op jit(solution)/shard_map/key_value_grad/pallas_call | solution.py:222
  844.9 5.8 fusion.88
  850.7 10.8 %fusion.86 = (bf16[1024,2048]{1,0:T(8,128)(2,1)}, f32[1024,2048]{1,0:T(8,128)}) fusion(f32[1024,2048]{1,0:T(8,128)} %fusion.88, f32[1024,2048]{1,0:T(8,128)S(1)} %bitcast.100, bf16[1024,512]{1,0:T(8,128)(2,1)S(1)} %bitcast.97, bf16[2048,512]{1,0:T(8,128)(2,1)S(1)} %copy-done.48), kind=kOutput, calls=%fused_computation.208 | convolution fusion | flops 2153775104 | bytes 32505856 | tf_op jit(solution)/shard_map/dot_general | solution.py:15
  865.3 3.7 fusion.44
  874.8 23.8 %collective-permute-start.52 = (bf16[256,1024]{1,0:T(8,128)(2,1)}, bf16[256,1024]{1,0:T(8,128)(2,1)}, u32[]{:S(2)}, u32[]{:S(2)}) collective-permute-start(bf16[256,1024]{1,0:T(8,128)(2,1)} %constant_dynamic-slice_fusion.7), channel_id=1, source_target_pairs={{0,8},{4,12},{8,0},{12,4},{16,24},{20,28},{24,16},{28,20},{1,9},{5... | collective-permute-start | bytes 1572872 | tf_op jit(solution)/shard_map/ppermute | solution.py:406
  899.4 4.6 add_convert_fusion.3
  905.3 5.7 collective-permute-done.52
  921.2 7.2 collective-permute-done.48
  929.2 5.4 collective-permute-done.49
  936.4 4.5 collective-permute-done.55
  945.4 9.7 unpack_cols.2
  960.0 4.0 collective-permute-done.50
  964.0 10.6 %collective-permute-done.65 = bf16[128,1024]{1,0:T(8,128)(2,1)S(1)} collective-permute-done((bf16[128,1024]{1,0:T(8,128)(2,1)S(1)}, bf16[128,1024]{1,0:T(8,128)(2,1)S(1)}, u32[]{:S(2)}, u32[]{:S(2)}) %collective-permute-start.65) | collective-permute-done | bytes 262176 | tf_op jit(solution)/shard_map/ppermute | solution.py:406
  977.7 6.3 collective-permute-done.69
  987.0 3.1 add_convert_fusion.6
  990.1 3.1 collective-permute-done.51
  997.0 6.5 unpack_turned.1
  1003.5 3.2 unpack_cols.3
  1006.7 7.7 unpack_rows.3
  1016.5 3.2 fusion.15
  (447 shorter events, 178.6 us)
Async XLA Ops:
  7.2 89.0 %all-gather.7.cloned.1.call-start = ((), (), s32[]{:S(2)}) async-start(), calls=%async_computation.5 | async-start | bytes 5242880 | tf_op jit(solution)/shard_map/all_gather | solution.py:577
  12.6 196.6 %all-gather.9.cloned.1.call-start = ((), (), s32[]{:S(2)}) async-start(), calls=%async_computation.6 | async-start | bytes 5242880 | tf_op jit(solution)/shard_map/all_gather | solution.py:577
  96.2 201.6 %all-gather.15.cloned.1.call-start = ((), (), s32[]{:S(2)}) async-start(), calls=%async_computation.12 | async-start | bytes 9437184 | tf_op jit(solution)/shard_map/all_gather | solution.py:668
  123.6 47.7 %collective-permute-start.1 = (bf16[2,4,2,128,512]{4,3,2,1,0:T(8,128)(2,1)}, bf16[2,4,2,128,512]{4,3,2,1,0:T(8,128)(2,1)}, u32[]{:S(2)}, u32[]{:S(2)}) collective-permute-start(bf16[2,4,2,128,512]{4,3,2,1,0:T(8,128)(2,1)} %bitcast.5.refs_0_.refs_8_), channel_id=1, source_target_pairs={{0,8},{4,12},{8,0},{12,4},{16,24},{20,28},{24,16},{28,20},{1,9},{5... | collective-permute-start | bytes 6291464 | tf_op jit(solution)/shard_map/ppermute | solution.py:406
  125.1 49.9 %collective-permute-start.3 = (bf16[2,4,2,128,512]{4,3,2,1,0:T(8,128)(2,1)}, bf16[2,4,2,128,512]{4,3,2,1,0:T(8,128)(2,1)}, u32[]{:S(2)}, u32[]{:S(2)}) collective-permute-start(bf16[2,4,2,128,512]{4,3,2,1,0:T(8,128)(2,1)} %bitcast.5.refs_0_.refs_8_), channel_id=1, source_target_pairs={{0,16},{4,20},{8,24},{12,28},{16,0},{20,4},{24,8},{28,12},{1,17},{... | collective-permute-start | bytes 6291464 | tf_op jit(solution)/shard_map/ppermute | solution.py:406
  173.5 27.6 %collective-permute-start.5 = (bf16[1,4,2,128,512]{4,3,2,1,0:T(8,128)(2,1)}, bf16[1,4,2,128,512]{4,3,2,1,0:T(8,128)(2,1)}, u32[]{:S(2)}, u32[]{:S(2)}) collective-permute-start(bf16[1,4,2,128,512]{4,3,2,1,0:T(8,128)(2,1)} %slice.103), channel_id=1, source_target_pairs={{0,16},{4,20},{8,24},{12,28},{16,0},{20,4},{24,8},{28,12},{1,17},{... | collective-permute-start | bytes 3145736 | tf_op jit(solution)/shard_map/ppermute | solution.py:406
  177.3 24.4 %collective-permute-start.7 = (bf16[1,4,2,128,512]{4,3,2,1,0:T(8,128)(2,1)}, bf16[1,4,2,128,512]{4,3,2,1,0:T(8,128)(2,1)}, u32[]{:S(2)}, u32[]{:S(2)}) collective-permute-start(bf16[1,4,2,128,512]{4,3,2,1,0:T(8,128)(2,1)} %slice.104), channel_id=1, source_target_pairs={{0,8},{4,12},{8,0},{12,4},{16,24},{20,28},{24,16},{28,20},{1,9},{5... | collective-permute-start | bytes 3145736 | tf_op jit(solution)/shard_map/ppermute | solution.py:406
  178.8 11.2 %collective-permute-start.9 = (bf16[64,2048]{1,0:T(8,128)(2,1)S(1)}, bf16[64,2048]{1,0:T(8,128)(2,1)S(1)}, u32[]{:S(2)}, u32[]{:S(2)}) collective-permute-start(bf16[64,2048]{1,0:T(8,128)(2,1)S(1)} %constant_dynamic-slice_fusion.16), channel_id=1, source_target_pairs={{0,1},{1,2},{2,3},{3,0},{4,5},{5,6},{6,7},{7,4},{8,9},{9,10},{10,1... | collective-permute-start | bytes 786440 | tf_op jit(solution)/shard_map/ppermute | solution.py:637
  178.8 19.8 %collective-permute-start.10 = (bf16[64,2048]{1,0:T(8,128)(2,1)S(1)}, bf16[64,2048]{1,0:T(8,128)(2,1)S(1)}, u32[]{:S(2)}, u32[]{:S(2)}) collective-permute-start(bf16[64,2048]{1,0:T(8,128)(2,1)S(1)} %constant_dynamic-slice_fusion.16), channel_id=1, source_target_pairs={{0,2},{1,3},{2,0},{3,1},{4,6},{5,7},{6,4},{7,5},{8,10},{9,11},{10,... | collective-permute-start | bytes 786440 | tf_op jit(solution)/shard_map/ppermute | solution.py:637
  180.4 18.2 %collective-permute-start.11 = (bf16[64,2048]{1,0:T(8,128)(2,1)S(1)}, bf16[64,2048]{1,0:T(8,128)(2,1)S(1)}, u32[]{:S(2)}, u32[]{:S(2)}) collective-permute-start(bf16[64,2048]{1,0:T(8,128)(2,1)S(1)} %constant_dynamic-slice_fusion.16), channel_id=1, source_target_pairs={{0,3},{1,0},{2,1},{3,2},{4,7},{5,4},{6,5},{7,6},{8,11},{9,8},{10,9... | collective-permute-start | bytes 786440 | tf_op jit(solution)/shard_map/ppermute | solution.py:637
  190.0 13.9 %collective-permute-start = (bf16[2,4,2,128,512]{4,3,2,1,0:T(8,128)(2,1)}, bf16[2,4,2,128,512]{4,3,2,1,0:T(8,128)(2,1)}, u32[]{:S(2)}, u32[]{:S(2)}) collective-permute-start(bf16[2,4,2,128,512]{4,3,2,1,0:T(8,128)(2,1)} %bitcast.5.refs_0_.refs_8_), channel_id=1, source_target_pairs={{0,4},{4,0},{8,12},{12,8},{16,20},{20,16},{24,28},{28,24},{1,5},{5... | collective-permute-start | bytes 6291464 | tf_op jit(solution)/shard_map/ppermute | solution.py:406
  198.6 10.5 %collective-permute-start.2 = (bf16[2,4,2,128,512]{4,3,2,1,0:T(8,128)(2,1)}, bf16[2,4,2,128,512]{4,3,2,1,0:T(8,128)(2,1)}, u32[]{:S(2)}, u32[]{:S(2)}) collective-permute-start(bf16[2,4,2,128,512]{4,3,2,1,0:T(8,128)(2,1)} %collective-permute-done.1.refs_2_.refs_10_), channel_id=1, source_target_pairs={{0,4},{4,0},{8,12},{12,8},{16,20},{20,16},{24,28},{28,24},{1,5},{5... | collective-permute-start | bytes 6291464 | tf_op jit(solution)/shard_map/ppermute | solution.py:406
  198.6 10.5 %collective-permute-start.4 = (bf16[2,4,2,128,512]{4,3,2,1,0:T(8,128)(2,1)}, bf16[2,4,2,128,512]{4,3,2,1,0:T(8,128)(2,1)}, u32[]{:S(2)}, u32[]{:S(2)}) collective-permute-start(bf16[2,4,2,128,512]{4,3,2,1,0:T(8,128)(2,1)} %collective-permute-done.3.refs_4_.refs_12_), channel_id=1, source_target_pairs={{0,4},{4,0},{8,12},{12,8},{16,20},{20,16},{24,28},{28,24},{1,5},{5... | collective-permute-start | bytes 6291464 | tf_op jit(solution)/shard_map/ppermute | solution.py:406
  209.2 175.7 %all-gather.11.cloned.1.call-start = ((), (), s32[]{:S(2)}) async-start(), calls=%async_computation.7 | async-start | bytes 5242880 | tf_op jit(solution)/shard_map/all_gather | solution.py:577
  306.8 239.5 %reduce-scatter.4.cloned.1.call-start = ((), (), s32[]{:S(2)}) async-start(), calls=%async_computation.8 | async-start | bytes 5242880 | tf_op jit(solution)/shard_map/reduce_scatter | solution.py:581
  306.9 31.8 %collective-permute-start.13 = (bf16[1,4,2,128,640]{4,3,2,1,0:T(8,128)(2,1)S(1)}, bf16[1,4,2,128,640]{4,3,2,1,0:T(8,128)(2,1)S(1)}, u32[]{:S(2)}, u32[]{:S(2)}) collective-permute-start(bf16[1,4,2,128,640]{4,3,2,1,0:T(8,128)(2,1)S(1)} %bitcast.76), channel_id=1, source_target_pairs={{0,8},{4,12},{8,0},{12,4},{16,24},{20,28},{24,16},{28,20},{1,9},{5... | collective-permute-start | bytes 3932168 | tf_op jit(solution)/shard_map/ppermute | solution.py:406
  307.0 56.7 %collective-permute-start.15 = (bf16[1,4,2,128,640]{4,3,2,1,0:T(8,128)(2,1)S(1)}, bf16[1,4,2,128,640]{4,3,2,1,0:T(8,128)(2,1)}, u32[]{:S(2)}, u32[]{:S(2)}) collective-permute-start(bf16[1,4,2,128,640]{4,3,2,1,0:T(8,128)(2,1)S(1)} %bitcast.77), channel_id=1, source_target_pairs={{0,16},{4,20},{8,24},{12,28},{16,0},{20,4},{24,8},{28,12},{1,17},{... | collective-permute-start | bytes 3932168 | tf_op jit(solution)/shard_map/ppermute | solution.py:406
  307.1 56.6 %collective-permute-start.17 = (bf16[1,4,2,128,640]{4,3,2,1,0:T(8,128)(2,1)S(1)}, bf16[1,4,2,128,640]{4,3,2,1,0:T(8,128)(2,1)}, u32[]{:S(2)}, u32[]{:S(2)}) collective-permute-start(bf16[1,4,2,128,640]{4,3,2,1,0:T(8,128)(2,1)S(1)} %bitcast.78), channel_id=1, source_target_pairs={{0,24},{4,28},{8,16},{12,20},{16,8},{20,12},{24,0},{28,4},{1,25},{... | collective-permute-start | bytes 3932168 | tf_op jit(solution)/shard_map/ppermute | solution.py:406
  310.5 53.7 %collective-permute-start.12 = (bf16[1,4,2,128,640]{4,3,2,1,0:T(8,128)(2,1)S(1)}, bf16[1,4,2,128,640]{4,3,2,1,0:T(8,128)(2,1)}, u32[]{:S(2)}, u32[]{:S(2)}) collective-permute-start(bf16[1,4,2,128,640]{4,3,2,1,0:T(8,128)(2,1)S(1)} %bitcast.79), channel_id=1, source_target_pairs={{0,4},{4,0},{8,12},{12,8},{16,20},{20,16},{24,28},{28,24},{1,5},{5... | collective-permute-start | bytes 3932168 | tf_op jit(solution)/shard_map/ppermute | solution.py:406
  338.7 25.5 %collective-permute-start.14 = (bf16[1,4,2,128,640]{4,3,2,1,0:T(8,128)(2,1)S(1)}, bf16[1,4,2,128,640]{4,3,2,1,0:T(8,128)(2,1)}, u32[]{:S(2)}, u32[]{:S(2)}) collective-permute-start(bf16[1,4,2,128,640]{4,3,2,1,0:T(8,128)(2,1)S(1)} %collective-permute-done.13.refs_2_.refs_18_), channel_id=1, source_target_pairs={{0,4},{4,0},{8,12},{12,8},{16,20},{20,16},{24,28},{28,24},{1,5},{5... | collective-permute-start | bytes 3932168 | tf_op jit(solution)/shard_map/ppermute | solution.py:406
  445.4 9.8 collective-permute-start.19
  445.4 300.8 %all-gather.13.cloned.1.call-start = ((), (), s32[]{:S(2)}) async-start(), calls=%async_computation.10 | async-start | bytes 5242880 | tf_op jit(solution)/shard_map/all_gather | solution.py:577
  453.3 57.4 %collective-permute-start.24 = (bf16[1408,1024]{1,0:T(8,128)(2,1)}, bf16[1408,1024]{1,0:T(8,128)(2,1)}, u32[]{:S(2)}, u32[]{:S(2)}) collective-permute-start(bf16[1408,1024]{1,0:T(8,128)(2,1)} %convolution_convert_fusion.2), channel_id=1, source_target_pairs={{0,4},{4,0},{8,12},{12,8},{16,20},{20,16},{24,28},{28,24},{1,5},{5... | collective-permute-start | bytes 8650760 | tf_op jit(solution)/shard_map/ppermute | solution.py:406
  466.9 33.9 %collective-permute-start.20 = (bf16[256,2816]{1,0:T(8,128)(2,1)}, bf16[256,2816]{1,0:T(8,128)(2,1)}, u32[]{:S(2)}, u32[]{:S(2)}) collective-permute-start(bf16[256,2816]{1,0:T(8,128)(2,1)} %constant_dynamic-slice_fusion.15), channel_id=1, source_target_pairs={{0,8},{4,12},{8,0},{12,4},{16,24},{20,28},{24,16},{28,20},{1,9},{5... | collective-permute-start | bytes 4325384 | tf_op jit(solution)/shard_map/ppermute | solution.py:406
  469.6 33.7 %collective-permute-start.21 = (bf16[256,2816]{1,0:T(8,128)(2,1)}, bf16[256,2816]{1,0:T(8,128)(2,1)}, u32[]{:S(2)}, u32[]{:S(2)}) collective-permute-start(bf16[256,2816]{1,0:T(8,128)(2,1)} %constant_dynamic-slice_fusion.14), channel_id=1, source_target_pairs={{0,16},{4,20},{8,24},{12,28},{16,0},{20,4},{24,8},{28,12},{1,17},{... | collective-permute-start | bytes 4325384 | tf_op jit(solution)/shard_map/ppermute | solution.py:406
  505.6 19.1 %collective-permute-start.22 = (bf16[128,2816]{1,0:T(8,128)(2,1)S(1)}, bf16[128,2816]{1,0:T(8,128)(2,1)S(1)}, u32[]{:S(2)}, u32[]{:S(2)}) collective-permute-start(bf16[128,2816]{1,0:T(8,128)(2,1)S(1)} %constant_dynamic-slice_fusion.13), channel_id=1, source_target_pairs={{0,16},{4,20},{8,24},{12,28},{16,0},{20,4},{24,8},{28,12},{1,17},{... | collective-permute-start | bytes 2162696 | tf_op jit(solution)/shard_map/ppermute | solution.py:406
  509.4 19.1 %collective-permute-start.23 = (bf16[128,2816]{1,0:T(8,128)(2,1)S(1)}, bf16[128,2816]{1,0:T(8,128)(2,1)S(1)}, u32[]{:S(2)}, u32[]{:S(2)}) collective-permute-start(bf16[128,2816]{1,0:T(8,128)(2,1)S(1)} %constant_dynamic-slice_fusion.12), channel_id=1, source_target_pairs={{0,8},{4,12},{8,0},{12,4},{16,24},{20,28},{24,16},{28,20},{1,9},{5... | collective-permute-start | bytes 2162696 | tf_op jit(solution)/shard_map/ppermute | solution.py:406
  516.1 27.9 %collective-permute-start.27 = (bf16[352,1024]{1,0:T(8,128)(2,1)S(1)}, bf16[352,1024]{1,0:T(8,128)(2,1)S(1)}, u32[]{:S(2)}, u32[]{:S(2)}) collective-permute-start(bf16[352,1024]{1,0:T(8,128)(2,1)S(1)} %constant_dynamic-slice_fusion.11), channel_id=1, source_target_pairs={{0,8},{4,12},{8,0},{12,4},{16,24},{20,28},{24,16},{28,20},{1,9},{5... | collective-permute-start | bytes 2162696 | tf_op jit(solution)/shard_map/ppermute | solution.py:406
  517.0 28.2 %collective-permute-start.28 = (bf16[352,1024]{1,0:T(8,128)(2,1)S(1)}, bf16[352,1024]{1,0:T(8,128)(2,1)S(1)}, u32[]{:S(2)}, u32[]{:S(2)}) collective-permute-start(bf16[352,1024]{1,0:T(8,128)(2,1)S(1)} %constant_dynamic-slice_fusion.10), channel_id=1, source_target_pairs={{0,16},{4,20},{8,24},{12,28},{16,0},{20,4},{24,8},{28,12},{1,17},{... | collective-permute-start | bytes 2162696 | tf_op jit(solution)/shard_map/ppermute | solution.py:406
  529.5 29.5 %collective-permute-start.25 = (bf16[128,2816]{1,0:T(8,128)(2,1)}, bf16[128,2816]{1,0:T(8,128)(2,1)}, u32[]{:S(2)}, u32[]{:S(2)}) collective-permute-start(bf16[128,2816]{1,0:T(8,128)(2,1)} %add_convert_fusion.11), channel_id=1, source_target_pairs={{0,16},{4,20},{8,24},{12,28},{16,0},{20,4},{24,8},{28,12},{1,17},{... | collective-permute-start | bytes 2162696 | tf_op jit(solution)/shard_map/ppermute | solution.py:406
  531.0 31.3 %collective-permute-start.26 = (bf16[128,2816]{1,0:T(8,128)(2,1)}, bf16[128,2816]{1,0:T(8,128)(2,1)}, u32[]{:S(2)}, u32[]{:S(2)}) collective-permute-start(bf16[128,2816]{1,0:T(8,128)(2,1)} %add_convert_fusion.10), channel_id=1, source_target_pairs={{0,8},{4,12},{8,0},{12,4},{16,24},{20,28},{24,16},{28,20},{1,9},{5... | collective-permute-start | bytes 2162696 | tf_op jit(solution)/shard_map/ppermute | solution.py:406
  593.7 393.3 %reduce-scatter.6.cloned.1.call-start = ((), (), s32[]{:S(2)}) async-start(), calls=%async_computation.9 | async-start | bytes 5242880 | tf_op jit(solution)/shard_map/reduce_scatter | solution.py:581
  593.7 31.9 %collective-permute-start.29 = (bf16[256,2816]{1,0:T(8,128)(2,1)}, bf16[256,2816]{1,0:T(8,128)(2,1)}, u32[]{:S(2)}, u32[]{:S(2)}) collective-permute-start(bf16[256,2816]{1,0:T(8,128)(2,1)} %maximum_select_fusion.2), channel_id=1, source_target_pairs={{0,8},{4,12},{8,0},{12,4},{16,24},{20,28},{24,16},{28,20},{1,9},{5... | collective-permute-start | bytes 4325384 | tf_op jit(solution)/shard_map/ppermute | solution.py:406
  595.7 34.8 %collective-permute-start.30 = (bf16[256,2816]{1,0:T(8,128)(2,1)}, bf16[256,2816]{1,0:T(8,128)(2,1)}, u32[]{:S(2)}, u32[]{:S(2)}) collective-permute-start(bf16[256,2816]{1,0:T(8,128)(2,1)} %maximum_select_fusion.3), channel_id=1, source_target_pairs={{0,16},{4,20},{8,24},{12,28},{16,0},{20,4},{24,8},{28,12},{1,17},{... | collective-permute-start | bytes 4325384 | tf_op jit(solution)/shard_map/ppermute | solution.py:406
  597.5 42.5 %collective-permute-start.31 = (bf16[176,1024]{1,0:T(8,128)(2,1)}, bf16[176,1024]{1,0:T(8,128)(2,1)}, u32[]{:S(2)}, u32[]{:S(2)}) collective-permute-start(bf16[176,1024]{1,0:T(8,128)(2,1)} %constant_dynamic-slice_fusion.9), channel_id=1, source_target_pairs={{0,16},{4,20},{8,24},{12,28},{16,0},{20,4},{24,8},{28,12},{1,17},{... | collective-permute-start | bytes 1081352 | tf_op jit(solution)/shard_map/ppermute | solution.py:406
  639.1 115.9 %collective-permute-start.42 = (bf16[1024,2816]{1,0:T(8,128)(2,1)}, bf16[1024,2816]{1,0:T(8,128)(2,1)}, u32[]{:S(2)}, u32[]{:S(2)}) collective-permute-start(bf16[1024,2816]{1,0:T(8,128)(2,1)} %pad_maximum_fusion.half_ref), channel_id=1, source_target_pairs={{0,4},{4,0},{8,12},{12,8},{16,20},{20,16},{24,28},{28,24},{1,5},{5... | collective-permute-start | bytes 17301512 | tf_op jit(solution)/shard_map/ppermute | solution.py:406
  639.9 11.1 %collective-permute-start.32 = (bf16[176,1024]{1,0:T(8,128)(2,1)}, bf16[176,1024]{1,0:T(8,128)(2,1)}, u32[]{:S(2)}, u32[]{:S(2)}) collective-permute-start(bf16[176,1024]{1,0:T(8,128)(2,1)} %constant_dynamic-slice_fusion.8), channel_id=1, source_target_pairs={{0,8},{4,12},{8,0},{12,4},{16,24},{20,28},{24,16},{28,20},{1,9},{5... | collective-permute-start | bytes 1081352 | tf_op jit(solution)/shard_map/ppermute | solution.py:406
  658.8 72.1 %collective-permute-start.34 = (bf16[1,4,2,128,640]{4,3,2,1,0:T(8,128)(2,1)S(1)}, bf16[1,4,2,128,640]{4,3,2,1,0:T(8,128)(2,1)}, u32[]{:S(2)}, u32[]{:S(2)}) collective-permute-start(bf16[1,4,2,128,640]{4,3,2,1,0:T(8,128)(2,1)S(1)} %pad_maximum_fusion.6.refs_8_.refs_24_), channel_id=1, source_target_pairs={{0,8},{4,12},{8,0},{12,4},{16,24},{20,28},{24,16},{28,20},{1,9},{5... | collective-permute-start | bytes 3932168 | tf_op jit(solution)/shard_map/ppermute | solution.py:406
  659.1 71.9 %collective-permute-start.36 = (bf16[1,4,2,128,640]{4,3,2,1,0:T(8,128)(2,1)S(1)}, bf16[1,4,2,128,640]{4,3,2,1,0:T(8,128)(2,1)}, u32[]{:S(2)}, u32[]{:S(2)}) collective-permute-start(bf16[1,4,2,128,640]{4,3,2,1,0:T(8,128)(2,1)S(1)} %pad_maximum_fusion.6.refs_8_.refs_24_), channel_id=1, source_target_pairs={{0,16},{4,20},{8,24},{12,28},{16,0},{20,4},{24,8},{28,12},{1,17},{... | collective-permute-start | bytes 3932168 | tf_op jit(solution)/shard_map/ppermute | solution.py:406
  659.1 72.0 %collective-permute-start.38 = (bf16[1,4,2,128,640]{4,3,2,1,0:T(8,128)(2,1)S(1)}, bf16[1,4,2,128,640]{4,3,2,1,0:T(8,128)(2,1)}, u32[]{:S(2)}, u32[]{:S(2)}) collective-permute-start(bf16[1,4,2,128,640]{4,3,2,1,0:T(8,128)(2,1)S(1)} %pad_maximum_fusion.6.refs_8_.refs_24_), channel_id=1, source_target_pairs={{0,24},{4,28},{8,16},{12,20},{16,8},{20,12},{24,0},{28,4},{1,25},{... | collective-permute-start | bytes 3932168 | tf_op jit(solution)/shard_map/ppermute | solution.py:406
  662.3 352.1 %reduce-scatter.8.cloned.1.call-start = ((), (), s32[]{:S(2)}) async-start(), calls=%async_computation.11 | async-start | bytes 5242880 | tf_op jit(solution)/shard_map/reduce_scatter | solution.py:581
  745.6 49.9 %collective-permute-start.43 = (bf16[352,1024]{1,0:T(8,128)(2,1)}, bf16[352,1024]{1,0:T(8,128)(2,1)}, u32[]{:S(2)}, u32[]{:S(2)}) collective-permute-start(bf16[352,1024]{1,0:T(8,128)(2,1)} %maximum_select_fusion.10), channel_id=1, source_target_pairs={{0,8},{4,12},{8,0},{12,4},{16,24},{20,28},{24,16},{28,20},{1,9},{5... | collective-permute-start | bytes 2162696 | tf_op jit(solution)/shard_map/ppermute | solution.py:406
  752.3 57.1 %collective-permute-start.45 = (bf16[1024,1024]{1,0:T(8,128)(2,1)S(1)}, bf16[1024,1024]{1,0:T(8,128)(2,1)}, u32[]{:S(2)}, u32[]{:S(2)}) collective-permute-start(bf16[1024,1024]{1,0:T(8,128)(2,1)S(1)} %pad_maximum_fusion.2), channel_id=1, source_target_pairs={{0,4},{4,0},{8,12},{12,8},{16,20},{20,16},{24,28},{28,24},{1,5},{5... | collective-permute-start | bytes 6291464 | tf_op jit(solution)/shard_map/ppermute | solution.py:406
  754.4 41.1 %collective-permute-start.44 = (bf16[352,1024]{1,0:T(8,128)(2,1)S(1)}, bf16[352,1024]{1,0:T(8,128)(2,1)S(1)}, u32[]{:S(2)}, u32[]{:S(2)}) collective-permute-start(bf16[352,1024]{1,0:T(8,128)(2,1)S(1)} %maximum_select_fusion.11), channel_id=1, source_target_pairs={{0,16},{4,20},{8,24},{12,28},{16,0},{20,4},{24,8},{28,12},{1,17},{... | collective-permute-start | bytes 2162696 | tf_op jit(solution)/shard_map/ppermute | solution.py:406
  800.7 144.7 %collective-permute-start.62 = (bf16[1408,1024]{1,0:T(8,128)(2,1)}, bf16[1408,1024]{1,0:T(8,128)(2,1)}, u32[]{:S(2)}, u32[]{:S(2)}) collective-permute-start(bf16[1408,1024]{1,0:T(8,128)(2,1)} %pad_maximum_fusion.1.half_ref), channel_id=1, source_target_pairs={{0,4},{4,0},{8,12},{12,8},{16,20},{20,16},{24,28},{28,24},{1,5},{5... | collective-permute-start | bytes 8650760 | tf_op jit(solution)/shard_map/ppermute | solution.py:406
  869.0 30.4 %collective-permute-start.46 = (bf16[1024,1024]{1,0:T(8,128)(2,1)}, bf16[1024,1024]{1,0:T(8,128)(2,1)}, u32[]{:S(2)}, u32[]{:S(2)}) collective-permute-start(bf16[1024,1024]{1,0:T(8,128)(2,1)} %fusion.44), channel_id=1, source_target_pairs={{0,4},{4,0},{8,12},{12,8},{16,20},{20,16},{24,28},{28,24},{1,5},{5... | collective-permute-start | bytes 6291464 | tf_op jit(solution)/shard_map/ppermute | solution.py:406
  874.8 36.2 %collective-permute-start.52 = (bf16[256,1024]{1,0:T(8,128)(2,1)}, bf16[256,1024]{1,0:T(8,128)(2,1)}, u32[]{:S(2)}, u32[]{:S(2)}) collective-permute-start(bf16[256,1024]{1,0:T(8,128)(2,1)} %constant_dynamic-slice_fusion.7), channel_id=1, source_target_pairs={{0,8},{4,12},{8,0},{12,4},{16,24},{20,28},{24,16},{28,20},{1,9},{5... | collective-permute-start | bytes 1572872 | tf_op jit(solution)/shard_map/ppermute | solution.py:406
  899.4 13.9 %collective-permute-start.53 = (bf16[256,1024]{1,0:T(8,128)(2,1)}, bf16[256,1024]{1,0:T(8,128)(2,1)}, u32[]{:S(2)}, u32[]{:S(2)}) collective-permute-start(bf16[256,1024]{1,0:T(8,128)(2,1)} %constant_dynamic-slice_fusion.6), channel_id=1, source_target_pairs={{0,16},{4,20},{8,24},{12,28},{16,0},{20,4},{24,8},{28,12},{1,17},{... | collective-permute-start | bytes 1572872 | tf_op jit(solution)/shard_map/ppermute | solution.py:406
  905.2 13.0 %collective-permute-start.47 = (f32[14,1024]{1,0:T(8,128)S(1)}, f32[14,1024]{1,0:T(8,128)S(1)}, u32[]{:S(2)}, u32[]{:S(2)}) collective-permute-start(f32[14,1024]{1,0:T(8,128)S(1)} %reshape.269), channel_id=1, source_target_pairs={{0,4},{4,0},{8,12},{12,8},{16,20},{20,16},{24,28},{28,24},{1,5},{5... | collective-permute-start | bytes 172040 | tf_op jit(solution)/shard_map/ppermute | solution.py:627
  914.3 21.6 %collective-permute-start.56 = (bf16[256,1024]{1,0:T(8,128)(2,1)S(1)}, bf16[256,1024]{1,0:T(8,128)(2,1)S(1)}, u32[]{:S(2)}, u32[]{:S(2)}) collective-permute-start(bf16[256,1024]{1,0:T(8,128)(2,1)S(1)} %constant_dynamic-slice_fusion.3), channel_id=1, source_target_pairs={{0,8},{4,12},{8,0},{12,4},{16,24},{20,28},{24,16},{28,20},{1,9},{5... | collective-permute-start | bytes 1572872 | tf_op jit(solution)/shard_map/ppermute | solution.py:406
  914.7 21.2 %collective-permute-start.57 = (bf16[256,1024]{1,0:T(8,128)(2,1)S(1)}, bf16[256,1024]{1,0:T(8,128)(2,1)S(1)}, u32[]{:S(2)}, u32[]{:S(2)}) collective-permute-start(bf16[256,1024]{1,0:T(8,128)(2,1)S(1)} %constant_dynamic-slice_fusion.2), channel_id=1, source_target_pairs={{0,16},{4,20},{8,24},{12,28},{16,0},{20,4},{24,8},{28,12},{1,17},{... | collective-permute-start | bytes 1572872 | tf_op jit(solution)/shard_map/ppermute | solution.py:406
  916.4 20.1 %collective-permute-start.54 = (bf16[128,1024]{1,0:T(8,128)(2,1)S(1)}, bf16[128,1024]{1,0:T(8,128)(2,1)S(1)}, u32[]{:S(2)}, u32[]{:S(2)}) collective-permute-start(bf16[128,1024]{1,0:T(8,128)(2,1)S(1)} %constant_dynamic-slice_fusion.5), channel_id=1, source_target_pairs={{0,16},{4,20},{8,24},{12,28},{16,0},{20,4},{24,8},{28,12},{1,17},{... | collective-permute-start | bytes 786440 | tf_op jit(solution)/shard_map/ppermute | solution.py:406
  918.2 10.3 %collective-permute-start.48 = (f32[14,1024]{1,0:T(8,128)S(1)}, f32[14,1024]{1,0:T(8,128)S(1)}, u32[]{:S(2)}, u32[]{:S(2)}) collective-permute-start(f32[14,1024]{1,0:T(8,128)S(1)} %add.367), channel_id=1, source_target_pairs={{0,8},{4,12},{8,0},{12,4},{16,24},{20,28},{24,16},{28,20},{1,9},{5... | collective-permute-start | bytes 172040 | tf_op jit(solution)/shard_map/ppermute | solution.py:627
  940.9 14.2 %collective-permute-start.60 = (bf16[128,1024]{1,0:T(8,128)(2,1)S(1)}, bf16[128,1024]{1,0:T(8,128)(2,1)S(1)}, u32[]{:S(2)}, u32[]{:S(2)}) collective-permute-start(bf16[128,1024]{1,0:T(8,128)(2,1)S(1)} %constant_dynamic-slice_fusion.1), channel_id=1, source_target_pairs={{0,16},{4,20},{8,24},{12,28},{16,0},{20,4},{24,8},{28,12},{1,17},{... | collective-permute-start | bytes 786440 | tf_op jit(solution)/shard_map/ppermute | solution.py:406
  941.8 13.2 %collective-permute-start.61 = (bf16[128,1024]{1,0:T(8,128)(2,1)S(1)}, bf16[128,1024]{1,0:T(8,128)(2,1)S(1)}, u32[]{:S(2)}, u32[]{:S(2)}) collective-permute-start(bf16[128,1024]{1,0:T(8,128)(2,1)S(1)} %constant_dynamic-slice_fusion), channel_id=1, source_target_pairs={{0,8},{4,12},{8,0},{12,4},{16,24},{20,28},{24,16},{28,20},{1,9},{5... | collective-permute-start | bytes 786440 | tf_op jit(solution)/shard_map/ppermute | solution.py:406
  943.2 12.1 %collective-permute-start.58 = (bf16[128,1024]{1,0:T(8,128)(2,1)S(1)}, bf16[128,1024]{1,0:T(8,128)(2,1)S(1)}, u32[]{:S(2)}, u32[]{:S(2)}) collective-permute-start(bf16[128,1024]{1,0:T(8,128)(2,1)S(1)} %add_convert_fusion.21), channel_id=1, source_target_pairs={{0,16},{4,20},{8,24},{12,28},{16,0},{20,4},{24,8},{28,12},{1,17},{... | collective-permute-start | bytes 786440 | tf_op jit(solution)/shard_map/ppermute | solution.py:406
  944.7 10.5 %collective-permute-start.59 = (bf16[128,1024]{1,0:T(8,128)(2,1)S(1)}, bf16[128,1024]{1,0:T(8,128)(2,1)S(1)}, u32[]{:S(2)}, u32[]{:S(2)}) collective-permute-start(bf16[128,1024]{1,0:T(8,128)(2,1)S(1)} %add_convert_fusion.20), channel_id=1, source_target_pairs={{0,8},{4,12},{8,0},{12,4},{16,24},{20,28},{24,16},{28,20},{1,9},{5... | collective-permute-start | bytes 786440 | tf_op jit(solution)/shard_map/ppermute | solution.py:406
  955.4 21.0 %collective-permute-start.63 = (bf16[256,1024]{1,0:T(8,128)(2,1)S(1)}, bf16[256,1024]{1,0:T(8,128)(2,1)S(1)}, u32[]{:S(2)}, u32[]{:S(2)}) collective-permute-start(bf16[256,1024]{1,0:T(8,128)(2,1)S(1)} %maximum_select_fusion.12), channel_id=1, source_target_pairs={{0,8},{4,12},{8,0},{12,4},{16,24},{20,28},{24,16},{28,20},{1,9},{5... | collective-permute-start | bytes 1572872 | tf_op jit(solution)/shard_map/ppermute | solution.py:406
  957.0 19.4 %collective-permute-start.64 = (bf16[256,1024]{1,0:T(8,128)(2,1)S(1)}, bf16[256,1024]{1,0:T(8,128)(2,1)S(1)}, u32[]{:S(2)}, u32[]{:S(2)}) collective-permute-start(bf16[256,1024]{1,0:T(8,128)(2,1)S(1)} %maximum_select_fusion.13), channel_id=1, source_target_pairs={{0,16},{4,20},{8,24},{12,28},{16,0},{20,4},{24,8},{28,12},{1,17},{... | collective-permute-start | bytes 1572872 | tf_op jit(solution)/shard_map/ppermute | solution.py:406
  957.8 16.8 %collective-permute-start.65 = (bf16[128,1024]{1,0:T(8,128)(2,1)S(1)}, bf16[128,1024]{1,0:T(8,128)(2,1)S(1)}, u32[]{:S(2)}, u32[]{:S(2)}) collective-permute-start(bf16[128,1024]{1,0:T(8,128)(2,1)S(1)} %add_convert_fusion.19), channel_id=1, source_target_pairs={{0,16},{4,20},{8,24},{12,28},{16,0},{20,4},{24,8},{28,12},{1,17},{... | collective-permute-start | bytes 786440 | tf_op jit(solution)/shard_map/ppermute | solution.py:406
  959.1 15.5 %collective-permute-start.66 = (bf16[128,1024]{1,0:T(8,128)(2,1)S(1)}, bf16[128,1024]{1,0:T(8,128)(2,1)S(1)}, u32[]{:S(2)}, u32[]{:S(2)}) collective-permute-start(bf16[128,1024]{1,0:T(8,128)(2,1)S(1)} %add_convert_fusion.18), channel_id=1, source_target_pairs={{0,8},{4,12},{8,0},{12,4},{16,24},{20,28},{24,16},{28,20},{1,9},{5... | collective-permute-start | bytes 786440 | tf_op jit(solution)/shard_map/ppermute | solution.py:406
  974.7 9.2 collective-permute-start.69
  977.6 19.4 %collective-permute-start.67 = (bf16[1024,1024]{1,0:T(8,128)(2,1)S(1)}, bf16[1024,1024]{1,0:T(8,128)(2,1)}, u32[]{:S(2)}, u32[]{:S(2)}) collective-permute-start(bf16[1024,1024]{1,0:T(8,128)(2,1)S(1)} %pad_maximum_fusion.3.half_ref), channel_id=1, source_target_pairs={{0,4},{4,0},{8,12},{12,8},{16,20},{20,16},{24,28},{28,24},{1,5},{5... | collective-permute-start | bytes 6291464 | tf_op jit(solution)/shard_map/ppermute | solution.py:406
  986.8 19.9 %collective-permute-start.70 = (bf16[1024,1024]{1,0:T(8,128)(2,1)}, bf16[1024,1024]{1,0:T(8,128)(2,1)}, u32[]{:S(2)}, u32[]{:S(2)}) collective-permute-start(bf16[1024,1024]{1,0:T(8,128)(2,1)} %pad_maximum_fusion.4.half_ref), channel_id=1, source_target_pairs={{0,4},{4,0},{8,12},{12,8},{16,20},{20,16},{24,28},{28,24},{1,5},{5... | collective-permute-start | bytes 6291464 | tf_op jit(solution)/shard_map/ppermute | solution.py:406
  (98 other events, 1102.3 us)
Sparse Core Ops, SparseCore 0:
  12.7 83.4 all-gather.6
  97.8 79.2 all-gather.8
  209.3 55.7 all-gather.14
  306.9 77.9 all-gather.10
  445.5 75.4 reduce-scatter.3
  593.8 79.3 all-gather.12
  676.1 75.2 reduce-scatter.5
  861.6 99.1 reduce-scatter.7

commit v6 on v5

--- a/solution.py
+++ b/solution.py
@@ -310,16 +310,11 @@
 
 def rotary_tables(positions):
     half = ROT // 2
-    freq = 10000.0 ** (-2.0 * jnp.arange(half, dtype=F32) / ROT)
+    dim = jnp.arange(2 * HEAD_DIM) % HEAD_DIM
+    freq = jnp.where(dim < ROT, 10000.0 ** (-2.0 * (dim % half).astype(F32) / ROT), 0.0)
     angles = positions.astype(F32)[:, None] * freq[None, :]
-    cos, sin = jnp.cos(angles), jnp.sin(angles)
-    rows = positions.shape[0]
-    one, none = jnp.ones((rows, HEAD_DIM - ROT), F32), jnp.zeros((rows, HEAD_DIM - ROT), F32)
-    zero = jnp.zeros_like(sin)
-    ctab = jnp.concatenate([cos, cos, one] * 2, axis=1)
-    above = jnp.concatenate([sin, zero, none] * 2, axis=1)
-    below = jnp.concatenate([zero, sin, none] * 2, axis=1)
-    return ctab, above, below
+    sin = jnp.sin(angles)
+    return jnp.cos(angles), jnp.where(dim < half, sin, 0.0), jnp.where(dim < half, 0.0, sin)
 
 
 def turn(x, ctab, above, below, sign):
@@ -523,62 +518,36 @@
     return lax.dynamic_slice_in_dim(x, which * w, w, 1)
 
 
-def unpack_cols_kernel(core_ref, half_ref, other_ref, out_ref):
-    c = half_ref.shape[1]
-    core = core_ref[0]
-    out_ref[:, pl.ds(pl.multiple_of(core * c, 128), c)] = half_ref[...].astype(F32)
-    out_ref[:, pl.ds(pl.multiple_of((1 - core) * c, 128), c)] = other_ref[...].astype(F32)
-
-
-def unpack_cols(half, other, r):
-    c = half.shape[1]
-    step = math.gcd(r, 256)
-    block = pl.BlockSpec((step, c), lambda i, _: (i, 0))
-    return pl.pallas_call(
-        unpack_cols_kernel,
-        grid_spec=pltpu.PrefetchScalarGridSpec(
-            num_scalar_prefetch=1, grid=(r // step,), in_specs=[block, block],
-            out_specs=pl.BlockSpec((step, 2 * c), lambda i, _: (i, 0))),
-        out_shape=jax.ShapeDtypeStruct((r, 2 * c), F32),
-        compiler_params=pltpu.CompilerParams(vmem_limit_bytes=40 * 2**20),
-        cost_estimate=pl.CostEstimate(flops=0, bytes_accessed=12 * r * c, transcendentals=0),
-        name="unpack_cols",
-    )((lax.axis_index("ctx") & 1)[None], half, other)
-
-
-def unpack_turned_kernel(core_ref, half_ref, other_ref, out_ref):
-    @pl.when(pl.program_id(0) == core_ref[0])
-    def _():
-        out_ref[...] = half_ref[...].astype(F32).T
-
-    @pl.when(pl.program_id(0) != core_ref[0])
-    def _():
-        out_ref[...] = other_ref[...].astype(F32).T
-
-
-def unpack_turned(half, other, r):
-    c = half.shape[1]
-    step = 256
-    blocks = c // step
-    block = pl.BlockSpec((r, step), lambda i, j, _: (1, j))
-    return pl.pallas_call(
-        unpack_turned_kernel,
-        grid_spec=pltpu.PrefetchScalarGridSpec(
-            num_scalar_prefetch=1, grid=(2, blocks), in_specs=[block, block],
-            out_specs=pl.BlockSpec((step, r), lambda i, j, _: (i * blocks + j, 0))),
-        out_shape=jax.ShapeDtypeStruct((2 * c, r), F32),
-        compiler_params=pltpu.CompilerParams(vmem_limit_bytes=40 * 2**20),
-        cost_estimate=pl.CostEstimate(flops=0, bytes_accessed=12 * r * c, transcendentals=0),
-        name="unpack_turned",
-    )((lax.axis_index("ctx") & 1)[None], half, other)
-
-
 def all_rows(x):
     return lax.all_gather(x, "tp", axis=0, tiled=True)
 
 
+def tp_shift(x, d):
+    n = lax.axis_size("tp")
+    return lax.ppermute(x, "tp", [(i, (i + d) % n) for i in range(n)])
+
+
+def part_of(x, d, axis):
+    n = lax.axis_size("tp")
+    w = x.shape[axis] // n
+    return lax.dynamic_slice_in_dim(x, (lax.axis_index("tp") + d) % n * w, w, axis)
+
+
+def exchange(x, split, join):
+    n, me = lax.axis_size("tp"), lax.axis_index("tp")
+    w = x.shape[join]
+    shape = list(x.shape)
+    shape[split] //= n
+    shape[join] *= n
+    out = jnp.zeros(shape, x.dtype)
+    for d in range(n):
+        got = tp_shift(part_of(x, d, split), d) if d else part_of(x, 0, split)
+        out = lax.dynamic_update_slice_in_dim(out, got, (me + n - d) % n * w, join)
+    return out
+
+
 def sum_rows(x):
-    return lax.psum_scatter(x, "tp", scatter_dimension=0, tiled=True).astype(F32)
+    return lax.psum_scatter(x, "tp", scatter_dimension=0, tiled=True)
 
 
 def gather_pair(kv):
@@ -669,7 +638,7 @@
 
     attn, q_ext = attend(place, own, q, keys, values)
     attn_rows = attn.reshape(-1, width)
-    attn_own = lax.all_to_all(attn_rows, "tp", split_axis=0, concat_axis=1, tiled=True)
+    attn_own = exchange(attn_rows, 0, 1)
     mixed = x + nn(attn_own, whole_w)
     normed_two, unit_two, inverse_two = layer_stats(mixed, gain_two, shift_two)
     rows_two = all_rows(after(normed_two.astype(BF16), dy_rows, whole_w))
@@ -683,101 +652,82 @@
     grad_two = sum_rows(part_two)
     act, rows_two, dy_rows, grad_gu = after((act, rows_two, dy_rows, grad_gu), part_two)
     gu = begin(lambda core: rc(columns(rows_two, core), grad_gu))
+    grad_down_w = rc(act, dy_rows).astype(BF16)
     held = take(gu)
     go(gu)
-    dw = begin(lambda core: rc(act, columns(dy_rows, core)))
-    act_late = after(act, held)
-    down = nn(act_late, down_w).astype(BF16)
-    held = take(dw), take(gu, down)
+    down = nn(after(act, held), down_w).astype(BF16)
+    held = take(gu, down)
+    grad_two, grad_down_w = after((grad_two, grad_down_w), held, down)
     go(gu)
-    go(dw, held)
-    grad_two = after(grad_two, take(gu, held))
-    go(gu)
-
-    norm_two, grad_gain_two, grad_shift_two = layer_back(grad_two, unit_two, inverse_two, gain_two)
+    grad_down_w = lax.psum(grad_down_w, "ctx")
+
+    norm_two, grad_gain_two, grad_shift_two = layer_back(grad_two.astype(F32), unit_two, inverse_two, gain_two)
     grad_mixed = cotangent.astype(F32) + norm_two
     branch_own = grad_mixed.astype(BF16)
     grad_attn = nt(branch_own, whole_w).astype(BF16)
-    grad_attn = after(grad_attn, take(gu), take(dw))
+    grad_attn = after(grad_attn, take(gu))
     go(gu)
-    go(dw)
-    grad_attn = lax.all_to_all(grad_attn, "tp", split_axis=1, concat_axis=0, tiled=True)
+    grad_attn = exchange(grad_attn, 1, 0)
     branch = all_rows(after(branch_own, grad_attn))
-    out_tokens = (mixed + sum_rows(after(down, grad_attn))).astype(BF16)
+    out_tokens = (mixed + sum_rows(after(down, grad_attn)).astype(F32)).astype(BF16)
     lane = jnp.arange(128)[None, :]
     ind = ((jnp.arange(width) // HEAD_DIM)[:, None] == lane // 3).astype(F32)
     delta = lax.dot_general(grad_attn.astype(F32) * attn_rows.astype(F32), ind, (((1,), (0,)), ((), ())),
                             precision=lax.Precision.HIGHEST, preferred_element_type=F32)
     do_ext = terms(-delta, lane).astype(BF16)
     do_sent = jnp.concatenate([grad_attn, do_ext], axis=1).reshape(shape)
-    grads = gather_other(after(do_sent, take(gu, grad_attn), take(dw, grad_attn)))
-    take_extra(gu)
-    go(gu)
+    grads = gather_other(after(do_sent, take(gu, grad_attn)))
     grad_q = query_grad(place, own, q, grad_attn.reshape(q.shape), q_ext, do_ext.reshape(q_ext.shape), tabs, keys, values)
     grad_q = grad_q.reshape(-1, width)
     q_part = nt(grad_q, query_w)
-    go(dw, q_part)
     grads = gather_cores(grads, q_part)
-    grad_gate_w, grad_up_w = unpack_rows(*take(gu, q_part), 2)
-    rows_q, branch = after((rows_one, branch), grads)
-    oq = begin(lambda core: jnp.concatenate([rc(attn_rows, columns(branch, core)), rc(grad_q, columns(rows_q, core))]))
-    held = take(dw, grads)
-    go(dw)
-    first = key_value_grad(place, own, kv, tabs, queries, after(grads, held, grad_gate_w), 0, SEQS // 2)
-    grads = after(grads, take(dw, first), take(oq, first))
-    take_extra(dw)
-    go(dw)
-    go(oq)
+    go(gu, grads)
+    first = key_value_grad(place, own, kv, tabs, queries, grads, 0, SEQS // 2)
+    grads = after(grads, take(gu, first))
+    take_extra(gu)
+    go(gu)
     second = key_value_grad(place, own, kv, tabs, queries, grads, SEQS // 2, SEQS // 2)
     grad_k, grad_v = (jnp.concatenate(pair).reshape(-1, width) for pair in zip(first, second))
     part_one = q_part + nt(grad_k, key_w) + nt(grad_v, value_w)
     part_sent = part_one.astype(BF16)
     grad_one = sum_rows(part_sent)
 
-    rows_one, grad_q, grad_k, grad_v = after((rows_one, grad_q, grad_k, grad_v), part_sent)
-    grad_kv = jnp.concatenate([grad_k, grad_v], axis=1)
-    dkv = begin(lambda core: rc(columns(rows_one, core), grad_kv))
+    rows_one, branch, grad_q, grad_k, grad_v = after((rows_one, branch, grad_q, grad_k, grad_v), part_sent)
+    grad_qkv = jnp.concatenate([grad_q, grad_k, grad_v], axis=1)
+    chain = begin(lambda core: rc(columns(rows_one, core), grad_qkv))
     unit_rows = (rows_one.astype(F32) - shift_one) / gain_one
-    bias_grad = jnp.concatenate([jnp.sum(g.astype(F32), axis=0) for g in (grad_q, grad_kv)])
+    bias_grad = jnp.sum(grad_qkv.astype(F32), axis=0)
     tp_row = (jnp.arange(n_tp) == lax.axis_index("tp"))[:, None]
     small = jnp.concatenate([
         jnp.sum(part_one * unit_rows, axis=0), jnp.sum(part_one, axis=0), grad_gain_two, grad_shift_two,
         jnp.where(tp_row, bias_grad[None, :], 0.0).reshape(-1)])
-    held = take(dkv)
-    go(dkv)
+    held = take(chain)
+    go(chain)
+    grad_output_w = lax.psum(after(rc(attn_rows, after(branch, held)).astype(BF16), grad_down_w), "ctx")
+    grad_gate_w, grad_up_w = unpack_rows(*take(gu, held), 2)
     sums = sum_over_all(after(small, held).reshape(-1, 1024))
+    small = next(sums), grad_gate_w
+    held = take(chain, small)
+    go(chain)
     small = next(sums), next(sums)
-    take(oq, held)
-    held = take(dkv, small)
-    go(oq)
-    go(dkv)
-    grad_down_w = unpack_cols(*take(dw, held), act.shape[1])
+    held = take(chain, small)
+    go(chain)
+    grad_down_w = after(grad_down_w, held).astype(F32)
     small = next(sums), grad_down_w
-    take(oq, held)
-    held = take(dkv, small)
-    go(oq)
-    go(dkv)
-    small = next(sums)
-    take(oq, held)
-    held = take(dkv, small)
-    go(oq)
-    go(dkv)
+    held = take(chain, small)
+    go(chain)
     for _ in range(4):
         small = next(sums)
-    take(oq, held)
-    take(dkv)
-    take_extra(oq)
-    take_extra(dkv)
-    go(oq)
-    go(dkv)
+    take(chain)
+    take_extra(chain)
+    go(chain)
     depth = x.shape[1]
     small = small.reshape(-1)
     norms = small[:4 * depth].reshape(4, depth)
     bias_sum = jnp.sum(jnp.where(tp_row, small[4 * depth:].reshape(n_tp, -1), 0.0), axis=0)
-    halves = take(oq)
-    grad_output_w, grad_query_w = unpack_cols(*halves, width), unpack_turned(*halves, width)
-    grad_key_w, grad_value_w = unpack_rows(*take(dkv), 2)
-    norm_one, _, _ = layer_back(grad_one, unit_one, inverse_one, gain_one)
+    grad_query_w, grad_key_w, grad_value_w = unpack_rows(*take(chain), 3)
+    grad_output_w = grad_output_w.astype(F32)
+    norm_one, _, _ = layer_back(grad_one.astype(F32), unit_one, inverse_one, gain_one)
     grad_tokens = (grad_mixed + norm_one).astype(BF16)
     return (
         out_tokens, grad_tokens, norms[0], norms[1], grad_query_w, grad_key_w, grad_value_w,

time: 1040 us -> 1030 us (level)
  waiting for transfers between devices: 372 us -> 479 us
  blocking collectives: 54.4 us -> 0 us
  local copies, waits for them, and re-layouts: 61.6 us -> 40.5 us
  Pallas kernels: 250 us -> 229 us
    reduce_scatter x3, waiting for transfers between devices: 0.01 us -> 74.7 us  [sum_rows(): return lax.psum_scatter(x, 'tp', scatter_dimension=0, tiled=True)]
    all_to_all x2 -> x0, blocking collectives: 54.4 us -> none  [the longest x1 29.2 us: local(): lax.all_to_all(attn_rows, 'tp', split_axis=0, concat_axis=1, tiled=True)]
    ppermute x0 -> x6, waiting for transfers between devices: none -> 30.1 us  [tp_shift(): return lax.ppermute(x, 'tp', [(i, (i + d) % n) for i in range(n)])]
    ppermute x63 -> x43, waiting for transfers between devices: 236 us -> 214 us  [ctx_swap(): return lax.ppermute(x, 'ctx', [(i, i ^ mask) for i in range(n)])]
    ppermute x63 -> x43, starting transfers between devices: 74.5 us -> 53.6 us  [ctx_swap(): return lax.ppermute(x, 'ctx', [(i, i ^ mask) for i in range(n)])]
    pallas_call x3 -> x0, Pallas kernels: 19.4 us -> none  [the longest x2 12.8 us: unpack_cols(): pl.pallas_call(unpack_cols_kernel, grid_spec=pltpu.PrefetchScalarGridSpec...]
    ppermute x3, waiting for transfers between devices: 15.9 us -> 29.8 us  [gather_tp(): lax.ppermute(x, 'tp', [(i, (i + d) % n) for i in range(n)])]
    dot_general x10 -> x6, matrix products: 51.4 us -> 41.4 us  [rc(): lax.dot_general(left, right, (((0,), (0,)), ((), ())), preferred_element_...]
  transfers between devices with their start and end apart: 79 -> 67, of which waited for: 34 -> 42; matrix products, arithmetic and copies ran while one was open for 17% -> 15% of each run, Pallas kernels for 22% -> 19%
where the time goes in v6:
time: 1030 us; the launch traced here: 1020 us
  waiting for transfers between devices  479 us (47%)
  Pallas kernels  229 us (22%)
  matrix products  110 us (11%)
  other arithmetic  73.9 us (7%)
  starting transfers between devices  71.9 us (7%)
  local copies, waits for them, and re-layouts  40.5 us (4%)
  between operations  15.6 us (2%)
    ppermute x43, waiting for transfers between devices, ctx_swap(): return lax.ppermute(x, 'ctx', [(i, i ^ mask) for i in range(n)])  214 us
    pallas_call x4, Pallas kernels, attention_call(): pl.pallas_call(kernel, grid_spec=pltpu.PrefetchScalarGridSpec(num_scalar_...  164 us
    all_gather x4, waiting for transfers between devices, all_rows(): return lax.all_gather(x, 'tp', axis=0, tiled=True)  104 us
    reduce_scatter x3, waiting for transfers between devices, sum_rows(): return lax.psum_scatter(x, 'tp', scatter_dimension=0, tiled=True)  74.7 us
    ppermute x43, starting transfers between devices, ctx_swap(): return lax.ppermute(x, 'ctx', [(i, i ^ mask) for i in range(n)])  53.6 us
    dot_general x6, matrix products, nt(): lax.dot_general(a, b, (((1,), (1,)), ((), ())), preferred_element_type=jn...  49.3 us
    dot_general x6, matrix products, rc(): lax.dot_general(left, right, (((0,), (0,)), ((), ())), preferred_element_...  41.4 us
    ppermute x6, waiting for transfers between devices, tp_shift(): return lax.ppermute(x, 'tp', [(i, (i + d) % n) for i in range(n)])  30.1 us
  transfers between devices with their start and end apart: 67, of which 42 were waited for; matrix products, arithmetic and copies ran while one was open for 15% of the time, Pallas kernels for 19%

profile of v6, /device:TPU:0, one launch (start us, length us, event | category | flops | bytes accessed | tf_op | source)
XLA Modules:
  0.0 1019.6 jit_solution(2567610458409209016)
XLA Ops:
  12.7 83.6 %all-gather.7.cloned.1.call-done.h_ref = bf16[1024,2048]{1,0:T(8,128)(2,1)} async-done(((bf16[256,2048]{1,0:T(8,128)(2,1)}), bf16[1024,2048]{1,0:T(8,128)(2,1)}) %all-gather.7.cloned.1.call-update) | async-done | bytes 4194320 | tf_op jit(solution)/shard_map/all_gather | solution.py:522
  98.6 11.6 %project.1 = (bf16[4,256,512]{2,1,0:T(8,128)(2,1)S(1)}, bf16[2,4,256,512]{3,2,1,0:T(8,128)(2,1)}) custom-call(bf16[1024,2048]{1,0:T(8,128)(2,1)} %all-gather.7.cloned.1.call-done.h_ref, bf16[2048,512]{1,0:T(8,128)(2,1)} %wq_ref.1, bf16[2048,512]{1,0:T(8,128)(2,1)} %wk_ref.1, bf16[2048,512]{1,0:T(8,128)(2,1)} %wv_ref.1, ...), custom_call_target="tpu_custom_call" | custom-call | flops 6442450944 | bytes 6291456 | tf_op jit(solution)/shard_map/project/pallas_call | solution.py:345
  114.2 44.7 %collective-permute-done.3.refs_4_.refs_12_ = bf16[2,4,2,128,512]{4,3,2,1,0:T(8,128)(2,1)} collective-permute-done((bf16[2,4,2,128,512]{4,3,2,1,0:T(8,128)(2,1)}, bf16[2,4,2,128,512]{4,3,2,1,0:T(8,128)(2,1)}, u32[]{:S(2)}, u32[]{:S(2)}) %collective-permute-start.3) | collective-permute-done | bytes 2097184 | tf_op jit(solution)/shard_map/ppermute | solution.py:401
  169.4 10.1 collective-permute-done.14
  179.5 19.8 %collective-permute-done.13 = bf16[64,2048]{1,0:T(8,128)(2,1)S(1)} collective-permute-done((bf16[64,2048]{1,0:T(8,128)(2,1)S(1)}, bf16[64,2048]{1,0:T(8,128)(2,1)S(1)}, u32[]{:S(2)}, u32[]{:S(2)}) %collective-permute-start.13) | collective-permute-done | bytes 262176 | tf_op jit(solution)/shard_map/ppermute | solution.py:606
  205.5 3.8 collective-permute-done.8.refs_15_
  210.5 50.1 %attend.1 = (bf16[4,256,512]{2,1,0:T(8,128)(2,1)S(1)}, bf16[4,256,128]{2,1,0:T(8,128)(2,1)S(1)}) custom-call(s32[4,16]{1,0:T(4,128)S(1)} %copy.42.place_ref, s32[4,2]{1,0:T(4,128)S(1)} %get-tuple-element.187.own_ref, bf16[4,256,512]{2,1,0:T(8,128)(2,1)S(1)} %copy-done.16, bf16[2,4,2,128,512]{4,3,2,1,0:T(8,128)(2,1)} %bitcast.5.refs_0_.refs_8_, ...), custom_call_target="tpu_custom_call" | custom-call | flops 8589934592 | bytes 16777216 | tf_op jit(solution)/shard_map/attend/pallas_call | solution.py:222
  263.6 3.8 collective-permute-start.11
  267.4 7.6 collective-permute-done.9
  276.7 6.8 collective-permute-done.10
  284.9 6.1 fusion.68
  296.4 3.2 collective-permute-start.18
  301.0 25.9 %collective-permute-done.20.refs_6_.refs_22_ = bf16[1,4,2,128,640]{4,3,2,1,0:T(8,128)(2,1)S(1)} collective-permute-done((bf16[1,4,2,128,640]{4,3,2,1,0:T(8,128)(2,1)S(1)}, bf16[1,4,2,128,640]{4,3,2,1,0:T(8,128)(2,1)S(1)}, u32[]{:S(2)}, u32[]{:S(2)}) %collective-permute-start.20) | collective-permute-done | bytes 1310752 | tf_op jit(solution)/shard_map/ppermute | solution.py:401
  326.9 27.0 %collective-permute-done.18.refs_4_.refs_20_ = bf16[1,4,2,128,640]{4,3,2,1,0:T(8,128)(2,1)} collective-permute-done((bf16[1,4,2,128,640]{4,3,2,1,0:T(8,128)(2,1)S(1)}, bf16[1,4,2,128,640]{4,3,2,1,0:T(8,128)(2,1)}, u32[]{:S(2)}, u32[]{:S(2)}) %collective-permute-start.18) | collective-permute-done | bytes 1310752 | tf_op jit(solution)/shard_map/ppermute | solution.py:401
  359.3 20.3 %all-gather.11.cloned.1.call-done.h_ref = bf16[1024,2048]{1,0:T(8,128)(2,1)} async-done(((bf16[256,2048]{1,0:T(8,128)(2,1)}), bf16[1024,2048]{1,0:T(8,128)(2,1)}) %all-gather.11.cloned.1.call-update) | async-done | bytes 4194320 | tf_op jit(solution)/shard_map/all_gather | solution.py:522
  379.6 28.4 %mlp.1 = (bf16[1024,1408]{1,0:T(8,128)(2,1)}, bf16[1024,2816]{1,0:T(8,128)(2,1)}) custom-call(bf16[1024,2048]{1,0:T(8,128)(2,1)} %all-gather.11.cloned.1.call-done.h_ref, bf16[1024,2048]{1,0:T(8,128)(2,1)} %all-gather.9.cloned.1.call-done.dy_ref, bf16[2048,1408]{1,0:T(8,128)(2,1)} %gate_ref.1, bf16[2048,1408]{1,0:T(8,128)(2,1)} %up_ref.1, ...), custom_call_target="tpu_custom_call" | custom-call | flops 17716740096 | bytes 38273024 | tf_op jit(solution)/shard_map/mlp/pallas_call | solution.py:385
  408.1 9.8 fusion.4
  417.8 11.1 %add_convert_fusion.1 = bf16[1024,2048]{1,0:T(8,128)(2,1)} fusion(f32[1024,2048]{1,0:T(8,128)S(1)} %fusion.4, bf16[2048,1408]{1,0:T(8,128)(2,1)} %up_ref.1, bf16[1024,2816]{1,0:T(8,128)(2,1)S(1)} %copy-done.69), kind=kOutput, calls=%fused_computation.3 | convolution fusion | flops 5909774336 | bytes 21233664 | tf_op jit(solution)/shard_map/dot_general | solution.py:15
  428.9 11.0 %convolution_convert_fusion.1 = bf16[1024,2816]{1,0:T(8,128)(2,1)} fusion(bf16[1024,2816]{1,0:T(8,128)(2,1)} %get-tuple-element.110, bf16[1024,2048]{1,0:T(8,128)(2,1)} %all-gather.11.cloned.1.call-done.h_ref, s32[]{:T(128)S(6)} %select_n.328), kind=kOutput, calls=%fused_computation.8 | convolution fusion | flops 5908463616 | bytes 13631492 | tf_op jit(solution)/shard_map/dot_general | solution.py:290
  440.0 9.7 collective-permute-done.22
  449.6 10.7 %add_convert_fusion = bf16[1024,2816]{1,0:T(8,128)(2,1)S(1)} fusion(bf16[1024,2816]{1,0:T(8,128)(2,1)} %collective-permute-done.22, bf16[1024,2816]{1,0:T(8,128)(2,1)} %get-tuple-element.110, bf16[1024,2048]{1,0:T(8,128)(2,1)} %all-gather.11.cloned.1.call-done.h_ref, s32[]{:T(128)S(6)} %select_n.327), kind=kOutput, calls=%fused_computation | convolution fusion | flops 5914230784 | bytes 19398660 | tf_op jit(solution)/shard_map/dot_general | solution.py:290
  466.2 10.8 %convolution_convert_fusion.2 = bf16[1024,2048]{1,0:T(8,128)(2,1)} fusion(bf16[1024,1408]{1,0:T(8,128)(2,1)S(1)} %copy-done.70, bf16[1408,2048]{1,0:T(8,128)(2,1)} %down_ref.1), kind=kOutput, calls=%fused_computation.9 | convolution fusion | flops 5907677184 | bytes 12845056 | tf_op jit(solution)/shard_map/dot_general | solution.py:19
  477.0 19.0 %collective-permute-done.23 = bf16[256,2816]{1,0:T(8,128)(2,1)} collective-permute-done((bf16[256,2816]{1,0:T(8,128)(2,1)}, bf16[256,2816]{1,0:T(8,128)(2,1)}, u32[]{:S(2)}, u32[]{:S(2)}) %collective-permute-start.23) | collective-permute-done | bytes 1441824 | tf_op jit(solution)/shard_map/ppermute | solution.py:401
  507.9 8.2 convolution_convert_fusion
  516.2 2.7 collective-permute-done.25
  521.0 3.0 collective-permute-done.26
  526.3 3.0 fusion.23
  529.4 3.9 fusion.63
  533.3 6.1 convolution_convert_fusion.5
  543.4 7.2 collective-permute-done.27
  550.7 8.5 collective-permute-done.28
  561.8 14.1 %collective-permute-done.30 = bf16[128,2816]{1,0:T(8,128)(2,1)} collective-permute-done((bf16[128,2816]{1,0:T(8,128)(2,1)}, bf16[128,2816]{1,0:T(8,128)(2,1)}, u32[]{:S(2)}, u32[]{:S(2)}) %collective-permute-start.30) | collective-permute-done | bytes 720928 | tf_op jit(solution)/shard_map/ppermute | solution.py:401
  580.2 2.9 maximum_select_fusion.4
  583.2 2.9 maximum_select_fusion.5
  586.1 2.8 collective-permute-start.37
  589.6 49.9 %query_grad.1 = bf16[4,256,512]{2,1,0:T(8,128)(2,1)S(1)} custom-call(s32[4,16]{1,0:T(4,128)S(1)} %copy.42.place_ref, s32[4,2]{1,0:T(4,128)S(1)} %get-tuple-element.187.own_ref, bf16[4,256,512]{2,1,0:T(8,128)(2,1)S(1)} %copy-done.17, bf16[4,256,512]{2,1,0:T(8,128)(2,1)S(1)} %bitcast.83, bf16[4,256,128]{2,1,0:T(8,128)(2,1)S(1)} %get-tuple-element.103.qx_ref, ...), custom_call_target="tpu_custom_call" | custom-call | flops 12884901888 | bytes 16777216 | tf_op jit(solution)/shard_map/query_grad/pallas_call | solution.py:222
  639.6 5.8 fusion.70
  652.3 10.5 %collective-permute-start.39 = (bf16[256,2816]{1,0:T(8,128)(2,1)}, bf16[256,2816]{1,0:T(8,128)(2,1)}, u32[]{:S(2)}, u32[]{:S(2)}) collective-permute-start(bf16[256,2816]{1,0:T(8,128)(2,1)} %maximum_select_fusion.4), channel_id=1, source_target_pairs={{0,8},{4,12},{8,0},{12,4},{16,24},{20,28},{24,16},{28,20},{1,9},{5... | collective-permute-start | bytes 4325384 | tf_op jit(solution)/shard_map/ppermute | solution.py:401
  666.3 32.0 %key_value_grad.2 = (bf16[2,256,512]{2,1,0:T(8,128)(2,1)S(1)}, bf16[2,256,512]{2,1,0:T(8,128)(2,1)S(1)}) custom-call(s32[4,16]{1,0:T(4,128)S(1)} %copy.42.place_ref, s32[4,2]{1,0:T(4,128)S(1)} %get-tuple-element.187.own_ref, bf16[2,4,256,512]{3,2,1,0:T(8,128)(2,1)} %get-tuple-element.97.k_ref.v_ref, bf16[2,4,256,512]{3,2,1,0:T(8,128)(2,1)} %get-tuple-element.97.k_ref.v_ref, ...), custom_call_target="tpu_custom_call" | custom-call | flops 8589934592 | bytes 8388608 | tf_op jit(solution)/shard_map/key_value_grad/pallas_call | solution.py:222
  698.4 15.1 %collective-permute-done.39 = bf16[256,2816]{1,0:T(8,128)(2,1)} collective-permute-done((bf16[256,2816]{1,0:T(8,128)(2,1)}, bf16[256,2816]{1,0:T(8,128)(2,1)}, u32[]{:S(2)}, u32[]{:S(2)}) %collective-permute-start.39) | collective-permute-done | bytes 1441824 | tf_op jit(solution)/shard_map/ppermute | solution.py:401
  713.7 3.0 maximum_select_fusion
  716.8 3.2 maximum_select_fusion.1
  720.0 3.0 pad_maximum_fusion.half_ref
  723.1 31.8 %key_value_grad.3 = (bf16[2,256,512]{2,1,0:T(8,128)(2,1)S(1)}, bf16[2,256,512]{2,1,0:T(8,128)(2,1)S(1)}) custom-call(s32[4,16]{1,0:T(4,128)S(1)} %copy.42.place_ref, s32[4,2]{1,0:T(4,128)S(1)} %get-tuple-element.187.own_ref, bf16[2,4,256,512]{3,2,1,0:T(8,128)(2,1)} %get-tuple-element.97.k_ref.v_ref, bf16[2,4,256,512]{3,2,1,0:T(8,128)(2,1)} %get-tuple-element.97.k_ref.v_ref, ...), custom_call_target="tpu_custom_call" | custom-call | flops 8589934592 | bytes 8388608 | tf_op jit(solution)/shard_map/key_value_grad/pallas_call | solution.py:222
  756.5 5.8 fusion.71
  762.3 10.9 %fusion.69 = (bf16[1024,2048]{1,0:T(8,128)(2,1)}, f32[1024,2048]{1,0:T(8,128)}) fusion(f32[1024,2048]{1,0:T(8,128)} %fusion.71, f32[1024,2048]{1,0:T(8,128)S(1)} %bitcast.93, bf16[1024,512]{1,0:T(8,128)(2,1)S(1)} %bitcast.90, bf16[2048,512]{1,0:T(8,128)(2,1)S(1)} %copy-done.48), kind=kOutput, calls=%fused_computation.188 | convolution fusion | flops 2153775104 | bytes 32505856 | tf_op jit(solution)/shard_map/dot_general | solution.py:15
  773.4 2.7 copy-done.44
  776.1 3.7 convolution_convert_fusion.3
  780.5 8.9 collective-permute-done.41
  789.3 4.0 add_convert_fusion.2
  795.9 3.8 convolution_convert_fusion.4
  802.8 5.6 fusion.62
  809.4 11.3 %collective-permute-start.47 = (bf16[256,1536]{1,0:T(8,128)(2,1)}, bf16[256,1536]{1,0:T(8,128)(2,1)}, u32[]{:S(2)}, u32[]{:S(2)}) collective-permute-start(bf16[256,1536]{1,0:T(8,128)(2,1)} %constant_dynamic-slice_fusion.2), channel_id=1, source_target_pairs={{0,8},{4,12},{8,0},{12,4},{16,24},{20,28},{24,16},{28,20},{1,9},{5... | collective-permute-start | bytes 2359304 | tf_op jit(solution)/shard_map/ppermute | solution.py:401
  823.1 15.2 %unpack_rows.2 = (f32[2048,1408]{1,0:T(8,128)}, f32[2048,1408]{1,0:T(8,128)}) custom-call(s32[1]{0:T(128)} %bitcast.19.core_ref, bf16[1024,2816]{1,0:T(8,128)(2,1)} %pad_maximum_fusion.half_ref, bf16[1024,2816]{1,0:T(8,128)(2,1)} %collective-permute-done.49.other_ref), custom_call_target="tpu_custom_call" | custom-call | bytes 34603008 | tf_op jit(solution)/shard_map/unpack_rows/pallas_call | solution.py:503
  846.3 9.4 collective-permute-done.43
  857.2 3.9 collective-permute-done.44
  864.7 3.1 collective-permute-done.45
  867.8 6.0 convert_element_type.246
  877.3 21.1 %collective-permute-done.55 = bf16[256,1536]{1,0:T(8,128)(2,1)S(1)} collective-permute-done((bf16[256,1536]{1,0:T(8,128)(2,1)S(1)}, bf16[256,1536]{1,0:T(8,128)(2,1)S(1)}, u32[]{:S(2)}, u32[]{:S(2)}) %collective-permute-start.55) | collective-permute-done | bytes 786464 | tf_op jit(solution)/shard_map/ppermute | solution.py:401
  912.8 6.2 all-reduce.6.cloned.1.call-done
  919.0 4.1 convert_element_type.248
  923.1 74.7 %reduce-scatter.8.cloned.1.call-done = bf16[256,2048]{1,0:T(8,128)(2,1)} async-done(((bf16[1024,2048]{1,0:T(8,128)(2,1)}), bf16[256,2048]{1,0:T(8,128)(2,1)}) %reduce-scatter.8.cloned.1.call-update) | async-done | bytes 1048592 | tf_op jit(solution)/shard_map/reduce_scatter | solution.py:550
  999.9 3.2 fusion.17
  1003.1 9.4 unpack_rows.3
  (373 shorter events, 136.4 us)
Async XLA Ops:
  7.2 89.0 %all-gather.7.cloned.1.call-start = ((), (), s32[]{:S(2)}) async-start(), calls=%async_computation.3 | async-start | bytes 5242880 | tf_op jit(solution)/shard_map/all_gather | solution.py:522
  12.6 197.1 %all-gather.9.cloned.1.call-start = ((), (), s32[]{:S(2)}) async-start(), calls=%async_computation.4 | async-start | bytes 5242880 | tf_op jit(solution)/shard_map/all_gather | solution.py:522
  96.3 188.6 %all-gather.15.cloned.1.call-start = ((), (), s32[]{:S(2)}) async-start(), calls=%async_computation.12 | async-start | bytes 9437184 | tf_op jit(solution)/shard_map/all_gather | solution.py:637
  111.2 47.7 %collective-permute-start.3 = (bf16[2,4,2,128,512]{4,3,2,1,0:T(8,128)(2,1)}, bf16[2,4,2,128,512]{4,3,2,1,0:T(8,128)(2,1)}, u32[]{:S(2)}, u32[]{:S(2)}) collective-permute-start(bf16[2,4,2,128,512]{4,3,2,1,0:T(8,128)(2,1)} %bitcast.5.refs_0_.refs_8_), channel_id=1, source_target_pairs={{0,16},{4,20},{8,24},{12,28},{16,0},{20,4},{24,8},{28,12},{1,17},{... | collective-permute-start | bytes 6291464 | tf_op jit(solution)/shard_map/ppermute | solution.py:401
  112.7 49.9 %collective-permute-start.1 = (bf16[2,4,2,128,512]{4,3,2,1,0:T(8,128)(2,1)}, bf16[2,4,2,128,512]{4,3,2,1,0:T(8,128)(2,1)}, u32[]{:S(2)}, u32[]{:S(2)}) collective-permute-start(bf16[2,4,2,128,512]{4,3,2,1,0:T(8,128)(2,1)} %bitcast.5.refs_0_.refs_8_), channel_id=1, source_target_pairs={{0,8},{4,12},{8,0},{12,4},{16,24},{20,28},{24,16},{28,20},{1,9},{5... | collective-permute-start | bytes 6291464 | tf_op jit(solution)/shard_map/ppermute | solution.py:401
  161.2 40.6 %collective-permute-start.7 = (bf16[1,4,2,128,512]{4,3,2,1,0:T(8,128)(2,1)}, bf16[1,4,2,128,512]{4,3,2,1,0:T(8,128)(2,1)}, u32[]{:S(2)}, u32[]{:S(2)}) collective-permute-start(bf16[1,4,2,128,512]{4,3,2,1,0:T(8,128)(2,1)} %slice.88), channel_id=1, source_target_pairs={{0,8},{4,12},{8,0},{12,4},{16,24},{20,28},{24,16},{28,20},{1,9},{5... | collective-permute-start | bytes 3145736 | tf_op jit(solution)/shard_map/ppermute | solution.py:401
  164.9 37.4 %collective-permute-start.5 = (bf16[1,4,2,128,512]{4,3,2,1,0:T(8,128)(2,1)}, bf16[1,4,2,128,512]{4,3,2,1,0:T(8,128)(2,1)}, u32[]{:S(2)}, u32[]{:S(2)}) collective-permute-start(bf16[1,4,2,128,512]{4,3,2,1,0:T(8,128)(2,1)} %slice.87), channel_id=1, source_target_pairs={{0,16},{4,20},{8,24},{12,28},{16,0},{20,4},{24,8},{28,12},{1,17},{... | collective-permute-start | bytes 3145736 | tf_op jit(solution)/shard_map/ppermute | solution.py:401
  166.4 13.1 %collective-permute-start.14 = (bf16[64,2048]{1,0:T(8,128)(2,1)S(1)}, bf16[64,2048]{1,0:T(8,128)(2,1)S(1)}, u32[]{:S(2)}, u32[]{:S(2)}) collective-permute-start(bf16[64,2048]{1,0:T(8,128)(2,1)S(1)} %constant_dynamic-slice_fusion.10), channel_id=1, source_target_pairs={{0,3},{1,0},{2,1},{3,2},{4,7},{5,4},{6,5},{7,6},{8,11},{9,8},{10,9... | collective-permute-start | bytes 786440 | tf_op jit(solution)/shard_map/ppermute | solution.py:606
  167.5 31.8 %collective-permute-start.13 = (bf16[64,2048]{1,0:T(8,128)(2,1)S(1)}, bf16[64,2048]{1,0:T(8,128)(2,1)S(1)}, u32[]{:S(2)}, u32[]{:S(2)}) collective-permute-start(bf16[64,2048]{1,0:T(8,128)(2,1)S(1)} %constant_dynamic-slice_fusion.10), channel_id=1, source_target_pairs={{0,2},{1,3},{2,0},{3,1},{4,6},{5,7},{6,4},{7,5},{8,10},{9,11},{10,... | collective-permute-start | bytes 786440 | tf_op jit(solution)/shard_map/ppermute | solution.py:606
  167.5 31.8 %collective-permute-start.12 = (bf16[64,2048]{1,0:T(8,128)(2,1)S(1)}, bf16[64,2048]{1,0:T(8,128)(2,1)S(1)}, u32[]{:S(2)}, u32[]{:S(2)}) collective-permute-start(bf16[64,2048]{1,0:T(8,128)(2,1)S(1)} %constant_dynamic-slice_fusion.10), channel_id=1, source_target_pairs={{0,1},{1,2},{2,3},{3,0},{4,5},{5,6},{6,7},{7,4},{8,9},{9,10},{10,1... | collective-permute-start | bytes 786440 | tf_op jit(solution)/shard_map/ppermute | solution.py:606
  179.5 26.0 %collective-permute-start = (bf16[2,4,2,128,512]{4,3,2,1,0:T(8,128)(2,1)}, bf16[2,4,2,128,512]{4,3,2,1,0:T(8,128)(2,1)}, u32[]{:S(2)}, u32[]{:S(2)}) collective-permute-start(bf16[2,4,2,128,512]{4,3,2,1,0:T(8,128)(2,1)} %bitcast.5.refs_0_.refs_8_), channel_id=1, source_target_pairs={{0,4},{4,0},{8,12},{12,8},{16,20},{20,16},{24,28},{28,24},{1,5},{5... | collective-permute-start | bytes 6291464 | tf_op jit(solution)/shard_map/ppermute | solution.py:401
  199.2 10.5 %collective-permute-start.4 = (bf16[2,4,2,128,512]{4,3,2,1,0:T(8,128)(2,1)}, bf16[2,4,2,128,512]{4,3,2,1,0:T(8,128)(2,1)}, u32[]{:S(2)}, u32[]{:S(2)}) collective-permute-start(bf16[2,4,2,128,512]{4,3,2,1,0:T(8,128)(2,1)} %collective-permute-done.3.refs_4_.refs_12_), channel_id=1, source_target_pairs={{0,4},{4,0},{8,12},{12,8},{16,20},{20,16},{24,28},{28,24},{1,5},{5... | collective-permute-start | bytes 6291464 | tf_op jit(solution)/shard_map/ppermute | solution.py:401
  199.2 10.5 %collective-permute-start.2 = (bf16[2,4,2,128,512]{4,3,2,1,0:T(8,128)(2,1)}, bf16[2,4,2,128,512]{4,3,2,1,0:T(8,128)(2,1)}, u32[]{:S(2)}, u32[]{:S(2)}) collective-permute-start(bf16[2,4,2,128,512]{4,3,2,1,0:T(8,128)(2,1)} %collective-permute-done.1.refs_2_.refs_10_), channel_id=1, source_target_pairs={{0,4},{4,0},{8,12},{12,8},{16,20},{20,16},{24,28},{28,24},{1,5},{5... | collective-permute-start | bytes 6291464 | tf_op jit(solution)/shard_map/ppermute | solution.py:401
  201.8 7.5 collective-permute-start.8
  202.3 7.5 collective-permute-start.6
  209.8 169.8 %all-gather.11.cloned.1.call-start = ((), (), s32[]{:S(2)}) async-start(), calls=%async_computation.5 | async-start | bytes 5242880 | tf_op jit(solution)/shard_map/all_gather | solution.py:522
  263.6 11.5 %collective-permute-start.9 = (bf16[256,512]{1,0:T(8,128)(2,1)}, bf16[256,512]{1,0:T(8,128)(2,1)}, u32[]{:S(2)}, u32[]{:S(2)}) collective-permute-start(bf16[256,512]{1,0:T(8,128)(2,1)} %get-tuple-element.198), channel_id=1, source_target_pairs={{0,1},{1,2},{2,3},{3,0},{4,5},{5,6},{6,7},{7,4},{8,9},{9,10},{10,1... | collective-permute-start | bytes 786440 | tf_op jit(solution)/shard_map/ppermute | solution.py:527
  263.6 19.9 %collective-permute-start.10 = (bf16[256,512]{1,0:T(8,128)(2,1)}, bf16[256,512]{1,0:T(8,128)(2,1)S(1)}, u32[]{:S(2)}, u32[]{:S(2)}) collective-permute-start(bf16[256,512]{1,0:T(8,128)(2,1)} %get-tuple-element.197), channel_id=1, source_target_pairs={{0,2},{1,3},{2,0},{3,1},{4,6},{5,7},{6,4},{7,5},{8,10},{9,11},{10,... | collective-permute-start | bytes 786440 | tf_op jit(solution)/shard_map/ppermute | solution.py:527
  263.6 20.6 %collective-permute-start.11 = (bf16[256,512]{1,0:T(8,128)(2,1)}, bf16[256,512]{1,0:T(8,128)(2,1)S(1)}, u32[]{:S(2)}, u32[]{:S(2)}) collective-permute-start(bf16[256,512]{1,0:T(8,128)(2,1)} %get-tuple-element.196), channel_id=1, source_target_pairs={{0,3},{1,0},{2,1},{3,2},{4,7},{5,4},{6,5},{7,6},{8,11},{9,8},{10,9... | collective-permute-start | bytes 786440 | tf_op jit(solution)/shard_map/ppermute | solution.py:527
  293.8 232.5 %reduce-scatter.4.cloned.1.call-start = ((), (), s32[]{:S(2)}) async-start(), calls=%async_computation.6 | async-start | bytes 5242880 | tf_op jit(solution)/shard_map/reduce_scatter | solution.py:550
  294.2 32.7 %collective-permute-start.20 = (bf16[1,4,2,128,640]{4,3,2,1,0:T(8,128)(2,1)S(1)}, bf16[1,4,2,128,640]{4,3,2,1,0:T(8,128)(2,1)S(1)}, u32[]{:S(2)}, u32[]{:S(2)}) collective-permute-start(bf16[1,4,2,128,640]{4,3,2,1,0:T(8,128)(2,1)S(1)} %bitcast.67), channel_id=1, source_target_pairs={{0,24},{4,28},{8,16},{12,20},{16,8},{20,12},{24,0},{28,4},{1,25},{... | collective-permute-start | bytes 3932168 | tf_op jit(solution)/shard_map/ppermute | solution.py:401
  296.4 57.5 %collective-permute-start.18 = (bf16[1,4,2,128,640]{4,3,2,1,0:T(8,128)(2,1)S(1)}, bf16[1,4,2,128,640]{4,3,2,1,0:T(8,128)(2,1)}, u32[]{:S(2)}, u32[]{:S(2)}) collective-permute-start(bf16[1,4,2,128,640]{4,3,2,1,0:T(8,128)(2,1)S(1)} %bitcast.68), channel_id=1, source_target_pairs={{0,16},{4,20},{8,24},{12,28},{16,0},{20,4},{24,8},{28,12},{1,17},{... | collective-permute-start | bytes 3932168 | tf_op jit(solution)/shard_map/ppermute | solution.py:401
  299.6 56.3 %collective-permute-start.16 = (bf16[1,4,2,128,640]{4,3,2,1,0:T(8,128)(2,1)S(1)}, bf16[1,4,2,128,640]{4,3,2,1,0:T(8,128)(2,1)}, u32[]{:S(2)}, u32[]{:S(2)}) collective-permute-start(bf16[1,4,2,128,640]{4,3,2,1,0:T(8,128)(2,1)S(1)} %bitcast.69), channel_id=1, source_target_pairs={{0,8},{4,12},{8,0},{12,4},{16,24},{20,28},{24,16},{28,20},{1,9},{5... | collective-permute-start | bytes 3932168 | tf_op jit(solution)/shard_map/ppermute | solution.py:401
  301.0 54.9 %collective-permute-start.15 = (bf16[1,4,2,128,640]{4,3,2,1,0:T(8,128)(2,1)S(1)}, bf16[1,4,2,128,640]{4,3,2,1,0:T(8,128)(2,1)}, u32[]{:S(2)}, u32[]{:S(2)}) collective-permute-start(bf16[1,4,2,128,640]{4,3,2,1,0:T(8,128)(2,1)S(1)} %bitcast.70), channel_id=1, source_target_pairs={{0,4},{4,0},{8,12},{12,8},{16,20},{20,16},{24,28},{28,24},{1,5},{5... | collective-permute-start | bytes 3932168 | tf_op jit(solution)/shard_map/ppermute | solution.py:401
  326.9 29.0 %collective-permute-start.21 = (bf16[1,4,2,128,640]{4,3,2,1,0:T(8,128)(2,1)S(1)}, bf16[1,4,2,128,640]{4,3,2,1,0:T(8,128)(2,1)}, u32[]{:S(2)}, u32[]{:S(2)}) collective-permute-start(bf16[1,4,2,128,640]{4,3,2,1,0:T(8,128)(2,1)S(1)} %collective-permute-done.20.refs_6_.refs_22_), channel_id=1, source_target_pairs={{0,4},{4,0},{8,12},{12,8},{16,20},{20,16},{24,28},{28,24},{1,5},{5... | collective-permute-start | bytes 3932168 | tf_op jit(solution)/shard_map/ppermute | solution.py:401
  353.9 3.4 collective-permute-start.19
  439.9 9.8 collective-permute-start.22
  439.9 333.3 %all-gather.13.cloned.1.call-start = ((), (), s32[]{:S(2)}) async-start(), calls=%async_computation.9 | async-start | bytes 5242880 | tf_op jit(solution)/shard_map/all_gather | solution.py:522
  462.0 34.0 %collective-permute-start.23 = (bf16[256,2816]{1,0:T(8,128)(2,1)}, bf16[256,2816]{1,0:T(8,128)(2,1)}, u32[]{:S(2)}, u32[]{:S(2)}) collective-permute-start(bf16[256,2816]{1,0:T(8,128)(2,1)} %constant_dynamic-slice_fusion.9), channel_id=1, source_target_pairs={{0,8},{4,12},{8,0},{12,4},{16,24},{20,28},{24,16},{28,20},{1,9},{5... | collective-permute-start | bytes 4325384 | tf_op jit(solution)/shard_map/ppermute | solution.py:401
  464.7 33.7 %collective-permute-start.24 = (bf16[256,2816]{1,0:T(8,128)(2,1)}, bf16[256,2816]{1,0:T(8,128)(2,1)}, u32[]{:S(2)}, u32[]{:S(2)}) collective-permute-start(bf16[256,2816]{1,0:T(8,128)(2,1)} %constant_dynamic-slice_fusion.8), channel_id=1, source_target_pairs={{0,16},{4,20},{8,24},{12,28},{16,0},{20,4},{24,8},{28,12},{1,17},{... | collective-permute-start | bytes 4325384 | tf_op jit(solution)/shard_map/ppermute | solution.py:401
  501.5 17.3 %collective-permute-start.25 = (bf16[128,2816]{1,0:T(8,128)(2,1)}, bf16[128,2816]{1,0:T(8,128)(2,1)S(1)}, u32[]{:S(2)}, u32[]{:S(2)}) collective-permute-start(bf16[128,2816]{1,0:T(8,128)(2,1)} %constant_dynamic-slice_fusion.7), channel_id=1, source_target_pairs={{0,16},{4,20},{8,24},{12,28},{16,0},{20,4},{24,8},{28,12},{1,17},{... | collective-permute-start | bytes 2162696 | tf_op jit(solution)/shard_map/ppermute | solution.py:401
  506.6 17.4 %collective-permute-start.26 = (bf16[128,2816]{1,0:T(8,128)(2,1)}, bf16[128,2816]{1,0:T(8,128)(2,1)}, u32[]{:S(2)}, u32[]{:S(2)}) collective-permute-start(bf16[128,2816]{1,0:T(8,128)(2,1)} %constant_dynamic-slice_fusion.6), channel_id=1, source_target_pairs={{0,8},{4,12},{8,0},{12,4},{16,24},{20,28},{24,16},{28,20},{1,9},{5... | collective-permute-start | bytes 2162696 | tf_op jit(solution)/shard_map/ppermute | solution.py:401
  539.6 11.1 %collective-permute-start.27 = (bf16[256,512]{1,0:T(8,128)(2,1)S(1)}, bf16[256,512]{1,0:T(8,128)(2,1)S(1)}, u32[]{:S(2)}, u32[]{:S(2)}) collective-permute-start(bf16[256,512]{1,0:T(8,128)(2,1)S(1)} %get-tuple-element.194), channel_id=1, source_target_pairs={{0,1},{1,2},{2,3},{3,0},{4,5},{5,6},{6,7},{7,4},{8,9},{9,10},{10,1... | collective-permute-start | bytes 786440 | tf_op jit(solution)/shard_map/ppermute | solution.py:527
  539.6 19.5 %collective-permute-start.28 = (bf16[256,512]{1,0:T(8,128)(2,1)S(1)}, bf16[256,512]{1,0:T(8,128)(2,1)S(1)}, u32[]{:S(2)}, u32[]{:S(2)}) collective-permute-start(bf16[256,512]{1,0:T(8,128)(2,1)S(1)} %get-tuple-element.193), channel_id=1, source_target_pairs={{0,2},{1,3},{2,0},{3,1},{4,6},{5,7},{6,4},{7,5},{8,10},{9,11},{10,... | collective-permute-start | bytes 786440 | tf_op jit(solution)/shard_map/ppermute | solution.py:527
  540.8 18.4 %collective-permute-start.29 = (bf16[256,512]{1,0:T(8,128)(2,1)S(1)}, bf16[256,512]{1,0:T(8,128)(2,1)S(1)}, u32[]{:S(2)}, u32[]{:S(2)}) collective-permute-start(bf16[256,512]{1,0:T(8,128)(2,1)S(1)} %get-tuple-element.192), channel_id=1, source_target_pairs={{0,3},{1,0},{2,1},{3,2},{4,7},{5,4},{6,5},{7,6},{8,11},{9,8},{10,9... | collective-permute-start | bytes 786440 | tf_op jit(solution)/shard_map/ppermute | solution.py:527
  559.3 240.4 %all-reduce.4.cloned.1.call-start = ((), (), s32[]{:S(2)}) async-start(), calls=%async_computation.10 | async-start | bytes 11534336 | tf_op jit(solution)/shard_map/psum | solution.py:662
  559.3 16.6 %collective-permute-start.30 = (bf16[128,2816]{1,0:T(8,128)(2,1)}, bf16[128,2816]{1,0:T(8,128)(2,1)}, u32[]{:S(2)}, u32[]{:S(2)}) collective-permute-start(bf16[128,2816]{1,0:T(8,128)(2,1)} %add_convert_fusion.10), channel_id=1, source_target_pairs={{0,16},{4,20},{8,24},{12,28},{16,0},{20,4},{24,8},{28,12},{1,17},{... | collective-permute-start | bytes 2162696 | tf_op jit(solution)/shard_map/ppermute | solution.py:401
  559.8 16.4 %collective-permute-start.31 = (bf16[128,2816]{1,0:T(8,128)(2,1)}, bf16[128,2816]{1,0:T(8,128)(2,1)}, u32[]{:S(2)}, u32[]{:S(2)}) collective-permute-start(bf16[128,2816]{1,0:T(8,128)(2,1)} %add_convert_fusion.9), channel_id=1, source_target_pairs={{0,8},{4,12},{8,0},{12,4},{16,24},{20,28},{24,16},{28,20},{1,9},{5... | collective-permute-start | bytes 2162696 | tf_op jit(solution)/shard_map/ppermute | solution.py:401
  561.8 342.9 %reduce-scatter.6.cloned.1.call-start = ((), (), s32[]{:S(2)}) async-start(), calls=%async_computation.7 | async-start | bytes 5242880 | tf_op jit(solution)/shard_map/reduce_scatter | solution.py:550
  586.1 59.3 %collective-permute-start.37 = (bf16[1,4,2,128,640]{4,3,2,1,0:T(8,128)(2,1)S(1)}, bf16[1,4,2,128,640]{4,3,2,1,0:T(8,128)(2,1)S(1)}, u32[]{:S(2)}, u32[]{:S(2)}) collective-permute-start(bf16[1,4,2,128,640]{4,3,2,1,0:T(8,128)(2,1)S(1)} %bitcast.75), channel_id=1, source_target_pairs={{0,24},{4,28},{8,16},{12,20},{16,8},{20,12},{24,0},{28,4},{1,25},{... | collective-permute-start | bytes 3932168 | tf_op jit(solution)/shard_map/ppermute | solution.py:401
  588.9 56.5 %collective-permute-start.35 = (bf16[1,4,2,128,640]{4,3,2,1,0:T(8,128)(2,1)S(1)}, bf16[1,4,2,128,640]{4,3,2,1,0:T(8,128)(2,1)S(1)}, u32[]{:S(2)}, u32[]{:S(2)}) collective-permute-start(bf16[1,4,2,128,640]{4,3,2,1,0:T(8,128)(2,1)S(1)} %bitcast.76), channel_id=1, source_target_pairs={{0,16},{4,20},{8,24},{12,28},{16,0},{20,4},{24,8},{28,12},{1,17},{... | collective-permute-start | bytes 3932168 | tf_op jit(solution)/shard_map/ppermute | solution.py:401
  589.3 56.1 %collective-permute-start.33 = (bf16[1,4,2,128,640]{4,3,2,1,0:T(8,128)(2,1)S(1)}, bf16[1,4,2,128,640]{4,3,2,1,0:T(8,128)(2,1)S(1)}, u32[]{:S(2)}, u32[]{:S(2)}) collective-permute-start(bf16[1,4,2,128,640]{4,3,2,1,0:T(8,128)(2,1)S(1)} %bitcast.77), channel_id=1, source_target_pairs={{0,8},{4,12},{8,0},{12,4},{16,24},{20,28},{24,16},{28,20},{1,9},{5... | collective-permute-start | bytes 3932168 | tf_op jit(solution)/shard_map/ppermute | solution.py:401
  589.6 56.5 %collective-permute-start.32 = (bf16[1,4,2,128,640]{4,3,2,1,0:T(8,128)(2,1)S(1)}, bf16[1,4,2,128,640]{4,3,2,1,0:T(8,128)(2,1)S(1)}, u32[]{:S(2)}, u32[]{:S(2)}) collective-permute-start(bf16[1,4,2,128,640]{4,3,2,1,0:T(8,128)(2,1)S(1)} %bitcast.78), channel_id=1, source_target_pairs={{0,4},{4,0},{8,12},{12,8},{16,20},{20,16},{24,28},{28,24},{1,5},{5... | collective-permute-start | bytes 3932168 | tf_op jit(solution)/shard_map/ppermute | solution.py:401
  645.5 4.9 collective-permute-start.36
  646.0 6.3 collective-permute-start.38
  652.3 61.2 %collective-permute-start.39 = (bf16[256,2816]{1,0:T(8,128)(2,1)}, bf16[256,2816]{1,0:T(8,128)(2,1)}, u32[]{:S(2)}, u32[]{:S(2)}) collective-permute-start(bf16[256,2816]{1,0:T(8,128)(2,1)} %maximum_select_fusion.4), channel_id=1, source_target_pairs={{0,8},{4,12},{8,0},{12,4},{16,24},{20,28},{24,16},{28,20},{1,9},{5... | collective-permute-start | bytes 4325384 | tf_op jit(solution)/shard_map/ppermute | solution.py:401
  662.8 51.0 %collective-permute-start.40 = (bf16[256,2816]{1,0:T(8,128)(2,1)}, bf16[256,2816]{1,0:T(8,128)(2,1)}, u32[]{:S(2)}, u32[]{:S(2)}) collective-permute-start(bf16[256,2816]{1,0:T(8,128)(2,1)} %maximum_select_fusion.5), channel_id=1, source_target_pairs={{0,16},{4,20},{8,24},{12,28},{16,0},{20,4},{24,8},{28,12},{1,17},{... | collective-permute-start | bytes 4325384 | tf_op jit(solution)/shard_map/ppermute | solution.py:401
  662.9 256.1 %all-reduce.6.cloned.1.call-start = ((), (), s32[]{:S(2)}) async-start(), calls=%async_computation.11 | async-start | bytes 4194304 | tf_op jit(solution)/shard_map/psum | solution.py:706
  779.9 9.4 collective-permute-start.41
  780.0 43.1 %collective-permute-start.49 = (bf16[1024,2816]{1,0:T(8,128)(2,1)}, bf16[1024,2816]{1,0:T(8,128)(2,1)}, u32[]{:S(2)}, u32[]{:S(2)}) collective-permute-start(bf16[1024,2816]{1,0:T(8,128)(2,1)} %pad_maximum_fusion.half_ref), channel_id=1, source_target_pairs={{0,4},{4,0},{8,12},{12,8},{16,20},{20,16},{24,28},{28,24},{1,5},{5... | collective-permute-start | bytes 17301512 | tf_op jit(solution)/shard_map/ppermute | solution.py:401
  799.8 198.0 %reduce-scatter.8.cloned.1.call-start = ((), (), s32[]{:S(2)}) async-start(), calls=%async_computation.8 | async-start | bytes 5242880 | tf_op jit(solution)/shard_map/reduce_scatter | solution.py:550
  809.4 29.4 %collective-permute-start.47 = (bf16[256,1536]{1,0:T(8,128)(2,1)}, bf16[256,1536]{1,0:T(8,128)(2,1)}, u32[]{:S(2)}, u32[]{:S(2)}) collective-permute-start(bf16[256,1536]{1,0:T(8,128)(2,1)} %constant_dynamic-slice_fusion.2), channel_id=1, source_target_pairs={{0,8},{4,12},{8,0},{12,4},{16,24},{20,28},{24,16},{28,20},{1,9},{5... | collective-permute-start | bytes 2359304 | tf_op jit(solution)/shard_map/ppermute | solution.py:401
  821.6 19.6 %collective-permute-start.48 = (bf16[256,1536]{1,0:T(8,128)(2,1)}, bf16[256,1536]{1,0:T(8,128)(2,1)}, u32[]{:S(2)}, u32[]{:S(2)}) collective-permute-start(bf16[256,1536]{1,0:T(8,128)(2,1)} %constant_dynamic-slice_fusion.1), channel_id=1, source_target_pairs={{0,16},{4,20},{8,24},{12,28},{16,0},{20,4},{24,8},{28,12},{1,17},{... | collective-permute-start | bytes 2359304 | tf_op jit(solution)/shard_map/ppermute | solution.py:401
  842.5 18.6 %collective-permute-start.50 = (bf16[128,1536]{1,0:T(8,128)(2,1)S(1)}, bf16[128,1536]{1,0:T(8,128)(2,1)S(1)}, u32[]{:S(2)}, u32[]{:S(2)}) collective-permute-start(bf16[128,1536]{1,0:T(8,128)(2,1)S(1)} %constant_dynamic-slice_fusion), channel_id=1, source_target_pairs={{0,16},{4,20},{8,24},{12,28},{16,0},{20,4},{24,8},{28,12},{1,17},{... | collective-permute-start | bytes 1179656 | tf_op jit(solution)/shard_map/ppermute | solution.py:401
  844.2 16.9 %collective-permute-start.51 = (bf16[128,1536]{1,0:T(8,128)(2,1)S(1)}, bf16[128,1536]{1,0:T(8,128)(2,1)S(1)}, u32[]{:S(2)}, u32[]{:S(2)}) collective-permute-start(bf16[128,1536]{1,0:T(8,128)(2,1)S(1)} %constant_dynamic-slice_fusion.15), channel_id=1, source_target_pairs={{0,8},{4,12},{8,0},{12,4},{16,24},{20,28},{24,16},{28,20},{1,9},{5... | collective-permute-start | bytes 1179656 | tf_op jit(solution)/shard_map/ppermute | solution.py:401
  844.6 11.1 %collective-permute-start.43 = (f32[14,1024]{1,0:T(8,128)S(1)}, f32[14,1024]{1,0:T(8,128)S(1)}, u32[]{:S(2)}, u32[]{:S(2)}) collective-permute-start(f32[14,1024]{1,0:T(8,128)S(1)} %add.398), channel_id=1, source_target_pairs={{0,8},{4,12},{8,0},{12,4},{16,24},{20,28},{24,16},{28,20},{1,9},{5... | collective-permute-start | bytes 172040 | tf_op jit(solution)/shard_map/ppermute | solution.py:596
  855.7 5.4 collective-permute-start.44
  861.2 13.2 %collective-permute-start.53 = (bf16[128,1536]{1,0:T(8,128)(2,1)S(1)}, bf16[128,1536]{1,0:T(8,128)(2,1)S(1)}, u32[]{:S(2)}, u32[]{:S(2)}) collective-permute-start(bf16[128,1536]{1,0:T(8,128)(2,1)S(1)} %add_convert_fusion.11), channel_id=1, source_target_pairs={{0,8},{4,12},{8,0},{12,4},{16,24},{20,28},{24,16},{28,20},{1,9},{5... | collective-permute-start | bytes 1179656 | tf_op jit(solution)/shard_map/ppermute | solution.py:401
  862.2 12.5 %collective-permute-start.52 = (bf16[128,1536]{1,0:T(8,128)(2,1)S(1)}, bf16[128,1536]{1,0:T(8,128)(2,1)S(1)}, u32[]{:S(2)}, u32[]{:S(2)}) collective-permute-start(bf16[128,1536]{1,0:T(8,128)(2,1)S(1)} %add_convert_fusion.12), channel_id=1, source_target_pairs={{0,16},{4,20},{8,24},{12,28},{16,0},{20,4},{24,8},{28,12},{1,17},{... | collective-permute-start | bytes 1179656 | tf_op jit(solution)/shard_map/ppermute | solution.py:401
  863.5 4.3 collective-permute-start.45
  874.9 23.5 %collective-permute-start.55 = (bf16[256,1536]{1,0:T(8,128)(2,1)S(1)}, bf16[256,1536]{1,0:T(8,128)(2,1)S(1)}, u32[]{:S(2)}, u32[]{:S(2)}) collective-permute-start(bf16[256,1536]{1,0:T(8,128)(2,1)S(1)} %maximum_select_fusion.7), channel_id=1, source_target_pairs={{0,16},{4,20},{8,24},{12,28},{16,0},{20,4},{24,8},{28,12},{1,17},{... | collective-permute-start | bytes 2359304 | tf_op jit(solution)/shard_map/ppermute | solution.py:401
  875.9 23.8 %collective-permute-start.54 = (bf16[256,1536]{1,0:T(8,128)(2,1)S(1)}, bf16[256,1536]{1,0:T(8,128)(2,1)S(1)}, u32[]{:S(2)}, u32[]{:S(2)}) collective-permute-start(bf16[256,1536]{1,0:T(8,128)(2,1)S(1)} %maximum_select_fusion.6), channel_id=1, source_target_pairs={{0,8},{4,12},{8,0},{12,4},{16,24},{20,28},{24,16},{28,20},{1,9},{5... | collective-permute-start | bytes 2359304 | tf_op jit(solution)/shard_map/ppermute | solution.py:401
  902.2 100.9 %collective-permute-start.56 = (bf16[1024,1536]{1,0:T(8,128)(2,1)}, bf16[1024,1536]{1,0:T(8,128)(2,1)}, u32[]{:S(2)}, u32[]{:S(2)}) collective-permute-start(bf16[1024,1536]{1,0:T(8,128)(2,1)} %pad_maximum_fusion.1.half_ref), channel_id=1, source_target_pairs={{0,4},{4,0},{8,12},{12,8},{16,20},{20,16},{24,28},{28,24},{1,5},{5... | collective-permute-start | bytes 9437192 | tf_op jit(solution)/shard_map/ppermute | solution.py:401
  902.2 6.8 collective-permute-start.46
  (79 other events, 1422.1 us)
Sparse Core Ops, SparseCore 0:
  12.8 83.4 all-gather.6
  97.8 86.8 all-gather.8
  209.9 52.5 all-gather.14
  294.0 85.6 all-gather.10
  440.0 75.4 reduce-scatter.3
  559.4 83.0 all-gather.12
  646.8 118.7 all-reduce.3
  768.5 76.8 reduce-scatter.5
  848.9 70.0 all-reduce.5
  921.8 75.9 reduce-scatter.7

commit v7 on v6

--- a/solution.py
+++ b/solution.py
@@ -518,6 +518,29 @@
     return lax.dynamic_slice_in_dim(x, which * w, w, 1)
 
 
+def unpack_cols_kernel(core_ref, half_ref, other_ref, out_ref):
+    c = half_ref.shape[1]
+    core = core_ref[0]
+    out_ref[:, pl.ds(pl.multiple_of(core * c, 128), c)] = half_ref[...].astype(F32)
+    out_ref[:, pl.ds(pl.multiple_of((1 - core) * c, 128), c)] = other_ref[...].astype(F32)
+
+
+def unpack_cols(half, other):
+    r, c = half.shape
+    step = math.gcd(r, 256)
+    block = pl.BlockSpec((step, c), lambda i, _: (i, 0))
+    return pl.pallas_call(
+        unpack_cols_kernel,
+        grid_spec=pltpu.PrefetchScalarGridSpec(
+            num_scalar_prefetch=1, grid=(r // step,), in_specs=[block, block],
+            out_specs=pl.BlockSpec((step, 2 * c), lambda i, _: (i, 0))),
+        out_shape=jax.ShapeDtypeStruct((r, 2 * c), F32),
+        compiler_params=pltpu.CompilerParams(vmem_limit_bytes=40 * 2**20),
+        cost_estimate=pl.CostEstimate(flops=0, bytes_accessed=12 * r * c, transcendentals=0),
+        name="unpack_cols",
+    )((lax.axis_index("ctx") & 1)[None], half, other)
+
+
 def all_rows(x):
     return lax.all_gather(x, "tp", axis=0, tiled=True)
 
@@ -652,21 +675,22 @@
     grad_two = sum_rows(part_two)
     act, rows_two, dy_rows, grad_gu = after((act, rows_two, dy_rows, grad_gu), part_two)
     gu = begin(lambda core: rc(columns(rows_two, core), grad_gu))
-    grad_down_w = rc(act, dy_rows).astype(BF16)
+    dw = begin(lambda core: rc(act, columns(dy_rows, core)))
     held = take(gu)
     go(gu)
     down = nn(after(act, held), down_w).astype(BF16)
-    held = take(gu, down)
-    grad_two, grad_down_w = after((grad_two, grad_down_w), held, down)
+    held = take(dw, held), take(gu, down)
     go(gu)
-    grad_down_w = lax.psum(grad_down_w, "ctx")
+    go(dw, held)
+    grad_two = after(grad_two, held)
 
     norm_two, grad_gain_two, grad_shift_two = layer_back(grad_two.astype(F32), unit_two, inverse_two, gain_two)
     grad_mixed = cotangent.astype(F32) + norm_two
     branch_own = grad_mixed.astype(BF16)
     grad_attn = nt(branch_own, whole_w).astype(BF16)
-    grad_attn = after(grad_attn, take(gu))
+    grad_attn = after(grad_attn, take(gu), take(dw))
     go(gu)
+    go(dw)
     grad_attn = exchange(grad_attn, 1, 0)
     branch = all_rows(after(branch_own, grad_attn))
     out_tokens = (mixed + sum_rows(after(down, grad_attn)).astype(F32)).astype(BF16)
@@ -676,16 +700,16 @@
                             precision=lax.Precision.HIGHEST, preferred_element_type=F32)
     do_ext = terms(-delta, lane).astype(BF16)
     do_sent = jnp.concatenate([grad_attn, do_ext], axis=1).reshape(shape)
-    grads = gather_other(after(do_sent, take(gu, grad_attn)))
+    grads = gather_other(after(do_sent, take(gu, grad_attn), take(dw, grad_attn)))
     grad_q = query_grad(place, own, q, grad_attn.reshape(q.shape), q_ext, do_ext.reshape(q_ext.shape), tabs, keys, values)
     grad_q = grad_q.reshape(-1, width)
     q_part = nt(grad_q, query_w)
     grads = gather_cores(grads, q_part)
     go(gu, grads)
+    go(dw, grads)
     first = key_value_grad(place, own, kv, tabs, queries, grads, 0, SEQS // 2)
-    grads = after(grads, take(gu, first))
-    take_extra(gu)
-    go(gu)
+    grads = after(grads, take(dw, first))
+    go(dw)
     second = key_value_grad(place, own, kv, tabs, queries, grads, SEQS // 2, SEQS // 2)
     grad_k, grad_v = (jnp.concatenate(pair).reshape(-1, width) for pair in zip(first, second))
     part_one = q_part + nt(grad_k, key_w) + nt(grad_v, value_w)
@@ -695,6 +719,9 @@
     rows_one, branch, grad_q, grad_k, grad_v = after((rows_one, branch, grad_q, grad_k, grad_v), part_sent)
     grad_qkv = jnp.concatenate([grad_q, grad_k, grad_v], axis=1)
     chain = begin(lambda core: rc(columns(rows_one, core), grad_qkv))
+    take(gu, part_sent)
+    take_extra(gu)
+    go(gu)
     unit_rows = (rows_one.astype(F32) - shift_one) / gain_one
     bias_grad = jnp.sum(grad_qkv.astype(F32), axis=0)
     tp_row = (jnp.arange(n_tp) == lax.axis_index("tp"))[:, None]
@@ -703,24 +730,25 @@
         jnp.where(tp_row, bias_grad[None, :], 0.0).reshape(-1)])
     held = take(chain)
     go(chain)
-    grad_output_w = lax.psum(after(rc(attn_rows, after(branch, held)).astype(BF16), grad_down_w), "ctx")
+    take(dw, held)
+    take_extra(dw)
+    go(dw)
+    grad_output_w = rc(attn_rows, after(branch, held)).astype(BF16)
+    sums = sum_over_all(after(small, held).reshape(-1, 1024))
     grad_gate_w, grad_up_w = unpack_rows(*take(gu, held), 2)
-    sums = sum_over_all(after(small, held).reshape(-1, 1024))
-    small = next(sums), grad_gate_w
-    held = take(chain, small)
+    held = take(chain, (grad_gate_w, grad_output_w))
     go(chain)
-    small = next(sums), next(sums)
-    held = take(chain, small)
+    grad_output_w = lax.psum(grad_output_w, "ctx")
+    grad_down_w = unpack_cols(*take(dw, held))
+    held = take(chain, grad_down_w)
     go(chain)
-    grad_down_w = after(grad_down_w, held).astype(F32)
-    small = next(sums), grad_down_w
-    held = take(chain, small)
+    held = take(chain, held)
     go(chain)
-    for _ in range(4):
-        small = next(sums)
     take(chain)
     take_extra(chain)
     go(chain)
+    for _ in range(9):
+        small = next(sums)
     depth = x.shape[1]
     small = small.reshape(-1)
     norms = small[:4 * depth].reshape(4, depth)

time: 1030 us -> 1030 us (level)
  waiting for transfers between devices: 479 us -> 458 us
  starting transfers between devices: 71.9 us -> 86.3 us
    reduce_scatter x3, waiting for transfers between devices: 74.7 us -> 54.6 us  [sum_rows(): return lax.psum_scatter(x, 'tp', scatter_dimension=0, tiled=True)]
    ppermute x43 -> x53, waiting for transfers between devices: 214 us -> 229 us  [ctx_swap(): return lax.ppermute(x, 'ctx', [(i, i ^ mask) for i in range(n)])]
    select_n x8 -> x12, other arithmetic: 13.7 us -> 22.3 us  [weight_grad(): jnp.where(lax.axis_index('ctx') >> o[i] & 1 == 0, jnp.concatenate([x, g])...]
    ppermute x43 -> x53, starting transfers between devices: 53.6 us -> 49.1 us  [ctx_swap(): return lax.ppermute(x, 'ctx', [(i, i ^ mask) for i in range(n)])]
    dot_general x6 -> x7, matrix products: 41.4 us -> 44.1 us  [rc(): lax.dot_general(left, right, (((0,), (0,)), ((), ())), preferred_element_...]
  transfers between devices with their start and end apart: 67 -> 76, of which waited for: 42 -> 42; matrix products, arithmetic and copies ran while one was open for 15% -> 15% of each run, Pallas kernels for 19% -> 19%
where the time goes in v7:
time: 1030 us; the launch traced here: 1020 us
  waiting for transfers between devices  458 us (44%)
  Pallas kernels  234 us (23%)
  matrix products  105 us (10%)
  starting transfers between devices  86.3 us (8%)
  other arithmetic  76.9 us (7%)
  local copies, waits for them, and re-layouts  42.6 us (4%)
  between operations  15.6 us (2%)
    ppermute x53, waiting for transfers between devices, ctx_swap(): return lax.ppermute(x, 'ctx', [(i, i ^ mask) for i in range(n)])  229 us
    pallas_call x4, Pallas kernels, attention_call(): pl.pallas_call(kernel, grid_spec=pltpu.PrefetchScalarGridSpec(num_scalar_...  162 us
    all_gather x4, waiting for transfers between devices, all_rows(): return lax.all_gather(x, 'tp', axis=0, tiled=True)  103 us
    reduce_scatter x3, waiting for transfers between devices, sum_rows(): return lax.psum_scatter(x, 'tp', scatter_dimension=0, tiled=True)  54.6 us
    ppermute x53, starting transfers between devices, ctx_swap(): return lax.ppermute(x, 'ctx', [(i, i ^ mask) for i in range(n)])  49.1 us
    dot_general x7, matrix products, rc(): lax.dot_general(left, right, (((0,), (0,)), ((), ())), preferred_element_...  44.1 us
    dot_general x6, matrix products, nt(): lax.dot_general(a, b, (((1,), (1,)), ((), ())), preferred_element_type=jn...  43.9 us
    ppermute x6, waiting for transfers between devices, tp_shift(): return lax.ppermute(x, 'tp', [(i, (i + d) % n) for i in range(n)])  31.6 us
  transfers between devices with their start and end apart: 76, of which 42 were waited for; matrix products, arithmetic and copies ran while one was open for 15% of the time, Pallas kernels for 19%

profile of v7, /device:TPU:0, one launch (start us, length us, event | category | flops | bytes accessed | tf_op | source)
XLA Modules:
  0.0 1019.4 jit_solution(6037792247380176177)
XLA Ops:
  12.7 83.6 %all-gather.7.cloned.1.call-done.h_ref = bf16[1024,2048]{1,0:T(8,128)(2,1)} async-done(((bf16[256,2048]{1,0:T(8,128)(2,1)}), bf16[1024,2048]{1,0:T(8,128)(2,1)}) %all-gather.7.cloned.1.call-update) | async-done | bytes 4194320 | tf_op jit(solution)/shard_map/all_gather | solution.py:545
  98.5 11.6 %project.1 = (bf16[4,256,512]{2,1,0:T(8,128)(2,1)S(1)}, bf16[2,4,256,512]{3,2,1,0:T(8,128)(2,1)}) custom-call(bf16[1024,2048]{1,0:T(8,128)(2,1)} %all-gather.7.cloned.1.call-done.h_ref, bf16[2048,512]{1,0:T(8,128)(2,1)} %wq_ref.1, bf16[2048,512]{1,0:T(8,128)(2,1)} %wk_ref.1, bf16[2048,512]{1,0:T(8,128)(2,1)} %wv_ref.1, ...), custom_call_target="tpu_custom_call" | custom-call | flops 6442450944 | bytes 6291456 | tf_op jit(solution)/shard_map/project/pallas_call | solution.py:345
  114.1 44.7 %collective-permute-done.1.refs_2_.refs_10_ = bf16[2,4,2,128,512]{4,3,2,1,0:T(8,128)(2,1)} collective-permute-done((bf16[2,4,2,128,512]{4,3,2,1,0:T(8,128)(2,1)}, bf16[2,4,2,128,512]{4,3,2,1,0:T(8,128)(2,1)}, u32[]{:S(2)}, u32[]{:S(2)}) %collective-permute-start.1) | collective-permute-done | bytes 2097184 | tf_op jit(solution)/shard_map/ppermute | solution.py:401
  170.2 12.7 %collective-permute-done.12 = bf16[64,2048]{1,0:T(8,128)(2,1)S(1)} collective-permute-done((bf16[64,2048]{1,0:T(8,128)(2,1)S(1)}, bf16[64,2048]{1,0:T(8,128)(2,1)S(1)}, u32[]{:S(2)}, u32[]{:S(2)}) %collective-permute-start.12) | collective-permute-done | bytes 262176 | tf_op jit(solution)/shard_map/ppermute | solution.py:629
  182.9 11.2 %collective-permute-done.13 = bf16[64,2048]{1,0:T(8,128)(2,1)S(1)} collective-permute-done((bf16[64,2048]{1,0:T(8,128)(2,1)S(1)}, bf16[64,2048]{1,0:T(8,128)(2,1)S(1)}, u32[]{:S(2)}, u32[]{:S(2)}) %collective-permute-start.13) | collective-permute-done | bytes 262176 | tf_op jit(solution)/shard_map/ppermute | solution.py:629
  199.4 4.7 collective-permute-done.6.refs_7_
  205.4 48.3 %attend.1 = (bf16[4,256,512]{2,1,0:T(8,128)(2,1)S(1)}, bf16[4,256,128]{2,1,0:T(8,128)(2,1)S(1)}) custom-call(s32[4,16]{1,0:T(4,128)S(1)} %copy.42.place_ref, s32[4,2]{1,0:T(4,128)S(1)} %get-tuple-element.219.own_ref, bf16[4,256,512]{2,1,0:T(8,128)(2,1)S(1)} %copy-done.13, bf16[2,4,2,128,512]{4,3,2,1,0:T(8,128)(2,1)} %bitcast.5.refs_0_.refs_8_, ...), custom_call_target="tpu_custom_call" | custom-call | flops 8589934592 | bytes 16777216 | tf_op jit(solution)/shard_map/attend/pallas_call | solution.py:222
  259.4 3.4 collective-permute-start.10
  262.8 4.2 collective-permute-done.9
  268.7 12.1 %collective-permute-done.10 = bf16[256,512]{1,0:T(8,128)(2,1)S(1)} collective-permute-done((bf16[256,512]{1,0:T(8,128)(2,1)}, bf16[256,512]{1,0:T(8,128)(2,1)S(1)}, u32[]{:S(2)}, u32[]{:S(2)}) %collective-permute-start.10) | collective-permute-done | bytes 262176 | tf_op jit(solution)/shard_map/ppermute | solution.py:550
  282.2 6.2 fusion.74
  295.2 28.1 %collective-permute-done.16.refs_2_.refs_18_ = bf16[1,4,2,128,640]{4,3,2,1,0:T(8,128)(2,1)S(1)} collective-permute-done((bf16[1,4,2,128,640]{4,3,2,1,0:T(8,128)(2,1)S(1)}, bf16[1,4,2,128,640]{4,3,2,1,0:T(8,128)(2,1)S(1)}, u32[]{:S(2)}, u32[]{:S(2)}) %collective-permute-start.16) | collective-permute-done | bytes 1310752 | tf_op jit(solution)/shard_map/ppermute | solution.py:401
  323.3 27.6 %collective-permute-done.18.refs_4_.refs_20_ = bf16[1,4,2,128,640]{4,3,2,1,0:T(8,128)(2,1)} collective-permute-done((bf16[1,4,2,128,640]{4,3,2,1,0:T(8,128)(2,1)S(1)}, bf16[1,4,2,128,640]{4,3,2,1,0:T(8,128)(2,1)}, u32[]{:S(2)}, u32[]{:S(2)}) %collective-permute-start.18) | collective-permute-done | bytes 1310752 | tf_op jit(solution)/shard_map/ppermute | solution.py:401
  356.2 19.1 %all-gather.11.cloned.1.call-done.h_ref = bf16[1024,2048]{1,0:T(8,128)(2,1)} async-done(((bf16[256,2048]{1,0:T(8,128)(2,1)}), bf16[1024,2048]{1,0:T(8,128)(2,1)}) %all-gather.11.cloned.1.call-update) | async-done | bytes 4194320 | tf_op jit(solution)/shard_map/all_gather | solution.py:545
  375.3 28.4 %mlp.1 = (bf16[1024,1408]{1,0:T(8,128)(2,1)}, bf16[1024,2816]{1,0:T(8,128)(2,1)}) custom-call(bf16[1024,2048]{1,0:T(8,128)(2,1)} %all-gather.11.cloned.1.call-done.h_ref, bf16[1024,2048]{1,0:T(8,128)(2,1)} %all-gather.9.cloned.1.call-done.dy_ref, bf16[2048,1408]{1,0:T(8,128)(2,1)} %gate_ref.1, bf16[2048,1408]{1,0:T(8,128)(2,1)} %up_ref.1, ...), custom_call_target="tpu_custom_call" | custom-call | flops 17716740096 | bytes 38273024 | tf_op jit(solution)/shard_map/mlp/pallas_call | solution.py:385
  403.8 9.8 fusion.4
  413.5 11.1 %add_convert_fusion.1 = bf16[1024,2048]{1,0:T(8,128)(2,1)} fusion(f32[1024,2048]{1,0:T(8,128)S(1)} %fusion.4, bf16[2048,1408]{1,0:T(8,128)(2,1)} %up_ref.1, bf16[1024,2816]{1,0:T(8,128)(2,1)S(1)} %copy-done.79), kind=kOutput, calls=%fused_computation.3 | convolution fusion | flops 5909774336 | bytes 21233664 | tf_op jit(solution)/shard_map/dot_general | solution.py:15
  424.6 11.0 %convolution_convert_fusion = bf16[1024,2816]{1,0:T(8,128)(2,1)} fusion(bf16[1024,2816]{1,0:T(8,128)(2,1)} %get-tuple-element.126, bf16[1024,2048]{1,0:T(8,128)(2,1)} %all-gather.11.cloned.1.call-done.h_ref, s32[]{:T(128)S(6)} %select_n.382), kind=kOutput, calls=%fused_computation.8 | convolution fusion | flops 5908463616 | bytes 13631492 | tf_op jit(solution)/shard_map/dot_general | solution.py:290
  435.6 9.5 all-gather.13.cloned.1.call-start
  445.1 5.8 convolution_convert_fusion.3
  451.5 3.3 fusion.35
  454.8 10.1 add_convert_fusion
  474.6 8.5 convolution_convert_fusion.1
  483.2 17.1 %collective-permute-done.24 = bf16[256,2816]{1,0:T(8,128)(2,1)} collective-permute-done((bf16[256,2816]{1,0:T(8,128)(2,1)}, bf16[256,2816]{1,0:T(8,128)(2,1)}, u32[]{:S(2)}, u32[]{:S(2)}) %collective-permute-start.24) | collective-permute-done | bytes 1441824 | tf_op jit(solution)/shard_map/ppermute | solution.py:401
  511.4 14.7 %collective-permute-done.28 = bf16[352,1024]{1,0:T(8,128)(2,1)S(1)} collective-permute-done((bf16[352,1024]{1,0:T(8,128)(2,1)S(1)}, bf16[352,1024]{1,0:T(8,128)(2,1)S(1)}, u32[]{:S(2)}, u32[]{:S(2)}) %collective-permute-start.28) | collective-permute-done | bytes 720928 | tf_op jit(solution)/shard_map/ppermute | solution.py:401
  528.3 11.7 %collective-permute-done.26 = bf16[128,2816]{1,0:T(8,128)(2,1)S(1)} collective-permute-done((bf16[128,2816]{1,0:T(8,128)(2,1)S(1)}, bf16[128,2816]{1,0:T(8,128)(2,1)S(1)}, u32[]{:S(2)}, u32[]{:S(2)}) %collective-permute-start.26) | collective-permute-done | bytes 720928 | tf_op jit(solution)/shard_map/ppermute | solution.py:401
  542.0 3.0 fusion.23
  545.1 3.9 fusion.68
  549.0 6.1 convolution_convert_fusion.5
  559.3 7.1 collective-permute-done.30
  566.5 8.1 collective-permute-done.31
  582.4 11.8 %collective-permute-done.33 = bf16[128,2816]{1,0:T(8,128)(2,1)} collective-permute-done((bf16[128,2816]{1,0:T(8,128)(2,1)}, bf16[128,2816]{1,0:T(8,128)(2,1)}, u32[]{:S(2)}, u32[]{:S(2)}) %collective-permute-start.33) | collective-permute-done | bytes 720928 | tf_op jit(solution)/shard_map/ppermute | solution.py:401
  595.6 3.5 collective-permute-done.35
  608.0 3.0 maximum_select_fusion.4
  617.5 48.0 %query_grad.1 = bf16[4,256,512]{2,1,0:T(8,128)(2,1)S(1)} custom-call(s32[4,16]{1,0:T(4,128)S(1)} %copy.42.place_ref, s32[4,2]{1,0:T(4,128)S(1)} %get-tuple-element.219.own_ref, bf16[4,256,512]{2,1,0:T(8,128)(2,1)S(1)} %copy-done.14, bf16[4,256,512]{2,1,0:T(8,128)(2,1)S(1)} %bitcast.83, bf16[4,256,128]{2,1,0:T(8,128)(2,1)S(1)} %get-tuple-element.119.qx_ref, ...), custom_call_target="tpu_custom_call" | custom-call | flops 12884901888 | bytes 16777216 | tf_op jit(solution)/shard_map/query_grad/pallas_call | solution.py:222
  665.5 5.8 fusion.76
  671.3 5.5 collective-permute-start.39
  683.5 3.8 collective-permute-start.45
  692.8 26.8 %key_value_grad.2 = (bf16[2,256,512]{2,1,0:T(8,128)(2,1)S(1)}, bf16[2,256,512]{2,1,0:T(8,128)(2,1)S(1)}) custom-call(s32[4,16]{1,0:T(4,128)S(1)} %copy.42.place_ref, s32[4,2]{1,0:T(4,128)S(1)} %get-tuple-element.219.own_ref, bf16[2,4,256,512]{3,2,1,0:T(8,128)(2,1)} %get-tuple-element.113.k_ref.v_ref, ...), custom_call_target="tpu_custom_call" | custom-call | flops 8589934592 | bytes 8388608 | tf_op jit(solution)/shard_map/key_value_grad/pallas_call | solution.py:222
  724.1 39.1 %key_value_grad.3 = (bf16[2,256,512]{2,1,0:T(8,128)(2,1)S(1)}, bf16[2,256,512]{2,1,0:T(8,128)(2,1)S(1)}) custom-call(s32[4,16]{1,0:T(4,128)S(1)} %copy.42.place_ref, s32[4,2]{1,0:T(4,128)S(1)} %get-tuple-element.219.own_ref, bf16[2,4,256,512]{3,2,1,0:T(8,128)(2,1)} %get-tuple-element.113.k_ref.v_ref, ...), custom_call_target="tpu_custom_call" | custom-call | flops 8589934592 | bytes 8388608 | tf_op jit(solution)/shard_map/key_value_grad/pallas_call | solution.py:222
  767.9 8.9 fusion.75
  776.8 3.4 maximum_select_fusion.1
  780.2 3.5 maximum_select_fusion
  786.1 5.1 convolution_convert_fusion.2
  791.4 3.3 pad_maximum_fusion.half_ref
  794.8 6.2 collective-permute-start.59
  801.0 5.2 add_convert_fusion.2
  810.6 7.2 collective-permute-done.59
  823.5 3.8 convolution_convert_fusion.4
  827.2 13.4 %unpack_rows.2 = (f32[2048,1408]{1,0:T(8,128)}, f32[2048,1408]{1,0:T(8,128)}) custom-call(s32[1]{0:T(128)} %bitcast.19.core_ref, bf16[1024,2816]{1,0:T(8,128)(2,1)} %pad_maximum_fusion.half_ref, bf16[1024,2816]{1,0:T(8,128)(2,1)} %collective-permute-done.56.other_ref), custom_call_target="tpu_custom_call" | custom-call | bytes 34603008 | tf_op jit(solution)/shard_map/unpack_rows/pallas_call | solution.py:503
  849.3 9.2 unpack_cols.1
  858.6 6.6 collective-permute-done.57
  870.2 9.2 collective-permute-done.62
  882.9 16.5 %collective-permute-done.65 = bf16[256,1536]{1,0:T(8,128)(2,1)S(1)} collective-permute-done((bf16[256,1536]{1,0:T(8,128)(2,1)S(1)}, bf16[256,1536]{1,0:T(8,128)(2,1)S(1)}, u32[]{:S(2)}, u32[]{:S(2)}) %collective-permute-start.65) | collective-permute-done | bytes 786464 | tf_op jit(solution)/shard_map/ppermute | solution.py:401
  905.8 3.2 collective-permute-start.48
  909.0 3.9 collective-permute-done.48
  914.1 3.9 collective-permute-done.49
  918.0 4.9 collective-permute-start.50
  925.1 3.3 collective-permute-start.51
  930.9 4.3 collective-permute-done.51
  939.0 4.2 convert_element_type.300
  943.2 54.6 %reduce-scatter.8.cloned.1.call-done = bf16[256,2048]{1,0:T(8,128)(2,1)} async-done(((bf16[1024,2048]{1,0:T(8,128)(2,1)}), bf16[256,2048]{1,0:T(8,128)(2,1)}) %reduce-scatter.8.cloned.1.call-update) | async-done | bytes 1048592 | tf_op jit(solution)/shard_map/reduce_scatter | solution.py:573
  999.8 3.2 fusion.17
  1003.1 9.4 unpack_rows.3
  (431 shorter events, 173.9 us)
Async XLA Ops:
  7.2 89.0 %all-gather.7.cloned.1.call-start = ((), (), s32[]{:S(2)}) async-start(), calls=%async_computation.3 | async-start | bytes 5242880 | tf_op jit(solution)/shard_map/all_gather | solution.py:545
  12.6 192.1 %all-gather.9.cloned.1.call-start = ((), (), s32[]{:S(2)}) async-start(), calls=%async_computation.4 | async-start | bytes 5242880 | tf_op jit(solution)/shard_map/all_gather | solution.py:545
  96.2 185.9 %all-gather.15.cloned.1.call-start = ((), (), s32[]{:S(2)}) async-start(), calls=%async_computation.11 | async-start | bytes 9437184 | tf_op jit(solution)/shard_map/all_gather | solution.py:660
  111.1 47.7 %collective-permute-start.1 = (bf16[2,4,2,128,512]{4,3,2,1,0:T(8,128)(2,1)}, bf16[2,4,2,128,512]{4,3,2,1,0:T(8,128)(2,1)}, u32[]{:S(2)}, u32[]{:S(2)}) collective-permute-start(bf16[2,4,2,128,512]{4,3,2,1,0:T(8,128)(2,1)} %bitcast.5.refs_0_.refs_8_), channel_id=1, source_target_pairs={{0,8},{4,12},{8,0},{12,4},{16,24},{20,28},{24,16},{28,20},{1,9},{5... | collective-permute-start | bytes 6291464 | tf_op jit(solution)/shard_map/ppermute | solution.py:401
  112.6 49.9 %collective-permute-start.3 = (bf16[2,4,2,128,512]{4,3,2,1,0:T(8,128)(2,1)}, bf16[2,4,2,128,512]{4,3,2,1,0:T(8,128)(2,1)}, u32[]{:S(2)}, u32[]{:S(2)}) collective-permute-start(bf16[2,4,2,128,512]{4,3,2,1,0:T(8,128)(2,1)} %bitcast.5.refs_0_.refs_8_), channel_id=1, source_target_pairs={{0,16},{4,20},{8,24},{12,28},{16,0},{20,4},{24,8},{28,12},{1,17},{... | collective-permute-start | bytes 6291464 | tf_op jit(solution)/shard_map/ppermute | solution.py:401
  161.1 35.6 %collective-permute-start.5 = (bf16[1,4,2,128,512]{4,3,2,1,0:T(8,128)(2,1)}, bf16[1,4,2,128,512]{4,3,2,1,0:T(8,128)(2,1)}, u32[]{:S(2)}, u32[]{:S(2)}) collective-permute-start(bf16[1,4,2,128,512]{4,3,2,1,0:T(8,128)(2,1)} %slice.95), channel_id=1, source_target_pairs={{0,16},{4,20},{8,24},{12,28},{16,0},{20,4},{24,8},{28,12},{1,17},{... | collective-permute-start | bytes 3145736 | tf_op jit(solution)/shard_map/ppermute | solution.py:401
  164.8 32.4 %collective-permute-start.7 = (bf16[1,4,2,128,512]{4,3,2,1,0:T(8,128)(2,1)}, bf16[1,4,2,128,512]{4,3,2,1,0:T(8,128)(2,1)}, u32[]{:S(2)}, u32[]{:S(2)}) collective-permute-start(bf16[1,4,2,128,512]{4,3,2,1,0:T(8,128)(2,1)} %slice.96), channel_id=1, source_target_pairs={{0,8},{4,12},{8,0},{12,4},{16,24},{20,28},{24,16},{28,20},{1,9},{5... | collective-permute-start | bytes 3145736 | tf_op jit(solution)/shard_map/ppermute | solution.py:401
  166.3 16.6 %collective-permute-start.12 = (bf16[64,2048]{1,0:T(8,128)(2,1)S(1)}, bf16[64,2048]{1,0:T(8,128)(2,1)S(1)}, u32[]{:S(2)}, u32[]{:S(2)}) collective-permute-start(bf16[64,2048]{1,0:T(8,128)(2,1)S(1)} %constant_dynamic-slice_fusion.14), channel_id=1, source_target_pairs={{0,1},{1,2},{2,3},{3,0},{4,5},{5,6},{6,7},{7,4},{8,9},{9,10},{10,1... | collective-permute-start | bytes 786440 | tf_op jit(solution)/shard_map/ppermute | solution.py:629
  166.4 27.8 %collective-permute-start.13 = (bf16[64,2048]{1,0:T(8,128)(2,1)S(1)}, bf16[64,2048]{1,0:T(8,128)(2,1)S(1)}, u32[]{:S(2)}, u32[]{:S(2)}) collective-permute-start(bf16[64,2048]{1,0:T(8,128)(2,1)S(1)} %constant_dynamic-slice_fusion.14), channel_id=1, source_target_pairs={{0,2},{1,3},{2,0},{3,1},{4,6},{5,7},{6,4},{7,5},{8,10},{9,11},{10,... | collective-permute-start | bytes 786440 | tf_op jit(solution)/shard_map/ppermute | solution.py:629
  168.0 26.2 %collective-permute-start.14 = (bf16[64,2048]{1,0:T(8,128)(2,1)S(1)}, bf16[64,2048]{1,0:T(8,128)(2,1)S(1)}, u32[]{:S(2)}, u32[]{:S(2)}) collective-permute-start(bf16[64,2048]{1,0:T(8,128)(2,1)S(1)} %constant_dynamic-slice_fusion.14), channel_id=1, source_target_pairs={{0,3},{1,0},{2,1},{3,2},{4,7},{5,4},{6,5},{7,6},{8,11},{9,8},{10,9... | collective-permute-start | bytes 786440 | tf_op jit(solution)/shard_map/ppermute | solution.py:629
  182.9 16.5 %collective-permute-start = (bf16[2,4,2,128,512]{4,3,2,1,0:T(8,128)(2,1)}, bf16[2,4,2,128,512]{4,3,2,1,0:T(8,128)(2,1)}, u32[]{:S(2)}, u32[]{:S(2)}) collective-permute-start(bf16[2,4,2,128,512]{4,3,2,1,0:T(8,128)(2,1)} %bitcast.5.refs_0_.refs_8_), channel_id=1, source_target_pairs={{0,4},{4,0},{8,12},{12,8},{16,20},{20,16},{24,28},{28,24},{1,5},{5... | collective-permute-start | bytes 6291464 | tf_op jit(solution)/shard_map/ppermute | solution.py:401
  194.1 10.5 %collective-permute-start.2 = (bf16[2,4,2,128,512]{4,3,2,1,0:T(8,128)(2,1)}, bf16[2,4,2,128,512]{4,3,2,1,0:T(8,128)(2,1)}, u32[]{:S(2)}, u32[]{:S(2)}) collective-permute-start(bf16[2,4,2,128,512]{4,3,2,1,0:T(8,128)(2,1)} %collective-permute-done.1.refs_2_.refs_10_), channel_id=1, source_target_pairs={{0,4},{4,0},{8,12},{12,8},{16,20},{20,16},{24,28},{28,24},{1,5},{5... | collective-permute-start | bytes 6291464 | tf_op jit(solution)/shard_map/ppermute | solution.py:401
  194.2 10.5 %collective-permute-start.4 = (bf16[2,4,2,128,512]{4,3,2,1,0:T(8,128)(2,1)}, bf16[2,4,2,128,512]{4,3,2,1,0:T(8,128)(2,1)}, u32[]{:S(2)}, u32[]{:S(2)}) collective-permute-start(bf16[2,4,2,128,512]{4,3,2,1,0:T(8,128)(2,1)} %collective-permute-done.3.refs_4_.refs_12_), channel_id=1, source_target_pairs={{0,4},{4,0},{8,12},{12,8},{16,20},{20,16},{24,28},{28,24},{1,5},{5... | collective-permute-start | bytes 6291464 | tf_op jit(solution)/shard_map/ppermute | solution.py:401
  204.7 170.6 %all-gather.11.cloned.1.call-start = ((), (), s32[]{:S(2)}) async-start(), calls=%async_computation.5 | async-start | bytes 5242880 | tf_op jit(solution)/shard_map/all_gather | solution.py:545
  256.6 10.4 %collective-permute-start.9 = (bf16[256,512]{1,0:T(8,128)(2,1)}, bf16[256,512]{1,0:T(8,128)(2,1)}, u32[]{:S(2)}, u32[]{:S(2)}) collective-permute-start(bf16[256,512]{1,0:T(8,128)(2,1)} %get-tuple-element.232), channel_id=1, source_target_pairs={{0,1},{1,2},{2,3},{3,0},{4,5},{5,6},{6,7},{7,4},{8,9},{9,10},{10,1... | collective-permute-start | bytes 786440 | tf_op jit(solution)/shard_map/ppermute | solution.py:550
  259.4 21.4 %collective-permute-start.10 = (bf16[256,512]{1,0:T(8,128)(2,1)}, bf16[256,512]{1,0:T(8,128)(2,1)S(1)}, u32[]{:S(2)}, u32[]{:S(2)}) collective-permute-start(bf16[256,512]{1,0:T(8,128)(2,1)} %get-tuple-element.231), channel_id=1, source_target_pairs={{0,2},{1,3},{2,0},{3,1},{4,6},{5,7},{6,4},{7,5},{8,10},{9,11},{10,... | collective-permute-start | bytes 786440 | tf_op jit(solution)/shard_map/ppermute | solution.py:550
  262.8 18.7 %collective-permute-start.11 = (bf16[256,512]{1,0:T(8,128)(2,1)}, bf16[256,512]{1,0:T(8,128)(2,1)S(1)}, u32[]{:S(2)}, u32[]{:S(2)}) collective-permute-start(bf16[256,512]{1,0:T(8,128)(2,1)} %get-tuple-element.230), channel_id=1, source_target_pairs={{0,3},{1,0},{2,1},{3,2},{4,7},{5,4},{6,5},{7,6},{8,11},{9,8},{10,9... | collective-permute-start | bytes 786440 | tf_op jit(solution)/shard_map/ppermute | solution.py:550
  291.2 250.9 %reduce-scatter.4.cloned.1.call-start = ((), (), s32[]{:S(2)}) async-start(), calls=%async_computation.6 | async-start | bytes 5242880 | tf_op jit(solution)/shard_map/reduce_scatter | solution.py:573
  291.6 31.7 %collective-permute-start.16 = (bf16[1,4,2,128,640]{4,3,2,1,0:T(8,128)(2,1)S(1)}, bf16[1,4,2,128,640]{4,3,2,1,0:T(8,128)(2,1)S(1)}, u32[]{:S(2)}, u32[]{:S(2)}) collective-permute-start(bf16[1,4,2,128,640]{4,3,2,1,0:T(8,128)(2,1)S(1)} %bitcast.67), channel_id=1, source_target_pairs={{0,8},{4,12},{8,0},{12,4},{16,24},{20,28},{24,16},{28,20},{1,9},{5... | collective-permute-start | bytes 3932168 | tf_op jit(solution)/shard_map/ppermute | solution.py:401
  292.7 58.3 %collective-permute-start.18 = (bf16[1,4,2,128,640]{4,3,2,1,0:T(8,128)(2,1)S(1)}, bf16[1,4,2,128,640]{4,3,2,1,0:T(8,128)(2,1)}, u32[]{:S(2)}, u32[]{:S(2)}) collective-permute-start(bf16[1,4,2,128,640]{4,3,2,1,0:T(8,128)(2,1)S(1)} %bitcast.68), channel_id=1, source_target_pairs={{0,16},{4,20},{8,24},{12,28},{16,0},{20,4},{24,8},{28,12},{1,17},{... | collective-permute-start | bytes 3932168 | tf_op jit(solution)/shard_map/ppermute | solution.py:401
  294.8 57.0 %collective-permute-start.20 = (bf16[1,4,2,128,640]{4,3,2,1,0:T(8,128)(2,1)S(1)}, bf16[1,4,2,128,640]{4,3,2,1,0:T(8,128)(2,1)}, u32[]{:S(2)}, u32[]{:S(2)}) collective-permute-start(bf16[1,4,2,128,640]{4,3,2,1,0:T(8,128)(2,1)S(1)} %bitcast.69), channel_id=1, source_target_pairs={{0,24},{4,28},{8,16},{12,20},{16,8},{20,12},{24,0},{28,4},{1,25},{... | collective-permute-start | bytes 3932168 | tf_op jit(solution)/shard_map/ppermute | solution.py:401
  295.2 56.6 %collective-permute-start.15 = (bf16[1,4,2,128,640]{4,3,2,1,0:T(8,128)(2,1)S(1)}, bf16[1,4,2,128,640]{4,3,2,1,0:T(8,128)(2,1)}, u32[]{:S(2)}, u32[]{:S(2)}) collective-permute-start(bf16[1,4,2,128,640]{4,3,2,1,0:T(8,128)(2,1)S(1)} %bitcast.70), channel_id=1, source_target_pairs={{0,4},{4,0},{8,12},{12,8},{16,20},{20,16},{24,28},{28,24},{1,5},{5... | collective-permute-start | bytes 3932168 | tf_op jit(solution)/shard_map/ppermute | solution.py:401
  323.3 28.5 %collective-permute-start.17 = (bf16[1,4,2,128,640]{4,3,2,1,0:T(8,128)(2,1)S(1)}, bf16[1,4,2,128,640]{4,3,2,1,0:T(8,128)(2,1)}, u32[]{:S(2)}, u32[]{:S(2)}) collective-permute-start(bf16[1,4,2,128,640]{4,3,2,1,0:T(8,128)(2,1)S(1)} %collective-permute-done.16.refs_2_.refs_18_), channel_id=1, source_target_pairs={{0,4},{4,0},{8,12},{12,8},{16,20},{20,16},{24,28},{28,24},{1,5},{5... | collective-permute-start | bytes 3932168 | tf_op jit(solution)/shard_map/ppermute | solution.py:401
  435.6 19.2 %collective-permute-start.22 = (bf16[1024,2816]{1,0:T(8,128)(2,1)}, bf16[1024,2816]{1,0:T(8,128)(2,1)}, u32[]{:S(2)}, u32[]{:S(2)}) collective-permute-start(bf16[1024,2816]{1,0:T(8,128)(2,1)} %convolution_convert_fusion), channel_id=1, source_target_pairs={{0,4},{4,0},{8,12},{12,8},{16,20},{20,16},{24,28},{28,24},{1,5},{5... | collective-permute-start | bytes 17301512 | tf_op jit(solution)/shard_map/ppermute | solution.py:401
  435.6 348.0 %all-gather.13.cloned.1.call-start = ((), (), s32[]{:S(2)}) async-start(), calls=%async_computation.9 | async-start | bytes 5242880 | tf_op jit(solution)/shard_map/all_gather | solution.py:545
  450.9 14.4 %collective-permute-start.23 = (bf16[1408,1024]{1,0:T(8,128)(2,1)S(1)}, bf16[1408,1024]{1,0:T(8,128)(2,1)S(1)}, u32[]{:S(2)}, u32[]{:S(2)}) collective-permute-start(bf16[1408,1024]{1,0:T(8,128)(2,1)S(1)} %convolution_convert_fusion.3), channel_id=1, source_target_pairs={{0,4},{4,0},{8,12},{12,8},{16,20},{20,16},{24,28},{28,24},{1,5},{5... | collective-permute-start | bytes 8650760 | tf_op jit(solution)/shard_map/ppermute | solution.py:401
  466.5 33.8 %collective-permute-start.24 = (bf16[256,2816]{1,0:T(8,128)(2,1)}, bf16[256,2816]{1,0:T(8,128)(2,1)}, u32[]{:S(2)}, u32[]{:S(2)}) collective-permute-start(bf16[256,2816]{1,0:T(8,128)(2,1)} %constant_dynamic-slice_fusion.13), channel_id=1, source_target_pairs={{0,8},{4,12},{8,0},{12,4},{16,24},{20,28},{24,16},{28,20},{1,9},{5... | collective-permute-start | bytes 4325384 | tf_op jit(solution)/shard_map/ppermute | solution.py:401
  469.2 33.5 %collective-permute-start.25 = (bf16[256,2816]{1,0:T(8,128)(2,1)}, bf16[256,2816]{1,0:T(8,128)(2,1)}, u32[]{:S(2)}, u32[]{:S(2)}) collective-permute-start(bf16[256,2816]{1,0:T(8,128)(2,1)} %constant_dynamic-slice_fusion.12), channel_id=1, source_target_pairs={{0,16},{4,20},{8,24},{12,28},{16,0},{20,4},{24,8},{28,12},{1,17},{... | collective-permute-start | bytes 4325384 | tf_op jit(solution)/shard_map/ppermute | solution.py:401
  506.9 19.1 %collective-permute-start.28 = (bf16[352,1024]{1,0:T(8,128)(2,1)S(1)}, bf16[352,1024]{1,0:T(8,128)(2,1)S(1)}, u32[]{:S(2)}, u32[]{:S(2)}) collective-permute-start(bf16[352,1024]{1,0:T(8,128)(2,1)S(1)} %constant_dynamic-slice_fusion.9), channel_id=1, source_target_pairs={{0,8},{4,12},{8,0},{12,4},{16,24},{20,28},{24,16},{28,20},{1,9},{5... | collective-permute-start | bytes 2162696 | tf_op jit(solution)/shard_map/ppermute | solution.py:401
  507.7 19.5 %collective-permute-start.29 = (bf16[352,1024]{1,0:T(8,128)(2,1)S(1)}, bf16[352,1024]{1,0:T(8,128)(2,1)S(1)}, u32[]{:S(2)}, u32[]{:S(2)}) collective-permute-start(bf16[352,1024]{1,0:T(8,128)(2,1)S(1)} %constant_dynamic-slice_fusion.8), channel_id=1, source_target_pairs={{0,16},{4,20},{8,24},{12,28},{16,0},{20,4},{24,8},{28,12},{1,17},{... | collective-permute-start | bytes 2162696 | tf_op jit(solution)/shard_map/ppermute | solution.py:401
  509.3 30.7 %collective-permute-start.26 = (bf16[128,2816]{1,0:T(8,128)(2,1)S(1)}, bf16[128,2816]{1,0:T(8,128)(2,1)S(1)}, u32[]{:S(2)}, u32[]{:S(2)}) collective-permute-start(bf16[128,2816]{1,0:T(8,128)(2,1)S(1)} %constant_dynamic-slice_fusion.11), channel_id=1, source_target_pairs={{0,16},{4,20},{8,24},{12,28},{16,0},{20,4},{24,8},{28,12},{1,17},{... | collective-permute-start | bytes 2162696 | tf_op jit(solution)/shard_map/ppermute | solution.py:401
  509.9 31.1 %collective-permute-start.27 = (bf16[128,2816]{1,0:T(8,128)(2,1)S(1)}, bf16[128,2816]{1,0:T(8,128)(2,1)S(1)}, u32[]{:S(2)}, u32[]{:S(2)}) collective-permute-start(bf16[128,2816]{1,0:T(8,128)(2,1)S(1)} %constant_dynamic-slice_fusion.10), channel_id=1, source_target_pairs={{0,8},{4,12},{8,0},{12,4},{16,24},{20,28},{24,16},{28,20},{1,9},{5... | collective-permute-start | bytes 2162696 | tf_op jit(solution)/shard_map/ppermute | solution.py:401
  555.3 11.1 %collective-permute-start.30 = (bf16[256,512]{1,0:T(8,128)(2,1)S(1)}, bf16[256,512]{1,0:T(8,128)(2,1)S(1)}, u32[]{:S(2)}, u32[]{:S(2)}) collective-permute-start(bf16[256,512]{1,0:T(8,128)(2,1)S(1)} %get-tuple-element.228), channel_id=1, source_target_pairs={{0,1},{1,2},{2,3},{3,0},{4,5},{5,6},{6,7},{7,4},{8,9},{9,10},{10,1... | collective-permute-start | bytes 786440 | tf_op jit(solution)/shard_map/ppermute | solution.py:550
  555.4 19.2 %collective-permute-start.31 = (bf16[256,512]{1,0:T(8,128)(2,1)S(1)}, bf16[256,512]{1,0:T(8,128)(2,1)S(1)}, u32[]{:S(2)}, u32[]{:S(2)}) collective-permute-start(bf16[256,512]{1,0:T(8,128)(2,1)S(1)} %get-tuple-element.227), channel_id=1, source_target_pairs={{0,2},{1,3},{2,0},{3,1},{4,6},{5,7},{6,4},{7,5},{8,10},{9,11},{10,... | collective-permute-start | bytes 786440 | tf_op jit(solution)/shard_map/ppermute | solution.py:550
  557.1 17.6 %collective-permute-start.32 = (bf16[256,512]{1,0:T(8,128)(2,1)S(1)}, bf16[256,512]{1,0:T(8,128)(2,1)S(1)}, u32[]{:S(2)}, u32[]{:S(2)}) collective-permute-start(bf16[256,512]{1,0:T(8,128)(2,1)S(1)} %get-tuple-element.226), channel_id=1, source_target_pairs={{0,3},{1,0},{2,1},{3,2},{4,7},{5,4},{6,5},{7,6},{8,11},{9,8},{10,9... | collective-permute-start | bytes 786440 | tf_op jit(solution)/shard_map/ppermute | solution.py:550
  574.7 353.7 %reduce-scatter.6.cloned.1.call-start = ((), (), s32[]{:S(2)}) async-start(), calls=%async_computation.7 | async-start | bytes 5242880 | tf_op jit(solution)/shard_map/reduce_scatter | solution.py:573
  574.8 19.5 %collective-permute-start.33 = (bf16[128,2816]{1,0:T(8,128)(2,1)}, bf16[128,2816]{1,0:T(8,128)(2,1)}, u32[]{:S(2)}, u32[]{:S(2)}) collective-permute-start(bf16[128,2816]{1,0:T(8,128)(2,1)} %add_convert_fusion.13), channel_id=1, source_target_pairs={{0,16},{4,20},{8,24},{12,28},{16,0},{20,4},{24,8},{28,12},{1,17},{... | collective-permute-start | bytes 2162696 | tf_op jit(solution)/shard_map/ppermute | solution.py:401
  576.2 19.4 %collective-permute-start.34 = (bf16[128,2816]{1,0:T(8,128)(2,1)}, bf16[128,2816]{1,0:T(8,128)(2,1)}, u32[]{:S(2)}, u32[]{:S(2)}) collective-permute-start(bf16[128,2816]{1,0:T(8,128)(2,1)} %add_convert_fusion.12), channel_id=1, source_target_pairs={{0,8},{4,12},{8,0},{12,4},{16,24},{20,28},{24,16},{28,20},{1,9},{5... | collective-permute-start | bytes 2162696 | tf_op jit(solution)/shard_map/ppermute | solution.py:401
  579.0 20.0 %collective-permute-start.35 = (bf16[176,1024]{1,0:T(8,128)(2,1)}, bf16[176,1024]{1,0:T(8,128)(2,1)}, u32[]{:S(2)}, u32[]{:S(2)}) collective-permute-start(bf16[176,1024]{1,0:T(8,128)(2,1)} %constant_dynamic-slice_fusion.4), channel_id=1, source_target_pairs={{0,16},{4,20},{8,24},{12,28},{16,0},{20,4},{24,8},{28,12},{1,17},{... | collective-permute-start | bytes 1081352 | tf_op jit(solution)/shard_map/ppermute | solution.py:401
  581.3 18.8 %collective-permute-start.36 = (bf16[176,1024]{1,0:T(8,128)(2,1)}, bf16[176,1024]{1,0:T(8,128)(2,1)}, u32[]{:S(2)}, u32[]{:S(2)}) collective-permute-start(bf16[176,1024]{1,0:T(8,128)(2,1)} %constant_dynamic-slice_fusion.3), channel_id=1, source_target_pairs={{0,8},{4,12},{8,0},{12,4},{16,24},{20,28},{24,16},{28,20},{1,9},{5... | collective-permute-start | bytes 1081352 | tf_op jit(solution)/shard_map/ppermute | solution.py:401
  613.9 63.4 %collective-permute-start.37 = (bf16[1,4,2,128,640]{4,3,2,1,0:T(8,128)(2,1)S(1)}, bf16[1,4,2,128,640]{4,3,2,1,0:T(8,128)(2,1)}, u32[]{:S(2)}, u32[]{:S(2)}) collective-permute-start(bf16[1,4,2,128,640]{4,3,2,1,0:T(8,128)(2,1)S(1)} %bitcast.75), channel_id=1, source_target_pairs={{0,4},{4,0},{8,12},{12,8},{16,20},{20,16},{24,28},{28,24},{1,5},{5... | collective-permute-start | bytes 3932168 | tf_op jit(solution)/shard_map/ppermute | solution.py:401
  613.9 57.3 %collective-permute-start.38 = (bf16[1,4,2,128,640]{4,3,2,1,0:T(8,128)(2,1)S(1)}, bf16[1,4,2,128,640]{4,3,2,1,0:T(8,128)(2,1)}, u32[]{:S(2)}, u32[]{:S(2)}) collective-permute-start(bf16[1,4,2,128,640]{4,3,2,1,0:T(8,128)(2,1)S(1)} %bitcast.76), channel_id=1, source_target_pairs={{0,8},{4,12},{8,0},{12,4},{16,24},{20,28},{24,16},{28,20},{1,9},{5... | collective-permute-start | bytes 3932168 | tf_op jit(solution)/shard_map/ppermute | solution.py:401
  615.0 61.7 %collective-permute-start.40 = (bf16[1,4,2,128,640]{4,3,2,1,0:T(8,128)(2,1)S(1)}, bf16[1,4,2,128,640]{4,3,2,1,0:T(8,128)(2,1)}, u32[]{:S(2)}, u32[]{:S(2)}) collective-permute-start(bf16[1,4,2,128,640]{4,3,2,1,0:T(8,128)(2,1)S(1)} %bitcast.77), channel_id=1, source_target_pairs={{0,16},{4,20},{8,24},{12,28},{16,0},{20,4},{24,8},{28,12},{1,17},{... | collective-permute-start | bytes 3932168 | tf_op jit(solution)/shard_map/ppermute | solution.py:401
  615.6 61.3 %collective-permute-start.42 = (bf16[1,4,2,128,640]{4,3,2,1,0:T(8,128)(2,1)S(1)}, bf16[1,4,2,128,640]{4,3,2,1,0:T(8,128)(2,1)}, u32[]{:S(2)}, u32[]{:S(2)}) collective-permute-start(bf16[1,4,2,128,640]{4,3,2,1,0:T(8,128)(2,1)S(1)} %bitcast.78), channel_id=1, source_target_pairs={{0,24},{4,28},{8,16},{12,20},{16,8},{20,12},{24,0},{28,4},{1,25},{... | collective-permute-start | bytes 3932168 | tf_op jit(solution)/shard_map/ppermute | solution.py:401
  677.3 261.6 %all-reduce.3.cloned.1.call-start = ((), (), s32[]{:S(2)}) async-start(), calls=%async_computation.10 | async-start | bytes 4194304 | tf_op jit(solution)/shard_map/psum | solution.py:741
  683.5 36.0 %collective-permute-start.44 = (bf16[176,1024]{1,0:T(8,128)(2,1)}, bf16[176,1024]{1,0:T(8,128)(2,1)S(1)}, u32[]{:S(2)}, u32[]{:S(2)}) collective-permute-start(bf16[176,1024]{1,0:T(8,128)(2,1)} %add_convert_fusion.17), channel_id=1, source_target_pairs={{0,16},{4,20},{8,24},{12,28},{16,0},{20,4},{24,8},{28,12},{1,17},{... | collective-permute-start | bytes 1081352 | tf_op jit(solution)/shard_map/ppermute | solution.py:401
  683.5 36.0 %collective-permute-start.45 = (bf16[176,1024]{1,0:T(8,128)(2,1)}, bf16[176,1024]{1,0:T(8,128)(2,1)S(1)}, u32[]{:S(2)}, u32[]{:S(2)}) collective-permute-start(bf16[176,1024]{1,0:T(8,128)(2,1)} %add_convert_fusion.16), channel_id=1, source_target_pairs={{0,8},{4,12},{8,0},{12,4},{16,24},{20,28},{24,16},{28,20},{1,9},{5... | collective-permute-start | bytes 1081352 | tf_op jit(solution)/shard_map/ppermute | solution.py:401
  687.3 89.5 %collective-permute-start.54 = (bf16[256,2816]{1,0:T(8,128)(2,1)}, bf16[256,2816]{1,0:T(8,128)(2,1)}, u32[]{:S(2)}, u32[]{:S(2)}) collective-permute-start(bf16[256,2816]{1,0:T(8,128)(2,1)} %maximum_select_fusion.4), channel_id=1, source_target_pairs={{0,8},{4,12},{8,0},{12,4},{16,24},{20,28},{24,16},{28,20},{1,9},{5... | collective-permute-start | bytes 4325384 | tf_op jit(solution)/shard_map/ppermute | solution.py:401
  687.4 89.4 %collective-permute-start.55 = (bf16[256,2816]{1,0:T(8,128)(2,1)}, bf16[256,2816]{1,0:T(8,128)(2,1)}, u32[]{:S(2)}, u32[]{:S(2)}) collective-permute-start(bf16[256,2816]{1,0:T(8,128)(2,1)} %maximum_select_fusion.5), channel_id=1, source_target_pairs={{0,16},{4,20},{8,24},{12,28},{16,0},{20,4},{24,8},{28,12},{1,17},{... | collective-permute-start | bytes 4325384 | tf_op jit(solution)/shard_map/ppermute | solution.py:401
  791.3 9.7 collective-permute-start.46
  794.7 32.5 %collective-permute-start.56 = (bf16[1024,2816]{1,0:T(8,128)(2,1)}, bf16[1024,2816]{1,0:T(8,128)(2,1)}, u32[]{:S(2)}, u32[]{:S(2)}) collective-permute-start(bf16[1024,2816]{1,0:T(8,128)(2,1)} %pad_maximum_fusion.half_ref), channel_id=1, source_target_pairs={{0,4},{4,0},{8,12},{12,8},{16,20},{20,16},{24,28},{28,24},{1,5},{5... | collective-permute-start | bytes 17301512 | tf_op jit(solution)/shard_map/ppermute | solution.py:401
  794.8 23.1 %collective-permute-start.59 = (bf16[352,1024]{1,0:T(8,128)(2,1)S(1)}, bf16[352,1024]{1,0:T(8,128)(2,1)S(1)}, u32[]{:S(2)}, u32[]{:S(2)}) collective-permute-start(bf16[352,1024]{1,0:T(8,128)(2,1)S(1)} %copy-done.52), channel_id=1, source_target_pairs={{0,8},{4,12},{8,0},{12,4},{16,24},{20,28},{24,16},{28,20},{1,9},{5... | collective-permute-start | bytes 2162696 | tf_op jit(solution)/shard_map/ppermute | solution.py:401
  800.9 19.0 %collective-permute-start.60 = (bf16[352,1024]{1,0:T(8,128)(2,1)S(1)}, bf16[352,1024]{1,0:T(8,128)(2,1)S(1)}, u32[]{:S(2)}, u32[]{:S(2)}) collective-permute-start(bf16[352,1024]{1,0:T(8,128)(2,1)S(1)} %copy-done.53), channel_id=1, source_target_pairs={{0,16},{4,20},{8,24},{12,28},{16,0},{20,4},{24,8},{28,12},{1,17},{... | collective-permute-start | bytes 2162696 | tf_op jit(solution)/shard_map/ppermute | solution.py:401
  807.4 33.2 %collective-permute-start.52 = (bf16[256,1536]{1,0:T(8,128)(2,1)}, bf16[256,1536]{1,0:T(8,128)(2,1)S(1)}, u32[]{:S(2)}, u32[]{:S(2)}) collective-permute-start(bf16[256,1536]{1,0:T(8,128)(2,1)} %constant_dynamic-slice_fusion.2), channel_id=1, source_target_pairs={{0,8},{4,12},{8,0},{12,4},{16,24},{20,28},{24,16},{28,20},{1,9},{5... | collective-permute-start | bytes 2359304 | tf_op jit(solution)/shard_map/ppermute | solution.py:401
  810.6 30.0 %collective-permute-start.53 = (bf16[256,1536]{1,0:T(8,128)(2,1)}, bf16[256,1536]{1,0:T(8,128)(2,1)S(1)}, u32[]{:S(2)}, u32[]{:S(2)}) collective-permute-start(bf16[256,1536]{1,0:T(8,128)(2,1)} %constant_dynamic-slice_fusion.1), channel_id=1, source_target_pairs={{0,16},{4,20},{8,24},{12,28},{16,0},{20,4},{24,8},{28,12},{1,17},{... | collective-permute-start | bytes 2359304 | tf_op jit(solution)/shard_map/ppermute | solution.py:401
  841.8 156.0 %reduce-scatter.8.cloned.1.call-start = ((), (), s32[]{:S(2)}) async-start(), calls=%async_computation.8 | async-start | bytes 5242880 | tf_op jit(solution)/shard_map/reduce_scatter | solution.py:573
  845.7 19.4 %collective-permute-start.57 = (bf16[128,1536]{1,0:T(8,128)(2,1)S(1)}, bf16[128,1536]{1,0:T(8,128)(2,1)S(1)}, u32[]{:S(2)}, u32[]{:S(2)}) collective-permute-start(bf16[128,1536]{1,0:T(8,128)(2,1)S(1)} %constant_dynamic-slice_fusion), channel_id=1, source_target_pairs={{0,16},{4,20},{8,24},{12,28},{16,0},{20,4},{24,8},{28,12},{1,17},{... | collective-permute-start | bytes 1179656 | tf_op jit(solution)/shard_map/ppermute | solution.py:401
  846.3 20.0 %collective-permute-start.58 = (bf16[128,1536]{1,0:T(8,128)(2,1)S(1)}, bf16[128,1536]{1,0:T(8,128)(2,1)S(1)}, u32[]{:S(2)}, u32[]{:S(2)}) collective-permute-start(bf16[128,1536]{1,0:T(8,128)(2,1)S(1)} %constant_dynamic-slice_fusion.19), channel_id=1, source_target_pairs={{0,8},{4,12},{8,0},{12,4},{16,24},{20,28},{24,16},{28,20},{1,9},{5... | collective-permute-start | bytes 1179656 | tf_op jit(solution)/shard_map/ppermute | solution.py:401
  866.4 13.0 %collective-permute-start.62 = (bf16[128,1536]{1,0:T(8,128)(2,1)S(1)}, bf16[128,1536]{1,0:T(8,128)(2,1)S(1)}, u32[]{:S(2)}, u32[]{:S(2)}) collective-permute-start(bf16[128,1536]{1,0:T(8,128)(2,1)S(1)} %add_convert_fusion.15), channel_id=1, source_target_pairs={{0,16},{4,20},{8,24},{12,28},{16,0},{20,4},{24,8},{28,12},{1,17},{... | collective-permute-start | bytes 1179656 | tf_op jit(solution)/shard_map/ppermute | solution.py:401
  868.1 13.4 %collective-permute-start.63 = (bf16[128,1536]{1,0:T(8,128)(2,1)S(1)}, bf16[128,1536]{1,0:T(8,128)(2,1)S(1)}, u32[]{:S(2)}, u32[]{:S(2)}) collective-permute-start(bf16[128,1536]{1,0:T(8,128)(2,1)S(1)} %add_convert_fusion.14), channel_id=1, source_target_pairs={{0,8},{4,12},{8,0},{12,4},{16,24},{20,28},{24,16},{28,20},{1,9},{5... | collective-permute-start | bytes 1179656 | tf_op jit(solution)/shard_map/ppermute | solution.py:401
  881.7 17.8 %collective-permute-start.65 = (bf16[256,1536]{1,0:T(8,128)(2,1)S(1)}, bf16[256,1536]{1,0:T(8,128)(2,1)S(1)}, u32[]{:S(2)}, u32[]{:S(2)}) collective-permute-start(bf16[256,1536]{1,0:T(8,128)(2,1)S(1)} %maximum_select_fusion.9), channel_id=1, source_target_pairs={{0,16},{4,20},{8,24},{12,28},{16,0},{20,4},{24,8},{28,12},{1,17},{... | collective-permute-start | bytes 2359304 | tf_op jit(solution)/shard_map/ppermute | solution.py:401
  882.1 18.5 %collective-permute-start.64 = (bf16[256,1536]{1,0:T(8,128)(2,1)S(1)}, bf16[256,1536]{1,0:T(8,128)(2,1)S(1)}, u32[]{:S(2)}, u32[]{:S(2)}) collective-permute-start(bf16[256,1536]{1,0:T(8,128)(2,1)S(1)} %maximum_select_fusion.8), channel_id=1, source_target_pairs={{0,8},{4,12},{8,0},{12,4},{16,24},{20,28},{24,16},{28,20},{1,9},{5... | collective-permute-start | bytes 2359304 | tf_op jit(solution)/shard_map/ppermute | solution.py:401
  903.1 100.0 %collective-permute-start.66 = (bf16[1024,1536]{1,0:T(8,128)(2,1)}, bf16[1024,1536]{1,0:T(8,128)(2,1)}, u32[]{:S(2)}, u32[]{:S(2)}) collective-permute-start(bf16[1024,1536]{1,0:T(8,128)(2,1)} %pad_maximum_fusion.1.half_ref), channel_id=1, source_target_pairs={{0,4},{4,0},{8,12},{12,8},{16,20},{20,16},{24,28},{28,24},{1,5},{5... | collective-permute-start | bytes 9437192 | tf_op jit(solution)/shard_map/ppermute | solution.py:401
  925.1 10.0 collective-permute-start.51
  (100 other events, 1444.5 us)
Sparse Core Ops, SparseCore 0:
  12.7 83.4 all-gather.6
  97.8 95.4 all-gather.8
  204.8 57.8 all-gather.14
  291.3 83.9 all-gather.10
  435.7 75.4 reduce-scatter.3
  574.8 83.4 all-gather.12
  677.5 81.6 reduce-scatter.5
  840.8 76.8 all-reduce.2
  920.6 77.1 reduce-scatter.7

commit v8 on v7

--- a/solution.py
+++ b/solution.py
@@ -161,17 +161,16 @@
         dq_ref[0, rows, :] = turn(grad, c_ref[rows], a_ref[rows], b_ref[rows], -1.0).astype(jnp.bfloat16)
 
 
-def dkv_kernel(place_ref, own_ref, k_ref, v_ref, c_ref, a_ref, b_ref, *refs, blocks, n, lead):
-    q_refs, do_refs, qx_refs, dox_refs = (refs[i * n:(i + 1) * n] for i in range(4))
-    dk_ref, dv_ref, qs, dos, acck, accv = refs[4 * n:]
+def dkv_kernel(place_ref, own_ref, slots_ref, k_ref, v_ref, c_ref, a_ref, b_ref, *refs, blocks, n, lead):
+    q_refs, qx_refs, (do_ref, dox_ref, dk_ref, dv_ref, qs, dos, acck, accv) = refs[:n], refs[n:2 * n], refs[2 * n:]
     s, pair = pl.program_id(0) + lead, pl.program_id(1)
     place_rows(place_ref, s, q_refs, qs)
-    place_rows(place_ref, s, do_refs, dos)
+    place_rows(slots_ref, s, [do_ref], dos)
 
     @pl.when(pair == 0)
     def _():
         place_rows(place_ref, s, qx_refs, qs, 128)
-        place_rows(place_ref, s, dox_refs, dos, 128)
+        place_rows(slots_ref, s, [dox_ref], dos, 128)
 
     ones = own_lanes(pair).astype(jnp.bfloat16)
     for w in range(2):
@@ -213,16 +212,16 @@
     return pl.BlockSpec((2 * BLK, 128), lambda s, h, *_: (s + lead, 0))
 
 
-def piece(x, first=0, lane=None, lead=0):
-    return pl.BlockSpec((1, 1, 2, BLK, 128), lambda s, h, *_: (first, s + lead, 0, 0, h if lane is None else lane))
-
-
-def attention_call(kernel, name, mats, seqs, pairs, blocks, in_specs, out_specs, out_shape, scratch, args):
+def piece(x, first=0, lane=None, lead=0, count=1):
+    return pl.BlockSpec((count, 1, 2, BLK, 128), lambda s, h, *_: (first, s + lead, 0, 0, h if lane is None else lane))
+
+
+def attention_call(kernel, name, mats, seqs, pairs, blocks, in_specs, out_specs, out_shape, scratch, args, prefetch=2):
     work = seqs * pairs * 2 * 2 * BLK * blocks * BLK // 2
     return pl.pallas_call(
         kernel,
         grid_spec=pltpu.PrefetchScalarGridSpec(
-            num_scalar_prefetch=2, grid=(seqs, pairs), in_specs=in_specs, out_specs=out_specs, scratch_shapes=scratch),
+            num_scalar_prefetch=prefetch, grid=(seqs, pairs), in_specs=in_specs, out_specs=out_specs, scratch_shapes=scratch),
         out_shape=out_shape,
         compiler_params=pltpu.CompilerParams(vmem_limit_bytes=40 * 2**20),
         cost_estimate=pl.CostEstimate(flops=work * 512 * mats, bytes_accessed=4 * seqs * pairs * blocks * BLK * 128, transcendentals=work),
@@ -258,21 +257,22 @@
         [place, own, q, do, q_ext, do_ext, *tabs] + [e[0] for e in keys + values])
 
 
-def key_value_grad(place, own, kv, tabs, queries, grads, lead, count):
+def key_value_grad(place, own, slots, kv, tabs, queries, grads, lead, count):
     pairs, blocks = kv.shape[3] // 128, place.shape[1]
     shape = (count,) + kv.shape[2:]
-    both = queries + grads
+    n = grads.shape[0]
 
     def own_part(i):
         return pl.BlockSpec((1, 1, 2 * BLK, 128), lambda s, h, *_: (i, s + lead, 0, h))
 
     return attention_call(
         functools.partial(dkv_kernel, blocks=blocks, n=len(queries), lead=lead), "key_value_grad", 4, count, pairs, blocks,
-        [own_part(0), own_part(1)] + [table(lead)] * 3 + [piece(x, lead=lead) for x in both]
-        + [piece(x, lane=pairs, lead=lead) for x in both], [OWN, OWN],
+        [own_part(0), own_part(1)] + [table(lead)] * 3 + [piece(x, lead=lead) for x in queries]
+        + [piece(x, lane=pairs, lead=lead) for x in queries]
+        + [piece(grads, lead=lead, count=n), piece(grads, lane=pairs, lead=lead, count=n)], [OWN, OWN],
         [jax.ShapeDtypeStruct(shape, jnp.bfloat16)] * 2,
         [rows_of(blocks, 256), rows_of(blocks, 256), acc_of(128), acc_of(128)],
-        [place, own, kv, kv, *tabs] + both * 2)
+        [place, own, slots, kv, kv, *tabs] + queries * 2 + [grads] * 2, prefetch=3)
 
 
 import math
@@ -472,12 +472,15 @@
         take(chain)
 
 
-def unpack_rows_kernel(core_ref, half_ref, other_ref, *out_refs):
+def unpack_rows_kernel(core_ref, half_ref, other_ref, *out_refs, turned):
     def put(src):
         at = 0
-        for out in out_refs:
-            out[...] = src[:, at:at + out.shape[1]].astype(F32)
-            at += out.shape[1]
+        for i, out in enumerate(out_refs):
+            if turned and i == len(out_refs) - 1:
+                out[...] = src[:, at:].astype(F32).T
+            else:
+                out[...] = src[:, at:at + out.shape[1]].astype(F32)
+                at += out.shape[1]
 
     @pl.when(pl.program_id(0) == core_ref[0])
     def _():
@@ -488,10 +491,11 @@
         put(other_ref)
 
 
-def unpack_rows(half, other, parts):
+def unpack_rows(half, other, parts, turned=False):
     r, c = half.shape
     step = math.gcd(r, 256)
     blocks = r // step
+    w = c // parts
     core = lax.axis_index("ctx") & 1
 
     def mine(i, j, core_ref):
@@ -500,13 +504,17 @@
     def theirs(i, j, core_ref):
         return jnp.where(i != core_ref[0], j, jnp.where(core_ref[0] == 1, blocks - 1, 0)), 0
 
+    specs = [pl.BlockSpec((step, w), lambda i, j, _: (i * blocks + j, 0))] * parts
+    shapes = [jax.ShapeDtypeStruct((2 * r, w), F32)] * parts
+    if turned:
+        specs[-1] = pl.BlockSpec((w, step), lambda i, j, _: (0, i * blocks + j))
+        shapes[-1] = jax.ShapeDtypeStruct((w, 2 * r), F32)
     return pl.pallas_call(
-        unpack_rows_kernel,
+        functools.partial(unpack_rows_kernel, turned=turned),
         grid_spec=pltpu.PrefetchScalarGridSpec(
             num_scalar_prefetch=1, grid=(2, blocks),
-            in_specs=[pl.BlockSpec((step, c), mine), pl.BlockSpec((step, c), theirs)],
-            out_specs=[pl.BlockSpec((step, c // parts), lambda i, j, _: (i * blocks + j, 0))] * parts),
-        out_shape=[jax.ShapeDtypeStruct((2 * r, c // parts), F32)] * parts,
+            in_specs=[pl.BlockSpec((step, c), mine), pl.BlockSpec((step, c), theirs)], out_specs=specs),
+        out_shape=shapes,
         compiler_params=pltpu.CompilerParams(vmem_limit_bytes=40 * 2**20),
         cost_estimate=pl.CostEstimate(flops=0, bytes_accessed=12 * r * c, transcendentals=0),
         name="unpack_rows",
@@ -679,7 +687,7 @@
     held = take(gu)
     go(gu)
     down = nn(after(act, held), down_w).astype(BF16)
-    held = take(dw, held), take(gu, down)
+    held = take(dw), take(gu, down)
     go(gu)
     go(dw, held)
     grad_two = after(grad_two, held)
@@ -688,37 +696,38 @@
     grad_mixed = cotangent.astype(F32) + norm_two
     branch_own = grad_mixed.astype(BF16)
     grad_attn = nt(branch_own, whole_w).astype(BF16)
-    grad_attn = after(grad_attn, take(gu), take(dw))
+    grad_attn = after(grad_attn, take(gu, grad_attn), take(dw, grad_attn))
     go(gu)
     go(dw)
     grad_attn = exchange(grad_attn, 1, 0)
-    branch = all_rows(after(branch_own, grad_attn))
-    out_tokens = (mixed + sum_rows(after(down, grad_attn)).astype(F32)).astype(BF16)
     lane = jnp.arange(128)[None, :]
     ind = ((jnp.arange(width) // HEAD_DIM)[:, None] == lane // 3).astype(F32)
     delta = lax.dot_general(grad_attn.astype(F32) * attn_rows.astype(F32), ind, (((1,), (0,)), ((), ())),
                             precision=lax.Precision.HIGHEST, preferred_element_type=F32)
     do_ext = terms(-delta, lane).astype(BF16)
     do_sent = jnp.concatenate([grad_attn, do_ext], axis=1).reshape(shape)
-    grads = gather_other(after(do_sent, take(gu, grad_attn), take(dw, grad_attn)))
+    grads = lax.all_gather(do_sent, "ctx", axis=0, tiled=True)
     grad_q = query_grad(place, own, q, grad_attn.reshape(q.shape), q_ext, do_ext.reshape(q_ext.shape), tabs, keys, values)
     grad_q = grad_q.reshape(-1, width)
     q_part = nt(grad_q, query_w)
-    grads = gather_cores(grads, q_part)
-    go(gu, grads)
-    go(dw, grads)
-    first = key_value_grad(place, own, kv, tabs, queries, grads, 0, SEQS // 2)
+    held = take(gu, q_part), take(dw, q_part)
+    go(gu)
+    go(dw)
+    grads = after(grads, held)
+    branch = all_rows(after(branch_own, grads))
+    first = key_value_grad(place, own, block_order, kv, tabs, queries, grads, 0, SEQS // 2)
     grads = after(grads, take(dw, first))
     go(dw)
-    second = key_value_grad(place, own, kv, tabs, queries, grads, SEQS // 2, SEQS // 2)
+    second = key_value_grad(place, own, block_order, kv, tabs, queries, grads, SEQS // 2, SEQS // 2)
     grad_k, grad_v = (jnp.concatenate(pair).reshape(-1, width) for pair in zip(first, second))
     part_one = q_part + nt(grad_k, key_w) + nt(grad_v, value_w)
-    part_sent = part_one.astype(BF16)
+    part_sent = after(part_one.astype(BF16), branch)
     grad_one = sum_rows(part_sent)
+    out_tokens = (mixed + sum_rows(after(down, grad_one)).astype(F32)).astype(BF16)
 
     rows_one, branch, grad_q, grad_k, grad_v = after((rows_one, branch, grad_q, grad_k, grad_v), part_sent)
     grad_qkv = jnp.concatenate([grad_q, grad_k, grad_v], axis=1)
-    chain = begin(lambda core: rc(columns(rows_one, core), grad_qkv))
+    chain = begin(lambda core: jnp.concatenate([rc(columns(rows_one, core), grad_qkv), rc(columns(branch, core), attn_rows)], axis=1))
     take(gu, part_sent)
     take_extra(gu)
     go(gu)
@@ -728,17 +737,17 @@
     small = jnp.concatenate([
         jnp.sum(part_one * unit_rows, axis=0), jnp.sum(part_one, axis=0), grad_gain_two, grad_shift_two,
         jnp.where(tp_row, bias_grad[None, :], 0.0).reshape(-1)])
+    sums = sum_over_all(small.reshape(-1, 1024))
+    for _ in range(9):
+        small = next(sums)
     held = take(chain)
     go(chain)
-    take(dw, held)
+    take(dw, (held, small))
     take_extra(dw)
     go(dw)
-    grad_output_w = rc(attn_rows, after(branch, held)).astype(BF16)
-    sums = sum_over_all(after(small, held).reshape(-1, 1024))
     grad_gate_w, grad_up_w = unpack_rows(*take(gu, held), 2)
-    held = take(chain, (grad_gate_w, grad_output_w))
+    held = take(chain, grad_gate_w)
     go(chain)
-    grad_output_w = lax.psum(grad_output_w, "ctx")
     grad_down_w = unpack_cols(*take(dw, held))
     held = take(chain, grad_down_w)
     go(chain)
@@ -747,14 +756,11 @@
     take(chain)
     take_extra(chain)
     go(chain)
-    for _ in range(9):
-        small = next(sums)
     depth = x.shape[1]
     small = small.reshape(-1)
     norms = small[:4 * depth].reshape(4, depth)
     bias_sum = jnp.sum(jnp.where(tp_row, small[4 * depth:].reshape(n_tp, -1), 0.0), axis=0)
-    grad_query_w, grad_key_w, grad_value_w = unpack_rows(*take(chain), 3)
-    grad_output_w = grad_output_w.astype(F32)
+    grad_query_w, grad_key_w, grad_value_w, grad_output_w = unpack_rows(*take(chain), 4, True)
     norm_one, _, _ = layer_back(grad_one.astype(F32), unit_one, inverse_one, gain_one)
     grad_tokens = (grad_mixed + norm_one).astype(BF16)
     return (

time: 1030 us -> 961 us (0.933)
  waiting for transfers between devices: 458 us -> 377 us
  starting transfers between devices: 86.3 us -> 73.6 us
  local copies, waits for them, and re-layouts: 42.6 us -> 54.3 us
    reduce_scatter x3, waiting for transfers between devices: 54.6 us -> 4.84 us  [sum_rows(): return lax.psum_scatter(x, 'tp', scatter_dimension=0, tiled=True)]
    ppermute x53 -> x46, waiting for transfers between devices: 229 us -> 191 us  [ctx_swap(): return lax.ppermute(x, 'ctx', [(i, i ^ mask) for i in range(n)])]
    ppermute x5, starting transfers between devices: 13.1 us -> 23.4 us  [sum_over_all(): x = x + lax.ppermute(x, axis, [(i, i ^ 1 << bit) for i in range(n)])]
    ppermute x53 -> x46, starting transfers between devices: 49.1 us -> 38.9 us  [ctx_swap(): return lax.ppermute(x, 'ctx', [(i, i ^ mask) for i in range(n)])]
    dot_general x7 -> x8, matrix products: 44.1 us -> 47.4 us  [rc(): lax.dot_general(left, right, (((0,), (0,)), ((), ())), preferred_element_...]
  transfers between devices with their start and end apart: 76 -> 69, of which waited for: 42 -> 30; matrix products, arithmetic and copies ran while one was open for 15% -> 17% of each run, Pallas kernels for 19% -> 22%
where the time goes in v8:
time: 961 us; the launch traced here: 952 us
  waiting for transfers between devices  377 us (39%)
  Pallas kernels  242 us (25%)
  matrix products  113 us (12%)
  other arithmetic  76.6 us (8%)
  starting transfers between devices  73.6 us (8%)
  local copies, waits for them, and re-layouts  54.3 us (6%)
  between operations  15.5 us (2%)
    ppermute x46, waiting for transfers between devices, ctx_swap(): return lax.ppermute(x, 'ctx', [(i, i ^ mask) for i in range(n)])  191 us
    pallas_call x4, Pallas kernels, attention_call(): pl.pallas_call(kernel, grid_spec=pltpu.PrefetchScalarGridSpec(num_scalar_...  168 us
    all_gather x4, waiting for transfers between devices, all_rows(): return lax.all_gather(x, 'tp', axis=0, tiled=True)  102 us
    dot_general x6, matrix products, nt(): lax.dot_general(a, b, (((1,), (1,)), ((), ())), preferred_element_type=jn...  49.5 us
    dot_general x8, matrix products, rc(): lax.dot_general(left, right, (((0,), (0,)), ((), ())), preferred_element_...  47.4 us
    ppermute x46, starting transfers between devices, ctx_swap(): return lax.ppermute(x, 'ctx', [(i, i ^ mask) for i in range(n)])  38.9 us
    ppermute x6, waiting for transfers between devices, tp_shift(): return lax.ppermute(x, 'tp', [(i, (i + d) % n) for i in range(n)])  31.4 us
    ppermute x3, waiting for transfers between devices, gather_tp(): lax.ppermute(x, 'tp', [(i, (i + d) % n) for i in range(n)])  29.9 us
  transfers between devices with their start and end apart: 69, of which 30 were waited for; matrix products, arithmetic and copies ran while one was open for 17% of the time, Pallas kernels for 22%

profile of v8, /device:TPU:0, one launch (start us, length us, event | category | flops | bytes accessed | tf_op | source)
XLA Modules:
  0.0 951.7 jit_solution(18235907257903017533)
XLA Ops:
  12.2 83.6 %all-gather.8.cloned.1.call-done.h_ref = bf16[1024,2048]{1,0:T(8,128)(2,1)} async-done(((bf16[256,2048]{1,0:T(8,128)(2,1)}), bf16[1024,2048]{1,0:T(8,128)(2,1)}) %all-gather.8.cloned.1.call-update) | async-done | bytes 4194320 | tf_op jit(solution)/shard_map/all_gather | solution.py:553
  98.0 11.6 %project.1 = (bf16[4,256,512]{2,1,0:T(8,128)(2,1)S(1)}, bf16[2,4,256,512]{3,2,1,0:T(8,128)(2,1)}) custom-call(bf16[1024,2048]{1,0:T(8,128)(2,1)} %all-gather.8.cloned.1.call-done.h_ref, bf16[2048,512]{1,0:T(8,128)(2,1)} %wq_ref.1, bf16[2048,512]{1,0:T(8,128)(2,1)} %wk_ref.1, bf16[2048,512]{1,0:T(8,128)(2,1)} %wv_ref.1, ...), custom_call_target="tpu_custom_call" | custom-call | flops 6442450944 | bytes 6291456 | tf_op jit(solution)/shard_map/project/pallas_call | solution.py:345
  113.6 44.7 %collective-permute-done.3.refs_4_.refs_12_ = bf16[2,4,2,128,512]{4,3,2,1,0:T(8,128)(2,1)} collective-permute-done((bf16[2,4,2,128,512]{4,3,2,1,0:T(8,128)(2,1)}, bf16[2,4,2,128,512]{4,3,2,1,0:T(8,128)(2,1)}, u32[]{:S(2)}, u32[]{:S(2)}) %collective-permute-start.3) | collective-permute-done | bytes 2097184 | tf_op jit(solution)/shard_map/ppermute | solution.py:401
  168.8 10.1 %collective-permute-done.14 = bf16[64,2048]{1,0:T(8,128)(2,1)S(1)} collective-permute-done((bf16[64,2048]{1,0:T(8,128)(2,1)S(1)}, bf16[64,2048]{1,0:T(8,128)(2,1)S(1)}, u32[]{:S(2)}, u32[]{:S(2)}) %collective-permute-start.14) | collective-permute-done | bytes 262176 | tf_op jit(solution)/shard_map/ppermute | solution.py:637
  178.9 19.8 %collective-permute-done.13 = bf16[64,2048]{1,0:T(8,128)(2,1)S(1)} collective-permute-done((bf16[64,2048]{1,0:T(8,128)(2,1)S(1)}, bf16[64,2048]{1,0:T(8,128)(2,1)S(1)}, u32[]{:S(2)}, u32[]{:S(2)}) %collective-permute-start.13) | collective-permute-done | bytes 262176 | tf_op jit(solution)/shard_map/ppermute | solution.py:637
  204.9 3.8 collective-permute-done.8.refs_15_
  210.0 55.9 %attend.1 = (bf16[4,256,512]{2,1,0:T(8,128)(2,1)S(1)}, bf16[4,256,128]{2,1,0:T(8,128)(2,1)S(1)}) custom-call(s32[4,16]{1,0:T(4,128)S(1)} %copy.52.place_ref, s32[4,2]{1,0:T(4,128)S(1)} %get-tuple-element.205.own_ref, bf16[4,256,512]{2,1,0:T(8,128)(2,1)S(1)} %copy-done.11, bf16[2,4,2,128,512]{4,3,2,1,0:T(8,128)(2,1)} %bitcast.5.refs_0_.refs_8_, ...), custom_call_target="tpu_custom_call" | custom-call | flops 8589934592 | bytes 16777216 | tf_op jit(solution)/shard_map/attend/pallas_call | solution.py:221
  268.7 3.8 collective-permute-start.11
  272.5 7.6 collective-permute-done.9
  281.8 8.5 collective-permute-done.10
  291.7 6.2 fusion.84
  301.2 3.4 collective-permute-start.16
  304.6 29.1 %collective-permute-done.20.refs_6_.refs_14_ = bf16[1,4,2,128,640]{4,3,2,1,0:T(8,128)(2,1)S(1)} collective-permute-done((bf16[1,4,2,128,640]{4,3,2,1,0:T(8,128)(2,1)S(1)}, bf16[1,4,2,128,640]{4,3,2,1,0:T(8,128)(2,1)S(1)}, u32[]{:S(2)}, u32[]{:S(2)}) %collective-permute-start.20) | collective-permute-done | bytes 1310752 | tf_op jit(solution)/shard_map/ppermute | solution.py:401
  333.7 24.8 %collective-permute-done.18.refs_4_.refs_12_ = bf16[1,4,2,128,640]{4,3,2,1,0:T(8,128)(2,1)} collective-permute-done((bf16[1,4,2,128,640]{4,3,2,1,0:T(8,128)(2,1)S(1)}, bf16[1,4,2,128,640]{4,3,2,1,0:T(8,128)(2,1)}, u32[]{:S(2)}, u32[]{:S(2)}) %collective-permute-start.18) | collective-permute-done | bytes 1310752 | tf_op jit(solution)/shard_map/ppermute | solution.py:401
  359.0 2.9 collective-permute-done.19.refs_5_.refs_13_
  363.7 18.2 %all-gather.12.cloned.1.call-done.h_ref = bf16[1024,2048]{1,0:T(8,128)(2,1)} async-done(((bf16[256,2048]{1,0:T(8,128)(2,1)}), bf16[1024,2048]{1,0:T(8,128)(2,1)}) %all-gather.12.cloned.1.call-update) | async-done | bytes 4194320 | tf_op jit(solution)/shard_map/all_gather | solution.py:553
  382.0 28.4 %mlp.1 = (bf16[1024,1408]{1,0:T(8,128)(2,1)}, bf16[1024,2816]{1,0:T(8,128)(2,1)}) custom-call(bf16[1024,2048]{1,0:T(8,128)(2,1)} %all-gather.12.cloned.1.call-done.h_ref, bf16[1024,2048]{1,0:T(8,128)(2,1)} %all-gather.10.cloned.1.call-done.dy_ref, bf16[2048,1408]{1,0:T(8,128)(2,1)} %gate_ref.1, bf16[2048,1408]{1,0:T(8,128)(2,1)} %up_ref.1, ...), custom_call_target="tpu_custom_call" | custom-call | flops 17716740096 | bytes 38273024 | tf_op jit(solution)/shard_map/mlp/pallas_call | solution.py:385
  410.4 9.7 %fusion.5 = f32[1024,2048]{1,0:T(8,128)S(1)} fusion(bf16[2048,1408]{1,0:T(8,128)(2,1)} %gate_ref.1, bf16[1024,2816]{1,0:T(8,128)(2,1)} %get-tuple-element.119), kind=kOutput, calls=%fused_computation.30 | convolution fusion | flops 5905580032 | bytes 17039360 | tf_op jit(solution)/shard_map/dot_general | solution.py:15
  420.2 11.1 %add_convert_fusion.1 = bf16[1024,2048]{1,0:T(8,128)(2,1)} fusion(f32[1024,2048]{1,0:T(8,128)S(1)} %fusion.5, bf16[2048,1408]{1,0:T(8,128)(2,1)} %up_ref.1, bf16[1024,2816]{1,0:T(8,128)(2,1)S(1)} %copy-done.79), kind=kOutput, calls=%fused_computation.5 | convolution fusion | flops 5909774336 | bytes 21233664 | tf_op jit(solution)/shard_map/dot_general | solution.py:15
  431.2 11.1 %convolution_convert_fusion = bf16[1024,2816]{1,0:T(8,128)(2,1)} fusion(bf16[1024,2816]{1,0:T(8,128)(2,1)} %get-tuple-element.119, bf16[1024,2048]{1,0:T(8,128)(2,1)} %all-gather.12.cloned.1.call-done.h_ref, s32[]{:T(128)S(6)} %select_n.384), kind=kOutput, calls=%fused_computation.9 | convolution fusion | flops 5908463616 | bytes 13631492 | tf_op jit(solution)/shard_map/dot_general | solution.py:290
  442.3 4.9 convolution_convert_fusion.3
  447.8 8.4 collective-permute-done.23
  456.2 6.6 add_convert_fusion.2
  464.8 10.5 %add_convert_fusion = bf16[1024,2816]{1,0:T(8,128)(2,1)S(1)} fusion(bf16[1024,2816]{1,0:T(8,128)(2,1)} %collective-permute-done.22, bf16[1024,2816]{1,0:T(8,128)(2,1)} %get-tuple-element.119, bf16[1024,2048]{1,0:T(8,128)(2,1)S(1)} %copy-done.75, s32[]{:T(128)S(6)} %select_n.383), kind=kOutput, calls=%fused_computation | convolution fusion | flops 5914230784 | bytes 19398660 | tf_op jit(solution)/shard_map/dot_general | solution.py:290
  481.3 8.4 convolution_convert_fusion.1
  489.7 21.3 %collective-permute-done.24 = bf16[256,2816]{1,0:T(8,128)(2,1)} collective-permute-done((bf16[256,2816]{1,0:T(8,128)(2,1)}, bf16[256,2816]{1,0:T(8,128)(2,1)}, u32[]{:S(2)}, u32[]{:S(2)}) %collective-permute-start.24) | collective-permute-done | bytes 1441824 | tf_op jit(solution)/shard_map/ppermute | solution.py:401
  525.2 3.0 fusion.24
  528.3 3.9 fusion.78
  532.1 6.2 convolution_convert_fusion.4
  538.3 11.0 %collective-permute-done.29 = bf16[352,1024]{1,0:T(8,128)(2,1)} collective-permute-done((bf16[352,1024]{1,0:T(8,128)(2,1)}, bf16[352,1024]{1,0:T(8,128)(2,1)}, u32[]{:S(2)}, u32[]{:S(2)}) %collective-permute-start.29) | collective-permute-done | bytes 720928 | tf_op jit(solution)/shard_map/ppermute | solution.py:401
  549.3 3.9 collective-permute-done.28
  563.7 2.6 collective-permute-start.32
  566.3 7.2 collective-permute-done.30
  573.6 8.2 collective-permute-done.31
  598.4 55.8 %query_grad.1 = bf16[4,256,512]{2,1,0:T(8,128)(2,1)S(1)} custom-call(s32[4,16]{1,0:T(4,128)S(1)} %copy.52.place_ref, s32[4,2]{1,0:T(4,128)S(1)} %get-tuple-element.205.own_ref, bf16[4,256,512]{2,1,0:T(8,128)(2,1)S(1)} %copy-done.12, bf16[4,256,512]{2,1,0:T(8,128)(2,1)S(1)} %bitcast.75, bf16[4,256,128]{2,1,0:T(8,128)(2,1)S(1)} %get-tuple-element.112.qx_ref, ...), custom_call_target="tpu_custom_call" | custom-call | flops 12884901888 | bytes 16777216 | tf_op jit(solution)/shard_map/query_grad/pallas_call | solution.py:221
  654.2 5.8 fusion.86
  670.8 19.7 %key_value_grad.2 = (bf16[2,256,512]{2,1,0:T(8,128)(2,1)S(1)}, bf16[2,256,512]{2,1,0:T(8,128)(2,1)S(1)}) custom-call(s32[4,16]{1,0:T(4,128)S(1)} %copy.52.place_ref, s32[4,2]{1,0:T(4,128)S(1)} %get-tuple-element.205.own_ref, s32[4,16]{1,0:T(4,128)S(1)} %copy-done.20, bf16[2,4,256,512]{3,2,1,0:T(8,128)(2,1)} %get-tuple-element.106.k_ref.v_ref, ...), custom_call_target="tpu_custom_call" | custom-call | flops 8589934592 | bytes 8388608 | tf_op jit(solution)/shard_map/key_value_grad/pallas_call | solution.py:221
  692.9 36.6 %key_value_grad.3 = (bf16[2,256,512]{2,1,0:T(8,128)(2,1)S(1)}, bf16[2,256,512]{2,1,0:T(8,128)(2,1)S(1)}) custom-call(s32[4,16]{1,0:T(4,128)S(1)} %copy.52.place_ref, s32[4,2]{1,0:T(4,128)S(1)} %get-tuple-element.205.own_ref, s32[4,16]{1,0:T(4,128)S(1)} %copy-done.20, bf16[2,4,256,512]{3,2,1,0:T(8,128)(2,1)} %get-tuple-element.106.k_ref.v_ref, ...), custom_call_target="tpu_custom_call" | custom-call | flops 8589934592 | bytes 8388608 | tf_op jit(solution)/shard_map/key_value_grad/pallas_call | solution.py:221
  731.4 5.8 fusion.87
  738.8 11.0 %fusion.85 = (bf16[1024,2048]{1,0:T(8,128)(2,1)}, f32[1024,2048]{1,0:T(8,128)}) fusion(f32[1024,2048]{1,0:T(8,128)} %fusion.87, f32[1024,2048]{1,0:T(8,128)S(1)} %bitcast.88, bf16[1024,512]{1,0:T(8,128)(2,1)S(1)} %bitcast.85, bf16[2048,512]{1,0:T(8,128)(2,1)S(1)} %copy-done.56), kind=kOutput, calls=%fused_computation.216 | convolution fusion | flops 2153775104 | bytes 32505856 | tf_op jit(solution)/shard_map/dot_general | solution.py:15
  751.0 2.9 fusion.47
  758.5 3.9 convolution_convert_fusion.2
  762.3 2.7 pad_maximum_fusion.1
  765.1 3.4 maximum_select_fusion
  770.8 4.8 pad_maximum_fusion.half_ref
  776.1 3.7 fusion.77
  779.9 5.2 collective-permute-done.39
  785.2 10.4 %collective-permute-start.40 = (f32[14,1024]{1,0:T(8,128)S(1)}, f32[14,1024]{1,0:T(8,128)S(1)}, u32[]{:S(2)}, u32[]{:S(2)}) collective-permute-start(f32[14,1024]{1,0:T(8,128)S(1)} %add.449), channel_id=1, source_target_pairs={{0,8},{4,12},{8,0},{12,4},{16,24},{20,28},{24,16},{28,20},{1,9},{5... | collective-permute-start | bytes 172040 | tf_op jit(solution)/shard_map/ppermute | solution.py:627
  798.0 8.4 collective-permute-start.41
  809.0 4.4 collective-permute-start.42
  813.4 6.1 fusion.30
  820.9 9.1 collective-permute-done.43
  830.0 3.1 fusion
  838.7 13.7 %unpack_rows.2 = (f32[2048,1408]{1,0:T(8,128)}, f32[2048,1408]{1,0:T(8,128)}) custom-call(s32[1]{0:T(128)} %bitcast.19.core_ref, bf16[1024,2816]{1,0:T(8,128)(2,1)} %pad_maximum_fusion.half_ref, bf16[1024,2816]{1,0:T(8,128)(2,1)} %collective-permute-done.49.other_ref), custom_call_target="tpu_custom_call" | custom-call | bytes 34603008 | tf_op jit(solution)/shard_map/unpack_rows/pallas_call | solution.py:512
  852.4 5.1 collective-permute-done.45
  864.1 2.6 add_convert_fusion.5
  868.3 8.9 unpack_cols.1
  881.0 10.2 %collective-permute-done.56 = bf16[128,2048]{1,0:T(8,128)(2,1)S(1)} collective-permute-done((bf16[128,2048]{1,0:T(8,128)(2,1)S(1)}, bf16[128,2048]{1,0:T(8,128)(2,1)S(1)}, u32[]{:S(2)}, u32[]{:S(2)}) %collective-permute-start.56) | collective-permute-done | bytes 524320 | tf_op jit(solution)/shard_map/ppermute | solution.py:401
  894.3 17.8 %collective-permute-done.58 = bf16[256,2048]{1,0:T(8,128)(2,1)S(1)} collective-permute-done((bf16[256,2048]{1,0:T(8,128)(2,1)S(1)}, bf16[256,2048]{1,0:T(8,128)(2,1)S(1)}, u32[]{:S(2)}, u32[]{:S(2)}) %collective-permute-start.58) | collective-permute-done | bytes 1048608 | tf_op jit(solution)/shard_map/ppermute | solution.py:401
  914.2 2.6 pad_maximum_fusion.2.half_ref
  922.5 3.1 fusion.18
  925.6 11.4 %unpack_rows.3 = (f32[2048,512]{1,0:T(8,128)}, f32[2048,512]{1,0:T(8,128)}, f32[2048,512]{1,0:T(8,128)}, f32[512,2048]{1,0:T(8,128)}) custom-call(s32[1]{0:T(128)} %bitcast.19.core_ref, bf16[1024,2048]{1,0:T(8,128)(2,1)} %pad_maximum_fusion.2.half_ref, bf16[1024,2048]{1,0:T(8,128)(2,1)} %collective-permute-done.59.other_ref), custom_call_target="tpu_custom_call" | custom-call | bytes 25165824 | tf_op jit(solution)/shard_map/unpack_rows/pallas_call | solution.py:512
  937.0 4.8 reduce-scatter.8.cloned.1.call-done
  941.8 3.1 add_convert_fusion.7
  (418 shorter events, 150.1 us)
Async XLA Ops:
  7.2 88.5 %all-gather.8.cloned.1.call-start = ((), (), s32[]{:S(2)}) async-start(), calls=%async_computation.3 | async-start | bytes 5242880 | tf_op jit(solution)/shard_map/all_gather | solution.py:553
  12.1 197.1 %all-gather.10.cloned.1.call-start = ((), (), s32[]{:S(2)}) async-start(), calls=%async_computation.4 | async-start | bytes 5242880 | tf_op jit(solution)/shard_map/all_gather | solution.py:553
  95.7 196.0 %all-gather.18.cloned.1.call-start = ((), (), s32[]{:S(2)}) async-start(), calls=%async_computation.11 | async-start | bytes 9437184 | tf_op jit(solution)/shard_map/all_gather | solution.py:668
  110.6 47.7 %collective-permute-start.3 = (bf16[2,4,2,128,512]{4,3,2,1,0:T(8,128)(2,1)}, bf16[2,4,2,128,512]{4,3,2,1,0:T(8,128)(2,1)}, u32[]{:S(2)}, u32[]{:S(2)}) collective-permute-start(bf16[2,4,2,128,512]{4,3,2,1,0:T(8,128)(2,1)} %bitcast.5.refs_0_.refs_8_), channel_id=1, source_target_pairs={{0,16},{4,20},{8,24},{12,28},{16,0},{20,4},{24,8},{28,12},{1,17},{... | collective-permute-start | bytes 6291464 | tf_op jit(solution)/shard_map/ppermute | solution.py:401
  112.1 49.9 %collective-permute-start.1 = (bf16[2,4,2,128,512]{4,3,2,1,0:T(8,128)(2,1)}, bf16[2,4,2,128,512]{4,3,2,1,0:T(8,128)(2,1)}, u32[]{:S(2)}, u32[]{:S(2)}) collective-permute-start(bf16[2,4,2,128,512]{4,3,2,1,0:T(8,128)(2,1)} %bitcast.5.refs_0_.refs_8_), channel_id=1, source_target_pairs={{0,8},{4,12},{8,0},{12,4},{16,24},{20,28},{24,16},{28,20},{1,9},{5... | collective-permute-start | bytes 6291464 | tf_op jit(solution)/shard_map/ppermute | solution.py:401
  160.6 40.6 %collective-permute-start.7 = (bf16[1,4,2,128,512]{4,3,2,1,0:T(8,128)(2,1)}, bf16[1,4,2,128,512]{4,3,2,1,0:T(8,128)(2,1)}, u32[]{:S(2)}, u32[]{:S(2)}) collective-permute-start(bf16[1,4,2,128,512]{4,3,2,1,0:T(8,128)(2,1)} %slice.96), channel_id=1, source_target_pairs={{0,8},{4,12},{8,0},{12,4},{16,24},{20,28},{24,16},{28,20},{1,9},{5... | collective-permute-start | bytes 3145736 | tf_op jit(solution)/shard_map/ppermute | solution.py:401
  164.3 37.4 %collective-permute-start.5 = (bf16[1,4,2,128,512]{4,3,2,1,0:T(8,128)(2,1)}, bf16[1,4,2,128,512]{4,3,2,1,0:T(8,128)(2,1)}, u32[]{:S(2)}, u32[]{:S(2)}) collective-permute-start(bf16[1,4,2,128,512]{4,3,2,1,0:T(8,128)(2,1)} %slice.95), channel_id=1, source_target_pairs={{0,16},{4,20},{8,24},{12,28},{16,0},{20,4},{24,8},{28,12},{1,17},{... | collective-permute-start | bytes 3145736 | tf_op jit(solution)/shard_map/ppermute | solution.py:401
  165.8 13.1 %collective-permute-start.14 = (bf16[64,2048]{1,0:T(8,128)(2,1)S(1)}, bf16[64,2048]{1,0:T(8,128)(2,1)S(1)}, u32[]{:S(2)}, u32[]{:S(2)}) collective-permute-start(bf16[64,2048]{1,0:T(8,128)(2,1)S(1)} %constant_dynamic-slice_fusion.14), channel_id=1, source_target_pairs={{0,3},{1,0},{2,1},{3,2},{4,7},{5,4},{6,5},{7,6},{8,11},{9,8},{10,9... | collective-permute-start | bytes 786440 | tf_op jit(solution)/shard_map/ppermute | solution.py:637
  166.9 31.8 %collective-permute-start.13 = (bf16[64,2048]{1,0:T(8,128)(2,1)S(1)}, bf16[64,2048]{1,0:T(8,128)(2,1)S(1)}, u32[]{:S(2)}, u32[]{:S(2)}) collective-permute-start(bf16[64,2048]{1,0:T(8,128)(2,1)S(1)} %constant_dynamic-slice_fusion.14), channel_id=1, source_target_pairs={{0,2},{1,3},{2,0},{3,1},{4,6},{5,7},{6,4},{7,5},{8,10},{9,11},{10,... | collective-permute-start | bytes 786440 | tf_op jit(solution)/shard_map/ppermute | solution.py:637
  166.9 31.8 %collective-permute-start.12 = (bf16[64,2048]{1,0:T(8,128)(2,1)S(1)}, bf16[64,2048]{1,0:T(8,128)(2,1)S(1)}, u32[]{:S(2)}, u32[]{:S(2)}) collective-permute-start(bf16[64,2048]{1,0:T(8,128)(2,1)S(1)} %constant_dynamic-slice_fusion.14), channel_id=1, source_target_pairs={{0,1},{1,2},{2,3},{3,0},{4,5},{5,6},{6,7},{7,4},{8,9},{9,10},{10,1... | collective-permute-start | bytes 786440 | tf_op jit(solution)/shard_map/ppermute | solution.py:637
  178.9 26.0 %collective-permute-start = (bf16[2,4,2,128,512]{4,3,2,1,0:T(8,128)(2,1)}, bf16[2,4,2,128,512]{4,3,2,1,0:T(8,128)(2,1)}, u32[]{:S(2)}, u32[]{:S(2)}) collective-permute-start(bf16[2,4,2,128,512]{4,3,2,1,0:T(8,128)(2,1)} %bitcast.5.refs_0_.refs_8_), channel_id=1, source_target_pairs={{0,4},{4,0},{8,12},{12,8},{16,20},{20,16},{24,28},{28,24},{1,5},{5... | collective-permute-start | bytes 6291464 | tf_op jit(solution)/shard_map/ppermute | solution.py:401
  198.7 10.5 %collective-permute-start.4 = (bf16[2,4,2,128,512]{4,3,2,1,0:T(8,128)(2,1)}, bf16[2,4,2,128,512]{4,3,2,1,0:T(8,128)(2,1)}, u32[]{:S(2)}, u32[]{:S(2)}) collective-permute-start(bf16[2,4,2,128,512]{4,3,2,1,0:T(8,128)(2,1)} %collective-permute-done.3.refs_4_.refs_12_), channel_id=1, source_target_pairs={{0,4},{4,0},{8,12},{12,8},{16,20},{20,16},{24,28},{28,24},{1,5},{5... | collective-permute-start | bytes 6291464 | tf_op jit(solution)/shard_map/ppermute | solution.py:401
  198.7 10.5 %collective-permute-start.2 = (bf16[2,4,2,128,512]{4,3,2,1,0:T(8,128)(2,1)}, bf16[2,4,2,128,512]{4,3,2,1,0:T(8,128)(2,1)}, u32[]{:S(2)}, u32[]{:S(2)}) collective-permute-start(bf16[2,4,2,128,512]{4,3,2,1,0:T(8,128)(2,1)} %collective-permute-done.1.refs_2_.refs_10_), channel_id=1, source_target_pairs={{0,4},{4,0},{8,12},{12,8},{16,20},{20,16},{24,28},{28,24},{1,5},{5... | collective-permute-start | bytes 6291464 | tf_op jit(solution)/shard_map/ppermute | solution.py:401
  209.2 172.7 %all-gather.12.cloned.1.call-start = ((), (), s32[]{:S(2)}) async-start(), calls=%async_computation.5 | async-start | bytes 5242880 | tf_op jit(solution)/shard_map/all_gather | solution.py:553
  268.7 11.4 %collective-permute-start.9 = (bf16[256,512]{1,0:T(8,128)(2,1)}, bf16[256,512]{1,0:T(8,128)(2,1)}, u32[]{:S(2)}, u32[]{:S(2)}) collective-permute-start(bf16[256,512]{1,0:T(8,128)(2,1)} %get-tuple-element.218), channel_id=1, source_target_pairs={{0,1},{1,2},{2,3},{3,0},{4,5},{5,6},{6,7},{7,4},{8,9},{9,10},{10,1... | collective-permute-start | bytes 786440 | tf_op jit(solution)/shard_map/ppermute | solution.py:558
  268.7 21.5 %collective-permute-start.10 = (bf16[256,512]{1,0:T(8,128)(2,1)}, bf16[256,512]{1,0:T(8,128)(2,1)S(1)}, u32[]{:S(2)}, u32[]{:S(2)}) collective-permute-start(bf16[256,512]{1,0:T(8,128)(2,1)} %get-tuple-element.217), channel_id=1, source_target_pairs={{0,2},{1,3},{2,0},{3,1},{4,6},{5,7},{6,4},{7,5},{8,10},{9,11},{10,... | collective-permute-start | bytes 786440 | tf_op jit(solution)/shard_map/ppermute | solution.py:558
  268.7 22.3 %collective-permute-start.11 = (bf16[256,512]{1,0:T(8,128)(2,1)}, bf16[256,512]{1,0:T(8,128)(2,1)S(1)}, u32[]{:S(2)}, u32[]{:S(2)}) collective-permute-start(bf16[256,512]{1,0:T(8,128)(2,1)} %get-tuple-element.216), channel_id=1, source_target_pairs={{0,3},{1,0},{2,1},{3,2},{4,7},{5,4},{6,5},{7,6},{8,11},{9,8},{10,9... | collective-permute-start | bytes 786440 | tf_op jit(solution)/shard_map/ppermute | solution.py:558
  300.7 224.5 %reduce-scatter.4.cloned.1.call-start = ((), (), s32[]{:S(2)}) async-start(), calls=%async_computation.6 | async-start | bytes 5242880 | tf_op jit(solution)/shard_map/reduce_scatter | solution.py:581
  301.0 32.7 %collective-permute-start.20 = (bf16[1,4,2,128,640]{4,3,2,1,0:T(8,128)(2,1)S(1)}, bf16[1,4,2,128,640]{4,3,2,1,0:T(8,128)(2,1)S(1)}, u32[]{:S(2)}, u32[]{:S(2)}) collective-permute-start(bf16[1,4,2,128,640]{4,3,2,1,0:T(8,128)(2,1)S(1)} %bitcast.67), channel_id=1, source_target_pairs={{0,24},{4,28},{8,16},{12,20},{16,8},{20,12},{24,0},{28,4},{1,25},{... | collective-permute-start | bytes 3932168 | tf_op jit(solution)/shard_map/ppermute | solution.py:401
  301.1 57.4 %collective-permute-start.18 = (bf16[1,4,2,128,640]{4,3,2,1,0:T(8,128)(2,1)S(1)}, bf16[1,4,2,128,640]{4,3,2,1,0:T(8,128)(2,1)}, u32[]{:S(2)}, u32[]{:S(2)}) collective-permute-start(bf16[1,4,2,128,640]{4,3,2,1,0:T(8,128)(2,1)S(1)} %bitcast.68), channel_id=1, source_target_pairs={{0,16},{4,20},{8,24},{12,28},{16,0},{20,4},{24,8},{28,12},{1,17},{... | collective-permute-start | bytes 3932168 | tf_op jit(solution)/shard_map/ppermute | solution.py:401
  301.2 57.3 %collective-permute-start.16 = (bf16[1,4,2,128,640]{4,3,2,1,0:T(8,128)(2,1)S(1)}, bf16[1,4,2,128,640]{4,3,2,1,0:T(8,128)(2,1)}, u32[]{:S(2)}, u32[]{:S(2)}) collective-permute-start(bf16[1,4,2,128,640]{4,3,2,1,0:T(8,128)(2,1)S(1)} %bitcast.69), channel_id=1, source_target_pairs={{0,8},{4,12},{8,0},{12,4},{16,24},{20,28},{24,16},{28,20},{1,9},{5... | collective-permute-start | bytes 3932168 | tf_op jit(solution)/shard_map/ppermute | solution.py:401
  304.6 54.4 %collective-permute-start.15 = (bf16[1,4,2,128,640]{4,3,2,1,0:T(8,128)(2,1)S(1)}, bf16[1,4,2,128,640]{4,3,2,1,0:T(8,128)(2,1)}, u32[]{:S(2)}, u32[]{:S(2)}) collective-permute-start(bf16[1,4,2,128,640]{4,3,2,1,0:T(8,128)(2,1)S(1)} %bitcast.70), channel_id=1, source_target_pairs={{0,4},{4,0},{8,12},{12,8},{16,20},{20,16},{24,28},{28,24},{1,5},{5... | collective-permute-start | bytes 3932168 | tf_op jit(solution)/shard_map/ppermute | solution.py:401
  333.7 25.3 %collective-permute-start.21 = (bf16[1,4,2,128,640]{4,3,2,1,0:T(8,128)(2,1)S(1)}, bf16[1,4,2,128,640]{4,3,2,1,0:T(8,128)(2,1)}, u32[]{:S(2)}, u32[]{:S(2)}) collective-permute-start(bf16[1,4,2,128,640]{4,3,2,1,0:T(8,128)(2,1)S(1)} %collective-permute-done.20.refs_6_.refs_14_), channel_id=1, source_target_pairs={{0,4},{4,0},{8,12},{12,8},{16,20},{20,16},{24,28},{28,24},{1,5},{5... | collective-permute-start | bytes 3932168 | tf_op jit(solution)/shard_map/ppermute | solution.py:401
  442.3 22.4 %collective-permute-start.22 = (bf16[1024,2816]{1,0:T(8,128)(2,1)}, bf16[1024,2816]{1,0:T(8,128)(2,1)}, u32[]{:S(2)}, u32[]{:S(2)}) collective-permute-start(bf16[1024,2816]{1,0:T(8,128)(2,1)} %convolution_convert_fusion), channel_id=1, source_target_pairs={{0,4},{4,0},{8,12},{12,8},{16,20},{20,16},{24,28},{28,24},{1,5},{5... | collective-permute-start | bytes 17301512 | tf_op jit(solution)/shard_map/ppermute | solution.py:401
  447.3 8.9 collective-permute-start.23
  447.8 216.8 %all-gather.14.cloned.1.call-start = ((), (), s32[]{:S(2)}) async-start(), calls=%async_computation.7 | async-start | bytes 11796480 | tf_op jit(solution)/shard_map/all_gather | solution.py:709
  477.1 33.9 %collective-permute-start.24 = (bf16[256,2816]{1,0:T(8,128)(2,1)}, bf16[256,2816]{1,0:T(8,128)(2,1)}, u32[]{:S(2)}, u32[]{:S(2)}) collective-permute-start(bf16[256,2816]{1,0:T(8,128)(2,1)} %constant_dynamic-slice_fusion.13), channel_id=1, source_target_pairs={{0,8},{4,12},{8,0},{12,4},{16,24},{20,28},{24,16},{28,20},{1,9},{5... | collective-permute-start | bytes 4325384 | tf_op jit(solution)/shard_map/ppermute | solution.py:401
  479.8 33.7 %collective-permute-start.25 = (bf16[256,2816]{1,0:T(8,128)(2,1)}, bf16[256,2816]{1,0:T(8,128)(2,1)}, u32[]{:S(2)}, u32[]{:S(2)}) collective-permute-start(bf16[256,2816]{1,0:T(8,128)(2,1)} %constant_dynamic-slice_fusion.12), channel_id=1, source_target_pairs={{0,16},{4,20},{8,24},{12,28},{16,0},{20,4},{24,8},{28,12},{1,17},{... | collective-permute-start | bytes 4325384 | tf_op jit(solution)/shard_map/ppermute | solution.py:401
  516.6 36.7 %collective-permute-start.26 = (bf16[128,2816]{1,0:T(8,128)(2,1)}, bf16[128,2816]{1,0:T(8,128)(2,1)}, u32[]{:S(2)}, u32[]{:S(2)}) collective-permute-start(bf16[128,2816]{1,0:T(8,128)(2,1)} %constant_dynamic-slice_fusion.11), channel_id=1, source_target_pairs={{0,16},{4,20},{8,24},{12,28},{16,0},{20,4},{24,8},{28,12},{1,17},{... | collective-permute-start | bytes 2162696 | tf_op jit(solution)/shard_map/ppermute | solution.py:401
  520.7 32.6 %collective-permute-start.27 = (bf16[128,2816]{1,0:T(8,128)(2,1)}, bf16[128,2816]{1,0:T(8,128)(2,1)}, u32[]{:S(2)}, u32[]{:S(2)}) collective-permute-start(bf16[128,2816]{1,0:T(8,128)(2,1)} %constant_dynamic-slice_fusion.10), channel_id=1, source_target_pairs={{0,8},{4,12},{8,0},{12,4},{16,24},{20,28},{24,16},{28,20},{1,9},{5... | collective-permute-start | bytes 2162696 | tf_op jit(solution)/shard_map/ppermute | solution.py:401
  522.2 27.1 %collective-permute-start.29 = (bf16[352,1024]{1,0:T(8,128)(2,1)}, bf16[352,1024]{1,0:T(8,128)(2,1)}, u32[]{:S(2)}, u32[]{:S(2)}) collective-permute-start(bf16[352,1024]{1,0:T(8,128)(2,1)} %constant_dynamic-slice_fusion.8), channel_id=1, source_target_pairs={{0,16},{4,20},{8,24},{12,28},{16,0},{20,4},{24,8},{28,12},{1,17},{... | collective-permute-start | bytes 2162696 | tf_op jit(solution)/shard_map/ppermute | solution.py:401
  523.6 29.7 %collective-permute-start.28 = (bf16[352,1024]{1,0:T(8,128)(2,1)}, bf16[352,1024]{1,0:T(8,128)(2,1)}, u32[]{:S(2)}, u32[]{:S(2)}) collective-permute-start(bf16[352,1024]{1,0:T(8,128)(2,1)} %constant_dynamic-slice_fusion.9), channel_id=1, source_target_pairs={{0,8},{4,12},{8,0},{12,4},{16,24},{20,28},{24,16},{28,20},{1,9},{5... | collective-permute-start | bytes 2162696 | tf_op jit(solution)/shard_map/ppermute | solution.py:401
  562.4 11.1 %collective-permute-start.30 = (bf16[256,512]{1,0:T(8,128)(2,1)S(1)}, bf16[256,512]{1,0:T(8,128)(2,1)S(1)}, u32[]{:S(2)}, u32[]{:S(2)}) collective-permute-start(bf16[256,512]{1,0:T(8,128)(2,1)S(1)} %get-tuple-element.214), channel_id=1, source_target_pairs={{0,1},{1,2},{2,3},{3,0},{4,5},{5,6},{6,7},{7,4},{8,9},{9,10},{10,1... | collective-permute-start | bytes 786440 | tf_op jit(solution)/shard_map/ppermute | solution.py:558
  562.5 19.3 %collective-permute-start.31 = (bf16[256,512]{1,0:T(8,128)(2,1)S(1)}, bf16[256,512]{1,0:T(8,128)(2,1)S(1)}, u32[]{:S(2)}, u32[]{:S(2)}) collective-permute-start(bf16[256,512]{1,0:T(8,128)(2,1)S(1)} %get-tuple-element.213), channel_id=1, source_target_pairs={{0,2},{1,3},{2,0},{3,1},{4,6},{5,7},{6,4},{7,5},{8,10},{9,11},{10,... | collective-permute-start | bytes 786440 | tf_op jit(solution)/shard_map/ppermute | solution.py:558
  563.7 18.0 %collective-permute-start.32 = (bf16[256,512]{1,0:T(8,128)(2,1)S(1)}, bf16[256,512]{1,0:T(8,128)(2,1)S(1)}, u32[]{:S(2)}, u32[]{:S(2)}) collective-permute-start(bf16[256,512]{1,0:T(8,128)(2,1)S(1)} %get-tuple-element.212), channel_id=1, source_target_pairs={{0,3},{1,0},{2,1},{3,2},{4,7},{5,4},{6,5},{7,6},{8,11},{9,8},{10,9... | collective-permute-start | bytes 786440 | tf_op jit(solution)/shard_map/ppermute | solution.py:558
  585.0 164.7 %all-gather.16.cloned.1.call-start = ((), (), s32[]{:S(2)}) async-start(), calls=%async_computation.8 | async-start | bytes 5242880 | tf_op jit(solution)/shard_map/all_gather | solution.py:553
  585.1 76.6 %collective-permute-start.34 = (bf16[128,2816]{1,0:T(8,128)(2,1)}, bf16[128,2816]{1,0:T(8,128)(2,1)S(1)}, u32[]{:S(2)}, u32[]{:S(2)}) collective-permute-start(bf16[128,2816]{1,0:T(8,128)(2,1)} %add_convert_fusion.11), channel_id=1, source_target_pairs={{0,8},{4,12},{8,0},{12,4},{16,24},{20,28},{24,16},{28,20},{1,9},{5... | collective-permute-start | bytes 2162696 | tf_op jit(solution)/shard_map/ppermute | solution.py:401
  585.6 76.1 %collective-permute-start.33 = (bf16[128,2816]{1,0:T(8,128)(2,1)}, bf16[128,2816]{1,0:T(8,128)(2,1)S(1)}, u32[]{:S(2)}, u32[]{:S(2)}) collective-permute-start(bf16[128,2816]{1,0:T(8,128)(2,1)} %add_convert_fusion.12), channel_id=1, source_target_pairs={{0,16},{4,20},{8,24},{12,28},{16,0},{20,4},{24,8},{28,12},{1,17},{... | collective-permute-start | bytes 2162696 | tf_op jit(solution)/shard_map/ppermute | solution.py:401
  587.5 72.5 %collective-permute-start.35 = (bf16[176,1024]{1,0:T(8,128)(2,1)S(1)}, bf16[176,1024]{1,0:T(8,128)(2,1)S(1)}, u32[]{:S(2)}, u32[]{:S(2)}) collective-permute-start(bf16[176,1024]{1,0:T(8,128)(2,1)S(1)} %constant_dynamic-slice_fusion.4), channel_id=1, source_target_pairs={{0,16},{4,20},{8,24},{12,28},{16,0},{20,4},{24,8},{28,12},{1,17},{... | collective-permute-start | bytes 1081352 | tf_op jit(solution)/shard_map/ppermute | solution.py:401
  589.7 70.3 %collective-permute-start.36 = (bf16[176,1024]{1,0:T(8,128)(2,1)S(1)}, bf16[176,1024]{1,0:T(8,128)(2,1)S(1)}, u32[]{:S(2)}, u32[]{:S(2)}) collective-permute-start(bf16[176,1024]{1,0:T(8,128)(2,1)S(1)} %constant_dynamic-slice_fusion.3), channel_id=1, source_target_pairs={{0,8},{4,12},{8,0},{12,4},{16,24},{20,28},{24,16},{28,20},{1,9},{5... | collective-permute-start | bytes 1081352 | tf_op jit(solution)/shard_map/ppermute | solution.py:401
  664.6 202.1 %reduce-scatter.6.cloned.1.call-start = ((), (), s32[]{:S(2)}) async-start(), calls=%async_computation.9 | async-start | bytes 5242880 | tf_op jit(solution)/shard_map/reduce_scatter | solution.py:581
  664.6 25.9 %collective-permute-start.38 = (bf16[176,1024]{1,0:T(8,128)(2,1)}, bf16[176,1024]{1,0:T(8,128)(2,1)S(1)}, u32[]{:S(2)}, u32[]{:S(2)}) collective-permute-start(bf16[176,1024]{1,0:T(8,128)(2,1)} %add_convert_fusion.15), channel_id=1, source_target_pairs={{0,8},{4,12},{8,0},{12,4},{16,24},{20,28},{24,16},{28,20},{1,9},{5... | collective-permute-start | bytes 1081352 | tf_op jit(solution)/shard_map/ppermute | solution.py:401
  664.7 25.8 %collective-permute-start.37 = (bf16[176,1024]{1,0:T(8,128)(2,1)}, bf16[176,1024]{1,0:T(8,128)(2,1)S(1)}, u32[]{:S(2)}, u32[]{:S(2)}) collective-permute-start(bf16[176,1024]{1,0:T(8,128)(2,1)} %add_convert_fusion.16), channel_id=1, source_target_pairs={{0,16},{4,20},{8,24},{12,28},{16,0},{20,4},{24,8},{28,12},{1,17},{... | collective-permute-start | bytes 1081352 | tf_op jit(solution)/shard_map/ppermute | solution.py:401
  664.8 85.1 %collective-permute-start.48 = (bf16[256,2816]{1,0:T(8,128)(2,1)}, bf16[256,2816]{1,0:T(8,128)(2,1)}, u32[]{:S(2)}, u32[]{:S(2)}) collective-permute-start(bf16[256,2816]{1,0:T(8,128)(2,1)} %maximum_select_fusion.5), channel_id=1, source_target_pairs={{0,16},{4,20},{8,24},{12,28},{16,0},{20,4},{24,8},{28,12},{1,17},{... | collective-permute-start | bytes 4325384 | tf_op jit(solution)/shard_map/ppermute | solution.py:401
  666.8 83.1 %collective-permute-start.47 = (bf16[256,2816]{1,0:T(8,128)(2,1)}, bf16[256,2816]{1,0:T(8,128)(2,1)}, u32[]{:S(2)}, u32[]{:S(2)}) collective-permute-start(bf16[256,2816]{1,0:T(8,128)(2,1)} %maximum_select_fusion.4), channel_id=1, source_target_pairs={{0,8},{4,12},{8,0},{12,4},{16,24},{20,28},{24,16},{28,20},{1,9},{5... | collective-permute-start | bytes 4325384 | tf_op jit(solution)/shard_map/ppermute | solution.py:401
  749.8 192.0 %reduce-scatter.8.cloned.1.call-start = ((), (), s32[]{:S(2)}) async-start(), calls=%async_computation.10 | async-start | bytes 5242880 | tf_op jit(solution)/shard_map/reduce_scatter | solution.py:581
  765.0 65.0 %collective-permute-start.44 = (bf16[1024,2048]{1,0:T(8,128)(2,1)}, bf16[1024,2048]{1,0:T(8,128)(2,1)}, u32[]{:S(2)}, u32[]{:S(2)}) collective-permute-start(bf16[1024,2048]{1,0:T(8,128)(2,1)} %pad_maximum_fusion.1), channel_id=1, source_target_pairs={{0,4},{4,0},{8,12},{12,8},{16,20},{20,16},{24,28},{28,24},{1,5},{5... | collective-permute-start | bytes 12582920 | tf_op jit(solution)/shard_map/ppermute | solution.py:401
  775.5 63.2 %collective-permute-start.49 = (bf16[1024,2816]{1,0:T(8,128)(2,1)}, bf16[1024,2816]{1,0:T(8,128)(2,1)}, u32[]{:S(2)}, u32[]{:S(2)}) collective-permute-start(bf16[1024,2816]{1,0:T(8,128)(2,1)} %pad_maximum_fusion.half_ref), channel_id=1, source_target_pairs={{0,4},{4,0},{8,12},{12,8},{16,20},{20,16},{24,28},{28,24},{1,5},{5... | collective-permute-start | bytes 17301512 | tf_op jit(solution)/shard_map/ppermute | solution.py:401
  785.2 12.8 %collective-permute-start.40 = (f32[14,1024]{1,0:T(8,128)S(1)}, f32[14,1024]{1,0:T(8,128)S(1)}, u32[]{:S(2)}, u32[]{:S(2)}) collective-permute-start(f32[14,1024]{1,0:T(8,128)S(1)} %add.449), channel_id=1, source_target_pairs={{0,8},{4,12},{8,0},{12,4},{16,24},{20,28},{24,16},{28,20},{1,9},{5... | collective-permute-start | bytes 172040 | tf_op jit(solution)/shard_map/ppermute | solution.py:627
  798.0 10.9 %collective-permute-start.41 = (f32[14,1024]{1,0:T(8,128)S(1)}, f32[14,1024]{1,0:T(8,128)S(1)}, u32[]{:S(2)}, u32[]{:S(2)}) collective-permute-start(f32[14,1024]{1,0:T(8,128)S(1)} %add.450), channel_id=1, source_target_pairs={{0,16},{4,20},{8,24},{12,28},{16,0},{20,4},{24,8},{28,12},{1,17},{... | collective-permute-start | bytes 172040 | tf_op jit(solution)/shard_map/ppermute | solution.py:627
  806.4 27.0 %collective-permute-start.53 = (bf16[352,1024]{1,0:T(8,128)(2,1)S(1)}, bf16[352,1024]{1,0:T(8,128)(2,1)S(1)}, u32[]{:S(2)}, u32[]{:S(2)}) collective-permute-start(bf16[352,1024]{1,0:T(8,128)(2,1)S(1)} %copy-done.55), channel_id=1, source_target_pairs={{0,16},{4,20},{8,24},{12,28},{16,0},{20,4},{24,8},{28,12},{1,17},{... | collective-permute-start | bytes 2162696 | tf_op jit(solution)/shard_map/ppermute | solution.py:401
  806.5 27.0 %collective-permute-start.52 = (bf16[352,1024]{1,0:T(8,128)(2,1)S(1)}, bf16[352,1024]{1,0:T(8,128)(2,1)S(1)}, u32[]{:S(2)}, u32[]{:S(2)}) collective-permute-start(bf16[352,1024]{1,0:T(8,128)(2,1)S(1)} %copy-done.54), channel_id=1, source_target_pairs={{0,8},{4,12},{8,0},{12,4},{16,24},{20,28},{24,16},{28,20},{1,9},{5... | collective-permute-start | bytes 2162696 | tf_op jit(solution)/shard_map/ppermute | solution.py:401
  809.0 10.5 %collective-permute-start.42 = (f32[14,1024]{1,0:T(8,128)S(1)}, f32[14,1024]{1,0:T(8,128)S(1)}, u32[]{:S(2)}, u32[]{:S(2)}) collective-permute-start(f32[14,1024]{1,0:T(8,128)S(1)} %add.451), channel_id=1, source_target_pairs={{0,1},{1,0},{2,3},{3,2},{4,5},{5,4},{6,7},{7,6},{8,9},{9,8},{10,11... | collective-permute-start | bytes 172040 | tf_op jit(solution)/shard_map/ppermute | solution.py:627
  819.5 10.5 %collective-permute-start.43 = (f32[14,1024]{1,0:T(8,128)S(1)}, f32[14,1024]{1,0:T(8,128)S(1)}, u32[]{:S(2)}, u32[]{:S(2)}) collective-permute-start(f32[14,1024]{1,0:T(8,128)S(1)} %add.452), channel_id=1, source_target_pairs={{0,2},{1,3},{2,0},{3,1},{4,6},{5,7},{6,4},{7,5},{8,10},{9,11},{10,... | collective-permute-start | bytes 172040 | tf_op jit(solution)/shard_map/ppermute | solution.py:627
  833.6 23.9 %collective-permute-start.45 = (bf16[256,2048]{1,0:T(8,128)(2,1)S(1)}, bf16[256,2048]{1,0:T(8,128)(2,1)}, u32[]{:S(2)}, u32[]{:S(2)}) collective-permute-start(bf16[256,2048]{1,0:T(8,128)(2,1)S(1)} %constant_dynamic-slice_fusion.2), channel_id=1, source_target_pairs={{0,8},{4,12},{8,0},{12,4},{16,24},{20,28},{24,16},{28,20},{1,9},{5... | collective-permute-start | bytes 3145736 | tf_op jit(solution)/shard_map/ppermute | solution.py:401
  835.6 23.3 %collective-permute-start.46 = (bf16[256,2048]{1,0:T(8,128)(2,1)S(1)}, bf16[256,2048]{1,0:T(8,128)(2,1)}, u32[]{:S(2)}, u32[]{:S(2)}) collective-permute-start(bf16[256,2048]{1,0:T(8,128)(2,1)S(1)} %constant_dynamic-slice_fusion.1), channel_id=1, source_target_pairs={{0,16},{4,20},{8,24},{12,28},{16,0},{20,4},{24,8},{28,12},{1,17},{... | collective-permute-start | bytes 3145736 | tf_op jit(solution)/shard_map/ppermute | solution.py:401
  838.6 29.7 %collective-permute-start.54 = (bf16[1408,1024]{1,0:T(8,128)(2,1)S(1)}, bf16[1408,1024]{1,0:T(8,128)(2,1)}, u32[]{:S(2)}, u32[]{:S(2)}) collective-permute-start(bf16[1408,1024]{1,0:T(8,128)(2,1)S(1)} %pad_maximum_fusion.3.half_ref), channel_id=1, source_target_pairs={{0,4},{4,0},{8,12},{12,8},{16,20},{20,16},{24,28},{28,24},{1,5},{5... | collective-permute-start | bytes 8650760 | tf_op jit(solution)/shard_map/ppermute | solution.py:401
  862.3 14.9 %collective-permute-start.50 = (bf16[128,2048]{1,0:T(8,128)(2,1)}, bf16[128,2048]{1,0:T(8,128)(2,1)S(1)}, u32[]{:S(2)}, u32[]{:S(2)}) collective-permute-start(bf16[128,2048]{1,0:T(8,128)(2,1)} %constant_dynamic-slice_fusion), channel_id=1, source_target_pairs={{0,16},{4,20},{8,24},{12,28},{16,0},{20,4},{24,8},{28,12},{1,17},{... | collective-permute-start | bytes 1572872 | tf_op jit(solution)/shard_map/ppermute | solution.py:401
  867.8 11.8 %collective-permute-start.51 = (bf16[128,2048]{1,0:T(8,128)(2,1)S(1)}, bf16[128,2048]{1,0:T(8,128)(2,1)S(1)}, u32[]{:S(2)}, u32[]{:S(2)}) collective-permute-start(bf16[128,2048]{1,0:T(8,128)(2,1)S(1)} %constant_dynamic-slice_fusion.19), channel_id=1, source_target_pairs={{0,8},{4,12},{8,0},{12,4},{16,24},{20,28},{24,16},{28,20},{1,9},{5... | collective-permute-start | bytes 1572872 | tf_op jit(solution)/shard_map/ppermute | solution.py:401
  879.8 11.4 %collective-permute-start.56 = (bf16[128,2048]{1,0:T(8,128)(2,1)S(1)}, bf16[128,2048]{1,0:T(8,128)(2,1)S(1)}, u32[]{:S(2)}, u32[]{:S(2)}) collective-permute-start(bf16[128,2048]{1,0:T(8,128)(2,1)S(1)} %add_convert_fusion.13), channel_id=1, source_target_pairs={{0,8},{4,12},{8,0},{12,4},{16,24},{20,28},{24,16},{28,20},{1,9},{5... | collective-permute-start | bytes 1572872 | tf_op jit(solution)/shard_map/ppermute | solution.py:401
  880.2 10.9 %collective-permute-start.55 = (bf16[128,2048]{1,0:T(8,128)(2,1)S(1)}, bf16[128,2048]{1,0:T(8,128)(2,1)S(1)}, u32[]{:S(2)}, u32[]{:S(2)}) collective-permute-start(bf16[128,2048]{1,0:T(8,128)(2,1)S(1)} %add_convert_fusion.14), channel_id=1, source_target_pairs={{0,16},{4,20},{8,24},{12,28},{16,0},{20,4},{24,8},{28,12},{1,17},{... | collective-permute-start | bytes 1572872 | tf_op jit(solution)/shard_map/ppermute | solution.py:401
  891.4 20.7 %collective-permute-start.58 = (bf16[256,2048]{1,0:T(8,128)(2,1)S(1)}, bf16[256,2048]{1,0:T(8,128)(2,1)S(1)}, u32[]{:S(2)}, u32[]{:S(2)}) collective-permute-start(bf16[256,2048]{1,0:T(8,128)(2,1)S(1)} %maximum_select_fusion.9), channel_id=1, source_target_pairs={{0,16},{4,20},{8,24},{12,28},{16,0},{20,4},{24,8},{28,12},{1,17},{... | collective-permute-start | bytes 3145736 | tf_op jit(solution)/shard_map/ppermute | solution.py:401
  892.1 21.0 %collective-permute-start.57 = (bf16[256,2048]{1,0:T(8,128)(2,1)S(1)}, bf16[256,2048]{1,0:T(8,128)(2,1)S(1)}, u32[]{:S(2)}, u32[]{:S(2)}) collective-permute-start(bf16[256,2048]{1,0:T(8,128)(2,1)S(1)} %maximum_select_fusion.8), channel_id=1, source_target_pairs={{0,8},{4,12},{8,0},{12,4},{16,24},{20,28},{24,16},{28,20},{1,9},{5... | collective-permute-start | bytes 3145736 | tf_op jit(solution)/shard_map/ppermute | solution.py:401
  916.8 8.8 collective-permute-start.59
  (93 other events, 1309.9 us)
Sparse Core Ops, SparseCore 0:
  12.2 83.4 all-gather.7
  97.3 86.8 all-gather.9
  209.4 52.6 all-gather.17
  300.8 81.1 all-gather.11
  447.9 75.3 reduce-scatter.3
  585.2 76.9 all-gather.13
  664.7 81.6 all-gather.15
  749.9 96.7 reduce-scatter.5
  866.8 74.9 reduce-scatter.7

commit v9 on v8

--- a/solution.py
+++ b/solution.py
@@ -223,7 +223,7 @@
         grid_spec=pltpu.PrefetchScalarGridSpec(
             num_scalar_prefetch=prefetch, grid=(seqs, pairs), in_specs=in_specs, out_specs=out_specs, scratch_shapes=scratch),
         out_shape=out_shape,
-        compiler_params=pltpu.CompilerParams(vmem_limit_bytes=40 * 2**20),
+        compiler_params=pltpu.CompilerParams(vmem_limit_bytes=60 * 2**20),
         cost_estimate=pl.CostEstimate(flops=work * 512 * mats, bytes_accessed=4 * seqs * pairs * blocks * BLK * 128, transcendentals=work),
         name=name,
     )(*args)
@@ -691,14 +691,14 @@
     go(gu)
     go(dw, held)
     grad_two = after(grad_two, held)
+    out_sum = sum_rows(after(down, grad_two))
 
     norm_two, grad_gain_two, grad_shift_two = layer_back(grad_two.astype(F32), unit_two, inverse_two, gain_two)
     grad_mixed = cotangent.astype(F32) + norm_two
     branch_own = grad_mixed.astype(BF16)
     grad_attn = nt(branch_own, whole_w).astype(BF16)
-    grad_attn = after(grad_attn, take(gu, grad_attn), take(dw, grad_attn))
+    held = take(gu, grad_attn)
     go(gu)
-    go(dw)
     grad_attn = exchange(grad_attn, 1, 0)
     lane = jnp.arange(128)[None, :]
     ind = ((jnp.arange(width) // HEAD_DIM)[:, None] == lane // 3).astype(F32)
@@ -706,6 +706,7 @@
                             precision=lax.Precision.HIGHEST, preferred_element_type=F32)
     do_ext = terms(-delta, lane).astype(BF16)
     do_sent = jnp.concatenate([grad_attn, do_ext], axis=1).reshape(shape)
+    do_sent = after(do_sent, held)
     grads = lax.all_gather(do_sent, "ctx", axis=0, tiled=True)
     grad_q = query_grad(place, own, q, grad_attn.reshape(q.shape), q_ext, do_ext.reshape(q_ext.shape), tabs, keys, values)
     grad_q = grad_q.reshape(-1, width)
@@ -723,44 +724,50 @@
     part_one = q_part + nt(grad_k, key_w) + nt(grad_v, value_w)
     part_sent = after(part_one.astype(BF16), branch)
     grad_one = sum_rows(part_sent)
-    out_tokens = (mixed + sum_rows(after(down, grad_one)).astype(F32)).astype(BF16)
+    mixed_late, out_sum = after((mixed, out_sum), part_sent)
+    out_tokens = (mixed_late + out_sum.astype(F32)).astype(BF16)
 
     rows_one, branch, grad_q, grad_k, grad_v = after((rows_one, branch, grad_q, grad_k, grad_v), part_sent)
     grad_qkv = jnp.concatenate([grad_q, grad_k, grad_v], axis=1)
-    chain = begin(lambda core: jnp.concatenate([rc(columns(rows_one, core), grad_qkv), rc(columns(branch, core), attn_rows)], axis=1))
+    chain = begin(lambda core: rc(columns(rows_one, core), grad_qkv))
     take(gu, part_sent)
     take_extra(gu)
     go(gu)
+    held = take(chain)
+    go(chain)
+    grad_output_w = rc(attn_rows, after(branch, held)).astype(BF16)
+    grad_output_w = lax.psum(after(grad_output_w, grad_one), "ctx")
     unit_rows = (rows_one.astype(F32) - shift_one) / gain_one
     bias_grad = jnp.sum(grad_qkv.astype(F32), axis=0)
     tp_row = (jnp.arange(n_tp) == lax.axis_index("tp"))[:, None]
     small = jnp.concatenate([
         jnp.sum(part_one * unit_rows, axis=0), jnp.sum(part_one, axis=0), grad_gain_two, grad_shift_two,
         jnp.where(tp_row, bias_grad[None, :], 0.0).reshape(-1)])
-    sums = sum_over_all(small.reshape(-1, 1024))
+    sums = sum_over_all(after(small, held).reshape(-1, 1024))
     for _ in range(9):
         small = next(sums)
-    held = take(chain)
-    go(chain)
-    take(dw, (held, small))
+    made = take(dw, held)
     take_extra(dw)
     go(dw)
+    held = take(chain, made)
+    go(chain)
+    held = take(chain, small)
+    go(chain)
     grad_gate_w, grad_up_w = unpack_rows(*take(gu, held), 2)
     held = take(chain, grad_gate_w)
     go(chain)
-    grad_down_w = unpack_cols(*take(dw, held))
-    held = take(chain, grad_down_w)
-    go(chain)
-    held = take(chain, held)
-    go(chain)
+    take(dw, held)
+    go(dw)
     take(chain)
     take_extra(chain)
     go(chain)
+    grad_down_w = unpack_cols(*take(dw))
     depth = x.shape[1]
     small = small.reshape(-1)
     norms = small[:4 * depth].reshape(4, depth)
     bias_sum = jnp.sum(jnp.where(tp_row, small[4 * depth:].reshape(n_tp, -1), 0.0), axis=0)
-    grad_query_w, grad_key_w, grad_value_w, grad_output_w = unpack_rows(*take(chain), 4, True)
+    grad_query_w, grad_key_w, grad_value_w = unpack_rows(*take(chain), 3)
+    grad_output_w = grad_output_w.astype(F32)
     norm_one, _, _ = layer_back(grad_one.astype(F32), unit_one, inverse_one, gain_one)
     grad_tokens = (grad_mixed + norm_one).astype(BF16)
     return (

time: 961 us -> 995 us (1.035)
  waiting for transfers between devices: 377 us -> 417 us
  local copies, waits for them, and re-layouts: 54.3 us -> 37.3 us
  matrix products: 113 us -> 125 us
    psum x0 -> x1, waiting for transfers between devices: none -> 46.7 us  [local(): grad_output_w = lax.psum(after(grad_output_w, grad_one), 'ctx')]
    ppermute x46, waiting for transfers between devices: 191 us -> 171 us  [ctx_swap(): return lax.ppermute(x, 'ctx', [(i, i ^ mask) for i in range(n)])]
    ppermute x5, starting transfers between devices: 23.4 us -> 6.02 us  [sum_over_all(): x = x + lax.ppermute(x, axis, [(i, i ^ 1 << bit) for i in range(n)])]
    unnamed x188 -> x166, local copies, waits for them, and re-layouts: 25.9 us -> 14.2 us
    dot_general x8 -> x7, matrix products: 47.4 us -> 58 us  [rc(): lax.dot_general(left, right, (((0,), (0,)), ((), ())), preferred_element_...]
  transfers between devices with their start and end apart: 69 -> 70, of which waited for: 30 -> 30; matrix products, arithmetic and copies ran while one was open for 17% -> 20% of each run, Pallas kernels for 22% -> 20%
where the time goes in v9:
time: 995 us; the launch traced here: 981 us
  waiting for transfers between devices  417 us (42%)
  Pallas kernels  239 us (24%)
  matrix products  125 us (13%)
  other arithmetic  84 us (8%)
  starting transfers between devices  63.7 us (6%)
  local copies, waits for them, and re-layouts  37.3 us (4%)
  between operations  15.8 us (2%)
    ppermute x46, waiting for transfers between devices, ctx_swap(): return lax.ppermute(x, 'ctx', [(i, i ^ mask) for i in range(n)])  171 us
    pallas_call x4, Pallas kernels, attention_call(): pl.pallas_call(kernel, grid_spec=pltpu.PrefetchScalarGridSpec(num_scalar_...  166 us
    all_gather x4, waiting for transfers between devices, all_rows(): return lax.all_gather(x, 'tp', axis=0, tiled=True)  101 us
    dot_general x7, matrix products, rc(): lax.dot_general(left, right, (((0,), (0,)), ((), ())), preferred_element_...  58 us
    dot_general x6, matrix products, nt(): lax.dot_general(a, b, (((1,), (1,)), ((), ())), preferred_element_type=jn...  51.1 us
    psum x1, waiting for transfers between devices, local(): grad_output_w = lax.psum(after(grad_output_w, grad_one), 'ctx')  46.7 us
    ppermute x46, starting transfers between devices, ctx_swap(): return lax.ppermute(x, 'ctx', [(i, i ^ mask) for i in range(n)])  44.8 us
    ppermute x6, waiting for transfers between devices, tp_shift(): return lax.ppermute(x, 'tp', [(i, (i + d) % n) for i in range(n)])  34.1 us
  transfers between devices with their start and end apart: 70, of which 30 were waited for; matrix products, arithmetic and copies ran while one was open for 20% of the time, Pallas kernels for 20%

profile of v9, /device:TPU:0, one launch (start us, length us, event | category | flops | bytes accessed | tf_op | source)
XLA Modules:
  0.0 981.2 jit_solution(11550446565281852253)
XLA Ops:
  12.2 83.6 %all-gather.8.cloned.1.call-done.h_ref = bf16[1024,2048]{1,0:T(8,128)(2,1)} async-done(((bf16[256,2048]{1,0:T(8,128)(2,1)}), bf16[1024,2048]{1,0:T(8,128)(2,1)}) %all-gather.8.cloned.1.call-update) | async-done | bytes 4194320 | tf_op jit(solution)/shard_map/all_gather | solution.py:553
  98.6 11.8 %project.1 = (bf16[4,256,512]{2,1,0:T(8,128)(2,1)S(1)}, bf16[2,4,256,512]{3,2,1,0:T(8,128)(2,1)}) custom-call(bf16[1024,2048]{1,0:T(8,128)(2,1)} %all-gather.8.cloned.1.call-done.h_ref, bf16[2048,512]{1,0:T(8,128)(2,1)} %wq_ref.1, bf16[2048,512]{1,0:T(8,128)(2,1)} %wk_ref.1, bf16[2048,512]{1,0:T(8,128)(2,1)} %wv_ref.1, ...), custom_call_target="tpu_custom_call" | custom-call | flops 6442450944 | bytes 6291456 | tf_op jit(solution)/shard_map/project/pallas_call | solution.py:345
  114.4 44.7 %collective-permute-done.3.refs_4_.refs_12_ = bf16[2,4,2,128,512]{4,3,2,1,0:T(8,128)(2,1)} collective-permute-done((bf16[2,4,2,128,512]{4,3,2,1,0:T(8,128)(2,1)}, bf16[2,4,2,128,512]{4,3,2,1,0:T(8,128)(2,1)}, u32[]{:S(2)}, u32[]{:S(2)}) %collective-permute-start.3) | collective-permute-done | bytes 2097184 | tf_op jit(solution)/shard_map/ppermute | solution.py:401
  168.7 10.2 %collective-permute-done.14 = bf16[64,2048]{1,0:T(8,128)(2,1)S(1)} collective-permute-done((bf16[64,2048]{1,0:T(8,128)(2,1)S(1)}, bf16[64,2048]{1,0:T(8,128)(2,1)S(1)}, u32[]{:S(2)}, u32[]{:S(2)}) %collective-permute-start.14) | collective-permute-done | bytes 262176 | tf_op jit(solution)/shard_map/ppermute | solution.py:637
  178.9 19.8 %collective-permute-done.13 = bf16[64,2048]{1,0:T(8,128)(2,1)S(1)} collective-permute-done((bf16[64,2048]{1,0:T(8,128)(2,1)S(1)}, bf16[64,2048]{1,0:T(8,128)(2,1)S(1)}, u32[]{:S(2)}, u32[]{:S(2)}) %collective-permute-start.13) | collective-permute-done | bytes 262176 | tf_op jit(solution)/shard_map/ppermute | solution.py:637
  200.1 6.0 collective-permute-done.8.refs_15_
  206.1 3.1 collective-permute-done.6.refs_7_
  210.6 50.6 %attend.1 = (bf16[4,256,512]{2,1,0:T(8,128)(2,1)}, bf16[4,256,128]{2,1,0:T(8,128)(2,1)}) custom-call(s32[4,16]{1,0:T(4,128)} %copy.48.place_ref, s32[4,2]{1,0:T(4,128)} %get-tuple-element.209.own_ref, bf16[4,256,512]{2,1,0:T(8,128)(2,1)} %copy-done.5, bf16[2,4,2,128,512]{4,3,2,1,0:T(8,128)(2,1)} %bitcast.5.refs_0_.refs_8_, ...), custom_call_target="tpu_custom_call" | custom-call | flops 8589934592 | bytes 16777216 | tf_op jit(solution)/shard_map/attend/pallas_call | solution.py:221
  263.5 3.8 collective-permute-start.11
  267.3 7.5 collective-permute-done.9
  274.8 10.0 %collective-permute-done.10 = bf16[256,512]{1,0:T(8,128)(2,1)S(1)} collective-permute-done((bf16[256,512]{1,0:T(8,128)(2,1)S(1)}, bf16[256,512]{1,0:T(8,128)(2,1)S(1)}, u32[]{:S(2)}, u32[]{:S(2)}) %collective-permute-start.10) | collective-permute-done | bytes 262176 | tf_op jit(solution)/shard_map/ppermute | solution.py:558
  285.8 6.1 fusion.76
  295.7 3.5 collective-permute-start.18
  300.6 28.0 %collective-permute-done.20.refs_6_.refs_14_ = bf16[1,4,2,128,640]{4,3,2,1,0:T(8,128)(2,1)} collective-permute-done((bf16[1,4,2,128,640]{4,3,2,1,0:T(8,128)(2,1)}, bf16[1,4,2,128,640]{4,3,2,1,0:T(8,128)(2,1)}, u32[]{:S(2)}, u32[]{:S(2)}) %collective-permute-start.20) | collective-permute-done | bytes 1310752 | tf_op jit(solution)/shard_map/ppermute | solution.py:401
  328.6 25.5 %collective-permute-done.18.refs_4_.refs_12_ = bf16[1,4,2,128,640]{4,3,2,1,0:T(8,128)(2,1)} collective-permute-done((bf16[1,4,2,128,640]{4,3,2,1,0:T(8,128)(2,1)}, bf16[1,4,2,128,640]{4,3,2,1,0:T(8,128)(2,1)}, u32[]{:S(2)}, u32[]{:S(2)}) %collective-permute-start.18) | collective-permute-done | bytes 1310752 | tf_op jit(solution)/shard_map/ppermute | solution.py:401
  354.7 2.9 collective-permute-done.19.refs_5_.refs_13_
  359.4 17.9 %all-gather.12.cloned.1.call-done.h_ref = bf16[1024,2048]{1,0:T(8,128)(2,1)} async-done(((bf16[256,2048]{1,0:T(8,128)(2,1)}), bf16[1024,2048]{1,0:T(8,128)(2,1)}) %all-gather.12.cloned.1.call-update) | async-done | bytes 4194320 | tf_op jit(solution)/shard_map/all_gather | solution.py:553
  377.3 28.4 %mlp.1 = (bf16[1024,1408]{1,0:T(8,128)(2,1)}, bf16[1024,2816]{1,0:T(8,128)(2,1)}) custom-call(bf16[1024,2048]{1,0:T(8,128)(2,1)} %all-gather.12.cloned.1.call-done.h_ref, bf16[1024,2048]{1,0:T(8,128)(2,1)} %all-gather.10.cloned.1.call-done.dy_ref, bf16[2048,1408]{1,0:T(8,128)(2,1)} %gate_ref.1, bf16[2048,1408]{1,0:T(8,128)(2,1)} %up_ref.1, ...), custom_call_target="tpu_custom_call" | custom-call | flops 17716740096 | bytes 38273024 | tf_op jit(solution)/shard_map/mlp/pallas_call | solution.py:385
  405.7 9.7 fusion.4
  415.5 11.1 %add_convert_fusion.1 = bf16[1024,2048]{1,0:T(8,128)(2,1)} fusion(f32[1024,2048]{1,0:T(8,128)S(1)} %fusion.4, bf16[2048,1408]{1,0:T(8,128)(2,1)} %up_ref.1, bf16[1024,2816]{1,0:T(8,128)(2,1)S(1)} %copy-done.68), kind=kOutput, calls=%fused_computation.3 | convolution fusion | flops 5909774336 | bytes 21233664 | tf_op jit(solution)/shard_map/dot_general | solution.py:15
  426.6 11.1 %convolution_convert_fusion = bf16[1024,2816]{1,0:T(8,128)(2,1)} fusion(bf16[1024,2816]{1,0:T(8,128)(2,1)} %get-tuple-element.121, bf16[1024,2048]{1,0:T(8,128)(2,1)} %all-gather.12.cloned.1.call-done.h_ref, s32[]{:T(128)S(6)} %select_n.382), kind=kOutput, calls=%fused_computation.8 | convolution fusion | flops 5908463616 | bytes 13631492 | tf_op jit(solution)/shard_map/dot_general | solution.py:290
  437.7 16.0 %convolution_convert_fusion.3 = bf16[1408,1024]{1,0:T(8,128)(2,1)} fusion(bf16[1024,1408]{1,0:T(8,128)(2,1)S(1)} %copy-done.69, bf16[1024,2048]{1,0:T(8,128)(2,1)S(1)} %copy-done.63, s32[]{:T(128)S(6)} %select_n.382), kind=kOutput, calls=%fused_computation.11 | convolution fusion | flops 2954231808 | bytes 7864324 | tf_op jit(solution)/shard_map/dot_general | solution.py:290
  454.0 5.3 collective-permute-done.23
  459.3 6.7 add_convert_fusion.3
  467.9 10.5 %add_convert_fusion = bf16[1024,2816]{1,0:T(8,128)(2,1)S(1)} fusion(bf16[1024,2816]{1,0:T(8,128)(2,1)} %collective-permute-done.22, bf16[1024,2816]{1,0:T(8,128)(2,1)} %get-tuple-element.121, bf16[1024,2048]{1,0:T(8,128)(2,1)S(1)} %copy-done.65, s32[]{:T(128)S(6)} %select_n.381), kind=kOutput, calls=%fused_computation | convolution fusion | flops 5914230784 | bytes 19398660 | tf_op jit(solution)/shard_map/dot_general | solution.py:290
  484.4 8.2 convolution_convert_fusion.1
  492.5 21.6 %collective-permute-done.24 = bf16[256,2816]{1,0:T(8,128)(2,1)} collective-permute-done((bf16[256,2816]{1,0:T(8,128)(2,1)}, bf16[256,2816]{1,0:T(8,128)(2,1)}, u32[]{:S(2)}, u32[]{:S(2)}) %collective-permute-start.24) | collective-permute-done | bytes 1441824 | tf_op jit(solution)/shard_map/ppermute | solution.py:401
  524.9 4.6 reduce-scatter.4.cloned.1.call-done
  529.4 2.9 fusion.23
  532.3 2.7 fusion.70
  535.0 6.1 convolution_convert_fusion.5
  550.9 12.3 %collective-permute-done.26 = bf16[256,512]{1,0:T(8,128)(2,1)S(1)} collective-permute-done((bf16[256,512]{1,0:T(8,128)(2,1)S(1)}, bf16[256,512]{1,0:T(8,128)(2,1)S(1)}, u32[]{:S(2)}, u32[]{:S(2)}) %collective-permute-start.26) | collective-permute-done | bytes 262176 | tf_op jit(solution)/shard_map/ppermute | solution.py:558
  563.2 4.3 collective-permute-done.27
  576.8 50.8 %query_grad.1 = bf16[4,256,512]{2,1,0:T(8,128)(2,1)} custom-call(s32[4,16]{1,0:T(4,128)} %copy.48.place_ref, s32[4,2]{1,0:T(4,128)} %get-tuple-element.209.own_ref, bf16[4,256,512]{2,1,0:T(8,128)(2,1)} %copy-done.5, bf16[4,256,512]{2,1,0:T(8,128)(2,1)} %bitcast.76, bf16[4,256,128]{2,1,0:T(8,128)(2,1)} %get-tuple-element.114.qx_ref, ...), custom_call_target="tpu_custom_call" | custom-call | flops 12884901888 | bytes 16777216 | tf_op jit(solution)/shard_map/query_grad/pallas_call | solution.py:221
  627.6 7.7 fusion.78
  641.1 3.3 maximum_select_fusion.5
  644.4 6.4 all-gather.14.cloned.1.call-done.refs_16_.refs_17_
  652.1 2.9 collective-permute-start.35
  657.8 25.1 %key_value_grad.2 = (bf16[2,256,512]{2,1,0:T(8,128)(2,1)}, bf16[2,256,512]{2,1,0:T(8,128)(2,1)}) custom-call(s32[4,16]{1,0:T(4,128)} %copy.48.place_ref, s32[4,2]{1,0:T(4,128)} %get-tuple-element.209.own_ref, s32[4,16]{1,0:T(4,128)} %slots_ref.3, bf16[2,4,256,512]{3,2,1,0:T(8,128)(2,1)} %get-tuple-element.108.k_ref.v_ref, ...), custom_call_target="tpu_custom_call" | custom-call | flops 8589934592 | bytes 8388608 | tf_op jit(solution)/shard_map/key_value_grad/pallas_call | solution.py:221
  686.6 39.9 %key_value_grad.3 = (bf16[2,256,512]{2,1,0:T(8,128)(2,1)}, bf16[2,256,512]{2,1,0:T(8,128)(2,1)}) custom-call(s32[4,16]{1,0:T(4,128)} %copy.48.place_ref, s32[4,2]{1,0:T(4,128)} %get-tuple-element.209.own_ref, s32[4,16]{1,0:T(4,128)} %slots_ref.3, bf16[2,4,256,512]{3,2,1,0:T(8,128)(2,1)} %get-tuple-element.108.k_ref.v_ref, ...), custom_call_target="tpu_custom_call" | custom-call | flops 8589934592 | bytes 8388608 | tf_op jit(solution)/shard_map/key_value_grad/pallas_call | solution.py:221
  728.7 5.8 fusion.79
  734.4 10.8 %fusion.77 = (bf16[1024,2048]{1,0:T(8,128)(2,1)}, f32[1024,2048]{1,0:T(8,128)}) fusion(f32[1024,2048]{1,0:T(8,128)} %fusion.79, f32[1024,2048]{1,0:T(8,128)S(1)} %bitcast.72, bf16[1024,512]{1,0:T(8,128)(2,1)S(1)} %bitcast.69, bf16[2048,512]{1,0:T(8,128)(2,1)S(1)} %copy-done.35), kind=kOutput, calls=%fused_computation.208 | convolution fusion | flops 2153775104 | bytes 32505856 | tf_op jit(solution)/shard_map/dot_general | solution.py:15
  747.7 4.8 convolution_convert_fusion.2
  753.1 6.2 collective-permute-start.46
  765.5 3.3 pad_maximum_fusion.half_ref
  768.8 2.5 convert_reduce_fusion
  771.3 4.3 fusion.69
  775.8 5.2 add_convert_fusion.2
  793.2 10.1 %collective-permute-done.43 = bf16[256,1536]{1,0:T(8,128)(2,1)} collective-permute-done((bf16[256,1536]{1,0:T(8,128)(2,1)}, bf16[256,1536]{1,0:T(8,128)(2,1)}, u32[]{:S(2)}, u32[]{:S(2)}) %collective-permute-start.43) | collective-permute-done | bytes 786464 | tf_op jit(solution)/shard_map/ppermute | solution.py:401
  812.6 7.0 collective-permute-done.39
  820.9 3.0 collective-permute-done.40
  825.3 4.9 collective-permute-done.41
  830.1 3.0 collective-permute-start.42
  833.1 5.9 collective-permute-done.42
  843.4 13.7 %unpack_rows.2 = (f32[2048,1408]{1,0:T(8,128)}, f32[2048,1408]{1,0:T(8,128)}) custom-call(s32[1]{0:T(128)} %bitcast.19.core_ref, bf16[1024,2816]{1,0:T(8,128)(2,1)} %pad_maximum_fusion.half_ref, bf16[1024,2816]{1,0:T(8,128)(2,1)} %collective-permute-done.53.other_ref), custom_call_target="tpu_custom_call" | custom-call | bytes 34603008 | tf_op jit(solution)/shard_map/unpack_rows/pallas_call | solution.py:512
  859.7 8.5 collective-permute-done.58
  870.2 2.5 maximum_select_fusion.7
  872.7 10.5 %collective-permute-done.55 = bf16[256,1536]{1,0:T(8,128)(2,1)} collective-permute-done((bf16[256,1536]{1,0:T(8,128)(2,1)S(1)}, bf16[256,1536]{1,0:T(8,128)(2,1)}, u32[]{:S(2)}, u32[]{:S(2)}) %collective-permute-start.55) | collective-permute-done | bytes 786464 | tf_op jit(solution)/shard_map/ppermute | solution.py:401
  891.4 3.8 convolution_convert_fusion.4
  901.4 3.4 fusion.17
  904.9 8.8 unpack_cols.1
  913.7 46.7 %all-reduce.3.cloned.1.call-done = bf16[512,2048]{1,0:T(8,128)(2,1)} async-done(((bf16[512,2048]{1,0:T(8,128)(2,1)}), bf16[512,2048]{1,0:T(8,128)(2,1)}) %all-reduce.3.cloned.1.call-update) | async-done | bytes 2097168 | tf_op jit(solution)/shard_map/psum | solution.py:739
  960.4 4.3 convert_element_type.300
  964.7 9.4 unpack_rows.3
  (397 shorter events, 144.6 us)
Async XLA Ops:
  7.2 88.5 %all-gather.8.cloned.1.call-start = ((), (), s32[]{:S(2)}) async-start(), calls=%async_computation.3 | async-start | bytes 5242880 | tf_op jit(solution)/shard_map/all_gather | solution.py:553
  12.1 197.1 %all-gather.10.cloned.1.call-start = ((), (), s32[]{:S(2)}) async-start(), calls=%async_computation.4 | async-start | bytes 5242880 | tf_op jit(solution)/shard_map/all_gather | solution.py:553
  95.7 189.2 %all-gather.18.cloned.1.call-start = ((), (), s32[]{:S(2)}) async-start(), calls=%async_computation.12 | async-start | bytes 9437184 | tf_op jit(solution)/shard_map/all_gather | solution.py:668
  111.4 47.7 %collective-permute-start.3 = (bf16[2,4,2,128,512]{4,3,2,1,0:T(8,128)(2,1)}, bf16[2,4,2,128,512]{4,3,2,1,0:T(8,128)(2,1)}, u32[]{:S(2)}, u32[]{:S(2)}) collective-permute-start(bf16[2,4,2,128,512]{4,3,2,1,0:T(8,128)(2,1)} %bitcast.5.refs_0_.refs_8_), channel_id=1, source_target_pairs={{0,16},{4,20},{8,24},{12,28},{16,0},{20,4},{24,8},{28,12},{1,17},{... | collective-permute-start | bytes 6291464 | tf_op jit(solution)/shard_map/ppermute | solution.py:401
  112.9 49.1 %collective-permute-start.1 = (bf16[2,4,2,128,512]{4,3,2,1,0:T(8,128)(2,1)}, bf16[2,4,2,128,512]{4,3,2,1,0:T(8,128)(2,1)}, u32[]{:S(2)}, u32[]{:S(2)}) collective-permute-start(bf16[2,4,2,128,512]{4,3,2,1,0:T(8,128)(2,1)} %bitcast.5.refs_0_.refs_8_), channel_id=1, source_target_pairs={{0,8},{4,12},{8,0},{12,4},{16,24},{20,28},{24,16},{28,20},{1,9},{5... | collective-permute-start | bytes 6291464 | tf_op jit(solution)/shard_map/ppermute | solution.py:401
  160.4 38.9 %collective-permute-start.7 = (bf16[1,4,2,128,512]{4,3,2,1,0:T(8,128)(2,1)S(1)}, bf16[1,4,2,128,512]{4,3,2,1,0:T(8,128)(2,1)}, u32[]{:S(2)}, u32[]{:S(2)}) collective-permute-start(bf16[1,4,2,128,512]{4,3,2,1,0:T(8,128)(2,1)S(1)} %slice.96), channel_id=1, source_target_pairs={{0,8},{4,12},{8,0},{12,4},{16,24},{20,28},{24,16},{28,20},{1,9},{5... | collective-permute-start | bytes 3145736 | tf_op jit(solution)/shard_map/ppermute | solution.py:401
  164.2 35.2 %collective-permute-start.5 = (bf16[1,4,2,128,512]{4,3,2,1,0:T(8,128)(2,1)}, bf16[1,4,2,128,512]{4,3,2,1,0:T(8,128)(2,1)}, u32[]{:S(2)}, u32[]{:S(2)}) collective-permute-start(bf16[1,4,2,128,512]{4,3,2,1,0:T(8,128)(2,1)} %slice.95), channel_id=1, source_target_pairs={{0,16},{4,20},{8,24},{12,28},{16,0},{20,4},{24,8},{28,12},{1,17},{... | collective-permute-start | bytes 3145736 | tf_op jit(solution)/shard_map/ppermute | solution.py:401
  165.7 13.2 %collective-permute-start.14 = (bf16[64,2048]{1,0:T(8,128)(2,1)S(1)}, bf16[64,2048]{1,0:T(8,128)(2,1)S(1)}, u32[]{:S(2)}, u32[]{:S(2)}) collective-permute-start(bf16[64,2048]{1,0:T(8,128)(2,1)S(1)} %constant_dynamic-slice_fusion.14), channel_id=1, source_target_pairs={{0,3},{1,0},{2,1},{3,2},{4,7},{5,4},{6,5},{7,6},{8,11},{9,8},{10,9... | collective-permute-start | bytes 786440 | tf_op jit(solution)/shard_map/ppermute | solution.py:637
  166.8 31.9 %collective-permute-start.13 = (bf16[64,2048]{1,0:T(8,128)(2,1)S(1)}, bf16[64,2048]{1,0:T(8,128)(2,1)S(1)}, u32[]{:S(2)}, u32[]{:S(2)}) collective-permute-start(bf16[64,2048]{1,0:T(8,128)(2,1)S(1)} %constant_dynamic-slice_fusion.14), channel_id=1, source_target_pairs={{0,2},{1,3},{2,0},{3,1},{4,6},{5,7},{6,4},{7,5},{8,10},{9,11},{10,... | collective-permute-start | bytes 786440 | tf_op jit(solution)/shard_map/ppermute | solution.py:637
  166.8 31.9 %collective-permute-start.12 = (bf16[64,2048]{1,0:T(8,128)(2,1)S(1)}, bf16[64,2048]{1,0:T(8,128)(2,1)S(1)}, u32[]{:S(2)}, u32[]{:S(2)}) collective-permute-start(bf16[64,2048]{1,0:T(8,128)(2,1)S(1)} %constant_dynamic-slice_fusion.14), channel_id=1, source_target_pairs={{0,1},{1,2},{2,3},{3,0},{4,5},{5,6},{6,7},{7,4},{8,9},{9,10},{10,1... | collective-permute-start | bytes 786440 | tf_op jit(solution)/shard_map/ppermute | solution.py:637
  178.9 21.1 %collective-permute-start = (bf16[2,4,2,128,512]{4,3,2,1,0:T(8,128)(2,1)}, bf16[2,4,2,128,512]{4,3,2,1,0:T(8,128)(2,1)}, u32[]{:S(2)}, u32[]{:S(2)}) collective-permute-start(bf16[2,4,2,128,512]{4,3,2,1,0:T(8,128)(2,1)} %bitcast.5.refs_0_.refs_8_), channel_id=1, source_target_pairs={{0,4},{4,0},{8,12},{12,8},{16,20},{20,16},{24,28},{28,24},{1,5},{5... | collective-permute-start | bytes 6291464 | tf_op jit(solution)/shard_map/ppermute | solution.py:401
  198.7 10.5 %collective-permute-start.4 = (bf16[2,4,2,128,512]{4,3,2,1,0:T(8,128)(2,1)}, bf16[2,4,2,128,512]{4,3,2,1,0:T(8,128)(2,1)}, u32[]{:S(2)}, u32[]{:S(2)}) collective-permute-start(bf16[2,4,2,128,512]{4,3,2,1,0:T(8,128)(2,1)} %collective-permute-done.3.refs_4_.refs_12_), channel_id=1, source_target_pairs={{0,4},{4,0},{8,12},{12,8},{16,20},{20,16},{24,28},{28,24},{1,5},{5... | collective-permute-start | bytes 6291464 | tf_op jit(solution)/shard_map/ppermute | solution.py:401
  198.7 10.5 %collective-permute-start.2 = (bf16[2,4,2,128,512]{4,3,2,1,0:T(8,128)(2,1)}, bf16[2,4,2,128,512]{4,3,2,1,0:T(8,128)(2,1)}, u32[]{:S(2)}, u32[]{:S(2)}) collective-permute-start(bf16[2,4,2,128,512]{4,3,2,1,0:T(8,128)(2,1)} %collective-permute-done.1.refs_2_.refs_10_), channel_id=1, source_target_pairs={{0,4},{4,0},{8,12},{12,8},{16,20},{20,16},{24,28},{28,24},{1,5},{5... | collective-permute-start | bytes 6291464 | tf_op jit(solution)/shard_map/ppermute | solution.py:401
  199.4 6.7 collective-permute-start.8
  199.5 9.7 collective-permute-start.6
  209.3 168.0 %all-gather.12.cloned.1.call-start = ((), (), s32[]{:S(2)}) async-start(), calls=%async_computation.5 | async-start | bytes 5242880 | tf_op jit(solution)/shard_map/all_gather | solution.py:553
  263.5 11.3 %collective-permute-start.9 = (bf16[256,512]{1,0:T(8,128)(2,1)}, bf16[256,512]{1,0:T(8,128)(2,1)S(1)}, u32[]{:S(2)}, u32[]{:S(2)}) collective-permute-start(bf16[256,512]{1,0:T(8,128)(2,1)} %get-tuple-element.222), channel_id=1, source_target_pairs={{0,1},{1,2},{2,3},{3,0},{4,5},{5,6},{6,7},{7,4},{8,9},{9,10},{10,1... | collective-permute-start | bytes 786440 | tf_op jit(solution)/shard_map/ppermute | solution.py:558
  263.5 21.3 %collective-permute-start.10 = (bf16[256,512]{1,0:T(8,128)(2,1)S(1)}, bf16[256,512]{1,0:T(8,128)(2,1)S(1)}, u32[]{:S(2)}, u32[]{:S(2)}) collective-permute-start(bf16[256,512]{1,0:T(8,128)(2,1)S(1)} %get-tuple-element.221), channel_id=1, source_target_pairs={{0,2},{1,3},{2,0},{3,1},{4,6},{5,7},{6,4},{7,5},{8,10},{9,11},{10,... | collective-permute-start | bytes 786440 | tf_op jit(solution)/shard_map/ppermute | solution.py:558
  263.5 21.4 %collective-permute-start.11 = (bf16[256,512]{1,0:T(8,128)(2,1)S(1)}, bf16[256,512]{1,0:T(8,128)(2,1)S(1)}, u32[]{:S(2)}, u32[]{:S(2)}) collective-permute-start(bf16[256,512]{1,0:T(8,128)(2,1)S(1)} %get-tuple-element.220), channel_id=1, source_target_pairs={{0,3},{1,0},{2,1},{3,2},{4,7},{5,4},{6,5},{7,6},{8,11},{9,8},{10,9... | collective-permute-start | bytes 786440 | tf_op jit(solution)/shard_map/ppermute | solution.py:558
  294.2 235.2 %reduce-scatter.4.cloned.1.call-start = ((), (), s32[]{:S(2)}) async-start(), calls=%async_computation.6 | async-start | bytes 5242880 | tf_op jit(solution)/shard_map/reduce_scatter | solution.py:581
  295.7 32.9 %collective-permute-start.20 = (bf16[1,4,2,128,640]{4,3,2,1,0:T(8,128)(2,1)}, bf16[1,4,2,128,640]{4,3,2,1,0:T(8,128)(2,1)}, u32[]{:S(2)}, u32[]{:S(2)}) collective-permute-start(bf16[1,4,2,128,640]{4,3,2,1,0:T(8,128)(2,1)} %bitcast.12.refs_0_.refs_8_), channel_id=1, source_target_pairs={{0,24},{4,28},{8,16},{12,20},{16,8},{20,12},{24,0},{28,4},{1,25},{... | collective-permute-start | bytes 3932168 | tf_op jit(solution)/shard_map/ppermute | solution.py:401
  295.7 58.5 %collective-permute-start.18 = (bf16[1,4,2,128,640]{4,3,2,1,0:T(8,128)(2,1)}, bf16[1,4,2,128,640]{4,3,2,1,0:T(8,128)(2,1)}, u32[]{:S(2)}, u32[]{:S(2)}) collective-permute-start(bf16[1,4,2,128,640]{4,3,2,1,0:T(8,128)(2,1)} %bitcast.12.refs_0_.refs_8_), channel_id=1, source_target_pairs={{0,16},{4,20},{8,24},{12,28},{16,0},{20,4},{24,8},{28,12},{1,17},{... | collective-permute-start | bytes 3932168 | tf_op jit(solution)/shard_map/ppermute | solution.py:401
  299.2 55.0 %collective-permute-start.16 = (bf16[1,4,2,128,640]{4,3,2,1,0:T(8,128)(2,1)}, bf16[1,4,2,128,640]{4,3,2,1,0:T(8,128)(2,1)}, u32[]{:S(2)}, u32[]{:S(2)}) collective-permute-start(bf16[1,4,2,128,640]{4,3,2,1,0:T(8,128)(2,1)} %bitcast.12.refs_0_.refs_8_), channel_id=1, source_target_pairs={{0,8},{4,12},{8,0},{12,4},{16,24},{20,28},{24,16},{28,20},{1,9},{5... | collective-permute-start | bytes 3932168 | tf_op jit(solution)/shard_map/ppermute | solution.py:401
  300.6 54.0 %collective-permute-start.15 = (bf16[1,4,2,128,640]{4,3,2,1,0:T(8,128)(2,1)}, bf16[1,4,2,128,640]{4,3,2,1,0:T(8,128)(2,1)}, u32[]{:S(2)}, u32[]{:S(2)}) collective-permute-start(bf16[1,4,2,128,640]{4,3,2,1,0:T(8,128)(2,1)} %bitcast.12.refs_0_.refs_8_), channel_id=1, source_target_pairs={{0,4},{4,0},{8,12},{12,8},{16,20},{20,16},{24,28},{28,24},{1,5},{5... | collective-permute-start | bytes 3932168 | tf_op jit(solution)/shard_map/ppermute | solution.py:401
  328.6 26.0 %collective-permute-start.21 = (bf16[1,4,2,128,640]{4,3,2,1,0:T(8,128)(2,1)}, bf16[1,4,2,128,640]{4,3,2,1,0:T(8,128)(2,1)}, u32[]{:S(2)}, u32[]{:S(2)}) collective-permute-start(bf16[1,4,2,128,640]{4,3,2,1,0:T(8,128)(2,1)} %collective-permute-done.20.refs_6_.refs_14_), channel_id=1, source_target_pairs={{0,4},{4,0},{8,12},{12,8},{16,20},{20,16},{24,28},{28,24},{1,5},{5... | collective-permute-start | bytes 3932168 | tf_op jit(solution)/shard_map/ppermute | solution.py:401
  437.7 30.2 %collective-permute-start.22 = (bf16[1024,2816]{1,0:T(8,128)(2,1)}, bf16[1024,2816]{1,0:T(8,128)(2,1)}, u32[]{:S(2)}, u32[]{:S(2)}) collective-permute-start(bf16[1024,2816]{1,0:T(8,128)(2,1)} %convolution_convert_fusion), channel_id=1, source_target_pairs={{0,4},{4,0},{8,12},{12,8},{16,20},{20,16},{24,28},{28,24},{1,5},{5... | collective-permute-start | bytes 17301512 | tf_op jit(solution)/shard_map/ppermute | solution.py:401
  454.0 196.8 %all-gather.14.cloned.1.call-start = ((), (), s32[]{:S(2)}) async-start(), calls=%async_computation.8 | async-start | bytes 11796480 | tf_op jit(solution)/shard_map/all_gather | solution.py:710
  480.1 34.0 %collective-permute-start.24 = (bf16[256,2816]{1,0:T(8,128)(2,1)}, bf16[256,2816]{1,0:T(8,128)(2,1)}, u32[]{:S(2)}, u32[]{:S(2)}) collective-permute-start(bf16[256,2816]{1,0:T(8,128)(2,1)} %constant_dynamic-slice_fusion.13), channel_id=1, source_target_pairs={{0,8},{4,12},{8,0},{12,4},{16,24},{20,28},{24,16},{28,20},{1,9},{5... | collective-permute-start | bytes 4325384 | tf_op jit(solution)/shard_map/ppermute | solution.py:401
  482.9 33.7 %collective-permute-start.25 = (bf16[256,2816]{1,0:T(8,128)(2,1)}, bf16[256,2816]{1,0:T(8,128)(2,1)}, u32[]{:S(2)}, u32[]{:S(2)}) collective-permute-start(bf16[256,2816]{1,0:T(8,128)(2,1)} %constant_dynamic-slice_fusion.12), channel_id=1, source_target_pairs={{0,16},{4,20},{8,24},{12,28},{16,0},{20,4},{24,8},{28,12},{1,17},{... | collective-permute-start | bytes 4325384 | tf_op jit(solution)/shard_map/ppermute | solution.py:401
  519.7 21.4 %collective-permute-start.29 = (bf16[128,2816]{1,0:T(8,128)(2,1)}, bf16[128,2816]{1,0:T(8,128)(2,1)}, u32[]{:S(2)}, u32[]{:S(2)}) collective-permute-start(bf16[128,2816]{1,0:T(8,128)(2,1)} %constant_dynamic-slice_fusion.8), channel_id=1, source_target_pairs={{0,16},{4,20},{8,24},{12,28},{16,0},{20,4},{24,8},{28,12},{1,17},{... | collective-permute-start | bytes 2162696 | tf_op jit(solution)/shard_map/ppermute | solution.py:401
  524.3 17.1 %collective-permute-start.30 = (bf16[128,2816]{1,0:T(8,128)(2,1)}, bf16[128,2816]{1,0:T(8,128)(2,1)}, u32[]{:S(2)}, u32[]{:S(2)}) collective-permute-start(bf16[128,2816]{1,0:T(8,128)(2,1)} %constant_dynamic-slice_fusion.7), channel_id=1, source_target_pairs={{0,8},{4,12},{8,0},{12,4},{16,24},{20,28},{24,16},{28,20},{1,9},{5... | collective-permute-start | bytes 2162696 | tf_op jit(solution)/shard_map/ppermute | solution.py:401
  541.7 25.9 %collective-permute-start.28 = (bf16[256,512]{1,0:T(8,128)(2,1)S(1)}, bf16[256,512]{1,0:T(8,128)(2,1)S(1)}, u32[]{:S(2)}, u32[]{:S(2)}) collective-permute-start(bf16[256,512]{1,0:T(8,128)(2,1)S(1)} %get-tuple-element.216), channel_id=1, source_target_pairs={{0,3},{1,0},{2,1},{3,2},{4,7},{5,4},{6,5},{7,6},{8,11},{9,8},{10,9... | collective-permute-start | bytes 786440 | tf_op jit(solution)/shard_map/ppermute | solution.py:558
  544.0 23.6 %collective-permute-start.27 = (bf16[256,512]{1,0:T(8,128)(2,1)S(1)}, bf16[256,512]{1,0:T(8,128)(2,1)S(1)}, u32[]{:S(2)}, u32[]{:S(2)}) collective-permute-start(bf16[256,512]{1,0:T(8,128)(2,1)S(1)} %get-tuple-element.217), channel_id=1, source_target_pairs={{0,2},{1,3},{2,0},{3,1},{4,6},{5,7},{6,4},{7,5},{8,10},{9,11},{10,... | collective-permute-start | bytes 786440 | tf_op jit(solution)/shard_map/ppermute | solution.py:558
  544.4 18.8 %collective-permute-start.26 = (bf16[256,512]{1,0:T(8,128)(2,1)S(1)}, bf16[256,512]{1,0:T(8,128)(2,1)S(1)}, u32[]{:S(2)}, u32[]{:S(2)}) collective-permute-start(bf16[256,512]{1,0:T(8,128)(2,1)S(1)} %get-tuple-element.218), channel_id=1, source_target_pairs={{0,1},{1,2},{2,3},{3,0},{4,5},{5,6},{6,7},{7,4},{8,9},{9,10},{10,1... | collective-permute-start | bytes 786440 | tf_op jit(solution)/shard_map/ppermute | solution.py:558
  570.2 175.0 %all-gather.16.cloned.1.call-start = ((), (), s32[]{:S(2)}) async-start(), calls=%async_computation.9 | async-start | bytes 5242880 | tf_op jit(solution)/shard_map/all_gather | solution.py:553
  571.8 63.5 %collective-permute-start.34 = (bf16[352,1024]{1,0:T(8,128)(2,1)}, bf16[352,1024]{1,0:T(8,128)(2,1)}, u32[]{:S(2)}, u32[]{:S(2)}) collective-permute-start(bf16[352,1024]{1,0:T(8,128)(2,1)} %constant_dynamic-slice_fusion.5), channel_id=1, source_target_pairs={{0,16},{4,20},{8,24},{12,28},{16,0},{20,4},{24,8},{28,12},{1,17},{... | collective-permute-start | bytes 2162696 | tf_op jit(solution)/shard_map/ppermute | solution.py:401
  574.2 61.1 %collective-permute-start.33 = (bf16[352,1024]{1,0:T(8,128)(2,1)}, bf16[352,1024]{1,0:T(8,128)(2,1)}, u32[]{:S(2)}, u32[]{:S(2)}) collective-permute-start(bf16[352,1024]{1,0:T(8,128)(2,1)} %constant_dynamic-slice_fusion.6), channel_id=1, source_target_pairs={{0,8},{4,12},{8,0},{12,4},{16,24},{20,28},{24,16},{28,20},{1,9},{5... | collective-permute-start | bytes 2162696 | tf_op jit(solution)/shard_map/ppermute | solution.py:401
  575.7 63.2 %collective-permute-start.32 = (bf16[128,2816]{1,0:T(8,128)(2,1)}, bf16[128,2816]{1,0:T(8,128)(2,1)}, u32[]{:S(2)}, u32[]{:S(2)}) collective-permute-start(bf16[128,2816]{1,0:T(8,128)(2,1)} %add_convert_fusion.12), channel_id=1, source_target_pairs={{0,8},{4,12},{8,0},{12,4},{16,24},{20,28},{24,16},{28,20},{1,9},{5... | collective-permute-start | bytes 2162696 | tf_op jit(solution)/shard_map/ppermute | solution.py:401
  576.2 62.7 %collective-permute-start.31 = (bf16[128,2816]{1,0:T(8,128)(2,1)}, bf16[128,2816]{1,0:T(8,128)(2,1)}, u32[]{:S(2)}, u32[]{:S(2)}) collective-permute-start(bf16[128,2816]{1,0:T(8,128)(2,1)} %add_convert_fusion.13), channel_id=1, source_target_pairs={{0,16},{4,20},{8,24},{12,28},{16,0},{20,4},{24,8},{28,12},{1,17},{... | collective-permute-start | bytes 2162696 | tf_op jit(solution)/shard_map/ppermute | solution.py:401
  650.8 208.9 %reduce-scatter.6.cloned.1.call-start = ((), (), s32[]{:S(2)}) async-start(), calls=%async_computation.7 | async-start | bytes 5242880 | tf_op jit(solution)/shard_map/reduce_scatter | solution.py:581
  651.6 247.4 %reduce-scatter.8.cloned.1.call-start = ((), (), s32[]{:S(2)}) async-start(), calls=%async_computation.10 | async-start | bytes 5242880 | tf_op jit(solution)/shard_map/reduce_scatter | solution.py:581
  652.1 30.8 %collective-permute-start.35 = (bf16[176,1024]{1,0:T(8,128)(2,1)S(1)}, bf16[176,1024]{1,0:T(8,128)(2,1)}, u32[]{:S(2)}, u32[]{:S(2)}) collective-permute-start(bf16[176,1024]{1,0:T(8,128)(2,1)S(1)} %constant_dynamic-slice_fusion.4), channel_id=1, source_target_pairs={{0,16},{4,20},{8,24},{12,28},{16,0},{20,4},{24,8},{28,12},{1,17},{... | collective-permute-start | bytes 1081352 | tf_op jit(solution)/shard_map/ppermute | solution.py:401
  655.8 27.2 %collective-permute-start.36 = (bf16[176,1024]{1,0:T(8,128)(2,1)}, bf16[176,1024]{1,0:T(8,128)(2,1)}, u32[]{:S(2)}, u32[]{:S(2)}) collective-permute-start(bf16[176,1024]{1,0:T(8,128)(2,1)} %constant_dynamic-slice_fusion.3), channel_id=1, source_target_pairs={{0,8},{4,12},{8,0},{12,4},{16,24},{20,28},{24,16},{28,20},{1,9},{5... | collective-permute-start | bytes 1081352 | tf_op jit(solution)/shard_map/ppermute | solution.py:401
  655.8 104.8 %collective-permute-start.52 = (bf16[256,2816]{1,0:T(8,128)(2,1)}, bf16[256,2816]{1,0:T(8,128)(2,1)}, u32[]{:S(2)}, u32[]{:S(2)}) collective-permute-start(bf16[256,2816]{1,0:T(8,128)(2,1)} %maximum_select_fusion.5), channel_id=1, source_target_pairs={{0,16},{4,20},{8,24},{12,28},{16,0},{20,4},{24,8},{28,12},{1,17},{... | collective-permute-start | bytes 4325384 | tf_op jit(solution)/shard_map/ppermute | solution.py:401
  656.4 104.1 %collective-permute-start.51 = (bf16[256,2816]{1,0:T(8,128)(2,1)S(1)}, bf16[256,2816]{1,0:T(8,128)(2,1)}, u32[]{:S(2)}, u32[]{:S(2)}) collective-permute-start(bf16[256,2816]{1,0:T(8,128)(2,1)S(1)} %maximum_select_fusion.4), channel_id=1, source_target_pairs={{0,8},{4,12},{8,0},{12,4},{16,24},{20,28},{24,16},{28,20},{1,9},{5... | collective-permute-start | bytes 4325384 | tf_op jit(solution)/shard_map/ppermute | solution.py:401
  752.5 23.1 %collective-permute-start.37 = (bf16[1024,1536]{1,0:T(8,128)(2,1)}, bf16[1024,1536]{1,0:T(8,128)(2,1)}, u32[]{:S(2)}, u32[]{:S(2)}) collective-permute-start(bf16[1024,1536]{1,0:T(8,128)(2,1)} %convolution_convert_fusion.2), channel_id=1, source_target_pairs={{0,4},{4,0},{8,12},{12,8},{16,20},{20,16},{24,28},{28,24},{1,5},{5... | collective-permute-start | bytes 9437192 | tf_op jit(solution)/shard_map/ppermute | solution.py:401
  753.1 35.5 %collective-permute-start.46 = (bf16[176,1024]{1,0:T(8,128)(2,1)}, bf16[176,1024]{1,0:T(8,128)(2,1)}, u32[]{:S(2)}, u32[]{:S(2)}) collective-permute-start(bf16[176,1024]{1,0:T(8,128)(2,1)} %add_convert_fusion.16), channel_id=1, source_target_pairs={{0,8},{4,12},{8,0},{12,4},{16,24},{20,28},{24,16},{28,20},{1,9},{5... | collective-permute-start | bytes 1081352 | tf_op jit(solution)/shard_map/ppermute | solution.py:401
  759.3 29.2 %collective-permute-start.45 = (bf16[176,1024]{1,0:T(8,128)(2,1)S(1)}, bf16[176,1024]{1,0:T(8,128)(2,1)}, u32[]{:S(2)}, u32[]{:S(2)}) collective-permute-start(bf16[176,1024]{1,0:T(8,128)(2,1)S(1)} %copy-done.36), channel_id=1, source_target_pairs={{0,16},{4,20},{8,24},{12,28},{16,0},{20,4},{24,8},{28,12},{1,17},{... | collective-permute-start | bytes 1081352 | tf_op jit(solution)/shard_map/ppermute | solution.py:401
  760.6 199.9 %all-reduce.3.cloned.1.call-start = ((), (), s32[]{:S(2)}) async-start(), calls=%async_computation.11 | async-start | bytes 4194304 | tf_op jit(solution)/shard_map/psum | solution.py:739
  768.8 74.6 %collective-permute-start.53 = (bf16[1024,2816]{1,0:T(8,128)(2,1)}, bf16[1024,2816]{1,0:T(8,128)(2,1)}, u32[]{:S(2)}, u32[]{:S(2)}) collective-permute-start(bf16[1024,2816]{1,0:T(8,128)(2,1)} %pad_maximum_fusion.half_ref), channel_id=1, source_target_pairs={{0,4},{4,0},{8,12},{12,8},{16,20},{20,16},{24,28},{28,24},{1,5},{5... | collective-permute-start | bytes 17301512 | tf_op jit(solution)/shard_map/ppermute | solution.py:401
  783.0 20.3 %collective-permute-start.43 = (bf16[256,1536]{1,0:T(8,128)(2,1)}, bf16[256,1536]{1,0:T(8,128)(2,1)}, u32[]{:S(2)}, u32[]{:S(2)}) collective-permute-start(bf16[256,1536]{1,0:T(8,128)(2,1)} %constant_dynamic-slice_fusion.2), channel_id=1, source_target_pairs={{0,8},{4,12},{8,0},{12,4},{16,24},{20,28},{24,16},{28,20},{1,9},{5... | collective-permute-start | bytes 2359304 | tf_op jit(solution)/shard_map/ppermute | solution.py:401
  783.2 20.1 %collective-permute-start.44 = (bf16[256,1536]{1,0:T(8,128)(2,1)}, bf16[256,1536]{1,0:T(8,128)(2,1)}, u32[]{:S(2)}, u32[]{:S(2)}) collective-permute-start(bf16[256,1536]{1,0:T(8,128)(2,1)} %constant_dynamic-slice_fusion.1), channel_id=1, source_target_pairs={{0,16},{4,20},{8,24},{12,28},{16,0},{20,4},{24,8},{28,12},{1,17},{... | collective-permute-start | bytes 2359304 | tf_op jit(solution)/shard_map/ppermute | solution.py:401
  805.5 33.5 %collective-permute-start.47 = (bf16[128,1536]{1,0:T(8,128)(2,1)}, bf16[128,1536]{1,0:T(8,128)(2,1)S(1)}, u32[]{:S(2)}, u32[]{:S(2)}) collective-permute-start(bf16[128,1536]{1,0:T(8,128)(2,1)} %constant_dynamic-slice_fusion), channel_id=1, source_target_pairs={{0,16},{4,20},{8,24},{12,28},{16,0},{20,4},{24,8},{28,12},{1,17},{... | collective-permute-start | bytes 1179656 | tf_op jit(solution)/shard_map/ppermute | solution.py:401
  807.7 31.3 %collective-permute-start.48 = (bf16[128,1536]{1,0:T(8,128)(2,1)S(1)}, bf16[128,1536]{1,0:T(8,128)(2,1)S(1)}, u32[]{:S(2)}, u32[]{:S(2)}) collective-permute-start(bf16[128,1536]{1,0:T(8,128)(2,1)S(1)} %constant_dynamic-slice_fusion.19), channel_id=1, source_target_pairs={{0,8},{4,12},{8,0},{12,4},{16,24},{20,28},{24,16},{28,20},{1,9},{5... | collective-permute-start | bytes 1179656 | tf_op jit(solution)/shard_map/ppermute | solution.py:401
  812.3 7.3 collective-permute-start.39
  830.1 8.9 collective-permute-start.42
  839.1 18.0 %collective-permute-start.50 = (bf16[128,1536]{1,0:T(8,128)(2,1)S(1)}, bf16[128,1536]{1,0:T(8,128)(2,1)S(1)}, u32[]{:S(2)}, u32[]{:S(2)}) collective-permute-start(bf16[128,1536]{1,0:T(8,128)(2,1)S(1)} %add_convert_fusion.14), channel_id=1, source_target_pairs={{0,8},{4,12},{8,0},{12,4},{16,24},{20,28},{24,16},{28,20},{1,9},{5... | collective-permute-start | bytes 1179656 | tf_op jit(solution)/shard_map/ppermute | solution.py:401
  840.5 16.6 %collective-permute-start.49 = (bf16[128,1536]{1,0:T(8,128)(2,1)S(1)}, bf16[128,1536]{1,0:T(8,128)(2,1)S(1)}, u32[]{:S(2)}, u32[]{:S(2)}) collective-permute-start(bf16[128,1536]{1,0:T(8,128)(2,1)S(1)} %add_convert_fusion.15), channel_id=1, source_target_pairs={{0,16},{4,20},{8,24},{12,28},{16,0},{20,4},{24,8},{28,12},{1,17},{... | collective-permute-start | bytes 1179656 | tf_op jit(solution)/shard_map/ppermute | solution.py:401
  841.5 26.7 %collective-permute-start.58 = (bf16[352,1024]{1,0:T(8,128)(2,1)}, bf16[352,1024]{1,0:T(8,128)(2,1)}, u32[]{:S(2)}, u32[]{:S(2)}) collective-permute-start(bf16[352,1024]{1,0:T(8,128)(2,1)} %maximum_select_fusion.11), channel_id=1, source_target_pairs={{0,16},{4,20},{8,24},{12,28},{16,0},{20,4},{24,8},{28,12},{1,17},{... | collective-permute-start | bytes 2162696 | tf_op jit(solution)/shard_map/ppermute | solution.py:401
  842.6 25.6 %collective-permute-start.57 = (bf16[352,1024]{1,0:T(8,128)(2,1)S(1)}, bf16[352,1024]{1,0:T(8,128)(2,1)}, u32[]{:S(2)}, u32[]{:S(2)}) collective-permute-start(bf16[352,1024]{1,0:T(8,128)(2,1)S(1)} %copy-done.34), channel_id=1, source_target_pairs={{0,8},{4,12},{8,0},{12,4},{16,24},{20,28},{24,16},{28,20},{1,9},{5... | collective-permute-start | bytes 2162696 | tf_op jit(solution)/shard_map/ppermute | solution.py:401
  857.3 25.9 %collective-permute-start.55 = (bf16[256,1536]{1,0:T(8,128)(2,1)S(1)}, bf16[256,1536]{1,0:T(8,128)(2,1)}, u32[]{:S(2)}, u32[]{:S(2)}) collective-permute-start(bf16[256,1536]{1,0:T(8,128)(2,1)S(1)} %maximum_select_fusion.9), channel_id=1, source_target_pairs={{0,16},{4,20},{8,24},{12,28},{16,0},{20,4},{24,8},{28,12},{1,17},{... | collective-permute-start | bytes 2359304 | tf_op jit(solution)/shard_map/ppermute | solution.py:401
  858.8 26.3 %collective-permute-start.54 = (bf16[256,1536]{1,0:T(8,128)(2,1)S(1)}, bf16[256,1536]{1,0:T(8,128)(2,1)S(1)}, u32[]{:S(2)}, u32[]{:S(2)}) collective-permute-start(bf16[256,1536]{1,0:T(8,128)(2,1)S(1)} %maximum_select_fusion.8), channel_id=1, source_target_pairs={{0,8},{4,12},{8,0},{12,4},{16,24},{20,28},{24,16},{28,20},{1,9},{5... | collective-permute-start | bytes 2359304 | tf_op jit(solution)/shard_map/ppermute | solution.py:401
  887.5 77.2 %collective-permute-start.56 = (bf16[1024,1536]{1,0:T(8,128)(2,1)}, bf16[1024,1536]{1,0:T(8,128)(2,1)}, u32[]{:S(2)}, u32[]{:S(2)}) collective-permute-start(bf16[1024,1536]{1,0:T(8,128)(2,1)} %pad_maximum_fusion.1.half_ref), channel_id=1, source_target_pairs={{0,4},{4,0},{8,12},{12,8},{16,20},{20,16},{24,28},{28,24},{1,5},{5... | collective-permute-start | bytes 9437192 | tf_op jit(solution)/shard_map/ppermute | solution.py:401
  887.8 17.1 %collective-permute-start.59 = (bf16[1408,1024]{1,0:T(8,128)(2,1)S(1)}, bf16[1408,1024]{1,0:T(8,128)(2,1)}, u32[]{:S(2)}, u32[]{:S(2)}) collective-permute-start(bf16[1408,1024]{1,0:T(8,128)(2,1)S(1)} %pad_maximum_fusion.2.half_ref), channel_id=1, source_target_pairs={{0,4},{4,0},{8,12},{12,8},{16,20},{20,16},{24,28},{28,24},{1,5},{5... | collective-permute-start | bytes 8650760 | tf_op jit(solution)/shard_map/ppermute | solution.py:401
  (83 other events, 1359.7 us)
Sparse Core Ops, SparseCore 0:
  12.2 83.4 all-gather.7
  97.3 86.9 all-gather.9
  209.4 52.5 all-gather.17
  294.3 82.9 all-gather.11
  454.1 75.2 reduce-scatter.3
  570.3 80.3 all-gather.13
  652.4 80.7 all-gather.15
  736.2 75.2 reduce-scatter.5
  814.4 80.0 reduce-scatter.7
  899.1 61.2 all-reduce.2

commit v10 on v9

--- a/solution.py
+++ b/solution.py
@@ -621,11 +621,10 @@
 
 
 def sum_over_all(x):
-    for axis in ("ctx", "tp"):
-        n = lax.axis_size(axis)
-        for bit in range(int(math.log2(n))):
-            x = x + lax.ppermute(x, axis, [(i, i ^ (1 << bit)) for i in range(n)])
-            yield x
+    steps = [(axis, bit) for axis in ("ctx", "tp") for bit in range(int(math.log2(lax.axis_size(axis))))]
+    for axis, bit in sorted(steps, key=lambda step: step[0] == "ctx" and step[1] > 0):
+        x = x + lax.ppermute(x, axis, [(i, i ^ (1 << bit)) for i in range(lax.axis_size(axis))])
+        yield x
     while True:
         yield x
 
@@ -691,7 +690,6 @@
     go(gu)
     go(dw, held)
     grad_two = after(grad_two, held)
-    out_sum = sum_rows(after(down, grad_two))
 
     norm_two, grad_gain_two, grad_shift_two = layer_back(grad_two.astype(F32), unit_two, inverse_two, gain_two)
     grad_mixed = cotangent.astype(F32) + norm_two
@@ -724,19 +722,16 @@
     part_one = q_part + nt(grad_k, key_w) + nt(grad_v, value_w)
     part_sent = after(part_one.astype(BF16), branch)
     grad_one = sum_rows(part_sent)
-    mixed_late, out_sum = after((mixed, out_sum), part_sent)
-    out_tokens = (mixed_late + out_sum.astype(F32)).astype(BF16)
+    out_tokens = (mixed + sum_rows(after(down, grad_one)).astype(F32)).astype(BF16)
 
     rows_one, branch, grad_q, grad_k, grad_v = after((rows_one, branch, grad_q, grad_k, grad_v), part_sent)
     grad_qkv = jnp.concatenate([grad_q, grad_k, grad_v], axis=1)
-    chain = begin(lambda core: rc(columns(rows_one, core), grad_qkv))
+    chain = begin(lambda core: jnp.concatenate([rc(columns(rows_one, core), grad_qkv), rc(columns(branch, core), attn_rows)], axis=1))
     take(gu, part_sent)
     take_extra(gu)
     go(gu)
     held = take(chain)
     go(chain)
-    grad_output_w = rc(attn_rows, after(branch, held)).astype(BF16)
-    grad_output_w = lax.psum(after(grad_output_w, grad_one), "ctx")
     unit_rows = (rows_one.astype(F32) - shift_one) / gain_one
     bias_grad = jnp.sum(grad_qkv.astype(F32), axis=0)
     tp_row = (jnp.arange(n_tp) == lax.axis_index("tp"))[:, None]
@@ -744,30 +739,31 @@
         jnp.sum(part_one * unit_rows, axis=0), jnp.sum(part_one, axis=0), grad_gain_two, grad_shift_two,
         jnp.where(tp_row, bias_grad[None, :], 0.0).reshape(-1)])
     sums = sum_over_all(after(small, held).reshape(-1, 1024))
-    for _ in range(9):
-        small = next(sums)
+    small = [next(sums) for _ in range(1 + int(math.log2(n_tp)))]
     made = take(dw, held)
     take_extra(dw)
     go(dw)
-    held = take(chain, made)
+    held = take(chain, (made, small))
     go(chain)
+    small = next(sums)
+    take(dw, held)
+    go(dw)
     held = take(chain, small)
     go(chain)
     grad_gate_w, grad_up_w = unpack_rows(*take(gu, held), 2)
-    held = take(chain, grad_gate_w)
+    for _ in range(4):
+        small = next(sums)
+    held = take(chain, (grad_gate_w, small))
     go(chain)
-    take(dw, held)
-    go(dw)
-    take(chain)
+    grad_down_w = unpack_cols(*take(dw, held))
+    take(chain, grad_down_w)
     take_extra(chain)
     go(chain)
-    grad_down_w = unpack_cols(*take(dw))
     depth = x.shape[1]
     small = small.reshape(-1)
     norms = small[:4 * depth].reshape(4, depth)
     bias_sum = jnp.sum(jnp.where(tp_row, small[4 * depth:].reshape(n_tp, -1), 0.0), axis=0)
-    grad_query_w, grad_key_w, grad_value_w = unpack_rows(*take(chain), 3)
-    grad_output_w = grad_output_w.astype(F32)
+    grad_query_w, grad_key_w, grad_value_w, grad_output_w = unpack_rows(*take(chain), 4, True)
     norm_one, _, _ = layer_back(grad_one.astype(F32), unit_one, inverse_one, gain_one)
     grad_tokens = (grad_mixed + norm_one).astype(BF16)
     return (

time: 995 us -> 949 us (0.954)
  waiting for transfers between devices: 417 us -> 384 us
    psum x1 -> x0, waiting for transfers between devices: 46.7 us -> none  [local(): grad_output_w = lax.psum(after(grad_output_w, grad_one), 'ctx')]
    ppermute x46, waiting for transfers between devices: 171 us -> 192 us  [ctx_swap(): return lax.ppermute(x, 'ctx', [(i, i ^ mask) for i in range(n)])]
    dot_general x7 -> x8, matrix products: 58 us -> 56.7 us  [rc(): lax.dot_general(left, right, (((0,), (0,)), ((), ())), preferred_element_...]
  transfers between devices with their start and end apart: 70 -> 69, of which waited for: 30 -> 31; matrix products, arithmetic and copies ran while one was open for 20% -> 19% of each run, Pallas kernels for 20% -> 22%
where the time goes in v10:
time: 949 us; the launch traced here: 943 us
  waiting for transfers between devices  384 us (40%)
  Pallas kernels  235 us (25%)
  matrix products  118 us (12%)
  other arithmetic  83 us (9%)
  starting transfers between devices  71.8 us (8%)
  local copies, waits for them, and re-layouts  36.3 us (4%)
  between operations  15.7 us (2%)
    ppermute x46, waiting for transfers between devices, ctx_swap(): return lax.ppermute(x, 'ctx', [(i, i ^ mask) for i in range(n)])  192 us
    pallas_call x4, Pallas kernels, attention_call(): pl.pallas_call(kernel, grid_spec=pltpu.PrefetchScalarGridSpec(num_scalar_...  163 us
    all_gather x4, waiting for transfers between devices, all_rows(): return lax.all_gather(x, 'tp', axis=0, tiled=True)  104 us
    dot_general x8, matrix products, rc(): lax.dot_general(left, right, (((0,), (0,)), ((), ())), preferred_element_...  56.7 us
    ppermute x46, starting transfers between devices, ctx_swap(): return lax.ppermute(x, 'ctx', [(i, i ^ mask) for i in range(n)])  51.5 us
    dot_general x6, matrix products, nt(): lax.dot_general(a, b, (((1,), (1,)), ((), ())), preferred_element_type=jn...  45.8 us
    ppermute x6, waiting for transfers between devices, tp_shift(): return lax.ppermute(x, 'tp', [(i, (i + d) % n) for i in range(n)])  32.8 us
    ppermute x3, waiting for transfers between devices, gather_tp(): lax.ppermute(x, 'tp', [(i, (i + d) % n) for i in range(n)])  29.1 us
  transfers between devices with their start and end apart: 69, of which 31 were waited for; matrix products, arithmetic and copies ran while one was open for 19% of the time, Pallas kernels for 22%

profile of v10, /device:TPU:0, one launch (start us, length us, event | category | flops | bytes accessed | tf_op | source)
XLA Modules:
  0.0 943.3 jit_solution(16806469241641461229)
XLA Ops:
  12.2 83.6 %all-gather.8.cloned.1.call-done.h_ref = bf16[1024,2048]{1,0:T(8,128)(2,1)} async-done(((bf16[256,2048]{1,0:T(8,128)(2,1)}), bf16[1024,2048]{1,0:T(8,128)(2,1)}) %all-gather.8.cloned.1.call-update) | async-done | bytes 4194320 | tf_op jit(solution)/shard_map/all_gather | solution.py:553
  98.6 11.8 %project.1 = (bf16[4,256,512]{2,1,0:T(8,128)(2,1)S(1)}, bf16[2,4,256,512]{3,2,1,0:T(8,128)(2,1)}) custom-call(bf16[1024,2048]{1,0:T(8,128)(2,1)} %all-gather.8.cloned.1.call-done.h_ref, bf16[2048,512]{1,0:T(8,128)(2,1)} %wq_ref.1, bf16[2048,512]{1,0:T(8,128)(2,1)} %wk_ref.1, bf16[2048,512]{1,0:T(8,128)(2,1)} %wv_ref.1, ...), custom_call_target="tpu_custom_call" | custom-call | flops 6442450944 | bytes 6291456 | tf_op jit(solution)/shard_map/project/pallas_call | solution.py:345
  114.4 44.7 %collective-permute-done.3.refs_4_.refs_12_ = bf16[2,4,2,128,512]{4,3,2,1,0:T(8,128)(2,1)} collective-permute-done((bf16[2,4,2,128,512]{4,3,2,1,0:T(8,128)(2,1)}, bf16[2,4,2,128,512]{4,3,2,1,0:T(8,128)(2,1)}, u32[]{:S(2)}, u32[]{:S(2)}) %collective-permute-start.3) | collective-permute-done | bytes 2097184 | tf_op jit(solution)/shard_map/ppermute | solution.py:401
  169.6 9.3 collective-permute-done.14
  178.9 19.8 %collective-permute-done.13 = bf16[64,2048]{1,0:T(8,128)(2,1)S(1)} collective-permute-done((bf16[64,2048]{1,0:T(8,128)(2,1)S(1)}, bf16[64,2048]{1,0:T(8,128)(2,1)S(1)}, u32[]{:S(2)}, u32[]{:S(2)}) %collective-permute-start.13) | collective-permute-done | bytes 262176 | tf_op jit(solution)/shard_map/ppermute | solution.py:636
  200.1 7.6 collective-permute-done.8.refs_15_
  210.6 46.8 %attend.1 = (bf16[4,256,512]{2,1,0:T(8,128)(2,1)}, bf16[4,256,128]{2,1,0:T(8,128)(2,1)}) custom-call(s32[4,16]{1,0:T(4,128)} %copy.52.place_ref, s32[4,2]{1,0:T(4,128)} %get-tuple-element.215.own_ref, bf16[4,256,512]{2,1,0:T(8,128)(2,1)} %copy-done.5, bf16[2,4,2,128,512]{4,3,2,1,0:T(8,128)(2,1)} %bitcast.5.refs_0_.refs_8_, ...), custom_call_target="tpu_custom_call" | custom-call | flops 8589934592 | bytes 16777216 | tf_op jit(solution)/shard_map/attend/pallas_call | solution.py:221
  259.5 3.8 collective-permute-start.11
  263.4 4.8 collective-permute-done.9
  268.2 11.5 %collective-permute-done.10 = bf16[256,512]{1,0:T(8,128)(2,1)S(1)} collective-permute-done((bf16[256,512]{1,0:T(8,128)(2,1)S(1)}, bf16[256,512]{1,0:T(8,128)(2,1)S(1)}, u32[]{:S(2)}, u32[]{:S(2)}) %collective-permute-start.10) | collective-permute-done | bytes 262176 | tf_op jit(solution)/shard_map/ppermute | solution.py:558
  280.7 6.1 fusion.84
  290.1 8.6 collective-permute-start.20
  299.4 29.0 %collective-permute-done.20.refs_6_.refs_14_ = bf16[1,4,2,128,640]{4,3,2,1,0:T(8,128)(2,1)S(1)} collective-permute-done((bf16[1,4,2,128,640]{4,3,2,1,0:T(8,128)(2,1)S(1)}, bf16[1,4,2,128,640]{4,3,2,1,0:T(8,128)(2,1)S(1)}, u32[]{:S(2)}, u32[]{:S(2)}) %collective-permute-start.20) | collective-permute-done | bytes 1310752 | tf_op jit(solution)/shard_map/ppermute | solution.py:401
  328.4 23.9 %collective-permute-done.18.refs_4_.refs_12_ = bf16[1,4,2,128,640]{4,3,2,1,0:T(8,128)(2,1)} collective-permute-done((bf16[1,4,2,128,640]{4,3,2,1,0:T(8,128)(2,1)S(1)}, bf16[1,4,2,128,640]{4,3,2,1,0:T(8,128)(2,1)}, u32[]{:S(2)}, u32[]{:S(2)}) %collective-permute-start.18) | collective-permute-done | bytes 1310752 | tf_op jit(solution)/shard_map/ppermute | solution.py:401
  352.8 2.9 collective-permute-done.19.refs_5_.refs_13_
  357.6 20.5 %all-gather.12.cloned.1.call-done.h_ref = bf16[1024,2048]{1,0:T(8,128)(2,1)} async-done(((bf16[256,2048]{1,0:T(8,128)(2,1)}), bf16[1024,2048]{1,0:T(8,128)(2,1)}) %all-gather.12.cloned.1.call-update) | async-done | bytes 4194320 | tf_op jit(solution)/shard_map/all_gather | solution.py:553
  378.1 28.4 %mlp.1 = (bf16[1024,1408]{1,0:T(8,128)(2,1)}, bf16[1024,2816]{1,0:T(8,128)(2,1)}) custom-call(bf16[1024,2048]{1,0:T(8,128)(2,1)} %all-gather.12.cloned.1.call-done.h_ref, bf16[1024,2048]{1,0:T(8,128)(2,1)} %all-gather.10.cloned.1.call-done.dy_ref, bf16[2048,1408]{1,0:T(8,128)(2,1)} %gate_ref.1, bf16[2048,1408]{1,0:T(8,128)(2,1)} %up_ref.1, ...), custom_call_target="tpu_custom_call" | custom-call | flops 17716740096 | bytes 38273024 | tf_op jit(solution)/shard_map/mlp/pallas_call | solution.py:385
  406.6 9.8 %fusion.5 = f32[1024,2048]{1,0:T(8,128)S(1)} fusion(bf16[2048,1408]{1,0:T(8,128)(2,1)} %gate_ref.1, bf16[1024,2816]{1,0:T(8,128)(2,1)} %get-tuple-element.124), kind=kOutput, calls=%fused_computation.30 | convolution fusion | flops 5905580032 | bytes 17039360 | tf_op jit(solution)/shard_map/dot_general | solution.py:15
  416.3 11.1 %add_convert_fusion.1 = bf16[1024,2048]{1,0:T(8,128)(2,1)} fusion(f32[1024,2048]{1,0:T(8,128)S(1)} %fusion.5, bf16[2048,1408]{1,0:T(8,128)(2,1)} %up_ref.1, bf16[1024,2816]{1,0:T(8,128)(2,1)S(1)} %copy-done.76), kind=kOutput, calls=%fused_computation.5 | convolution fusion | flops 5909774336 | bytes 21233664 | tf_op jit(solution)/shard_map/dot_general | solution.py:15
  427.4 11.1 %convolution_convert_fusion = bf16[1024,2816]{1,0:T(8,128)(2,1)} fusion(bf16[1024,2816]{1,0:T(8,128)(2,1)} %get-tuple-element.124, bf16[1024,2048]{1,0:T(8,128)(2,1)} %all-gather.12.cloned.1.call-done.h_ref, s32[]{:T(128)S(6)} %select_n.384), kind=kOutput, calls=%fused_computation.9 | convolution fusion | flops 5908463616 | bytes 13631492 | tf_op jit(solution)/shard_map/dot_general | solution.py:290
  438.5 16.0 %convolution_convert_fusion.3 = bf16[1408,1024]{1,0:T(8,128)(2,1)} fusion(bf16[1024,1408]{1,0:T(8,128)(2,1)S(1)} %copy-done.77, bf16[1024,2048]{1,0:T(8,128)(2,1)S(1)} %copy-done.69, s32[]{:T(128)S(6)} %select_n.384), kind=kOutput, calls=%fused_computation.14 | convolution fusion | flops 2954231808 | bytes 7864324 | tf_op jit(solution)/shard_map/dot_general | solution.py:290
  456.5 3.6 collective-permute-done.23
  460.2 7.3 add_convert_fusion.2
  469.4 10.5 %add_convert_fusion = bf16[1024,2816]{1,0:T(8,128)(2,1)S(1)} fusion(bf16[1024,2816]{1,0:T(8,128)(2,1)} %collective-permute-done.22, bf16[1024,2816]{1,0:T(8,128)(2,1)} %get-tuple-element.124, bf16[1024,2048]{1,0:T(8,128)(2,1)S(1)} %copy-done.70, s32[]{:T(128)S(6)} %select_n.383), kind=kOutput, calls=%fused_computation | convolution fusion | flops 5914230784 | bytes 19398660 | tf_op jit(solution)/shard_map/dot_general | solution.py:290
  486.0 8.2 convolution_convert_fusion.1
  494.2 21.4 %collective-permute-done.24 = bf16[256,2816]{1,0:T(8,128)(2,1)S(1)} collective-permute-done((bf16[256,2816]{1,0:T(8,128)(2,1)}, bf16[256,2816]{1,0:T(8,128)(2,1)S(1)}, u32[]{:S(2)}, u32[]{:S(2)}) %collective-permute-start.24) | collective-permute-done | bytes 1441824 | tf_op jit(solution)/shard_map/ppermute | solution.py:401
  518.1 2.6 add_convert_fusion.4
  528.3 3.6 reduce-scatter.4.cloned.1.call-done
  531.9 3.0 fusion.24
  534.9 3.3 fusion.78
  538.2 6.2 convolution_convert_fusion.4
  554.3 12.2 %collective-permute-done.26 = bf16[256,512]{1,0:T(8,128)(2,1)S(1)} collective-permute-done((bf16[256,512]{1,0:T(8,128)(2,1)S(1)}, bf16[256,512]{1,0:T(8,128)(2,1)S(1)}, u32[]{:S(2)}, u32[]{:S(2)}) %collective-permute-start.26) | collective-permute-done | bytes 262176 | tf_op jit(solution)/shard_map/ppermute | solution.py:558
  566.6 4.3 collective-permute-done.27
  580.1 46.8 %query_grad.1 = bf16[4,256,512]{2,1,0:T(8,128)(2,1)} custom-call(s32[4,16]{1,0:T(4,128)} %copy.52.place_ref, s32[4,2]{1,0:T(4,128)} %get-tuple-element.215.own_ref, bf16[4,256,512]{2,1,0:T(8,128)(2,1)} %copy-done.5, bf16[4,256,512]{2,1,0:T(8,128)(2,1)} %bitcast.84, bf16[4,256,128]{2,1,0:T(8,128)(2,1)} %get-tuple-element.117.qx_ref, ...), custom_call_target="tpu_custom_call" | custom-call | flops 12884901888 | bytes 16777216 | tf_op jit(solution)/shard_map/query_grad/pallas_call | solution.py:221
  627.0 7.7 fusion.86
  638.3 3.3 maximum_select_fusion.4
  641.6 3.3 maximum_select_fusion.5
  644.9 9.3 all-gather.14.cloned.1.call-done.refs_16_.refs_17_
  655.3 6.9 collective-permute-start.36
  662.4 32.3 %key_value_grad.2 = (bf16[2,256,512]{2,1,0:T(8,128)(2,1)}, bf16[2,256,512]{2,1,0:T(8,128)(2,1)}) custom-call(s32[4,16]{1,0:T(4,128)} %copy.52.place_ref, s32[4,2]{1,0:T(4,128)} %get-tuple-element.215.own_ref, s32[4,16]{1,0:T(4,128)} %slots_ref.3, bf16[2,4,256,512]{3,2,1,0:T(8,128)(2,1)} %get-tuple-element.111.k_ref.v_ref, ...), custom_call_target="tpu_custom_call" | custom-call | flops 8589934592 | bytes 8388608 | tf_op jit(solution)/shard_map/key_value_grad/pallas_call | solution.py:221
  695.7 37.5 %key_value_grad.3 = (bf16[2,256,512]{2,1,0:T(8,128)(2,1)}, bf16[2,256,512]{2,1,0:T(8,128)(2,1)}) custom-call(s32[4,16]{1,0:T(4,128)} %copy.52.place_ref, s32[4,2]{1,0:T(4,128)} %get-tuple-element.215.own_ref, s32[4,16]{1,0:T(4,128)} %slots_ref.3, bf16[2,4,256,512]{3,2,1,0:T(8,128)(2,1)} %get-tuple-element.111.k_ref.v_ref, ...), custom_call_target="tpu_custom_call" | custom-call | flops 8589934592 | bytes 8388608 | tf_op jit(solution)/shard_map/key_value_grad/pallas_call | solution.py:221
  737.9 8.7 fusion.85
  746.9 3.2 fusion.47
  754.0 3.7 convolution_convert_fusion.2
  757.7 2.7 pad_maximum_fusion.1
  760.4 3.2 maximum_select_fusion
  763.6 4.3 maximum_select_fusion.1
  767.8 4.8 pad_maximum_fusion.half_ref
  773.1 3.7 fusion.77
  780.5 3.5 fusion.30
  784.0 3.2 fusion
  795.1 26.7 %collective-permute-done.46 = bf16[176,1024]{1,0:T(8,128)(2,1)S(1)} collective-permute-done((bf16[176,1024]{1,0:T(8,128)(2,1)S(1)}, bf16[176,1024]{1,0:T(8,128)(2,1)S(1)}, u32[]{:S(2)}, u32[]{:S(2)}) %collective-permute-start.46) | collective-permute-done | bytes 360480 | tf_op jit(solution)/shard_map/ppermute | solution.py:401
  826.1 2.9 collective-permute-start.40
  833.9 2.9 collective-permute-done.41
  843.8 4.6 collective-permute-done.57
  848.4 4.6 collective-permute-done.56
  856.6 7.2 collective-permute-done.48
  870.7 7.9 collective-permute-done.42
  878.6 13.4 %unpack_rows.2 = (f32[2048,1408]{1,0:T(8,128)}, f32[2048,1408]{1,0:T(8,128)}) custom-call(s32[1]{0:T(128)} %bitcast.19.core_ref, bf16[1024,2816]{1,0:T(8,128)(2,1)} %pad_maximum_fusion.half_ref, bf16[1024,2816]{1,0:T(8,128)(2,1)} %collective-permute-done.53.other_ref), custom_call_target="tpu_custom_call" | custom-call | bytes 34603008 | tf_op jit(solution)/shard_map/unpack_rows/pallas_call | solution.py:512
  895.1 6.2 unpack_cols.1
  901.3 7.2 collective-permute-done.55
  918.7 3.4 fusion.18
  922.1 11.4 %unpack_rows.3 = (f32[2048,512]{1,0:T(8,128)}, f32[2048,512]{1,0:T(8,128)}, f32[2048,512]{1,0:T(8,128)}, f32[512,2048]{1,0:T(8,128)}) custom-call(s32[1]{0:T(128)} %bitcast.19.core_ref, bf16[1024,2048]{1,0:T(8,128)(2,1)} %pad_maximum_fusion.2.half_ref, bf16[1024,2048]{1,0:T(8,128)(2,1)} %collective-permute-done.59.other_ref), custom_call_target="tpu_custom_call" | custom-call | bytes 25165824 | tf_op jit(solution)/shard_map/unpack_rows/pallas_call | solution.py:512
  933.4 3.1 add_convert_fusion.7
  (412 shorter events, 140.5 us)
Async XLA Ops:
  7.2 88.5 %all-gather.8.cloned.1.call-start = ((), (), s32[]{:S(2)}) async-start(), calls=%async_computation.3 | async-start | bytes 5242880 | tf_op jit(solution)/shard_map/all_gather | solution.py:553
  12.1 197.1 %all-gather.10.cloned.1.call-start = ((), (), s32[]{:S(2)}) async-start(), calls=%async_computation.4 | async-start | bytes 5242880 | tf_op jit(solution)/shard_map/all_gather | solution.py:553
  95.7 184.0 %all-gather.18.cloned.1.call-start = ((), (), s32[]{:S(2)}) async-start(), calls=%async_computation.11 | async-start | bytes 9437184 | tf_op jit(solution)/shard_map/all_gather | solution.py:667
  111.5 47.7 %collective-permute-start.3 = (bf16[2,4,2,128,512]{4,3,2,1,0:T(8,128)(2,1)}, bf16[2,4,2,128,512]{4,3,2,1,0:T(8,128)(2,1)}, u32[]{:S(2)}, u32[]{:S(2)}) collective-permute-start(bf16[2,4,2,128,512]{4,3,2,1,0:T(8,128)(2,1)} %bitcast.5.refs_0_.refs_8_), channel_id=1, source_target_pairs={{0,16},{4,20},{8,24},{12,28},{16,0},{20,4},{24,8},{28,12},{1,17},{... | collective-permute-start | bytes 6291464 | tf_op jit(solution)/shard_map/ppermute | solution.py:401
  112.9 49.9 %collective-permute-start.1 = (bf16[2,4,2,128,512]{4,3,2,1,0:T(8,128)(2,1)}, bf16[2,4,2,128,512]{4,3,2,1,0:T(8,128)(2,1)}, u32[]{:S(2)}, u32[]{:S(2)}) collective-permute-start(bf16[2,4,2,128,512]{4,3,2,1,0:T(8,128)(2,1)} %bitcast.5.refs_0_.refs_8_), channel_id=1, source_target_pairs={{0,8},{4,12},{8,0},{12,4},{16,24},{20,28},{24,16},{28,20},{1,9},{5... | collective-permute-start | bytes 6291464 | tf_op jit(solution)/shard_map/ppermute | solution.py:401
  161.4 38.0 %collective-permute-start.7 = (bf16[1,4,2,128,512]{4,3,2,1,0:T(8,128)(2,1)}, bf16[1,4,2,128,512]{4,3,2,1,0:T(8,128)(2,1)}, u32[]{:S(2)}, u32[]{:S(2)}) collective-permute-start(bf16[1,4,2,128,512]{4,3,2,1,0:T(8,128)(2,1)} %slice.96), channel_id=1, source_target_pairs={{0,8},{4,12},{8,0},{12,4},{16,24},{20,28},{24,16},{28,20},{1,9},{5... | collective-permute-start | bytes 3145736 | tf_op jit(solution)/shard_map/ppermute | solution.py:401
  165.1 34.3 %collective-permute-start.5 = (bf16[1,4,2,128,512]{4,3,2,1,0:T(8,128)(2,1)}, bf16[1,4,2,128,512]{4,3,2,1,0:T(8,128)(2,1)}, u32[]{:S(2)}, u32[]{:S(2)}) collective-permute-start(bf16[1,4,2,128,512]{4,3,2,1,0:T(8,128)(2,1)} %slice.95), channel_id=1, source_target_pairs={{0,16},{4,20},{8,24},{12,28},{16,0},{20,4},{24,8},{28,12},{1,17},{... | collective-permute-start | bytes 3145736 | tf_op jit(solution)/shard_map/ppermute | solution.py:401
  166.6 12.3 %collective-permute-start.14 = (bf16[64,2048]{1,0:T(8,128)(2,1)S(1)}, bf16[64,2048]{1,0:T(8,128)(2,1)S(1)}, u32[]{:S(2)}, u32[]{:S(2)}) collective-permute-start(bf16[64,2048]{1,0:T(8,128)(2,1)S(1)} %constant_dynamic-slice_fusion.14), channel_id=1, source_target_pairs={{0,3},{1,0},{2,1},{3,2},{4,7},{5,4},{6,5},{7,6},{8,11},{9,8},{10,9... | collective-permute-start | bytes 786440 | tf_op jit(solution)/shard_map/ppermute | solution.py:636
  167.7 31.0 %collective-permute-start.13 = (bf16[64,2048]{1,0:T(8,128)(2,1)S(1)}, bf16[64,2048]{1,0:T(8,128)(2,1)S(1)}, u32[]{:S(2)}, u32[]{:S(2)}) collective-permute-start(bf16[64,2048]{1,0:T(8,128)(2,1)S(1)} %constant_dynamic-slice_fusion.14), channel_id=1, source_target_pairs={{0,2},{1,3},{2,0},{3,1},{4,6},{5,7},{6,4},{7,5},{8,10},{9,11},{10,... | collective-permute-start | bytes 786440 | tf_op jit(solution)/shard_map/ppermute | solution.py:636
  167.7 31.0 %collective-permute-start.12 = (bf16[64,2048]{1,0:T(8,128)(2,1)S(1)}, bf16[64,2048]{1,0:T(8,128)(2,1)S(1)}, u32[]{:S(2)}, u32[]{:S(2)}) collective-permute-start(bf16[64,2048]{1,0:T(8,128)(2,1)S(1)} %constant_dynamic-slice_fusion.14), channel_id=1, source_target_pairs={{0,1},{1,2},{2,3},{3,0},{4,5},{5,6},{6,7},{7,4},{8,9},{9,10},{10,1... | collective-permute-start | bytes 786440 | tf_op jit(solution)/shard_map/ppermute | solution.py:636
  178.9 21.1 %collective-permute-start = (bf16[2,4,2,128,512]{4,3,2,1,0:T(8,128)(2,1)}, bf16[2,4,2,128,512]{4,3,2,1,0:T(8,128)(2,1)}, u32[]{:S(2)}, u32[]{:S(2)}) collective-permute-start(bf16[2,4,2,128,512]{4,3,2,1,0:T(8,128)(2,1)} %bitcast.5.refs_0_.refs_8_), channel_id=1, source_target_pairs={{0,4},{4,0},{8,12},{12,8},{16,20},{20,16},{24,28},{28,24},{1,5},{5... | collective-permute-start | bytes 6291464 | tf_op jit(solution)/shard_map/ppermute | solution.py:401
  198.7 10.5 %collective-permute-start.4 = (bf16[2,4,2,128,512]{4,3,2,1,0:T(8,128)(2,1)}, bf16[2,4,2,128,512]{4,3,2,1,0:T(8,128)(2,1)}, u32[]{:S(2)}, u32[]{:S(2)}) collective-permute-start(bf16[2,4,2,128,512]{4,3,2,1,0:T(8,128)(2,1)} %collective-permute-done.3.refs_4_.refs_12_), channel_id=1, source_target_pairs={{0,4},{4,0},{8,12},{12,8},{16,20},{20,16},{24,28},{28,24},{1,5},{5... | collective-permute-start | bytes 6291464 | tf_op jit(solution)/shard_map/ppermute | solution.py:401
  198.7 10.5 %collective-permute-start.2 = (bf16[2,4,2,128,512]{4,3,2,1,0:T(8,128)(2,1)}, bf16[2,4,2,128,512]{4,3,2,1,0:T(8,128)(2,1)}, u32[]{:S(2)}, u32[]{:S(2)}) collective-permute-start(bf16[2,4,2,128,512]{4,3,2,1,0:T(8,128)(2,1)} %collective-permute-done.1.refs_2_.refs_10_), channel_id=1, source_target_pairs={{0,4},{4,0},{8,12},{12,8},{16,20},{20,16},{24,28},{28,24},{1,5},{5... | collective-permute-start | bytes 6291464 | tf_op jit(solution)/shard_map/ppermute | solution.py:401
  199.4 8.3 collective-permute-start.8
  199.5 9.7 %collective-permute-start.6 = (bf16[1,4,2,128,512]{4,3,2,1,0:T(8,128)(2,1)}, bf16[1,4,2,128,512]{4,3,2,1,0:T(8,128)(2,1)}, u32[]{:S(2)}, u32[]{:S(2)}) collective-permute-start(bf16[1,4,2,128,512]{4,3,2,1,0:T(8,128)(2,1)} %collective-permute-done.5.refs_6_), channel_id=1, source_target_pairs={{0,4},{4,0},{8,12},{12,8},{16,20},{20,16},{24,28},{28,24},{1,5},{5... | collective-permute-start | bytes 3145736 | tf_op jit(solution)/shard_map/ppermute | solution.py:401
  209.3 168.9 %all-gather.12.cloned.1.call-start = ((), (), s32[]{:S(2)}) async-start(), calls=%async_computation.5 | async-start | bytes 5242880 | tf_op jit(solution)/shard_map/all_gather | solution.py:553
  259.5 8.6 collective-permute-start.9
  259.5 20.1 %collective-permute-start.10 = (bf16[256,512]{1,0:T(8,128)(2,1)S(1)}, bf16[256,512]{1,0:T(8,128)(2,1)S(1)}, u32[]{:S(2)}, u32[]{:S(2)}) collective-permute-start(bf16[256,512]{1,0:T(8,128)(2,1)S(1)} %get-tuple-element.227), channel_id=1, source_target_pairs={{0,2},{1,3},{2,0},{3,1},{4,6},{5,7},{6,4},{7,5},{8,10},{9,11},{10,... | collective-permute-start | bytes 786440 | tf_op jit(solution)/shard_map/ppermute | solution.py:558
  259.5 20.2 %collective-permute-start.11 = (bf16[256,512]{1,0:T(8,128)(2,1)S(1)}, bf16[256,512]{1,0:T(8,128)(2,1)S(1)}, u32[]{:S(2)}, u32[]{:S(2)}) collective-permute-start(bf16[256,512]{1,0:T(8,128)(2,1)S(1)} %get-tuple-element.226), channel_id=1, source_target_pairs={{0,3},{1,0},{2,1},{3,2},{4,7},{5,4},{6,5},{7,6},{8,11},{9,8},{10,9... | collective-permute-start | bytes 786440 | tf_op jit(solution)/shard_map/ppermute | solution.py:558
  289.7 242.2 %reduce-scatter.4.cloned.1.call-start = ((), (), s32[]{:S(2)}) async-start(), calls=%async_computation.6 | async-start | bytes 5242880 | tf_op jit(solution)/shard_map/reduce_scatter | solution.py:581
  290.1 38.3 %collective-permute-start.20 = (bf16[1,4,2,128,640]{4,3,2,1,0:T(8,128)(2,1)S(1)}, bf16[1,4,2,128,640]{4,3,2,1,0:T(8,128)(2,1)S(1)}, u32[]{:S(2)}, u32[]{:S(2)}) collective-permute-start(bf16[1,4,2,128,640]{4,3,2,1,0:T(8,128)(2,1)S(1)} %bitcast.69), channel_id=1, source_target_pairs={{0,24},{4,28},{8,16},{12,20},{16,8},{20,12},{24,0},{28,4},{1,25},{... | collective-permute-start | bytes 3932168 | tf_op jit(solution)/shard_map/ppermute | solution.py:401
  298.7 53.6 %collective-permute-start.18 = (bf16[1,4,2,128,640]{4,3,2,1,0:T(8,128)(2,1)S(1)}, bf16[1,4,2,128,640]{4,3,2,1,0:T(8,128)(2,1)}, u32[]{:S(2)}, u32[]{:S(2)}) collective-permute-start(bf16[1,4,2,128,640]{4,3,2,1,0:T(8,128)(2,1)S(1)} %bitcast.70), channel_id=1, source_target_pairs={{0,16},{4,20},{8,24},{12,28},{16,0},{20,4},{24,8},{28,12},{1,17},{... | collective-permute-start | bytes 3932168 | tf_op jit(solution)/shard_map/ppermute | solution.py:401
  298.7 53.6 %collective-permute-start.16 = (bf16[1,4,2,128,640]{4,3,2,1,0:T(8,128)(2,1)S(1)}, bf16[1,4,2,128,640]{4,3,2,1,0:T(8,128)(2,1)}, u32[]{:S(2)}, u32[]{:S(2)}) collective-permute-start(bf16[1,4,2,128,640]{4,3,2,1,0:T(8,128)(2,1)S(1)} %bitcast.71), channel_id=1, source_target_pairs={{0,8},{4,12},{8,0},{12,4},{16,24},{20,28},{24,16},{28,20},{1,9},{5... | collective-permute-start | bytes 3932168 | tf_op jit(solution)/shard_map/ppermute | solution.py:401
  299.4 53.5 %collective-permute-start.15 = (bf16[1,4,2,128,640]{4,3,2,1,0:T(8,128)(2,1)S(1)}, bf16[1,4,2,128,640]{4,3,2,1,0:T(8,128)(2,1)}, u32[]{:S(2)}, u32[]{:S(2)}) collective-permute-start(bf16[1,4,2,128,640]{4,3,2,1,0:T(8,128)(2,1)S(1)} %bitcast.72), channel_id=1, source_target_pairs={{0,4},{4,0},{8,12},{12,8},{16,20},{20,16},{24,28},{28,24},{1,5},{5... | collective-permute-start | bytes 3932168 | tf_op jit(solution)/shard_map/ppermute | solution.py:401
  328.4 24.4 %collective-permute-start.21 = (bf16[1,4,2,128,640]{4,3,2,1,0:T(8,128)(2,1)S(1)}, bf16[1,4,2,128,640]{4,3,2,1,0:T(8,128)(2,1)}, u32[]{:S(2)}, u32[]{:S(2)}) collective-permute-start(bf16[1,4,2,128,640]{4,3,2,1,0:T(8,128)(2,1)S(1)} %collective-permute-done.20.refs_6_.refs_14_), channel_id=1, source_target_pairs={{0,4},{4,0},{8,12},{12,8},{16,20},{20,16},{24,28},{28,24},{1,5},{5... | collective-permute-start | bytes 3932168 | tf_op jit(solution)/shard_map/ppermute | solution.py:401
  438.5 30.9 %collective-permute-start.22 = (bf16[1024,2816]{1,0:T(8,128)(2,1)}, bf16[1024,2816]{1,0:T(8,128)(2,1)}, u32[]{:S(2)}, u32[]{:S(2)}) collective-permute-start(bf16[1024,2816]{1,0:T(8,128)(2,1)} %convolution_convert_fusion), channel_id=1, source_target_pairs={{0,4},{4,0},{8,12},{12,8},{16,20},{20,16},{24,28},{28,24},{1,5},{5... | collective-permute-start | bytes 17301512 | tf_op jit(solution)/shard_map/ppermute | solution.py:401
  454.5 5.6 collective-permute-start.23
  456.5 197.7 %all-gather.14.cloned.1.call-start = ((), (), s32[]{:S(2)}) async-start(), calls=%async_computation.7 | async-start | bytes 11796480 | tf_op jit(solution)/shard_map/all_gather | solution.py:708
  481.7 33.9 %collective-permute-start.24 = (bf16[256,2816]{1,0:T(8,128)(2,1)}, bf16[256,2816]{1,0:T(8,128)(2,1)S(1)}, u32[]{:S(2)}, u32[]{:S(2)}) collective-permute-start(bf16[256,2816]{1,0:T(8,128)(2,1)} %constant_dynamic-slice_fusion.13), channel_id=1, source_target_pairs={{0,8},{4,12},{8,0},{12,4},{16,24},{20,28},{24,16},{28,20},{1,9},{5... | collective-permute-start | bytes 4325384 | tf_op jit(solution)/shard_map/ppermute | solution.py:401
  484.5 33.6 %collective-permute-start.25 = (bf16[256,2816]{1,0:T(8,128)(2,1)}, bf16[256,2816]{1,0:T(8,128)(2,1)S(1)}, u32[]{:S(2)}, u32[]{:S(2)}) collective-permute-start(bf16[256,2816]{1,0:T(8,128)(2,1)} %constant_dynamic-slice_fusion.12), channel_id=1, source_target_pairs={{0,16},{4,20},{8,24},{12,28},{16,0},{20,4},{24,8},{28,12},{1,17},{... | collective-permute-start | bytes 4325384 | tf_op jit(solution)/shard_map/ppermute | solution.py:401
  521.7 22.7 %collective-permute-start.29 = (bf16[128,2816]{1,0:T(8,128)(2,1)}, bf16[128,2816]{1,0:T(8,128)(2,1)}, u32[]{:S(2)}, u32[]{:S(2)}) collective-permute-start(bf16[128,2816]{1,0:T(8,128)(2,1)} %constant_dynamic-slice_fusion.8), channel_id=1, source_target_pairs={{0,16},{4,20},{8,24},{12,28},{16,0},{20,4},{24,8},{28,12},{1,17},{... | collective-permute-start | bytes 2162696 | tf_op jit(solution)/shard_map/ppermute | solution.py:401
  526.9 17.5 %collective-permute-start.30 = (bf16[128,2816]{1,0:T(8,128)(2,1)}, bf16[128,2816]{1,0:T(8,128)(2,1)}, u32[]{:S(2)}, u32[]{:S(2)}) collective-permute-start(bf16[128,2816]{1,0:T(8,128)(2,1)} %constant_dynamic-slice_fusion.7), channel_id=1, source_target_pairs={{0,8},{4,12},{8,0},{12,4},{16,24},{20,28},{24,16},{28,20},{1,9},{5... | collective-permute-start | bytes 2162696 | tf_op jit(solution)/shard_map/ppermute | solution.py:401
  544.7 26.2 %collective-permute-start.28 = (bf16[256,512]{1,0:T(8,128)(2,1)S(1)}, bf16[256,512]{1,0:T(8,128)(2,1)S(1)}, u32[]{:S(2)}, u32[]{:S(2)}) collective-permute-start(bf16[256,512]{1,0:T(8,128)(2,1)S(1)} %get-tuple-element.222), channel_id=1, source_target_pairs={{0,3},{1,0},{2,1},{3,2},{4,7},{5,4},{6,5},{7,6},{8,11},{9,8},{10,9... | collective-permute-start | bytes 786440 | tf_op jit(solution)/shard_map/ppermute | solution.py:558
  547.3 23.6 %collective-permute-start.27 = (bf16[256,512]{1,0:T(8,128)(2,1)S(1)}, bf16[256,512]{1,0:T(8,128)(2,1)S(1)}, u32[]{:S(2)}, u32[]{:S(2)}) collective-permute-start(bf16[256,512]{1,0:T(8,128)(2,1)S(1)} %get-tuple-element.223), channel_id=1, source_target_pairs={{0,2},{1,3},{2,0},{3,1},{4,6},{5,7},{6,4},{7,5},{8,10},{9,11},{10,... | collective-permute-start | bytes 786440 | tf_op jit(solution)/shard_map/ppermute | solution.py:558
  547.7 18.8 %collective-permute-start.26 = (bf16[256,512]{1,0:T(8,128)(2,1)S(1)}, bf16[256,512]{1,0:T(8,128)(2,1)S(1)}, u32[]{:S(2)}, u32[]{:S(2)}) collective-permute-start(bf16[256,512]{1,0:T(8,128)(2,1)S(1)} %get-tuple-element.224), channel_id=1, source_target_pairs={{0,1},{1,2},{2,3},{3,0},{4,5},{5,6},{6,7},{7,4},{8,9},{9,10},{10,1... | collective-permute-start | bytes 786440 | tf_op jit(solution)/shard_map/ppermute | solution.py:558
  573.6 173.1 %all-gather.16.cloned.1.call-start = ((), (), s32[]{:S(2)}) async-start(), calls=%async_computation.8 | async-start | bytes 5242880 | tf_op jit(solution)/shard_map/all_gather | solution.py:553
  575.2 59.5 %collective-permute-start.34 = (bf16[352,1024]{1,0:T(8,128)(2,1)}, bf16[352,1024]{1,0:T(8,128)(2,1)}, u32[]{:S(2)}, u32[]{:S(2)}) collective-permute-start(bf16[352,1024]{1,0:T(8,128)(2,1)} %constant_dynamic-slice_fusion.5), channel_id=1, source_target_pairs={{0,16},{4,20},{8,24},{12,28},{16,0},{20,4},{24,8},{28,12},{1,17},{... | collective-permute-start | bytes 2162696 | tf_op jit(solution)/shard_map/ppermute | solution.py:401
  577.6 57.1 %collective-permute-start.33 = (bf16[352,1024]{1,0:T(8,128)(2,1)}, bf16[352,1024]{1,0:T(8,128)(2,1)}, u32[]{:S(2)}, u32[]{:S(2)}) collective-permute-start(bf16[352,1024]{1,0:T(8,128)(2,1)} %constant_dynamic-slice_fusion.6), channel_id=1, source_target_pairs={{0,8},{4,12},{8,0},{12,4},{16,24},{20,28},{24,16},{28,20},{1,9},{5... | collective-permute-start | bytes 2162696 | tf_op jit(solution)/shard_map/ppermute | solution.py:401
  579.0 59.3 %collective-permute-start.32 = (bf16[128,2816]{1,0:T(8,128)(2,1)}, bf16[128,2816]{1,0:T(8,128)(2,1)}, u32[]{:S(2)}, u32[]{:S(2)}) collective-permute-start(bf16[128,2816]{1,0:T(8,128)(2,1)} %add_convert_fusion.11), channel_id=1, source_target_pairs={{0,8},{4,12},{8,0},{12,4},{16,24},{20,28},{24,16},{28,20},{1,9},{5... | collective-permute-start | bytes 2162696 | tf_op jit(solution)/shard_map/ppermute | solution.py:401
  579.6 58.7 %collective-permute-start.31 = (bf16[128,2816]{1,0:T(8,128)(2,1)}, bf16[128,2816]{1,0:T(8,128)(2,1)}, u32[]{:S(2)}, u32[]{:S(2)}) collective-permute-start(bf16[128,2816]{1,0:T(8,128)(2,1)} %add_convert_fusion.12), channel_id=1, source_target_pairs={{0,16},{4,20},{8,24},{12,28},{16,0},{20,4},{24,8},{28,12},{1,17},{... | collective-permute-start | bytes 2162696 | tf_op jit(solution)/shard_map/ppermute | solution.py:401
  654.2 202.0 %reduce-scatter.6.cloned.1.call-start = ((), (), s32[]{:S(2)}) async-start(), calls=%async_computation.9 | async-start | bytes 5242880 | tf_op jit(solution)/shard_map/reduce_scatter | solution.py:581
  654.7 40.0 %collective-permute-start.35 = (bf16[176,1024]{1,0:T(8,128)(2,1)S(1)}, bf16[176,1024]{1,0:T(8,128)(2,1)S(1)}, u32[]{:S(2)}, u32[]{:S(2)}) collective-permute-start(bf16[176,1024]{1,0:T(8,128)(2,1)S(1)} %constant_dynamic-slice_fusion.4), channel_id=1, source_target_pairs={{0,16},{4,20},{8,24},{12,28},{16,0},{20,4},{24,8},{28,12},{1,17},{... | collective-permute-start | bytes 1081352 | tf_op jit(solution)/shard_map/ppermute | solution.py:401
  655.3 39.3 %collective-permute-start.36 = (bf16[176,1024]{1,0:T(8,128)(2,1)S(1)}, bf16[176,1024]{1,0:T(8,128)(2,1)S(1)}, u32[]{:S(2)}, u32[]{:S(2)}) collective-permute-start(bf16[176,1024]{1,0:T(8,128)(2,1)S(1)} %constant_dynamic-slice_fusion.3), channel_id=1, source_target_pairs={{0,8},{4,12},{8,0},{12,4},{16,24},{20,28},{24,16},{28,20},{1,9},{5... | collective-permute-start | bytes 1081352 | tf_op jit(solution)/shard_map/ppermute | solution.py:401
  662.2 84.7 %collective-permute-start.52 = (bf16[256,2816]{1,0:T(8,128)(2,1)}, bf16[256,2816]{1,0:T(8,128)(2,1)}, u32[]{:S(2)}, u32[]{:S(2)}) collective-permute-start(bf16[256,2816]{1,0:T(8,128)(2,1)} %maximum_select_fusion.5), channel_id=1, source_target_pairs={{0,16},{4,20},{8,24},{12,28},{16,0},{20,4},{24,8},{28,12},{1,17},{... | collective-permute-start | bytes 4325384 | tf_op jit(solution)/shard_map/ppermute | solution.py:401
  662.2 84.7 %collective-permute-start.51 = (bf16[256,2816]{1,0:T(8,128)(2,1)}, bf16[256,2816]{1,0:T(8,128)(2,1)}, u32[]{:S(2)}, u32[]{:S(2)}) collective-permute-start(bf16[256,2816]{1,0:T(8,128)(2,1)} %maximum_select_fusion.4), channel_id=1, source_target_pairs={{0,8},{4,12},{8,0},{12,4},{16,24},{20,28},{24,16},{28,20},{1,9},{5... | collective-permute-start | bytes 4325384 | tf_op jit(solution)/shard_map/ppermute | solution.py:401
  746.7 186.8 %reduce-scatter.8.cloned.1.call-start = ((), (), s32[]{:S(2)}) async-start(), calls=%async_computation.10 | async-start | bytes 5242880 | tf_op jit(solution)/shard_map/reduce_scatter | solution.py:581
  760.4 23.7 %collective-permute-start.37 = (bf16[1024,2048]{1,0:T(8,128)(2,1)}, bf16[1024,2048]{1,0:T(8,128)(2,1)}, u32[]{:S(2)}, u32[]{:S(2)}) collective-permute-start(bf16[1024,2048]{1,0:T(8,128)(2,1)} %pad_maximum_fusion.1), channel_id=1, source_target_pairs={{0,4},{4,0},{8,12},{12,8},{16,20},{20,16},{24,28},{28,24},{1,5},{5... | collective-permute-start | bytes 12582920 | tf_op jit(solution)/shard_map/ppermute | solution.py:401
  772.6 106.0 %collective-permute-start.53 = (bf16[1024,2816]{1,0:T(8,128)(2,1)}, bf16[1024,2816]{1,0:T(8,128)(2,1)}, u32[]{:S(2)}, u32[]{:S(2)}) collective-permute-start(bf16[1024,2816]{1,0:T(8,128)(2,1)} %pad_maximum_fusion.half_ref), channel_id=1, source_target_pairs={{0,4},{4,0},{8,12},{12,8},{16,20},{20,16},{24,28},{28,24},{1,5},{5... | collective-permute-start | bytes 17301512 | tf_op jit(solution)/shard_map/ppermute | solution.py:401
  788.7 50.5 %collective-permute-start.43 = (bf16[256,2048]{1,0:T(8,128)(2,1)}, bf16[256,2048]{1,0:T(8,128)(2,1)}, u32[]{:S(2)}, u32[]{:S(2)}) collective-permute-start(bf16[256,2048]{1,0:T(8,128)(2,1)} %constant_dynamic-slice_fusion.2), channel_id=1, source_target_pairs={{0,8},{4,12},{8,0},{12,4},{16,24},{20,28},{24,16},{28,20},{1,9},{5... | collective-permute-start | bytes 3145736 | tf_op jit(solution)/shard_map/ppermute | solution.py:401
  791.6 47.6 %collective-permute-start.44 = (bf16[256,2048]{1,0:T(8,128)(2,1)}, bf16[256,2048]{1,0:T(8,128)(2,1)}, u32[]{:S(2)}, u32[]{:S(2)}) collective-permute-start(bf16[256,2048]{1,0:T(8,128)(2,1)} %constant_dynamic-slice_fusion.1), channel_id=1, source_target_pairs={{0,16},{4,20},{8,24},{12,28},{16,0},{20,4},{24,8},{28,12},{1,17},{... | collective-permute-start | bytes 3145736 | tf_op jit(solution)/shard_map/ppermute | solution.py:401
  791.9 29.9 %collective-permute-start.46 = (bf16[176,1024]{1,0:T(8,128)(2,1)S(1)}, bf16[176,1024]{1,0:T(8,128)(2,1)S(1)}, u32[]{:S(2)}, u32[]{:S(2)}) collective-permute-start(bf16[176,1024]{1,0:T(8,128)(2,1)S(1)} %copy-done.38), channel_id=1, source_target_pairs={{0,8},{4,12},{8,0},{12,4},{16,24},{20,28},{24,16},{28,20},{1,9},{5... | collective-permute-start | bytes 1081352 | tf_op jit(solution)/shard_map/ppermute | solution.py:401
  794.0 30.4 %collective-permute-start.45 = (bf16[176,1024]{1,0:T(8,128)(2,1)S(1)}, bf16[176,1024]{1,0:T(8,128)(2,1)S(1)}, u32[]{:S(2)}, u32[]{:S(2)}) collective-permute-start(bf16[176,1024]{1,0:T(8,128)(2,1)S(1)} %add_convert_fusion.16), channel_id=1, source_target_pairs={{0,16},{4,20},{8,24},{12,28},{16,0},{20,4},{24,8},{28,12},{1,17},{... | collective-permute-start | bytes 1081352 | tf_op jit(solution)/shard_map/ppermute | solution.py:401
  826.1 5.7 collective-permute-start.40
  829.3 19.1 %collective-permute-start.57 = (bf16[352,1024]{1,0:T(8,128)(2,1)S(1)}, bf16[352,1024]{1,0:T(8,128)(2,1)S(1)}, u32[]{:S(2)}, u32[]{:S(2)}) collective-permute-start(bf16[352,1024]{1,0:T(8,128)(2,1)S(1)} %maximum_select_fusion.11), channel_id=1, source_target_pairs={{0,16},{4,20},{8,24},{12,28},{16,0},{20,4},{24,8},{28,12},{1,17},{... | collective-permute-start | bytes 2162696 | tf_op jit(solution)/shard_map/ppermute | solution.py:401
  836.8 16.2 %collective-permute-start.56 = (bf16[352,1024]{1,0:T(8,128)(2,1)S(1)}, bf16[352,1024]{1,0:T(8,128)(2,1)S(1)}, u32[]{:S(2)}, u32[]{:S(2)}) collective-permute-start(bf16[352,1024]{1,0:T(8,128)(2,1)S(1)} %maximum_select_fusion.10), channel_id=1, source_target_pairs={{0,8},{4,12},{8,0},{12,4},{16,24},{20,28},{24,16},{28,20},{1,9},{5... | collective-permute-start | bytes 2162696 | tf_op jit(solution)/shard_map/ppermute | solution.py:401
  841.8 14.8 %collective-permute-start.47 = (bf16[128,2048]{1,0:T(8,128)(2,1)}, bf16[128,2048]{1,0:T(8,128)(2,1)}, u32[]{:S(2)}, u32[]{:S(2)}) collective-permute-start(bf16[128,2048]{1,0:T(8,128)(2,1)} %constant_dynamic-slice_fusion), channel_id=1, source_target_pairs={{0,16},{4,20},{8,24},{12,28},{16,0},{20,4},{24,8},{28,12},{1,17},{... | collective-permute-start | bytes 1572872 | tf_op jit(solution)/shard_map/ppermute | solution.py:401
  853.1 10.7 %collective-permute-start.48 = (bf16[128,2048]{1,0:T(8,128)(2,1)S(1)}, bf16[128,2048]{1,0:T(8,128)(2,1)}, u32[]{:S(2)}, u32[]{:S(2)}) collective-permute-start(bf16[128,2048]{1,0:T(8,128)(2,1)S(1)} %constant_dynamic-slice_fusion.19), channel_id=1, source_target_pairs={{0,8},{4,12},{8,0},{12,4},{16,24},{20,28},{24,16},{28,20},{1,9},{5... | collective-permute-start | bytes 1572872 | tf_op jit(solution)/shard_map/ppermute | solution.py:401
  856.5 38.6 %collective-permute-start.58 = (bf16[1408,1024]{1,0:T(8,128)(2,1)S(1)}, bf16[1408,1024]{1,0:T(8,128)(2,1)S(1)}, u32[]{:S(2)}, u32[]{:S(2)}) collective-permute-start(bf16[1408,1024]{1,0:T(8,128)(2,1)S(1)} %pad_maximum_fusion.3.half_ref), channel_id=1, source_target_pairs={{0,4},{4,0},{8,12},{12,8},{16,20},{20,16},{24,28},{28,24},{1,5},{5... | collective-permute-start | bytes 8650760 | tf_op jit(solution)/shard_map/ppermute | solution.py:401
  865.0 27.1 %collective-permute-start.50 = (bf16[128,2048]{1,0:T(8,128)(2,1)S(1)}, bf16[128,2048]{1,0:T(8,128)(2,1)S(1)}, u32[]{:S(2)}, u32[]{:S(2)}) collective-permute-start(bf16[128,2048]{1,0:T(8,128)(2,1)S(1)} %add_convert_fusion.13), channel_id=1, source_target_pairs={{0,8},{4,12},{8,0},{12,4},{16,24},{20,28},{24,16},{28,20},{1,9},{5... | collective-permute-start | bytes 1572872 | tf_op jit(solution)/shard_map/ppermute | solution.py:401
  868.6 23.4 %collective-permute-start.49 = (bf16[128,2048]{1,0:T(8,128)(2,1)S(1)}, bf16[128,2048]{1,0:T(8,128)(2,1)S(1)}, u32[]{:S(2)}, u32[]{:S(2)}) collective-permute-start(bf16[128,2048]{1,0:T(8,128)(2,1)S(1)} %add_convert_fusion.14), channel_id=1, source_target_pairs={{0,16},{4,20},{8,24},{12,28},{16,0},{20,4},{24,8},{28,12},{1,17},{... | collective-permute-start | bytes 1572872 | tf_op jit(solution)/shard_map/ppermute | solution.py:401
  868.9 9.7 %collective-permute-start.42 = (f32[14,1024]{1,0:T(8,128)S(1)}, f32[14,1024]{1,0:T(8,128)S(1)}, u32[]{:S(2)}, u32[]{:S(2)}) collective-permute-start(f32[14,1024]{1,0:T(8,128)S(1)} %copy-done.48), channel_id=1, source_target_pairs={{0,16},{4,20},{8,24},{12,28},{16,0},{20,4},{24,8},{28,12},{1,17},{... | collective-permute-start | bytes 172040 | tf_op jit(solution)/shard_map/ppermute | solution.py:626
  892.3 16.2 %collective-permute-start.55 = (bf16[256,2048]{1,0:T(8,128)(2,1)S(1)}, bf16[256,2048]{1,0:T(8,128)(2,1)S(1)}, u32[]{:S(2)}, u32[]{:S(2)}) collective-permute-start(bf16[256,2048]{1,0:T(8,128)(2,1)S(1)} %maximum_select_fusion.9), channel_id=1, source_target_pairs={{0,16},{4,20},{8,24},{12,28},{16,0},{20,4},{24,8},{28,12},{1,17},{... | collective-permute-start | bytes 3145736 | tf_op jit(solution)/shard_map/ppermute | solution.py:401
  893.0 16.5 %collective-permute-start.54 = (bf16[256,2048]{1,0:T(8,128)(2,1)S(1)}, bf16[256,2048]{1,0:T(8,128)(2,1)S(1)}, u32[]{:S(2)}, u32[]{:S(2)}) collective-permute-start(bf16[256,2048]{1,0:T(8,128)(2,1)S(1)} %maximum_select_fusion.8), channel_id=1, source_target_pairs={{0,8},{4,12},{8,0},{12,4},{16,24},{20,28},{24,16},{28,20},{1,9},{5... | collective-permute-start | bytes 3145736 | tf_op jit(solution)/shard_map/ppermute | solution.py:401
  914.2 7.9 collective-permute-start.59
  (90 other events, 1507.6 us)
Sparse Core Ops, SparseCore 0:
  12.2 83.4 all-gather.7
  97.3 85.6 all-gather.9
  209.4 52.5 all-gather.17
  289.8 88.2 all-gather.11
  456.6 75.2 reduce-scatter.3
  573.7 80.4 all-gather.13
  656.4 83.2 all-gather.15
  746.8 76.5 reduce-scatter.5
  856.3 76.0 reduce-scatter.7

commit v11 on v10

--- a/solution.py
+++ b/solution.py
@@ -5,7 +5,7 @@
 from jax.experimental.pallas import tpu as pltpu
 
 BLK = 128
-CB = 4
+CB = 8
 CH = BLK * CB
 NEG = -1e30
 SCALE = 0.125
@@ -43,236 +43,248 @@
     return lane_of(shape) // 3 == 2 * pair + row_of(shape) // BLK
 
 
+def lanes_of(pair):
+    return slice(pair * 128, (pair + 1) * 128)
+
+
 def terms(x, lane):
     first = x.astype(jnp.bfloat16).astype(jnp.float32)
     second = (x - first).astype(jnp.bfloat16).astype(jnp.float32)
     return jnp.where(lane % 3 == 0, first, jnp.where(lane % 3 == 1, second, x - first - second))
 
 
-def place_rows(place_ref, s, refs, dst_ref, lane=0):
+def place_rows(place_ref, s, refs, dst_ref, ext=False):
+    pairs = dst_ref.shape[0]
     at = 0
     for ref in refs:
         for j in range(ref.shape[0]):
             for w in range(2):
-                row = pl.multiple_of(place_ref[s, at] * BLK, BLK)
-                dst_ref[pl.ds(row, BLK), lane:lane + 128] = ref[j, 0, w]
+                rows = pl.ds(pl.multiple_of(place_ref[s, at] * BLK, BLK), BLK)
+                for p in range(pairs):
+                    dst_ref[p, rows, 0:128] = ref[j, 0, w, :, p * 128:(p + 1) * 128]
+                    if ext:
+                        dst_ref[p, rows, 128:256] = ref[j, 0, w, :, pairs * 128:]
                 at += 1
 
 
-def fwd_kernel(place_ref, own_ref, q_ref, *refs, blocks, n):
-    k_refs, v_refs, (o_ref, ext_ref, ks, vs, scr, acc) = refs[:n], refs[n:2 * n], refs[2 * n:]
-    s, pair = pl.program_id(0), pl.program_id(1)
-
-    @pl.when((s == 0) & (pair == 0))
+def sweep(full, step):
+    def one(c, carry):
+        step(c, False)
+        return carry
+
+    lax.fori_loop(0, full, one, 0)
+    step(full, True)
+
+
+def span(c):
+    return pl.ds(pl.multiple_of(c * CH, CH), CH)
+
+
+def may_see(query_block, c):
+    shape = (2 * BLK, CH)
+    return c * CH + lane_of(shape) <= query_block * BLK + row_of(shape) % BLK
+
+
+def fwd_kernel(place_ref, own_ref, q_ref, *refs, pairs, n):
+    k_refs, v_refs, (o_ref, ext_ref, ks, vs, qs, scr, run, acc) = refs[:n], refs[n:2 * n], refs[2 * n:]
+    s = pl.program_id(0)
+
+    @pl.when(s == 0)
     def _():
-        vs[:, 128:256] = jnp.ones((blocks * BLK, 128), jnp.bfloat16)
-
-    @pl.when(pair == 0)
-    def _():
-        ext_ref[...] = jnp.zeros_like(ext_ref)
+        for p in range(pairs):
+            vs[p, :, 128:256] = jnp.ones((vs.shape[1], 128), jnp.bfloat16)
 
     place_rows(place_ref, s, k_refs, ks)
     place_rows(place_ref, s, v_refs, vs)
+
     for w in range(2):
         rows = slice(w * BLK, (w + 1) * BLK)
         pos = own_ref[s, w]
-        last = pos // CB
-        qs = split_heads(q_ref[0, rows, :] * jnp.bfloat16(SCALE))
-
-        def tiles_max(run, sc):
-            for t in range(CB):
-                run = jnp.maximum(run, sc[:, t * 128:(t + 1) * 128])
-            return run
-
-        def score(c, run):
-            at = pl.multiple_of(c * CH, CH)
-            sc = nt(qs, ks[pl.ds(at, CH), :])
-            scr[c] = sc
-            return tiles_max(run, sc)
-
-        run = lax.fori_loop(0, last, score, jnp.full((2 * BLK, 128), NEG, jnp.float32))
-        at = pl.multiple_of(last * CH, CH)
-        sc = nt(qs, ks[pl.ds(at, CH), :])
-        qpos = pos * BLK + row_of((2 * BLK, CH)) % BLK
-        kpos = last * CH + lane_of((2 * BLK, CH))
-        sc = jnp.where(kpos <= qpos, sc, NEG)
-        scr[last] = sc
-        run = tiles_max(run, sc)
-        top = jnp.broadcast_to(jnp.max(run, axis=1, keepdims=True), (2 * BLK, 128))
-        topc = jnp.concatenate([top] * CB, axis=1)
+        for p in range(pairs):
+            qs[p] = split_heads(q_ref[0, rows, lanes_of(p)] * jnp.bfloat16(SCALE))
+        run[...] = jnp.full_like(run, NEG)
         acc[...] = jnp.zeros_like(acc)
 
-        def weigh(c, carry):
-            at = pl.multiple_of(c * CH, CH)
-            p = jnp.exp(scr[c] - topc).astype(jnp.bfloat16)
-            acc[...] += nn(p, vs[pl.ds(at, CH), :])
-            return carry
-
-        lax.fori_loop(0, last + 1, weigh, 0)
-        total = acc[:, 128:256]
-        o_ref[0, rows, :] = join_heads(acc[:, 0:128] / total).astype(jnp.bfloat16)
+        def score(c, masked):
+            for p in range(pairs):
+                sc = nt(qs[p], ks[p, span(c), :])
+                if masked:
+                    sc = jnp.where(may_see(pos, c), sc, NEG)
+                scr[p, :, span(c)] = sc
+                top = run[p]
+                for t in range(CB):
+                    top = jnp.maximum(top, sc[:, t * 128:(t + 1) * 128])
+                run[p] = top
+
+        sweep(pos // CB, score)
+        for p in range(pairs):
+            run[p] = jnp.broadcast_to(jnp.max(run[p], axis=1, keepdims=True), (2 * BLK, 128))
+
+        def weigh(c, masked):
+            for p in range(pairs):
+                weight = jnp.exp(scr[p, :, span(c)] - jnp.concatenate([run[p]] * CB, axis=1)).astype(jnp.bfloat16)
+                acc[p] += nn(weight, vs[p, span(c), :])
+
+        sweep(pos // CB, weigh)
         lane = lane_of((2 * BLK, 128))
-        mine = jnp.where(own_lanes(pair), terms(-(top + jnp.log(total)), lane), 0.0)
-        ext_ref[0, rows, :] = (ext_ref[0, rows, :].astype(jnp.float32) + mine[:BLK] + mine[BLK:]).astype(jnp.bfloat16)
-
-
-def dq_kernel(place_ref, own_ref, q_ref, do_ref, qx_ref, dox_ref, c_ref, a_ref, b_ref, *refs, blocks, n):
-    k_refs, v_refs, (dq_ref, ks, vs, acc) = refs[:n], refs[n:2 * n], refs[2 * n:]
-    s, pair = pl.program_id(0), pl.program_id(1)
-
-    @pl.when((s == 0) & (pair == 0))
+        ext = jnp.zeros((BLK, 128), jnp.float32)
+        for p in range(pairs):
+            total = acc[p, :, 128:256]
+            o_ref[0, rows, lanes_of(p)] = join_heads(acc[p, :, 0:128] / total).astype(jnp.bfloat16)
+            mine = jnp.where(own_lanes(p), terms(-(run[p] + jnp.log(total)), lane), 0.0)
+            ext = ext + mine[:BLK] + mine[BLK:]
+        ext_ref[0, rows, :] = ext.astype(jnp.bfloat16)
+
+
+def dq_kernel(place_ref, own_ref, q_ref, do_ref, qx_ref, dox_ref, c_ref, a_ref, b_ref, *refs, pairs, n):
+    k_refs, v_refs, (dq_ref, ks, vs, qs, dos, acc) = refs[:n], refs[n:2 * n], refs[2 * n:]
+    s = pl.program_id(0)
+
+    @pl.when(s == 0)
     def _():
-        ks[:, 128:256] = jnp.ones((blocks * BLK, 128), jnp.bfloat16)
-        vs[:, 128:256] = jnp.ones((blocks * BLK, 128), jnp.bfloat16)
+        for ref in (ks, vs):
+            for p in range(pairs):
+                ref[p, :, 128:256] = jnp.ones((ref.shape[1], 128), jnp.bfloat16)
 
     place_rows(place_ref, s, k_refs, ks)
     place_rows(place_ref, s, v_refs, vs)
-    mine = own_lanes(pair)
+
     for w in range(2):
         rows = slice(w * BLK, (w + 1) * BLK)
         pos = own_ref[s, w]
-        last = pos // CB
-
-        def extend(tile, ext):
+
+        def extend(tile, ext, p):
             both = jnp.concatenate([ext, ext], axis=0)
-            return jnp.concatenate([split_heads(tile), jnp.where(mine, both, jnp.zeros_like(both))], axis=1)
-
-        qs = extend(q_ref[0, rows, :] * jnp.bfloat16(SCALE), qx_ref[0, rows, :])
-        dos = extend(do_ref[0, rows, :], dox_ref[0, rows, :])
+            return jnp.concatenate([split_heads(tile), jnp.where(own_lanes(p), both, jnp.zeros_like(both))], axis=1)
+
+        for p in range(pairs):
+            qs[p] = extend(q_ref[0, rows, lanes_of(p)] * jnp.bfloat16(SCALE), qx_ref[0, rows, :], p)
+            dos[p] = extend(do_ref[0, rows, lanes_of(p)], dox_ref[0, rows, :], p)
         acc[...] = jnp.zeros_like(acc)
 
-        def step(c, mask):
-            at = pl.multiple_of(c * CH, CH)
-            p = jnp.exp(nt(qs, ks[pl.ds(at, CH), :]))
-            if mask is not None:
-                p = jnp.where(mask, p, 0.0)
-            ds = (p * nt(dos, vs[pl.ds(at, CH), :])).astype(jnp.bfloat16)
-            acc[...] += nn(ds, ks[pl.ds(at, CH), 0:128])
-
-        def body(c, carry):
-            step(c, None)
-            return carry
-
-        lax.fori_loop(0, last, body, 0)
-        qpos = pos * BLK + row_of((2 * BLK, CH)) % BLK
-        kpos = last * CH + lane_of((2 * BLK, CH))
-        step(last, kpos <= qpos)
-        grad = join_heads(acc[...]) * SCALE
-        dq_ref[0, rows, :] = turn(grad, c_ref[rows], a_ref[rows], b_ref[rows], -1.0).astype(jnp.bfloat16)
-
-
-def dkv_kernel(place_ref, own_ref, slots_ref, k_ref, v_ref, c_ref, a_ref, b_ref, *refs, blocks, n, lead):
-    q_refs, qx_refs, (do_ref, dox_ref, dk_ref, dv_ref, qs, dos, acck, accv) = refs[:n], refs[n:2 * n], refs[2 * n:]
-    s, pair = pl.program_id(0) + lead, pl.program_id(1)
-    place_rows(place_ref, s, q_refs, qs)
-    place_rows(slots_ref, s, [do_ref], dos)
-
-    @pl.when(pair == 0)
-    def _():
-        place_rows(place_ref, s, qx_refs, qs, 128)
-        place_rows(slots_ref, s, [dox_ref], dos, 128)
-
-    ones = own_lanes(pair).astype(jnp.bfloat16)
+        def step(c, masked):
+            for p in range(pairs):
+                prob = jnp.exp(nt(qs[p], ks[p, span(c), :]))
+                if masked:
+                    prob = jnp.where(may_see(pos, c), prob, 0.0)
+                ds = (prob * nt(dos[p], vs[p, span(c), :])).astype(jnp.bfloat16)
+                acc[p] += nn(ds, ks[p, span(c), 0:128])
+
+        sweep(pos // CB, step)
+        for p in range(pairs):
+            grad = join_heads(acc[p]) * SCALE
+            dq_ref[0, rows, lanes_of(p)] = turn(grad, c_ref[rows], a_ref[rows], b_ref[rows], -1.0).astype(jnp.bfloat16)
+
+
+def dkv_kernel(place_ref, own_ref, kv_ref, c_ref, a_ref, b_ref, *refs, pairs, n, lead):
+    q_refs, do_refs, (dk_ref, dv_ref, qs, dos, kw, vw, acck, accv) = refs[:n], refs[n:2 * n], refs[2 * n:]
+    s = pl.program_id(0) + lead
+    place_rows(place_ref, s, q_refs, qs, True)
+    place_rows(place_ref, s, do_refs, dos, True)
+    chunks = qs.shape[1] // CH
+
     for w in range(2):
         rows = slice(w * BLK, (w + 1) * BLK)
         pos = own_ref[s, w]
         first = pos // CB
-        kw = jnp.concatenate([split_heads(k_ref[0, 0, rows, :] * jnp.bfloat16(SCALE)), ones], axis=1)
-        vw = jnp.concatenate([split_heads(v_ref[0, 0, rows, :]), ones], axis=1)
+        for p in range(pairs):
+            ones = own_lanes(p).astype(jnp.bfloat16)
+            kw[p] = jnp.concatenate([split_heads(kv_ref[0, 0, rows, lanes_of(p)] * jnp.bfloat16(SCALE)), ones], axis=1)
+            vw[p] = jnp.concatenate([split_heads(kv_ref[1, 0, rows, lanes_of(p)]), ones], axis=1)
         acck[...] = jnp.zeros_like(acck)
         accv[...] = jnp.zeros_like(accv)
 
-        def step(c, mask):
-            at = pl.multiple_of(c * CH, CH)
-            p = jnp.exp(nt(kw, qs[pl.ds(at, CH), :]))
-            if mask is not None:
-                p = jnp.where(mask, p, 0.0)
-            accv[...] += nn(p.astype(jnp.bfloat16), dos[pl.ds(at, CH), 0:128])
-            ds = (p * nt(vw, dos[pl.ds(at, CH), :])).astype(jnp.bfloat16)
-            acck[...] += nn(ds, qs[pl.ds(at, CH), 0:128])
-
-        def body(c, carry):
-            step(c, None)
+        def step(c, masked):
+            for p in range(pairs):
+                prob = jnp.exp(nt(kw[p], qs[p, span(c), :]))
+                if masked:
+                    shape = (2 * BLK, CH)
+                    prob = jnp.where(pos * BLK + row_of(shape) % BLK <= c * CH + lane_of(shape), prob, 0.0)
+                accv[p] += nn(prob.astype(jnp.bfloat16), dos[p, span(c), 0:128])
+                ds = (prob * nt(vw[p], dos[p, span(c), :])).astype(jnp.bfloat16)
+                acck[p] += nn(ds, qs[p, span(c), 0:128])
+
+        def one(c, carry):
+            step(c, False)
             return carry
 
-        kpos = pos * BLK + row_of((2 * BLK, CH)) % BLK
-        qpos = first * CH + lane_of((2 * BLK, CH))
-        step(first, kpos <= qpos)
-        lax.fori_loop(first + 1, blocks // CB, body, 0)
-        grad = join_heads(acck[...]) * SCALE
-        dk_ref[0, rows, :] = turn(grad, c_ref[rows], a_ref[rows], b_ref[rows], -1.0).astype(jnp.bfloat16)
-        dv_ref[0, rows, :] = join_heads(accv[...]).astype(jnp.bfloat16)
-
-
-OWN = pl.BlockSpec((1, 2 * BLK, 128), lambda s, h, *_: (s, 0, h))
-EXT = pl.BlockSpec((1, 2 * BLK, 128), lambda s, h, *_: (s, 0, 0))
+        step(first, True)
+        lax.fori_loop(first + 1, chunks, one, 0)
+        for p in range(pairs):
+            grad = join_heads(acck[p]) * SCALE
+            dk_ref[0, rows, lanes_of(p)] = turn(grad, c_ref[rows], a_ref[rows], b_ref[rows], -1.0).astype(jnp.bfloat16)
+            dv_ref[0, rows, lanes_of(p)] = join_heads(accv[p]).astype(jnp.bfloat16)
+
+
+def own(width):
+    return pl.BlockSpec((1, 2 * BLK, width), lambda s, *_: (s, 0, 0))
 
 
 def table(lead=0):
-    return pl.BlockSpec((2 * BLK, 128), lambda s, h, *_: (s + lead, 0))
-
-
-def piece(x, first=0, lane=None, lead=0, count=1):
-    return pl.BlockSpec((count, 1, 2, BLK, 128), lambda s, h, *_: (first, s + lead, 0, 0, h if lane is None else lane))
-
-
-def attention_call(kernel, name, mats, seqs, pairs, blocks, in_specs, out_specs, out_shape, scratch, args, prefetch=2):
+    return pl.BlockSpec((2 * BLK, 128), lambda s, *_: (s + lead, 0))
+
+
+def piece(x, first=0, lead=0):
+    return pl.BlockSpec((1, 1, 2, BLK, x.shape[4]), lambda s, *_: (first, s + lead, 0, 0, 0))
+
+
+def attention_call(kernel, name, mats, seqs, pairs, blocks, in_specs, out_specs, out_shape, scratch, args):
     work = seqs * pairs * 2 * 2 * BLK * blocks * BLK // 2
     return pl.pallas_call(
         kernel,
         grid_spec=pltpu.PrefetchScalarGridSpec(
-            num_scalar_prefetch=prefetch, grid=(seqs, pairs), in_specs=in_specs, out_specs=out_specs, scratch_shapes=scratch),
+            num_scalar_prefetch=2, grid=(seqs,), in_specs=in_specs, out_specs=out_specs, scratch_shapes=scratch),
         out_shape=out_shape,
         compiler_params=pltpu.CompilerParams(vmem_limit_bytes=60 * 2**20),
-        cost_estimate=pl.CostEstimate(flops=work * 512 * mats, bytes_accessed=4 * seqs * pairs * blocks * BLK * 128, transcendentals=work),
+        cost_estimate=pl.CostEstimate(flops=work * 64 * mats, bytes_accessed=seqs * pairs * blocks * BLK * 128, transcendentals=0),
         name=name,
     )(*args)
 
 
-def rows_of(blocks, lanes):
-    return pltpu.VMEM((blocks * BLK, lanes), jnp.bfloat16)
-
-
-def acc_of(lanes):
-    return pltpu.VMEM((2 * BLK, lanes), jnp.float32)
-
-
-def attend(place, own, q, keys, values):
-    seqs, pairs, blocks = q.shape[0], q.shape[2] // 128, place.shape[1]
+def rows_of(pairs, blocks, lanes):
+    return pltpu.VMEM((pairs, blocks * BLK, lanes), jnp.bfloat16)
+
+
+def acc_of(pairs, lanes, dtype=jnp.float32):
+    return pltpu.VMEM((pairs, 2 * BLK, lanes), dtype)
+
+
+def attend(place, own_blocks, q, keys, values):
+    seqs, width, blocks = q.shape[0], q.shape[2], place.shape[1]
+    pairs = width // 128
     return attention_call(
-        functools.partial(fwd_kernel, blocks=blocks, n=len(keys)), "attend", 2, seqs, pairs, blocks,
-        [OWN] + [piece(*e) for e in keys + values], [OWN, EXT],
+        functools.partial(fwd_kernel, pairs=pairs, n=len(keys)), "attend", 2, seqs, pairs, blocks,
+        [own(width)] + [piece(*e) for e in keys + values], [own(width), own(128)],
         [jax.ShapeDtypeStruct(q.shape, jnp.bfloat16), jax.ShapeDtypeStruct(q.shape[:2] + (128,), jnp.bfloat16)],
-        [rows_of(blocks, 128), rows_of(blocks, 256), pltpu.VMEM((blocks // CB, 2 * BLK, CH), jnp.float32), acc_of(256)],
-        [place, own, q] + [e[0] for e in keys + values])
-
-
-def query_grad(place, own, q, do, q_ext, do_ext, tabs, keys, values):
-    seqs, pairs, blocks = q.shape[0], q.shape[2] // 128, place.shape[1]
+        [rows_of(pairs, blocks, 128), rows_of(pairs, blocks, 256), acc_of(pairs, 128, jnp.bfloat16), acc_of(pairs, blocks * BLK),
+         acc_of(pairs, 128), acc_of(pairs, 256)],
+        [place, own_blocks, q] + [e[0] for e in keys + values])
+
+
+def query_grad(place, own_blocks, q, do, q_ext, do_ext, tabs, keys, values):
+    seqs, width, blocks = q.shape[0], q.shape[2], place.shape[1]
+    pairs = width // 128
     return attention_call(
-        functools.partial(dq_kernel, blocks=blocks, n=len(keys)), "query_grad", 3, seqs, pairs, blocks,
-        [OWN, OWN, EXT, EXT] + [table()] * 3 + [piece(*e) for e in keys + values], OWN,
+        functools.partial(dq_kernel, pairs=pairs, n=len(keys)), "query_grad", 3, seqs, pairs, blocks,
+        [own(width), own(width), own(128), own(128)] + [table()] * 3 + [piece(*e) for e in keys + values], own(width),
         jax.ShapeDtypeStruct(q.shape, jnp.bfloat16),
-        [rows_of(blocks, 256), rows_of(blocks, 256), acc_of(128)],
-        [place, own, q, do, q_ext, do_ext, *tabs] + [e[0] for e in keys + values])
-
-
-def key_value_grad(place, own, slots, kv, tabs, queries, grads, lead, count):
-    pairs, blocks = kv.shape[3] // 128, place.shape[1]
+        [rows_of(pairs, blocks, 256), rows_of(pairs, blocks, 256), acc_of(pairs, 256, jnp.bfloat16), acc_of(pairs, 256, jnp.bfloat16),
+         acc_of(pairs, 128)],
+        [place, own_blocks, q, do, q_ext, do_ext, *tabs] + [e[0] for e in keys + values])
+
+
+def key_value_grad(place, own_blocks, kv, tabs, queries, grads, lead, count):
+    width, blocks = kv.shape[3], place.shape[1]
+    pairs = width // 128
     shape = (count,) + kv.shape[2:]
-    n = grads.shape[0]
-
-    def own_part(i):
-        return pl.BlockSpec((1, 1, 2 * BLK, 128), lambda s, h, *_: (i, s + lead, 0, h))
-
     return attention_call(
-        functools.partial(dkv_kernel, blocks=blocks, n=len(queries), lead=lead), "key_value_grad", 4, count, pairs, blocks,
-        [own_part(0), own_part(1)] + [table(lead)] * 3 + [piece(x, lead=lead) for x in queries]
-        + [piece(x, lane=pairs, lead=lead) for x in queries]
-        + [piece(grads, lead=lead, count=n), piece(grads, lane=pairs, lead=lead, count=n)], [OWN, OWN],
+        functools.partial(dkv_kernel, pairs=pairs, n=len(queries), lead=lead), "key_value_grad", 4, count, pairs, blocks,
+        [pl.BlockSpec((2, 1, 2 * BLK, width), lambda s, *_: (0, s + lead, 0, 0))] + [table(lead)] * 3
+        + [piece(x, lead=lead) for x in queries + grads], [own(width)] * 2,
         [jax.ShapeDtypeStruct(shape, jnp.bfloat16)] * 2,
-        [rows_of(blocks, 256), rows_of(blocks, 256), acc_of(128), acc_of(128)],
-        [place, own, slots, kv, kv, *tabs] + queries * 2 + [grads] * 2, prefetch=3)
+        [rows_of(pairs, blocks, 256), rows_of(pairs, blocks, 256), acc_of(pairs, 256, jnp.bfloat16), acc_of(pairs, 256, jnp.bfloat16),
+         acc_of(pairs, 128), acc_of(pairs, 128)],
+        [place, own_blocks, kv, *tabs] + queries + grads)
 
 
 import math
@@ -417,9 +429,10 @@
     return lax.dynamic_slice_in_dim(x, (side if mine else 1 - side) * r, r, 0)
 
 
-def weight_grad(part):
+def weight_grad(part, flying):
     core = lax.axis_index("ctx") & 1
     got = ctx_swap(part(1 - core).astype(BF16), 1)
+    flying[:] = [got]
     gate = yield
     half = (part(core) + after(got, gate).astype(F32)).astype(BF16)
     bits = list(range(1, int(math.log2(lax.axis_size("ctx")))))
@@ -430,6 +443,7 @@
     for i in range(len(bits)):
         streams = after(streams, gate)
         got = [ctx_swap(half_of(x, o[i], False), 1 << o[i]) for x, o in zip(streams, orders)]
+        flying[:] = got
         gate = yield
         streams, got = after((streams, got), gate)
         streams = [add16(half_of(x, o[i], True), g) for x, o, g in zip(streams, orders, got)]
@@ -437,6 +451,7 @@
     for i in reversed(range(len(bits))):
         streams = after(streams, gate)
         got = [ctx_swap(x, 1 << o[i]) for x, o in zip(streams, orders)]
+        flying[:] = got
         gate = yield
         streams, got = after((streams, got), gate)
         streams = [
@@ -452,8 +467,8 @@
     yield after((streams, other), gate)
 
 
-def begin(*args):
-    chain = weight_grad(*args)
+def begin(part, flying=None):
+    chain = weight_grad(part, [] if flying is None else flying)
     next(chain)
     return chain
 
@@ -681,8 +696,9 @@
     part_two = (nt(grad_gu[:, :ff], gate_w) + nt(grad_gu[:, ff:], up_w)).astype(BF16)
     grad_two = sum_rows(part_two)
     act, rows_two, dy_rows, grad_gu = after((act, rows_two, dy_rows, grad_gu), part_two)
-    gu = begin(lambda core: rc(columns(rows_two, core), grad_gu))
-    dw = begin(lambda core: rc(act, columns(dy_rows, core)))
+    gu_fly, dw_fly = [], []
+    gu = begin(lambda core: rc(columns(rows_two, core), grad_gu), gu_fly)
+    dw = begin(lambda core: rc(act, columns(dy_rows, core)), dw_fly)
     held = take(gu)
     go(gu)
     down = nn(after(act, held), down_w).astype(BF16)
@@ -705,60 +721,62 @@
     do_ext = terms(-delta, lane).astype(BF16)
     do_sent = jnp.concatenate([grad_attn, do_ext], axis=1).reshape(shape)
     do_sent = after(do_sent, held)
-    grads = lax.all_gather(do_sent, "ctx", axis=0, tiled=True)
+    branch = all_rows(after(branch_own, do_sent))
+    out_sum = sum_rows(after(down, do_sent))
+    grads = gather_other(do_sent)
     grad_q = query_grad(place, own, q, grad_attn.reshape(q.shape), q_ext, do_ext.reshape(q_ext.shape), tabs, keys, values)
-    grad_q = grad_q.reshape(-1, width)
+    grad_q = after(grad_q.reshape(-1, width), [grads[j] for j in grads if j > 1])
+    grads = gather_cores(grads, grad_q)
     q_part = nt(grad_q, query_w)
-    held = take(gu, q_part), take(dw, q_part)
+    first = key_value_grad(place, own, kv, tabs, queries, grads, 0, SEQS // 2)
+    grads = after(grads, take(gu, first), take(dw, first))
     go(gu)
     go(dw)
-    grads = after(grads, held)
-    branch = all_rows(after(branch_own, grads))
-    first = key_value_grad(place, own, block_order, kv, tabs, queries, grads, 0, SEQS // 2)
-    grads = after(grads, take(dw, first))
-    go(dw)
-    second = key_value_grad(place, own, block_order, kv, tabs, queries, grads, SEQS // 2, SEQS // 2)
+    second = key_value_grad(place, own, kv, tabs, queries, grads, SEQS // 2, SEQS // 2)
+    second = after(second, dw_fly)
     grad_k, grad_v = (jnp.concatenate(pair).reshape(-1, width) for pair in zip(first, second))
     part_one = q_part + nt(grad_k, key_w) + nt(grad_v, value_w)
     part_sent = after(part_one.astype(BF16), branch)
     grad_one = sum_rows(part_sent)
-    out_tokens = (mixed + sum_rows(after(down, grad_one)).astype(F32)).astype(BF16)
-
-    rows_one, branch, grad_q, grad_k, grad_v = after((rows_one, branch, grad_q, grad_k, grad_v), part_sent)
+
+    rows_one, branch, grad_q, grad_k, grad_v = after((rows_one, branch, grad_q, grad_k, grad_v), part_sent, gu_fly)
     grad_qkv = jnp.concatenate([grad_q, grad_k, grad_v], axis=1)
     chain = begin(lambda core: jnp.concatenate([rc(columns(rows_one, core), grad_qkv), rc(columns(branch, core), attn_rows)], axis=1))
-    take(gu, part_sent)
+    held = take(chain)
+    go(chain)
+    take(gu, held)
     take_extra(gu)
     go(gu)
-    held = take(chain)
-    go(chain)
+    take(dw, held)
+    go(dw)
     unit_rows = (rows_one.astype(F32) - shift_one) / gain_one
     bias_grad = jnp.sum(grad_qkv.astype(F32), axis=0)
     tp_row = (jnp.arange(n_tp) == lax.axis_index("tp"))[:, None]
     small = jnp.concatenate([
         jnp.sum(part_one * unit_rows, axis=0), jnp.sum(part_one, axis=0), grad_gain_two, grad_shift_two,
         jnp.where(tp_row, bias_grad[None, :], 0.0).reshape(-1)])
+    held = take(chain)
+    go(chain)
+    take(dw, held)
+    go(dw)
+    held = take(chain)
+    go(chain)
+    take(dw, held)
+    take_extra(dw)
+    go(dw)
+    mixed_late, out_sum = after((mixed, out_sum), held)
+    out_tokens = (mixed_late + out_sum.astype(F32)).astype(BF16)
+    grad_gate_w, grad_up_w = unpack_rows(*take(gu, held), 2)
+    held = take(chain, grad_gate_w)
+    go(chain)
     sums = sum_over_all(after(small, held).reshape(-1, 1024))
     small = [next(sums) for _ in range(1 + int(math.log2(n_tp)))]
-    made = take(dw, held)
-    take_extra(dw)
-    go(dw)
-    held = take(chain, (made, small))
+    grad_down_w = unpack_cols(*take(dw, held))
+    take(chain, (grad_down_w, small))
+    take_extra(chain)
     go(chain)
-    small = next(sums)
-    take(dw, held)
-    go(dw)
-    held = take(chain, small)
-    go(chain)
-    grad_gate_w, grad_up_w = unpack_rows(*take(gu, held), 2)
     for _ in range(4):
         small = next(sums)
-    held = take(chain, (grad_gate_w, small))
-    go(chain)
-    grad_down_w = unpack_cols(*take(dw, held))
-    take(chain, grad_down_w)
-    take_extra(chain)
-    go(chain)
     depth = x.shape[1]
     small = small.reshape(-1)
     norms = small[:4 * depth].reshape(4, depth)

time: 949 us -> 902 us (0.950)
  Pallas kernels: 235 us -> 192 us
    pallas_call x4, Pallas kernels: 163 us -> 107 us  [attention_call(): pl.pallas_call(kernel, grid_spec=pltpu.PrefetchScalarGridSpec(num_scalar_...]
    ppermute x46 -> x53, waiting for transfers between devices: 192 us -> 221 us  [ctx_swap(): return lax.ppermute(x, 'ctx', [(i, i ^ mask) for i in range(n)])]
    pallas_call x1, Pallas kernels: 28.4 us -> 39.5 us  [mlp(): pl.pallas_call(mlp_kernel, grid=(total // step,), in_specs=[block, block,...]
    ppermute x46 -> x53, starting transfers between devices: 51.5 us -> 50.1 us  [ctx_swap(): return lax.ppermute(x, 'ctx', [(i, i ^ mask) for i in range(n)])]
  transfers between devices with their start and end apart: 69 -> 75, of which waited for: 31 -> 35; matrix products, arithmetic and copies ran while one was open for 19% -> 19% of each run, Pallas kernels for 22% -> 16%
where the time goes in v11:
time: 902 us; the launch traced here: 896 us
  waiting for transfers between devices  392 us (43%)
  Pallas kernels  192 us (21%)
  matrix products  110 us (12%)
  other arithmetic  73.9 us (8%)
  starting transfers between devices  70.7 us (8%)
  local copies, waits for them, and re-layouts  40.3 us (4%)
  between operations  15.9 us (2%)
    ppermute x53, waiting for transfers between devices, ctx_swap(): return lax.ppermute(x, 'ctx', [(i, i ^ mask) for i in range(n)])  221 us
    pallas_call x4, Pallas kernels, attention_call(): pl.pallas_call(kernel, grid_spec=pltpu.PrefetchScalarGridSpec(num_scalar_...  107 us
    all_gather x4, waiting for transfers between devices, all_rows(): return lax.all_gather(x, 'tp', axis=0, tiled=True)  101 us
    ppermute x53, starting transfers between devices, ctx_swap(): return lax.ppermute(x, 'ctx', [(i, i ^ mask) for i in range(n)])  50.1 us
    dot_general x8, matrix products, rc(): lax.dot_general(left, right, (((0,), (0,)), ((), ())), preferred_element_...  48.7 us
    dot_general x6, matrix products, nt(): lax.dot_general(a, b, (((1,), (1,)), ((), ())), preferred_element_type=jn...  45.9 us
    pallas_call x1, Pallas kernels, mlp(): pl.pallas_call(mlp_kernel, grid=(total // step,), in_specs=[block, block,...  39.5 us
    ppermute x6, waiting for transfers between devices, tp_shift(): return lax.ppermute(x, 'tp', [(i, (i + d) % n) for i in range(n)])  32.7 us
  transfers between devices with their start and end apart: 75, of which 35 were waited for; matrix products, arithmetic and copies ran while one was open for 19% of the time, Pallas kernels for 16%

profile of v11, /device:TPU:0, one launch (start us, length us, event | category | flops | bytes accessed | tf_op | source)
XLA Modules:
  0.0 895.6 jit_solution(9055376791707589259)
XLA Ops:
  12.7 83.6 %all-gather.7.cloned.1.call-done.h_ref = bf16[1024,2048]{1,0:T(8,128)(2,1)} async-done(((bf16[256,2048]{1,0:T(8,128)(2,1)}), bf16[1024,2048]{1,0:T(8,128)(2,1)}) %all-gather.7.cloned.1.call-update) | async-done | bytes 4194320 | tf_op jit(solution)/shard_map/all_gather | solution.py:568
  99.2 11.8 %project.1 = (bf16[4,256,512]{2,1,0:T(8,128)(2,1)S(1)}, bf16[2,4,256,512]{3,2,1,0:T(8,128)(2,1)}) custom-call(bf16[1024,2048]{1,0:T(8,128)(2,1)} %all-gather.7.cloned.1.call-done.h_ref, bf16[2048,512]{1,0:T(8,128)(2,1)} %wq_ref.1, bf16[2048,512]{1,0:T(8,128)(2,1)} %wk_ref.1, bf16[2048,512]{1,0:T(8,128)(2,1)} %wv_ref.1, ...), custom_call_target="tpu_custom_call" | custom-call | flops 6442450944 | bytes 6291456 | tf_op jit(solution)/shard_map/project/pallas_call | solution.py:357
  114.9 44.7 %collective-permute-done.3.refs_4_.refs_12_ = bf16[2,4,2,128,512]{4,3,2,1,0:T(8,128)(2,1)} collective-permute-done((bf16[2,4,2,128,512]{4,3,2,1,0:T(8,128)(2,1)}, bf16[2,4,2,128,512]{4,3,2,1,0:T(8,128)(2,1)}, u32[]{:S(2)}, u32[]{:S(2)}) %collective-permute-start.3) | collective-permute-done | bytes 2097184 | tf_op jit(solution)/shard_map/ppermute | solution.py:413
  170.1 9.3 %collective-permute-done.14 = bf16[64,2048]{1,0:T(8,128)(2,1)S(1)} collective-permute-done((bf16[64,2048]{1,0:T(8,128)(2,1)S(1)}, bf16[64,2048]{1,0:T(8,128)(2,1)S(1)}, u32[]{:S(2)}, u32[]{:S(2)}) %collective-permute-start.14) | collective-permute-done | bytes 262176 | tf_op jit(solution)/shard_map/ppermute | solution.py:651
  179.5 19.8 %collective-permute-done.13 = bf16[64,2048]{1,0:T(8,128)(2,1)S(1)} collective-permute-done((bf16[64,2048]{1,0:T(8,128)(2,1)S(1)}, bf16[64,2048]{1,0:T(8,128)(2,1)S(1)}, u32[]{:S(2)}, u32[]{:S(2)}) %collective-permute-start.13) | collective-permute-done | bytes 262176 | tf_op jit(solution)/shard_map/ppermute | solution.py:651
  206.2 3.4 collective-permute-done.8.refs_15_
  211.5 28.5 %attend.1 = (bf16[4,256,512]{2,1,0:T(8,128)(2,1)}, bf16[4,256,128]{2,1,0:T(8,128)(2,1)}) custom-call(s32[4,16]{1,0:T(4,128)} %copy.44.place_ref, s32[4,2]{1,0:T(4,128)} %get-tuple-element.227.own_ref, bf16[4,256,512]{2,1,0:T(8,128)(2,1)} %copy-done.2, bf16[2,4,2,128,512]{4,3,2,1,0:T(8,128)(2,1)} %bitcast.5.refs_0_.refs_8_, ...), custom_call_target="tpu_custom_call" | custom-call | flops 1073741824 | bytes 4194304 | tf_op jit(solution)/shard_map/attend/pallas_call | solution.py:233
  242.2 3.8 collective-permute-start.11
  246.1 7.5 collective-permute-done.9
  253.6 10.0 %collective-permute-done.10 = bf16[256,512]{1,0:T(8,128)(2,1)S(1)} collective-permute-done((bf16[256,512]{1,0:T(8,128)(2,1)S(1)}, bf16[256,512]{1,0:T(8,128)(2,1)S(1)}, u32[]{:S(2)}, u32[]{:S(2)}) %collective-permute-start.10) | collective-permute-done | bytes 262176 | tf_op jit(solution)/shard_map/ppermute | solution.py:573
  264.6 6.1 fusion.84
  277.8 29.4 %collective-permute-done.20.refs_6_ = bf16[1,4,2,128,640]{4,3,2,1,0:T(8,128)(2,1)} collective-permute-done((bf16[1,4,2,128,640]{4,3,2,1,0:T(8,128)(2,1)}, bf16[1,4,2,128,640]{4,3,2,1,0:T(8,128)(2,1)}, u32[]{:S(2)}, u32[]{:S(2)}) %collective-permute-start.20) | collective-permute-done | bytes 1310752 | tf_op jit(solution)/shard_map/ppermute | solution.py:413
  307.2 27.2 %collective-permute-done.18.refs_4_ = bf16[1,4,2,128,640]{4,3,2,1,0:T(8,128)(2,1)} collective-permute-done((bf16[1,4,2,128,640]{4,3,2,1,0:T(8,128)(2,1)}, bf16[1,4,2,128,640]{4,3,2,1,0:T(8,128)(2,1)}, u32[]{:S(2)}, u32[]{:S(2)}) %collective-permute-start.18) | collective-permute-done | bytes 1310752 | tf_op jit(solution)/shard_map/ppermute | solution.py:413
  334.8 2.9 collective-permute-done.19.refs_5_
  339.6 17.6 %all-gather.11.cloned.1.call-done.h_ref = bf16[1024,2048]{1,0:T(8,128)(2,1)} async-done(((bf16[256,2048]{1,0:T(8,128)(2,1)}), bf16[1024,2048]{1,0:T(8,128)(2,1)}) %all-gather.11.cloned.1.call-update) | async-done | bytes 4194320 | tf_op jit(solution)/shard_map/all_gather | solution.py:568
  357.1 39.5 %mlp.1 = (bf16[1024,1408]{1,0:T(8,128)(2,1)}, bf16[1024,2816]{1,0:T(8,128)(2,1)}) custom-call(bf16[1024,2048]{1,0:T(8,128)(2,1)} %all-gather.11.cloned.1.call-done.h_ref, bf16[1024,2048]{1,0:T(8,128)(2,1)} %all-gather.9.cloned.1.call-done.dy_ref, bf16[2048,1408]{1,0:T(8,128)(2,1)} %gate_ref.1, bf16[2048,1408]{1,0:T(8,128)(2,1)} %up_ref.1, ...), custom_call_target="tpu_custom_call" | custom-call | flops 17716740096 | bytes 38273024 | tf_op jit(solution)/shard_map/mlp/pallas_call | solution.py:397
  396.7 9.8 %fusion.5 = f32[1024,2048]{1,0:T(8,128)S(1)} fusion(bf16[2048,1408]{1,0:T(8,128)(2,1)} %gate_ref.1, bf16[1024,2816]{1,0:T(8,128)(2,1)} %get-tuple-element.130), kind=kOutput, calls=%fused_computation.30 | convolution fusion | flops 5905580032 | bytes 17039360 | tf_op jit(solution)/shard_map/dot_general | solution.py:15
  406.4 11.1 %add_convert_fusion.1 = bf16[1024,2048]{1,0:T(8,128)(2,1)} fusion(f32[1024,2048]{1,0:T(8,128)S(1)} %fusion.5, bf16[2048,1408]{1,0:T(8,128)(2,1)} %up_ref.1, bf16[1024,2816]{1,0:T(8,128)(2,1)S(1)} %copy-done.78), kind=kOutput, calls=%fused_computation.5 | convolution fusion | flops 5909774336 | bytes 21233664 | tf_op jit(solution)/shard_map/dot_general | solution.py:15
  417.5 11.1 %convolution_convert_fusion = bf16[1024,2816]{1,0:T(8,128)(2,1)} fusion(bf16[1024,2816]{1,0:T(8,128)(2,1)} %get-tuple-element.130, bf16[1024,2048]{1,0:T(8,128)(2,1)} %all-gather.11.cloned.1.call-done.h_ref, s32[]{:T(128)S(6)} %select_n.384), kind=kOutput, calls=%fused_computation.9 | convolution fusion | flops 5908463616 | bytes 13631492 | tf_op jit(solution)/shard_map/dot_general | solution.py:302
  428.6 4.5 convolution_convert_fusion.3
  433.7 8.7 collective-permute-done.23
  442.5 6.6 add_convert_fusion.2
  451.1 10.9 %add_convert_fusion = bf16[1024,2816]{1,0:T(8,128)(2,1)S(1)} fusion(bf16[1024,2816]{1,0:T(8,128)(2,1)} %collective-permute-done.22, bf16[1024,2816]{1,0:T(8,128)(2,1)} %get-tuple-element.130, bf16[1024,2048]{1,0:T(8,128)(2,1)S(1)} %copy-done.75, s32[]{:T(128)S(6)} %select_n.383), kind=kOutput, calls=%fused_computation | convolution fusion | flops 5914230784 | bytes 19398660 | tf_op jit(solution)/shard_map/dot_general | solution.py:302
  468.0 8.2 convolution_convert_fusion.1
  476.1 21.6 %collective-permute-done.24 = bf16[256,2816]{1,0:T(8,128)(2,1)} collective-permute-done((bf16[256,2816]{1,0:T(8,128)(2,1)}, bf16[256,2816]{1,0:T(8,128)(2,1)}, u32[]{:S(2)}, u32[]{:S(2)}) %collective-permute-start.24) | collective-permute-done | bytes 1441824 | tf_op jit(solution)/shard_map/ppermute | solution.py:413
  511.5 2.6 fusion.78
  514.1 6.1 convolution_convert_fusion.4
  520.6 4.3 collective-permute-done.30
  532.1 10.8 %collective-permute-done.26 = bf16[256,512]{1,0:T(8,128)(2,1)S(1)} collective-permute-done((bf16[256,512]{1,0:T(8,128)(2,1)S(1)}, bf16[256,512]{1,0:T(8,128)(2,1)S(1)}, u32[]{:S(2)}, u32[]{:S(2)}) %collective-permute-start.26) | collective-permute-done | bytes 262176 | tf_op jit(solution)/shard_map/ppermute | solution.py:573
  542.9 4.4 collective-permute-done.27
  552.5 33.4 %query_grad.1 = bf16[4,256,512]{2,1,0:T(8,128)(2,1)} custom-call(s32[4,16]{1,0:T(4,128)} %copy.44.place_ref, s32[4,2]{1,0:T(4,128)} %get-tuple-element.227.own_ref, bf16[4,256,512]{2,1,0:T(8,128)(2,1)} %copy-done.2, bf16[4,256,512]{2,1,0:T(8,128)(2,1)} %bitcast.77, bf16[4,256,128]{2,1,0:T(8,128)(2,1)} %get-tuple-element.123.qx_ref, ...), custom_call_target="tpu_custom_call" | custom-call | flops 1610612736 | bytes 4194304 | tf_op jit(solution)/shard_map/query_grad/pallas_call | solution.py:233
  585.9 20.4 %collective-permute-done.32.refs_12_ = bf16[1,4,2,128,640]{4,3,2,1,0:T(8,128)(2,1)} collective-permute-done((bf16[1,4,2,128,640]{4,3,2,1,0:T(8,128)(2,1)S(1)}, bf16[1,4,2,128,640]{4,3,2,1,0:T(8,128)(2,1)}, u32[]{:S(2)}, u32[]{:S(2)}) %collective-permute-start.32) | collective-permute-done | bytes 1310752 | tf_op jit(solution)/shard_map/ppermute | solution.py:413
  614.4 22.6 %key_value_grad.2 = (bf16[2,256,512]{2,1,0:T(8,128)(2,1)}, bf16[2,256,512]{2,1,0:T(8,128)(2,1)}) custom-call(s32[4,16]{1,0:T(4,128)} %copy.44.place_ref, s32[4,2]{1,0:T(4,128)} %get-tuple-element.227.own_ref, bf16[2,4,256,512]{3,2,1,0:T(8,128)(2,1)} %get-tuple-element.117.kv_ref, f32[1024,128]{1,0:T(8,128)} %copy-done.6, f32[1024,128]{1,0:T(8,128)} %copy-done.5, ...), custom_call_target="tpu_custom_call" | custom-call | flops 1073741824 | bytes 2097152 | tf_op jit(solution)/shard_map/key_value_grad/pallas_call | solution.py:233
  637.0 7.6 collective-permute-done.39
  654.2 2.8 maximum_select_fusion.4
  657.5 22.5 %key_value_grad.3 = (bf16[2,256,512]{2,1,0:T(8,128)(2,1)}, bf16[2,256,512]{2,1,0:T(8,128)(2,1)}) custom-call(s32[4,16]{1,0:T(4,128)} %copy.44.place_ref, s32[4,2]{1,0:T(4,128)} %get-tuple-element.227.own_ref, bf16[2,4,256,512]{3,2,1,0:T(8,128)(2,1)} %get-tuple-element.117.kv_ref, f32[1024,128]{1,0:T(8,128)} %copy-done.6, f32[1024,128]{1,0:T(8,128)} %copy-done.5, ...), custom_call_target="tpu_custom_call" | custom-call | flops 1073741824 | bytes 2097152 | tf_op jit(solution)/shard_map/key_value_grad/pallas_call | solution.py:233
  685.0 5.8 fusion.86
  690.8 10.8 %fusion.85 = (bf16[1024,2048]{1,0:T(8,128)(2,1)}, f32[1024,2048]{1,0:T(8,128)}) fusion(f32[1024,2048]{1,0:T(8,128)S(1)} %fusion.87, f32[1024,2048]{1,0:T(8,128)} %fusion.86, bf16[1024,512]{1,0:T(8,128)(2,1)S(1)} %bitcast.75, bf16[2048,512]{1,0:T(8,128)(2,1)S(1)} %copy-done.44), kind=kOutput, calls=%fused_computation.216 | convolution fusion | flops 2153775104 | bytes 32505856 | tf_op jit(solution)/shard_map/dot_general | solution.py:15
  701.6 3.3 fusion.47
  708.3 4.1 convolution_convert_fusion.2
  712.4 2.7 pad_maximum_fusion.1
  715.6 3.0 fusion.29
  718.7 5.1 fusion.31
  723.8 3.1 fusion
  729.5 3.2 maximum_select_fusion
  734.8 2.8 pad_maximum_fusion.half_ref
  744.5 10.4 %collective-permute-done.47 = bf16[256,2048]{1,0:T(8,128)(2,1)} collective-permute-done((bf16[256,2048]{1,0:T(8,128)(2,1)}, bf16[256,2048]{1,0:T(8,128)(2,1)}, u32[]{:S(2)}, u32[]{:S(2)}) %collective-permute-start.47) | collective-permute-done | bytes 1048608 | tf_op jit(solution)/shard_map/ppermute | solution.py:413
  756.6 3.0 collective-permute-start.48
  759.6 4.8 collective-permute-done.49
  764.8 7.3 collective-permute-done.61
  776.9 6.4 collective-permute-done.48
  789.0 9.8 %collective-permute-done.64 = bf16[352,1024]{1,0:T(8,128)(2,1)S(1)} collective-permute-done((bf16[352,1024]{1,0:T(8,128)(2,1)S(1)}, bf16[352,1024]{1,0:T(8,128)(2,1)S(1)}, u32[]{:S(2)}, u32[]{:S(2)}) %collective-permute-start.64) | collective-permute-done | bytes 720928 | tf_op jit(solution)/shard_map/ppermute | solution.py:413
  798.8 3.7 collective-permute-done.63
  808.5 13.7 %unpack_rows.2 = (f32[2048,1408]{1,0:T(8,128)}, f32[2048,1408]{1,0:T(8,128)}) custom-call(s32[1]{0:T(128)} %bitcast.19.core_ref, bf16[1024,2816]{1,0:T(8,128)(2,1)} %pad_maximum_fusion.half_ref, bf16[1024,2816]{1,0:T(8,128)(2,1)} %collective-permute-done.53.other_ref), custom_call_target="tpu_custom_call" | custom-call | bytes 34603008 | tf_op jit(solution)/shard_map/unpack_rows/pallas_call | solution.py:527
  829.7 3.3 collective-permute-start.55
  835.5 3.8 collective-permute-start.56
  839.3 8.8 unpack_cols.1
  850.5 3.3 maximum_select_fusion.2
  853.8 3.5 maximum_select_fusion.3
  857.3 2.6 pad_maximum_fusion.2.half_ref
  860.0 2.6 add_convert_fusion.5
  866.4 2.6 collective-permute-done.57
  869.4 3.1 fusion.18
  877.2 11.4 %unpack_rows.3 = (f32[2048,512]{1,0:T(8,128)}, f32[2048,512]{1,0:T(8,128)}, f32[2048,512]{1,0:T(8,128)}, f32[512,2048]{1,0:T(8,128)}) custom-call(s32[1]{0:T(128)} %bitcast.19.core_ref, bf16[1024,2048]{1,0:T(8,128)(2,1)} %pad_maximum_fusion.2.half_ref, bf16[1024,2048]{1,0:T(8,128)(2,1)} %collective-permute-done.66.other_ref), custom_call_target="tpu_custom_call" | custom-call | bytes 25165824 | tf_op jit(solution)/shard_map/unpack_rows/pallas_call | solution.py:527
  (422 shorter events, 156.7 us)
Async XLA Ops:
  7.2 89.0 %all-gather.7.cloned.1.call-start = ((), (), s32[]{:S(2)}) async-start(), calls=%async_computation.3 | async-start | bytes 5242880 | tf_op jit(solution)/shard_map/all_gather | solution.py:568
  12.6 197.1 %all-gather.9.cloned.1.call-start = ((), (), s32[]{:S(2)}) async-start(), calls=%async_computation.4 | async-start | bytes 5242880 | tf_op jit(solution)/shard_map/all_gather | solution.py:568
  96.3 167.4 %all-gather.15.cloned.1.call-start = ((), (), s32[]{:S(2)}) async-start(), calls=%async_computation.10 | async-start | bytes 9437184 | tf_op jit(solution)/shard_map/all_gather | solution.py:682
  112.0 47.7 %collective-permute-start.3 = (bf16[2,4,2,128,512]{4,3,2,1,0:T(8,128)(2,1)}, bf16[2,4,2,128,512]{4,3,2,1,0:T(8,128)(2,1)}, u32[]{:S(2)}, u32[]{:S(2)}) collective-permute-start(bf16[2,4,2,128,512]{4,3,2,1,0:T(8,128)(2,1)} %bitcast.5.refs_0_.refs_8_), channel_id=1, source_target_pairs={{0,16},{4,20},{8,24},{12,28},{16,0},{20,4},{24,8},{28,12},{1,17},{... | collective-permute-start | bytes 6291464 | tf_op jit(solution)/shard_map/ppermute | solution.py:413
  113.4 49.9 %collective-permute-start.1 = (bf16[2,4,2,128,512]{4,3,2,1,0:T(8,128)(2,1)}, bf16[2,4,2,128,512]{4,3,2,1,0:T(8,128)(2,1)}, u32[]{:S(2)}, u32[]{:S(2)}) collective-permute-start(bf16[2,4,2,128,512]{4,3,2,1,0:T(8,128)(2,1)} %bitcast.5.refs_0_.refs_8_), channel_id=1, source_target_pairs={{0,8},{4,12},{8,0},{12,4},{16,24},{20,28},{24,16},{28,20},{1,9},{5... | collective-permute-start | bytes 6291464 | tf_op jit(solution)/shard_map/ppermute | solution.py:413
  161.9 40.6 %collective-permute-start.7 = (bf16[1,4,2,128,512]{4,3,2,1,0:T(8,128)(2,1)}, bf16[1,4,2,128,512]{4,3,2,1,0:T(8,128)(2,1)S(1)}, u32[]{:S(2)}, u32[]{:S(2)}) collective-permute-start(bf16[1,4,2,128,512]{4,3,2,1,0:T(8,128)(2,1)} %slice.96), channel_id=1, source_target_pairs={{0,8},{4,12},{8,0},{12,4},{16,24},{20,28},{24,16},{28,20},{1,9},{5... | collective-permute-start | bytes 3145736 | tf_op jit(solution)/shard_map/ppermute | solution.py:413
  165.6 37.4 %collective-permute-start.5 = (bf16[1,4,2,128,512]{4,3,2,1,0:T(8,128)(2,1)}, bf16[1,4,2,128,512]{4,3,2,1,0:T(8,128)(2,1)}, u32[]{:S(2)}, u32[]{:S(2)}) collective-permute-start(bf16[1,4,2,128,512]{4,3,2,1,0:T(8,128)(2,1)} %slice.95), channel_id=1, source_target_pairs={{0,16},{4,20},{8,24},{12,28},{16,0},{20,4},{24,8},{28,12},{1,17},{... | collective-permute-start | bytes 3145736 | tf_op jit(solution)/shard_map/ppermute | solution.py:413
  167.1 12.3 %collective-permute-start.14 = (bf16[64,2048]{1,0:T(8,128)(2,1)S(1)}, bf16[64,2048]{1,0:T(8,128)(2,1)S(1)}, u32[]{:S(2)}, u32[]{:S(2)}) collective-permute-start(bf16[64,2048]{1,0:T(8,128)(2,1)S(1)} %constant_dynamic-slice_fusion.15), channel_id=1, source_target_pairs={{0,3},{1,0},{2,1},{3,2},{4,7},{5,4},{6,5},{7,6},{8,11},{9,8},{10,9... | collective-permute-start | bytes 786440 | tf_op jit(solution)/shard_map/ppermute | solution.py:651
  168.2 31.0 %collective-permute-start.13 = (bf16[64,2048]{1,0:T(8,128)(2,1)S(1)}, bf16[64,2048]{1,0:T(8,128)(2,1)S(1)}, u32[]{:S(2)}, u32[]{:S(2)}) collective-permute-start(bf16[64,2048]{1,0:T(8,128)(2,1)S(1)} %constant_dynamic-slice_fusion.15), channel_id=1, source_target_pairs={{0,2},{1,3},{2,0},{3,1},{4,6},{5,7},{6,4},{7,5},{8,10},{9,11},{10,... | collective-permute-start | bytes 786440 | tf_op jit(solution)/shard_map/ppermute | solution.py:651
  168.2 31.0 %collective-permute-start.12 = (bf16[64,2048]{1,0:T(8,128)(2,1)S(1)}, bf16[64,2048]{1,0:T(8,128)(2,1)S(1)}, u32[]{:S(2)}, u32[]{:S(2)}) collective-permute-start(bf16[64,2048]{1,0:T(8,128)(2,1)S(1)} %constant_dynamic-slice_fusion.15), channel_id=1, source_target_pairs={{0,1},{1,2},{2,3},{3,0},{4,5},{5,6},{6,7},{7,4},{8,9},{9,10},{10,1... | collective-permute-start | bytes 786440 | tf_op jit(solution)/shard_map/ppermute | solution.py:651
  179.5 26.7 %collective-permute-start = (bf16[2,4,2,128,512]{4,3,2,1,0:T(8,128)(2,1)}, bf16[2,4,2,128,512]{4,3,2,1,0:T(8,128)(2,1)S(1)}, u32[]{:S(2)}, u32[]{:S(2)}) collective-permute-start(bf16[2,4,2,128,512]{4,3,2,1,0:T(8,128)(2,1)} %bitcast.5.refs_0_.refs_8_), channel_id=1, source_target_pairs={{0,4},{4,0},{8,12},{12,8},{16,20},{20,16},{24,28},{28,24},{1,5},{5... | collective-permute-start | bytes 6291464 | tf_op jit(solution)/shard_map/ppermute | solution.py:413
  199.2 10.5 %collective-permute-start.4 = (bf16[2,4,2,128,512]{4,3,2,1,0:T(8,128)(2,1)}, bf16[2,4,2,128,512]{4,3,2,1,0:T(8,128)(2,1)}, u32[]{:S(2)}, u32[]{:S(2)}) collective-permute-start(bf16[2,4,2,128,512]{4,3,2,1,0:T(8,128)(2,1)} %collective-permute-done.3.refs_4_.refs_12_), channel_id=1, source_target_pairs={{0,4},{4,0},{8,12},{12,8},{16,20},{20,16},{24,28},{28,24},{1,5},{5... | collective-permute-start | bytes 6291464 | tf_op jit(solution)/shard_map/ppermute | solution.py:413
  200.6 9.1 %collective-permute-start.2 = (bf16[2,4,2,128,512]{4,3,2,1,0:T(8,128)(2,1)}, bf16[2,4,2,128,512]{4,3,2,1,0:T(8,128)(2,1)}, u32[]{:S(2)}, u32[]{:S(2)}) collective-permute-start(bf16[2,4,2,128,512]{4,3,2,1,0:T(8,128)(2,1)} %collective-permute-done.1.refs_2_.refs_10_), channel_id=1, source_target_pairs={{0,4},{4,0},{8,12},{12,8},{16,20},{20,16},{24,28},{28,24},{1,5},{5... | collective-permute-start | bytes 6291464 | tf_op jit(solution)/shard_map/ppermute | solution.py:413
  209.8 147.3 %all-gather.11.cloned.1.call-start = ((), (), s32[]{:S(2)}) async-start(), calls=%async_computation.5 | async-start | bytes 5242880 | tf_op jit(solution)/shard_map/all_gather | solution.py:568
  242.2 11.3 %collective-permute-start.9 = (bf16[256,512]{1,0:T(8,128)(2,1)}, bf16[256,512]{1,0:T(8,128)(2,1)S(1)}, u32[]{:S(2)}, u32[]{:S(2)}) collective-permute-start(bf16[256,512]{1,0:T(8,128)(2,1)} %get-tuple-element.240), channel_id=1, source_target_pairs={{0,1},{1,2},{2,3},{3,0},{4,5},{5,6},{6,7},{7,4},{8,9},{9,10},{10,1... | collective-permute-start | bytes 786440 | tf_op jit(solution)/shard_map/ppermute | solution.py:573
  242.2 21.3 %collective-permute-start.10 = (bf16[256,512]{1,0:T(8,128)(2,1)S(1)}, bf16[256,512]{1,0:T(8,128)(2,1)S(1)}, u32[]{:S(2)}, u32[]{:S(2)}) collective-permute-start(bf16[256,512]{1,0:T(8,128)(2,1)S(1)} %get-tuple-element.239), channel_id=1, source_target_pairs={{0,2},{1,3},{2,0},{3,1},{4,6},{5,7},{6,4},{7,5},{8,10},{9,11},{10,... | collective-permute-start | bytes 786440 | tf_op jit(solution)/shard_map/ppermute | solution.py:573
  242.2 21.4 %collective-permute-start.11 = (bf16[256,512]{1,0:T(8,128)(2,1)S(1)}, bf16[256,512]{1,0:T(8,128)(2,1)S(1)}, u32[]{:S(2)}, u32[]{:S(2)}) collective-permute-start(bf16[256,512]{1,0:T(8,128)(2,1)S(1)} %get-tuple-element.238), channel_id=1, source_target_pairs={{0,3},{1,0},{2,1},{3,2},{4,7},{5,4},{6,5},{7,6},{8,11},{9,8},{10,9... | collective-permute-start | bytes 786440 | tf_op jit(solution)/shard_map/ppermute | solution.py:573
  273.0 236.1 %reduce-scatter.4.cloned.1.call-start = ((), (), s32[]{:S(2)}) async-start(), calls=%async_computation.6 | async-start | bytes 5242880 | tf_op jit(solution)/shard_map/reduce_scatter | solution.py:596
  274.3 32.9 %collective-permute-start.20 = (bf16[1,4,2,128,640]{4,3,2,1,0:T(8,128)(2,1)}, bf16[1,4,2,128,640]{4,3,2,1,0:T(8,128)(2,1)}, u32[]{:S(2)}, u32[]{:S(2)}) collective-permute-start(bf16[1,4,2,128,640]{4,3,2,1,0:T(8,128)(2,1)} %bitcast.12.refs_0_), channel_id=1, source_target_pairs={{0,24},{4,28},{8,16},{12,20},{16,8},{20,12},{24,0},{28,4},{1,25},{... | collective-permute-start | bytes 3932168 | tf_op jit(solution)/shard_map/ppermute | solution.py:413
  276.1 58.2 %collective-permute-start.18 = (bf16[1,4,2,128,640]{4,3,2,1,0:T(8,128)(2,1)}, bf16[1,4,2,128,640]{4,3,2,1,0:T(8,128)(2,1)}, u32[]{:S(2)}, u32[]{:S(2)}) collective-permute-start(bf16[1,4,2,128,640]{4,3,2,1,0:T(8,128)(2,1)} %bitcast.12.refs_0_), channel_id=1, source_target_pairs={{0,16},{4,20},{8,24},{12,28},{16,0},{20,4},{24,8},{28,12},{1,17},{... | collective-permute-start | bytes 3932168 | tf_op jit(solution)/shard_map/ppermute | solution.py:413
  277.2 57.2 %collective-permute-start.16 = (bf16[1,4,2,128,640]{4,3,2,1,0:T(8,128)(2,1)}, bf16[1,4,2,128,640]{4,3,2,1,0:T(8,128)(2,1)}, u32[]{:S(2)}, u32[]{:S(2)}) collective-permute-start(bf16[1,4,2,128,640]{4,3,2,1,0:T(8,128)(2,1)} %bitcast.12.refs_0_), channel_id=1, source_target_pairs={{0,8},{4,12},{8,0},{12,4},{16,24},{20,28},{24,16},{28,20},{1,9},{5... | collective-permute-start | bytes 3932168 | tf_op jit(solution)/shard_map/ppermute | solution.py:413
  277.8 57.1 %collective-permute-start.15 = (bf16[1,4,2,128,640]{4,3,2,1,0:T(8,128)(2,1)}, bf16[1,4,2,128,640]{4,3,2,1,0:T(8,128)(2,1)}, u32[]{:S(2)}, u32[]{:S(2)}) collective-permute-start(bf16[1,4,2,128,640]{4,3,2,1,0:T(8,128)(2,1)} %bitcast.12.refs_0_), channel_id=1, source_target_pairs={{0,4},{4,0},{8,12},{12,8},{16,20},{20,16},{24,28},{28,24},{1,5},{5... | collective-permute-start | bytes 3932168 | tf_op jit(solution)/shard_map/ppermute | solution.py:413
  307.2 27.7 %collective-permute-start.21 = (bf16[1,4,2,128,640]{4,3,2,1,0:T(8,128)(2,1)}, bf16[1,4,2,128,640]{4,3,2,1,0:T(8,128)(2,1)}, u32[]{:S(2)}, u32[]{:S(2)}) collective-permute-start(bf16[1,4,2,128,640]{4,3,2,1,0:T(8,128)(2,1)} %collective-permute-done.20.refs_6_), channel_id=1, source_target_pairs={{0,4},{4,0},{8,12},{12,8},{16,20},{20,16},{24,28},{28,24},{1,5},{5... | collective-permute-start | bytes 3932168 | tf_op jit(solution)/shard_map/ppermute | solution.py:413
  428.6 22.5 %collective-permute-start.22 = (bf16[1024,2816]{1,0:T(8,128)(2,1)}, bf16[1024,2816]{1,0:T(8,128)(2,1)}, u32[]{:S(2)}, u32[]{:S(2)}) collective-permute-start(bf16[1024,2816]{1,0:T(8,128)(2,1)} %convolution_convert_fusion), channel_id=1, source_target_pairs={{0,4},{4,0},{8,12},{12,8},{16,20},{20,16},{24,28},{28,24},{1,5},{5... | collective-permute-start | bytes 17301512 | tf_op jit(solution)/shard_map/ppermute | solution.py:413
  433.2 9.3 %collective-permute-start.23 = (bf16[1408,1024]{1,0:T(8,128)(2,1)}, bf16[1408,1024]{1,0:T(8,128)(2,1)}, u32[]{:S(2)}, u32[]{:S(2)}) collective-permute-start(bf16[1408,1024]{1,0:T(8,128)(2,1)} %convolution_convert_fusion.3), channel_id=1, source_target_pairs={{0,4},{4,0},{8,12},{12,8},{16,20},{20,16},{24,28},{28,24},{1,5},{5... | collective-permute-start | bytes 8650760 | tf_op jit(solution)/shard_map/ppermute | solution.py:413
  433.7 267.9 %all-gather.13.cloned.1.call-start = ((), (), s32[]{:S(2)}) async-start(), calls=%async_computation.8 | async-start | bytes 5242880 | tf_op jit(solution)/shard_map/all_gather | solution.py:568
  463.8 33.9 %collective-permute-start.24 = (bf16[256,2816]{1,0:T(8,128)(2,1)}, bf16[256,2816]{1,0:T(8,128)(2,1)}, u32[]{:S(2)}, u32[]{:S(2)}) collective-permute-start(bf16[256,2816]{1,0:T(8,128)(2,1)} %constant_dynamic-slice_fusion.14), channel_id=1, source_target_pairs={{0,8},{4,12},{8,0},{12,4},{16,24},{20,28},{24,16},{28,20},{1,9},{5... | collective-permute-start | bytes 4325384 | tf_op jit(solution)/shard_map/ppermute | solution.py:413
  466.5 33.7 %collective-permute-start.25 = (bf16[256,2816]{1,0:T(8,128)(2,1)}, bf16[256,2816]{1,0:T(8,128)(2,1)}, u32[]{:S(2)}, u32[]{:S(2)}) collective-permute-start(bf16[256,2816]{1,0:T(8,128)(2,1)} %constant_dynamic-slice_fusion.13), channel_id=1, source_target_pairs={{0,16},{4,20},{8,24},{12,28},{16,0},{20,4},{24,8},{28,12},{1,17},{... | collective-permute-start | bytes 4325384 | tf_op jit(solution)/shard_map/ppermute | solution.py:413
  503.2 17.3 %collective-permute-start.29 = (bf16[128,2816]{1,0:T(8,128)(2,1)}, bf16[128,2816]{1,0:T(8,128)(2,1)}, u32[]{:S(2)}, u32[]{:S(2)}) collective-permute-start(bf16[128,2816]{1,0:T(8,128)(2,1)} %constant_dynamic-slice_fusion.9), channel_id=1, source_target_pairs={{0,16},{4,20},{8,24},{12,28},{16,0},{20,4},{24,8},{28,12},{1,17},{... | collective-permute-start | bytes 2162696 | tf_op jit(solution)/shard_map/ppermute | solution.py:413
  507.8 17.1 %collective-permute-start.30 = (bf16[128,2816]{1,0:T(8,128)(2,1)}, bf16[128,2816]{1,0:T(8,128)(2,1)}, u32[]{:S(2)}, u32[]{:S(2)}) collective-permute-start(bf16[128,2816]{1,0:T(8,128)(2,1)} %constant_dynamic-slice_fusion.8), channel_id=1, source_target_pairs={{0,8},{4,12},{8,0},{12,4},{16,24},{20,28},{24,16},{28,20},{1,9},{5... | collective-permute-start | bytes 2162696 | tf_op jit(solution)/shard_map/ppermute | solution.py:413
  525.1 22.2 %collective-permute-start.28 = (bf16[256,512]{1,0:T(8,128)(2,1)S(1)}, bf16[256,512]{1,0:T(8,128)(2,1)S(1)}, u32[]{:S(2)}, u32[]{:S(2)}) collective-permute-start(bf16[256,512]{1,0:T(8,128)(2,1)S(1)} %get-tuple-element.234), channel_id=1, source_target_pairs={{0,3},{1,0},{2,1},{3,2},{4,7},{5,4},{6,5},{7,6},{8,11},{9,8},{10,9... | collective-permute-start | bytes 786440 | tf_op jit(solution)/shard_map/ppermute | solution.py:573
  526.0 21.2 %collective-permute-start.27 = (bf16[256,512]{1,0:T(8,128)(2,1)S(1)}, bf16[256,512]{1,0:T(8,128)(2,1)S(1)}, u32[]{:S(2)}, u32[]{:S(2)}) collective-permute-start(bf16[256,512]{1,0:T(8,128)(2,1)S(1)} %get-tuple-element.235), channel_id=1, source_target_pairs={{0,2},{1,3},{2,0},{3,1},{4,6},{5,7},{6,4},{7,5},{8,10},{9,11},{10,... | collective-permute-start | bytes 786440 | tf_op jit(solution)/shard_map/ppermute | solution.py:573
  526.2 16.6 %collective-permute-start.26 = (bf16[256,512]{1,0:T(8,128)(2,1)S(1)}, bf16[256,512]{1,0:T(8,128)(2,1)S(1)}, u32[]{:S(2)}, u32[]{:S(2)}) collective-permute-start(bf16[256,512]{1,0:T(8,128)(2,1)S(1)} %get-tuple-element.236), channel_id=1, source_target_pairs={{0,1},{1,2},{2,3},{3,0},{4,5},{5,6},{6,7},{7,4},{8,9},{9,10},{10,1... | collective-permute-start | bytes 786440 | tf_op jit(solution)/shard_map/ppermute | solution.py:573
  548.9 311.1 %reduce-scatter.6.cloned.1.call-start = ((), (), s32[]{:S(2)}) async-start(), calls=%async_computation.7 | async-start | bytes 5242880 | tf_op jit(solution)/shard_map/reduce_scatter | solution.py:596
  548.9 37.0 %collective-permute-start.33 = (bf16[1,4,2,128,640]{4,3,2,1,0:T(8,128)(2,1)S(1)}, bf16[1,4,2,128,640]{4,3,2,1,0:T(8,128)(2,1)}, u32[]{:S(2)}, u32[]{:S(2)}) collective-permute-start(bf16[1,4,2,128,640]{4,3,2,1,0:T(8,128)(2,1)S(1)} %bitcast.69), channel_id=1, source_target_pairs={{0,24},{4,28},{8,16},{12,20},{16,8},{20,12},{24,0},{28,4},{1,25},{... | collective-permute-start | bytes 3932168 | tf_op jit(solution)/shard_map/ppermute | solution.py:413
  550.8 55.6 %collective-permute-start.32 = (bf16[1,4,2,128,640]{4,3,2,1,0:T(8,128)(2,1)S(1)}, bf16[1,4,2,128,640]{4,3,2,1,0:T(8,128)(2,1)}, u32[]{:S(2)}, u32[]{:S(2)}) collective-permute-start(bf16[1,4,2,128,640]{4,3,2,1,0:T(8,128)(2,1)S(1)} %bitcast.70), channel_id=1, source_target_pairs={{0,16},{4,20},{8,24},{12,28},{16,0},{20,4},{24,8},{28,12},{1,17},{... | collective-permute-start | bytes 3932168 | tf_op jit(solution)/shard_map/ppermute | solution.py:413
  551.3 55.0 %collective-permute-start.31 = (bf16[1,4,2,128,640]{4,3,2,1,0:T(8,128)(2,1)S(1)}, bf16[1,4,2,128,640]{4,3,2,1,0:T(8,128)(2,1)}, u32[]{:S(2)}, u32[]{:S(2)}) collective-permute-start(bf16[1,4,2,128,640]{4,3,2,1,0:T(8,128)(2,1)S(1)} %bitcast.71), channel_id=1, source_target_pairs={{0,8},{4,12},{8,0},{12,4},{16,24},{20,28},{24,16},{28,20},{1,9},{5... | collective-permute-start | bytes 3932168 | tf_op jit(solution)/shard_map/ppermute | solution.py:413
  552.5 58.1 %collective-permute-start.34 = (bf16[1,4,2,128,640]{4,3,2,1,0:T(8,128)(2,1)S(1)}, bf16[1,4,2,128,640]{4,3,2,1,0:T(8,128)(2,1)}, u32[]{:S(2)}, u32[]{:S(2)}) collective-permute-start(bf16[1,4,2,128,640]{4,3,2,1,0:T(8,128)(2,1)S(1)} %bitcast.72), channel_id=1, source_target_pairs={{0,4},{4,0},{8,12},{12,8},{16,20},{20,16},{24,28},{28,24},{1,5},{5... | collective-permute-start | bytes 3932168 | tf_op jit(solution)/shard_map/ppermute | solution.py:413
  607.8 29.2 %collective-permute-start.41 = (bf16[352,1024]{1,0:T(8,128)(2,1)}, bf16[352,1024]{1,0:T(8,128)(2,1)}, u32[]{:S(2)}, u32[]{:S(2)}) collective-permute-start(bf16[352,1024]{1,0:T(8,128)(2,1)} %constant_dynamic-slice_fusion.6), channel_id=1, source_target_pairs={{0,16},{4,20},{8,24},{12,28},{16,0},{20,4},{24,8},{28,12},{1,17},{... | collective-permute-start | bytes 2162696 | tf_op jit(solution)/shard_map/ppermute | solution.py:413
  610.6 26.4 %collective-permute-start.40 = (bf16[352,1024]{1,0:T(8,128)(2,1)}, bf16[352,1024]{1,0:T(8,128)(2,1)}, u32[]{:S(2)}, u32[]{:S(2)}) collective-permute-start(bf16[352,1024]{1,0:T(8,128)(2,1)} %constant_dynamic-slice_fusion.7), channel_id=1, source_target_pairs={{0,8},{4,12},{8,0},{12,4},{16,24},{20,28},{24,16},{28,20},{1,9},{5... | collective-permute-start | bytes 2162696 | tf_op jit(solution)/shard_map/ppermute | solution.py:413
  612.2 32.5 %collective-permute-start.39 = (bf16[128,2816]{1,0:T(8,128)(2,1)}, bf16[128,2816]{1,0:T(8,128)(2,1)}, u32[]{:S(2)}, u32[]{:S(2)}) collective-permute-start(bf16[128,2816]{1,0:T(8,128)(2,1)} %add_convert_fusion.11), channel_id=1, source_target_pairs={{0,8},{4,12},{8,0},{12,4},{16,24},{20,28},{24,16},{28,20},{1,9},{5... | collective-permute-start | bytes 2162696 | tf_op jit(solution)/shard_map/ppermute | solution.py:413
  612.6 32.0 %collective-permute-start.38 = (bf16[128,2816]{1,0:T(8,128)(2,1)S(1)}, bf16[128,2816]{1,0:T(8,128)(2,1)}, u32[]{:S(2)}, u32[]{:S(2)}) collective-permute-start(bf16[128,2816]{1,0:T(8,128)(2,1)S(1)} %add_convert_fusion.12), channel_id=1, source_target_pairs={{0,16},{4,20},{8,24},{12,28},{16,0},{20,4},{24,8},{28,12},{1,17},{... | collective-permute-start | bytes 2162696 | tf_op jit(solution)/shard_map/ppermute | solution.py:413
  613.9 248.6 %reduce-scatter.8.cloned.1.call-start = ((), (), s32[]{:S(2)}) async-start(), calls=%async_computation.9 | async-start | bytes 5242880 | tf_op jit(solution)/shard_map/reduce_scatter | solution.py:596
  646.1 34.0 %collective-permute-start.42 = (bf16[176,1024]{1,0:T(8,128)(2,1)S(1)}, bf16[176,1024]{1,0:T(8,128)(2,1)}, u32[]{:S(2)}, u32[]{:S(2)}) collective-permute-start(bf16[176,1024]{1,0:T(8,128)(2,1)S(1)} %constant_dynamic-slice_fusion.5), channel_id=1, source_target_pairs={{0,16},{4,20},{8,24},{12,28},{16,0},{20,4},{24,8},{28,12},{1,17},{... | collective-permute-start | bytes 1081352 | tf_op jit(solution)/shard_map/ppermute | solution.py:413
  649.6 30.4 %collective-permute-start.43 = (bf16[176,1024]{1,0:T(8,128)(2,1)S(1)}, bf16[176,1024]{1,0:T(8,128)(2,1)S(1)}, u32[]{:S(2)}, u32[]{:S(2)}) collective-permute-start(bf16[176,1024]{1,0:T(8,128)(2,1)S(1)} %constant_dynamic-slice_fusion.4), channel_id=1, source_target_pairs={{0,8},{4,12},{8,0},{12,4},{16,24},{20,28},{24,16},{28,20},{1,9},{5... | collective-permute-start | bytes 1081352 | tf_op jit(solution)/shard_map/ppermute | solution.py:413
  653.6 48.0 %collective-permute-start.45 = (bf16[256,2816]{1,0:T(8,128)(2,1)S(1)}, bf16[256,2816]{1,0:T(8,128)(2,1)}, u32[]{:S(2)}, u32[]{:S(2)}) collective-permute-start(bf16[256,2816]{1,0:T(8,128)(2,1)S(1)} %maximum_select_fusion.5), channel_id=1, source_target_pairs={{0,16},{4,20},{8,24},{12,28},{16,0},{20,4},{24,8},{28,12},{1,17},{... | collective-permute-start | bytes 4325384 | tf_op jit(solution)/shard_map/ppermute | solution.py:413
  657.1 44.5 %collective-permute-start.44 = (bf16[256,2816]{1,0:T(8,128)(2,1)}, bf16[256,2816]{1,0:T(8,128)(2,1)}, u32[]{:S(2)}, u32[]{:S(2)}) collective-permute-start(bf16[256,2816]{1,0:T(8,128)(2,1)} %maximum_select_fusion.4), channel_id=1, source_target_pairs={{0,8},{4,12},{8,0},{12,4},{16,24},{20,28},{24,16},{28,20},{1,9},{5... | collective-permute-start | bytes 4325384 | tf_op jit(solution)/shard_map/ppermute | solution.py:413
  715.0 8.8 collective-permute-start.46
  728.6 26.3 %collective-permute-start.47 = (bf16[256,2048]{1,0:T(8,128)(2,1)}, bf16[256,2048]{1,0:T(8,128)(2,1)}, u32[]{:S(2)}, u32[]{:S(2)}) collective-permute-start(bf16[256,2048]{1,0:T(8,128)(2,1)} %constant_dynamic-slice_fusion.3), channel_id=1, source_target_pairs={{0,8},{4,12},{8,0},{12,4},{16,24},{20,28},{24,16},{28,20},{1,9},{5... | collective-permute-start | bytes 3145736 | tf_op jit(solution)/shard_map/ppermute | solution.py:413
  737.6 70.9 %collective-permute-start.53 = (bf16[1024,2816]{1,0:T(8,128)(2,1)}, bf16[1024,2816]{1,0:T(8,128)(2,1)}, u32[]{:S(2)}, u32[]{:S(2)}) collective-permute-start(bf16[1024,2816]{1,0:T(8,128)(2,1)} %pad_maximum_fusion.half_ref), channel_id=1, source_target_pairs={{0,4},{4,0},{8,12},{12,8},{16,20},{20,16},{24,28},{28,24},{1,5},{5... | collective-permute-start | bytes 17301512 | tf_op jit(solution)/shard_map/ppermute | solution.py:413
  738.0 26.4 %collective-permute-start.49 = (bf16[256,2048]{1,0:T(8,128)(2,1)S(1)}, bf16[256,2048]{1,0:T(8,128)(2,1)S(1)}, u32[]{:S(2)}, u32[]{:S(2)}) collective-permute-start(bf16[256,2048]{1,0:T(8,128)(2,1)S(1)} %constant_dynamic-slice_fusion.1), channel_id=1, source_target_pairs={{0,16},{4,20},{8,24},{12,28},{16,0},{20,4},{24,8},{28,12},{1,17},{... | collective-permute-start | bytes 3145736 | tf_op jit(solution)/shard_map/ppermute | solution.py:413
  740.5 24.2 %collective-permute-start.62 = (bf16[176,1024]{1,0:T(8,128)(2,1)S(1)}, bf16[176,1024]{1,0:T(8,128)(2,1)S(1)}, u32[]{:S(2)}, u32[]{:S(2)}) collective-permute-start(bf16[176,1024]{1,0:T(8,128)(2,1)S(1)} %add_convert_fusion.15), channel_id=1, source_target_pairs={{0,8},{4,12},{8,0},{12,4},{16,24},{20,28},{24,16},{28,20},{1,9},{5... | collective-permute-start | bytes 1081352 | tf_op jit(solution)/shard_map/ppermute | solution.py:413
  743.5 28.7 %collective-permute-start.61 = (bf16[176,1024]{1,0:T(8,128)(2,1)S(1)}, bf16[176,1024]{1,0:T(8,128)(2,1)S(1)}, u32[]{:S(2)}, u32[]{:S(2)}) collective-permute-start(bf16[176,1024]{1,0:T(8,128)(2,1)S(1)} %add_convert_fusion.16), channel_id=1, source_target_pairs={{0,16},{4,20},{8,24},{12,28},{16,0},{20,4},{24,8},{28,12},{1,17},{... | collective-permute-start | bytes 1081352 | tf_op jit(solution)/shard_map/ppermute | solution.py:413
  756.6 26.8 %collective-permute-start.48 = (bf16[128,2048]{1,0:T(8,128)(2,1)S(1)}, bf16[128,2048]{1,0:T(8,128)(2,1)S(1)}, u32[]{:S(2)}, u32[]{:S(2)}) collective-permute-start(bf16[128,2048]{1,0:T(8,128)(2,1)S(1)} %constant_dynamic-slice_fusion.2), channel_id=1, source_target_pairs={{0,16},{4,20},{8,24},{12,28},{16,0},{20,4},{24,8},{28,12},{1,17},{... | collective-permute-start | bytes 1572872 | tf_op jit(solution)/shard_map/ppermute | solution.py:413
  772.2 14.9 %collective-permute-start.50 = (bf16[128,2048]{1,0:T(8,128)(2,1)S(1)}, bf16[128,2048]{1,0:T(8,128)(2,1)S(1)}, u32[]{:S(2)}, u32[]{:S(2)}) collective-permute-start(bf16[128,2048]{1,0:T(8,128)(2,1)S(1)} %constant_dynamic-slice_fusion), channel_id=1, source_target_pairs={{0,8},{4,12},{8,0},{12,4},{16,24},{20,28},{24,16},{28,20},{1,9},{5... | collective-permute-start | bytes 1572872 | tf_op jit(solution)/shard_map/ppermute | solution.py:413
  774.2 24.6 %collective-permute-start.64 = (bf16[352,1024]{1,0:T(8,128)(2,1)S(1)}, bf16[352,1024]{1,0:T(8,128)(2,1)S(1)}, u32[]{:S(2)}, u32[]{:S(2)}) collective-permute-start(bf16[352,1024]{1,0:T(8,128)(2,1)S(1)} %maximum_select_fusion.11), channel_id=1, source_target_pairs={{0,16},{4,20},{8,24},{12,28},{16,0},{20,4},{24,8},{28,12},{1,17},{... | collective-permute-start | bytes 2162696 | tf_op jit(solution)/shard_map/ppermute | solution.py:413
  776.6 26.0 %collective-permute-start.63 = (bf16[352,1024]{1,0:T(8,128)(2,1)S(1)}, bf16[352,1024]{1,0:T(8,128)(2,1)S(1)}, u32[]{:S(2)}, u32[]{:S(2)}) collective-permute-start(bf16[352,1024]{1,0:T(8,128)(2,1)S(1)} %maximum_select_fusion.10), channel_id=1, source_target_pairs={{0,8},{4,12},{8,0},{12,4},{16,24},{20,28},{24,16},{28,20},{1,9},{5... | collective-permute-start | bytes 2162696 | tf_op jit(solution)/shard_map/ppermute | solution.py:413
  783.5 38.7 %collective-permute-start.51 = (bf16[128,2048]{1,0:T(8,128)(2,1)S(1)}, bf16[128,2048]{1,0:T(8,128)(2,1)S(1)}, u32[]{:S(2)}, u32[]{:S(2)}) collective-permute-start(bf16[128,2048]{1,0:T(8,128)(2,1)S(1)} %add_convert_fusion.14), channel_id=1, source_target_pairs={{0,16},{4,20},{8,24},{12,28},{16,0},{20,4},{24,8},{28,12},{1,17},{... | collective-permute-start | bytes 1572872 | tf_op jit(solution)/shard_map/ppermute | solution.py:413
  787.2 34.9 %collective-permute-start.52 = (bf16[128,2048]{1,0:T(8,128)(2,1)S(1)}, bf16[128,2048]{1,0:T(8,128)(2,1)S(1)}, u32[]{:S(2)}, u32[]{:S(2)}) collective-permute-start(bf16[128,2048]{1,0:T(8,128)(2,1)S(1)} %add_convert_fusion.13), channel_id=1, source_target_pairs={{0,8},{4,12},{8,0},{12,4},{16,24},{20,28},{24,16},{28,20},{1,9},{5... | collective-permute-start | bytes 1572872 | tf_op jit(solution)/shard_map/ppermute | solution.py:413
  804.1 35.2 %collective-permute-start.65 = (bf16[1408,1024]{1,0:T(8,128)(2,1)S(1)}, bf16[1408,1024]{1,0:T(8,128)(2,1)}, u32[]{:S(2)}, u32[]{:S(2)}) collective-permute-start(bf16[1408,1024]{1,0:T(8,128)(2,1)S(1)} %pad_maximum_fusion.3.half_ref), channel_id=1, source_target_pairs={{0,4},{4,0},{8,12},{12,8},{16,20},{20,16},{24,28},{28,24},{1,5},{5... | collective-permute-start | bytes 8650760 | tf_op jit(solution)/shard_map/ppermute | solution.py:413
  823.4 24.7 %collective-permute-start.60 = (bf16[256,2048]{1,0:T(8,128)(2,1)}, bf16[256,2048]{1,0:T(8,128)(2,1)}, u32[]{:S(2)}, u32[]{:S(2)}) collective-permute-start(bf16[256,2048]{1,0:T(8,128)(2,1)} %maximum_select_fusion.9), channel_id=1, source_target_pairs={{0,16},{4,20},{8,24},{12,28},{16,0},{20,4},{24,8},{28,12},{1,17},{... | collective-permute-start | bytes 3145736 | tf_op jit(solution)/shard_map/ppermute | solution.py:413
  826.5 24.0 %collective-permute-start.59 = (bf16[256,2048]{1,0:T(8,128)(2,1)}, bf16[256,2048]{1,0:T(8,128)(2,1)}, u32[]{:S(2)}, u32[]{:S(2)}) collective-permute-start(bf16[256,2048]{1,0:T(8,128)(2,1)} %maximum_select_fusion.8), channel_id=1, source_target_pairs={{0,8},{4,12},{8,0},{12,4},{16,24},{20,28},{24,16},{28,20},{1,9},{5... | collective-permute-start | bytes 3145736 | tf_op jit(solution)/shard_map/ppermute | solution.py:413
  835.5 12.6 %collective-permute-start.56 = (f32[14,1024]{1,0:T(8,128)S(1)}, f32[14,1024]{1,0:T(8,128)S(1)}, u32[]{:S(2)}, u32[]{:S(2)}) collective-permute-start(f32[14,1024]{1,0:T(8,128)S(1)} %add.451), channel_id=1, source_target_pairs={{0,2},{1,3},{2,0},{3,1},{4,6},{5,7},{6,4},{7,5},{8,10},{9,11},{10,... | collective-permute-start | bytes 172040 | tf_op jit(solution)/shard_map/ppermute | solution.py:641
  859.9 17.3 %collective-permute-start.66 = (bf16[1024,2048]{1,0:T(8,128)(2,1)}, bf16[1024,2048]{1,0:T(8,128)(2,1)}, u32[]{:S(2)}, u32[]{:S(2)}) collective-permute-start(bf16[1024,2048]{1,0:T(8,128)(2,1)} %pad_maximum_fusion.2.half_ref), channel_id=1, source_target_pairs={{0,4},{4,0},{8,12},{12,8},{16,20},{20,16},{24,28},{28,24},{1,5},{5... | collective-permute-start | bytes 12582920 | tf_op jit(solution)/shard_map/ppermute | solution.py:413
  (96 other events, 1485.2 us)
Sparse Core Ops, SparseCore 0:
  12.8 83.4 all-gather.6
  97.8 85.6 all-gather.8
  209.9 52.5 all-gather.14
  273.1 83.9 all-gather.10
  433.8 75.2 reduce-scatter.3
  549.0 80.3 all-gather.12
  632.4 75.2 reduce-scatter.5
  738.0 80.5 reduce-scatter.7

commit v12 on v11

--- a/solution.py
+++ b/solution.py
@@ -720,7 +720,7 @@
                             precision=lax.Precision.HIGHEST, preferred_element_type=F32)
     do_ext = terms(-delta, lane).astype(BF16)
     do_sent = jnp.concatenate([grad_attn, do_ext], axis=1).reshape(shape)
-    do_sent = after(do_sent, held)
+    do_sent = after(do_sent, held, gu_fly)
     branch = all_rows(after(branch_own, do_sent))
     out_sum = sum_rows(after(down, do_sent))
     grads = gather_other(do_sent)
@@ -728,9 +728,10 @@
     grad_q = after(grad_q.reshape(-1, width), [grads[j] for j in grads if j > 1])
     grads = gather_cores(grads, grad_q)
     q_part = nt(grad_q, query_w)
+    take(gu, grad_q)
+    go(gu, grads)
     first = key_value_grad(place, own, kv, tabs, queries, grads, 0, SEQS // 2)
-    grads = after(grads, take(gu, first), take(dw, first))
-    go(gu)
+    grads = after(grads, take(dw, first))
     go(dw)
     second = key_value_grad(place, own, kv, tabs, queries, grads, SEQS // 2, SEQS // 2)
     second = after(second, dw_fly)
@@ -747,33 +748,33 @@
     take(gu, held)
     take_extra(gu)
     go(gu)
-    take(dw, held)
-    go(dw)
     unit_rows = (rows_one.astype(F32) - shift_one) / gain_one
     bias_grad = jnp.sum(grad_qkv.astype(F32), axis=0)
     tp_row = (jnp.arange(n_tp) == lax.axis_index("tp"))[:, None]
     small = jnp.concatenate([
         jnp.sum(part_one * unit_rows, axis=0), jnp.sum(part_one, axis=0), grad_gain_two, grad_shift_two,
         jnp.where(tp_row, bias_grad[None, :], 0.0).reshape(-1)])
-    held = take(chain)
-    go(chain)
     take(dw, held)
     go(dw)
     held = take(chain)
     go(chain)
+    held = take(chain, list(dw_fly))
+    go(chain)
     take(dw, held)
     take_extra(dw)
     go(dw)
+    sums = sum_over_all(after(small, held).reshape(-1, 1024))
+    small = [next(sums) for _ in range(1 + int(math.log2(n_tp)))]
+    grad_gate_w, grad_up_w = unpack_rows(*take(gu, held), 2)
+    held = take(chain, (small, grad_gate_w, list(dw_fly)))
+    take_extra(chain)
+    go(chain)
     mixed_late, out_sum = after((mixed, out_sum), held)
     out_tokens = (mixed_late + out_sum.astype(F32)).astype(BF16)
-    grad_gate_w, grad_up_w = unpack_rows(*take(gu, held), 2)
-    held = take(chain, grad_gate_w)
-    go(chain)
-    sums = sum_over_all(after(small, held).reshape(-1, 1024))
-    small = [next(sums) for _ in range(1 + int(math.log2(n_tp)))]
-    grad_down_w = unpack_cols(*take(dw, held))
-    take(chain, (grad_down_w, small))
-    take_extra(chain)
+    take(dw, held)
+    go(dw)
+    grad_down_w = unpack_cols(*take(dw))
+    take(chain, grad_down_w)
     go(chain)
     for _ in range(4):
         small = next(sums)

time: 902 us -> 920 us (1.020)
  other arithmetic: 73.9 us -> 89.7 us
  Pallas kernels: 192 us -> 178 us
  local copies, waits for them, and re-layouts: 40.3 us -> 53.4 us
  waiting for transfers between devices: 392 us -> 402 us
    pallas_call x1, Pallas kernels: 39.5 us -> 28.8 us  [mlp(): pl.pallas_call(mlp_kernel, grid=(total // step,), in_specs=[block, block,...]
    unnamed x182 -> x208, local copies, waits for them, and re-layouts: 14.5 us -> 21.7 us
  transfers between devices with their start and end apart: 75 -> 75, of which waited for: 35 -> 35; matrix products, arithmetic and copies ran while one was open for 19% -> 20% of each run, Pallas kernels for 16% -> 15%
where the time goes in v12:
time: 920 us; the launch traced here: 917 us
  waiting for transfers between devices  402 us (44%)
  Pallas kernels  178 us (19%)
  matrix products  110 us (12%)
  other arithmetic  89.7 us (10%)
  starting transfers between devices  67.7 us (7%)
  local copies, waits for them, and re-layouts  53.4 us (6%)
  between operations  16 us (2%)
    ppermute x53, waiting for transfers between devices, ctx_swap(): return lax.ppermute(x, 'ctx', [(i, i ^ mask) for i in range(n)])  216 us
    pallas_call x4, Pallas kernels, attention_call(): pl.pallas_call(kernel, grid_spec=pltpu.PrefetchScalarGridSpec(num_scalar_...  106 us
    all_gather x4, waiting for transfers between devices, all_rows(): return lax.all_gather(x, 'tp', axis=0, tiled=True)  103 us
    ppermute x53, starting transfers between devices, ctx_swap(): return lax.ppermute(x, 'ctx', [(i, i ^ mask) for i in range(n)])  49.5 us
    dot_general x8, matrix products, rc(): lax.dot_general(left, right, (((0,), (0,)), ((), ())), preferred_element_...  48.2 us
    dot_general x6, matrix products, nt(): lax.dot_general(a, b, (((1,), (1,)), ((), ())), preferred_element_type=jn...  45.9 us
    ppermute x6, waiting for transfers between devices, tp_shift(): return lax.ppermute(x, 'tp', [(i, (i + d) % n) for i in range(n)])  35.1 us
    ppermute x3, waiting for transfers between devices, gather_tp(): lax.ppermute(x, 'tp', [(i, (i + d) % n) for i in range(n)])  29.1 us
  transfers between devices with their start and end apart: 75, of which 35 were waited for; matrix products, arithmetic and copies ran while one was open for 20% of the time, Pallas kernels for 15%

profile of v12, /device:TPU:0, one launch (start us, length us, event | category | flops | bytes accessed | tf_op | source)
XLA Modules:
  0.0 916.5 jit_solution(8831925092898820003)
XLA Ops:
  12.7 83.6 %all-gather.7.cloned.1.call-done.h_ref = bf16[1024,2048]{1,0:T(8,128)(2,1)} async-done(((bf16[256,2048]{1,0:T(8,128)(2,1)}), bf16[1024,2048]{1,0:T(8,128)(2,1)}) %all-gather.7.cloned.1.call-update) | async-done | bytes 4194320 | tf_op jit(solution)/shard_map/all_gather | solution.py:568
  99.2 11.8 %project.1 = (bf16[4,256,512]{2,1,0:T(8,128)(2,1)S(1)}, bf16[2,4,256,512]{3,2,1,0:T(8,128)(2,1)}) custom-call(bf16[1024,2048]{1,0:T(8,128)(2,1)} %all-gather.7.cloned.1.call-done.h_ref, bf16[2048,512]{1,0:T(8,128)(2,1)} %wq_ref.1, bf16[2048,512]{1,0:T(8,128)(2,1)} %wk_ref.1, bf16[2048,512]{1,0:T(8,128)(2,1)} %wv_ref.1, ...), custom_call_target="tpu_custom_call" | custom-call | flops 6442450944 | bytes 6291456 | tf_op jit(solution)/shard_map/project/pallas_call | solution.py:357
  115.0 44.7 %collective-permute-done.3.refs_4_.refs_12_ = bf16[2,4,2,128,512]{4,3,2,1,0:T(8,128)(2,1)} collective-permute-done((bf16[2,4,2,128,512]{4,3,2,1,0:T(8,128)(2,1)}, bf16[2,4,2,128,512]{4,3,2,1,0:T(8,128)(2,1)}, u32[]{:S(2)}, u32[]{:S(2)}) %collective-permute-start.3) | collective-permute-done | bytes 2097184 | tf_op jit(solution)/shard_map/ppermute | solution.py:413
  170.2 9.3 %collective-permute-done.14 = bf16[64,2048]{1,0:T(8,128)(2,1)} collective-permute-done((bf16[64,2048]{1,0:T(8,128)(2,1)S(1)}, bf16[64,2048]{1,0:T(8,128)(2,1)}, u32[]{:S(2)}, u32[]{:S(2)}) %collective-permute-start.14) | collective-permute-done | bytes 262176 | tf_op jit(solution)/shard_map/ppermute | solution.py:651
  179.5 19.8 %collective-permute-done.13 = bf16[64,2048]{1,0:T(8,128)(2,1)S(1)} collective-permute-done((bf16[64,2048]{1,0:T(8,128)(2,1)S(1)}, bf16[64,2048]{1,0:T(8,128)(2,1)S(1)}, u32[]{:S(2)}, u32[]{:S(2)}) %collective-permute-start.13) | collective-permute-done | bytes 262176 | tf_op jit(solution)/shard_map/ppermute | solution.py:651
  211.3 27.0 %attend.1 = (bf16[4,256,512]{2,1,0:T(8,128)(2,1)}, bf16[4,256,128]{2,1,0:T(8,128)(2,1)}) custom-call(s32[4,16]{1,0:T(4,128)} %copy.44.place_ref, s32[4,2]{1,0:T(4,128)} %get-tuple-element.235.own_ref, bf16[4,256,512]{2,1,0:T(8,128)(2,1)} %copy-done.2, bf16[2,4,2,128,512]{4,3,2,1,0:T(8,128)(2,1)} %bitcast.5.refs_0_.refs_8_, ...), custom_call_target="tpu_custom_call" | custom-call | flops 1073741824 | bytes 4194304 | tf_op jit(solution)/shard_map/attend/pallas_call | solution.py:233
  240.6 3.8 collective-permute-start.11
  244.4 7.5 collective-permute-done.9
  251.9 10.0 %collective-permute-done.10 = bf16[256,512]{1,0:T(8,128)(2,1)S(1)} collective-permute-done((bf16[256,512]{1,0:T(8,128)(2,1)S(1)}, bf16[256,512]{1,0:T(8,128)(2,1)S(1)}, u32[]{:S(2)}, u32[]{:S(2)}) %collective-permute-start.10) | collective-permute-done | bytes 262176 | tf_op jit(solution)/shard_map/ppermute | solution.py:573
  263.0 6.1 fusion.84
  272.6 6.7 collective-permute-start.20
  279.9 29.4 %collective-permute-done.20.refs_6_ = bf16[1,4,2,128,640]{4,3,2,1,0:T(8,128)(2,1)S(1)} collective-permute-done((bf16[1,4,2,128,640]{4,3,2,1,0:T(8,128)(2,1)}, bf16[1,4,2,128,640]{4,3,2,1,0:T(8,128)(2,1)S(1)}, u32[]{:S(2)}, u32[]{:S(2)}) %collective-permute-start.20) | collective-permute-done | bytes 1310752 | tf_op jit(solution)/shard_map/ppermute | solution.py:413
  309.3 26.0 %collective-permute-done.18.refs_4_ = bf16[1,4,2,128,640]{4,3,2,1,0:T(8,128)(2,1)} collective-permute-done((bf16[1,4,2,128,640]{4,3,2,1,0:T(8,128)(2,1)}, bf16[1,4,2,128,640]{4,3,2,1,0:T(8,128)(2,1)}, u32[]{:S(2)}, u32[]{:S(2)}) %collective-permute-start.18) | collective-permute-done | bytes 1310752 | tf_op jit(solution)/shard_map/ppermute | solution.py:413
  335.8 2.9 collective-permute-done.19.refs_5_
  340.5 19.0 %all-gather.11.cloned.1.call-done.h_ref = bf16[1024,2048]{1,0:T(8,128)(2,1)} async-done(((bf16[256,2048]{1,0:T(8,128)(2,1)}), bf16[1024,2048]{1,0:T(8,128)(2,1)}) %all-gather.11.cloned.1.call-update) | async-done | bytes 4194320 | tf_op jit(solution)/shard_map/all_gather | solution.py:568
  359.5 28.8 %mlp.1 = (bf16[1024,1408]{1,0:T(8,128)(2,1)}, bf16[1024,2816]{1,0:T(8,128)(2,1)}) custom-call(bf16[1024,2048]{1,0:T(8,128)(2,1)} %all-gather.11.cloned.1.call-done.h_ref, bf16[1024,2048]{1,0:T(8,128)(2,1)} %all-gather.9.cloned.1.call-done.dy_ref, bf16[2048,1408]{1,0:T(8,128)(2,1)} %gate_ref.1, bf16[2048,1408]{1,0:T(8,128)(2,1)} %up_ref.1, ...), custom_call_target="tpu_custom_call" | custom-call | flops 17716740096 | bytes 38273024 | tf_op jit(solution)/shard_map/mlp/pallas_call | solution.py:397
  388.4 9.8 %fusion.5 = f32[1024,2048]{1,0:T(8,128)S(1)} fusion(bf16[2048,1408]{1,0:T(8,128)(2,1)} %gate_ref.1, bf16[1024,2816]{1,0:T(8,128)(2,1)} %get-tuple-element.134), kind=kOutput, calls=%fused_computation.30 | convolution fusion | flops 5905580032 | bytes 17039360 | tf_op jit(solution)/shard_map/dot_general | solution.py:15
  398.1 11.1 %add_convert_fusion.1 = bf16[1024,2048]{1,0:T(8,128)(2,1)} fusion(f32[1024,2048]{1,0:T(8,128)S(1)} %fusion.5, bf16[2048,1408]{1,0:T(8,128)(2,1)} %up_ref.1, bf16[1024,2816]{1,0:T(8,128)(2,1)S(1)} %copy-done.91), kind=kOutput, calls=%fused_computation.5 | convolution fusion | flops 5909774336 | bytes 21233664 | tf_op jit(solution)/shard_map/dot_general | solution.py:15
  409.2 11.1 %convolution_convert_fusion = bf16[1024,2816]{1,0:T(8,128)(2,1)} fusion(bf16[1024,2816]{1,0:T(8,128)(2,1)} %get-tuple-element.134, bf16[1024,2048]{1,0:T(8,128)(2,1)} %all-gather.11.cloned.1.call-done.h_ref, s32[]{:T(128)S(6)} %select_n.384), kind=kOutput, calls=%fused_computation.9 | convolution fusion | flops 5908463616 | bytes 13631492 | tf_op jit(solution)/shard_map/dot_general | solution.py:302
  420.3 4.5 convolution_convert_fusion.3
  427.1 7.1 collective-permute-done.23
  434.2 6.6 add_convert_fusion.2
  442.8 10.7 %add_convert_fusion = bf16[1024,2816]{1,0:T(8,128)(2,1)S(1)} fusion(bf16[1024,2816]{1,0:T(8,128)(2,1)} %collective-permute-done.22, bf16[1024,2816]{1,0:T(8,128)(2,1)} %get-tuple-element.134, bf16[1024,2048]{1,0:T(8,128)(2,1)S(1)} %copy-done.85, s32[]{:T(128)S(6)} %select_n.383), kind=kOutput, calls=%fused_computation | convolution fusion | flops 5914230784 | bytes 19398660 | tf_op jit(solution)/shard_map/dot_general | solution.py:302
  459.4 8.2 convolution_convert_fusion.1
  467.6 21.5 %collective-permute-done.24 = bf16[256,2816]{1,0:T(8,128)(2,1)S(1)} collective-permute-done((bf16[256,2816]{1,0:T(8,128)(2,1)}, bf16[256,2816]{1,0:T(8,128)(2,1)S(1)}, u32[]{:S(2)}, u32[]{:S(2)}) %collective-permute-start.24) | collective-permute-done | bytes 1441824 | tf_op jit(solution)/shard_map/ppermute | solution.py:413
  502.5 3.0 fusion.24
  505.5 3.3 fusion.78
  508.8 6.2 convolution_convert_fusion.4
  526.3 13.4 %collective-permute-done.26 = bf16[256,512]{1,0:T(8,128)(2,1)S(1)} collective-permute-done((bf16[256,512]{1,0:T(8,128)(2,1)S(1)}, bf16[256,512]{1,0:T(8,128)(2,1)S(1)}, u32[]{:S(2)}, u32[]{:S(2)}) %collective-permute-start.26) | collective-permute-done | bytes 262176 | tf_op jit(solution)/shard_map/ppermute | solution.py:573
  539.7 4.3 collective-permute-done.27
  552.1 31.2 %query_grad.1 = bf16[4,256,512]{2,1,0:T(8,128)(2,1)} custom-call(s32[4,16]{1,0:T(4,128)} %copy.44.place_ref, s32[4,2]{1,0:T(4,128)} %get-tuple-element.235.own_ref, bf16[4,256,512]{2,1,0:T(8,128)(2,1)} %copy-done.2, bf16[4,256,512]{2,1,0:T(8,128)(2,1)} %bitcast.71, bf16[4,256,128]{2,1,0:T(8,128)(2,1)} %get-tuple-element.127.qx_ref, ...), custom_call_target="tpu_custom_call" | custom-call | flops 1610612736 | bytes 4194304 | tf_op jit(solution)/shard_map/query_grad/pallas_call | solution.py:233
  583.3 24.0 %collective-permute-done.34.refs_12_ = bf16[1,4,2,128,640]{4,3,2,1,0:T(8,128)(2,1)} collective-permute-done((bf16[1,4,2,128,640]{4,3,2,1,0:T(8,128)(2,1)}, bf16[1,4,2,128,640]{4,3,2,1,0:T(8,128)(2,1)}, u32[]{:S(2)}, u32[]{:S(2)}) %collective-permute-start.34) | collective-permute-done | bytes 1310752 | tf_op jit(solution)/shard_map/ppermute | solution.py:413
  612.9 3.2 maximum_select_fusion.4
  616.1 24.9 %key_value_grad.2 = (bf16[2,256,512]{2,1,0:T(8,128)(2,1)}, bf16[2,256,512]{2,1,0:T(8,128)(2,1)}) custom-call(s32[4,16]{1,0:T(4,128)} %copy.44.place_ref, s32[4,2]{1,0:T(4,128)} %get-tuple-element.235.own_ref, bf16[2,4,256,512]{3,2,1,0:T(8,128)(2,1)} %get-tuple-element.121.kv_ref, f32[1024,128]{1,0:T(8,128)} %copy-done.6, f32[1024,128]{1,0:T(8,128)} %copy-done.5, ...), custom_call_target="tpu_custom_call" | custom-call | flops 1073741824 | bytes 2097152 | tf_op jit(solution)/shard_map/key_value_grad/pallas_call | solution.py:233
  651.2 22.8 %key_value_grad.3 = (bf16[2,256,512]{2,1,0:T(8,128)(2,1)}, bf16[2,256,512]{2,1,0:T(8,128)(2,1)}) custom-call(s32[4,16]{1,0:T(4,128)} %copy.44.place_ref, s32[4,2]{1,0:T(4,128)} %get-tuple-element.235.own_ref, bf16[2,4,256,512]{3,2,1,0:T(8,128)(2,1)} %get-tuple-element.121.kv_ref, f32[1024,128]{1,0:T(8,128)} %copy-done.6, f32[1024,128]{1,0:T(8,128)} %copy-done.5, ...), custom_call_target="tpu_custom_call" | custom-call | flops 1073741824 | bytes 2097152 | tf_op jit(solution)/shard_map/key_value_grad/pallas_call | solution.py:233
  678.7 5.8 fusion.86
  684.5 10.8 %fusion.85 = (bf16[1024,2048]{1,0:T(8,128)(2,1)}, f32[1024,2048]{1,0:T(8,128)}) fusion(f32[1024,2048]{1,0:T(8,128)S(1)} %fusion.87, f32[1024,2048]{1,0:T(8,128)} %fusion.86, bf16[1024,512]{1,0:T(8,128)(2,1)S(1)} %bitcast.69, bf16[2048,512]{1,0:T(8,128)(2,1)S(1)} %copy-done.41), kind=kOutput, calls=%fused_computation.216 | convolution fusion | flops 2153775104 | bytes 32505856 | tf_op jit(solution)/shard_map/dot_general | solution.py:15
  695.3 3.3 fusion.47
  701.9 3.7 convolution_convert_fusion.2
  705.6 2.7 pad_maximum_fusion.1
  708.2 2.7 collective-permute-start.46
  712.2 3.0 fusion.29
  715.2 5.1 fusion.31
  720.4 3.4 fusion
  725.4 3.1 maximum_select_fusion
  728.5 4.3 maximum_select_fusion.1
  732.8 4.8 pad_maximum_fusion.half_ref
  737.7 4.3 fusion.77
  742.1 4.0 collective-permute-start.47
  747.4 22.7 %collective-permute-done.47 = bf16[256,2048]{1,0:T(8,128)(2,1)S(1)} collective-permute-done((bf16[256,2048]{1,0:T(8,128)(2,1)S(1)}, bf16[256,2048]{1,0:T(8,128)(2,1)S(1)}, u32[]{:S(2)}, u32[]{:S(2)}) %collective-permute-start.47) | collective-permute-done | bytes 1048608 | tf_op jit(solution)/shard_map/ppermute | solution.py:413
  783.1 9.9 %collective-permute-done.51 = bf16[176,1024]{1,0:T(8,128)(2,1)} collective-permute-done((bf16[176,1024]{1,0:T(8,128)(2,1)}, bf16[176,1024]{1,0:T(8,128)(2,1)}, u32[]{:S(2)}, u32[]{:S(2)}) %collective-permute-start.51) | collective-permute-done | bytes 360480 | tf_op jit(solution)/shard_map/ppermute | solution.py:413
  808.2 2.6 collective-permute-done.56
  811.4 3.9 collective-permute-start.57
  815.8 2.5 collective-permute-done.57
  821.6 13.6 %unpack_rows.2 = (f32[2048,1408]{1,0:T(8,128)}, f32[2048,1408]{1,0:T(8,128)}) custom-call(s32[1]{0:T(128)} %bitcast.19.core_ref, bf16[1024,2816]{1,0:T(8,128)(2,1)} %pad_maximum_fusion.half_ref, bf16[1024,2816]{1,0:T(8,128)(2,1)} %collective-permute-done.58.other_ref), custom_call_target="tpu_custom_call" | custom-call | bytes 34603008 | tf_op jit(solution)/shard_map/unpack_rows/pallas_call | solution.py:527
  843.8 4.3 collective-permute-done.65.other_ref
  848.1 6.5 unpack_cols.1
  854.6 13.8 %collective-permute-done.64 = bf16[256,2048]{1,0:T(8,128)(2,1)S(1)} collective-permute-done((bf16[256,2048]{1,0:T(8,128)(2,1)S(1)}, bf16[256,2048]{1,0:T(8,128)(2,1)S(1)}, u32[]{:S(2)}, u32[]{:S(2)}) %collective-permute-start.64) | collective-permute-done | bytes 1048608 | tf_op jit(solution)/shard_map/ppermute | solution.py:413
  870.6 2.6 pad_maximum_fusion.2.half_ref
  873.7 4.0 collective-permute-done.61
  879.4 2.7 collective-permute-done.62
  888.0 3.1 fusion.18
  891.1 4.5 reduce-scatter.6.cloned.1.call-done
  898.1 11.4 %unpack_rows.3 = (f32[2048,512]{1,0:T(8,128)}, f32[2048,512]{1,0:T(8,128)}, f32[2048,512]{1,0:T(8,128)}, f32[512,2048]{1,0:T(8,128)}) custom-call(s32[1]{0:T(128)} %bitcast.19.core_ref, bf16[1024,2048]{1,0:T(8,128)(2,1)} %pad_maximum_fusion.2.half_ref, bf16[1024,2048]{1,0:T(8,128)(2,1)} %collective-permute-done.66.other_ref), custom_call_target="tpu_custom_call" | custom-call | bytes 25165824 | tf_op jit(solution)/shard_map/unpack_rows/pallas_call | solution.py:527
  (448 shorter events, 168.2 us)
Async XLA Ops:
  7.2 89.0 %all-gather.7.cloned.1.call-start = ((), (), s32[]{:S(2)}) async-start(), calls=%async_computation.3 | async-start | bytes 5242880 | tf_op jit(solution)/shard_map/all_gather | solution.py:568
  12.7 197.1 %all-gather.9.cloned.1.call-start = ((), (), s32[]{:S(2)}) async-start(), calls=%async_computation.4 | async-start | bytes 5242880 | tf_op jit(solution)/shard_map/all_gather | solution.py:568
  96.3 166.2 %all-gather.15.cloned.1.call-start = ((), (), s32[]{:S(2)}) async-start(), calls=%async_computation.10 | async-start | bytes 9437184 | tf_op jit(solution)/shard_map/all_gather | solution.py:682
  112.0 47.7 %collective-permute-start.3 = (bf16[2,4,2,128,512]{4,3,2,1,0:T(8,128)(2,1)}, bf16[2,4,2,128,512]{4,3,2,1,0:T(8,128)(2,1)}, u32[]{:S(2)}, u32[]{:S(2)}) collective-permute-start(bf16[2,4,2,128,512]{4,3,2,1,0:T(8,128)(2,1)} %bitcast.5.refs_0_.refs_8_), channel_id=1, source_target_pairs={{0,16},{4,20},{8,24},{12,28},{16,0},{20,4},{24,8},{28,12},{1,17},{... | collective-permute-start | bytes 6291464 | tf_op jit(solution)/shard_map/ppermute | solution.py:413
  113.5 49.9 %collective-permute-start.1 = (bf16[2,4,2,128,512]{4,3,2,1,0:T(8,128)(2,1)}, bf16[2,4,2,128,512]{4,3,2,1,0:T(8,128)(2,1)}, u32[]{:S(2)}, u32[]{:S(2)}) collective-permute-start(bf16[2,4,2,128,512]{4,3,2,1,0:T(8,128)(2,1)} %bitcast.5.refs_0_.refs_8_), channel_id=1, source_target_pairs={{0,8},{4,12},{8,0},{12,4},{16,24},{20,28},{24,16},{28,20},{1,9},{5... | collective-permute-start | bytes 6291464 | tf_op jit(solution)/shard_map/ppermute | solution.py:413
  161.9 40.5 %collective-permute-start.7 = (bf16[1,4,2,128,512]{4,3,2,1,0:T(8,128)(2,1)}, bf16[1,4,2,128,512]{4,3,2,1,0:T(8,128)(2,1)S(1)}, u32[]{:S(2)}, u32[]{:S(2)}) collective-permute-start(bf16[1,4,2,128,512]{4,3,2,1,0:T(8,128)(2,1)} %slice.96), channel_id=1, source_target_pairs={{0,8},{4,12},{8,0},{12,4},{16,24},{20,28},{24,16},{28,20},{1,9},{5... | collective-permute-start | bytes 3145736 | tf_op jit(solution)/shard_map/ppermute | solution.py:413
  165.7 37.3 %collective-permute-start.5 = (bf16[1,4,2,128,512]{4,3,2,1,0:T(8,128)(2,1)}, bf16[1,4,2,128,512]{4,3,2,1,0:T(8,128)(2,1)}, u32[]{:S(2)}, u32[]{:S(2)}) collective-permute-start(bf16[1,4,2,128,512]{4,3,2,1,0:T(8,128)(2,1)} %slice.95), channel_id=1, source_target_pairs={{0,16},{4,20},{8,24},{12,28},{16,0},{20,4},{24,8},{28,12},{1,17},{... | collective-permute-start | bytes 3145736 | tf_op jit(solution)/shard_map/ppermute | solution.py:413
  167.2 12.3 %collective-permute-start.14 = (bf16[64,2048]{1,0:T(8,128)(2,1)S(1)}, bf16[64,2048]{1,0:T(8,128)(2,1)}, u32[]{:S(2)}, u32[]{:S(2)}) collective-permute-start(bf16[64,2048]{1,0:T(8,128)(2,1)S(1)} %constant_dynamic-slice_fusion.15), channel_id=1, source_target_pairs={{0,3},{1,0},{2,1},{3,2},{4,7},{5,4},{6,5},{7,6},{8,11},{9,8},{10,9... | collective-permute-start | bytes 786440 | tf_op jit(solution)/shard_map/ppermute | solution.py:651
  168.3 31.0 %collective-permute-start.13 = (bf16[64,2048]{1,0:T(8,128)(2,1)S(1)}, bf16[64,2048]{1,0:T(8,128)(2,1)S(1)}, u32[]{:S(2)}, u32[]{:S(2)}) collective-permute-start(bf16[64,2048]{1,0:T(8,128)(2,1)S(1)} %constant_dynamic-slice_fusion.15), channel_id=1, source_target_pairs={{0,2},{1,3},{2,0},{3,1},{4,6},{5,7},{6,4},{7,5},{8,10},{9,11},{10,... | collective-permute-start | bytes 786440 | tf_op jit(solution)/shard_map/ppermute | solution.py:651
  168.3 31.0 %collective-permute-start.12 = (bf16[64,2048]{1,0:T(8,128)(2,1)S(1)}, bf16[64,2048]{1,0:T(8,128)(2,1)S(1)}, u32[]{:S(2)}, u32[]{:S(2)}) collective-permute-start(bf16[64,2048]{1,0:T(8,128)(2,1)S(1)} %constant_dynamic-slice_fusion.15), channel_id=1, source_target_pairs={{0,1},{1,2},{2,3},{3,0},{4,5},{5,6},{6,7},{7,4},{8,9},{9,10},{10,1... | collective-permute-start | bytes 786440 | tf_op jit(solution)/shard_map/ppermute | solution.py:651
  179.5 27.6 %collective-permute-start = (bf16[2,4,2,128,512]{4,3,2,1,0:T(8,128)(2,1)}, bf16[2,4,2,128,512]{4,3,2,1,0:T(8,128)(2,1)S(1)}, u32[]{:S(2)}, u32[]{:S(2)}) collective-permute-start(bf16[2,4,2,128,512]{4,3,2,1,0:T(8,128)(2,1)} %bitcast.5.refs_0_.refs_8_), channel_id=1, source_target_pairs={{0,4},{4,0},{8,12},{12,8},{16,20},{20,16},{24,28},{28,24},{1,5},{5... | collective-permute-start | bytes 6291464 | tf_op jit(solution)/shard_map/ppermute | solution.py:413
  199.3 10.5 %collective-permute-start.4 = (bf16[2,4,2,128,512]{4,3,2,1,0:T(8,128)(2,1)}, bf16[2,4,2,128,512]{4,3,2,1,0:T(8,128)(2,1)}, u32[]{:S(2)}, u32[]{:S(2)}) collective-permute-start(bf16[2,4,2,128,512]{4,3,2,1,0:T(8,128)(2,1)} %collective-permute-done.3.refs_4_.refs_12_), channel_id=1, source_target_pairs={{0,4},{4,0},{8,12},{12,8},{16,20},{20,16},{24,28},{28,24},{1,5},{5... | collective-permute-start | bytes 6291464 | tf_op jit(solution)/shard_map/ppermute | solution.py:413
  200.7 9.1 collective-permute-start.2
  209.8 149.7 %all-gather.11.cloned.1.call-start = ((), (), s32[]{:S(2)}) async-start(), calls=%async_computation.5 | async-start | bytes 5242880 | tf_op jit(solution)/shard_map/all_gather | solution.py:568
  240.6 11.3 %collective-permute-start.9 = (bf16[256,512]{1,0:T(8,128)(2,1)}, bf16[256,512]{1,0:T(8,128)(2,1)S(1)}, u32[]{:S(2)}, u32[]{:S(2)}) collective-permute-start(bf16[256,512]{1,0:T(8,128)(2,1)} %get-tuple-element.248), channel_id=1, source_target_pairs={{0,1},{1,2},{2,3},{3,0},{4,5},{5,6},{6,7},{7,4},{8,9},{9,10},{10,1... | collective-permute-start | bytes 786440 | tf_op jit(solution)/shard_map/ppermute | solution.py:573
  240.6 21.3 %collective-permute-start.10 = (bf16[256,512]{1,0:T(8,128)(2,1)S(1)}, bf16[256,512]{1,0:T(8,128)(2,1)S(1)}, u32[]{:S(2)}, u32[]{:S(2)}) collective-permute-start(bf16[256,512]{1,0:T(8,128)(2,1)S(1)} %get-tuple-element.247), channel_id=1, source_target_pairs={{0,2},{1,3},{2,0},{3,1},{4,6},{5,7},{6,4},{7,5},{8,10},{9,11},{10,... | collective-permute-start | bytes 786440 | tf_op jit(solution)/shard_map/ppermute | solution.py:573
  240.6 21.4 %collective-permute-start.11 = (bf16[256,512]{1,0:T(8,128)(2,1)S(1)}, bf16[256,512]{1,0:T(8,128)(2,1)S(1)}, u32[]{:S(2)}, u32[]{:S(2)}) collective-permute-start(bf16[256,512]{1,0:T(8,128)(2,1)S(1)} %get-tuple-element.246), channel_id=1, source_target_pairs={{0,3},{1,0},{2,1},{3,2},{4,7},{5,4},{6,5},{7,6},{8,11},{9,8},{10,9... | collective-permute-start | bytes 786440 | tf_op jit(solution)/shard_map/ppermute | solution.py:573
  271.3 231.2 %reduce-scatter.4.cloned.1.call-start = ((), (), s32[]{:S(2)}) async-start(), calls=%async_computation.6 | async-start | bytes 5242880 | tf_op jit(solution)/shard_map/reduce_scatter | solution.py:596
  272.6 36.7 %collective-permute-start.20 = (bf16[1,4,2,128,640]{4,3,2,1,0:T(8,128)(2,1)}, bf16[1,4,2,128,640]{4,3,2,1,0:T(8,128)(2,1)S(1)}, u32[]{:S(2)}, u32[]{:S(2)}) collective-permute-start(bf16[1,4,2,128,640]{4,3,2,1,0:T(8,128)(2,1)} %bitcast.12.refs_0_), channel_id=1, source_target_pairs={{0,24},{4,28},{8,16},{12,20},{16,8},{20,12},{24,0},{28,4},{1,25},{... | collective-permute-start | bytes 3932168 | tf_op jit(solution)/shard_map/ppermute | solution.py:413
  279.3 56.0 %collective-permute-start.18 = (bf16[1,4,2,128,640]{4,3,2,1,0:T(8,128)(2,1)}, bf16[1,4,2,128,640]{4,3,2,1,0:T(8,128)(2,1)}, u32[]{:S(2)}, u32[]{:S(2)}) collective-permute-start(bf16[1,4,2,128,640]{4,3,2,1,0:T(8,128)(2,1)} %bitcast.12.refs_0_), channel_id=1, source_target_pairs={{0,16},{4,20},{8,24},{12,28},{16,0},{20,4},{24,8},{28,12},{1,17},{... | collective-permute-start | bytes 3932168 | tf_op jit(solution)/shard_map/ppermute | solution.py:413
  279.3 56.0 %collective-permute-start.16 = (bf16[1,4,2,128,640]{4,3,2,1,0:T(8,128)(2,1)}, bf16[1,4,2,128,640]{4,3,2,1,0:T(8,128)(2,1)}, u32[]{:S(2)}, u32[]{:S(2)}) collective-permute-start(bf16[1,4,2,128,640]{4,3,2,1,0:T(8,128)(2,1)} %bitcast.12.refs_0_), channel_id=1, source_target_pairs={{0,8},{4,12},{8,0},{12,4},{16,24},{20,28},{24,16},{28,20},{1,9},{5... | collective-permute-start | bytes 3932168 | tf_op jit(solution)/shard_map/ppermute | solution.py:413
  279.9 55.9 %collective-permute-start.15 = (bf16[1,4,2,128,640]{4,3,2,1,0:T(8,128)(2,1)}, bf16[1,4,2,128,640]{4,3,2,1,0:T(8,128)(2,1)}, u32[]{:S(2)}, u32[]{:S(2)}) collective-permute-start(bf16[1,4,2,128,640]{4,3,2,1,0:T(8,128)(2,1)} %bitcast.12.refs_0_), channel_id=1, source_target_pairs={{0,4},{4,0},{8,12},{12,8},{16,20},{20,16},{24,28},{28,24},{1,5},{5... | collective-permute-start | bytes 3932168 | tf_op jit(solution)/shard_map/ppermute | solution.py:413
  309.3 26.6 %collective-permute-start.21 = (bf16[1,4,2,128,640]{4,3,2,1,0:T(8,128)(2,1)S(1)}, bf16[1,4,2,128,640]{4,3,2,1,0:T(8,128)(2,1)}, u32[]{:S(2)}, u32[]{:S(2)}) collective-permute-start(bf16[1,4,2,128,640]{4,3,2,1,0:T(8,128)(2,1)S(1)} %collective-permute-done.20.refs_6_), channel_id=1, source_target_pairs={{0,4},{4,0},{8,12},{12,8},{16,20},{20,16},{24,28},{28,24},{1,5},{5... | collective-permute-start | bytes 3932168 | tf_op jit(solution)/shard_map/ppermute | solution.py:413
  420.3 22.4 %collective-permute-start.22 = (bf16[1024,2816]{1,0:T(8,128)(2,1)}, bf16[1024,2816]{1,0:T(8,128)(2,1)}, u32[]{:S(2)}, u32[]{:S(2)}) collective-permute-start(bf16[1024,2816]{1,0:T(8,128)(2,1)} %convolution_convert_fusion), channel_id=1, source_target_pairs={{0,4},{4,0},{8,12},{12,8},{16,20},{20,16},{24,28},{28,24},{1,5},{5... | collective-permute-start | bytes 17301512 | tf_op jit(solution)/shard_map/ppermute | solution.py:413
  424.9 9.3 %collective-permute-start.23 = (bf16[1408,1024]{1,0:T(8,128)(2,1)}, bf16[1408,1024]{1,0:T(8,128)(2,1)}, u32[]{:S(2)}, u32[]{:S(2)}) collective-permute-start(bf16[1408,1024]{1,0:T(8,128)(2,1)} %convolution_convert_fusion.3), channel_id=1, source_target_pairs={{0,4},{4,0},{8,12},{12,8},{16,20},{20,16},{24,28},{28,24},{1,5},{5... | collective-permute-start | bytes 8650760 | tf_op jit(solution)/shard_map/ppermute | solution.py:413
  427.0 268.2 %all-gather.13.cloned.1.call-start = ((), (), s32[]{:S(2)}) async-start(), calls=%async_computation.8 | async-start | bytes 5242880 | tf_op jit(solution)/shard_map/all_gather | solution.py:568
  455.2 33.9 %collective-permute-start.24 = (bf16[256,2816]{1,0:T(8,128)(2,1)}, bf16[256,2816]{1,0:T(8,128)(2,1)S(1)}, u32[]{:S(2)}, u32[]{:S(2)}) collective-permute-start(bf16[256,2816]{1,0:T(8,128)(2,1)} %constant_dynamic-slice_fusion.14), channel_id=1, source_target_pairs={{0,8},{4,12},{8,0},{12,4},{16,24},{20,28},{24,16},{28,20},{1,9},{5... | collective-permute-start | bytes 4325384 | tf_op jit(solution)/shard_map/ppermute | solution.py:413
  458.0 33.7 %collective-permute-start.25 = (bf16[256,2816]{1,0:T(8,128)(2,1)}, bf16[256,2816]{1,0:T(8,128)(2,1)}, u32[]{:S(2)}, u32[]{:S(2)}) collective-permute-start(bf16[256,2816]{1,0:T(8,128)(2,1)} %constant_dynamic-slice_fusion.13), channel_id=1, source_target_pairs={{0,16},{4,20},{8,24},{12,28},{16,0},{20,4},{24,8},{28,12},{1,17},{... | collective-permute-start | bytes 4325384 | tf_op jit(solution)/shard_map/ppermute | solution.py:413
  494.7 20.3 %collective-permute-start.29 = (bf16[128,2816]{1,0:T(8,128)(2,1)}, bf16[128,2816]{1,0:T(8,128)(2,1)}, u32[]{:S(2)}, u32[]{:S(2)}) collective-permute-start(bf16[128,2816]{1,0:T(8,128)(2,1)} %constant_dynamic-slice_fusion.9), channel_id=1, source_target_pairs={{0,16},{4,20},{8,24},{12,28},{16,0},{20,4},{24,8},{28,12},{1,17},{... | collective-permute-start | bytes 2162696 | tf_op jit(solution)/shard_map/ppermute | solution.py:413
  500.0 17.1 %collective-permute-start.30 = (bf16[128,2816]{1,0:T(8,128)(2,1)}, bf16[128,2816]{1,0:T(8,128)(2,1)}, u32[]{:S(2)}, u32[]{:S(2)}) collective-permute-start(bf16[128,2816]{1,0:T(8,128)(2,1)} %constant_dynamic-slice_fusion.8), channel_id=1, source_target_pairs={{0,8},{4,12},{8,0},{12,4},{16,24},{20,28},{24,16},{28,20},{1,9},{5... | collective-permute-start | bytes 2162696 | tf_op jit(solution)/shard_map/ppermute | solution.py:413
  518.4 28.3 %collective-permute-start.32 = (bf16[128,2816]{1,0:T(8,128)(2,1)S(1)}, bf16[128,2816]{1,0:T(8,128)(2,1)S(1)}, u32[]{:S(2)}, u32[]{:S(2)}) collective-permute-start(bf16[128,2816]{1,0:T(8,128)(2,1)S(1)} %add_convert_fusion.11), channel_id=1, source_target_pairs={{0,8},{4,12},{8,0},{12,4},{16,24},{20,28},{24,16},{28,20},{1,9},{5... | collective-permute-start | bytes 2162696 | tf_op jit(solution)/shard_map/ppermute | solution.py:413
  520.3 23.8 %collective-permute-start.28 = (bf16[256,512]{1,0:T(8,128)(2,1)S(1)}, bf16[256,512]{1,0:T(8,128)(2,1)S(1)}, u32[]{:S(2)}, u32[]{:S(2)}) collective-permute-start(bf16[256,512]{1,0:T(8,128)(2,1)S(1)} %get-tuple-element.242), channel_id=1, source_target_pairs={{0,3},{1,0},{2,1},{3,2},{4,7},{5,4},{6,5},{7,6},{8,11},{9,8},{10,9... | collective-permute-start | bytes 786440 | tf_op jit(solution)/shard_map/ppermute | solution.py:573
  521.5 22.5 %collective-permute-start.27 = (bf16[256,512]{1,0:T(8,128)(2,1)S(1)}, bf16[256,512]{1,0:T(8,128)(2,1)S(1)}, u32[]{:S(2)}, u32[]{:S(2)}) collective-permute-start(bf16[256,512]{1,0:T(8,128)(2,1)S(1)} %get-tuple-element.243), channel_id=1, source_target_pairs={{0,2},{1,3},{2,0},{3,1},{4,6},{5,7},{6,4},{7,5},{8,10},{9,11},{10,... | collective-permute-start | bytes 786440 | tf_op jit(solution)/shard_map/ppermute | solution.py:573
  521.5 18.2 %collective-permute-start.26 = (bf16[256,512]{1,0:T(8,128)(2,1)S(1)}, bf16[256,512]{1,0:T(8,128)(2,1)S(1)}, u32[]{:S(2)}, u32[]{:S(2)}) collective-permute-start(bf16[256,512]{1,0:T(8,128)(2,1)S(1)} %get-tuple-element.244), channel_id=1, source_target_pairs={{0,1},{1,2},{2,3},{3,0},{4,5},{5,6},{6,7},{7,4},{8,9},{9,10},{10,1... | collective-permute-start | bytes 786440 | tf_op jit(solution)/shard_map/ppermute | solution.py:573
  524.9 21.8 %collective-permute-start.31 = (bf16[128,2816]{1,0:T(8,128)(2,1)S(1)}, bf16[128,2816]{1,0:T(8,128)(2,1)S(1)}, u32[]{:S(2)}, u32[]{:S(2)}) collective-permute-start(bf16[128,2816]{1,0:T(8,128)(2,1)S(1)} %add_convert_fusion.12), channel_id=1, source_target_pairs={{0,16},{4,20},{8,24},{12,28},{16,0},{20,4},{24,8},{28,12},{1,17},{... | collective-permute-start | bytes 2162696 | tf_op jit(solution)/shard_map/ppermute | solution.py:413
  548.4 34.9 %collective-permute-start.35 = (bf16[1,4,2,128,640]{4,3,2,1,0:T(8,128)(2,1)}, bf16[1,4,2,128,640]{4,3,2,1,0:T(8,128)(2,1)}, u32[]{:S(2)}, u32[]{:S(2)}) collective-permute-start(bf16[1,4,2,128,640]{4,3,2,1,0:T(8,128)(2,1)} %bitcast.13.refs_8_), channel_id=1, source_target_pairs={{0,24},{4,28},{8,16},{12,20},{16,8},{20,12},{24,0},{28,4},{1,25},{... | collective-permute-start | bytes 3932168 | tf_op jit(solution)/shard_map/ppermute | solution.py:413
  549.9 57.4 %collective-permute-start.34 = (bf16[1,4,2,128,640]{4,3,2,1,0:T(8,128)(2,1)}, bf16[1,4,2,128,640]{4,3,2,1,0:T(8,128)(2,1)}, u32[]{:S(2)}, u32[]{:S(2)}) collective-permute-start(bf16[1,4,2,128,640]{4,3,2,1,0:T(8,128)(2,1)} %bitcast.13.refs_8_), channel_id=1, source_target_pairs={{0,16},{4,20},{8,24},{12,28},{16,0},{20,4},{24,8},{28,12},{1,17},{... | collective-permute-start | bytes 3932168 | tf_op jit(solution)/shard_map/ppermute | solution.py:413
  550.4 57.0 %collective-permute-start.33 = (bf16[1,4,2,128,640]{4,3,2,1,0:T(8,128)(2,1)}, bf16[1,4,2,128,640]{4,3,2,1,0:T(8,128)(2,1)}, u32[]{:S(2)}, u32[]{:S(2)}) collective-permute-start(bf16[1,4,2,128,640]{4,3,2,1,0:T(8,128)(2,1)} %bitcast.13.refs_8_), channel_id=1, source_target_pairs={{0,8},{4,12},{8,0},{12,4},{16,24},{20,28},{24,16},{28,20},{1,9},{5... | collective-permute-start | bytes 3932168 | tf_op jit(solution)/shard_map/ppermute | solution.py:413
  551.9 334.0 %reduce-scatter.8.cloned.1.call-start = ((), (), s32[]{:S(2)}) async-start(), calls=%async_computation.9 | async-start | bytes 5242880 | tf_op jit(solution)/shard_map/reduce_scatter | solution.py:596
  552.0 59.7 %collective-permute-start.36 = (bf16[1,4,2,128,640]{4,3,2,1,0:T(8,128)(2,1)}, bf16[1,4,2,128,640]{4,3,2,1,0:T(8,128)(2,1)}, u32[]{:S(2)}, u32[]{:S(2)}) collective-permute-start(bf16[1,4,2,128,640]{4,3,2,1,0:T(8,128)(2,1)} %bitcast.13.refs_8_), channel_id=1, source_target_pairs={{0,4},{4,0},{8,12},{12,8},{16,20},{20,16},{24,28},{28,24},{1,5},{5... | collective-permute-start | bytes 3932168 | tf_op jit(solution)/shard_map/ppermute | solution.py:413
  607.5 8.6 collective-permute-start.37
  607.5 8.6 collective-permute-start.38
  608.9 32.1 %collective-permute-start.41 = (bf16[352,1024]{1,0:T(8,128)(2,1)}, bf16[352,1024]{1,0:T(8,128)(2,1)}, u32[]{:S(2)}, u32[]{:S(2)}) collective-permute-start(bf16[352,1024]{1,0:T(8,128)(2,1)} %constant_dynamic-slice_fusion.6), channel_id=1, source_target_pairs={{0,16},{4,20},{8,24},{12,28},{16,0},{20,4},{24,8},{28,12},{1,17},{... | collective-permute-start | bytes 2162696 | tf_op jit(solution)/shard_map/ppermute | solution.py:413
  611.7 29.3 %collective-permute-start.40 = (bf16[352,1024]{1,0:T(8,128)(2,1)}, bf16[352,1024]{1,0:T(8,128)(2,1)}, u32[]{:S(2)}, u32[]{:S(2)}) collective-permute-start(bf16[352,1024]{1,0:T(8,128)(2,1)} %constant_dynamic-slice_fusion.7), channel_id=1, source_target_pairs={{0,8},{4,12},{8,0},{12,4},{16,24},{20,28},{24,16},{28,20},{1,9},{5... | collective-permute-start | bytes 2162696 | tf_op jit(solution)/shard_map/ppermute | solution.py:413
  643.4 30.7 %collective-permute-start.42 = (bf16[176,1024]{1,0:T(8,128)(2,1)}, bf16[176,1024]{1,0:T(8,128)(2,1)}, u32[]{:S(2)}, u32[]{:S(2)}) collective-permute-start(bf16[176,1024]{1,0:T(8,128)(2,1)} %constant_dynamic-slice_fusion.5), channel_id=1, source_target_pairs={{0,16},{4,20},{8,24},{12,28},{16,0},{20,4},{24,8},{28,12},{1,17},{... | collective-permute-start | bytes 1081352 | tf_op jit(solution)/shard_map/ppermute | solution.py:413
  645.8 28.3 %collective-permute-start.43 = (bf16[176,1024]{1,0:T(8,128)(2,1)S(1)}, bf16[176,1024]{1,0:T(8,128)(2,1)S(1)}, u32[]{:S(2)}, u32[]{:S(2)}) collective-permute-start(bf16[176,1024]{1,0:T(8,128)(2,1)S(1)} %constant_dynamic-slice_fusion.4), channel_id=1, source_target_pairs={{0,8},{4,12},{8,0},{12,4},{16,24},{20,28},{24,16},{28,20},{1,9},{5... | collective-permute-start | bytes 1081352 | tf_op jit(solution)/shard_map/ppermute | solution.py:413
  647.2 48.0 %collective-permute-start.44 = (bf16[256,2816]{1,0:T(8,128)(2,1)}, bf16[256,2816]{1,0:T(8,128)(2,1)}, u32[]{:S(2)}, u32[]{:S(2)}) collective-permute-start(bf16[256,2816]{1,0:T(8,128)(2,1)} %maximum_select_fusion.4), channel_id=1, source_target_pairs={{0,8},{4,12},{8,0},{12,4},{16,24},{20,28},{24,16},{28,20},{1,9},{5... | collective-permute-start | bytes 4325384 | tf_op jit(solution)/shard_map/ppermute | solution.py:413
  649.3 46.0 %collective-permute-start.45 = (bf16[256,2816]{1,0:T(8,128)(2,1)}, bf16[256,2816]{1,0:T(8,128)(2,1)}, u32[]{:S(2)}, u32[]{:S(2)}) collective-permute-start(bf16[256,2816]{1,0:T(8,128)(2,1)} %maximum_select_fusion.5), channel_id=1, source_target_pairs={{0,16},{4,20},{8,24},{12,28},{16,0},{20,4},{24,8},{28,12},{1,17},{... | collective-permute-start | bytes 4325384 | tf_op jit(solution)/shard_map/ppermute | solution.py:413
  708.2 12.1 %collective-permute-start.46 = (bf16[1024,2048]{1,0:T(8,128)(2,1)}, bf16[1024,2048]{1,0:T(8,128)(2,1)}, u32[]{:S(2)}, u32[]{:S(2)}) collective-permute-start(bf16[1024,2048]{1,0:T(8,128)(2,1)} %pad_maximum_fusion.1), channel_id=1, source_target_pairs={{0,4},{4,0},{8,12},{12,8},{16,20},{20,16},{24,28},{28,24},{1,5},{5... | collective-permute-start | bytes 12582920 | tf_op jit(solution)/shard_map/ppermute | solution.py:413
  711.0 184.6 %reduce-scatter.6.cloned.1.call-start = ((), (), s32[]{:S(2)}) async-start(), calls=%async_computation.7 | async-start | bytes 5242880 | tf_op jit(solution)/shard_map/reduce_scatter | solution.py:596
  737.6 84.0 %collective-permute-start.58 = (bf16[1024,2816]{1,0:T(8,128)(2,1)}, bf16[1024,2816]{1,0:T(8,128)(2,1)}, u32[]{:S(2)}, u32[]{:S(2)}) collective-permute-start(bf16[1024,2816]{1,0:T(8,128)(2,1)} %pad_maximum_fusion.half_ref), channel_id=1, source_target_pairs={{0,4},{4,0},{8,12},{12,8},{16,20},{20,16},{24,28},{28,24},{1,5},{5... | collective-permute-start | bytes 17301512 | tf_op jit(solution)/shard_map/ppermute | solution.py:413
  742.1 28.0 %collective-permute-start.47 = (bf16[256,2048]{1,0:T(8,128)(2,1)S(1)}, bf16[256,2048]{1,0:T(8,128)(2,1)S(1)}, u32[]{:S(2)}, u32[]{:S(2)}) collective-permute-start(bf16[256,2048]{1,0:T(8,128)(2,1)S(1)} %constant_dynamic-slice_fusion.3), channel_id=1, source_target_pairs={{0,8},{4,12},{8,0},{12,4},{16,24},{20,28},{24,16},{28,20},{1,9},{5... | collective-permute-start | bytes 3145736 | tf_op jit(solution)/shard_map/ppermute | solution.py:413
  746.7 25.3 %collective-permute-start.48 = (bf16[256,2048]{1,0:T(8,128)(2,1)S(1)}, bf16[256,2048]{1,0:T(8,128)(2,1)S(1)}, u32[]{:S(2)}, u32[]{:S(2)}) collective-permute-start(bf16[256,2048]{1,0:T(8,128)(2,1)S(1)} %constant_dynamic-slice_fusion.2), channel_id=1, source_target_pairs={{0,16},{4,20},{8,24},{12,28},{16,0},{20,4},{24,8},{28,12},{1,17},{... | collective-permute-start | bytes 3145736 | tf_op jit(solution)/shard_map/ppermute | solution.py:413
  747.0 36.1 %collective-permute-start.52 = (bf16[176,1024]{1,0:T(8,128)(2,1)S(1)}, bf16[176,1024]{1,0:T(8,128)(2,1)}, u32[]{:S(2)}, u32[]{:S(2)}) collective-permute-start(bf16[176,1024]{1,0:T(8,128)(2,1)S(1)} %add_convert_fusion.15), channel_id=1, source_target_pairs={{0,8},{4,12},{8,0},{12,4},{16,24},{20,28},{24,16},{28,20},{1,9},{5... | collective-permute-start | bytes 1081352 | tf_op jit(solution)/shard_map/ppermute | solution.py:413
  771.4 21.7 %collective-permute-start.49 = (bf16[128,2048]{1,0:T(8,128)(2,1)}, bf16[128,2048]{1,0:T(8,128)(2,1)}, u32[]{:S(2)}, u32[]{:S(2)}) collective-permute-start(bf16[128,2048]{1,0:T(8,128)(2,1)} %constant_dynamic-slice_fusion.1), channel_id=1, source_target_pairs={{0,16},{4,20},{8,24},{12,28},{16,0},{20,4},{24,8},{28,12},{1,17},{... | collective-permute-start | bytes 1572872 | tf_op jit(solution)/shard_map/ppermute | solution.py:413
  774.3 18.8 %collective-permute-start.50 = (bf16[128,2048]{1,0:T(8,128)(2,1)}, bf16[128,2048]{1,0:T(8,128)(2,1)}, u32[]{:S(2)}, u32[]{:S(2)}) collective-permute-start(bf16[128,2048]{1,0:T(8,128)(2,1)} %constant_dynamic-slice_fusion), channel_id=1, source_target_pairs={{0,8},{4,12},{8,0},{12,4},{16,24},{20,28},{24,16},{28,20},{1,9},{5... | collective-permute-start | bytes 1572872 | tf_op jit(solution)/shard_map/ppermute | solution.py:413
  777.4 15.7 %collective-permute-start.51 = (bf16[176,1024]{1,0:T(8,128)(2,1)}, bf16[176,1024]{1,0:T(8,128)(2,1)}, u32[]{:S(2)}, u32[]{:S(2)}) collective-permute-start(bf16[176,1024]{1,0:T(8,128)(2,1)} %add_convert_fusion.16), channel_id=1, source_target_pairs={{0,16},{4,20},{8,24},{12,28},{16,0},{20,4},{24,8},{28,12},{1,17},{... | collective-permute-start | bytes 1081352 | tf_op jit(solution)/shard_map/ppermute | solution.py:413
  798.5 36.7 %collective-permute-start.60 = (bf16[352,1024]{1,0:T(8,128)(2,1)S(1)}, bf16[352,1024]{1,0:T(8,128)(2,1)}, u32[]{:S(2)}, u32[]{:S(2)}) collective-permute-start(bf16[352,1024]{1,0:T(8,128)(2,1)S(1)} %maximum_select_fusion.11), channel_id=1, source_target_pairs={{0,16},{4,20},{8,24},{12,28},{16,0},{20,4},{24,8},{28,12},{1,17},{... | collective-permute-start | bytes 2162696 | tf_op jit(solution)/shard_map/ppermute | solution.py:413
  800.5 34.8 %collective-permute-start.59 = (bf16[352,1024]{1,0:T(8,128)(2,1)S(1)}, bf16[352,1024]{1,0:T(8,128)(2,1)}, u32[]{:S(2)}, u32[]{:S(2)}) collective-permute-start(bf16[352,1024]{1,0:T(8,128)(2,1)S(1)} %maximum_select_fusion.10), channel_id=1, source_target_pairs={{0,8},{4,12},{8,0},{12,4},{16,24},{20,28},{24,16},{28,20},{1,9},{5... | collective-permute-start | bytes 2162696 | tf_op jit(solution)/shard_map/ppermute | solution.py:413
  815.3 19.9 %collective-permute-start.54 = (bf16[128,2048]{1,0:T(8,128)(2,1)}, bf16[128,2048]{1,0:T(8,128)(2,1)}, u32[]{:S(2)}, u32[]{:S(2)}) collective-permute-start(bf16[128,2048]{1,0:T(8,128)(2,1)} %add_convert_fusion.13), channel_id=1, source_target_pairs={{0,8},{4,12},{8,0},{12,4},{16,24},{20,28},{24,16},{28,20},{1,9},{5... | collective-permute-start | bytes 1572872 | tf_op jit(solution)/shard_map/ppermute | solution.py:413
  818.9 16.3 %collective-permute-start.53 = (bf16[128,2048]{1,0:T(8,128)(2,1)}, bf16[128,2048]{1,0:T(8,128)(2,1)}, u32[]{:S(2)}, u32[]{:S(2)}) collective-permute-start(bf16[128,2048]{1,0:T(8,128)(2,1)} %add_convert_fusion.14), channel_id=1, source_target_pairs={{0,16},{4,20},{8,24},{12,28},{16,0},{20,4},{24,8},{28,12},{1,17},{... | collective-permute-start | bytes 1572872 | tf_op jit(solution)/shard_map/ppermute | solution.py:413
  842.8 25.6 %collective-permute-start.64 = (bf16[256,2048]{1,0:T(8,128)(2,1)S(1)}, bf16[256,2048]{1,0:T(8,128)(2,1)S(1)}, u32[]{:S(2)}, u32[]{:S(2)}) collective-permute-start(bf16[256,2048]{1,0:T(8,128)(2,1)S(1)} %maximum_select_fusion.9), channel_id=1, source_target_pairs={{0,16},{4,20},{8,24},{12,28},{16,0},{20,4},{24,8},{28,12},{1,17},{... | collective-permute-start | bytes 3145736 | tf_op jit(solution)/shard_map/ppermute | solution.py:413
  843.4 25.2 %collective-permute-start.63 = (bf16[256,2048]{1,0:T(8,128)(2,1)S(1)}, bf16[256,2048]{1,0:T(8,128)(2,1)S(1)}, u32[]{:S(2)}, u32[]{:S(2)}) collective-permute-start(bf16[256,2048]{1,0:T(8,128)(2,1)S(1)} %maximum_select_fusion.8), channel_id=1, source_target_pairs={{0,8},{4,12},{8,0},{12,4},{16,24},{20,28},{24,16},{28,20},{1,9},{5... | collective-permute-start | bytes 3145736 | tf_op jit(solution)/shard_map/ppermute | solution.py:413
  873.2 24.8 %collective-permute-start.66 = (bf16[1024,2048]{1,0:T(8,128)(2,1)}, bf16[1024,2048]{1,0:T(8,128)(2,1)}, u32[]{:S(2)}, u32[]{:S(2)}) collective-permute-start(bf16[1024,2048]{1,0:T(8,128)(2,1)} %pad_maximum_fusion.2.half_ref), channel_id=1, source_target_pairs={{0,4},{4,0},{8,12},{12,8},{16,20},{20,16},{24,28},{28,24},{1,5},{5... | collective-permute-start | bytes 12582920 | tf_op jit(solution)/shard_map/ppermute | solution.py:413
  (109 other events, 1359.9 us)
Sparse Core Ops, SparseCore 0:
  12.8 83.4 all-gather.6
  97.8 85.6 all-gather.8
  209.9 52.5 all-gather.14
  271.4 88.0 all-gather.10
  427.2 75.2 reduce-scatter.3
  552.0 80.0 all-gather.12
  711.1 79.6 reduce-scatter.7
  820.8 74.7 reduce-scatter.5

commit v13 on v12

--- a/solution.py
+++ b/solution.py
@@ -427,6 +427,31 @@
     side = (lax.axis_index("ctx") >> bit) & 1
     r = x.shape[0] // 2
     return lax.dynamic_slice_in_dim(x, (side if mine else 1 - side) * r, r, 0)
+
+
+def assemble_kernel(source_ref, *refs):
+    *in_refs, out_ref = refs
+    for k, ref in enumerate(in_refs):
+
+        @pl.when(source_ref[pl.program_id(0)] == k)
+        def _(ref=ref):
+            out_ref[...] = ref[...]
+
+
+def assemble(pieces, source):
+    r, c = pieces[0].shape
+    count = len(pieces)
+    return pl.pallas_call(
+        assemble_kernel,
+        grid_spec=pltpu.PrefetchScalarGridSpec(
+            num_scalar_prefetch=1, grid=(count,),
+            in_specs=[pl.BlockSpec((r, c), lambda j, _: (0, 0), pipeline_mode=pl.Buffered(1))] * count,
+            out_specs=pl.BlockSpec((r, c), lambda j, _: (j, 0))),
+        out_shape=jax.ShapeDtypeStruct((count * r, c), BF16),
+        compiler_params=pltpu.CompilerParams(vmem_limit_bytes=40 * 2**20),
+        cost_estimate=pl.CostEstimate(flops=0, bytes_accessed=1024, transcendentals=0),
+        name="assemble",
+    )(source, *pieces)
 
 
 def weight_grad(part, flying):
@@ -454,12 +479,15 @@
         flying[:] = got
         gate = yield
         streams, got = after((streams, got), gate)
-        streams = [
-            jnp.where(((lax.axis_index("ctx") >> o[i]) & 1) == 0, jnp.concatenate([x, g]), jnp.concatenate([g, x]))
-            for x, o, g in zip(streams, orders, got)
-        ]
+        sides = [(lax.axis_index("ctx") >> o[i]) & 1 for o in orders]
         if i == 0:
-            streams = jnp.concatenate(streams)
+            source = jnp.stack([sides[0], 1 - sides[0], 2 + sides[1], 3 - sides[1]])
+            streams = assemble([streams[0], got[0], streams[1], got[1]], source)
+        else:
+            streams = [
+                jnp.where(side == 0, jnp.concatenate([x, g]), jnp.concatenate([g, x]))
+                for x, side, g in zip(streams, sides, got)
+            ]
         gate = yield streams
     streams = after(streams, gate)
     other = ctx_swap(streams, 1)
@@ -531,7 +559,7 @@
             in_specs=[pl.BlockSpec((step, c), mine), pl.BlockSpec((step, c), theirs)], out_specs=specs),
         out_shape=shapes,
         compiler_params=pltpu.CompilerParams(vmem_limit_bytes=40 * 2**20),
-        cost_estimate=pl.CostEstimate(flops=0, bytes_accessed=12 * r * c, transcendentals=0),
+        cost_estimate=pl.CostEstimate(flops=0, bytes_accessed=1024, transcendentals=0),
         name="unpack_rows",
     )(core[None], half, other)
 
@@ -559,7 +587,7 @@
             out_specs=pl.BlockSpec((step, 2 * c), lambda i, _: (i, 0))),
         out_shape=jax.ShapeDtypeStruct((r, 2 * c), F32),
         compiler_params=pltpu.CompilerParams(vmem_limit_bytes=40 * 2**20),
-        cost_estimate=pl.CostEstimate(flops=0, bytes_accessed=12 * r * c, transcendentals=0),
+        cost_estimate=pl.CostEstimate(flops=0, bytes_accessed=1024, transcendentals=0),
         name="unpack_cols",
     )((lax.axis_index("ctx") & 1)[None], half, other)
 
@@ -728,7 +756,7 @@
     grad_q = after(grad_q.reshape(-1, width), [grads[j] for j in grads if j > 1])
     grads = gather_cores(grads, grad_q)
     q_part = nt(grad_q, query_w)
-    take(gu, grad_q)
+    grads = after(grads, take(gu, grad_q))
     go(gu, grads)
     first = key_value_grad(place, own, kv, tabs, queries, grads, 0, SEQS // 2)
     grads = after(grads, take(dw, first))
@@ -738,13 +766,12 @@
     grad_k, grad_v = (jnp.concatenate(pair).reshape(-1, width) for pair in zip(first, second))
     part_one = q_part + nt(grad_k, key_w) + nt(grad_v, value_w)
     part_sent = after(part_one.astype(BF16), branch)
-    grad_one = sum_rows(part_sent)
-
     rows_one, branch, grad_q, grad_k, grad_v = after((rows_one, branch, grad_q, grad_k, grad_v), part_sent, gu_fly)
     grad_qkv = jnp.concatenate([grad_q, grad_k, grad_v], axis=1)
     chain = begin(lambda core: jnp.concatenate([rc(columns(rows_one, core), grad_qkv), rc(columns(branch, core), attn_rows)], axis=1))
     held = take(chain)
     go(chain)
+    grad_one = sum_rows(after(part_sent, out_sum, held))
     take(gu, held)
     take_extra(gu)
     go(gu)
@@ -756,25 +783,25 @@
         jnp.where(tp_row, bias_grad[None, :], 0.0).reshape(-1)])
     take(dw, held)
     go(dw)
-    held = take(chain)
+    held = take(chain, out_sum)
     go(chain)
     held = take(chain, list(dw_fly))
     go(chain)
     take(dw, held)
     take_extra(dw)
     go(dw)
-    sums = sum_over_all(after(small, held).reshape(-1, 1024))
-    small = [next(sums) for _ in range(1 + int(math.log2(n_tp)))]
     grad_gate_w, grad_up_w = unpack_rows(*take(gu, held), 2)
-    held = take(chain, (small, grad_gate_w, list(dw_fly)))
+    held = take(chain, (grad_gate_w, list(dw_fly)))
     take_extra(chain)
     go(chain)
     mixed_late, out_sum = after((mixed, out_sum), held)
     out_tokens = (mixed_late + out_sum.astype(F32)).astype(BF16)
     take(dw, held)
     go(dw)
+    sums = sum_over_all(after(small, held).reshape(-1, 1024))
+    small = [next(sums) for _ in range(1 + int(math.log2(n_tp)))]
     grad_down_w = unpack_cols(*take(dw))
-    take(chain, grad_down_w)
+    take(chain, (grad_down_w, small))
     go(chain)
     for _ in range(4):
         small = next(sums)

time: 920 us -> 899 us (0.977)
  other arithmetic: 89.7 us -> 58.8 us
  Pallas kernels: 178 us -> 192 us
    select_n x12 -> x6, other arithmetic: 24.2 us -> 5.85 us  [weight_grad(): jnp.where(side == 0, jnp.concatenate([x, g]), jnp.concatenate([g, x]))]
    pallas_call x0 -> x3, Pallas kernels: none -> 12.6 us  [assemble(): pl.pallas_call(assemble_kernel, grid_spec=pltpu.PrefetchScalarGridSpec(nu...]
    unnamed x208 -> x202, local copies, waits for them, and re-layouts: 21.7 us -> 14.6 us
  transfers between devices with their start and end apart: 75 -> 75, of which waited for: 35 -> 36; matrix products, arithmetic and copies ran while one was open for 20% -> 17% of each run, Pallas kernels for 15% -> 17%
where the time goes in v13:
time: 899 us; the launch traced here: 894 us
  waiting for transfers between devices  410 us (46%)
  Pallas kernels  192 us (21%)
  matrix products  110 us (12%)
  starting transfers between devices  62.1 us (7%)
  other arithmetic  58.8 us (7%)
  local copies, waits for them, and re-layouts  44.9 us (5%)
  between operations  15.9 us (2%)
    ppermute x53, waiting for transfers between devices, ctx_swap(): return lax.ppermute(x, 'ctx', [(i, i ^ mask) for i in range(n)])  219 us
    pallas_call x4, Pallas kernels, attention_call(): pl.pallas_call(kernel, grid_spec=pltpu.PrefetchScalarGridSpec(num_scalar_...  105 us
    all_gather x4, waiting for transfers between devices, all_rows(): return lax.all_gather(x, 'tp', axis=0, tiled=True)  102 us
    dot_general x8, matrix products, rc(): lax.dot_general(left, right, (((0,), (0,)), ((), ())), preferred_element_...  48.7 us
    dot_general x6, matrix products, nt(): lax.dot_general(a, b, (((1,), (1,)), ((), ())), preferred_element_type=jn...  45.9 us
    ppermute x53, starting transfers between devices, ctx_swap(): return lax.ppermute(x, 'ctx', [(i, i ^ mask) for i in range(n)])  43.9 us
    ppermute x6, waiting for transfers between devices, tp_shift(): return lax.ppermute(x, 'tp', [(i, (i + d) % n) for i in range(n)])  33.3 us
    ppermute x3, waiting for transfers between devices, gather_tp(): lax.ppermute(x, 'tp', [(i, (i + d) % n) for i in range(n)])  29.1 us
  transfers between devices with their start and end apart: 75, of which 36 were waited for; matrix products, arithmetic and copies ran while one was open for 17% of the time, Pallas kernels for 17%

profile of v13, /device:TPU:0, one launch (start us, length us, event | category | flops | bytes accessed | tf_op | source)
XLA Modules:
  0.0 893.5 jit_solution(246089738949414751)
XLA Ops:
  12.7 83.6 %all-gather.7.cloned.1.call-done.h_ref = bf16[1024,2048]{1,0:T(8,128)(2,1)} async-done(((bf16[256,2048]{1,0:T(8,128)(2,1)}), bf16[1024,2048]{1,0:T(8,128)(2,1)}) %all-gather.7.cloned.1.call-update) | async-done | bytes 4194320 | tf_op jit(solution)/shard_map/all_gather | solution.py:596
  99.2 11.8 %project.1 = (bf16[4,256,512]{2,1,0:T(8,128)(2,1)S(1)}, bf16[2,4,256,512]{3,2,1,0:T(8,128)(2,1)}) custom-call(bf16[1024,2048]{1,0:T(8,128)(2,1)} %all-gather.7.cloned.1.call-done.h_ref, bf16[2048,512]{1,0:T(8,128)(2,1)} %wq_ref.1, bf16[2048,512]{1,0:T(8,128)(2,1)} %wk_ref.1, bf16[2048,512]{1,0:T(8,128)(2,1)} %wv_ref.1, ...), custom_call_target="tpu_custom_call" | custom-call | flops 6442450944 | bytes 6291456 | tf_op jit(solution)/shard_map/project/pallas_call | solution.py:357
  114.9 44.7 %collective-permute-done.3.refs_4_.refs_12_ = bf16[2,4,2,128,512]{4,3,2,1,0:T(8,128)(2,1)} collective-permute-done((bf16[2,4,2,128,512]{4,3,2,1,0:T(8,128)(2,1)}, bf16[2,4,2,128,512]{4,3,2,1,0:T(8,128)(2,1)}, u32[]{:S(2)}, u32[]{:S(2)}) %collective-permute-start.3) | collective-permute-done | bytes 2097184 | tf_op jit(solution)/shard_map/ppermute | solution.py:413
  163.4 2.3 slice.95
  170.2 9.3 %collective-permute-done.14 = bf16[64,2048]{1,0:T(8,128)(2,1)S(1)} collective-permute-done((bf16[64,2048]{1,0:T(8,128)(2,1)S(1)}, bf16[64,2048]{1,0:T(8,128)(2,1)S(1)}, u32[]{:S(2)}, u32[]{:S(2)}) %collective-permute-start.14) | collective-permute-done | bytes 262176 | tf_op jit(solution)/shard_map/ppermute | solution.py:679
  179.5 19.8 %collective-permute-done.13 = bf16[64,2048]{1,0:T(8,128)(2,1)S(1)} collective-permute-done((bf16[64,2048]{1,0:T(8,128)(2,1)S(1)}, bf16[64,2048]{1,0:T(8,128)(2,1)S(1)}, u32[]{:S(2)}, u32[]{:S(2)}) %collective-permute-start.13) | collective-permute-done | bytes 262176 | tf_op jit(solution)/shard_map/ppermute | solution.py:679
  206.2 3.4 collective-permute-done.8.refs_15_
  211.4 24.1 %attend.1 = (bf16[4,256,512]{2,1,0:T(8,128)(2,1)}, bf16[4,256,128]{2,1,0:T(8,128)(2,1)}) custom-call(s32[4,16]{1,0:T(4,128)} %copy.44.place_ref, s32[4,2]{1,0:T(4,128)} %get-tuple-element.261.own_ref, bf16[4,256,512]{2,1,0:T(8,128)(2,1)} %copy-done.2, bf16[2,4,2,128,512]{4,3,2,1,0:T(8,128)(2,1)} %bitcast.5.refs_0_.refs_8_, ...), custom_call_target="tpu_custom_call" | custom-call | flops 1073741824 | bytes 4194304 | tf_op jit(solution)/shard_map/attend/pallas_call | solution.py:233
  235.6 2.4 constant_dynamic-slice_fusion.16
  238.0 3.8 collective-permute-start.11
  241.8 4.8 collective-permute-done.9
  246.6 11.5 %collective-permute-done.10 = bf16[256,512]{1,0:T(8,128)(2,1)S(1)} collective-permute-done((bf16[256,512]{1,0:T(8,128)(2,1)S(1)}, bf16[256,512]{1,0:T(8,128)(2,1)S(1)}, u32[]{:S(2)}, u32[]{:S(2)}) %collective-permute-start.10) | collective-permute-done | bytes 262176 | tf_op jit(solution)/shard_map/ppermute | solution.py:601
  258.2 4.3 all-gather.15.cloned.1.call-done
  262.5 6.1 fusion.84
  273.8 5.6 collective-permute-start.18
  279.7 25.0 %collective-permute-done.20.refs_6_ = bf16[1,4,2,128,640]{4,3,2,1,0:T(8,128)(2,1)} collective-permute-done((bf16[1,4,2,128,640]{4,3,2,1,0:T(8,128)(2,1)}, bf16[1,4,2,128,640]{4,3,2,1,0:T(8,128)(2,1)}, u32[]{:S(2)}, u32[]{:S(2)}) %collective-permute-start.20) | collective-permute-done | bytes 1310752 | tf_op jit(solution)/shard_map/ppermute | solution.py:413
  305.5 29.4 %collective-permute-done.18.refs_4_ = bf16[1,4,2,128,640]{4,3,2,1,0:T(8,128)(2,1)} collective-permute-done((bf16[1,4,2,128,640]{4,3,2,1,0:T(8,128)(2,1)}, bf16[1,4,2,128,640]{4,3,2,1,0:T(8,128)(2,1)}, u32[]{:S(2)}, u32[]{:S(2)}) %collective-permute-start.18) | collective-permute-done | bytes 1310752 | tf_op jit(solution)/shard_map/ppermute | solution.py:413
  340.2 18.8 %all-gather.11.cloned.1.call-done.h_ref = bf16[1024,2048]{1,0:T(8,128)(2,1)} async-done(((bf16[256,2048]{1,0:T(8,128)(2,1)}), bf16[1024,2048]{1,0:T(8,128)(2,1)}) %all-gather.11.cloned.1.call-update) | async-done | bytes 4194320 | tf_op jit(solution)/shard_map/all_gather | solution.py:596
  358.9 28.9 %mlp.1 = (bf16[1024,1408]{1,0:T(8,128)(2,1)}, bf16[1024,2816]{1,0:T(8,128)(2,1)}) custom-call(bf16[1024,2048]{1,0:T(8,128)(2,1)} %all-gather.11.cloned.1.call-done.h_ref, bf16[1024,2048]{1,0:T(8,128)(2,1)} %all-gather.9.cloned.1.call-done.dy_ref, bf16[2048,1408]{1,0:T(8,128)(2,1)} %gate_ref.1, bf16[2048,1408]{1,0:T(8,128)(2,1)} %up_ref.1, ...), custom_call_target="tpu_custom_call" | custom-call | flops 17716740096 | bytes 38273024 | tf_op jit(solution)/shard_map/mlp/pallas_call | solution.py:397
  387.8 9.7 %fusion.5 = f32[1024,2048]{1,0:T(8,128)S(1)} fusion(bf16[2048,1408]{1,0:T(8,128)(2,1)} %gate_ref.1, bf16[1024,2816]{1,0:T(8,128)(2,1)} %get-tuple-element.147), kind=kOutput, calls=%fused_computation.25 | convolution fusion | flops 5905580032 | bytes 17039360 | tf_op jit(solution)/shard_map/dot_general | solution.py:15
  397.6 11.1 %add_convert_fusion.1 = bf16[1024,2048]{1,0:T(8,128)(2,1)} fusion(f32[1024,2048]{1,0:T(8,128)S(1)} %fusion.5, bf16[2048,1408]{1,0:T(8,128)(2,1)} %up_ref.1, bf16[1024,2816]{1,0:T(8,128)(2,1)S(1)} %copy-done.90), kind=kOutput, calls=%fused_computation.5 | convolution fusion | flops 5909774336 | bytes 21233664 | tf_op jit(solution)/shard_map/dot_general | solution.py:15
  408.7 11.1 %convolution_convert_fusion = bf16[1024,2816]{1,0:T(8,128)(2,1)} fusion(bf16[1024,2816]{1,0:T(8,128)(2,1)} %get-tuple-element.147, bf16[1024,2048]{1,0:T(8,128)(2,1)} %all-gather.11.cloned.1.call-done.h_ref, s32[]{:T(128)S(6)} %select_n.342), kind=kOutput, calls=%fused_computation.8 | convolution fusion | flops 5908463616 | bytes 13631492 | tf_op jit(solution)/shard_map/dot_general | solution.py:302
  419.8 4.5 convolution_convert_fusion.3
  424.9 8.7 collective-permute-done.23
  433.7 6.6 add_convert_fusion.2
  442.2 10.8 %add_convert_fusion = bf16[1024,2816]{1,0:T(8,128)(2,1)S(1)} fusion(bf16[1024,2816]{1,0:T(8,128)(2,1)} %collective-permute-done.22, bf16[1024,2816]{1,0:T(8,128)(2,1)} %get-tuple-element.147, bf16[1024,2048]{1,0:T(8,128)(2,1)S(1)} %copy-done.87, s32[]{:T(128)S(6)} %select_n.341), kind=kOutput, calls=%fused_computation | convolution fusion | flops 5914230784 | bytes 19398660 | tf_op jit(solution)/shard_map/dot_general | solution.py:302
  459.0 8.2 convolution_convert_fusion.1
  467.1 21.6 %collective-permute-done.24 = bf16[256,2816]{1,0:T(8,128)(2,1)} collective-permute-done((bf16[256,2816]{1,0:T(8,128)(2,1)}, bf16[256,2816]{1,0:T(8,128)(2,1)}, u32[]{:S(2)}, u32[]{:S(2)}) %collective-permute-start.24) | collective-permute-done | bytes 1441824 | tf_op jit(solution)/shard_map/ppermute | solution.py:413
  488.7 2.4 collective-permute-done.25
  500.3 2.3 fusion.24
  502.7 2.6 fusion.78
  505.3 6.2 convolution_convert_fusion.4
  511.6 4.3 collective-permute-done.30
  519.2 2.3 collective-permute-start.26
  523.4 12.6 %collective-permute-done.26 = bf16[256,512]{1,0:T(8,128)(2,1)S(1)} collective-permute-done((bf16[256,512]{1,0:T(8,128)(2,1)S(1)}, bf16[256,512]{1,0:T(8,128)(2,1)S(1)}, u32[]{:S(2)}, u32[]{:S(2)}) %collective-permute-start.26) | collective-permute-done | bytes 262176 | tf_op jit(solution)/shard_map/ppermute | solution.py:601
  536.1 4.4 collective-permute-done.27
  547.5 27.9 %query_grad.1 = bf16[4,256,512]{2,1,0:T(8,128)(2,1)} custom-call(s32[4,16]{1,0:T(4,128)} %copy.44.place_ref, s32[4,2]{1,0:T(4,128)} %get-tuple-element.261.own_ref, bf16[4,256,512]{2,1,0:T(8,128)(2,1)} %copy-done.2, bf16[4,256,512]{2,1,0:T(8,128)(2,1)} %bitcast.79, bf16[4,256,128]{2,1,0:T(8,128)(2,1)} %get-tuple-element.140.qx_ref, ...), custom_call_target="tpu_custom_call" | custom-call | flops 1610612736 | bytes 4194304 | tf_op jit(solution)/shard_map/query_grad/pallas_call | solution.py:233
  576.7 24.5 %collective-permute-done.34.refs_12_ = bf16[1,4,2,128,640]{4,3,2,1,0:T(8,128)(2,1)} collective-permute-done((bf16[1,4,2,128,640]{4,3,2,1,0:T(8,128)(2,1)S(1)}, bf16[1,4,2,128,640]{4,3,2,1,0:T(8,128)(2,1)}, u32[]{:S(2)}, u32[]{:S(2)}) %collective-permute-start.34) | collective-permute-done | bytes 1310752 | tf_op jit(solution)/shard_map/ppermute | solution.py:413
  609.3 27.4 %key_value_grad.2 = (bf16[2,256,512]{2,1,0:T(8,128)(2,1)}, bf16[2,256,512]{2,1,0:T(8,128)(2,1)}) custom-call(s32[4,16]{1,0:T(4,128)} %copy.44.place_ref, s32[4,2]{1,0:T(4,128)} %get-tuple-element.261.own_ref, bf16[2,4,256,512]{3,2,1,0:T(8,128)(2,1)} %get-tuple-element.134.kv_ref, f32[1024,128]{1,0:T(8,128)} %copy-done.6, f32[1024,128]{1,0:T(8,128)} %copy-done.5, ...), custom_call_target="tpu_custom_call" | custom-call | flops 1073741824 | bytes 2097152 | tf_op jit(solution)/shard_map/key_value_grad/pallas_call | solution.py:233
  645.8 25.3 %key_value_grad.3 = (bf16[2,256,512]{2,1,0:T(8,128)(2,1)}, bf16[2,256,512]{2,1,0:T(8,128)(2,1)}) custom-call(s32[4,16]{1,0:T(4,128)} %copy.44.place_ref, s32[4,2]{1,0:T(4,128)} %get-tuple-element.261.own_ref, bf16[2,4,256,512]{3,2,1,0:T(8,128)(2,1)} %get-tuple-element.134.kv_ref, f32[1024,128]{1,0:T(8,128)} %copy-done.6, f32[1024,128]{1,0:T(8,128)} %copy-done.5, ...), custom_call_target="tpu_custom_call" | custom-call | flops 1073741824 | bytes 2097152 | tf_op jit(solution)/shard_map/key_value_grad/pallas_call | solution.py:233
  673.2 2.4 fusion.87
  675.7 5.8 fusion.86
  681.4 10.8 %fusion.85 = (bf16[1024,2048]{1,0:T(8,128)(2,1)}, f32[1024,2048]{1,0:T(8,128)}) fusion(f32[1024,2048]{1,0:T(8,128)S(1)} %fusion.87, f32[1024,2048]{1,0:T(8,128)} %fusion.86, bf16[1024,512]{1,0:T(8,128)(2,1)S(1)} %bitcast.77, bf16[2048,512]{1,0:T(8,128)(2,1)S(1)} %copy-done.52), kind=kOutput, calls=%fused_computation.208 | convolution fusion | flops 2153775104 | bytes 32505856 | tf_op jit(solution)/shard_map/dot_general | solution.py:15
  692.2 3.3 fusion.47
  698.9 3.9 convolution_convert_fusion.2
  702.8 2.7 pad_maximum_fusion
  705.5 3.3 fusion.29
  708.8 5.1 fusion.31
  714.0 3.1 fusion
  717.4 6.2 assemble.3.half_ref
  729.6 23.1 %collective-permute-done.47 = bf16[256,2048]{1,0:T(8,128)(2,1)} collective-permute-done((bf16[256,2048]{1,0:T(8,128)(2,1)}, bf16[256,2048]{1,0:T(8,128)(2,1)}, u32[]{:S(2)}, u32[]{:S(2)}) %collective-permute-start.47) | collective-permute-done | bytes 1048608 | tf_op jit(solution)/shard_map/ppermute | solution.py:413
  762.9 12.7 %collective-permute-done.51 = bf16[176,1024]{1,0:T(8,128)(2,1)S(1)} collective-permute-done((bf16[176,1024]{1,0:T(8,128)(2,1)}, bf16[176,1024]{1,0:T(8,128)(2,1)S(1)}, u32[]{:S(2)}, u32[]{:S(2)}) %collective-permute-start.51) | collective-permute-done | bytes 360480 | tf_op jit(solution)/shard_map/ppermute | solution.py:413
  785.7 13.6 %unpack_rows.2 = (f32[2048,1408]{1,0:T(8,128)}, f32[2048,1408]{1,0:T(8,128)}) custom-call(s32[1]{0:T(128)} %bitcast.19.core_ref, bf16[1024,2816]{1,0:T(8,128)(2,1)} %assemble.3.half_ref, bf16[1024,2816]{1,0:T(8,128)(2,1)} %collective-permute-done.55.other_ref), custom_call_target="tpu_custom_call" | custom-call | bytes 1024 | tf_op jit(solution)/shard_map/unpack_rows/pallas_call | solution.py:555
  799.3 10.0 %collective-permute-done.54 = bf16[128,2048]{1,0:T(8,128)(2,1)S(1)} collective-permute-done((bf16[128,2048]{1,0:T(8,128)(2,1)S(1)}, bf16[128,2048]{1,0:T(8,128)(2,1)S(1)}, u32[]{:S(2)}, u32[]{:S(2)}) %collective-permute-start.54) | collective-permute-done | bytes 524320 | tf_op jit(solution)/shard_map/ppermute | solution.py:413
  815.0 4.7 fusion.77
  824.0 2.4 collective-permute-start.59
  826.5 5.5 collective-permute-done.59
  832.0 3.0 collective-permute-start.60
  835.0 8.0 collective-permute-done.60
  843.0 8.8 unpack_cols.1
  851.9 5.5 assemble.5.half_ref
  858.1 3.8 collective-permute-done.61
  872.0 3.1 fusion.18
  875.1 11.4 %unpack_rows.3 = (f32[2048,512]{1,0:T(8,128)}, f32[2048,512]{1,0:T(8,128)}, f32[2048,512]{1,0:T(8,128)}, f32[512,2048]{1,0:T(8,128)}) custom-call(s32[1]{0:T(128)} %bitcast.19.core_ref, bf16[1024,2048]{1,0:T(8,128)(2,1)} %assemble.5.half_ref, bf16[1024,2048]{1,0:T(8,128)(2,1)} %collective-permute-done.66.other_ref), custom_call_target="tpu_custom_call" | custom-call | bytes 1024 | tf_op jit(solution)/shard_map/unpack_rows/pallas_call | solution.py:555
  (436 shorter events, 141.4 us)
Async XLA Ops:
  7.2 89.0 %all-gather.7.cloned.1.call-start = ((), (), s32[]{:S(2)}) async-start(), calls=%async_computation.3 | async-start | bytes 5242880 | tf_op jit(solution)/shard_map/all_gather | solution.py:596
  12.7 197.1 %all-gather.9.cloned.1.call-start = ((), (), s32[]{:S(2)}) async-start(), calls=%async_computation.4 | async-start | bytes 5242880 | tf_op jit(solution)/shard_map/all_gather | solution.py:596
  96.3 166.2 %all-gather.15.cloned.1.call-start = ((), (), s32[]{:S(2)}) async-start(), calls=%async_computation.10 | async-start | bytes 9437184 | tf_op jit(solution)/shard_map/all_gather | solution.py:710
  112.0 47.7 %collective-permute-start.3 = (bf16[2,4,2,128,512]{4,3,2,1,0:T(8,128)(2,1)}, bf16[2,4,2,128,512]{4,3,2,1,0:T(8,128)(2,1)}, u32[]{:S(2)}, u32[]{:S(2)}) collective-permute-start(bf16[2,4,2,128,512]{4,3,2,1,0:T(8,128)(2,1)} %bitcast.5.refs_0_.refs_8_), channel_id=1, source_target_pairs={{0,16},{4,20},{8,24},{12,28},{16,0},{20,4},{24,8},{28,12},{1,17},{... | collective-permute-start | bytes 6291464 | tf_op jit(solution)/shard_map/ppermute | solution.py:413
  113.5 49.9 %collective-permute-start.1 = (bf16[2,4,2,128,512]{4,3,2,1,0:T(8,128)(2,1)}, bf16[2,4,2,128,512]{4,3,2,1,0:T(8,128)(2,1)}, u32[]{:S(2)}, u32[]{:S(2)}) collective-permute-start(bf16[2,4,2,128,512]{4,3,2,1,0:T(8,128)(2,1)} %bitcast.5.refs_0_.refs_8_), channel_id=1, source_target_pairs={{0,8},{4,12},{8,0},{12,4},{16,24},{20,28},{24,16},{28,20},{1,9},{5... | collective-permute-start | bytes 6291464 | tf_op jit(solution)/shard_map/ppermute | solution.py:413
  161.9 40.6 %collective-permute-start.7 = (bf16[1,4,2,128,512]{4,3,2,1,0:T(8,128)(2,1)}, bf16[1,4,2,128,512]{4,3,2,1,0:T(8,128)(2,1)S(1)}, u32[]{:S(2)}, u32[]{:S(2)}) collective-permute-start(bf16[1,4,2,128,512]{4,3,2,1,0:T(8,128)(2,1)} %slice.96), channel_id=1, source_target_pairs={{0,8},{4,12},{8,0},{12,4},{16,24},{20,28},{24,16},{28,20},{1,9},{5... | collective-permute-start | bytes 3145736 | tf_op jit(solution)/shard_map/ppermute | solution.py:413
  165.6 37.4 %collective-permute-start.5 = (bf16[1,4,2,128,512]{4,3,2,1,0:T(8,128)(2,1)}, bf16[1,4,2,128,512]{4,3,2,1,0:T(8,128)(2,1)}, u32[]{:S(2)}, u32[]{:S(2)}) collective-permute-start(bf16[1,4,2,128,512]{4,3,2,1,0:T(8,128)(2,1)} %slice.95), channel_id=1, source_target_pairs={{0,16},{4,20},{8,24},{12,28},{16,0},{20,4},{24,8},{28,12},{1,17},{... | collective-permute-start | bytes 3145736 | tf_op jit(solution)/shard_map/ppermute | solution.py:413
  167.1 12.3 %collective-permute-start.14 = (bf16[64,2048]{1,0:T(8,128)(2,1)S(1)}, bf16[64,2048]{1,0:T(8,128)(2,1)S(1)}, u32[]{:S(2)}, u32[]{:S(2)}) collective-permute-start(bf16[64,2048]{1,0:T(8,128)(2,1)S(1)} %constant_dynamic-slice_fusion.15), channel_id=1, source_target_pairs={{0,3},{1,0},{2,1},{3,2},{4,7},{5,4},{6,5},{7,6},{8,11},{9,8},{10,9... | collective-permute-start | bytes 786440 | tf_op jit(solution)/shard_map/ppermute | solution.py:679
  168.2 31.0 %collective-permute-start.13 = (bf16[64,2048]{1,0:T(8,128)(2,1)S(1)}, bf16[64,2048]{1,0:T(8,128)(2,1)S(1)}, u32[]{:S(2)}, u32[]{:S(2)}) collective-permute-start(bf16[64,2048]{1,0:T(8,128)(2,1)S(1)} %constant_dynamic-slice_fusion.15), channel_id=1, source_target_pairs={{0,2},{1,3},{2,0},{3,1},{4,6},{5,7},{6,4},{7,5},{8,10},{9,11},{10,... | collective-permute-start | bytes 786440 | tf_op jit(solution)/shard_map/ppermute | solution.py:679
  168.2 31.0 %collective-permute-start.12 = (bf16[64,2048]{1,0:T(8,128)(2,1)S(1)}, bf16[64,2048]{1,0:T(8,128)(2,1)S(1)}, u32[]{:S(2)}, u32[]{:S(2)}) collective-permute-start(bf16[64,2048]{1,0:T(8,128)(2,1)S(1)} %constant_dynamic-slice_fusion.15), channel_id=1, source_target_pairs={{0,1},{1,2},{2,3},{3,0},{4,5},{5,6},{6,7},{7,4},{8,9},{9,10},{10,1... | collective-permute-start | bytes 786440 | tf_op jit(solution)/shard_map/ppermute | solution.py:679
  179.5 26.7 %collective-permute-start = (bf16[2,4,2,128,512]{4,3,2,1,0:T(8,128)(2,1)}, bf16[2,4,2,128,512]{4,3,2,1,0:T(8,128)(2,1)S(1)}, u32[]{:S(2)}, u32[]{:S(2)}) collective-permute-start(bf16[2,4,2,128,512]{4,3,2,1,0:T(8,128)(2,1)} %bitcast.5.refs_0_.refs_8_), channel_id=1, source_target_pairs={{0,4},{4,0},{8,12},{12,8},{16,20},{20,16},{24,28},{28,24},{1,5},{5... | collective-permute-start | bytes 6291464 | tf_op jit(solution)/shard_map/ppermute | solution.py:413
  199.3 10.5 %collective-permute-start.4 = (bf16[2,4,2,128,512]{4,3,2,1,0:T(8,128)(2,1)}, bf16[2,4,2,128,512]{4,3,2,1,0:T(8,128)(2,1)}, u32[]{:S(2)}, u32[]{:S(2)}) collective-permute-start(bf16[2,4,2,128,512]{4,3,2,1,0:T(8,128)(2,1)} %collective-permute-done.3.refs_4_.refs_12_), channel_id=1, source_target_pairs={{0,4},{4,0},{8,12},{12,8},{16,20},{20,16},{24,28},{28,24},{1,5},{5... | collective-permute-start | bytes 6291464 | tf_op jit(solution)/shard_map/ppermute | solution.py:413
  200.7 9.1 %collective-permute-start.2 = (bf16[2,4,2,128,512]{4,3,2,1,0:T(8,128)(2,1)}, bf16[2,4,2,128,512]{4,3,2,1,0:T(8,128)(2,1)}, u32[]{:S(2)}, u32[]{:S(2)}) collective-permute-start(bf16[2,4,2,128,512]{4,3,2,1,0:T(8,128)(2,1)} %collective-permute-done.1.refs_2_.refs_10_), channel_id=1, source_target_pairs={{0,4},{4,0},{8,12},{12,8},{16,20},{20,16},{24,28},{28,24},{1,5},{5... | collective-permute-start | bytes 6291464 | tf_op jit(solution)/shard_map/ppermute | solution.py:413
  209.8 149.1 %all-gather.11.cloned.1.call-start = ((), (), s32[]{:S(2)}) async-start(), calls=%async_computation.5 | async-start | bytes 5242880 | tf_op jit(solution)/shard_map/all_gather | solution.py:596
  238.0 8.6 collective-permute-start.9
  238.0 20.1 %collective-permute-start.10 = (bf16[256,512]{1,0:T(8,128)(2,1)S(1)}, bf16[256,512]{1,0:T(8,128)(2,1)S(1)}, u32[]{:S(2)}, u32[]{:S(2)}) collective-permute-start(bf16[256,512]{1,0:T(8,128)(2,1)S(1)} %get-tuple-element.273), channel_id=1, source_target_pairs={{0,2},{1,3},{2,0},{3,1},{4,6},{5,7},{6,4},{7,5},{8,10},{9,11},{10,... | collective-permute-start | bytes 786440 | tf_op jit(solution)/shard_map/ppermute | solution.py:601
  238.0 20.2 %collective-permute-start.11 = (bf16[256,512]{1,0:T(8,128)(2,1)S(1)}, bf16[256,512]{1,0:T(8,128)(2,1)S(1)}, u32[]{:S(2)}, u32[]{:S(2)}) collective-permute-start(bf16[256,512]{1,0:T(8,128)(2,1)S(1)} %get-tuple-element.272), channel_id=1, source_target_pairs={{0,3},{1,0},{2,1},{3,2},{4,7},{5,4},{6,5},{7,6},{8,11},{9,8},{10,9... | collective-permute-start | bytes 786440 | tf_op jit(solution)/shard_map/ppermute | solution.py:601
  270.9 229.5 %reduce-scatter.4.cloned.1.call-start = ((), (), s32[]{:S(2)}) async-start(), calls=%async_computation.6 | async-start | bytes 5242880 | tf_op jit(solution)/shard_map/reduce_scatter | solution.py:624
  272.1 32.6 %collective-permute-start.20 = (bf16[1,4,2,128,640]{4,3,2,1,0:T(8,128)(2,1)}, bf16[1,4,2,128,640]{4,3,2,1,0:T(8,128)(2,1)}, u32[]{:S(2)}, u32[]{:S(2)}) collective-permute-start(bf16[1,4,2,128,640]{4,3,2,1,0:T(8,128)(2,1)} %bitcast.12.refs_0_), channel_id=1, source_target_pairs={{0,24},{4,28},{8,16},{12,20},{16,8},{20,12},{24,0},{28,4},{1,25},{... | collective-permute-start | bytes 3932168 | tf_op jit(solution)/shard_map/ppermute | solution.py:413
  273.8 61.1 %collective-permute-start.18 = (bf16[1,4,2,128,640]{4,3,2,1,0:T(8,128)(2,1)}, bf16[1,4,2,128,640]{4,3,2,1,0:T(8,128)(2,1)}, u32[]{:S(2)}, u32[]{:S(2)}) collective-permute-start(bf16[1,4,2,128,640]{4,3,2,1,0:T(8,128)(2,1)} %bitcast.12.refs_0_), channel_id=1, source_target_pairs={{0,16},{4,20},{8,24},{12,28},{16,0},{20,4},{24,8},{28,12},{1,17},{... | collective-permute-start | bytes 3932168 | tf_op jit(solution)/shard_map/ppermute | solution.py:413
  279.4 56.4 %collective-permute-start.16 = (bf16[1,4,2,128,640]{4,3,2,1,0:T(8,128)(2,1)}, bf16[1,4,2,128,640]{4,3,2,1,0:T(8,128)(2,1)}, u32[]{:S(2)}, u32[]{:S(2)}) collective-permute-start(bf16[1,4,2,128,640]{4,3,2,1,0:T(8,128)(2,1)} %bitcast.12.refs_0_), channel_id=1, source_target_pairs={{0,8},{4,12},{8,0},{12,4},{16,24},{20,28},{24,16},{28,20},{1,9},{5... | collective-permute-start | bytes 3932168 | tf_op jit(solution)/shard_map/ppermute | solution.py:413
  279.4 56.7 %collective-permute-start.15 = (bf16[1,4,2,128,640]{4,3,2,1,0:T(8,128)(2,1)}, bf16[1,4,2,128,640]{4,3,2,1,0:T(8,128)(2,1)}, u32[]{:S(2)}, u32[]{:S(2)}) collective-permute-start(bf16[1,4,2,128,640]{4,3,2,1,0:T(8,128)(2,1)} %bitcast.12.refs_0_), channel_id=1, source_target_pairs={{0,4},{4,0},{8,12},{12,8},{16,20},{20,16},{24,28},{28,24},{1,5},{5... | collective-permute-start | bytes 3932168 | tf_op jit(solution)/shard_map/ppermute | solution.py:413
  304.7 31.4 %collective-permute-start.21 = (bf16[1,4,2,128,640]{4,3,2,1,0:T(8,128)(2,1)}, bf16[1,4,2,128,640]{4,3,2,1,0:T(8,128)(2,1)}, u32[]{:S(2)}, u32[]{:S(2)}) collective-permute-start(bf16[1,4,2,128,640]{4,3,2,1,0:T(8,128)(2,1)} %collective-permute-done.20.refs_6_), channel_id=1, source_target_pairs={{0,4},{4,0},{8,12},{12,8},{16,20},{20,16},{24,28},{28,24},{1,5},{5... | collective-permute-start | bytes 3932168 | tf_op jit(solution)/shard_map/ppermute | solution.py:413
  419.8 22.4 %collective-permute-start.22 = (bf16[1024,2816]{1,0:T(8,128)(2,1)}, bf16[1024,2816]{1,0:T(8,128)(2,1)}, u32[]{:S(2)}, u32[]{:S(2)}) collective-permute-start(bf16[1024,2816]{1,0:T(8,128)(2,1)} %convolution_convert_fusion), channel_id=1, source_target_pairs={{0,4},{4,0},{8,12},{12,8},{16,20},{20,16},{24,28},{28,24},{1,5},{5... | collective-permute-start | bytes 17301512 | tf_op jit(solution)/shard_map/ppermute | solution.py:413
  424.3 9.3 %collective-permute-start.23 = (bf16[1408,1024]{1,0:T(8,128)(2,1)}, bf16[1408,1024]{1,0:T(8,128)(2,1)}, u32[]{:S(2)}, u32[]{:S(2)}) collective-permute-start(bf16[1408,1024]{1,0:T(8,128)(2,1)} %convolution_convert_fusion.3), channel_id=1, source_target_pairs={{0,4},{4,0},{8,12},{12,8},{16,20},{20,16},{24,28},{28,24},{1,5},{5... | collective-permute-start | bytes 8650760 | tf_op jit(solution)/shard_map/ppermute | solution.py:413
  424.9 267.3 %all-gather.13.cloned.1.call-start = ((), (), s32[]{:S(2)}) async-start(), calls=%async_computation.8 | async-start | bytes 5242880 | tf_op jit(solution)/shard_map/all_gather | solution.py:596
  454.8 33.9 %collective-permute-start.24 = (bf16[256,2816]{1,0:T(8,128)(2,1)}, bf16[256,2816]{1,0:T(8,128)(2,1)}, u32[]{:S(2)}, u32[]{:S(2)}) collective-permute-start(bf16[256,2816]{1,0:T(8,128)(2,1)} %constant_dynamic-slice_fusion.14), channel_id=1, source_target_pairs={{0,8},{4,12},{8,0},{12,4},{16,24},{20,28},{24,16},{28,20},{1,9},{5... | collective-permute-start | bytes 4325384 | tf_op jit(solution)/shard_map/ppermute | solution.py:413
  457.5 33.7 %collective-permute-start.25 = (bf16[256,2816]{1,0:T(8,128)(2,1)}, bf16[256,2816]{1,0:T(8,128)(2,1)}, u32[]{:S(2)}, u32[]{:S(2)}) collective-permute-start(bf16[256,2816]{1,0:T(8,128)(2,1)} %constant_dynamic-slice_fusion.13), channel_id=1, source_target_pairs={{0,16},{4,20},{8,24},{12,28},{16,0},{20,4},{24,8},{28,12},{1,17},{... | collective-permute-start | bytes 4325384 | tf_op jit(solution)/shard_map/ppermute | solution.py:413
  494.3 17.3 %collective-permute-start.29 = (bf16[128,2816]{1,0:T(8,128)(2,1)}, bf16[128,2816]{1,0:T(8,128)(2,1)}, u32[]{:S(2)}, u32[]{:S(2)}) collective-permute-start(bf16[128,2816]{1,0:T(8,128)(2,1)} %constant_dynamic-slice_fusion.9), channel_id=1, source_target_pairs={{0,16},{4,20},{8,24},{12,28},{16,0},{20,4},{24,8},{28,12},{1,17},{... | collective-permute-start | bytes 2162696 | tf_op jit(solution)/shard_map/ppermute | solution.py:413
  498.8 17.1 %collective-permute-start.30 = (bf16[128,2816]{1,0:T(8,128)(2,1)}, bf16[128,2816]{1,0:T(8,128)(2,1)}, u32[]{:S(2)}, u32[]{:S(2)}) collective-permute-start(bf16[128,2816]{1,0:T(8,128)(2,1)} %constant_dynamic-slice_fusion.8), channel_id=1, source_target_pairs={{0,8},{4,12},{8,0},{12,4},{16,24},{20,28},{24,16},{28,20},{1,9},{5... | collective-permute-start | bytes 2162696 | tf_op jit(solution)/shard_map/ppermute | solution.py:413
  517.2 24.8 %collective-permute-start.32 = (bf16[128,2816]{1,0:T(8,128)(2,1)S(1)}, bf16[128,2816]{1,0:T(8,128)(2,1)S(1)}, u32[]{:S(2)}, u32[]{:S(2)}) collective-permute-start(bf16[128,2816]{1,0:T(8,128)(2,1)S(1)} %add_convert_fusion.11), channel_id=1, source_target_pairs={{0,8},{4,12},{8,0},{12,4},{16,24},{20,28},{24,16},{28,20},{1,9},{5... | collective-permute-start | bytes 2162696 | tf_op jit(solution)/shard_map/ppermute | solution.py:413
  518.1 22.4 %collective-permute-start.28 = (bf16[256,512]{1,0:T(8,128)(2,1)S(1)}, bf16[256,512]{1,0:T(8,128)(2,1)S(1)}, u32[]{:S(2)}, u32[]{:S(2)}) collective-permute-start(bf16[256,512]{1,0:T(8,128)(2,1)S(1)} %get-tuple-element.268), channel_id=1, source_target_pairs={{0,3},{1,0},{2,1},{3,2},{4,7},{5,4},{6,5},{7,6},{8,11},{9,8},{10,9... | collective-permute-start | bytes 786440 | tf_op jit(solution)/shard_map/ppermute | solution.py:601
  518.9 21.5 %collective-permute-start.27 = (bf16[256,512]{1,0:T(8,128)(2,1)S(1)}, bf16[256,512]{1,0:T(8,128)(2,1)S(1)}, u32[]{:S(2)}, u32[]{:S(2)}) collective-permute-start(bf16[256,512]{1,0:T(8,128)(2,1)S(1)} %get-tuple-element.269), channel_id=1, source_target_pairs={{0,2},{1,3},{2,0},{3,1},{4,6},{5,7},{6,4},{7,5},{8,10},{9,11},{10,... | collective-permute-start | bytes 786440 | tf_op jit(solution)/shard_map/ppermute | solution.py:601
  519.2 16.9 %collective-permute-start.26 = (bf16[256,512]{1,0:T(8,128)(2,1)S(1)}, bf16[256,512]{1,0:T(8,128)(2,1)S(1)}, u32[]{:S(2)}, u32[]{:S(2)}) collective-permute-start(bf16[256,512]{1,0:T(8,128)(2,1)S(1)} %get-tuple-element.270), channel_id=1, source_target_pairs={{0,1},{1,2},{2,3},{3,0},{4,5},{5,6},{6,7},{7,4},{8,9},{9,10},{10,1... | collective-permute-start | bytes 786440 | tf_op jit(solution)/shard_map/ppermute | solution.py:601
  522.8 19.3 %collective-permute-start.31 = (bf16[128,2816]{1,0:T(8,128)(2,1)S(1)}, bf16[128,2816]{1,0:T(8,128)(2,1)S(1)}, u32[]{:S(2)}, u32[]{:S(2)}) collective-permute-start(bf16[128,2816]{1,0:T(8,128)(2,1)S(1)} %add_convert_fusion.12), channel_id=1, source_target_pairs={{0,16},{4,20},{8,24},{12,28},{16,0},{20,4},{24,8},{28,12},{1,17},{... | collective-permute-start | bytes 2162696 | tf_op jit(solution)/shard_map/ppermute | solution.py:413
  543.9 185.8 %reduce-scatter.6.cloned.1.call-start = ((), (), s32[]{:S(2)}) async-start(), calls=%async_computation.7 | async-start | bytes 5242880 | tf_op jit(solution)/shard_map/reduce_scatter | solution.py:624
  543.9 32.8 %collective-permute-start.35 = (bf16[1,4,2,128,640]{4,3,2,1,0:T(8,128)(2,1)S(1)}, bf16[1,4,2,128,640]{4,3,2,1,0:T(8,128)(2,1)}, u32[]{:S(2)}, u32[]{:S(2)}) collective-permute-start(bf16[1,4,2,128,640]{4,3,2,1,0:T(8,128)(2,1)S(1)} %bitcast.71), channel_id=1, source_target_pairs={{0,24},{4,28},{8,16},{12,20},{16,8},{20,12},{24,0},{28,4},{1,25},{... | collective-permute-start | bytes 3932168 | tf_op jit(solution)/shard_map/ppermute | solution.py:413
  545.4 55.7 %collective-permute-start.34 = (bf16[1,4,2,128,640]{4,3,2,1,0:T(8,128)(2,1)S(1)}, bf16[1,4,2,128,640]{4,3,2,1,0:T(8,128)(2,1)}, u32[]{:S(2)}, u32[]{:S(2)}) collective-permute-start(bf16[1,4,2,128,640]{4,3,2,1,0:T(8,128)(2,1)S(1)} %bitcast.72), channel_id=1, source_target_pairs={{0,16},{4,20},{8,24},{12,28},{16,0},{20,4},{24,8},{28,12},{1,17},{... | collective-permute-start | bytes 3932168 | tf_op jit(solution)/shard_map/ppermute | solution.py:413
  546.5 55.7 %collective-permute-start.33 = (bf16[1,4,2,128,640]{4,3,2,1,0:T(8,128)(2,1)S(1)}, bf16[1,4,2,128,640]{4,3,2,1,0:T(8,128)(2,1)}, u32[]{:S(2)}, u32[]{:S(2)}) collective-permute-start(bf16[1,4,2,128,640]{4,3,2,1,0:T(8,128)(2,1)S(1)} %bitcast.73), channel_id=1, source_target_pairs={{0,8},{4,12},{8,0},{12,4},{16,24},{20,28},{24,16},{28,20},{1,9},{5... | collective-permute-start | bytes 3932168 | tf_op jit(solution)/shard_map/ppermute | solution.py:413
  547.5 58.7 %collective-permute-start.36 = (bf16[1,4,2,128,640]{4,3,2,1,0:T(8,128)(2,1)S(1)}, bf16[1,4,2,128,640]{4,3,2,1,0:T(8,128)(2,1)}, u32[]{:S(2)}, u32[]{:S(2)}) collective-permute-start(bf16[1,4,2,128,640]{4,3,2,1,0:T(8,128)(2,1)S(1)} %bitcast.74), channel_id=1, source_target_pairs={{0,4},{4,0},{8,12},{12,8},{16,20},{20,16},{24,28},{28,24},{1,5},{5... | collective-permute-start | bytes 3932168 | tf_op jit(solution)/shard_map/ppermute | solution.py:413
  603.6 33.1 %collective-permute-start.41 = (bf16[352,1024]{1,0:T(8,128)(2,1)}, bf16[352,1024]{1,0:T(8,128)(2,1)}, u32[]{:S(2)}, u32[]{:S(2)}) collective-permute-start(bf16[352,1024]{1,0:T(8,128)(2,1)} %constant_dynamic-slice_fusion.6), channel_id=1, source_target_pairs={{0,16},{4,20},{8,24},{12,28},{16,0},{20,4},{24,8},{28,12},{1,17},{... | collective-permute-start | bytes 2162696 | tf_op jit(solution)/shard_map/ppermute | solution.py:413
  606.2 30.5 %collective-permute-start.40 = (bf16[352,1024]{1,0:T(8,128)(2,1)}, bf16[352,1024]{1,0:T(8,128)(2,1)}, u32[]{:S(2)}, u32[]{:S(2)}) collective-permute-start(bf16[352,1024]{1,0:T(8,128)(2,1)} %constant_dynamic-slice_fusion.7), channel_id=1, source_target_pairs={{0,8},{4,12},{8,0},{12,4},{16,24},{20,28},{24,16},{28,20},{1,9},{5... | collective-permute-start | bytes 2162696 | tf_op jit(solution)/shard_map/ppermute | solution.py:413
  639.3 31.9 %collective-permute-start.42 = (bf16[176,1024]{1,0:T(8,128)(2,1)}, bf16[176,1024]{1,0:T(8,128)(2,1)}, u32[]{:S(2)}, u32[]{:S(2)}) collective-permute-start(bf16[176,1024]{1,0:T(8,128)(2,1)} %constant_dynamic-slice_fusion.5), channel_id=1, source_target_pairs={{0,16},{4,20},{8,24},{12,28},{16,0},{20,4},{24,8},{28,12},{1,17},{... | collective-permute-start | bytes 1081352 | tf_op jit(solution)/shard_map/ppermute | solution.py:413
  641.6 29.5 %collective-permute-start.43 = (bf16[176,1024]{1,0:T(8,128)(2,1)}, bf16[176,1024]{1,0:T(8,128)(2,1)}, u32[]{:S(2)}, u32[]{:S(2)}) collective-permute-start(bf16[176,1024]{1,0:T(8,128)(2,1)} %constant_dynamic-slice_fusion.4), channel_id=1, source_target_pairs={{0,8},{4,12},{8,0},{12,4},{16,24},{20,28},{24,16},{28,20},{1,9},{5... | collective-permute-start | bytes 1081352 | tf_op jit(solution)/shard_map/ppermute | solution.py:413
  641.7 228.4 %reduce-scatter.8.cloned.1.call-start = ((), (), s32[]{:S(2)}) async-start(), calls=%async_computation.9 | async-start | bytes 5242880 | tf_op jit(solution)/shard_map/reduce_scatter | solution.py:624
  641.7 50.5 %collective-permute-start.44 = (bf16[256,2816]{1,0:T(8,128)(2,1)S(1)}, bf16[256,2816]{1,0:T(8,128)(2,1)}, u32[]{:S(2)}, u32[]{:S(2)}) collective-permute-start(bf16[256,2816]{1,0:T(8,128)(2,1)S(1)} %maximum_select_fusion.refs_0_), channel_id=1, source_target_pairs={{0,8},{4,12},{8,0},{12,4},{16,24},{20,28},{24,16},{28,20},{1,9},{5... | collective-permute-start | bytes 4325384 | tf_op jit(solution)/shard_map/ppermute | solution.py:413
  643.8 48.4 %collective-permute-start.45 = (bf16[256,2816]{1,0:T(8,128)(2,1)S(1)}, bf16[256,2816]{1,0:T(8,128)(2,1)}, u32[]{:S(2)}, u32[]{:S(2)}) collective-permute-start(bf16[256,2816]{1,0:T(8,128)(2,1)S(1)} %maximum_select_fusion.1.refs_2_), channel_id=1, source_target_pairs={{0,16},{4,20},{8,24},{12,28},{16,0},{20,4},{24,8},{28,12},{1,17},{... | collective-permute-start | bytes 4325384 | tf_op jit(solution)/shard_map/ppermute | solution.py:413
  705.4 8.5 collective-permute-start.46
  723.6 62.1 %collective-permute-start.55 = (bf16[1024,2816]{1,0:T(8,128)(2,1)}, bf16[1024,2816]{1,0:T(8,128)(2,1)}, u32[]{:S(2)}, u32[]{:S(2)}) collective-permute-start(bf16[1024,2816]{1,0:T(8,128)(2,1)} %assemble.3.half_ref), channel_id=1, source_target_pairs={{0,4},{4,0},{8,12},{12,8},{16,20},{20,16},{24,28},{28,24},{1,5},{5... | collective-permute-start | bytes 17301512 | tf_op jit(solution)/shard_map/ppermute | solution.py:413
  726.4 26.3 %collective-permute-start.47 = (bf16[256,2048]{1,0:T(8,128)(2,1)}, bf16[256,2048]{1,0:T(8,128)(2,1)}, u32[]{:S(2)}, u32[]{:S(2)}) collective-permute-start(bf16[256,2048]{1,0:T(8,128)(2,1)} %constant_dynamic-slice_fusion.3), channel_id=1, source_target_pairs={{0,8},{4,12},{8,0},{12,4},{16,24},{20,28},{24,16},{28,20},{1,9},{5... | collective-permute-start | bytes 3145736 | tf_op jit(solution)/shard_map/ppermute | solution.py:413
  726.4 26.3 %collective-permute-start.48 = (bf16[256,2048]{1,0:T(8,128)(2,1)}, bf16[256,2048]{1,0:T(8,128)(2,1)}, u32[]{:S(2)}, u32[]{:S(2)}) collective-permute-start(bf16[256,2048]{1,0:T(8,128)(2,1)} %constant_dynamic-slice_fusion.2), channel_id=1, source_target_pairs={{0,16},{4,20},{8,24},{12,28},{16,0},{20,4},{24,8},{28,12},{1,17},{... | collective-permute-start | bytes 3145736 | tf_op jit(solution)/shard_map/ppermute | solution.py:413
  727.7 35.2 %collective-permute-start.52 = (bf16[176,1024]{1,0:T(8,128)(2,1)S(1)}, bf16[176,1024]{1,0:T(8,128)(2,1)}, u32[]{:S(2)}, u32[]{:S(2)}) collective-permute-start(bf16[176,1024]{1,0:T(8,128)(2,1)S(1)} %add_convert_fusion.15), channel_id=1, source_target_pairs={{0,8},{4,12},{8,0},{12,4},{16,24},{20,28},{24,16},{28,20},{1,9},{5... | collective-permute-start | bytes 1081352 | tf_op jit(solution)/shard_map/ppermute | solution.py:413
  755.6 20.0 %collective-permute-start.49 = (bf16[128,2048]{1,0:T(8,128)(2,1)}, bf16[128,2048]{1,0:T(8,128)(2,1)}, u32[]{:S(2)}, u32[]{:S(2)}) collective-permute-start(bf16[128,2048]{1,0:T(8,128)(2,1)} %constant_dynamic-slice_fusion.1), channel_id=1, source_target_pairs={{0,16},{4,20},{8,24},{12,28},{16,0},{20,4},{24,8},{28,12},{1,17},{... | collective-permute-start | bytes 1572872 | tf_op jit(solution)/shard_map/ppermute | solution.py:413
  758.2 18.1 %collective-permute-start.50 = (bf16[128,2048]{1,0:T(8,128)(2,1)}, bf16[128,2048]{1,0:T(8,128)(2,1)}, u32[]{:S(2)}, u32[]{:S(2)}) collective-permute-start(bf16[128,2048]{1,0:T(8,128)(2,1)} %constant_dynamic-slice_fusion), channel_id=1, source_target_pairs={{0,8},{4,12},{8,0},{12,4},{16,24},{20,28},{24,16},{28,20},{1,9},{5... | collective-permute-start | bytes 1572872 | tf_op jit(solution)/shard_map/ppermute | solution.py:413
  761.1 14.5 %collective-permute-start.51 = (bf16[176,1024]{1,0:T(8,128)(2,1)}, bf16[176,1024]{1,0:T(8,128)(2,1)S(1)}, u32[]{:S(2)}, u32[]{:S(2)}) collective-permute-start(bf16[176,1024]{1,0:T(8,128)(2,1)} %add_convert_fusion.16), channel_id=1, source_target_pairs={{0,16},{4,20},{8,24},{12,28},{16,0},{20,4},{24,8},{28,12},{1,17},{... | collective-permute-start | bytes 1081352 | tf_op jit(solution)/shard_map/ppermute | solution.py:413
  780.2 29.1 %collective-permute-start.57 = (bf16[352,1024]{1,0:T(8,128)(2,1)S(1)}, bf16[352,1024]{1,0:T(8,128)(2,1)S(1)}, u32[]{:S(2)}, u32[]{:S(2)}) collective-permute-start(bf16[352,1024]{1,0:T(8,128)(2,1)S(1)} %maximum_select_fusion.5.refs_2_), channel_id=1, source_target_pairs={{0,16},{4,20},{8,24},{12,28},{16,0},{20,4},{24,8},{28,12},{1,17},{... | collective-permute-start | bytes 2162696 | tf_op jit(solution)/shard_map/ppermute | solution.py:413
  782.0 27.3 %collective-permute-start.56 = (bf16[352,1024]{1,0:T(8,128)(2,1)S(1)}, bf16[352,1024]{1,0:T(8,128)(2,1)S(1)}, u32[]{:S(2)}, u32[]{:S(2)}) collective-permute-start(bf16[352,1024]{1,0:T(8,128)(2,1)S(1)} %maximum_select_fusion.4.refs_0_), channel_id=1, source_target_pairs={{0,8},{4,12},{8,0},{12,4},{16,24},{20,28},{24,16},{28,20},{1,9},{5... | collective-permute-start | bytes 2162696 | tf_op jit(solution)/shard_map/ppermute | solution.py:413
  783.7 25.6 %collective-permute-start.54 = (bf16[128,2048]{1,0:T(8,128)(2,1)S(1)}, bf16[128,2048]{1,0:T(8,128)(2,1)S(1)}, u32[]{:S(2)}, u32[]{:S(2)}) collective-permute-start(bf16[128,2048]{1,0:T(8,128)(2,1)S(1)} %add_convert_fusion.13), channel_id=1, source_target_pairs={{0,8},{4,12},{8,0},{12,4},{16,24},{20,28},{24,16},{28,20},{1,9},{5... | collective-permute-start | bytes 1572872 | tf_op jit(solution)/shard_map/ppermute | solution.py:413
  784.1 25.2 %collective-permute-start.53 = (bf16[128,2048]{1,0:T(8,128)(2,1)S(1)}, bf16[128,2048]{1,0:T(8,128)(2,1)S(1)}, u32[]{:S(2)}, u32[]{:S(2)}) collective-permute-start(bf16[128,2048]{1,0:T(8,128)(2,1)S(1)} %add_convert_fusion.14), channel_id=1, source_target_pairs={{0,16},{4,20},{8,24},{12,28},{16,0},{20,4},{24,8},{28,12},{1,17},{... | collective-permute-start | bytes 1572872 | tf_op jit(solution)/shard_map/ppermute | solution.py:413
  812.7 30.3 %collective-permute-start.65 = (bf16[1408,1024]{1,0:T(8,128)(2,1)S(1)}, bf16[1408,1024]{1,0:T(8,128)(2,1)}, u32[]{:S(2)}, u32[]{:S(2)}) collective-permute-start(bf16[1408,1024]{1,0:T(8,128)(2,1)S(1)} %assemble.4.half_ref), channel_id=1, source_target_pairs={{0,4},{4,0},{8,12},{12,8},{16,20},{20,16},{24,28},{28,24},{1,5},{5... | collective-permute-start | bytes 8650760 | tf_op jit(solution)/shard_map/ppermute | solution.py:413
  819.6 32.2 %collective-permute-start.64 = (bf16[256,2048]{1,0:T(8,128)(2,1)}, bf16[256,2048]{1,0:T(8,128)(2,1)}, u32[]{:S(2)}, u32[]{:S(2)}) collective-permute-start(bf16[256,2048]{1,0:T(8,128)(2,1)} %maximum_select_fusion.3.refs_2_), channel_id=1, source_target_pairs={{0,16},{4,20},{8,24},{12,28},{16,0},{20,4},{24,8},{28,12},{1,17},{... | collective-permute-start | bytes 3145736 | tf_op jit(solution)/shard_map/ppermute | solution.py:413
  820.8 31.1 %collective-permute-start.63 = (bf16[256,2048]{1,0:T(8,128)(2,1)}, bf16[256,2048]{1,0:T(8,128)(2,1)}, u32[]{:S(2)}, u32[]{:S(2)}) collective-permute-start(bf16[256,2048]{1,0:T(8,128)(2,1)} %maximum_select_fusion.2.refs_0_), channel_id=1, source_target_pairs={{0,8},{4,12},{8,0},{12,4},{16,24},{20,28},{24,16},{28,20},{1,9},{5... | collective-permute-start | bytes 3145736 | tf_op jit(solution)/shard_map/ppermute | solution.py:413
  832.0 11.0 %collective-permute-start.60 = (f32[14,1024]{1,0:T(8,128)S(1)}, f32[14,1024]{1,0:T(8,128)S(1)}, u32[]{:S(2)}, u32[]{:S(2)}) collective-permute-start(f32[14,1024]{1,0:T(8,128)S(1)} %add.461), channel_id=1, source_target_pairs={{0,2},{1,3},{2,0},{3,1},{4,6},{5,7},{6,4},{7,5},{8,10},{9,11},{10,... | collective-permute-start | bytes 172040 | tf_op jit(solution)/shard_map/ppermute | solution.py:669
  857.4 17.7 %collective-permute-start.66 = (bf16[1024,2048]{1,0:T(8,128)(2,1)}, bf16[1024,2048]{1,0:T(8,128)(2,1)}, u32[]{:S(2)}, u32[]{:S(2)}) collective-permute-start(bf16[1024,2048]{1,0:T(8,128)(2,1)} %assemble.5.half_ref), channel_id=1, source_target_pairs={{0,4},{4,0},{8,12},{12,8},{16,20},{20,16},{24,28},{28,24},{1,5},{5... | collective-permute-start | bytes 12582920 | tf_op jit(solution)/shard_map/ppermute | solution.py:413
  (106 other events, 1450.8 us)
Sparse Core Ops, SparseCore 0:
  12.8 83.4 all-gather.6
  97.8 85.6 all-gather.8
  209.9 52.5 all-gather.14
  271.0 87.9 all-gather.10
  425.0 75.2 reduce-scatter.3
  544.0 80.0 all-gather.12
  641.8 79.6 reduce-scatter.5
  763.0 80.2 reduce-scatter.7

commit v14 on v13

--- a/solution.py
+++ b/solution.py
@@ -762,46 +762,45 @@
     grads = after(grads, take(dw, first))
     go(dw)
     second = key_value_grad(place, own, kv, tabs, queries, grads, SEQS // 2, SEQS // 2)
-    second = after(second, dw_fly)
+    second = after(second, take(dw, second))
+    go(dw)
     grad_k, grad_v = (jnp.concatenate(pair).reshape(-1, width) for pair in zip(first, second))
     part_one = q_part + nt(grad_k, key_w) + nt(grad_v, value_w)
     part_sent = after(part_one.astype(BF16), branch)
-    rows_one, branch, grad_q, grad_k, grad_v = after((rows_one, branch, grad_q, grad_k, grad_v), part_sent, gu_fly)
+    rows_one, branch, grad_q, grad_k, grad_v = after((rows_one, branch, grad_q, grad_k, grad_v), part_sent, gu_fly, dw_fly)
     grad_qkv = jnp.concatenate([grad_q, grad_k, grad_v], axis=1)
     chain = begin(lambda core: jnp.concatenate([rc(columns(rows_one, core), grad_qkv), rc(columns(branch, core), attn_rows)], axis=1))
-    held = take(chain)
+    take(dw, part_sent)
+    go(dw)
+    held = take(chain, (list(dw_fly), out_sum))
     go(chain)
     grad_one = sum_rows(after(part_sent, out_sum, held))
     take(gu, held)
     take_extra(gu)
     go(gu)
+    take(dw, held)
+    take_extra(dw)
+    go(dw)
     unit_rows = (rows_one.astype(F32) - shift_one) / gain_one
     bias_grad = jnp.sum(grad_qkv.astype(F32), axis=0)
     tp_row = (jnp.arange(n_tp) == lax.axis_index("tp"))[:, None]
     small = jnp.concatenate([
         jnp.sum(part_one * unit_rows, axis=0), jnp.sum(part_one, axis=0), grad_gain_two, grad_shift_two,
         jnp.where(tp_row, bias_grad[None, :], 0.0).reshape(-1)])
-    take(dw, held)
-    go(dw)
-    held = take(chain, out_sum)
+    held = take(chain)
     go(chain)
-    held = take(chain, list(dw_fly))
+    held = take(chain)
     go(chain)
-    take(dw, held)
-    take_extra(dw)
-    go(dw)
-    grad_gate_w, grad_up_w = unpack_rows(*take(gu, held), 2)
-    held = take(chain, (grad_gate_w, list(dw_fly)))
+    grad_down_w = unpack_cols(*take(dw, held))
+    held = take(chain, grad_down_w)
     take_extra(chain)
     go(chain)
     mixed_late, out_sum = after((mixed, out_sum), held)
     out_tokens = (mixed_late + out_sum.astype(F32)).astype(BF16)
-    take(dw, held)
-    go(dw)
+    grad_gate_w, grad_up_w = unpack_rows(*take(gu, held), 2)
     sums = sum_over_all(after(small, held).reshape(-1, 1024))
     small = [next(sums) for _ in range(1 + int(math.log2(n_tp)))]
-    grad_down_w = unpack_cols(*take(dw))
-    take(chain, (grad_down_w, small))
+    take(chain, (grad_gate_w, small))
     go(chain)
     for _ in range(4):
         small = next(sums)

time: 899 us -> 877 us (0.976)
  waiting for transfers between devices: 410 us -> 385 us
    ppermute x53, waiting for transfers between devices: 219 us -> 198 us  [ctx_swap(): return lax.ppermute(x, 'ctx', [(i, i ^ mask) for i in range(n)])]
where the time goes in v14:
time: 877 us; the launch traced here: 869 us
  waiting for transfers between devices  385 us (44%)
  Pallas kernels  190 us (22%)
  matrix products  111 us (13%)
  starting transfers between devices  67.1 us (8%)
  other arithmetic  56.2 us (6%)
  local copies, waits for them, and re-layouts  44.9 us (5%)
  between operations  15.9 us (2%)
    ppermute x53, waiting for transfers between devices, ctx_swap(): return lax.ppermute(x, 'ctx', [(i, i ^ mask) for i in range(n)])  198 us
    pallas_call x4, Pallas kernels, attention_call(): pl.pallas_call(kernel, grid_spec=pltpu.PrefetchScalarGridSpec(num_scalar_...  107 us
    all_gather x4, waiting for transfers between devices, all_rows(): return lax.all_gather(x, 'tp', axis=0, tiled=True)  103 us
    dot_general x8, matrix products, rc(): lax.dot_general(left, right, (((0,), (0,)), ((), ())), preferred_element_...  49 us
    ppermute x53, starting transfers between devices, ctx_swap(): return lax.ppermute(x, 'ctx', [(i, i ^ mask) for i in range(n)])  47.9 us
    dot_general x6, matrix products, nt(): lax.dot_general(a, b, (((1,), (1,)), ((), ())), preferred_element_type=jn...  45.9 us
    ppermute x6, waiting for transfers between devices, tp_shift(): return lax.ppermute(x, 'tp', [(i, (i + d) % n) for i in range(n)])  34 us
    ppermute x3, waiting for transfers between devices, gather_tp(): lax.ppermute(x, 'tp', [(i, (i + d) % n) for i in range(n)])  29.1 us
  transfers between devices with their start and end apart: 75, of which 36 were waited for; matrix products, arithmetic and copies ran while one was open for 17% of the time, Pallas kernels for 17%

profile of v14, /device:TPU:0, one launch (start us, length us, event | category | flops | bytes accessed | tf_op | source)
XLA Modules:
  0.0 869.0 jit_solution(16647815346774188134)
XLA Ops:
  12.7 83.6 %all-gather.7.cloned.1.call-done.h_ref = bf16[1024,2048]{1,0:T(8,128)(2,1)} async-done(((bf16[256,2048]{1,0:T(8,128)(2,1)}), bf16[1024,2048]{1,0:T(8,128)(2,1)}) %all-gather.7.cloned.1.call-update) | async-done | bytes 4194320 | tf_op jit(solution)/shard_map/all_gather | solution.py:596
  99.2 11.8 %project.1 = (bf16[4,256,512]{2,1,0:T(8,128)(2,1)S(1)}, bf16[2,4,256,512]{3,2,1,0:T(8,128)(2,1)}) custom-call(bf16[1024,2048]{1,0:T(8,128)(2,1)} %all-gather.7.cloned.1.call-done.h_ref, bf16[2048,512]{1,0:T(8,128)(2,1)} %wq_ref.1, bf16[2048,512]{1,0:T(8,128)(2,1)} %wk_ref.1, bf16[2048,512]{1,0:T(8,128)(2,1)} %wv_ref.1, ...), custom_call_target="tpu_custom_call" | custom-call | flops 6442450944 | bytes 6291456 | tf_op jit(solution)/shard_map/project/pallas_call | solution.py:357
  114.9 44.7 %collective-permute-done.3.refs_4_.refs_12_ = bf16[2,4,2,128,512]{4,3,2,1,0:T(8,128)(2,1)} collective-permute-done((bf16[2,4,2,128,512]{4,3,2,1,0:T(8,128)(2,1)}, bf16[2,4,2,128,512]{4,3,2,1,0:T(8,128)(2,1)}, u32[]{:S(2)}, u32[]{:S(2)}) %collective-permute-start.3) | collective-permute-done | bytes 2097184 | tf_op jit(solution)/shard_map/ppermute | solution.py:413
  170.2 9.3 %collective-permute-done.14 = bf16[64,2048]{1,0:T(8,128)(2,1)S(1)} collective-permute-done((bf16[64,2048]{1,0:T(8,128)(2,1)S(1)}, bf16[64,2048]{1,0:T(8,128)(2,1)S(1)}, u32[]{:S(2)}, u32[]{:S(2)}) %collective-permute-start.14) | collective-permute-done | bytes 262176 | tf_op jit(solution)/shard_map/ppermute | solution.py:679
  179.5 19.8 %collective-permute-done.13 = bf16[64,2048]{1,0:T(8,128)(2,1)S(1)} collective-permute-done((bf16[64,2048]{1,0:T(8,128)(2,1)S(1)}, bf16[64,2048]{1,0:T(8,128)(2,1)S(1)}, u32[]{:S(2)}, u32[]{:S(2)}) %collective-permute-start.13) | collective-permute-done | bytes 262176 | tf_op jit(solution)/shard_map/ppermute | solution.py:679
  206.2 3.4 collective-permute-done.8.refs_15_
  211.4 27.0 %attend.1 = (bf16[4,256,512]{2,1,0:T(8,128)(2,1)}, bf16[4,256,128]{2,1,0:T(8,128)(2,1)}) custom-call(s32[4,16]{1,0:T(4,128)} %copy.44.place_ref, s32[4,2]{1,0:T(4,128)} %get-tuple-element.251.own_ref, bf16[4,256,512]{2,1,0:T(8,128)(2,1)} %copy-done.2, bf16[2,4,2,128,512]{4,3,2,1,0:T(8,128)(2,1)} %bitcast.5.refs_0_.refs_8_, ...), custom_call_target="tpu_custom_call" | custom-call | flops 1073741824 | bytes 4194304 | tf_op jit(solution)/shard_map/attend/pallas_call | solution.py:233
  240.6 3.8 collective-permute-start.11
  244.4 7.0 collective-permute-done.9
  251.5 9.9 %collective-permute-done.10 = bf16[256,512]{1,0:T(8,128)(2,1)S(1)} collective-permute-done((bf16[256,512]{1,0:T(8,128)(2,1)S(1)}, bf16[256,512]{1,0:T(8,128)(2,1)S(1)}, u32[]{:S(2)}, u32[]{:S(2)}) %collective-permute-start.10) | collective-permute-done | bytes 262176 | tf_op jit(solution)/shard_map/ppermute | solution.py:601
  262.5 6.1 fusion.84
  272.1 5.8 collective-permute-start.20
  278.5 29.5 %collective-permute-done.20.refs_6_ = bf16[1,4,2,128,640]{4,3,2,1,0:T(8,128)(2,1)} collective-permute-done((bf16[1,4,2,128,640]{4,3,2,1,0:T(8,128)(2,1)}, bf16[1,4,2,128,640]{4,3,2,1,0:T(8,128)(2,1)}, u32[]{:S(2)}, u32[]{:S(2)}) %collective-permute-start.20) | collective-permute-done | bytes 1310752 | tf_op jit(solution)/shard_map/ppermute | solution.py:413
  307.9 25.7 %collective-permute-done.18.refs_4_ = bf16[1,4,2,128,640]{4,3,2,1,0:T(8,128)(2,1)} collective-permute-done((bf16[1,4,2,128,640]{4,3,2,1,0:T(8,128)(2,1)}, bf16[1,4,2,128,640]{4,3,2,1,0:T(8,128)(2,1)}, u32[]{:S(2)}, u32[]{:S(2)}) %collective-permute-start.18) | collective-permute-done | bytes 1310752 | tf_op jit(solution)/shard_map/ppermute | solution.py:413
  334.2 2.9 collective-permute-done.19.refs_5_
  338.9 19.1 %all-gather.11.cloned.1.call-done.h_ref = bf16[1024,2048]{1,0:T(8,128)(2,1)} async-done(((bf16[256,2048]{1,0:T(8,128)(2,1)}), bf16[1024,2048]{1,0:T(8,128)(2,1)}) %all-gather.11.cloned.1.call-update) | async-done | bytes 4194320 | tf_op jit(solution)/shard_map/all_gather | solution.py:596
  358.1 28.9 %mlp.1 = (bf16[1024,1408]{1,0:T(8,128)(2,1)}, bf16[1024,2816]{1,0:T(8,128)(2,1)}) custom-call(bf16[1024,2048]{1,0:T(8,128)(2,1)} %all-gather.11.cloned.1.call-done.h_ref, bf16[1024,2048]{1,0:T(8,128)(2,1)} %all-gather.9.cloned.1.call-done.dy_ref, bf16[2048,1408]{1,0:T(8,128)(2,1)} %gate_ref.1, bf16[2048,1408]{1,0:T(8,128)(2,1)} %up_ref.1, ...), custom_call_target="tpu_custom_call" | custom-call | flops 17716740096 | bytes 38273024 | tf_op jit(solution)/shard_map/mlp/pallas_call | solution.py:397
  387.0 9.7 %fusion.5 = f32[1024,2048]{1,0:T(8,128)S(1)} fusion(bf16[2048,1408]{1,0:T(8,128)(2,1)} %gate_ref.1, bf16[1024,2816]{1,0:T(8,128)(2,1)} %get-tuple-element.142), kind=kOutput, calls=%fused_computation.25 | convolution fusion | flops 5905580032 | bytes 17039360 | tf_op jit(solution)/shard_map/dot_general | solution.py:15
  396.7 11.1 %add_convert_fusion.1 = bf16[1024,2048]{1,0:T(8,128)(2,1)} fusion(f32[1024,2048]{1,0:T(8,128)S(1)} %fusion.5, bf16[2048,1408]{1,0:T(8,128)(2,1)} %up_ref.1, bf16[1024,2816]{1,0:T(8,128)(2,1)S(1)} %copy-done.92), kind=kOutput, calls=%fused_computation.5 | convolution fusion | flops 5909774336 | bytes 21233664 | tf_op jit(solution)/shard_map/dot_general | solution.py:15
  407.8 11.1 %convolution_convert_fusion = bf16[1024,2816]{1,0:T(8,128)(2,1)} fusion(bf16[1024,2816]{1,0:T(8,128)(2,1)} %get-tuple-element.142, bf16[1024,2048]{1,0:T(8,128)(2,1)} %all-gather.11.cloned.1.call-done.h_ref, s32[]{:T(128)S(6)} %select_n.342), kind=kOutput, calls=%fused_computation.8 | convolution fusion | flops 5908463616 | bytes 13631492 | tf_op jit(solution)/shard_map/dot_general | solution.py:302
  418.9 4.5 convolution_convert_fusion.3
  424.0 8.7 %collective-permute-done.23 = bf16[1408,1024]{1,0:T(8,128)(2,1)} collective-permute-done((bf16[1408,1024]{1,0:T(8,128)(2,1)}, bf16[1408,1024]{1,0:T(8,128)(2,1)}, u32[]{:S(2)}, u32[]{:S(2)}) %collective-permute-start.23) | collective-permute-done | bytes 2883616 | tf_op jit(solution)/shard_map/ppermute | solution.py:413
  432.8 6.6 add_convert_fusion.2
  441.3 10.8 %add_convert_fusion = bf16[1024,2816]{1,0:T(8,128)(2,1)S(1)} fusion(bf16[1024,2816]{1,0:T(8,128)(2,1)} %collective-permute-done.22, bf16[1024,2816]{1,0:T(8,128)(2,1)} %get-tuple-element.142, bf16[1024,2048]{1,0:T(8,128)(2,1)S(1)} %copy-done.89, s32[]{:T(128)S(6)} %select_n.341), kind=kOutput, calls=%fused_computation | convolution fusion | flops 5914230784 | bytes 19398660 | tf_op jit(solution)/shard_map/dot_general | solution.py:302
  458.1 8.2 convolution_convert_fusion.1
  466.3 21.6 %collective-permute-done.24 = bf16[256,2816]{1,0:T(8,128)(2,1)} collective-permute-done((bf16[256,2816]{1,0:T(8,128)(2,1)}, bf16[256,2816]{1,0:T(8,128)(2,1)}, u32[]{:S(2)}, u32[]{:S(2)}) %collective-permute-start.24) | collective-permute-done | bytes 1441824 | tf_op jit(solution)/shard_map/ppermute | solution.py:413
  487.8 2.4 collective-permute-done.25
  499.4 2.3 fusion.24
  501.8 2.6 fusion.78
  504.4 6.2 convolution_convert_fusion.4
  510.7 4.3 collective-permute-done.30
  518.3 2.3 collective-permute-start.26
  522.5 12.6 %collective-permute-done.26 = bf16[256,512]{1,0:T(8,128)(2,1)S(1)} collective-permute-done((bf16[256,512]{1,0:T(8,128)(2,1)S(1)}, bf16[256,512]{1,0:T(8,128)(2,1)S(1)}, u32[]{:S(2)}, u32[]{:S(2)}) %collective-permute-start.26) | collective-permute-done | bytes 262176 | tf_op jit(solution)/shard_map/ppermute | solution.py:601
  535.2 4.4 collective-permute-done.27
  546.6 31.6 %query_grad.1 = bf16[4,256,512]{2,1,0:T(8,128)(2,1)} custom-call(s32[4,16]{1,0:T(4,128)} %copy.44.place_ref, s32[4,2]{1,0:T(4,128)} %get-tuple-element.251.own_ref, bf16[4,256,512]{2,1,0:T(8,128)(2,1)} %copy-done.2, bf16[4,256,512]{2,1,0:T(8,128)(2,1)} %bitcast.79, bf16[4,256,128]{2,1,0:T(8,128)(2,1)} %get-tuple-element.135.qx_ref, ...), custom_call_target="tpu_custom_call" | custom-call | flops 1610612736 | bytes 4194304 | tf_op jit(solution)/shard_map/query_grad/pallas_call | solution.py:233
  578.2 22.0 %collective-permute-done.34.refs_12_ = bf16[1,4,2,128,640]{4,3,2,1,0:T(8,128)(2,1)} collective-permute-done((bf16[1,4,2,128,640]{4,3,2,1,0:T(8,128)(2,1)S(1)}, bf16[1,4,2,128,640]{4,3,2,1,0:T(8,128)(2,1)}, u32[]{:S(2)}, u32[]{:S(2)}) %collective-permute-start.34) | collective-permute-done | bytes 1310752 | tf_op jit(solution)/shard_map/ppermute | solution.py:413
  608.4 25.0 %key_value_grad.2 = (bf16[2,256,512]{2,1,0:T(8,128)(2,1)}, bf16[2,256,512]{2,1,0:T(8,128)(2,1)}) custom-call(s32[4,16]{1,0:T(4,128)} %copy.44.place_ref, s32[4,2]{1,0:T(4,128)} %get-tuple-element.251.own_ref, bf16[2,4,256,512]{3,2,1,0:T(8,128)(2,1)} %get-tuple-element.129.kv_ref, f32[1024,128]{1,0:T(8,128)} %copy-done.6, f32[1024,128]{1,0:T(8,128)} %copy-done.5, ...), custom_call_target="tpu_custom_call" | custom-call | flops 1073741824 | bytes 2097152 | tf_op jit(solution)/shard_map/key_value_grad/pallas_call | solution.py:233
  641.8 22.9 %key_value_grad.3 = (bf16[2,256,512]{2,1,0:T(8,128)(2,1)}, bf16[2,256,512]{2,1,0:T(8,128)(2,1)}) custom-call(s32[4,16]{1,0:T(4,128)} %copy.44.place_ref, s32[4,2]{1,0:T(4,128)} %get-tuple-element.251.own_ref, bf16[2,4,256,512]{3,2,1,0:T(8,128)(2,1)} %get-tuple-element.129.kv_ref, f32[1024,128]{1,0:T(8,128)} %copy-done.6, f32[1024,128]{1,0:T(8,128)} %copy-done.5, ...), custom_call_target="tpu_custom_call" | custom-call | flops 1073741824 | bytes 2097152 | tf_op jit(solution)/shard_map/key_value_grad/pallas_call | solution.py:233
  668.2 4.9 collective-permute-start.46
  673.3 2.4 fusion.87
  675.8 5.8 fusion.86
  681.5 10.8 %fusion.85 = (bf16[1024,2048]{1,0:T(8,128)(2,1)}, f32[1024,2048]{1,0:T(8,128)}) fusion(f32[1024,2048]{1,0:T(8,128)S(1)} %fusion.87, f32[1024,2048]{1,0:T(8,128)} %fusion.86, bf16[1024,512]{1,0:T(8,128)(2,1)S(1)} %bitcast.78, bf16[2048,512]{1,0:T(8,128)(2,1)S(1)} %copy-done.53), kind=kOutput, calls=%fused_computation.208 | convolution fusion | flops 2153775104 | bytes 32505856 | tf_op jit(solution)/shard_map/dot_general | solution.py:15
  695.2 4.1 fusion.47
  699.3 3.7 convolution_convert_fusion.2
  703.0 2.8 pad_maximum_fusion
  712.9 2.6 fusion.29
  715.5 5.5 fusion.31
  721.1 5.0 collective-permute-done.50.refs_3_
  727.0 2.5 collective-permute-done.49.refs_1_
  730.3 5.3 fusion
  746.1 5.9 assemble.4.half_ref
  752.5 9.7 %collective-permute-done.51 = bf16[256,2048]{1,0:T(8,128)(2,1)} collective-permute-done((bf16[256,2048]{1,0:T(8,128)(2,1)}, bf16[256,2048]{1,0:T(8,128)(2,1)}, u32[]{:S(2)}, u32[]{:S(2)}) %collective-permute-start.51) | collective-permute-done | bytes 1048608 | tf_op jit(solution)/shard_map/ppermute | solution.py:413
  768.1 8.5 collective-permute-done.52
  780.7 4.7 fusion.77
  785.9 6.3 unpack_cols.1
  796.0 2.8 collective-permute-start.59
  798.8 4.9 collective-permute-done.59
  803.7 2.9 collective-permute-start.60
  806.6 8.2 collective-permute-done.60
  814.8 13.5 %unpack_rows.2 = (f32[2048,1408]{1,0:T(8,128)}, f32[2048,1408]{1,0:T(8,128)}) custom-call(s32[1]{0:T(128)} %bitcast.19.core_ref, bf16[1024,2816]{1,0:T(8,128)(2,1)} %assemble.4.half_ref, bf16[1024,2816]{1,0:T(8,128)(2,1)} %collective-permute-done.65.other_ref), custom_call_target="tpu_custom_call" | custom-call | bytes 1024 | tf_op jit(solution)/shard_map/unpack_rows/pallas_call | solution.py:555
  828.4 4.6 assemble.5.half_ref
  834.2 3.2 collective-permute-done.61
  847.6 3.1 fusion.18
  850.6 11.4 %unpack_rows.3 = (f32[2048,512]{1,0:T(8,128)}, f32[2048,512]{1,0:T(8,128)}, f32[2048,512]{1,0:T(8,128)}, f32[512,2048]{1,0:T(8,128)}) custom-call(s32[1]{0:T(128)} %bitcast.19.core_ref, bf16[1024,2048]{1,0:T(8,128)(2,1)} %assemble.5.half_ref, bf16[1024,2048]{1,0:T(8,128)(2,1)} %collective-permute-done.66.other_ref), custom_call_target="tpu_custom_call" | custom-call | bytes 1024 | tf_op jit(solution)/shard_map/unpack_rows/pallas_call | solution.py:555
  (440 shorter events, 138.7 us)
Async XLA Ops:
  7.2 89.0 %all-gather.7.cloned.1.call-start = ((), (), s32[]{:S(2)}) async-start(), calls=%async_computation.3 | async-start | bytes 5242880 | tf_op jit(solution)/shard_map/all_gather | solution.py:596
  12.7 197.1 %all-gather.9.cloned.1.call-start = ((), (), s32[]{:S(2)}) async-start(), calls=%async_computation.4 | async-start | bytes 5242880 | tf_op jit(solution)/shard_map/all_gather | solution.py:596
  96.3 166.2 %all-gather.15.cloned.1.call-start = ((), (), s32[]{:S(2)}) async-start(), calls=%async_computation.10 | async-start | bytes 9437184 | tf_op jit(solution)/shard_map/all_gather | solution.py:710
  112.0 47.7 %collective-permute-start.3 = (bf16[2,4,2,128,512]{4,3,2,1,0:T(8,128)(2,1)}, bf16[2,4,2,128,512]{4,3,2,1,0:T(8,128)(2,1)}, u32[]{:S(2)}, u32[]{:S(2)}) collective-permute-start(bf16[2,4,2,128,512]{4,3,2,1,0:T(8,128)(2,1)} %bitcast.5.refs_0_.refs_8_), channel_id=1, source_target_pairs={{0,16},{4,20},{8,24},{12,28},{16,0},{20,4},{24,8},{28,12},{1,17},{... | collective-permute-start | bytes 6291464 | tf_op jit(solution)/shard_map/ppermute | solution.py:413
  113.5 49.9 %collective-permute-start.1 = (bf16[2,4,2,128,512]{4,3,2,1,0:T(8,128)(2,1)}, bf16[2,4,2,128,512]{4,3,2,1,0:T(8,128)(2,1)}, u32[]{:S(2)}, u32[]{:S(2)}) collective-permute-start(bf16[2,4,2,128,512]{4,3,2,1,0:T(8,128)(2,1)} %bitcast.5.refs_0_.refs_8_), channel_id=1, source_target_pairs={{0,8},{4,12},{8,0},{12,4},{16,24},{20,28},{24,16},{28,20},{1,9},{5... | collective-permute-start | bytes 6291464 | tf_op jit(solution)/shard_map/ppermute | solution.py:413
  161.9 40.6 %collective-permute-start.7 = (bf16[1,4,2,128,512]{4,3,2,1,0:T(8,128)(2,1)}, bf16[1,4,2,128,512]{4,3,2,1,0:T(8,128)(2,1)S(1)}, u32[]{:S(2)}, u32[]{:S(2)}) collective-permute-start(bf16[1,4,2,128,512]{4,3,2,1,0:T(8,128)(2,1)} %slice.96), channel_id=1, source_target_pairs={{0,8},{4,12},{8,0},{12,4},{16,24},{20,28},{24,16},{28,20},{1,9},{5... | collective-permute-start | bytes 3145736 | tf_op jit(solution)/shard_map/ppermute | solution.py:413
  165.6 37.4 %collective-permute-start.5 = (bf16[1,4,2,128,512]{4,3,2,1,0:T(8,128)(2,1)}, bf16[1,4,2,128,512]{4,3,2,1,0:T(8,128)(2,1)}, u32[]{:S(2)}, u32[]{:S(2)}) collective-permute-start(bf16[1,4,2,128,512]{4,3,2,1,0:T(8,128)(2,1)} %slice.95), channel_id=1, source_target_pairs={{0,16},{4,20},{8,24},{12,28},{16,0},{20,4},{24,8},{28,12},{1,17},{... | collective-permute-start | bytes 3145736 | tf_op jit(solution)/shard_map/ppermute | solution.py:413
  167.1 12.3 %collective-permute-start.14 = (bf16[64,2048]{1,0:T(8,128)(2,1)S(1)}, bf16[64,2048]{1,0:T(8,128)(2,1)S(1)}, u32[]{:S(2)}, u32[]{:S(2)}) collective-permute-start(bf16[64,2048]{1,0:T(8,128)(2,1)S(1)} %constant_dynamic-slice_fusion.15), channel_id=1, source_target_pairs={{0,3},{1,0},{2,1},{3,2},{4,7},{5,4},{6,5},{7,6},{8,11},{9,8},{10,9... | collective-permute-start | bytes 786440 | tf_op jit(solution)/shard_map/ppermute | solution.py:679
  168.2 31.0 %collective-permute-start.13 = (bf16[64,2048]{1,0:T(8,128)(2,1)S(1)}, bf16[64,2048]{1,0:T(8,128)(2,1)S(1)}, u32[]{:S(2)}, u32[]{:S(2)}) collective-permute-start(bf16[64,2048]{1,0:T(8,128)(2,1)S(1)} %constant_dynamic-slice_fusion.15), channel_id=1, source_target_pairs={{0,2},{1,3},{2,0},{3,1},{4,6},{5,7},{6,4},{7,5},{8,10},{9,11},{10,... | collective-permute-start | bytes 786440 | tf_op jit(solution)/shard_map/ppermute | solution.py:679
  168.2 31.0 %collective-permute-start.12 = (bf16[64,2048]{1,0:T(8,128)(2,1)S(1)}, bf16[64,2048]{1,0:T(8,128)(2,1)S(1)}, u32[]{:S(2)}, u32[]{:S(2)}) collective-permute-start(bf16[64,2048]{1,0:T(8,128)(2,1)S(1)} %constant_dynamic-slice_fusion.15), channel_id=1, source_target_pairs={{0,1},{1,2},{2,3},{3,0},{4,5},{5,6},{6,7},{7,4},{8,9},{9,10},{10,1... | collective-permute-start | bytes 786440 | tf_op jit(solution)/shard_map/ppermute | solution.py:679
  179.5 26.7 %collective-permute-start = (bf16[2,4,2,128,512]{4,3,2,1,0:T(8,128)(2,1)}, bf16[2,4,2,128,512]{4,3,2,1,0:T(8,128)(2,1)S(1)}, u32[]{:S(2)}, u32[]{:S(2)}) collective-permute-start(bf16[2,4,2,128,512]{4,3,2,1,0:T(8,128)(2,1)} %bitcast.5.refs_0_.refs_8_), channel_id=1, source_target_pairs={{0,4},{4,0},{8,12},{12,8},{16,20},{20,16},{24,28},{28,24},{1,5},{5... | collective-permute-start | bytes 6291464 | tf_op jit(solution)/shard_map/ppermute | solution.py:413
  199.3 10.5 %collective-permute-start.4 = (bf16[2,4,2,128,512]{4,3,2,1,0:T(8,128)(2,1)}, bf16[2,4,2,128,512]{4,3,2,1,0:T(8,128)(2,1)}, u32[]{:S(2)}, u32[]{:S(2)}) collective-permute-start(bf16[2,4,2,128,512]{4,3,2,1,0:T(8,128)(2,1)} %collective-permute-done.3.refs_4_.refs_12_), channel_id=1, source_target_pairs={{0,4},{4,0},{8,12},{12,8},{16,20},{20,16},{24,28},{28,24},{1,5},{5... | collective-permute-start | bytes 6291464 | tf_op jit(solution)/shard_map/ppermute | solution.py:413
  200.7 9.1 %collective-permute-start.2 = (bf16[2,4,2,128,512]{4,3,2,1,0:T(8,128)(2,1)}, bf16[2,4,2,128,512]{4,3,2,1,0:T(8,128)(2,1)}, u32[]{:S(2)}, u32[]{:S(2)}) collective-permute-start(bf16[2,4,2,128,512]{4,3,2,1,0:T(8,128)(2,1)} %collective-permute-done.1.refs_2_.refs_10_), channel_id=1, source_target_pairs={{0,4},{4,0},{8,12},{12,8},{16,20},{20,16},{24,28},{28,24},{1,5},{5... | collective-permute-start | bytes 6291464 | tf_op jit(solution)/shard_map/ppermute | solution.py:413
  209.8 148.3 %all-gather.11.cloned.1.call-start = ((), (), s32[]{:S(2)}) async-start(), calls=%async_computation.5 | async-start | bytes 5242880 | tf_op jit(solution)/shard_map/all_gather | solution.py:596
  240.6 10.8 %collective-permute-start.9 = (bf16[256,512]{1,0:T(8,128)(2,1)}, bf16[256,512]{1,0:T(8,128)(2,1)S(1)}, u32[]{:S(2)}, u32[]{:S(2)}) collective-permute-start(bf16[256,512]{1,0:T(8,128)(2,1)} %get-tuple-element.264), channel_id=1, source_target_pairs={{0,1},{1,2},{2,3},{3,0},{4,5},{5,6},{6,7},{7,4},{8,9},{9,10},{10,1... | collective-permute-start | bytes 786440 | tf_op jit(solution)/shard_map/ppermute | solution.py:601
  240.6 20.8 %collective-permute-start.10 = (bf16[256,512]{1,0:T(8,128)(2,1)S(1)}, bf16[256,512]{1,0:T(8,128)(2,1)S(1)}, u32[]{:S(2)}, u32[]{:S(2)}) collective-permute-start(bf16[256,512]{1,0:T(8,128)(2,1)S(1)} %get-tuple-element.263), channel_id=1, source_target_pairs={{0,2},{1,3},{2,0},{3,1},{4,6},{5,7},{6,4},{7,5},{8,10},{9,11},{10,... | collective-permute-start | bytes 786440 | tf_op jit(solution)/shard_map/ppermute | solution.py:601
  240.6 20.8 %collective-permute-start.11 = (bf16[256,512]{1,0:T(8,128)(2,1)S(1)}, bf16[256,512]{1,0:T(8,128)(2,1)S(1)}, u32[]{:S(2)}, u32[]{:S(2)}) collective-permute-start(bf16[256,512]{1,0:T(8,128)(2,1)S(1)} %get-tuple-element.262), channel_id=1, source_target_pairs={{0,3},{1,0},{2,1},{3,2},{4,7},{5,4},{6,5},{7,6},{8,11},{9,8},{10,9... | collective-permute-start | bytes 786440 | tf_op jit(solution)/shard_map/ppermute | solution.py:601
  270.9 228.6 %reduce-scatter.4.cloned.1.call-start = ((), (), s32[]{:S(2)}) async-start(), calls=%async_computation.6 | async-start | bytes 5242880 | tf_op jit(solution)/shard_map/reduce_scatter | solution.py:624
  272.1 35.8 %collective-permute-start.20 = (bf16[1,4,2,128,640]{4,3,2,1,0:T(8,128)(2,1)}, bf16[1,4,2,128,640]{4,3,2,1,0:T(8,128)(2,1)}, u32[]{:S(2)}, u32[]{:S(2)}) collective-permute-start(bf16[1,4,2,128,640]{4,3,2,1,0:T(8,128)(2,1)} %bitcast.12.refs_0_), channel_id=1, source_target_pairs={{0,24},{4,28},{8,16},{12,20},{16,8},{20,12},{24,0},{28,4},{1,25},{... | collective-permute-start | bytes 3932168 | tf_op jit(solution)/shard_map/ppermute | solution.py:413
  277.9 55.8 %collective-permute-start.18 = (bf16[1,4,2,128,640]{4,3,2,1,0:T(8,128)(2,1)}, bf16[1,4,2,128,640]{4,3,2,1,0:T(8,128)(2,1)}, u32[]{:S(2)}, u32[]{:S(2)}) collective-permute-start(bf16[1,4,2,128,640]{4,3,2,1,0:T(8,128)(2,1)} %bitcast.12.refs_0_), channel_id=1, source_target_pairs={{0,16},{4,20},{8,24},{12,28},{16,0},{20,4},{24,8},{28,12},{1,17},{... | collective-permute-start | bytes 3932168 | tf_op jit(solution)/shard_map/ppermute | solution.py:413
  277.9 55.8 %collective-permute-start.16 = (bf16[1,4,2,128,640]{4,3,2,1,0:T(8,128)(2,1)}, bf16[1,4,2,128,640]{4,3,2,1,0:T(8,128)(2,1)}, u32[]{:S(2)}, u32[]{:S(2)}) collective-permute-start(bf16[1,4,2,128,640]{4,3,2,1,0:T(8,128)(2,1)} %bitcast.12.refs_0_), channel_id=1, source_target_pairs={{0,8},{4,12},{8,0},{12,4},{16,24},{20,28},{24,16},{28,20},{1,9},{5... | collective-permute-start | bytes 3932168 | tf_op jit(solution)/shard_map/ppermute | solution.py:413
  278.4 55.7 %collective-permute-start.15 = (bf16[1,4,2,128,640]{4,3,2,1,0:T(8,128)(2,1)}, bf16[1,4,2,128,640]{4,3,2,1,0:T(8,128)(2,1)}, u32[]{:S(2)}, u32[]{:S(2)}) collective-permute-start(bf16[1,4,2,128,640]{4,3,2,1,0:T(8,128)(2,1)} %bitcast.12.refs_0_), channel_id=1, source_target_pairs={{0,4},{4,0},{8,12},{12,8},{16,20},{20,16},{24,28},{28,24},{1,5},{5... | collective-permute-start | bytes 3932168 | tf_op jit(solution)/shard_map/ppermute | solution.py:413
  307.9 26.3 %collective-permute-start.21 = (bf16[1,4,2,128,640]{4,3,2,1,0:T(8,128)(2,1)}, bf16[1,4,2,128,640]{4,3,2,1,0:T(8,128)(2,1)}, u32[]{:S(2)}, u32[]{:S(2)}) collective-permute-start(bf16[1,4,2,128,640]{4,3,2,1,0:T(8,128)(2,1)} %collective-permute-done.20.refs_6_), channel_id=1, source_target_pairs={{0,4},{4,0},{8,12},{12,8},{16,20},{20,16},{24,28},{28,24},{1,5},{5... | collective-permute-start | bytes 3932168 | tf_op jit(solution)/shard_map/ppermute | solution.py:413
  418.9 22.4 %collective-permute-start.22 = (bf16[1024,2816]{1,0:T(8,128)(2,1)}, bf16[1024,2816]{1,0:T(8,128)(2,1)}, u32[]{:S(2)}, u32[]{:S(2)}) collective-permute-start(bf16[1024,2816]{1,0:T(8,128)(2,1)} %convolution_convert_fusion), channel_id=1, source_target_pairs={{0,4},{4,0},{8,12},{12,8},{16,20},{20,16},{24,28},{28,24},{1,5},{5... | collective-permute-start | bytes 17301512 | tf_op jit(solution)/shard_map/ppermute | solution.py:413
  423.4 9.3 %collective-permute-start.23 = (bf16[1408,1024]{1,0:T(8,128)(2,1)}, bf16[1408,1024]{1,0:T(8,128)(2,1)}, u32[]{:S(2)}, u32[]{:S(2)}) collective-permute-start(bf16[1408,1024]{1,0:T(8,128)(2,1)} %convolution_convert_fusion.3), channel_id=1, source_target_pairs={{0,4},{4,0},{8,12},{12,8},{16,20},{20,16},{24,28},{28,24},{1,5},{5... | collective-permute-start | bytes 8650760 | tf_op jit(solution)/shard_map/ppermute | solution.py:413
  424.0 268.3 %all-gather.13.cloned.1.call-start = ((), (), s32[]{:S(2)}) async-start(), calls=%async_computation.8 | async-start | bytes 5242880 | tf_op jit(solution)/shard_map/all_gather | solution.py:596
  453.9 33.9 %collective-permute-start.24 = (bf16[256,2816]{1,0:T(8,128)(2,1)}, bf16[256,2816]{1,0:T(8,128)(2,1)}, u32[]{:S(2)}, u32[]{:S(2)}) collective-permute-start(bf16[256,2816]{1,0:T(8,128)(2,1)} %constant_dynamic-slice_fusion.14), channel_id=1, source_target_pairs={{0,8},{4,12},{8,0},{12,4},{16,24},{20,28},{24,16},{28,20},{1,9},{5... | collective-permute-start | bytes 4325384 | tf_op jit(solution)/shard_map/ppermute | solution.py:413
  456.6 33.7 %collective-permute-start.25 = (bf16[256,2816]{1,0:T(8,128)(2,1)}, bf16[256,2816]{1,0:T(8,128)(2,1)}, u32[]{:S(2)}, u32[]{:S(2)}) collective-permute-start(bf16[256,2816]{1,0:T(8,128)(2,1)} %constant_dynamic-slice_fusion.13), channel_id=1, source_target_pairs={{0,16},{4,20},{8,24},{12,28},{16,0},{20,4},{24,8},{28,12},{1,17},{... | collective-permute-start | bytes 4325384 | tf_op jit(solution)/shard_map/ppermute | solution.py:413
  493.4 17.3 %collective-permute-start.29 = (bf16[128,2816]{1,0:T(8,128)(2,1)}, bf16[128,2816]{1,0:T(8,128)(2,1)}, u32[]{:S(2)}, u32[]{:S(2)}) collective-permute-start(bf16[128,2816]{1,0:T(8,128)(2,1)} %constant_dynamic-slice_fusion.9), channel_id=1, source_target_pairs={{0,16},{4,20},{8,24},{12,28},{16,0},{20,4},{24,8},{28,12},{1,17},{... | collective-permute-start | bytes 2162696 | tf_op jit(solution)/shard_map/ppermute | solution.py:413
  498.0 17.1 %collective-permute-start.30 = (bf16[128,2816]{1,0:T(8,128)(2,1)}, bf16[128,2816]{1,0:T(8,128)(2,1)}, u32[]{:S(2)}, u32[]{:S(2)}) collective-permute-start(bf16[128,2816]{1,0:T(8,128)(2,1)} %constant_dynamic-slice_fusion.8), channel_id=1, source_target_pairs={{0,8},{4,12},{8,0},{12,4},{16,24},{20,28},{24,16},{28,20},{1,9},{5... | collective-permute-start | bytes 2162696 | tf_op jit(solution)/shard_map/ppermute | solution.py:413
  516.3 24.8 %collective-permute-start.32 = (bf16[128,2816]{1,0:T(8,128)(2,1)S(1)}, bf16[128,2816]{1,0:T(8,128)(2,1)S(1)}, u32[]{:S(2)}, u32[]{:S(2)}) collective-permute-start(bf16[128,2816]{1,0:T(8,128)(2,1)S(1)} %add_convert_fusion.11), channel_id=1, source_target_pairs={{0,8},{4,12},{8,0},{12,4},{16,24},{20,28},{24,16},{28,20},{1,9},{5... | collective-permute-start | bytes 2162696 | tf_op jit(solution)/shard_map/ppermute | solution.py:413
  517.2 22.4 %collective-permute-start.28 = (bf16[256,512]{1,0:T(8,128)(2,1)S(1)}, bf16[256,512]{1,0:T(8,128)(2,1)S(1)}, u32[]{:S(2)}, u32[]{:S(2)}) collective-permute-start(bf16[256,512]{1,0:T(8,128)(2,1)S(1)} %get-tuple-element.258), channel_id=1, source_target_pairs={{0,3},{1,0},{2,1},{3,2},{4,7},{5,4},{6,5},{7,6},{8,11},{9,8},{10,9... | collective-permute-start | bytes 786440 | tf_op jit(solution)/shard_map/ppermute | solution.py:601
  518.1 21.5 %collective-permute-start.27 = (bf16[256,512]{1,0:T(8,128)(2,1)S(1)}, bf16[256,512]{1,0:T(8,128)(2,1)S(1)}, u32[]{:S(2)}, u32[]{:S(2)}) collective-permute-start(bf16[256,512]{1,0:T(8,128)(2,1)S(1)} %get-tuple-element.259), channel_id=1, source_target_pairs={{0,2},{1,3},{2,0},{3,1},{4,6},{5,7},{6,4},{7,5},{8,10},{9,11},{10,... | collective-permute-start | bytes 786440 | tf_op jit(solution)/shard_map/ppermute | solution.py:601
  518.3 16.9 %collective-permute-start.26 = (bf16[256,512]{1,0:T(8,128)(2,1)S(1)}, bf16[256,512]{1,0:T(8,128)(2,1)S(1)}, u32[]{:S(2)}, u32[]{:S(2)}) collective-permute-start(bf16[256,512]{1,0:T(8,128)(2,1)S(1)} %get-tuple-element.260), channel_id=1, source_target_pairs={{0,1},{1,2},{2,3},{3,0},{4,5},{5,6},{6,7},{7,4},{8,9},{9,10},{10,1... | collective-permute-start | bytes 786440 | tf_op jit(solution)/shard_map/ppermute | solution.py:601
  521.9 19.3 %collective-permute-start.31 = (bf16[128,2816]{1,0:T(8,128)(2,1)S(1)}, bf16[128,2816]{1,0:T(8,128)(2,1)S(1)}, u32[]{:S(2)}, u32[]{:S(2)}) collective-permute-start(bf16[128,2816]{1,0:T(8,128)(2,1)S(1)} %add_convert_fusion.12), channel_id=1, source_target_pairs={{0,16},{4,20},{8,24},{12,28},{16,0},{20,4},{24,8},{28,12},{1,17},{... | collective-permute-start | bytes 2162696 | tf_op jit(solution)/shard_map/ppermute | solution.py:413
  543.0 187.4 %reduce-scatter.6.cloned.1.call-start = ((), (), s32[]{:S(2)}) async-start(), calls=%async_computation.7 | async-start | bytes 5242880 | tf_op jit(solution)/shard_map/reduce_scatter | solution.py:624
  543.0 35.2 %collective-permute-start.35 = (bf16[1,4,2,128,640]{4,3,2,1,0:T(8,128)(2,1)S(1)}, bf16[1,4,2,128,640]{4,3,2,1,0:T(8,128)(2,1)}, u32[]{:S(2)}, u32[]{:S(2)}) collective-permute-start(bf16[1,4,2,128,640]{4,3,2,1,0:T(8,128)(2,1)S(1)} %bitcast.71), channel_id=1, source_target_pairs={{0,24},{4,28},{8,16},{12,20},{16,8},{20,12},{24,0},{28,4},{1,25},{... | collective-permute-start | bytes 3932168 | tf_op jit(solution)/shard_map/ppermute | solution.py:413
  544.5 55.7 %collective-permute-start.34 = (bf16[1,4,2,128,640]{4,3,2,1,0:T(8,128)(2,1)S(1)}, bf16[1,4,2,128,640]{4,3,2,1,0:T(8,128)(2,1)}, u32[]{:S(2)}, u32[]{:S(2)}) collective-permute-start(bf16[1,4,2,128,640]{4,3,2,1,0:T(8,128)(2,1)S(1)} %bitcast.72), channel_id=1, source_target_pairs={{0,16},{4,20},{8,24},{12,28},{16,0},{20,4},{24,8},{28,12},{1,17},{... | collective-permute-start | bytes 3932168 | tf_op jit(solution)/shard_map/ppermute | solution.py:413
  545.6 55.7 %collective-permute-start.33 = (bf16[1,4,2,128,640]{4,3,2,1,0:T(8,128)(2,1)S(1)}, bf16[1,4,2,128,640]{4,3,2,1,0:T(8,128)(2,1)}, u32[]{:S(2)}, u32[]{:S(2)}) collective-permute-start(bf16[1,4,2,128,640]{4,3,2,1,0:T(8,128)(2,1)S(1)} %bitcast.73), channel_id=1, source_target_pairs={{0,8},{4,12},{8,0},{12,4},{16,24},{20,28},{24,16},{28,20},{1,9},{5... | collective-permute-start | bytes 3932168 | tf_op jit(solution)/shard_map/ppermute | solution.py:413
  546.6 58.7 %collective-permute-start.36 = (bf16[1,4,2,128,640]{4,3,2,1,0:T(8,128)(2,1)S(1)}, bf16[1,4,2,128,640]{4,3,2,1,0:T(8,128)(2,1)}, u32[]{:S(2)}, u32[]{:S(2)}) collective-permute-start(bf16[1,4,2,128,640]{4,3,2,1,0:T(8,128)(2,1)S(1)} %bitcast.74), channel_id=1, source_target_pairs={{0,4},{4,0},{8,12},{12,8},{16,20},{20,16},{24,28},{28,24},{1,5},{5... | collective-permute-start | bytes 3932168 | tf_op jit(solution)/shard_map/ppermute | solution.py:413
  602.7 30.7 %collective-permute-start.41 = (bf16[352,1024]{1,0:T(8,128)(2,1)}, bf16[352,1024]{1,0:T(8,128)(2,1)}, u32[]{:S(2)}, u32[]{:S(2)}) collective-permute-start(bf16[352,1024]{1,0:T(8,128)(2,1)} %constant_dynamic-slice_fusion.6), channel_id=1, source_target_pairs={{0,16},{4,20},{8,24},{12,28},{16,0},{20,4},{24,8},{28,12},{1,17},{... | collective-permute-start | bytes 2162696 | tf_op jit(solution)/shard_map/ppermute | solution.py:413
  605.3 28.1 %collective-permute-start.40 = (bf16[352,1024]{1,0:T(8,128)(2,1)}, bf16[352,1024]{1,0:T(8,128)(2,1)}, u32[]{:S(2)}, u32[]{:S(2)}) collective-permute-start(bf16[352,1024]{1,0:T(8,128)(2,1)} %constant_dynamic-slice_fusion.7), channel_id=1, source_target_pairs={{0,8},{4,12},{8,0},{12,4},{16,24},{20,28},{24,16},{28,20},{1,9},{5... | collective-permute-start | bytes 2162696 | tf_op jit(solution)/shard_map/ppermute | solution.py:413
  635.2 29.5 %collective-permute-start.42 = (bf16[176,1024]{1,0:T(8,128)(2,1)S(1)}, bf16[176,1024]{1,0:T(8,128)(2,1)}, u32[]{:S(2)}, u32[]{:S(2)}) collective-permute-start(bf16[176,1024]{1,0:T(8,128)(2,1)S(1)} %constant_dynamic-slice_fusion.5), channel_id=1, source_target_pairs={{0,16},{4,20},{8,24},{12,28},{16,0},{20,4},{24,8},{28,12},{1,17},{... | collective-permute-start | bytes 1081352 | tf_op jit(solution)/shard_map/ppermute | solution.py:413
  637.8 27.0 %collective-permute-start.43 = (bf16[176,1024]{1,0:T(8,128)(2,1)}, bf16[176,1024]{1,0:T(8,128)(2,1)}, u32[]{:S(2)}, u32[]{:S(2)}) collective-permute-start(bf16[176,1024]{1,0:T(8,128)(2,1)} %constant_dynamic-slice_fusion.4), channel_id=1, source_target_pairs={{0,8},{4,12},{8,0},{12,4},{16,24},{20,28},{24,16},{28,20},{1,9},{5... | collective-permute-start | bytes 1081352 | tf_op jit(solution)/shard_map/ppermute | solution.py:413
  637.8 207.9 %reduce-scatter.8.cloned.1.call-start = ((), (), s32[]{:S(2)}) async-start(), calls=%async_computation.9 | async-start | bytes 5242880 | tf_op jit(solution)/shard_map/reduce_scatter | solution.py:624
  637.8 54.5 %collective-permute-start.44 = (bf16[256,2816]{1,0:T(8,128)(2,1)S(1)}, bf16[256,2816]{1,0:T(8,128)(2,1)}, u32[]{:S(2)}, u32[]{:S(2)}) collective-permute-start(bf16[256,2816]{1,0:T(8,128)(2,1)S(1)} %maximum_select_fusion.refs_0_), channel_id=1, source_target_pairs={{0,8},{4,12},{8,0},{12,4},{16,24},{20,28},{24,16},{28,20},{1,9},{5... | collective-permute-start | bytes 4325384 | tf_op jit(solution)/shard_map/ppermute | solution.py:413
  639.9 52.4 %collective-permute-start.45 = (bf16[256,2816]{1,0:T(8,128)(2,1)S(1)}, bf16[256,2816]{1,0:T(8,128)(2,1)}, u32[]{:S(2)}, u32[]{:S(2)}) collective-permute-start(bf16[256,2816]{1,0:T(8,128)(2,1)S(1)} %maximum_select_fusion.1.refs_2_), channel_id=1, source_target_pairs={{0,16},{4,20},{8,24},{12,28},{16,0},{20,4},{24,8},{28,12},{1,17},{... | collective-permute-start | bytes 4325384 | tf_op jit(solution)/shard_map/ppermute | solution.py:413
  666.1 26.2 %collective-permute-start.47 = (bf16[176,1024]{1,0:T(8,128)(2,1)S(1)}, bf16[176,1024]{1,0:T(8,128)(2,1)}, u32[]{:S(2)}, u32[]{:S(2)}) collective-permute-start(bf16[176,1024]{1,0:T(8,128)(2,1)S(1)} %add_convert_fusion.15), channel_id=1, source_target_pairs={{0,8},{4,12},{8,0},{12,4},{16,24},{20,28},{24,16},{28,20},{1,9},{5... | collective-permute-start | bytes 1081352 | tf_op jit(solution)/shard_map/ppermute | solution.py:413
  668.2 24.1 %collective-permute-start.46 = (bf16[176,1024]{1,0:T(8,128)(2,1)}, bf16[176,1024]{1,0:T(8,128)(2,1)}, u32[]{:S(2)}, u32[]{:S(2)}) collective-permute-start(bf16[176,1024]{1,0:T(8,128)(2,1)} %add_convert_fusion.16), channel_id=1, source_target_pairs={{0,16},{4,20},{8,24},{12,28},{16,0},{20,4},{24,8},{28,12},{1,17},{... | collective-permute-start | bytes 1081352 | tf_op jit(solution)/shard_map/ppermute | solution.py:413
  705.8 24.6 %collective-permute-start.48 = (bf16[1024,2048]{1,0:T(8,128)(2,1)}, bf16[1024,2048]{1,0:T(8,128)(2,1)}, u32[]{:S(2)}, u32[]{:S(2)}) collective-permute-start(bf16[1024,2048]{1,0:T(8,128)(2,1)} %pad_maximum_fusion), channel_id=1, source_target_pairs={{0,4},{4,0},{8,12},{12,8},{16,20},{20,16},{24,28},{28,24},{1,5},{5... | collective-permute-start | bytes 12582920 | tf_op jit(solution)/shard_map/ppermute | solution.py:413
  707.2 18.9 %collective-permute-start.50 = (bf16[352,1024]{1,0:T(8,128)(2,1)S(1)}, bf16[352,1024]{1,0:T(8,128)(2,1)S(1)}, u32[]{:S(2)}, u32[]{:S(2)}) collective-permute-start(bf16[352,1024]{1,0:T(8,128)(2,1)S(1)} %maximum_select_fusion.5.refs_2_), channel_id=1, source_target_pairs={{0,16},{4,20},{8,24},{12,28},{16,0},{20,4},{24,8},{28,12},{1,17},{... | collective-permute-start | bytes 2162696 | tf_op jit(solution)/shard_map/ppermute | solution.py:413
  710.9 18.6 %collective-permute-start.49 = (bf16[352,1024]{1,0:T(8,128)(2,1)S(1)}, bf16[352,1024]{1,0:T(8,128)(2,1)S(1)}, u32[]{:S(2)}, u32[]{:S(2)}) collective-permute-start(bf16[352,1024]{1,0:T(8,128)(2,1)S(1)} %maximum_select_fusion.4.refs_0_), channel_id=1, source_target_pairs={{0,8},{4,12},{8,0},{12,4},{16,24},{20,28},{24,16},{28,20},{1,9},{5... | collective-permute-start | bytes 2162696 | tf_op jit(solution)/shard_map/ppermute | solution.py:413
  737.2 25.1 %collective-permute-start.51 = (bf16[256,2048]{1,0:T(8,128)(2,1)}, bf16[256,2048]{1,0:T(8,128)(2,1)}, u32[]{:S(2)}, u32[]{:S(2)}) collective-permute-start(bf16[256,2048]{1,0:T(8,128)(2,1)} %constant_dynamic-slice_fusion.3), channel_id=1, source_target_pairs={{0,8},{4,12},{8,0},{12,4},{16,24},{20,28},{24,16},{28,20},{1,9},{5... | collective-permute-start | bytes 3145736 | tf_op jit(solution)/shard_map/ppermute | solution.py:413
  740.1 24.7 %collective-permute-start.53 = (bf16[256,2048]{1,0:T(8,128)(2,1)}, bf16[256,2048]{1,0:T(8,128)(2,1)}, u32[]{:S(2)}, u32[]{:S(2)}) collective-permute-start(bf16[256,2048]{1,0:T(8,128)(2,1)} %constant_dynamic-slice_fusion.1), channel_id=1, source_target_pairs={{0,16},{4,20},{8,24},{12,28},{16,0},{20,4},{24,8},{28,12},{1,17},{... | collective-permute-start | bytes 3145736 | tf_op jit(solution)/shard_map/ppermute | solution.py:413
  746.0 39.9 %collective-permute-start.57 = (bf16[1408,1024]{1,0:T(8,128)(2,1)S(1)}, bf16[1408,1024]{1,0:T(8,128)(2,1)S(1)}, u32[]{:S(2)}, u32[]{:S(2)}) collective-permute-start(bf16[1408,1024]{1,0:T(8,128)(2,1)S(1)} %assemble.3.half_ref), channel_id=1, source_target_pairs={{0,4},{4,0},{8,12},{12,8},{16,20},{20,16},{24,28},{28,24},{1,5},{5... | collective-permute-start | bytes 8650760 | tf_op jit(solution)/shard_map/ppermute | solution.py:413
  751.9 62.9 %collective-permute-start.65 = (bf16[1024,2816]{1,0:T(8,128)(2,1)}, bf16[1024,2816]{1,0:T(8,128)(2,1)}, u32[]{:S(2)}, u32[]{:S(2)}) collective-permute-start(bf16[1024,2816]{1,0:T(8,128)(2,1)} %assemble.4.half_ref), channel_id=1, source_target_pairs={{0,4},{4,0},{8,12},{12,8},{16,20},{20,16},{24,28},{28,24},{1,5},{5... | collective-permute-start | bytes 17301512 | tf_op jit(solution)/shard_map/ppermute | solution.py:413
  764.0 12.6 %collective-permute-start.52 = (bf16[128,2048]{1,0:T(8,128)(2,1)S(1)}, bf16[128,2048]{1,0:T(8,128)(2,1)S(1)}, u32[]{:S(2)}, u32[]{:S(2)}) collective-permute-start(bf16[128,2048]{1,0:T(8,128)(2,1)S(1)} %constant_dynamic-slice_fusion.2), channel_id=1, source_target_pairs={{0,16},{4,20},{8,24},{12,28},{16,0},{20,4},{24,8},{28,12},{1,17},{... | collective-permute-start | bytes 1572872 | tf_op jit(solution)/shard_map/ppermute | solution.py:413
  766.5 12.6 %collective-permute-start.54 = (bf16[128,2048]{1,0:T(8,128)(2,1)S(1)}, bf16[128,2048]{1,0:T(8,128)(2,1)S(1)}, u32[]{:S(2)}, u32[]{:S(2)}) collective-permute-start(bf16[128,2048]{1,0:T(8,128)(2,1)S(1)} %constant_dynamic-slice_fusion), channel_id=1, source_target_pairs={{0,8},{4,12},{8,0},{12,4},{16,24},{20,28},{24,16},{28,20},{1,9},{5... | collective-permute-start | bytes 1572872 | tf_op jit(solution)/shard_map/ppermute | solution.py:413
  776.8 15.4 %collective-permute-start.55 = (bf16[128,2048]{1,0:T(8,128)(2,1)S(1)}, bf16[128,2048]{1,0:T(8,128)(2,1)S(1)}, u32[]{:S(2)}, u32[]{:S(2)}) collective-permute-start(bf16[128,2048]{1,0:T(8,128)(2,1)S(1)} %add_convert_fusion.14), channel_id=1, source_target_pairs={{0,16},{4,20},{8,24},{12,28},{16,0},{20,4},{24,8},{28,12},{1,17},{... | collective-permute-start | bytes 1572872 | tf_op jit(solution)/shard_map/ppermute | solution.py:413
  779.2 13.0 %collective-permute-start.56 = (bf16[128,2048]{1,0:T(8,128)(2,1)S(1)}, bf16[128,2048]{1,0:T(8,128)(2,1)S(1)}, u32[]{:S(2)}, u32[]{:S(2)}) collective-permute-start(bf16[128,2048]{1,0:T(8,128)(2,1)S(1)} %add_convert_fusion.13), channel_id=1, source_target_pairs={{0,8},{4,12},{8,0},{12,4},{16,24},{20,28},{24,16},{28,20},{1,9},{5... | collective-permute-start | bytes 1572872 | tf_op jit(solution)/shard_map/ppermute | solution.py:413
  792.4 35.9 %collective-permute-start.64 = (bf16[256,2048]{1,0:T(8,128)(2,1)S(1)}, bf16[256,2048]{1,0:T(8,128)(2,1)S(1)}, u32[]{:S(2)}, u32[]{:S(2)}) collective-permute-start(bf16[256,2048]{1,0:T(8,128)(2,1)S(1)} %maximum_select_fusion.3.refs_2_), channel_id=1, source_target_pairs={{0,16},{4,20},{8,24},{12,28},{16,0},{20,4},{24,8},{28,12},{1,17},{... | collective-permute-start | bytes 3145736 | tf_op jit(solution)/shard_map/ppermute | solution.py:413
  793.6 34.7 %collective-permute-start.63 = (bf16[256,2048]{1,0:T(8,128)(2,1)S(1)}, bf16[256,2048]{1,0:T(8,128)(2,1)}, u32[]{:S(2)}, u32[]{:S(2)}) collective-permute-start(bf16[256,2048]{1,0:T(8,128)(2,1)S(1)} %maximum_select_fusion.2.refs_0_), channel_id=1, source_target_pairs={{0,8},{4,12},{8,0},{12,4},{16,24},{20,28},{24,16},{28,20},{1,9},{5... | collective-permute-start | bytes 3145736 | tf_op jit(solution)/shard_map/ppermute | solution.py:413
  803.7 11.1 %collective-permute-start.60 = (f32[14,1024]{1,0:T(8,128)S(1)}, f32[14,1024]{1,0:T(8,128)S(1)}, u32[]{:S(2)}, u32[]{:S(2)}) collective-permute-start(f32[14,1024]{1,0:T(8,128)S(1)} %add.461), channel_id=1, source_target_pairs={{0,2},{1,3},{2,0},{3,1},{4,6},{5,7},{6,4},{7,5},{8,10},{9,11},{10,... | collective-permute-start | bytes 172040 | tf_op jit(solution)/shard_map/ppermute | solution.py:669
  832.9 17.7 %collective-permute-start.66 = (bf16[1024,2048]{1,0:T(8,128)(2,1)}, bf16[1024,2048]{1,0:T(8,128)(2,1)}, u32[]{:S(2)}, u32[]{:S(2)}) collective-permute-start(bf16[1024,2048]{1,0:T(8,128)(2,1)} %assemble.5.half_ref), channel_id=1, source_target_pairs={{0,4},{4,0},{8,12},{12,8},{16,20},{20,16},{24,28},{28,24},{1,5},{5... | collective-permute-start | bytes 12582920 | tf_op jit(solution)/shard_map/ppermute | solution.py:413
  (108 other events, 1476.0 us)
Sparse Core Ops, SparseCore 0:
  12.8 83.4 all-gather.6
  97.8 85.6 all-gather.8
  209.9 52.5 all-gather.14
  271.0 87.0 all-gather.10
  424.1 75.2 reduce-scatter.3
  543.1 80.0 all-gather.12
  637.9 79.5 reduce-scatter.5
  740.8 80.7 reduce-scatter.7

commit v15 on v14

--- a/solution.py
+++ b/solution.py
@@ -787,9 +787,11 @@
     small = jnp.concatenate([
         jnp.sum(part_one * unit_rows, axis=0), jnp.sum(part_one, axis=0), grad_gain_two, grad_shift_two,
         jnp.where(tp_row, bias_grad[None, :], 0.0).reshape(-1)])
+    sums = sum_over_all(after(small, held).reshape(-1, 1024))
+    small = [next(sums) for _ in range(1 + int(math.log2(n_tp)))]
     held = take(chain)
     go(chain)
-    held = take(chain)
+    held = take(chain, small)
     go(chain)
     grad_down_w = unpack_cols(*take(dw, held))
     held = take(chain, grad_down_w)
@@ -798,9 +800,7 @@
     mixed_late, out_sum = after((mixed, out_sum), held)
     out_tokens = (mixed_late + out_sum.astype(F32)).astype(BF16)
     grad_gate_w, grad_up_w = unpack_rows(*take(gu, held), 2)
-    sums = sum_over_all(after(small, held).reshape(-1, 1024))
-    small = [next(sums) for _ in range(1 + int(math.log2(n_tp)))]
-    take(chain, (grad_gate_w, small))
+    take(chain, grad_gate_w)
     go(chain)
     for _ in range(4):
         small = next(sums)

time: 877 us -> 885 us (level)
  waiting for transfers between devices: 385 us -> 394 us
where the time goes in v15:
time: 885 us; the launch traced here: 879 us
  waiting for transfers between devices  394 us (45%)
  Pallas kernels  192 us (22%)
  matrix products  111 us (13%)
  starting transfers between devices  61.4 us (7%)
  other arithmetic  59.3 us (7%)
  local copies, waits for them, and re-layouts  45.8 us (5%)
  between operations  15.9 us (2%)
    ppermute x53, waiting for transfers between devices, ctx_swap(): return lax.ppermute(x, 'ctx', [(i, i ^ mask) for i in range(n)])  201 us
    pallas_call x4, Pallas kernels, attention_call(): pl.pallas_call(kernel, grid_spec=pltpu.PrefetchScalarGridSpec(num_scalar_...  108 us
    all_gather x4, waiting for transfers between devices, all_rows(): return lax.all_gather(x, 'tp', axis=0, tiled=True)  102 us
    dot_general x8, matrix products, rc(): lax.dot_general(left, right, (((0,), (0,)), ((), ())), preferred_element_...  48.9 us
    ppermute x53, starting transfers between devices, ctx_swap(): return lax.ppermute(x, 'ctx', [(i, i ^ mask) for i in range(n)])  46.2 us
    dot_general x6, matrix products, nt(): lax.dot_general(a, b, (((1,), (1,)), ((), ())), preferred_element_type=jn...  46 us
    ppermute x6, waiting for transfers between devices, tp_shift(): return lax.ppermute(x, 'tp', [(i, (i + d) % n) for i in range(n)])  35.1 us
    ppermute x3, waiting for transfers between devices, gather_tp(): lax.ppermute(x, 'tp', [(i, (i + d) % n) for i in range(n)])  29.1 us
  transfers between devices with their start and end apart: 75, of which 36 were waited for; matrix products, arithmetic and copies ran while one was open for 17% of the time, Pallas kernels for 17%

profile of v15, /device:TPU:0, one launch (start us, length us, event | category | flops | bytes accessed | tf_op | source)
XLA Modules:
  0.0 879.4 jit_solution(10203474799618174578)
XLA Ops:
  12.7 83.6 %all-gather.7.cloned.1.call-done.h_ref = bf16[1024,2048]{1,0:T(8,128)(2,1)} async-done(((bf16[256,2048]{1,0:T(8,128)(2,1)}), bf16[1024,2048]{1,0:T(8,128)(2,1)}) %all-gather.7.cloned.1.call-update) | async-done | bytes 4194320 | tf_op jit(solution)/shard_map/all_gather | solution.py:596
  99.2 11.8 %project.1 = (bf16[4,256,512]{2,1,0:T(8,128)(2,1)S(1)}, bf16[2,4,256,512]{3,2,1,0:T(8,128)(2,1)}) custom-call(bf16[1024,2048]{1,0:T(8,128)(2,1)} %all-gather.7.cloned.1.call-done.h_ref, bf16[2048,512]{1,0:T(8,128)(2,1)} %wq_ref.1, bf16[2048,512]{1,0:T(8,128)(2,1)} %wk_ref.1, bf16[2048,512]{1,0:T(8,128)(2,1)} %wv_ref.1, ...), custom_call_target="tpu_custom_call" | custom-call | flops 6442450944 | bytes 6291456 | tf_op jit(solution)/shard_map/project/pallas_call | solution.py:357
  114.9 44.7 %collective-permute-done.3.refs_4_.refs_12_ = bf16[2,4,2,128,512]{4,3,2,1,0:T(8,128)(2,1)} collective-permute-done((bf16[2,4,2,128,512]{4,3,2,1,0:T(8,128)(2,1)}, bf16[2,4,2,128,512]{4,3,2,1,0:T(8,128)(2,1)}, u32[]{:S(2)}, u32[]{:S(2)}) %collective-permute-start.3) | collective-permute-done | bytes 2097184 | tf_op jit(solution)/shard_map/ppermute | solution.py:413
  170.1 9.3 %collective-permute-done.14 = bf16[64,2048]{1,0:T(8,128)(2,1)S(1)} collective-permute-done((bf16[64,2048]{1,0:T(8,128)(2,1)S(1)}, bf16[64,2048]{1,0:T(8,128)(2,1)S(1)}, u32[]{:S(2)}, u32[]{:S(2)}) %collective-permute-start.14) | collective-permute-done | bytes 262176 | tf_op jit(solution)/shard_map/ppermute | solution.py:679
  179.5 19.8 %collective-permute-done.13 = bf16[64,2048]{1,0:T(8,128)(2,1)S(1)} collective-permute-done((bf16[64,2048]{1,0:T(8,128)(2,1)S(1)}, bf16[64,2048]{1,0:T(8,128)(2,1)S(1)}, u32[]{:S(2)}, u32[]{:S(2)}) %collective-permute-start.13) | collective-permute-done | bytes 262176 | tf_op jit(solution)/shard_map/ppermute | solution.py:679
  206.2 3.4 collective-permute-done.8.refs_15_
  211.3 29.9 %attend.1 = (bf16[4,256,512]{2,1,0:T(8,128)(2,1)}, bf16[4,256,128]{2,1,0:T(8,128)(2,1)}) custom-call(s32[4,16]{1,0:T(4,128)} %copy.44.place_ref, s32[4,2]{1,0:T(4,128)} %get-tuple-element.259.own_ref, bf16[4,256,512]{2,1,0:T(8,128)(2,1)} %copy-done.2, bf16[2,4,2,128,512]{4,3,2,1,0:T(8,128)(2,1)} %bitcast.5.refs_0_.refs_8_, ...), custom_call_target="tpu_custom_call" | custom-call | flops 1073741824 | bytes 4194304 | tf_op jit(solution)/shard_map/attend/pallas_call | solution.py:233
  243.5 3.8 collective-permute-start.11
  247.3 7.5 collective-permute-done.9
  254.8 10.0 %collective-permute-done.10 = bf16[256,512]{1,0:T(8,128)(2,1)S(1)} collective-permute-done((bf16[256,512]{1,0:T(8,128)(2,1)S(1)}, bf16[256,512]{1,0:T(8,128)(2,1)S(1)}, u32[]{:S(2)}, u32[]{:S(2)}) %collective-permute-start.10) | collective-permute-done | bytes 262176 | tf_op jit(solution)/shard_map/ppermute | solution.py:601
  265.9 6.1 fusion.84
  279.0 29.4 %collective-permute-done.20.refs_6_ = bf16[1,4,2,128,640]{4,3,2,1,0:T(8,128)(2,1)} collective-permute-done((bf16[1,4,2,128,640]{4,3,2,1,0:T(8,128)(2,1)}, bf16[1,4,2,128,640]{4,3,2,1,0:T(8,128)(2,1)}, u32[]{:S(2)}, u32[]{:S(2)}) %collective-permute-start.20) | collective-permute-done | bytes 1310752 | tf_op jit(solution)/shard_map/ppermute | solution.py:413
  308.4 24.8 %collective-permute-done.18.refs_4_ = bf16[1,4,2,128,640]{4,3,2,1,0:T(8,128)(2,1)} collective-permute-done((bf16[1,4,2,128,640]{4,3,2,1,0:T(8,128)(2,1)}, bf16[1,4,2,128,640]{4,3,2,1,0:T(8,128)(2,1)}, u32[]{:S(2)}, u32[]{:S(2)}) %collective-permute-start.18) | collective-permute-done | bytes 1310752 | tf_op jit(solution)/shard_map/ppermute | solution.py:413
  333.8 2.9 collective-permute-done.19.refs_5_
  338.5 18.1 %all-gather.11.cloned.1.call-done.h_ref = bf16[1024,2048]{1,0:T(8,128)(2,1)} async-done(((bf16[256,2048]{1,0:T(8,128)(2,1)}), bf16[1024,2048]{1,0:T(8,128)(2,1)}) %all-gather.11.cloned.1.call-update) | async-done | bytes 4194320 | tf_op jit(solution)/shard_map/all_gather | solution.py:596
  356.6 28.9 %mlp.1 = (bf16[1024,1408]{1,0:T(8,128)(2,1)}, bf16[1024,2816]{1,0:T(8,128)(2,1)}) custom-call(bf16[1024,2048]{1,0:T(8,128)(2,1)} %all-gather.11.cloned.1.call-done.h_ref, bf16[1024,2048]{1,0:T(8,128)(2,1)} %all-gather.9.cloned.1.call-done.dy_ref, bf16[2048,1408]{1,0:T(8,128)(2,1)} %gate_ref.1, bf16[2048,1408]{1,0:T(8,128)(2,1)} %up_ref.1, ...), custom_call_target="tpu_custom_call" | custom-call | flops 17716740096 | bytes 38273024 | tf_op jit(solution)/shard_map/mlp/pallas_call | solution.py:397
  385.5 9.8 %fusion.5 = f32[1024,2048]{1,0:T(8,128)S(1)} fusion(bf16[2048,1408]{1,0:T(8,128)(2,1)} %gate_ref.1, bf16[1024,2816]{1,0:T(8,128)(2,1)} %get-tuple-element.146), kind=kOutput, calls=%fused_computation.25 | convolution fusion | flops 5905580032 | bytes 17039360 | tf_op jit(solution)/shard_map/dot_general | solution.py:15
  395.3 11.1 %add_convert_fusion.1 = bf16[1024,2048]{1,0:T(8,128)(2,1)} fusion(f32[1024,2048]{1,0:T(8,128)S(1)} %fusion.5, bf16[2048,1408]{1,0:T(8,128)(2,1)} %up_ref.1, bf16[1024,2816]{1,0:T(8,128)(2,1)S(1)} %copy-done.96), kind=kOutput, calls=%fused_computation.5 | convolution fusion | flops 5909774336 | bytes 21233664 | tf_op jit(solution)/shard_map/dot_general | solution.py:15
  406.4 11.1 %convolution_convert_fusion = bf16[1024,2816]{1,0:T(8,128)(2,1)} fusion(bf16[1024,2816]{1,0:T(8,128)(2,1)} %get-tuple-element.146, bf16[1024,2048]{1,0:T(8,128)(2,1)} %all-gather.11.cloned.1.call-done.h_ref, s32[]{:T(128)S(6)} %select_n.342), kind=kOutput, calls=%fused_computation.8 | convolution fusion | flops 5908463616 | bytes 13631492 | tf_op jit(solution)/shard_map/dot_general | solution.py:302
  417.5 4.5 convolution_convert_fusion.3
  422.6 8.7 collective-permute-done.23
  431.3 6.6 add_convert_fusion.2
  439.9 10.8 %add_convert_fusion = bf16[1024,2816]{1,0:T(8,128)(2,1)S(1)} fusion(bf16[1024,2816]{1,0:T(8,128)(2,1)} %collective-permute-done.22, bf16[1024,2816]{1,0:T(8,128)(2,1)} %get-tuple-element.146, bf16[1024,2048]{1,0:T(8,128)(2,1)S(1)} %copy-done.93, s32[]{:T(128)S(6)} %select_n.341), kind=kOutput, calls=%fused_computation | convolution fusion | flops 5914230784 | bytes 19398660 | tf_op jit(solution)/shard_map/dot_general | solution.py:302
  456.6 8.2 convolution_convert_fusion.1
  464.8 21.6 %collective-permute-done.24 = bf16[256,2816]{1,0:T(8,128)(2,1)} collective-permute-done((bf16[256,2816]{1,0:T(8,128)(2,1)}, bf16[256,2816]{1,0:T(8,128)(2,1)}, u32[]{:S(2)}, u32[]{:S(2)}) %collective-permute-start.24) | collective-permute-done | bytes 1441824 | tf_op jit(solution)/shard_map/ppermute | solution.py:413
  486.4 2.4 collective-permute-done.25
  498.0 2.9 fusion.24
  500.9 2.6 fusion.78
  503.5 6.2 convolution_convert_fusion.4
  509.7 3.9 collective-permute-done.30
  516.8 2.3 collective-permute-start.26
  521.1 13.3 %collective-permute-done.26 = bf16[256,512]{1,0:T(8,128)(2,1)S(1)} collective-permute-done((bf16[256,512]{1,0:T(8,128)(2,1)S(1)}, bf16[256,512]{1,0:T(8,128)(2,1)S(1)}, u32[]{:S(2)}, u32[]{:S(2)}) %collective-permute-start.26) | collective-permute-done | bytes 262176 | tf_op jit(solution)/shard_map/ppermute | solution.py:601
  534.4 4.3 collective-permute-done.27
  545.7 35.4 %query_grad.1 = bf16[4,256,512]{2,1,0:T(8,128)(2,1)} custom-call(s32[4,16]{1,0:T(4,128)} %copy.44.place_ref, s32[4,2]{1,0:T(4,128)} %get-tuple-element.259.own_ref, bf16[4,256,512]{2,1,0:T(8,128)(2,1)} %copy-done.2, bf16[4,256,512]{2,1,0:T(8,128)(2,1)} %bitcast.79, bf16[4,256,128]{2,1,0:T(8,128)(2,1)} %get-tuple-element.139.qx_ref, ...), custom_call_target="tpu_custom_call" | custom-call | flops 1610612736 | bytes 4194304 | tf_op jit(solution)/shard_map/query_grad/pallas_call | solution.py:233
  581.1 18.9 %collective-permute-done.34.refs_12_ = bf16[1,4,2,128,640]{4,3,2,1,0:T(8,128)(2,1)} collective-permute-done((bf16[1,4,2,128,640]{4,3,2,1,0:T(8,128)(2,1)S(1)}, bf16[1,4,2,128,640]{4,3,2,1,0:T(8,128)(2,1)}, u32[]{:S(2)}, u32[]{:S(2)}) %collective-permute-start.34) | collective-permute-done | bytes 1310752 | tf_op jit(solution)/shard_map/ppermute | solution.py:413
  608.1 20.1 %key_value_grad.2 = (bf16[2,256,512]{2,1,0:T(8,128)(2,1)}, bf16[2,256,512]{2,1,0:T(8,128)(2,1)}) custom-call(s32[4,16]{1,0:T(4,128)} %copy.44.place_ref, s32[4,2]{1,0:T(4,128)} %get-tuple-element.259.own_ref, bf16[2,4,256,512]{3,2,1,0:T(8,128)(2,1)} %get-tuple-element.133.kv_ref, f32[1024,128]{1,0:T(8,128)} %copy-done.6, f32[1024,128]{1,0:T(8,128)} %copy-done.5, ...), custom_call_target="tpu_custom_call" | custom-call | flops 1073741824 | bytes 2097152 | tf_op jit(solution)/shard_map/key_value_grad/pallas_call | solution.py:233
  630.0 3.1 collective-permute-start.42
  635.4 4.6 collective-permute-start.43
  642.1 22.9 %key_value_grad.3 = (bf16[2,256,512]{2,1,0:T(8,128)(2,1)}, bf16[2,256,512]{2,1,0:T(8,128)(2,1)}) custom-call(s32[4,16]{1,0:T(4,128)} %copy.44.place_ref, s32[4,2]{1,0:T(4,128)} %get-tuple-element.259.own_ref, bf16[2,4,256,512]{3,2,1,0:T(8,128)(2,1)} %get-tuple-element.133.kv_ref, f32[1024,128]{1,0:T(8,128)} %copy-done.6, f32[1024,128]{1,0:T(8,128)} %copy-done.5, ...), custom_call_target="tpu_custom_call" | custom-call | flops 1073741824 | bytes 2097152 | tf_op jit(solution)/shard_map/key_value_grad/pallas_call | solution.py:233
  671.9 2.4 fusion.87
  674.3 5.8 fusion.86
  680.1 10.8 %fusion.85 = (bf16[1024,2048]{1,0:T(8,128)(2,1)}, f32[1024,2048]{1,0:T(8,128)}) fusion(f32[1024,2048]{1,0:T(8,128)S(1)} %fusion.87, f32[1024,2048]{1,0:T(8,128)} %fusion.86, bf16[1024,512]{1,0:T(8,128)(2,1)S(1)} %bitcast.78, bf16[2048,512]{1,0:T(8,128)(2,1)S(1)} %copy-done.56), kind=kOutput, calls=%fused_computation.208 | convolution fusion | flops 2153775104 | bytes 32505856 | tf_op jit(solution)/shard_map/dot_general | solution.py:15
  693.9 4.1 fusion.47
  698.0 3.7 convolution_convert_fusion.2
  701.7 2.7 pad_maximum_fusion
  708.3 2.8 collective-permute-start.49
  711.2 5.8 fusion.77
  717.4 2.6 fusion.29
  720.0 5.5 fusion.31
  728.5 5.3 fusion
  738.9 5.6 assemble.4.half_ref
  747.2 14.5 %collective-permute-done.51 = bf16[256,2048]{1,0:T(8,128)(2,1)} collective-permute-done((bf16[256,2048]{1,0:T(8,128)(2,1)}, bf16[256,2048]{1,0:T(8,128)(2,1)}, u32[]{:S(2)}, u32[]{:S(2)}) %collective-permute-start.51) | collective-permute-done | bytes 1048608 | tf_op jit(solution)/shard_map/ppermute | solution.py:413
  764.6 6.1 collective-permute-done.52
  776.1 6.9 collective-permute-done.56
  784.3 10.2 %collective-permute-done.57 = f32[14,1024]{1,0:T(8,128)S(1)} collective-permute-done((f32[14,1024]{1,0:T(8,128)S(1)}, f32[14,1024]{1,0:T(8,128)S(1)}, u32[]{:S(2)}, u32[]{:S(2)}) %collective-permute-start.57) | collective-permute-done | bytes 57376 | tf_op jit(solution)/shard_map/ppermute | solution.py:669
  799.1 8.8 %unpack_cols.1 = f32[1408,2048]{1,0:T(8,128)} custom-call(s32[1]{0:T(128)} %bitcast.19.core_ref, bf16[1408,1024]{1,0:T(8,128)(2,1)S(1)} %assemble.3.half_ref, bf16[1408,1024]{1,0:T(8,128)(2,1)} %collective-permute-done.60.other_ref), custom_call_target="tpu_custom_call" | custom-call | bytes 1024 | tf_op jit(solution)/shard_map/unpack_cols/pallas_call | solution.py:583
  814.1 13.6 %unpack_rows.2 = (f32[2048,1408]{1,0:T(8,128)}, f32[2048,1408]{1,0:T(8,128)}) custom-call(s32[1]{0:T(128)} %bitcast.19.core_ref, bf16[1024,2816]{1,0:T(8,128)(2,1)} %assemble.4.half_ref, bf16[1024,2816]{1,0:T(8,128)(2,1)} %collective-permute-done.65.other_ref), custom_call_target="tpu_custom_call" | custom-call | bytes 1024 | tf_op jit(solution)/shard_map/unpack_rows/pallas_call | solution.py:555
  827.7 8.0 collective-permute-done.64.refs_3_
  837.5 3.1 assemble.5.half_ref
  841.1 4.0 collective-permute-done.61
  845.5 4.0 collective-permute-done.62
  853.3 2.6 add_convert_fusion.5
  857.9 3.1 fusion.18
  861.0 11.4 %unpack_rows.3 = (f32[2048,512]{1,0:T(8,128)}, f32[2048,512]{1,0:T(8,128)}, f32[2048,512]{1,0:T(8,128)}, f32[512,2048]{1,0:T(8,128)}) custom-call(s32[1]{0:T(128)} %bitcast.19.core_ref, bf16[1024,2048]{1,0:T(8,128)(2,1)} %assemble.5.half_ref, bf16[1024,2048]{1,0:T(8,128)(2,1)} %collective-permute-done.66.other_ref), custom_call_target="tpu_custom_call" | custom-call | bytes 1024 | tf_op jit(solution)/shard_map/unpack_rows/pallas_call | solution.py:555
  (448 shorter events, 141.2 us)
Async XLA Ops:
  7.2 89.0 %all-gather.7.cloned.1.call-start = ((), (), s32[]{:S(2)}) async-start(), calls=%async_computation.3 | async-start | bytes 5242880 | tf_op jit(solution)/shard_map/all_gather | solution.py:596
  12.6 197.1 %all-gather.9.cloned.1.call-start = ((), (), s32[]{:S(2)}) async-start(), calls=%async_computation.4 | async-start | bytes 5242880 | tf_op jit(solution)/shard_map/all_gather | solution.py:596
  96.3 168.7 %all-gather.15.cloned.1.call-start = ((), (), s32[]{:S(2)}) async-start(), calls=%async_computation.10 | async-start | bytes 9437184 | tf_op jit(solution)/shard_map/all_gather | solution.py:710
  112.0 47.7 %collective-permute-start.3 = (bf16[2,4,2,128,512]{4,3,2,1,0:T(8,128)(2,1)}, bf16[2,4,2,128,512]{4,3,2,1,0:T(8,128)(2,1)}, u32[]{:S(2)}, u32[]{:S(2)}) collective-permute-start(bf16[2,4,2,128,512]{4,3,2,1,0:T(8,128)(2,1)} %bitcast.5.refs_0_.refs_8_), channel_id=1, source_target_pairs={{0,16},{4,20},{8,24},{12,28},{16,0},{20,4},{24,8},{28,12},{1,17},{... | collective-permute-start | bytes 6291464 | tf_op jit(solution)/shard_map/ppermute | solution.py:413
  113.4 49.9 %collective-permute-start.1 = (bf16[2,4,2,128,512]{4,3,2,1,0:T(8,128)(2,1)}, bf16[2,4,2,128,512]{4,3,2,1,0:T(8,128)(2,1)}, u32[]{:S(2)}, u32[]{:S(2)}) collective-permute-start(bf16[2,4,2,128,512]{4,3,2,1,0:T(8,128)(2,1)} %bitcast.5.refs_0_.refs_8_), channel_id=1, source_target_pairs={{0,8},{4,12},{8,0},{12,4},{16,24},{20,28},{24,16},{28,20},{1,9},{5... | collective-permute-start | bytes 6291464 | tf_op jit(solution)/shard_map/ppermute | solution.py:413
  161.9 40.6 %collective-permute-start.7 = (bf16[1,4,2,128,512]{4,3,2,1,0:T(8,128)(2,1)}, bf16[1,4,2,128,512]{4,3,2,1,0:T(8,128)(2,1)S(1)}, u32[]{:S(2)}, u32[]{:S(2)}) collective-permute-start(bf16[1,4,2,128,512]{4,3,2,1,0:T(8,128)(2,1)} %slice.96), channel_id=1, source_target_pairs={{0,8},{4,12},{8,0},{12,4},{16,24},{20,28},{24,16},{28,20},{1,9},{5... | collective-permute-start | bytes 3145736 | tf_op jit(solution)/shard_map/ppermute | solution.py:413
  165.6 37.4 %collective-permute-start.5 = (bf16[1,4,2,128,512]{4,3,2,1,0:T(8,128)(2,1)}, bf16[1,4,2,128,512]{4,3,2,1,0:T(8,128)(2,1)}, u32[]{:S(2)}, u32[]{:S(2)}) collective-permute-start(bf16[1,4,2,128,512]{4,3,2,1,0:T(8,128)(2,1)} %slice.95), channel_id=1, source_target_pairs={{0,16},{4,20},{8,24},{12,28},{16,0},{20,4},{24,8},{28,12},{1,17},{... | collective-permute-start | bytes 3145736 | tf_op jit(solution)/shard_map/ppermute | solution.py:413
  167.1 12.3 %collective-permute-start.14 = (bf16[64,2048]{1,0:T(8,128)(2,1)S(1)}, bf16[64,2048]{1,0:T(8,128)(2,1)S(1)}, u32[]{:S(2)}, u32[]{:S(2)}) collective-permute-start(bf16[64,2048]{1,0:T(8,128)(2,1)S(1)} %constant_dynamic-slice_fusion.15), channel_id=1, source_target_pairs={{0,3},{1,0},{2,1},{3,2},{4,7},{5,4},{6,5},{7,6},{8,11},{9,8},{10,9... | collective-permute-start | bytes 786440 | tf_op jit(solution)/shard_map/ppermute | solution.py:679
  168.2 31.0 %collective-permute-start.13 = (bf16[64,2048]{1,0:T(8,128)(2,1)S(1)}, bf16[64,2048]{1,0:T(8,128)(2,1)S(1)}, u32[]{:S(2)}, u32[]{:S(2)}) collective-permute-start(bf16[64,2048]{1,0:T(8,128)(2,1)S(1)} %constant_dynamic-slice_fusion.15), channel_id=1, source_target_pairs={{0,2},{1,3},{2,0},{3,1},{4,6},{5,7},{6,4},{7,5},{8,10},{9,11},{10,... | collective-permute-start | bytes 786440 | tf_op jit(solution)/shard_map/ppermute | solution.py:679
  168.2 31.0 %collective-permute-start.12 = (bf16[64,2048]{1,0:T(8,128)(2,1)S(1)}, bf16[64,2048]{1,0:T(8,128)(2,1)S(1)}, u32[]{:S(2)}, u32[]{:S(2)}) collective-permute-start(bf16[64,2048]{1,0:T(8,128)(2,1)S(1)} %constant_dynamic-slice_fusion.15), channel_id=1, source_target_pairs={{0,1},{1,2},{2,3},{3,0},{4,5},{5,6},{6,7},{7,4},{8,9},{9,10},{10,1... | collective-permute-start | bytes 786440 | tf_op jit(solution)/shard_map/ppermute | solution.py:679
  179.5 26.7 %collective-permute-start = (bf16[2,4,2,128,512]{4,3,2,1,0:T(8,128)(2,1)}, bf16[2,4,2,128,512]{4,3,2,1,0:T(8,128)(2,1)S(1)}, u32[]{:S(2)}, u32[]{:S(2)}) collective-permute-start(bf16[2,4,2,128,512]{4,3,2,1,0:T(8,128)(2,1)} %bitcast.5.refs_0_.refs_8_), channel_id=1, source_target_pairs={{0,4},{4,0},{8,12},{12,8},{16,20},{20,16},{24,28},{28,24},{1,5},{5... | collective-permute-start | bytes 6291464 | tf_op jit(solution)/shard_map/ppermute | solution.py:413
  199.2 10.5 %collective-permute-start.4 = (bf16[2,4,2,128,512]{4,3,2,1,0:T(8,128)(2,1)}, bf16[2,4,2,128,512]{4,3,2,1,0:T(8,128)(2,1)}, u32[]{:S(2)}, u32[]{:S(2)}) collective-permute-start(bf16[2,4,2,128,512]{4,3,2,1,0:T(8,128)(2,1)} %collective-permute-done.3.refs_4_.refs_12_), channel_id=1, source_target_pairs={{0,4},{4,0},{8,12},{12,8},{16,20},{20,16},{24,28},{28,24},{1,5},{5... | collective-permute-start | bytes 6291464 | tf_op jit(solution)/shard_map/ppermute | solution.py:413
  200.6 9.1 %collective-permute-start.2 = (bf16[2,4,2,128,512]{4,3,2,1,0:T(8,128)(2,1)}, bf16[2,4,2,128,512]{4,3,2,1,0:T(8,128)(2,1)}, u32[]{:S(2)}, u32[]{:S(2)}) collective-permute-start(bf16[2,4,2,128,512]{4,3,2,1,0:T(8,128)(2,1)} %collective-permute-done.1.refs_2_.refs_10_), channel_id=1, source_target_pairs={{0,4},{4,0},{8,12},{12,8},{16,20},{20,16},{24,28},{28,24},{1,5},{5... | collective-permute-start | bytes 6291464 | tf_op jit(solution)/shard_map/ppermute | solution.py:413
  209.8 146.8 %all-gather.11.cloned.1.call-start = ((), (), s32[]{:S(2)}) async-start(), calls=%async_computation.5 | async-start | bytes 5242880 | tf_op jit(solution)/shard_map/all_gather | solution.py:596
  243.5 11.3 %collective-permute-start.9 = (bf16[256,512]{1,0:T(8,128)(2,1)}, bf16[256,512]{1,0:T(8,128)(2,1)S(1)}, u32[]{:S(2)}, u32[]{:S(2)}) collective-permute-start(bf16[256,512]{1,0:T(8,128)(2,1)} %get-tuple-element.272), channel_id=1, source_target_pairs={{0,1},{1,2},{2,3},{3,0},{4,5},{5,6},{6,7},{7,4},{8,9},{9,10},{10,1... | collective-permute-start | bytes 786440 | tf_op jit(solution)/shard_map/ppermute | solution.py:601
  243.5 21.3 %collective-permute-start.10 = (bf16[256,512]{1,0:T(8,128)(2,1)S(1)}, bf16[256,512]{1,0:T(8,128)(2,1)S(1)}, u32[]{:S(2)}, u32[]{:S(2)}) collective-permute-start(bf16[256,512]{1,0:T(8,128)(2,1)S(1)} %get-tuple-element.271), channel_id=1, source_target_pairs={{0,2},{1,3},{2,0},{3,1},{4,6},{5,7},{6,4},{7,5},{8,10},{9,11},{10,... | collective-permute-start | bytes 786440 | tf_op jit(solution)/shard_map/ppermute | solution.py:601
  243.5 21.4 %collective-permute-start.11 = (bf16[256,512]{1,0:T(8,128)(2,1)S(1)}, bf16[256,512]{1,0:T(8,128)(2,1)S(1)}, u32[]{:S(2)}, u32[]{:S(2)}) collective-permute-start(bf16[256,512]{1,0:T(8,128)(2,1)S(1)} %get-tuple-element.270), channel_id=1, source_target_pairs={{0,3},{1,0},{2,1},{3,2},{4,7},{5,4},{6,5},{7,6},{8,11},{9,8},{10,9... | collective-permute-start | bytes 786440 | tf_op jit(solution)/shard_map/ppermute | solution.py:601
  274.2 223.7 %reduce-scatter.4.cloned.1.call-start = ((), (), s32[]{:S(2)}) async-start(), calls=%async_computation.6 | async-start | bytes 5242880 | tf_op jit(solution)/shard_map/reduce_scatter | solution.py:624
  275.5 32.9 %collective-permute-start.20 = (bf16[1,4,2,128,640]{4,3,2,1,0:T(8,128)(2,1)}, bf16[1,4,2,128,640]{4,3,2,1,0:T(8,128)(2,1)}, u32[]{:S(2)}, u32[]{:S(2)}) collective-permute-start(bf16[1,4,2,128,640]{4,3,2,1,0:T(8,128)(2,1)} %bitcast.12.refs_0_), channel_id=1, source_target_pairs={{0,24},{4,28},{8,16},{12,20},{16,8},{20,12},{24,0},{28,4},{1,25},{... | collective-permute-start | bytes 3932168 | tf_op jit(solution)/shard_map/ppermute | solution.py:413
  276.9 56.4 %collective-permute-start.18 = (bf16[1,4,2,128,640]{4,3,2,1,0:T(8,128)(2,1)}, bf16[1,4,2,128,640]{4,3,2,1,0:T(8,128)(2,1)}, u32[]{:S(2)}, u32[]{:S(2)}) collective-permute-start(bf16[1,4,2,128,640]{4,3,2,1,0:T(8,128)(2,1)} %bitcast.12.refs_0_), channel_id=1, source_target_pairs={{0,16},{4,20},{8,24},{12,28},{16,0},{20,4},{24,8},{28,12},{1,17},{... | collective-permute-start | bytes 3932168 | tf_op jit(solution)/shard_map/ppermute | solution.py:413
  276.9 56.4 %collective-permute-start.16 = (bf16[1,4,2,128,640]{4,3,2,1,0:T(8,128)(2,1)}, bf16[1,4,2,128,640]{4,3,2,1,0:T(8,128)(2,1)}, u32[]{:S(2)}, u32[]{:S(2)}) collective-permute-start(bf16[1,4,2,128,640]{4,3,2,1,0:T(8,128)(2,1)} %bitcast.12.refs_0_), channel_id=1, source_target_pairs={{0,8},{4,12},{8,0},{12,4},{16,24},{20,28},{24,16},{28,20},{1,9},{5... | collective-permute-start | bytes 3932168 | tf_op jit(solution)/shard_map/ppermute | solution.py:413
  279.0 54.8 %collective-permute-start.15 = (bf16[1,4,2,128,640]{4,3,2,1,0:T(8,128)(2,1)}, bf16[1,4,2,128,640]{4,3,2,1,0:T(8,128)(2,1)}, u32[]{:S(2)}, u32[]{:S(2)}) collective-permute-start(bf16[1,4,2,128,640]{4,3,2,1,0:T(8,128)(2,1)} %bitcast.12.refs_0_), channel_id=1, source_target_pairs={{0,4},{4,0},{8,12},{12,8},{16,20},{20,16},{24,28},{28,24},{1,5},{5... | collective-permute-start | bytes 3932168 | tf_op jit(solution)/shard_map/ppermute | solution.py:413
  308.4 25.4 %collective-permute-start.21 = (bf16[1,4,2,128,640]{4,3,2,1,0:T(8,128)(2,1)}, bf16[1,4,2,128,640]{4,3,2,1,0:T(8,128)(2,1)}, u32[]{:S(2)}, u32[]{:S(2)}) collective-permute-start(bf16[1,4,2,128,640]{4,3,2,1,0:T(8,128)(2,1)} %collective-permute-done.20.refs_6_), channel_id=1, source_target_pairs={{0,4},{4,0},{8,12},{12,8},{16,20},{20,16},{24,28},{28,24},{1,5},{5... | collective-permute-start | bytes 3932168 | tf_op jit(solution)/shard_map/ppermute | solution.py:413
  417.5 22.5 %collective-permute-start.22 = (bf16[1024,2816]{1,0:T(8,128)(2,1)}, bf16[1024,2816]{1,0:T(8,128)(2,1)}, u32[]{:S(2)}, u32[]{:S(2)}) collective-permute-start(bf16[1024,2816]{1,0:T(8,128)(2,1)} %convolution_convert_fusion), channel_id=1, source_target_pairs={{0,4},{4,0},{8,12},{12,8},{16,20},{20,16},{24,28},{28,24},{1,5},{5... | collective-permute-start | bytes 17301512 | tf_op jit(solution)/shard_map/ppermute | solution.py:413
  422.0 9.3 %collective-permute-start.23 = (bf16[1408,1024]{1,0:T(8,128)(2,1)}, bf16[1408,1024]{1,0:T(8,128)(2,1)}, u32[]{:S(2)}, u32[]{:S(2)}) collective-permute-start(bf16[1408,1024]{1,0:T(8,128)(2,1)} %convolution_convert_fusion.3), channel_id=1, source_target_pairs={{0,4},{4,0},{8,12},{12,8},{16,20},{20,16},{24,28},{28,24},{1,5},{5... | collective-permute-start | bytes 8650760 | tf_op jit(solution)/shard_map/ppermute | solution.py:413
  422.5 268.4 %all-gather.13.cloned.1.call-start = ((), (), s32[]{:S(2)}) async-start(), calls=%async_computation.8 | async-start | bytes 5242880 | tf_op jit(solution)/shard_map/all_gather | solution.py:596
  452.4 33.9 %collective-permute-start.24 = (bf16[256,2816]{1,0:T(8,128)(2,1)}, bf16[256,2816]{1,0:T(8,128)(2,1)}, u32[]{:S(2)}, u32[]{:S(2)}) collective-permute-start(bf16[256,2816]{1,0:T(8,128)(2,1)} %constant_dynamic-slice_fusion.14), channel_id=1, source_target_pairs={{0,8},{4,12},{8,0},{12,4},{16,24},{20,28},{24,16},{28,20},{1,9},{5... | collective-permute-start | bytes 4325384 | tf_op jit(solution)/shard_map/ppermute | solution.py:413
  455.1 33.7 %collective-permute-start.25 = (bf16[256,2816]{1,0:T(8,128)(2,1)}, bf16[256,2816]{1,0:T(8,128)(2,1)}, u32[]{:S(2)}, u32[]{:S(2)}) collective-permute-start(bf16[256,2816]{1,0:T(8,128)(2,1)} %constant_dynamic-slice_fusion.13), channel_id=1, source_target_pairs={{0,16},{4,20},{8,24},{12,28},{16,0},{20,4},{24,8},{28,12},{1,17},{... | collective-permute-start | bytes 4325384 | tf_op jit(solution)/shard_map/ppermute | solution.py:413
  491.9 17.8 %collective-permute-start.29 = (bf16[128,2816]{1,0:T(8,128)(2,1)}, bf16[128,2816]{1,0:T(8,128)(2,1)}, u32[]{:S(2)}, u32[]{:S(2)}) collective-permute-start(bf16[128,2816]{1,0:T(8,128)(2,1)} %constant_dynamic-slice_fusion.9), channel_id=1, source_target_pairs={{0,16},{4,20},{8,24},{12,28},{16,0},{20,4},{24,8},{28,12},{1,17},{... | collective-permute-start | bytes 2162696 | tf_op jit(solution)/shard_map/ppermute | solution.py:413
  496.5 17.1 %collective-permute-start.30 = (bf16[128,2816]{1,0:T(8,128)(2,1)}, bf16[128,2816]{1,0:T(8,128)(2,1)}, u32[]{:S(2)}, u32[]{:S(2)}) collective-permute-start(bf16[128,2816]{1,0:T(8,128)(2,1)} %constant_dynamic-slice_fusion.8), channel_id=1, source_target_pairs={{0,8},{4,12},{8,0},{12,4},{16,24},{20,28},{24,16},{28,20},{1,9},{5... | collective-permute-start | bytes 2162696 | tf_op jit(solution)/shard_map/ppermute | solution.py:413
  514.9 25.4 %collective-permute-start.32 = (bf16[128,2816]{1,0:T(8,128)(2,1)S(1)}, bf16[128,2816]{1,0:T(8,128)(2,1)S(1)}, u32[]{:S(2)}, u32[]{:S(2)}) collective-permute-start(bf16[128,2816]{1,0:T(8,128)(2,1)S(1)} %add_convert_fusion.11), channel_id=1, source_target_pairs={{0,8},{4,12},{8,0},{12,4},{16,24},{20,28},{24,16},{28,20},{1,9},{5... | collective-permute-start | bytes 2162696 | tf_op jit(solution)/shard_map/ppermute | solution.py:413
  515.8 23.0 %collective-permute-start.28 = (bf16[256,512]{1,0:T(8,128)(2,1)S(1)}, bf16[256,512]{1,0:T(8,128)(2,1)S(1)}, u32[]{:S(2)}, u32[]{:S(2)}) collective-permute-start(bf16[256,512]{1,0:T(8,128)(2,1)S(1)} %get-tuple-element.266), channel_id=1, source_target_pairs={{0,3},{1,0},{2,1},{3,2},{4,7},{5,4},{6,5},{7,6},{8,11},{9,8},{10,9... | collective-permute-start | bytes 786440 | tf_op jit(solution)/shard_map/ppermute | solution.py:601
  516.6 22.1 %collective-permute-start.27 = (bf16[256,512]{1,0:T(8,128)(2,1)S(1)}, bf16[256,512]{1,0:T(8,128)(2,1)S(1)}, u32[]{:S(2)}, u32[]{:S(2)}) collective-permute-start(bf16[256,512]{1,0:T(8,128)(2,1)S(1)} %get-tuple-element.267), channel_id=1, source_target_pairs={{0,2},{1,3},{2,0},{3,1},{4,6},{5,7},{6,4},{7,5},{8,10},{9,11},{10,... | collective-permute-start | bytes 786440 | tf_op jit(solution)/shard_map/ppermute | solution.py:601
  516.8 17.5 %collective-permute-start.26 = (bf16[256,512]{1,0:T(8,128)(2,1)S(1)}, bf16[256,512]{1,0:T(8,128)(2,1)S(1)}, u32[]{:S(2)}, u32[]{:S(2)}) collective-permute-start(bf16[256,512]{1,0:T(8,128)(2,1)S(1)} %get-tuple-element.268), channel_id=1, source_target_pairs={{0,1},{1,2},{2,3},{3,0},{4,5},{5,6},{6,7},{7,4},{8,9},{9,10},{10,1... | collective-permute-start | bytes 786440 | tf_op jit(solution)/shard_map/ppermute | solution.py:601
  520.4 19.9 %collective-permute-start.31 = (bf16[128,2816]{1,0:T(8,128)(2,1)S(1)}, bf16[128,2816]{1,0:T(8,128)(2,1)S(1)}, u32[]{:S(2)}, u32[]{:S(2)}) collective-permute-start(bf16[128,2816]{1,0:T(8,128)(2,1)S(1)} %add_convert_fusion.12), channel_id=1, source_target_pairs={{0,16},{4,20},{8,24},{12,28},{16,0},{20,4},{24,8},{28,12},{1,17},{... | collective-permute-start | bytes 2162696 | tf_op jit(solution)/shard_map/ppermute | solution.py:413
  542.1 186.4 %reduce-scatter.6.cloned.1.call-start = ((), (), s32[]{:S(2)}) async-start(), calls=%async_computation.7 | async-start | bytes 5242880 | tf_op jit(solution)/shard_map/reduce_scatter | solution.py:624
  542.1 38.9 %collective-permute-start.35 = (bf16[1,4,2,128,640]{4,3,2,1,0:T(8,128)(2,1)S(1)}, bf16[1,4,2,128,640]{4,3,2,1,0:T(8,128)(2,1)}, u32[]{:S(2)}, u32[]{:S(2)}) collective-permute-start(bf16[1,4,2,128,640]{4,3,2,1,0:T(8,128)(2,1)S(1)} %bitcast.71), channel_id=1, source_target_pairs={{0,24},{4,28},{8,16},{12,20},{16,8},{20,12},{24,0},{28,4},{1,25},{... | collective-permute-start | bytes 3932168 | tf_op jit(solution)/shard_map/ppermute | solution.py:413
  543.7 56.3 %collective-permute-start.34 = (bf16[1,4,2,128,640]{4,3,2,1,0:T(8,128)(2,1)S(1)}, bf16[1,4,2,128,640]{4,3,2,1,0:T(8,128)(2,1)}, u32[]{:S(2)}, u32[]{:S(2)}) collective-permute-start(bf16[1,4,2,128,640]{4,3,2,1,0:T(8,128)(2,1)S(1)} %bitcast.72), channel_id=1, source_target_pairs={{0,16},{4,20},{8,24},{12,28},{16,0},{20,4},{24,8},{28,12},{1,17},{... | collective-permute-start | bytes 3932168 | tf_op jit(solution)/shard_map/ppermute | solution.py:413
  544.2 56.8 %collective-permute-start.33 = (bf16[1,4,2,128,640]{4,3,2,1,0:T(8,128)(2,1)S(1)}, bf16[1,4,2,128,640]{4,3,2,1,0:T(8,128)(2,1)}, u32[]{:S(2)}, u32[]{:S(2)}) collective-permute-start(bf16[1,4,2,128,640]{4,3,2,1,0:T(8,128)(2,1)S(1)} %bitcast.73), channel_id=1, source_target_pairs={{0,8},{4,12},{8,0},{12,4},{16,24},{20,28},{24,16},{28,20},{1,9},{5... | collective-permute-start | bytes 3932168 | tf_op jit(solution)/shard_map/ppermute | solution.py:413
  545.7 59.4 %collective-permute-start.36 = (bf16[1,4,2,128,640]{4,3,2,1,0:T(8,128)(2,1)S(1)}, bf16[1,4,2,128,640]{4,3,2,1,0:T(8,128)(2,1)}, u32[]{:S(2)}, u32[]{:S(2)}) collective-permute-start(bf16[1,4,2,128,640]{4,3,2,1,0:T(8,128)(2,1)S(1)} %bitcast.74), channel_id=1, source_target_pairs={{0,4},{4,0},{8,12},{12,8},{16,20},{20,16},{24,28},{28,24},{1,5},{5... | collective-permute-start | bytes 3932168 | tf_op jit(solution)/shard_map/ppermute | solution.py:413
  602.4 25.8 %collective-permute-start.41 = (bf16[352,1024]{1,0:T(8,128)(2,1)}, bf16[352,1024]{1,0:T(8,128)(2,1)}, u32[]{:S(2)}, u32[]{:S(2)}) collective-permute-start(bf16[352,1024]{1,0:T(8,128)(2,1)} %constant_dynamic-slice_fusion.6), channel_id=1, source_target_pairs={{0,16},{4,20},{8,24},{12,28},{16,0},{20,4},{24,8},{28,12},{1,17},{... | collective-permute-start | bytes 2162696 | tf_op jit(solution)/shard_map/ppermute | solution.py:413
  605.0 23.2 %collective-permute-start.40 = (bf16[352,1024]{1,0:T(8,128)(2,1)}, bf16[352,1024]{1,0:T(8,128)(2,1)}, u32[]{:S(2)}, u32[]{:S(2)}) collective-permute-start(bf16[352,1024]{1,0:T(8,128)(2,1)} %constant_dynamic-slice_fusion.7), channel_id=1, source_target_pairs={{0,8},{4,12},{8,0},{12,4},{16,24},{20,28},{24,16},{28,20},{1,9},{5... | collective-permute-start | bytes 2162696 | tf_op jit(solution)/shard_map/ppermute | solution.py:413
  630.0 35.0 %collective-permute-start.42 = (bf16[176,1024]{1,0:T(8,128)(2,1)S(1)}, bf16[176,1024]{1,0:T(8,128)(2,1)}, u32[]{:S(2)}, u32[]{:S(2)}) collective-permute-start(bf16[176,1024]{1,0:T(8,128)(2,1)S(1)} %constant_dynamic-slice_fusion.5), channel_id=1, source_target_pairs={{0,16},{4,20},{8,24},{12,28},{16,0},{20,4},{24,8},{28,12},{1,17},{... | collective-permute-start | bytes 1081352 | tf_op jit(solution)/shard_map/ppermute | solution.py:413
  635.4 29.6 %collective-permute-start.43 = (bf16[176,1024]{1,0:T(8,128)(2,1)}, bf16[176,1024]{1,0:T(8,128)(2,1)}, u32[]{:S(2)}, u32[]{:S(2)}) collective-permute-start(bf16[176,1024]{1,0:T(8,128)(2,1)} %constant_dynamic-slice_fusion.4), channel_id=1, source_target_pairs={{0,8},{4,12},{8,0},{12,4},{16,24},{20,28},{24,16},{28,20},{1,9},{5... | collective-permute-start | bytes 1081352 | tf_op jit(solution)/shard_map/ppermute | solution.py:413
  640.0 215.8 %reduce-scatter.8.cloned.1.call-start = ((), (), s32[]{:S(2)}) async-start(), calls=%async_computation.9 | async-start | bytes 5242880 | tf_op jit(solution)/shard_map/reduce_scatter | solution.py:624
  640.1 50.9 %collective-permute-start.44 = (bf16[256,2816]{1,0:T(8,128)(2,1)S(1)}, bf16[256,2816]{1,0:T(8,128)(2,1)}, u32[]{:S(2)}, u32[]{:S(2)}) collective-permute-start(bf16[256,2816]{1,0:T(8,128)(2,1)S(1)} %maximum_select_fusion.refs_0_), channel_id=1, source_target_pairs={{0,8},{4,12},{8,0},{12,4},{16,24},{20,28},{24,16},{28,20},{1,9},{5... | collective-permute-start | bytes 4325384 | tf_op jit(solution)/shard_map/ppermute | solution.py:413
  640.1 50.9 %collective-permute-start.45 = (bf16[256,2816]{1,0:T(8,128)(2,1)S(1)}, bf16[256,2816]{1,0:T(8,128)(2,1)}, u32[]{:S(2)}, u32[]{:S(2)}) collective-permute-start(bf16[256,2816]{1,0:T(8,128)(2,1)S(1)} %maximum_select_fusion.1.refs_2_), channel_id=1, source_target_pairs={{0,16},{4,20},{8,24},{12,28},{16,0},{20,4},{24,8},{28,12},{1,17},{... | collective-permute-start | bytes 4325384 | tf_op jit(solution)/shard_map/ppermute | solution.py:413
  666.4 24.6 %collective-permute-start.47 = (bf16[176,1024]{1,0:T(8,128)(2,1)S(1)}, bf16[176,1024]{1,0:T(8,128)(2,1)}, u32[]{:S(2)}, u32[]{:S(2)}) collective-permute-start(bf16[176,1024]{1,0:T(8,128)(2,1)S(1)} %add_convert_fusion.15), channel_id=1, source_target_pairs={{0,8},{4,12},{8,0},{12,4},{16,24},{20,28},{24,16},{28,20},{1,9},{5... | collective-permute-start | bytes 1081352 | tf_op jit(solution)/shard_map/ppermute | solution.py:413
  670.3 20.7 %collective-permute-start.46 = (bf16[176,1024]{1,0:T(8,128)(2,1)}, bf16[176,1024]{1,0:T(8,128)(2,1)}, u32[]{:S(2)}, u32[]{:S(2)}) collective-permute-start(bf16[176,1024]{1,0:T(8,128)(2,1)} %add_convert_fusion.16), channel_id=1, source_target_pairs={{0,16},{4,20},{8,24},{12,28},{16,0},{20,4},{24,8},{28,12},{1,17},{... | collective-permute-start | bytes 1081352 | tf_op jit(solution)/shard_map/ppermute | solution.py:413
  704.3 24.2 %collective-permute-start.48 = (bf16[1024,2048]{1,0:T(8,128)(2,1)}, bf16[1024,2048]{1,0:T(8,128)(2,1)}, u32[]{:S(2)}, u32[]{:S(2)}) collective-permute-start(bf16[1024,2048]{1,0:T(8,128)(2,1)} %pad_maximum_fusion), channel_id=1, source_target_pairs={{0,4},{4,0},{8,12},{12,8},{16,20},{20,16},{24,28},{28,24},{1,5},{5... | collective-permute-start | bytes 12582920 | tf_op jit(solution)/shard_map/ppermute | solution.py:413
  705.8 19.7 %collective-permute-start.50 = (bf16[352,1024]{1,0:T(8,128)(2,1)S(1)}, bf16[352,1024]{1,0:T(8,128)(2,1)S(1)}, u32[]{:S(2)}, u32[]{:S(2)}) collective-permute-start(bf16[352,1024]{1,0:T(8,128)(2,1)S(1)} %maximum_select_fusion.5.refs_2_), channel_id=1, source_target_pairs={{0,16},{4,20},{8,24},{12,28},{16,0},{20,4},{24,8},{28,12},{1,17},{... | collective-permute-start | bytes 2162696 | tf_op jit(solution)/shard_map/ppermute | solution.py:413
  708.3 19.3 %collective-permute-start.49 = (bf16[352,1024]{1,0:T(8,128)(2,1)S(1)}, bf16[352,1024]{1,0:T(8,128)(2,1)S(1)}, u32[]{:S(2)}, u32[]{:S(2)}) collective-permute-start(bf16[352,1024]{1,0:T(8,128)(2,1)S(1)} %maximum_select_fusion.4.refs_0_), channel_id=1, source_target_pairs={{0,8},{4,12},{8,0},{12,4},{16,24},{20,28},{24,16},{28,20},{1,9},{5... | collective-permute-start | bytes 2162696 | tf_op jit(solution)/shard_map/ppermute | solution.py:413
  736.6 25.1 %collective-permute-start.51 = (bf16[256,2048]{1,0:T(8,128)(2,1)}, bf16[256,2048]{1,0:T(8,128)(2,1)}, u32[]{:S(2)}, u32[]{:S(2)}) collective-permute-start(bf16[256,2048]{1,0:T(8,128)(2,1)} %constant_dynamic-slice_fusion.3), channel_id=1, source_target_pairs={{0,8},{4,12},{8,0},{12,4},{16,24},{20,28},{24,16},{28,20},{1,9},{5... | collective-permute-start | bytes 3145736 | tf_op jit(solution)/shard_map/ppermute | solution.py:413
  744.5 69.6 %collective-permute-start.65 = (bf16[1024,2816]{1,0:T(8,128)(2,1)}, bf16[1024,2816]{1,0:T(8,128)(2,1)}, u32[]{:S(2)}, u32[]{:S(2)}) collective-permute-start(bf16[1024,2816]{1,0:T(8,128)(2,1)} %assemble.4.half_ref), channel_id=1, source_target_pairs={{0,4},{4,0},{8,12},{12,8},{16,20},{20,16},{24,28},{28,24},{1,5},{5... | collective-permute-start | bytes 17301512 | tf_op jit(solution)/shard_map/ppermute | solution.py:413
  744.6 26.0 %collective-permute-start.52 = (bf16[256,2048]{1,0:T(8,128)(2,1)S(1)}, bf16[256,2048]{1,0:T(8,128)(2,1)S(1)}, u32[]{:S(2)}, u32[]{:S(2)}) collective-permute-start(bf16[256,2048]{1,0:T(8,128)(2,1)S(1)} %constant_dynamic-slice_fusion.2), channel_id=1, source_target_pairs={{0,16},{4,20},{8,24},{12,28},{16,0},{20,4},{24,8},{28,12},{1,17},{... | collective-permute-start | bytes 3145736 | tf_op jit(solution)/shard_map/ppermute | solution.py:413
  747.1 52.0 %collective-permute-start.60 = (bf16[1408,1024]{1,0:T(8,128)(2,1)S(1)}, bf16[1408,1024]{1,0:T(8,128)(2,1)}, u32[]{:S(2)}, u32[]{:S(2)}) collective-permute-start(bf16[1408,1024]{1,0:T(8,128)(2,1)S(1)} %assemble.3.half_ref), channel_id=1, source_target_pairs={{0,4},{4,0},{8,12},{12,8},{16,20},{20,16},{24,28},{28,24},{1,5},{5... | collective-permute-start | bytes 8650760 | tf_op jit(solution)/shard_map/ppermute | solution.py:413
  764.3 30.2 %collective-permute-start.53 = (bf16[128,2048]{1,0:T(8,128)(2,1)}, bf16[128,2048]{1,0:T(8,128)(2,1)S(1)}, u32[]{:S(2)}, u32[]{:S(2)}) collective-permute-start(bf16[128,2048]{1,0:T(8,128)(2,1)} %constant_dynamic-slice_fusion.1), channel_id=1, source_target_pairs={{0,16},{4,20},{8,24},{12,28},{16,0},{20,4},{24,8},{28,12},{1,17},{... | collective-permute-start | bytes 1572872 | tf_op jit(solution)/shard_map/ppermute | solution.py:413
  772.2 22.3 %collective-permute-start.54 = (bf16[128,2048]{1,0:T(8,128)(2,1)}, bf16[128,2048]{1,0:T(8,128)(2,1)}, u32[]{:S(2)}, u32[]{:S(2)}) collective-permute-start(bf16[128,2048]{1,0:T(8,128)(2,1)} %constant_dynamic-slice_fusion), channel_id=1, source_target_pairs={{0,8},{4,12},{8,0},{12,4},{16,24},{20,28},{24,16},{28,20},{1,9},{5... | collective-permute-start | bytes 1572872 | tf_op jit(solution)/shard_map/ppermute | solution.py:413
  783.0 11.5 %collective-permute-start.57 = (f32[14,1024]{1,0:T(8,128)S(1)}, f32[14,1024]{1,0:T(8,128)S(1)}, u32[]{:S(2)}, u32[]{:S(2)}) collective-permute-start(f32[14,1024]{1,0:T(8,128)S(1)} %add.456), channel_id=1, source_target_pairs={{0,2},{1,3},{2,0},{3,1},{4,6},{5,7},{6,4},{7,5},{8,10},{9,11},{10,... | collective-permute-start | bytes 172040 | tf_op jit(solution)/shard_map/ppermute | solution.py:669
  795.9 14.1 %collective-permute-start.59 = (bf16[128,2048]{1,0:T(8,128)(2,1)S(1)}, bf16[128,2048]{1,0:T(8,128)(2,1)S(1)}, u32[]{:S(2)}, u32[]{:S(2)}) collective-permute-start(bf16[128,2048]{1,0:T(8,128)(2,1)S(1)} %add_convert_fusion.13), channel_id=1, source_target_pairs={{0,8},{4,12},{8,0},{12,4},{16,24},{20,28},{24,16},{28,20},{1,9},{5... | collective-permute-start | bytes 1572872 | tf_op jit(solution)/shard_map/ppermute | solution.py:413
  797.7 13.6 %collective-permute-start.58 = (bf16[128,2048]{1,0:T(8,128)(2,1)S(1)}, bf16[128,2048]{1,0:T(8,128)(2,1)S(1)}, u32[]{:S(2)}, u32[]{:S(2)}) collective-permute-start(bf16[128,2048]{1,0:T(8,128)(2,1)S(1)} %add_convert_fusion.14), channel_id=1, source_target_pairs={{0,16},{4,20},{8,24},{12,28},{16,0},{20,4},{24,8},{28,12},{1,17},{... | collective-permute-start | bytes 1572872 | tf_op jit(solution)/shard_map/ppermute | solution.py:413
  811.6 24.1 %collective-permute-start.64 = (bf16[256,2048]{1,0:T(8,128)(2,1)S(1)}, bf16[256,2048]{1,0:T(8,128)(2,1)S(1)}, u32[]{:S(2)}, u32[]{:S(2)}) collective-permute-start(bf16[256,2048]{1,0:T(8,128)(2,1)S(1)} %maximum_select_fusion.3.refs_2_), channel_id=1, source_target_pairs={{0,16},{4,20},{8,24},{12,28},{16,0},{20,4},{24,8},{28,12},{1,17},{... | collective-permute-start | bytes 3145736 | tf_op jit(solution)/shard_map/ppermute | solution.py:413
  813.4 24.0 %collective-permute-start.63 = (bf16[256,2048]{1,0:T(8,128)(2,1)S(1)}, bf16[256,2048]{1,0:T(8,128)(2,1)S(1)}, u32[]{:S(2)}, u32[]{:S(2)}) collective-permute-start(bf16[256,2048]{1,0:T(8,128)(2,1)S(1)} %maximum_select_fusion.2.refs_0_), channel_id=1, source_target_pairs={{0,8},{4,12},{8,0},{12,4},{16,24},{20,28},{24,16},{28,20},{1,9},{5... | collective-permute-start | bytes 3145736 | tf_op jit(solution)/shard_map/ppermute | solution.py:413
  840.6 20.4 %collective-permute-start.66 = (bf16[1024,2048]{1,0:T(8,128)(2,1)}, bf16[1024,2048]{1,0:T(8,128)(2,1)}, u32[]{:S(2)}, u32[]{:S(2)}) collective-permute-start(bf16[1024,2048]{1,0:T(8,128)(2,1)} %assemble.5.half_ref), channel_id=1, source_target_pairs={{0,4},{4,0},{8,12},{12,8},{16,20},{20,16},{24,28},{28,24},{1,5},{5... | collective-permute-start | bytes 12582920 | tf_op jit(solution)/shard_map/ppermute | solution.py:413
  (112 other events, 1456.9 us)
Sparse Core Ops, SparseCore 0:
  12.7 83.4 all-gather.6
  97.8 85.6 all-gather.8
  209.9 52.5 all-gather.14
  274.4 82.2 all-gather.10
  422.7 75.2 reduce-scatter.3
  542.2 80.0 all-gather.12
  640.1 77.7 reduce-scatter.5
  739.0 79.7 reduce-scatter.7
